TPU v7x, 32 devices: a whole 2x2x4 slice. The times are simulated.
32 devices in a mesh: ka: 4 (over y, x), pts: 8 (over z, core).
Axes of the slice: x: 2, y: 2, z: 4, core: 2. Of those that a mesh axis runs over, the one named last changes fastest.
Arguments:
- orbitals: bfloat16 [32, 2, 512, 2048], P('ka', None, None, 'pts'), may hold values from -1.078125 to 1.078125
- coulomb: bfloat16 [32, 32, 2048], P('ka', None, 'pts'), may hold values from -6 to 6
Outputs:
- exchange: bfloat16 [512, 32, 2, 512], P('pts', 'ka')
All inputs are finite; a program needn't handle non-finite values.
Results may differ from a plain program's by a relative error of at most 0.0064.
Values may be sent and summed in bfloat16 or wider, within the bound.
No kernel may reach another device: no remote copies, remote signals or barrier semaphores. Data moves between devices by JAX's collectives and lax.ppermute only.
A program may use at most 64 MiB of HBM per device.

v0:
```python
import math

import jax
import jax.numpy as jnp
from jax import lax
from jax.sharding import PartitionSpec as P

COLS_DEV = 4


def phase_tables(left_idx, right_idx, modulus):
    product = left_idx[:, None] * right_idx[None, :] % modulus
    angles = product.astype(jnp.float32) * (2.0 * math.pi / modulus)
    return (jnp.cos(angles), jnp.sin(angles))


def phase_mix(weights, values):
    return jnp.einsum("rq,qcm->rcm", weights, values, precision=lax.Precision.HIGHEST)


def forward_terms(cosine, sine_table, tiles_wide):
    real_part = phase_mix(cosine, tiles_wide[:, 0]) - phase_mix(sine_table, tiles_wide[:, 1])
    imag_part = phase_mix(sine_table, tiles_wide[:, 0]) + phase_mix(cosine, tiles_wide[:, 1])
    return jnp.stack([real_part, imag_part], 1)


def backward_terms(cosine, sine_table, cells_wide):
    real_part = phase_mix(cosine, cells_wide[:, 0]) + phase_mix(sine_table, cells_wide[:, 1])
    imag_part = phase_mix(cosine, cells_wide[:, 1]) - phase_mix(sine_table, cells_wide[:, 0])
    return jnp.stack([real_part, imag_part], 1)


def contract(left_op, right_op):
    return jnp.einsum("knc,knm->kcm", left_op, right_op, preferred_element_type=jnp.float32)


def point_sum(left_op, right_op):
    return jnp.einsum("kam,kcm->akc", left_op, right_op, preferred_element_type=jnp.float32)


def column_sum(left_op, right_op):
    return jnp.einsum("akc,knc->akn", left_op, right_op, precision=lax.Precision.HIGHEST)


def body(orbitals, coulomb):
    local_k = orbitals.shape[0]
    total_k = local_k * lax.axis_size("ka")
    edge_cols = orbitals[:, :, :, :COLS_DEV]
    columns = lax.all_gather(edge_cols, "pts", axis=3, tiled=True)
    col_re = columns[:, 0]
    col_im = columns[:, 1]
    orb_re = orbitals[:, 0]
    orb_im = orbitals[:, 1]
    tile_set = jnp.stack(
        [
            contract(col_re, orb_re) + contract(col_im, orb_im),
            contract(col_re, orb_im) - contract(col_im, orb_re),
        ],
        1,
    ).astype(jnp.bfloat16)
    part_tiles = lax.all_to_all(tile_set, "ka", split_axis=2, concat_axis=0, tiled=True)
    part_coulomb = lax.all_to_all(coulomb[:, None], "ka", split_axis=2, concat_axis=0, tiled=True)
    indices = jnp.arange(total_k, dtype=jnp.int32)
    cosine, sine_table = phase_tables(indices, indices, total_k)
    cell_tiles = (
        forward_terms(cosine, sine_table, part_tiles.astype(jnp.float32))
        * part_coulomb.astype(jnp.float32)
    ).astype(jnp.bfloat16)
    regrouped = (
        backward_terms(cosine, sine_table, cell_tiles.astype(jnp.float32)) / total_k
    ).astype(jnp.bfloat16)
    kernel = lax.all_to_all(regrouped, "ka", split_axis=0, concat_axis=2, tiled=True)
    ker_re = kernel[:, 0]
    ker_im = kernel[:, 1]
    row_re = orbitals[:, 0]
    row_im = orbitals[:, 1]
    summed_rows = lax.psum_scatter(
        jnp.stack(
            [
                point_sum(row_re, ker_re) + point_sum(row_im, ker_im),
                point_sum(row_re, ker_im) - point_sum(row_im, ker_re),
            ],
            2,
        ),
        "pts",
        scatter_dimension=0,
        tiled=True,
    )
    w_re = summed_rows[:, :, 0]
    w_im = summed_rows[:, :, 1]
    cols_re = col_re.astype(jnp.float32)
    cols_im = col_im.astype(jnp.float32)
    result = jnp.stack(
        [
            column_sum(w_re, cols_re) - column_sum(w_im, cols_im),
            column_sum(w_re, cols_im) + column_sum(w_im, cols_re),
        ],
        2,
    )
    factor = 1.0 / math.sqrt(orbitals.shape[3] * lax.axis_size("pts"))
    return (result * factor).astype(jnp.bfloat16)


def solution(mesh):
    in_specs = (P("ka", None, None, "pts"), P("ka", None, "pts"))
    out_specs = P("pts", "ka", None, None)
    return jax.shard_map(body, mesh=mesh, in_specs=in_specs, out_specs=out_specs, check_vma=False)
```

profile of v0, /device:TPU:0, one launch (start us, length us, event | category | flops | bytes accessed | tf_op | source)
XLA Modules:
  0.0 112.6 jit_solution(17926046626241678218)
XLA Ops:
  6.5 1.6 %copy.47 = bf16[8,32,256]{2,0,1:T(8,128)(2,1)} copy(bf16[8,32,256]{2,1,0:T(8,128)(2,1)} %param.3) | data formatting | bytes 262144 | tf_op args[1]
  8.2 5.2 %all-to-all-start.1 = ((bf16[8,1,32,256]{3,0,1,2:T(8,128)(2,1)}), bf16[8,1,32,256]{3,0,1,2:T(8,128)(2,1)S(1)}, u32[]{:S(2)}, u32[]{:S(2)}) async-start(bf16[8,1,32,256]{3,0,1,2:T(8,128)(2,1)} %bitcast.160), calls=%async_computation.1 | async-start | bytes 262144 | tf_op jit(solution)/shard_map/all_to_all | solution.py:62
  13.3 1.6 %slice-done = bf16[8,2,512,4]{3,2,1,0:T(8,128)(2,1)S(1)} async-done(((bf16[8,2,512,256]{3,2,1,0:T(8,128)(2,1)}), bf16[8,2,512,4]{3,2,1,0:T(8,128)(2,1)S(1)}, s32[]{:S(2)}) %slice-start) | async-done | bytes 65560 | tf_op jit(solution)/shard_map/slice | solution.py:48
  14.9 0.9 copy.24
  15.9 15.2 %all_gather.3 = bf16[8,2,512,32]{2,0,1,3:T(8,128)(2,1)S(1)} all-gather(bf16[8,2,512,4]{2,0,1,3:T(8,128)(2,1)S(1)} %copy.24), channel_id=1, replica_groups=mesh['ka'=4,'pts'=8] {'pts'}, dimensions={3}, use_global_device_ids=true | all-gather | bytes 589824 | tf_op jit(solution)/shard_map/all_gather | solution.py:49
  31.1 2.0 %fusion.5 = f32[8,32,256]{2,1,0:T(8,128)S(1)} fusion(bf16[8,2,512,256]{3,2,1,0:T(8,128)(2,1)} %param.2, bf16[8,1,512,32]{2,0,1,3:T(8,128)(2,1)S(1)} %get-tuple-element.7), kind=kOutput, calls=%fused_computation.6 | convolution fusion | flops 67108864 | bytes 2621440 | tf_op jit(solution)/shard_map/knc,knm->kcm/dot_general | solution.py:34
  33.1 0.4 fusion.7
  33.5 0.4 fusion.58
  33.9 0.4 fusion.55
  34.3 0.9 copy.15
  35.2 4.2 %all-to-all-start = ((bf16[8,2,32,256]{3,0,1,2:T(8,128)(2,1)}), bf16[8,2,32,256]{3,0,1,2:T(8,128)(2,1)S(1)}, u32[]{:S(2)}, u32[]{:S(2)}) async-start(bf16[8,2,32,256]{3,0,1,2:T(8,128)(2,1)} %copy.15), calls=%async_computation | async-start | bytes 524288 | tf_op jit(solution)/shard_map/all_to_all | solution.py:61
  39.4 5.8 %all-to-all-done = bf16[8,2,32,256]{3,0,1,2:T(8,128)(2,1)S(1)} async-done(((bf16[8,2,32,256]{3,0,1,2:T(8,128)(2,1)}), bf16[8,2,32,256]{3,0,1,2:T(8,128)(2,1)S(1)}, u32[]{:S(2)}, u32[]{:S(2)}) %all-to-all-start) | async-done | bytes 262176 | tf_op jit(solution)/shard_map/all_to_all | solution.py:61
  45.3 0.3 fusion.69
  45.6 0.3 fusion.70
  45.9 0.3 fusion.47
  46.3 0.3 fusion.48
  47.3 0.3 fusion.45
  47.7 0.3 fusion.46
  48.2 8.1 %all_to_all.45 = bf16[32,2,8,256]{3,2,1,0:T(8,128)(2,1)S(1)} all-to-all(bf16[32,2,8,256]{3,2,1,0:T(8,128)(2,1)S(1)} %copy.19), channel_id=1, replica_groups=mesh['ka'=4,'pts'=8] {'ka'}, dimensions={0} | all-to-all | bytes 524288 | tf_op jit(solution)/shard_map/all_to_all | solution.py:72
  56.4 0.7 fusion.1
  57.1 0.7 fusion.3
  57.8 0.7 fusion.36
  58.5 0.7 fusion.30
  59.4 3.7 %copy.22 = f32[512,8,2,32]{3,1,2,0:T(8,128)} copy(f32[512,8,2,32]{0,3,1,2:T(8,128)S(1)} %pad_maximum_fusion) | data formatting | bytes 2097152
  63.0 4.4 %reshape.15 = f32[512,512]{1,0:T(8,128)} reshape(f32[512,2,8,32]{3,2,1,0:T(8,128)} %bitcast.161) | data formatting | bytes 2097152
  67.5 31.9 %reduce-scatter.4.cloned.1.call-done = f32[64,512]{1,0:T(8,128)} async-done(((f32[512,512]{1,0:T(8,128)}), f32[64,512]{1,0:T(8,128)}) %reduce-scatter.4.cloned.1.call-update) | async-done | bytes 131088
  99.4 1.1 reshape.16
  100.6 0.6 fusion.64
  101.3 0.6 fusion.63
  102.0 0.7 fusion.17
  102.7 0.6 fusion.18
  103.7 2.1 %copy.21 = bf16[64,8,2,512]{3,2,1,0:T(2,128)(2,1)} copy(bf16[64,8,2,512]{3,0,1,2:T(8,128)(2,1)S(1)} %fusion) | data formatting | bytes 2097152 | tf_op jit(solution)/shard_map/convert_element_type | solution.py:101
  (23 shorter events, 1.8 us)
Async XLA Ops:
  8.2 27.0 %all-to-all-start.1 = ((bf16[8,1,32,256]{3,0,1,2:T(8,128)(2,1)}), bf16[8,1,32,256]{3,0,1,2:T(8,128)(2,1)S(1)}, u32[]{:S(2)}, u32[]{:S(2)}) async-start(bf16[8,1,32,256]{3,0,1,2:T(8,128)(2,1)} %bitcast.160), calls=%async_computation.1 | async-start | bytes 262144 | tf_op jit(solution)/shard_map/all_to_all | solution.py:62
  13.3 1.6 %slice-start = ((bf16[8,2,512,256]{3,2,1,0:T(8,128)(2,1)}), bf16[8,2,512,4]{3,2,1,0:T(8,128)(2,1)S(1)}, s32[]{:S(2)}) async-start(bf16[8,2,512,256]{3,2,1,0:T(8,128)(2,1)} %param.2), calls=%async_computation.5 | async-start | bytes 4194304 | tf_op jit(solution)/shard_map/slice | solution.py:48
  15.9 17.2 %copy-start = (bf16[8,2,512,256]{3,2,1,0:T(8,128)(2,1)S(1)}, bf16[8,2,512,256]{3,2,1,0:T(8,128)(2,1)}, u32[]{:S(2)}) copy-start(bf16[8,2,512,256]{3,2,1,0:T(8,128)(2,1)} %param.2) | copy-start | bytes 12582916
  35.2 10.1 %all-to-all-start = ((bf16[8,2,32,256]{3,0,1,2:T(8,128)(2,1)}), bf16[8,2,32,256]{3,0,1,2:T(8,128)(2,1)S(1)}, u32[]{:S(2)}, u32[]{:S(2)}) async-start(bf16[8,2,32,256]{3,0,1,2:T(8,128)(2,1)} %copy.15), calls=%async_computation | async-start | bytes 524288 | tf_op jit(solution)/shard_map/all_to_all | solution.py:61
  39.4 60.0 %reduce-scatter.4.cloned.1.call-start = ((), (), s32[]{:S(2)}) async-start(), calls=%async_computation.4 | async-start | bytes 1179648
  46.7 9.7 %copy-start.1 = (bf16[8,2,512,256]{3,2,1,0:T(8,128)(2,1)S(1)}, bf16[8,2,512,256]{3,2,1,0:T(8,128)(2,1)}, u32[]{:S(2)}) copy-start(bf16[8,2,512,256]{3,2,1,0:T(8,128)(2,1)} %param.2) | copy-start | bytes 12582916
Sparse Core Ops, SparseCore 0:
  67.6 31.7 reduce-scatter.3
where the time goes:
time: 113 us
  waiting for transfers between devices  37.8 us (33%)
  blocking collectives  23.3 us (21%)
  local copies, waits for them, and re-layouts  16.7 us (15%)
  between operations  13.6 us (12%)
  matrix products  11.2 us (10%)
  starting transfers between devices  9.35 us (8%)
    unnamed x2, waiting for transfers between devices  31.9 us
    all_gather x1, blocking collectives, body(): columns = lax.all_gather(edge_cols, 'pts', axis=3, tiled=True)  15.2 us
    unnamed x11, local copies, waits for them, and re-layouts  12 us
    all_to_all x1, blocking collectives, body(): lax.all_to_all(regrouped, 'ka', split_axis=0, concat_axis=2, tiled=True)  8.11 us
    all_to_all x1, waiting for transfers between devices, body(): lax.all_to_all(tile_set, 'ka', split_axis=2, concat_axis=0, tiled=True)  5.85 us
    all_to_all x1, starting transfers between devices, body(): lax.all_to_all(coulomb[:, None], 'ka', split_axis=2, concat_axis=0, tiled...  5.16 us
    all_to_all x1, starting transfers between devices, body(): lax.all_to_all(tile_set, 'ka', split_axis=2, concat_axis=0, tiled=True)  4.19 us
    dot_general x4, matrix products, contract(): jnp.einsum('knc,knm->kcm', left_op, right_op, preferred_element_type=jnp....  3.21 us
  transfers between devices with their start and end apart: 3, of which 2 were waited for; matrix products, arithmetic and copies ran while one was open for 5% of the time, Pallas kernels for 0%

commit v1 on v0

v1 whole, which is shorter than its diff:
```python
import functools
import math

import jax
import jax.numpy as jnp
import ml_dtypes
import numpy as np
from jax import lax
from jax.experimental import pallas as pl
from jax.experimental.pallas import tpu as pltpu
from jax.sharding import PartitionSpec as P

BF16 = jnp.bfloat16
F32 = jnp.float32
LANES = 128
ROWS = 16
MIB = 1 << 20


def split_terms(table):
    high = table.astype(ml_dtypes.bfloat16)
    low = (table - high.astype(np.float64)).astype(ml_dtypes.bfloat16)
    return np.concatenate([high, low], axis=1)


def phase_tables(total):
    index = np.arange(total)
    angles = (index[:, None] * index[None, :] % total) * (2.0 * math.pi / total)
    cosine, sine = np.cos(angles), np.sin(angles)
    forward = np.zeros((2, total, total, 2))
    forward[0, :, :, 0] = cosine
    forward[0, :, :, 1] = -sine
    forward[1, :, :, 0] = sine
    forward[1, :, :, 1] = cosine
    backward = np.zeros((total, 2, 2, total))
    backward[:, 0, 0] = cosine
    backward[:, 0, 1] = sine
    backward[:, 1, 1] = cosine
    backward[:, 1, 0] = -sine
    size = 2 * total
    return (
        split_terms(forward.reshape(size, size)),
        split_terms(backward.reshape(size, size) / total),
    )


def column_selector(group, blocks, per_block, shares):
    total = blocks * per_block
    share = total // shares
    table = np.zeros((group, 2, shares, 2, share, blocks, group, 2, per_block), np.float32)
    for k in range(group):
        for col in range(total):
            d, c = divmod(col, share)
            b, j = divmod(col, per_block)
            table[k, 0, d, 0, c, b, k, 0, j] = 1.0
            table[k, 0, d, 1, c, b, k, 1, j] = -1.0
            table[k, 1, d, 0, c, b, k, 1, j] = 1.0
            table[k, 1, d, 1, c, b, k, 0, j] = 1.0
    return table.reshape(group * 4 * total, blocks * group * 2 * per_block).astype(ml_dtypes.bfloat16)


def dot(left, right, dims=((1,), (0,))):
    return lax.dot_general(left, right, (dims, ((), ())), preferred_element_type=F32)


def spread(wide, start, stride, value):
    for t in range(wide.shape[0]):
        wide[t, pl.ds(start, value.shape[0], stride=stride), :] = value[:, t * LANES : (t + 1) * LANES]


def take(wide, start, size):
    return jnp.concatenate([wide[t, pl.ds(start, size), :] for t in range(wide.shape[0])], axis=1)


def tiled(rows, lanes):
    return pltpu.VMEM((lanes // LANES, rows, LANES), F32)


def call(kernel, out_shape, n_in, scratch=(), limit=24, flops=0, size=0):
    whole = pl.BlockSpec(memory_space=pltpu.VMEM)
    return pl.pallas_call(
        kernel,
        out_shape=out_shape,
        in_specs=[whole] * n_in,
        out_specs=jax.tree.map(lambda _: whole, out_shape),
        scratch_shapes=list(scratch),
        compiler_params=pltpu.CompilerParams(vmem_limit_bytes=limit * MIB),
        cost_estimate=pl.CostEstimate(flops=flops, bytes_accessed=size, transcendentals=0),
    )


def edge_kernel(per_block, orb_ref, out_ref):
    group = orb_ref.shape[0]
    row = lax.broadcasted_iota(jnp.int32, (2 * per_block, LANES), 0)
    lane = lax.broadcasted_iota(jnp.int32, (2 * per_block, LANES), 1)
    first = jnp.where(row < per_block, (row == lane).astype(F32), 0.0).astype(BF16)
    second = jnp.where(row >= per_block, (row - per_block == lane).astype(F32), 0.0).astype(BF16)
    rows = []
    for k in range(group):
        rows.append(
            dot(first, orb_ref[k, 0], ((1,), (1,))) + dot(second, orb_ref[k, 1], ((1,), (1,)))
        )
    out_ref[...] = jnp.concatenate(rows, axis=0).astype(BF16)


def coulomb_kernel(shares, coulomb_ref, *refs):
    outs, wide = refs[:shares], refs[shares]
    cells, columns, points = coulomb_ref.shape
    share = columns // shares
    me = lax.axis_index("ka")
    wide[...] = coulomb_ref[...].astype(F32)
    for s in range(shares):
        dest = jnp.bitwise_xor(me, s)
        start = pl.multiple_of(dest * share, share)
        for r in range(cells):
            outs[s][r] = wide[r, pl.ds(start, share), :].astype(BF16)


def tile_kernel(shares, blocks, per_block, *refs):
    edges, orb_ref, sel_ref = refs[:blocks], refs[blocks], refs[blocks + 1]
    outs = refs[blocks + 2 : blocks + 2 + shares]
    form_ref, gathered, wide = refs[blocks + 2 + shares :]
    local_k, _, norb, points = orb_ref.shape
    group = ROWS // (2 * per_block)
    total = blocks * per_block
    share = total // shares
    rows = 2 * total
    me = lax.axis_index("ka")
    block = lax.axis_index("pts")
    for s in range(blocks):
        gathered[jnp.bitwise_xor(block, s)] = edges[s][...]
    for g in range(local_k // group):
        stacked = jnp.concatenate(
            [gathered[b, g * ROWS : (g + 1) * ROWS] for b in range(blocks)], axis=0
        )
        forms = dot(sel_ref[...], stacked).astype(BF16)
        for kk in range(group):
            k = g * group + kk
            left = forms[2 * kk * rows : (2 * kk + 1) * rows]
            right = forms[(2 * kk + 1) * rows : (2 * kk + 2) * rows]
            form = jnp.concatenate([left, right], axis=1)
            form_ref[k] = form
            tile = dot(form, orb_ref[k].reshape(2 * norb, points))
            for d in range(shares):
                for part in range(2):
                    low = (2 * d + part) * share
                    start = d * share * 2 * local_k + 2 * k + part
                    spread(wide, start, 2 * local_k, tile[low : low + share])
    size = share * 2 * local_k
    for s in range(shares):
        dest = jnp.bitwise_xor(me, s)
        outs[s][...] = take(wide, pl.multiple_of(dest * size, size), size).astype(BF16)


def transform_kernel(shares, total, share, *refs):
    tiles, coulombs = refs[:shares], refs[shares : 2 * shares]
    fwd_ref, bwd_ref = refs[2 * shares : 2 * shares + 2]
    outs = refs[2 * shares + 2 : 3 * shares + 2]
    gathered, weight, wide = refs[3 * shares + 2 :]
    local_k = total // shares
    me = lax.axis_index("ka")
    for s in range(shares):
        src = jnp.bitwise_xor(me, s)
        gathered[src] = tiles[s][...].astype(gathered.dtype)
        for r in range(local_k):
            spread(weight, src * local_k + r, total, coulombs[s][r].astype(F32))
    rows = 2 * local_k
    columns = []
    for c in range(share):
        columns.append(
            jnp.concatenate([gathered[a, c * rows : (c + 1) * rows] for a in range(shares)], axis=0).astype(BF16)
        )
    values = jnp.concatenate(columns, axis=1)
    cells = dot(fwd_ref[...], jnp.concatenate([values, values], axis=0))
    scale = jnp.concatenate([take(weight, c * total, total) for c in range(share)], axis=1)
    cells = (cells * jnp.concatenate([scale, scale], axis=0)).astype(BF16)
    kernel = dot(bwd_ref[...], jnp.concatenate([cells, cells], axis=0))
    points = kernel.shape[1] // share
    for c in range(share):
        spread(wide, c, share, kernel[:, c * points : (c + 1) * points])
    size = 2 * local_k * share
    for s in range(shares):
        dest = jnp.bitwise_xor(me, s)
        outs[s][...] = take(wide, pl.multiple_of(dest * size, size), size).astype(BF16)


def weight_kernel(shares, flip, out_rows, *refs):
    pieces, orb_ref, out_ref, gathered = refs[:shares], refs[shares], refs[shares + 1], refs[shares + 2]
    local_k, _, norb, points = orb_ref.shape
    total_rows = gathered.shape[1]
    half = total_rows // local_k // 2
    me = lax.axis_index("ka")
    core = jnp.bitwise_xor(jnp.bitwise_and(lax.axis_index("pts"), 1), flip)
    for s in range(shares):
        gathered[jnp.bitwise_xor(me, s)] = pieces[s][...]
    lanes = 2 * half * shares
    group = max(1, LANES // lanes)
    chunks = norb // out_rows // 2
    for g in range(local_k // group):
        right, left = [], []
        for kk in range(group):
            k = g * group + kk
            first, second = [], []
            for a in range(shares):
                piece = gathered[a, k * 2 * half : (k + 1) * 2 * half].astype(F32)
                first.append(piece)
                second.extend([piece[half:], -piece[:half]])
            first = jnp.concatenate(first, axis=0).astype(BF16)
            second = jnp.concatenate(second, axis=0).astype(BF16)
            zero = jnp.zeros_like(first)
            parts = [zero] * (2 * group)
            parts[2 * kk], parts[2 * kk + 1] = first, second
            right.append(jnp.concatenate(parts, axis=1))
            left.append(k)
        right = jnp.concatenate(right, axis=0)
        for z in range(chunks):
            start = pl.multiple_of((2 * z + core) * out_rows, out_rows)
            rows = jnp.concatenate(
                [orb_ref[k, part, pl.ds(start, out_rows), :] for k in left for part in range(2)], axis=1
            )
            out_ref[z, :, g * group * lanes : (g + 1) * group * lanes] = dot(
                rows, right, ((1,), (1,))
            ).astype(out_ref.dtype)


def pair_kernel(chunks, keep_ref, came_ref, own_ref, *outs):
    z = lax.shift_right_logical(lax.axis_index("pts"), 1)
    for s in range(chunks):
        dest = jnp.bitwise_xor(z, s)
        value = keep_ref[dest] + came_ref[dest].astype(F32)
        if s == 0:
            own_ref[...] = value
        else:
            outs[s - 1][...] = value.astype(BF16)


def exchange_kernel(chunks, scale, *refs):
    pieces, form_ref, out_ref, wide = refs[:chunks], refs[chunks], refs[chunks + 1], refs[chunks + 2]
    local_k, lanes, twice = form_ref.shape
    norb = twice // 2
    out_rows = pieces[0].shape[0]
    total = pieces[0][...]
    for s in range(1, chunks):
        total = total + pieces[s][...].astype(F32)
    total = total * scale
    high = total.astype(BF16)
    low = (total - high.astype(F32)).astype(BF16)
    group = max(1, LANES // lanes)
    width = group * lanes
    lane = lax.broadcasted_iota(jnp.int32, (out_rows, width), 1)
    zero = jnp.zeros((out_rows, width), BF16)
    for g in range(local_k // group):
        high_g = high[:, g * width : (g + 1) * width]
        low_g = low[:, g * width : (g + 1) * width]
        left = []
        for kk in range(group):
            keep = (lane >= kk * lanes) & (lane < (kk + 1) * lanes)
            left.append(
                jnp.concatenate([jnp.where(keep, high_g, zero), jnp.where(keep, low_g, zero)], axis=1)
            )
        forms = [form_ref[g * group + kk] for kk in range(group)]
        result = dot(jnp.concatenate(left, axis=0), jnp.concatenate(forms + forms, axis=0))
        for kk in range(group):
            k = g * group + kk
            for part in range(2):
                value = result[kk * out_rows : (kk + 1) * out_rows, part * norb : (part + 1) * norb]
                spread(wide, 2 * k + part, 2 * local_k, value)
    for t in range(norb // LANES):
        value = wide[t].astype(BF16).reshape(out_rows, local_k, 2, LANES)
        out_ref[:, :, :, t * LANES : (t + 1) * LANES] = value


def swap(value, axis, mask):
    size = lax.axis_size(axis)
    return lax.ppermute(value, axis, [(i, i ^ mask) for i in range(size)])


def body(orbitals, coulomb):
    shares, blocks = lax.axis_size("ka"), lax.axis_size("pts")
    local_k, _, norb, points = orbitals.shape
    columns = coulomb.shape[1]
    per_block = columns // blocks
    share = columns // shares
    total = local_k * shares
    out_rows = norb // blocks
    chunks = blocks // 2
    group = ROWS // (2 * per_block)
    shape = jax.ShapeDtypeStruct

    edge = pl.pallas_call(
        functools.partial(edge_kernel, per_block),
        out_shape=shape((local_k * 2 * per_block, norb), BF16),
        grid=(local_k // group,),
        in_specs=[pl.BlockSpec((group, 2, norb, LANES), lambda g: (g, 0, 0, 0))],
        out_specs=pl.BlockSpec((ROWS, norb), lambda g: (g, 0)),
        cost_estimate=pl.CostEstimate(flops=0, bytes_accessed=2 * MIB, transcendentals=0),
    )(orbitals)
    edges = [edge] + [None] * (blocks - 1)
    for s in range(1, chunks):
        edges[2 * s] = swap(edge, "pts", 2 * s)
    for s in range(chunks):
        edges[2 * s + 1] = swap(edges[2 * s], "pts", 1)

    own = call(
        functools.partial(coulomb_kernel, shares),
        [shape((local_k, share, points), BF16)] * shares,
        1,
        [pltpu.VMEM((local_k, columns, points), F32)],
        size=2 * MIB,
    )(coulomb)
    coulombs = [own[0]] + [swap(own[s], "ka", s) for s in range(1, shares)]

    selector = jnp.asarray(column_selector(group, blocks, per_block, shares))
    piece = shape((share * 2 * local_k, points), BF16)
    *tiles, forms = call(
        functools.partial(tile_kernel, shares, blocks, per_block),
        [piece] * shares + [shape((local_k, 2 * columns, 2 * norb), BF16)],
        blocks + 2,
        [
            pltpu.VMEM((blocks, local_k * 2 * per_block, norb), BF16),
            tiled(columns * 2 * local_k, points),
        ],
        size=8 * MIB,
    )(*edges, orbitals, selector)
    tiles = [tiles[0]] + [swap(tiles[s], "ka", s) for s in range(1, shares)]

    forward, backward = phase_tables(total)
    kernels = call(
        functools.partial(transform_kernel, shares, total, share),
        [piece] * shares,
        2 * shares + 2,
        [
            pltpu.VMEM((shares, share * 2 * local_k, points), BF16 if local_k % 8 == 0 else F32),
            tiled(share * total, points),
            tiled(2 * total * share, points),
        ],
        size=2 * MIB,
    )(*tiles, *coulombs, jnp.asarray(forward), jnp.asarray(backward))
    kernels = [kernels[0]] + [swap(kernels[s], "ka", s) for s in range(1, shares)]

    lanes = local_k * 2 * columns
    halves = []
    for flip, kind in ((1, BF16), (0, F32)):
        halves.append(
            call(
                functools.partial(weight_kernel, shares, flip, out_rows),
                shape((chunks, out_rows, lanes), kind),
                shares + 1,
                [pltpu.VMEM((shares, share * 2 * local_k, points), BF16)],
                size=6 * MIB,
            )(*kernels, orbitals)
        )
    came = swap(halves[0], "pts", 1)
    own_sum, *sums = call(
        functools.partial(pair_kernel, chunks),
        [shape((out_rows, lanes), F32)] + [shape((out_rows, lanes), BF16)] * (chunks - 1),
        2,
        size=1 * MIB,
    )(halves[1], came)
    sums = [own_sum] + [swap(sums[s - 1], "pts", 2 * s) for s in range(1, chunks)]
    return call(
        functools.partial(exchange_kernel, chunks, 1.0 / math.sqrt(points * blocks)),
        shape((out_rows, local_k, 2, norb), BF16),
        chunks + 1,
        [tiled(out_rows * 2 * local_k, norb)],
        size=4 * MIB,
    )(*sums, forms)


def solution(mesh):
    in_specs = (P("ka", None, None, "pts"), P("ka", None, "pts"))
    out_specs = P("pts", "ka", None, None)
    return jax.shard_map(body, mesh=mesh, in_specs=in_specs, out_specs=out_specs, check_vma=False)
```

time: 113 us -> 53.7 us (0.48)
  blocking collectives: 23.3 us -> 0 us
  waiting for transfers between devices: 37.8 us -> 17.7 us
  local copies, waits for them, and re-layouts: 16.7 us -> 3.04 us
  between operations: 13.6 us -> 0.11 us
  starting transfers between devices: 9.35 us -> 21.6 us
  matrix products: 11.2 us -> 0 us
  Pallas kernels: 0 us -> 11.1 us
    unnamed x2 -> x0, waiting for transfers between devices: 31.9 us -> none
    ppermute x0 -> x20, starting transfers between devices: none -> 21.6 us  [swap(): return lax.ppermute(value, axis, [(i, i ^ mask) for i in range(size)])]
    ppermute x0 -> x20, waiting for transfers between devices: none -> 17.7 us  [swap(): return lax.ppermute(value, axis, [(i, i ^ mask) for i in range(size)])]
    all_gather x1 -> x0, blocking collectives: 15.2 us -> none  [body(): columns = lax.all_gather(edge_cols, 'pts', axis=3, tiled=True)]
    dot_general x20 -> x0, matrix products: 11.2 us -> none  [the longest x4 3.21 us: contract(): jnp.einsum('knc,knm->kcm', left_op, right_op, preferred_element_type=jnp....]
    pallas_call x0 -> x8, Pallas kernels: none -> 11.1 us  [the longest x1 3.89 us: body(): pl.pallas_call(functools.partial(edge_kernel, per_block), out_shape=shape...]
    all_to_all x2 -> x0, starting transfers between devices: 9.35 us -> none  [the longest x1 5.16 us: body(): lax.all_to_all(coulomb[:, None], 'ka', split_axis=2, concat_axis=0, tiled...]
    unnamed x11 -> x14, local copies, waits for them, and re-layouts: 12 us -> 3.04 us
  transfers between devices with their start and end apart: 3 -> 20, of which waited for: 2 -> 10; matrix products, arithmetic and copies ran while one was open for 5% -> 0% of each run, Pallas kernels for 0% -> 5%
where the time goes in v1:
time: 53.7 us; the launch traced here: 53.5 us
  starting transfers between devices  21.6 us (40%)
  waiting for transfers between devices  17.7 us (33%)
  Pallas kernels  11.1 us (21%)
  local copies, waits for them, and re-layouts  3.04 us (6%)
    ppermute x20, starting transfers between devices, swap(): return lax.ppermute(value, axis, [(i, i ^ mask) for i in range(size)])  21.6 us
    ppermute x20, waiting for transfers between devices, swap(): return lax.ppermute(value, axis, [(i, i ^ mask) for i in range(size)])  17.7 us
    pallas_call x1, Pallas kernels, body(): pl.pallas_call(functools.partial(edge_kernel, per_block), out_shape=shape...  3.89 us
    unnamed x14, local copies, waits for them, and re-layouts  3.04 us
    pallas_call x1, Pallas kernels, body(): call(functools.partial(exchange_kernel, chunks, 1.0 / math.sqrt(points *...  2.8 us
    pallas_call x2, Pallas kernels, body(): call(functools.partial(weight_kernel, shares, flip, out_rows), shape((chu...  2.33 us
    pallas_call x1, Pallas kernels, body(): call(functools.partial(tile_kernel, shares, blocks, per_block), [piece] *...  1.39 us
  transfers between devices with their start and end apart: 20, of which 10 were waited for; matrix products, arithmetic and copies ran while one was open for 0% of the time, Pallas kernels for 5%

profile of v1, /device:TPU:0, one launch (start us, length us, event | category | flops | bytes accessed | tf_op | source)
XLA Modules:
  0.0 53.5 jit_solution(5221534824950401366)
XLA Ops:
  0.0 3.9 %shard_map.55.refs_0_ = bf16[64,512]{1,0:T(8,128)(2,1)} custom-call(bf16[8,2,512,256]{3,2,1,0:T(8,128)(2,1)} %refs_4_.3), custom_call_target="tpu_custom_call" | custom-call | bytes 2097152 | tf_op jit(solution)/shard_map/pallas_call | solution.py:290
  3.9 5.1 %collective-permute-start.5 = (bf16[64,512]{1,0:T(8,128)(2,1)}, bf16[64,512]{1,0:T(8,128)(2,1)S(1)}, u32[]{:S(2)}, u32[]{:S(2)}) collective-permute-start(bf16[64,512]{1,0:T(8,128)(2,1)} %shard_map.55.refs_0_), channel_id=1, source_target_pairs={{0,6},{1,7},{2,4},{3,5},{4,2},{5,3},{6,0},{7,1},{8,14},{9,15},{10,... | collective-permute-start | bytes 196616 | tf_op jit(solution)/shard_map/ppermute | solution.py:275
  9.0 0.6 %collective-permute-start.1 = (bf16[64,512]{1,0:T(8,128)(2,1)}, bf16[64,512]{1,0:T(8,128)(2,1)S(1)}, u32[]{:S(2)}, u32[]{:S(2)}) collective-permute-start(bf16[64,512]{1,0:T(8,128)(2,1)} %shard_map.55.refs_0_), channel_id=1, source_target_pairs={{0,2},{1,3},{2,0},{3,1},{4,6},{5,7},{6,4},{7,5},{8,10},{9,11},{10,... | collective-permute-start | bytes 196616 | tf_op jit(solution)/shard_map/ppermute | solution.py:275
  9.5 2.2 %collective-permute-done.5.refs_6_ = bf16[64,512]{1,0:T(8,128)(2,1)S(1)} collective-permute-done((bf16[64,512]{1,0:T(8,128)(2,1)}, bf16[64,512]{1,0:T(8,128)(2,1)S(1)}, u32[]{:S(2)}, u32[]{:S(2)}) %collective-permute-start.5) | collective-permute-done | bytes 65568 | tf_op jit(solution)/shard_map/ppermute | solution.py:275
  11.8 3.0 %collective-permute-done.3.refs_4_ = bf16[64,512]{1,0:T(8,128)(2,1)S(1)} collective-permute-done((bf16[64,512]{1,0:T(8,128)(2,1)}, bf16[64,512]{1,0:T(8,128)(2,1)S(1)}, u32[]{:S(2)}, u32[]{:S(2)}) %collective-permute-start.3) | collective-permute-done | bytes 65568 | tf_op jit(solution)/shard_map/ppermute | solution.py:275
  14.8 0.5 collective-permute-start.2
  15.3 1.6 %collective-permute-start.10 = (bf16[8,8,256]{2,1,0:T(8,128)(2,1)S(1)}, bf16[8,8,256]{2,1,0:T(8,128)(2,1)S(1)}, u32[]{:S(2)}, u32[]{:S(2)}) collective-permute-start(bf16[8,8,256]{2,1,0:T(8,128)(2,1)S(1)} %get-tuple-element.27), channel_id=1, source_target_pairs={{0,8},{8,0},{16,24},{24,16},{1,9},{9,1},{17,25},{25,17},{2,10},{10... | collective-permute-start | bytes 98312 | tf_op jit(solution)/shard_map/ppermute | solution.py:275
  16.9 2.2 %copy-done = bf16[8,2,512,256]{3,2,1,0:T(8,128)(2,1)S(1)} copy-done((bf16[8,2,512,256]{3,2,1,0:T(8,128)(2,1)S(1)}, bf16[8,2,512,256]{3,2,1,0:T(8,128)(2,1)}, u32[]{:S(2)}) %copy-start) | copy-done | bytes 4194328
  19.1 0.8 %copy-done.2 = bf16[64,512]{1,0:T(8,128)(2,1)S(1)} copy-done((bf16[64,512]{1,0:T(8,128)(2,1)S(1)}, bf16[64,512]{1,0:T(8,128)(2,1)}, u32[]{:S(2)}) %copy-start.2) | copy-done | bytes 65560
  20.0 1.4 %shard_map.56 = (bf16[128,256]{1,0:T(8,128)(2,1)S(1)}, bf16[128,256]{1,0:T(8,128)(2,1)S(1)}, bf16[128,256]{1,0:T(8,128)(2,1)S(1)}, bf16[128,256]{1,0:T(8,128)(2,1)S(1)}, bf16[8,64,1024]{2,1,0:T(8,128)(2,1)S(1)}) custom-call(bf16[64,512]{1,0:T(8,128)(2,1)S(1)} %copy-done.2, bf16[64,512]{1,0:T(8,128)(2,1)S(1)} %collective-permute-done.refs_1_, ...), custom_call_target="tpu_custom_call" | custom-call | bytes 8388608 | tf_op jit(solution)/shard_map/pallas_call | solution.py:315
  21.4 0.8 %collective-permute-start.7 = (bf16[128,256]{1,0:T(8,128)(2,1)S(1)}, bf16[128,256]{1,0:T(8,128)(2,1)S(1)}, u32[]{:S(2)}, u32[]{:S(2)}) collective-permute-start(bf16[128,256]{1,0:T(8,128)(2,1)S(1)} %get-tuple-element.23), channel_id=1, source_target_pairs={{0,8},{8,0},{16,24},{24,16},{1,9},{9,1},{17,25},{25,17},{2,10},{10... | collective-permute-start | bytes 196616 | tf_op jit(solution)/shard_map/ppermute | solution.py:275
  22.2 1.5 %collective-permute-start.8 = (bf16[128,256]{1,0:T(8,128)(2,1)S(1)}, bf16[128,256]{1,0:T(8,128)(2,1)S(1)}, u32[]{:S(2)}, u32[]{:S(2)}) collective-permute-start(bf16[128,256]{1,0:T(8,128)(2,1)S(1)} %get-tuple-element.24), channel_id=1, source_target_pairs={{0,16},{8,24},{16,0},{24,8},{1,17},{9,25},{17,1},{25,9},{2,18},{10... | collective-permute-start | bytes 196616 | tf_op jit(solution)/shard_map/ppermute | solution.py:275
  23.7 1.2 %collective-permute-start.9 = (bf16[128,256]{1,0:T(8,128)(2,1)S(1)}, bf16[128,256]{1,0:T(8,128)(2,1)S(1)}, u32[]{:S(2)}, u32[]{:S(2)}) collective-permute-start(bf16[128,256]{1,0:T(8,128)(2,1)S(1)} %get-tuple-element.25), channel_id=1, source_target_pairs={{0,24},{8,16},{16,8},{24,0},{1,25},{9,17},{17,9},{25,1},{2,26},{10... | collective-permute-start | bytes 196616 | tf_op jit(solution)/shard_map/ppermute | solution.py:275
  24.9 1.5 %collective-permute-start.11 = (bf16[8,8,256]{2,1,0:T(8,128)(2,1)S(1)}, bf16[8,8,256]{2,1,0:T(8,128)(2,1)S(1)}, u32[]{:S(2)}, u32[]{:S(2)}) collective-permute-start(bf16[8,8,256]{2,1,0:T(8,128)(2,1)S(1)} %get-tuple-element.28), channel_id=1, source_target_pairs={{0,16},{8,24},{16,0},{24,8},{1,17},{9,25},{17,1},{25,9},{2,18},{10... | collective-permute-start | bytes 98312 | tf_op jit(solution)/shard_map/ppermute | solution.py:275
  26.4 0.7 %collective-permute-start.12 = (bf16[8,8,256]{2,1,0:T(8,128)(2,1)S(1)}, bf16[8,8,256]{2,1,0:T(8,128)(2,1)S(1)}, u32[]{:S(2)}, u32[]{:S(2)}) collective-permute-start(bf16[8,8,256]{2,1,0:T(8,128)(2,1)S(1)} %get-tuple-element.29), channel_id=1, source_target_pairs={{0,24},{8,16},{16,8},{24,0},{1,25},{9,17},{17,9},{25,1},{2,26},{10... | collective-permute-start | bytes 98312 | tf_op jit(solution)/shard_map/ppermute | solution.py:275
  27.1 2.4 %collective-permute-done.11.refs_6_ = bf16[8,8,256]{2,1,0:T(8,128)(2,1)S(1)} collective-permute-done((bf16[8,8,256]{2,1,0:T(8,128)(2,1)S(1)}, bf16[8,8,256]{2,1,0:T(8,128)(2,1)S(1)}, u32[]{:S(2)}, u32[]{:S(2)}) %collective-permute-start.11) | collective-permute-done | bytes 32800 | tf_op jit(solution)/shard_map/ppermute | solution.py:275
  29.6 1.7 %collective-permute-done.12.refs_7_ = bf16[8,8,256]{2,1,0:T(8,128)(2,1)S(1)} collective-permute-done((bf16[8,8,256]{2,1,0:T(8,128)(2,1)S(1)}, bf16[8,8,256]{2,1,0:T(8,128)(2,1)S(1)}, u32[]{:S(2)}, u32[]{:S(2)}) %collective-permute-start.12) | collective-permute-done | bytes 32800 | tf_op jit(solution)/shard_map/ppermute | solution.py:275
  31.3 0.6 %shard_map.58 = (bf16[128,256]{1,0:T(8,128)(2,1)S(1)}, bf16[128,256]{1,0:T(8,128)(2,1)S(1)}, bf16[128,256]{1,0:T(8,128)(2,1)S(1)}, bf16[128,256]{1,0:T(8,128)(2,1)S(1)}) custom-call(bf16[128,256]{1,0:T(8,128)(2,1)S(1)} %get-tuple-element.22.refs_0_, bf16[128,256]{1,0:T(8,128)(2,1)S(1)} %collective-permute-done.7.refs_1_, ...), custom_call_target="tpu_custom_call" | custom-call | bytes 2097152 | tf_op jit(solution)/shard_map/pallas_call | solution.py:328
  31.9 0.8 %collective-permute-start.13 = (bf16[128,256]{1,0:T(8,128)(2,1)S(1)}, bf16[128,256]{1,0:T(8,128)(2,1)S(1)}, u32[]{:S(2)}, u32[]{:S(2)}) collective-permute-start(bf16[128,256]{1,0:T(8,128)(2,1)S(1)} %get-tuple-element.31), channel_id=1, source_target_pairs={{0,8},{8,0},{16,24},{24,16},{1,9},{9,1},{17,25},{25,17},{2,10},{10... | collective-permute-start | bytes 196616 | tf_op jit(solution)/shard_map/ppermute | solution.py:275
  32.7 0.5 collective-permute-start.14
  33.2 2.2 %collective-permute-start.15 = (bf16[128,256]{1,0:T(8,128)(2,1)S(1)}, bf16[128,256]{1,0:T(8,128)(2,1)S(1)}, u32[]{:S(2)}, u32[]{:S(2)}) collective-permute-start(bf16[128,256]{1,0:T(8,128)(2,1)S(1)} %get-tuple-element.33), channel_id=1, source_target_pairs={{0,24},{8,16},{16,8},{24,0},{1,25},{9,17},{17,9},{25,1},{2,26},{10... | collective-permute-start | bytes 196616 | tf_op jit(solution)/shard_map/ppermute | solution.py:275
  35.4 0.8 %collective-permute-done.13.refs_1_ = bf16[128,256]{1,0:T(8,128)(2,1)S(1)} collective-permute-done((bf16[128,256]{1,0:T(8,128)(2,1)S(1)}, bf16[128,256]{1,0:T(8,128)(2,1)S(1)}, u32[]{:S(2)}, u32[]{:S(2)}) %collective-permute-start.13) | collective-permute-done | bytes 65568 | tf_op jit(solution)/shard_map/ppermute | solution.py:275
  36.2 0.8 %collective-permute-done.14.refs_2_ = bf16[128,256]{1,0:T(8,128)(2,1)S(1)} collective-permute-done((bf16[128,256]{1,0:T(8,128)(2,1)S(1)}, bf16[128,256]{1,0:T(8,128)(2,1)S(1)}, u32[]{:S(2)}, u32[]{:S(2)}) %collective-permute-start.14) | collective-permute-done | bytes 65568 | tf_op jit(solution)/shard_map/ppermute | solution.py:275
  37.0 1.4 %collective-permute-done.15.refs_3_ = bf16[128,256]{1,0:T(8,128)(2,1)S(1)} collective-permute-done((bf16[128,256]{1,0:T(8,128)(2,1)S(1)}, bf16[128,256]{1,0:T(8,128)(2,1)S(1)}, u32[]{:S(2)}, u32[]{:S(2)}) %collective-permute-start.15) | collective-permute-done | bytes 65568 | tf_op jit(solution)/shard_map/ppermute | solution.py:275
  38.4 1.2 %shard_map.60 = bf16[4,64,512]{2,1,0:T(8,128)(2,1)S(1)} custom-call(bf16[128,256]{1,0:T(8,128)(2,1)S(1)} %get-tuple-element.30.refs_0_, bf16[128,256]{1,0:T(8,128)(2,1)S(1)} %collective-permute-done.13.refs_1_, bf16[128,256]{1,0:T(8,128)(2,1)S(1)} %collective-permute-done.14.refs_2_, bf16[128,256]{1,0:T(8,128)(2,1)S(1)} %collective-permute-done.15.refs_3_, ...), custom_call_target="tpu_custom_call" | custom-call | bytes 6291456 | tf_op jit(solution)/shard_map/pallas_call | solution.py:345
  39.6 1.2 %shard_map.59.keep_ref = f32[4,64,512]{2,1,0:T(8,128)S(1)} custom-call(bf16[128,256]{1,0:T(8,128)(2,1)S(1)} %get-tuple-element.30.refs_0_, bf16[128,256]{1,0:T(8,128)(2,1)S(1)} %collective-permute-done.13.refs_1_, bf16[128,256]{1,0:T(8,128)(2,1)S(1)} %collective-permute-done.14.refs_2_, bf16[128,256]{1,0:T(8,128)(2,1)S(1)} %collective-permute-done.15.refs_3_, ...), custom_call_target="tpu_custom_call" | custom-call | bytes 6291456 | tf_op jit(solution)/shard_map/pallas_call | solution.py:345
  41.2 1.0 %collective-permute-start.17 = (bf16[64,512]{1,0:T(8,128)(2,1)S(1)}, bf16[64,512]{1,0:T(8,128)(2,1)S(1)}, u32[]{:S(2)}, u32[]{:S(2)}) collective-permute-start(bf16[64,512]{1,0:T(8,128)(2,1)S(1)} %get-tuple-element.35), channel_id=1, source_target_pairs={{0,2},{1,3},{2,0},{3,1},{4,6},{5,7},{6,4},{7,5},{8,10},{9,11},{10,... | collective-permute-start | bytes 196616 | tf_op jit(solution)/shard_map/ppermute | solution.py:275
  42.2 2.3 %collective-permute-start.18 = (bf16[64,512]{1,0:T(8,128)(2,1)S(1)}, bf16[64,512]{1,0:T(8,128)(2,1)S(1)}, u32[]{:S(2)}, u32[]{:S(2)}) collective-permute-start(bf16[64,512]{1,0:T(8,128)(2,1)S(1)} %get-tuple-element.36), channel_id=1, source_target_pairs={{0,4},{1,5},{2,6},{3,7},{4,0},{5,1},{6,2},{7,3},{8,12},{9,13},{10,... | collective-permute-start | bytes 196616 | tf_op jit(solution)/shard_map/ppermute | solution.py:275
  44.5 1.2 %collective-permute-start.19 = (bf16[64,512]{1,0:T(8,128)(2,1)S(1)}, bf16[64,512]{1,0:T(8,128)(2,1)S(1)}, u32[]{:S(2)}, u32[]{:S(2)}) collective-permute-start(bf16[64,512]{1,0:T(8,128)(2,1)S(1)} %get-tuple-element.37), channel_id=1, source_target_pairs={{0,6},{1,7},{2,4},{3,5},{4,2},{5,3},{6,0},{7,1},{8,14},{9,15},{10,... | collective-permute-start | bytes 196616 | tf_op jit(solution)/shard_map/ppermute | solution.py:275
  45.7 4.1 %collective-permute-done.18.refs_2_ = bf16[64,512]{1,0:T(8,128)(2,1)S(1)} collective-permute-done((bf16[64,512]{1,0:T(8,128)(2,1)S(1)}, bf16[64,512]{1,0:T(8,128)(2,1)S(1)}, u32[]{:S(2)}, u32[]{:S(2)}) %collective-permute-start.18) | collective-permute-done | bytes 65568 | tf_op jit(solution)/shard_map/ppermute | solution.py:275
  49.8 0.9 %collective-permute-done.19.refs_3_ = bf16[64,512]{1,0:T(8,128)(2,1)S(1)} collective-permute-done((bf16[64,512]{1,0:T(8,128)(2,1)S(1)}, bf16[64,512]{1,0:T(8,128)(2,1)S(1)}, u32[]{:S(2)}, u32[]{:S(2)}) %collective-permute-start.19) | collective-permute-done | bytes 65568 | tf_op jit(solution)/shard_map/ppermute | solution.py:275
  50.7 2.8 %shard_map.62 = bf16[64,8,2,512]{3,2,1,0:T(2,128)(2,1)} custom-call(f32[64,512]{1,0:T(8,128)S(1)} %get-tuple-element.34.refs_0_, bf16[64,512]{1,0:T(8,128)(2,1)S(1)} %collective-permute-done.17.refs_1_, bf16[64,512]{1,0:T(8,128)(2,1)S(1)} %collective-permute-done.18.refs_2_, bf16[64,512]{1,0:T(8,128)(2,1)S(1)} %collective-permute-done.19.refs_3_, ...), custom_call_target="tpu_custom_call" | custom-call | bytes 4194304 | tf_op jit(solution)/shard_map/pallas_call | solution.py:361
  (30 shorter events, 0.6 us)
Async XLA Ops:
  0.0 16.9 %copy-start.4 = (bf16[256,128]{1,0:T(8,128)(2,1)S(1)}, bf16[256,128]{1,0:T(8,128)(2,1)}, u32[]{:S(2)}) copy-start(bf16[256,128]{1,0:T(8,128)(2,1)} %constant.6.clone.refs_9_) | copy-start | bytes 196612
  0.0 31.3 %copy-start.5 = (bf16[64,128]{1,0:T(8,128)(2,1)S(1)}, bf16[64,128]{1,0:T(8,128)(2,1)}, u32[]{:S(2)}) copy-start(bf16[64,128]{1,0:T(8,128)(2,1)} %constant.8.clone.refs_9_) | copy-start | bytes 49156
  0.0 31.3 %copy-start.6 = (bf16[64,128]{1,0:T(8,128)(2,1)S(1)}, bf16[64,128]{1,0:T(8,128)(2,1)}, u32[]{:S(2)}) copy-start(bf16[64,128]{1,0:T(8,128)(2,1)} %constant.7.clone.refs_8_) | copy-start | bytes 49156
  0.0 15.3 %copy-start.3 = (bf16[8,32,256]{2,1,0:T(8,128)(2,1)S(1)}, bf16[8,32,256]{2,1,0:T(8,128)(2,1)}, u32[]{:S(2)}) copy-start(bf16[8,32,256]{2,1,0:T(8,128)(2,1)} %coulomb_ref.1) | copy-start | bytes 393220
  3.9 7.9 %collective-permute-start.5 = (bf16[64,512]{1,0:T(8,128)(2,1)}, bf16[64,512]{1,0:T(8,128)(2,1)S(1)}, u32[]{:S(2)}, u32[]{:S(2)}) collective-permute-start(bf16[64,512]{1,0:T(8,128)(2,1)} %shard_map.55.refs_0_), channel_id=1, source_target_pairs={{0,6},{1,7},{2,4},{3,5},{4,2},{5,3},{6,0},{7,1},{8,14},{9,15},{10,... | collective-permute-start | bytes 196616 | tf_op jit(solution)/shard_map/ppermute | solution.py:275
  9.0 5.8 %collective-permute-start.3 = (bf16[64,512]{1,0:T(8,128)(2,1)}, bf16[64,512]{1,0:T(8,128)(2,1)S(1)}, u32[]{:S(2)}, u32[]{:S(2)}) collective-permute-start(bf16[64,512]{1,0:T(8,128)(2,1)} %shard_map.55.refs_0_), channel_id=1, source_target_pairs={{0,4},{1,5},{2,6},{3,7},{4,0},{5,1},{6,2},{7,3},{8,12},{9,13},{10,... | collective-permute-start | bytes 196616 | tf_op jit(solution)/shard_map/ppermute | solution.py:275
  9.0 5.8 %collective-permute-start.1 = (bf16[64,512]{1,0:T(8,128)(2,1)}, bf16[64,512]{1,0:T(8,128)(2,1)S(1)}, u32[]{:S(2)}, u32[]{:S(2)}) collective-permute-start(bf16[64,512]{1,0:T(8,128)(2,1)} %shard_map.55.refs_0_), channel_id=1, source_target_pairs={{0,2},{1,3},{2,0},{3,1},{4,6},{5,7},{6,4},{7,5},{8,10},{9,11},{10,... | collective-permute-start | bytes 196616 | tf_op jit(solution)/shard_map/ppermute | solution.py:275
  9.5 7.4 %collective-permute-start = (bf16[64,512]{1,0:T(8,128)(2,1)}, bf16[64,512]{1,0:T(8,128)(2,1)S(1)}, u32[]{:S(2)}, u32[]{:S(2)}) collective-permute-start(bf16[64,512]{1,0:T(8,128)(2,1)} %shard_map.55.refs_0_), channel_id=1, source_target_pairs={{0,1},{1,0},{2,3},{3,2},{4,5},{5,4},{6,7},{7,6},{8,9},{9,8},{10,11... | collective-permute-start | bytes 196616 | tf_op jit(solution)/shard_map/ppermute | solution.py:275
  11.8 5.1 %collective-permute-start.6 = (bf16[64,512]{1,0:T(8,128)(2,1)S(1)}, bf16[64,512]{1,0:T(8,128)(2,1)S(1)}, u32[]{:S(2)}, u32[]{:S(2)}) collective-permute-start(bf16[64,512]{1,0:T(8,128)(2,1)S(1)} %collective-permute-done.5.refs_6_), channel_id=1, source_target_pairs={{0,1},{1,0},{2,3},{3,2},{4,5},{5,4},{6,7},{7,6},{8,9},{9,8},{10,11... | collective-permute-start | bytes 196616 | tf_op jit(solution)/shard_map/ppermute | solution.py:275
  14.8 2.1 %collective-permute-start.4 = (bf16[64,512]{1,0:T(8,128)(2,1)S(1)}, bf16[64,512]{1,0:T(8,128)(2,1)S(1)}, u32[]{:S(2)}, u32[]{:S(2)}) collective-permute-start(bf16[64,512]{1,0:T(8,128)(2,1)S(1)} %collective-permute-done.3.refs_4_), channel_id=1, source_target_pairs={{0,1},{1,0},{2,3},{3,2},{4,5},{5,4},{6,7},{7,6},{8,9},{9,8},{10,11... | collective-permute-start | bytes 196616 | tf_op jit(solution)/shard_map/ppermute | solution.py:275
  14.8 2.1 %collective-permute-start.2 = (bf16[64,512]{1,0:T(8,128)(2,1)S(1)}, bf16[64,512]{1,0:T(8,128)(2,1)S(1)}, u32[]{:S(2)}, u32[]{:S(2)}) collective-permute-start(bf16[64,512]{1,0:T(8,128)(2,1)S(1)} %collective-permute-done.1.refs_2_), channel_id=1, source_target_pairs={{0,1},{1,0},{2,3},{3,2},{4,5},{5,4},{6,7},{7,6},{8,9},{9,8},{10,11... | collective-permute-start | bytes 196616 | tf_op jit(solution)/shard_map/ppermute | solution.py:275
  15.3 11.1 %collective-permute-start.10 = (bf16[8,8,256]{2,1,0:T(8,128)(2,1)S(1)}, bf16[8,8,256]{2,1,0:T(8,128)(2,1)S(1)}, u32[]{:S(2)}, u32[]{:S(2)}) collective-permute-start(bf16[8,8,256]{2,1,0:T(8,128)(2,1)S(1)} %get-tuple-element.27), channel_id=1, source_target_pairs={{0,8},{8,0},{16,24},{24,16},{1,9},{9,1},{17,25},{25,17},{2,10},{10... | collective-permute-start | bytes 98312 | tf_op jit(solution)/shard_map/ppermute | solution.py:275
  16.9 2.2 %copy-start = (bf16[8,2,512,256]{3,2,1,0:T(8,128)(2,1)S(1)}, bf16[8,2,512,256]{3,2,1,0:T(8,128)(2,1)}, u32[]{:S(2)}) copy-start(bf16[8,2,512,256]{3,2,1,0:T(8,128)(2,1)} %refs_4_.3) | copy-start | bytes 12582916
  19.1 0.8 %copy-start.2 = (bf16[64,512]{1,0:T(8,128)(2,1)S(1)}, bf16[64,512]{1,0:T(8,128)(2,1)}, u32[]{:S(2)}) copy-start(bf16[64,512]{1,0:T(8,128)(2,1)} %shard_map.55.refs_0_) | copy-start | bytes 196612
  20.0 18.4 %copy-start.1 = (bf16[8,2,512,256]{3,2,1,0:T(8,128)(2,1)S(1)}, bf16[8,2,512,256]{3,2,1,0:T(8,128)(2,1)}, u32[]{:S(2)}) copy-start(bf16[8,2,512,256]{3,2,1,0:T(8,128)(2,1)} %refs_4_.3) | copy-start | bytes 12582916
  21.4 9.9 %collective-permute-start.7 = (bf16[128,256]{1,0:T(8,128)(2,1)S(1)}, bf16[128,256]{1,0:T(8,128)(2,1)S(1)}, u32[]{:S(2)}, u32[]{:S(2)}) collective-permute-start(bf16[128,256]{1,0:T(8,128)(2,1)S(1)} %get-tuple-element.23), channel_id=1, source_target_pairs={{0,8},{8,0},{16,24},{24,16},{1,9},{9,1},{17,25},{25,17},{2,10},{10... | collective-permute-start | bytes 196616 | tf_op jit(solution)/shard_map/ppermute | solution.py:275
  22.2 9.1 %collective-permute-start.8 = (bf16[128,256]{1,0:T(8,128)(2,1)S(1)}, bf16[128,256]{1,0:T(8,128)(2,1)S(1)}, u32[]{:S(2)}, u32[]{:S(2)}) collective-permute-start(bf16[128,256]{1,0:T(8,128)(2,1)S(1)} %get-tuple-element.24), channel_id=1, source_target_pairs={{0,16},{8,24},{16,0},{24,8},{1,17},{9,25},{17,1},{25,9},{2,18},{10... | collective-permute-start | bytes 196616 | tf_op jit(solution)/shard_map/ppermute | solution.py:275
  23.7 7.6 %collective-permute-start.9 = (bf16[128,256]{1,0:T(8,128)(2,1)S(1)}, bf16[128,256]{1,0:T(8,128)(2,1)S(1)}, u32[]{:S(2)}, u32[]{:S(2)}) collective-permute-start(bf16[128,256]{1,0:T(8,128)(2,1)S(1)} %get-tuple-element.25), channel_id=1, source_target_pairs={{0,24},{8,16},{16,8},{24,0},{1,25},{9,17},{17,9},{25,1},{2,26},{10... | collective-permute-start | bytes 196616 | tf_op jit(solution)/shard_map/ppermute | solution.py:275
  24.9 4.7 %collective-permute-start.11 = (bf16[8,8,256]{2,1,0:T(8,128)(2,1)S(1)}, bf16[8,8,256]{2,1,0:T(8,128)(2,1)S(1)}, u32[]{:S(2)}, u32[]{:S(2)}) collective-permute-start(bf16[8,8,256]{2,1,0:T(8,128)(2,1)S(1)} %get-tuple-element.28), channel_id=1, source_target_pairs={{0,16},{8,24},{16,0},{24,8},{1,17},{9,25},{17,1},{25,9},{2,18},{10... | collective-permute-start | bytes 98312 | tf_op jit(solution)/shard_map/ppermute | solution.py:275
  26.4 4.8 %collective-permute-start.12 = (bf16[8,8,256]{2,1,0:T(8,128)(2,1)S(1)}, bf16[8,8,256]{2,1,0:T(8,128)(2,1)S(1)}, u32[]{:S(2)}, u32[]{:S(2)}) collective-permute-start(bf16[8,8,256]{2,1,0:T(8,128)(2,1)S(1)} %get-tuple-element.29), channel_id=1, source_target_pairs={{0,24},{8,16},{16,8},{24,0},{1,25},{9,17},{17,9},{25,1},{2,26},{10... | collective-permute-start | bytes 98312 | tf_op jit(solution)/shard_map/ppermute | solution.py:275
  31.9 4.3 %collective-permute-start.13 = (bf16[128,256]{1,0:T(8,128)(2,1)S(1)}, bf16[128,256]{1,0:T(8,128)(2,1)S(1)}, u32[]{:S(2)}, u32[]{:S(2)}) collective-permute-start(bf16[128,256]{1,0:T(8,128)(2,1)S(1)} %get-tuple-element.31), channel_id=1, source_target_pairs={{0,8},{8,0},{16,24},{24,16},{1,9},{9,1},{17,25},{25,17},{2,10},{10... | collective-permute-start | bytes 196616 | tf_op jit(solution)/shard_map/ppermute | solution.py:275
  32.7 4.3 %collective-permute-start.14 = (bf16[128,256]{1,0:T(8,128)(2,1)S(1)}, bf16[128,256]{1,0:T(8,128)(2,1)S(1)}, u32[]{:S(2)}, u32[]{:S(2)}) collective-permute-start(bf16[128,256]{1,0:T(8,128)(2,1)S(1)} %get-tuple-element.32), channel_id=1, source_target_pairs={{0,16},{8,24},{16,0},{24,8},{1,17},{9,25},{17,1},{25,9},{2,18},{10... | collective-permute-start | bytes 196616 | tf_op jit(solution)/shard_map/ppermute | solution.py:275
  33.2 5.2 %collective-permute-start.15 = (bf16[128,256]{1,0:T(8,128)(2,1)S(1)}, bf16[128,256]{1,0:T(8,128)(2,1)S(1)}, u32[]{:S(2)}, u32[]{:S(2)}) collective-permute-start(bf16[128,256]{1,0:T(8,128)(2,1)S(1)} %get-tuple-element.33), channel_id=1, source_target_pairs={{0,24},{8,16},{16,8},{24,0},{1,25},{9,17},{17,9},{25,1},{2,26},{10... | collective-permute-start | bytes 196616 | tf_op jit(solution)/shard_map/ppermute | solution.py:275
  39.6 1.6 %collective-permute-start.16 = (bf16[4,64,512]{2,1,0:T(8,128)(2,1)S(1)}, bf16[4,64,512]{2,1,0:T(8,128)(2,1)S(1)}, u32[]{:S(2)}, u32[]{:S(2)}) collective-permute-start(bf16[4,64,512]{2,1,0:T(8,128)(2,1)S(1)} %shard_map.60), channel_id=1, source_target_pairs={{0,1},{1,0},{2,3},{3,2},{4,5},{5,4},{6,7},{7,6},{8,9},{9,8},{10,11... | collective-permute-start | bytes 786440 | tf_op jit(solution)/shard_map/ppermute | solution.py:275
  41.2 4.5 %collective-permute-start.17 = (bf16[64,512]{1,0:T(8,128)(2,1)S(1)}, bf16[64,512]{1,0:T(8,128)(2,1)S(1)}, u32[]{:S(2)}, u32[]{:S(2)}) collective-permute-start(bf16[64,512]{1,0:T(8,128)(2,1)S(1)} %get-tuple-element.35), channel_id=1, source_target_pairs={{0,2},{1,3},{2,0},{3,1},{4,6},{5,7},{6,4},{7,5},{8,10},{9,11},{10,... | collective-permute-start | bytes 196616 | tf_op jit(solution)/shard_map/ppermute | solution.py:275
  42.2 7.6 %collective-permute-start.18 = (bf16[64,512]{1,0:T(8,128)(2,1)S(1)}, bf16[64,512]{1,0:T(8,128)(2,1)S(1)}, u32[]{:S(2)}, u32[]{:S(2)}) collective-permute-start(bf16[64,512]{1,0:T(8,128)(2,1)S(1)} %get-tuple-element.36), channel_id=1, source_target_pairs={{0,4},{1,5},{2,6},{3,7},{4,0},{5,1},{6,2},{7,3},{8,12},{9,13},{10,... | collective-permute-start | bytes 196616 | tf_op jit(solution)/shard_map/ppermute | solution.py:275
  44.5 6.2 %collective-permute-start.19 = (bf16[64,512]{1,0:T(8,128)(2,1)S(1)}, bf16[64,512]{1,0:T(8,128)(2,1)S(1)}, u32[]{:S(2)}, u32[]{:S(2)}) collective-permute-start(bf16[64,512]{1,0:T(8,128)(2,1)S(1)} %get-tuple-element.37), channel_id=1, source_target_pairs={{0,6},{1,7},{2,4},{3,5},{4,2},{5,3},{6,0},{7,1},{8,14},{9,15},{10,... | collective-permute-start | bytes 196616 | tf_op jit(solution)/shard_map/ppermute | solution.py:275

commit v2 on v1

--- a/solution.py
+++ b/solution.py
@@ -76,12 +76,12 @@
     return pltpu.VMEM((lanes // LANES, rows, LANES), F32)
 
 
-def call(kernel, out_shape, n_in, scratch=(), limit=24, flops=0, size=0):
-    whole = pl.BlockSpec(memory_space=pltpu.VMEM)
+def call(kernel, out_shape, n_in, scratch=(), limit=24, flops=0, size=0, unread=0):
+    whole, anywhere = pl.BlockSpec(memory_space=pltpu.VMEM), pl.BlockSpec(memory_space=pl.ANY)
     return pl.pallas_call(
         kernel,
         out_shape=out_shape,
-        in_specs=[whole] * n_in,
+        in_specs=[whole] * n_in + [anywhere] * unread,
         out_specs=jax.tree.map(lambda _: whole, out_shape),
         scratch_shapes=list(scratch),
         compiler_params=pltpu.CompilerParams(vmem_limit_bytes=limit * MIB),
@@ -89,21 +89,29 @@
     )
 
 
-def edge_kernel(per_block, orb_ref, out_ref):
-    group = orb_ref.shape[0]
+def edge_kernel(per_block, orb_hbm, edge_ref, orb_ref, sems):
+    local_k = orb_hbm.shape[0]
+    copies = [pltpu.make_async_copy(orb_hbm.at[k], orb_ref.at[k], sems.at[k]) for k in range(local_k)]
+    for copy in copies:
+        copy.start()
     row = lax.broadcasted_iota(jnp.int32, (2 * per_block, LANES), 0)
     lane = lax.broadcasted_iota(jnp.int32, (2 * per_block, LANES), 1)
-    first = jnp.where(row < per_block, (row == lane).astype(F32), 0.0).astype(BF16)
-    second = jnp.where(row >= per_block, (row - per_block == lane).astype(F32), 0.0).astype(BF16)
-    rows = []
-    for k in range(group):
-        rows.append(
-            dot(first, orb_ref[k, 0], ((1,), (1,))) + dot(second, orb_ref[k, 1], ((1,), (1,)))
-        )
-    out_ref[...] = jnp.concatenate(rows, axis=0).astype(BF16)
-
-
-def coulomb_kernel(shares, coulomb_ref, *refs):
+    one, zero = jnp.ones(row.shape, F32), jnp.zeros(row.shape, F32)
+    first = jnp.where((row < per_block) & (row == lane), one, zero).astype(BF16)
+    second = jnp.where((row >= per_block) & (row == lane + per_block), one, zero).astype(BF16)
+    group = ROWS // (2 * per_block)
+    for g in range(local_k // group):
+        rows = []
+        for k in range(g * group, (g + 1) * group):
+            copies[k].wait()
+            rows.append(
+                dot(first, orb_ref[k, 0, :, :LANES], ((1,), (1,)))
+                + dot(second, orb_ref[k, 1, :, :LANES], ((1,), (1,)))
+            )
+        edge_ref[g * ROWS : (g + 1) * ROWS] = jnp.concatenate(rows, axis=0).astype(BF16)
+
+
+def coulomb_kernel(shares, coulomb_ref, _, *refs):
     outs, wide = refs[:shares], refs[shares]
     cells, columns, points = coulomb_ref.shape
     share = columns // shares
@@ -118,8 +126,9 @@
 
 def tile_kernel(shares, blocks, per_block, *refs):
     edges, orb_ref, sel_ref = refs[:blocks], refs[blocks], refs[blocks + 1]
-    outs = refs[blocks + 2 : blocks + 2 + shares]
-    form_ref, gathered, wide = refs[blocks + 2 + shares :]
+    refs = refs[blocks + 2 + shares - 1 :]
+    outs = refs[:shares]
+    form_ref, gathered, wide = refs[shares:]
     local_k, _, norb, points = orb_ref.shape
     group = ROWS // (2 * per_block)
     total = blocks * per_block
@@ -235,7 +244,8 @@
 
 
 def exchange_kernel(chunks, scale, *refs):
-    pieces, form_ref, out_ref, wide = refs[:chunks], refs[chunks], refs[chunks + 1], refs[chunks + 2]
+    pieces, form_ref, out_hbm = refs[:chunks], refs[chunks], refs[chunks + 1]
+    wide, out_ref, sems = refs[chunks + 2 :]
     local_k, lanes, twice = form_ref.shape
     norb = twice // 2
     out_rows = pieces[0].shape[0]
@@ -265,9 +275,18 @@
             for part in range(2):
                 value = result[kk * out_rows : (kk + 1) * out_rows, part * norb : (part + 1) * norb]
                 spread(wide, 2 * k + part, 2 * local_k, value)
-    for t in range(norb // LANES):
-        value = wide[t].astype(BF16).reshape(out_rows, local_k, 2, LANES)
-        out_ref[:, :, :, t * LANES : (t + 1) * LANES] = value
+    steps = sems.shape[0]
+    step = out_rows // steps
+    copies = []
+    for i in range(steps):
+        rows = pl.ds(i * step, step)
+        for t in range(norb // LANES):
+            value = wide[t, i * step * 2 * local_k : (i + 1) * step * 2 * local_k].astype(BF16)
+            out_ref[rows, :, :, t * LANES : (t + 1) * LANES] = value.reshape(step, local_k, 2, LANES)
+        copies.append(pltpu.make_async_copy(out_ref.at[rows], out_hbm.at[rows], sems.at[i]))
+        copies[-1].start()
+    for copy in copies:
+        copy.wait()
 
 
 def swap(value, axis, mask):
@@ -287,13 +306,15 @@
     group = ROWS // (2 * per_block)
     shape = jax.ShapeDtypeStruct
 
-    edge = pl.pallas_call(
+    vmem, anywhere = pl.BlockSpec(memory_space=pltpu.VMEM), pl.BlockSpec(memory_space=pl.ANY)
+    edge, orbitals = pl.pallas_call(
         functools.partial(edge_kernel, per_block),
-        out_shape=shape((local_k * 2 * per_block, norb), BF16),
-        grid=(local_k // group,),
-        in_specs=[pl.BlockSpec((group, 2, norb, LANES), lambda g: (g, 0, 0, 0))],
-        out_specs=pl.BlockSpec((ROWS, norb), lambda g: (g, 0)),
-        cost_estimate=pl.CostEstimate(flops=0, bytes_accessed=2 * MIB, transcendentals=0),
+        out_shape=[shape((local_k * 2 * per_block, norb), BF16), shape(orbitals.shape, BF16)],
+        in_specs=[pl.BlockSpec(memory_space=pltpu.HBM)],
+        out_specs=[vmem, vmem],
+        scratch_shapes=[pltpu.SemaphoreType.DMA((local_k,))],
+        compiler_params=pltpu.CompilerParams(vmem_limit_bytes=57 * MIB),
+        cost_estimate=pl.CostEstimate(flops=0, bytes_accessed=8 * MIB, transcendentals=0),
     )(orbitals)
     edges = [edge] + [None] * (blocks - 1)
     for s in range(1, chunks):
@@ -307,7 +328,8 @@
         1,
         [pltpu.VMEM((local_k, columns, points), F32)],
         size=2 * MIB,
-    )(coulomb)
+        unread=1,
+    )(coulomb, edges[1])
     coulombs = [own[0]] + [swap(own[s], "ka", s) for s in range(1, shares)]
 
     selector = jnp.asarray(column_selector(group, blocks, per_block, shares))
@@ -321,7 +343,8 @@
             tiled(columns * 2 * local_k, points),
         ],
         size=8 * MIB,
-    )(*edges, orbitals, selector)
+        unread=shares - 1,
+    )(*edges, orbitals, selector, *coulombs[1:])
     tiles = [tiles[0]] + [swap(tiles[s], "ka", s) for s in range(1, shares)]
 
     forward, backward = phase_tables(total)
@@ -358,12 +381,18 @@
         size=1 * MIB,
     )(halves[1], came)
     sums = [own_sum] + [swap(sums[s - 1], "pts", 2 * s) for s in range(1, chunks)]
-    return call(
+    return pl.pallas_call(
         functools.partial(exchange_kernel, chunks, 1.0 / math.sqrt(points * blocks)),
-        shape((out_rows, local_k, 2, norb), BF16),
-        chunks + 1,
-        [tiled(out_rows * 2 * local_k, norb)],
-        size=4 * MIB,
+        out_shape=shape((out_rows, local_k, 2, norb), BF16),
+        in_specs=[vmem] * (chunks + 1),
+        out_specs=pl.BlockSpec(memory_space=pltpu.HBM),
+        scratch_shapes=[
+            tiled(out_rows * 2 * local_k, norb),
+            pltpu.VMEM((out_rows, local_k, 2, norb), BF16),
+            pltpu.SemaphoreType.DMA((4,)),
+        ],
+        compiler_params=pltpu.CompilerParams(vmem_limit_bytes=24 * MIB),
+        cost_estimate=pl.CostEstimate(flops=0, bytes_accessed=4 * MIB, transcendentals=0),
     )(*sums, forms)
 
 

time: 53.7 us -> 57.7 us (1.074)
  waiting for transfers between devices: 17.7 us -> 19.9 us
  starting transfers between devices: 21.6 us -> 22.7 us
  Pallas kernels: 11.1 us -> 11.9 us
    ppermute x20, waiting for transfers between devices: 17.7 us -> 19.9 us  [swap(): return lax.ppermute(value, axis, [(i, i ^ mask) for i in range(size)])]
    ppermute x20, starting transfers between devices: 21.6 us -> 22.7 us  [swap(): return lax.ppermute(value, axis, [(i, i ^ mask) for i in range(size)])]
    pallas_call x2, Pallas kernels: 6.69 us -> 7.5 us  [the longest x1 4.46 us: body(): pl.pallas_call(functools.partial(edge_kernel, per_block), out_shape=[shap...]
  transfers between devices with their start and end apart: 20 -> 20, of which waited for: 10 -> 14; matrix products, arithmetic and copies ran while one was open for 0% -> 0% of each run, Pallas kernels for 5% -> 2%
where the time goes in v2:
time: 57.7 us; the launch traced here: 57.5 us
  starting transfers between devices  22.7 us (39%)
  waiting for transfers between devices  19.9 us (34%)
  Pallas kernels  11.9 us (21%)
  local copies, waits for them, and re-layouts  3.04 us (5%)
    ppermute x20, starting transfers between devices, swap(): return lax.ppermute(value, axis, [(i, i ^ mask) for i in range(size)])  22.7 us
    ppermute x20, waiting for transfers between devices, swap(): return lax.ppermute(value, axis, [(i, i ^ mask) for i in range(size)])  19.9 us
    pallas_call x1, Pallas kernels, body(): pl.pallas_call(functools.partial(edge_kernel, per_block), out_shape=[shap...  4.46 us
    unnamed x14, local copies, waits for them, and re-layouts  3.04 us
    pallas_call x1, Pallas kernels, body(): pl.pallas_call(functools.partial(exchange_kernel, chunks, 1.0 / math.sqrt...  3.04 us
    pallas_call x2, Pallas kernels, body(): call(functools.partial(weight_kernel, shares, flip, out_rows), shape((chu...  2.33 us
    pallas_call x1, Pallas kernels, body(): call(functools.partial(tile_kernel, shares, blocks, per_block), [piece] *...  1.38 us
  transfers between devices with their start and end apart: 20, of which 14 were waited for; matrix products, arithmetic and copies ran while one was open for 0% of the time, Pallas kernels for 2%

profile of v2, /device:TPU:0, one launch (start us, length us, event | category | flops | bytes accessed | tf_op | source)
XLA Modules:
  0.0 57.5 jit_solution(15995613605985511917)
XLA Ops:
  0.0 4.5 %shard_map.55 = (bf16[64,512]{1,0:T(8,128)(2,1)}, bf16[8,2,512,256]{3,2,1,0:T(8,128)(2,1)}) custom-call(bf16[8,2,512,256]{3,2,1,0:T(8,128)(2,1)} %orb_hbm.1), custom_call_target="tpu_custom_call" | custom-call | bytes 8388608 | tf_op jit(solution)/shard_map/pallas_call | solution.py:310
  5.0 4.7 %collective-permute-start.5 = (bf16[64,512]{1,0:T(8,128)(2,1)}, bf16[64,512]{1,0:T(8,128)(2,1)S(1)}, u32[]{:S(2)}, u32[]{:S(2)}) collective-permute-start(bf16[64,512]{1,0:T(8,128)(2,1)} %get-tuple-element.24.refs_0_), channel_id=1, source_target_pairs={{0,6},{1,7},{2,4},{3,5},{4,2},{5,3},{6,0},{7,1},{8,14},{9,15},{10,... | collective-permute-start | bytes 196616 | tf_op jit(solution)/shard_map/ppermute | solution.py:294
  9.7 0.7 %collective-permute-start.1 = (bf16[64,512]{1,0:T(8,128)(2,1)}, bf16[64,512]{1,0:T(8,128)(2,1)S(1)}, u32[]{:S(2)}, u32[]{:S(2)}) collective-permute-start(bf16[64,512]{1,0:T(8,128)(2,1)} %get-tuple-element.24.refs_0_), channel_id=1, source_target_pairs={{0,2},{1,3},{2,0},{3,1},{4,6},{5,7},{6,4},{7,5},{8,10},{9,11},{10,... | collective-permute-start | bytes 196616 | tf_op jit(solution)/shard_map/ppermute | solution.py:294
  10.4 1.7 %collective-permute-start.7 = (bf16[8,8,256]{2,1,0:T(8,128)(2,1)S(1)}, bf16[8,8,256]{2,1,0:T(8,128)(2,1)S(1)}, u32[]{:S(2)}, u32[]{:S(2)}) collective-permute-start(bf16[8,8,256]{2,1,0:T(8,128)(2,1)S(1)} %get-tuple-element.26), channel_id=1, source_target_pairs={{0,8},{8,0},{16,24},{24,16},{1,9},{9,1},{17,25},{25,17},{2,10},{10... | collective-permute-start | bytes 98312 | tf_op jit(solution)/shard_map/ppermute | solution.py:294
  12.1 0.7 %collective-permute-done.5.refs_6_ = bf16[64,512]{1,0:T(8,128)(2,1)S(1)} collective-permute-done((bf16[64,512]{1,0:T(8,128)(2,1)}, bf16[64,512]{1,0:T(8,128)(2,1)S(1)}, u32[]{:S(2)}, u32[]{:S(2)}) %collective-permute-start.5) | collective-permute-done | bytes 65568 | tf_op jit(solution)/shard_map/ppermute | solution.py:294
  12.8 3.2 %collective-permute-done.3.refs_4_ = bf16[64,512]{1,0:T(8,128)(2,1)S(1)} collective-permute-done((bf16[64,512]{1,0:T(8,128)(2,1)}, bf16[64,512]{1,0:T(8,128)(2,1)S(1)}, u32[]{:S(2)}, u32[]{:S(2)}) %collective-permute-start.3) | collective-permute-done | bytes 65568 | tf_op jit(solution)/shard_map/ppermute | solution.py:294
  16.5 1.5 %collective-permute-start.8 = (bf16[8,8,256]{2,1,0:T(8,128)(2,1)S(1)}, bf16[8,8,256]{2,1,0:T(8,128)(2,1)S(1)}, u32[]{:S(2)}, u32[]{:S(2)}) collective-permute-start(bf16[8,8,256]{2,1,0:T(8,128)(2,1)S(1)} %get-tuple-element.27), channel_id=1, source_target_pairs={{0,16},{8,24},{16,0},{24,8},{1,17},{9,25},{17,1},{25,9},{2,18},{10... | collective-permute-start | bytes 98312 | tf_op jit(solution)/shard_map/ppermute | solution.py:294
  18.0 1.4 %collective-permute-start.9 = (bf16[8,8,256]{2,1,0:T(8,128)(2,1)S(1)}, bf16[8,8,256]{2,1,0:T(8,128)(2,1)S(1)}, u32[]{:S(2)}, u32[]{:S(2)}) collective-permute-start(bf16[8,8,256]{2,1,0:T(8,128)(2,1)S(1)} %get-tuple-element.28), channel_id=1, source_target_pairs={{0,24},{8,16},{16,8},{24,0},{1,25},{9,17},{17,9},{25,1},{2,26},{10... | collective-permute-start | bytes 98312 | tf_op jit(solution)/shard_map/ppermute | solution.py:294
  19.4 1.0 %collective-permute-done.8.refs_11_.refs_6_ = bf16[8,8,256]{2,1,0:T(8,128)(2,1)S(1)} collective-permute-done((bf16[8,8,256]{2,1,0:T(8,128)(2,1)S(1)}, bf16[8,8,256]{2,1,0:T(8,128)(2,1)S(1)}, u32[]{:S(2)}, u32[]{:S(2)}) %collective-permute-start.8) | collective-permute-done | bytes 32800 | tf_op jit(solution)/shard_map/ppermute | solution.py:294
  20.4 2.4 %collective-permute-done.9.refs_12_.refs_7_ = bf16[8,8,256]{2,1,0:T(8,128)(2,1)S(1)} collective-permute-done((bf16[8,8,256]{2,1,0:T(8,128)(2,1)S(1)}, bf16[8,8,256]{2,1,0:T(8,128)(2,1)S(1)}, u32[]{:S(2)}, u32[]{:S(2)}) %collective-permute-start.9) | collective-permute-done | bytes 32800 | tf_op jit(solution)/shard_map/ppermute | solution.py:294
  22.9 2.2 %copy-done = bf16[8,2,512,256]{3,2,1,0:T(8,128)(2,1)S(1)} copy-done((bf16[8,2,512,256]{3,2,1,0:T(8,128)(2,1)S(1)}, bf16[8,2,512,256]{3,2,1,0:T(8,128)(2,1)}, u32[]{:S(2)}) %copy-start) | copy-done | bytes 4194328
  25.0 0.8 %copy-done.4 = bf16[64,512]{1,0:T(8,128)(2,1)S(1)} copy-done((bf16[64,512]{1,0:T(8,128)(2,1)S(1)}, bf16[64,512]{1,0:T(8,128)(2,1)}, u32[]{:S(2)}) %copy-start.4) | copy-done | bytes 65560
  25.9 1.4 %shard_map.57 = (bf16[128,256]{1,0:T(8,128)(2,1)S(1)}, bf16[128,256]{1,0:T(8,128)(2,1)S(1)}, bf16[128,256]{1,0:T(8,128)(2,1)S(1)}, bf16[128,256]{1,0:T(8,128)(2,1)S(1)}, bf16[8,64,1024]{2,1,0:T(8,128)(2,1)S(1)}) custom-call(bf16[64,512]{1,0:T(8,128)(2,1)S(1)} %copy-done.4, bf16[64,512]{1,0:T(8,128)(2,1)S(1)} %collective-permute-done._.refs_1_, ...), custom_call_target="tpu_custom_call" | custom-call | bytes 8388608 | tf_op jit(solution)/shard_map/pallas_call | solution.py:337
  27.3 1.6 %collective-permute-start.10 = (bf16[128,256]{1,0:T(8,128)(2,1)S(1)}, bf16[128,256]{1,0:T(8,128)(2,1)S(1)}, u32[]{:S(2)}, u32[]{:S(2)}) collective-permute-start(bf16[128,256]{1,0:T(8,128)(2,1)S(1)} %get-tuple-element.30), channel_id=1, source_target_pairs={{0,8},{8,0},{16,24},{24,16},{1,9},{9,1},{17,25},{25,17},{2,10},{10... | collective-permute-start | bytes 196616 | tf_op jit(solution)/shard_map/ppermute | solution.py:294
  29.3 1.5 %collective-permute-start.12 = (bf16[128,256]{1,0:T(8,128)(2,1)S(1)}, bf16[128,256]{1,0:T(8,128)(2,1)S(1)}, u32[]{:S(2)}, u32[]{:S(2)}) collective-permute-start(bf16[128,256]{1,0:T(8,128)(2,1)S(1)} %get-tuple-element.32), channel_id=1, source_target_pairs={{0,24},{8,16},{16,8},{24,0},{1,25},{9,17},{17,9},{25,1},{2,26},{10... | collective-permute-start | bytes 196616 | tf_op jit(solution)/shard_map/ppermute | solution.py:294
  30.8 1.5 %collective-permute-done.10.refs_1_ = bf16[128,256]{1,0:T(8,128)(2,1)S(1)} collective-permute-done((bf16[128,256]{1,0:T(8,128)(2,1)S(1)}, bf16[128,256]{1,0:T(8,128)(2,1)S(1)}, u32[]{:S(2)}, u32[]{:S(2)}) %collective-permute-start.10) | collective-permute-done | bytes 65568 | tf_op jit(solution)/shard_map/ppermute | solution.py:294
  32.3 0.8 %collective-permute-done.11.refs_2_ = bf16[128,256]{1,0:T(8,128)(2,1)S(1)} collective-permute-done((bf16[128,256]{1,0:T(8,128)(2,1)S(1)}, bf16[128,256]{1,0:T(8,128)(2,1)S(1)}, u32[]{:S(2)}, u32[]{:S(2)}) %collective-permute-start.11) | collective-permute-done | bytes 65568 | tf_op jit(solution)/shard_map/ppermute | solution.py:294
  33.1 1.4 %collective-permute-done.12.refs_3_ = bf16[128,256]{1,0:T(8,128)(2,1)S(1)} collective-permute-done((bf16[128,256]{1,0:T(8,128)(2,1)S(1)}, bf16[128,256]{1,0:T(8,128)(2,1)S(1)}, u32[]{:S(2)}, u32[]{:S(2)}) %collective-permute-start.12) | collective-permute-done | bytes 65568 | tf_op jit(solution)/shard_map/ppermute | solution.py:294
  34.5 0.6 %shard_map.58 = (bf16[128,256]{1,0:T(8,128)(2,1)S(1)}, bf16[128,256]{1,0:T(8,128)(2,1)S(1)}, bf16[128,256]{1,0:T(8,128)(2,1)S(1)}, bf16[128,256]{1,0:T(8,128)(2,1)S(1)}) custom-call(bf16[128,256]{1,0:T(8,128)(2,1)S(1)} %get-tuple-element.29.refs_0_, bf16[128,256]{1,0:T(8,128)(2,1)S(1)} %collective-permute-done.10.refs_1_, ...), custom_call_target="tpu_custom_call" | custom-call | bytes 2097152 | tf_op jit(solution)/shard_map/pallas_call | solution.py:351
  35.1 0.6 %collective-permute-start.13 = (bf16[128,256]{1,0:T(8,128)(2,1)S(1)}, bf16[128,256]{1,0:T(8,128)(2,1)S(1)}, u32[]{:S(2)}, u32[]{:S(2)}) collective-permute-start(bf16[128,256]{1,0:T(8,128)(2,1)S(1)} %get-tuple-element.35), channel_id=1, source_target_pairs={{0,8},{8,0},{16,24},{24,16},{1,9},{9,1},{17,25},{25,17},{2,10},{10... | collective-permute-start | bytes 196616 | tf_op jit(solution)/shard_map/ppermute | solution.py:294
  35.7 1.5 %collective-permute-start.14 = (bf16[128,256]{1,0:T(8,128)(2,1)S(1)}, bf16[128,256]{1,0:T(8,128)(2,1)S(1)}, u32[]{:S(2)}, u32[]{:S(2)}) collective-permute-start(bf16[128,256]{1,0:T(8,128)(2,1)S(1)} %get-tuple-element.36), channel_id=1, source_target_pairs={{0,16},{8,24},{16,0},{24,8},{1,17},{9,25},{17,1},{25,9},{2,18},{10... | collective-permute-start | bytes 196616 | tf_op jit(solution)/shard_map/ppermute | solution.py:294
  37.2 1.4 %collective-permute-start.15 = (bf16[128,256]{1,0:T(8,128)(2,1)S(1)}, bf16[128,256]{1,0:T(8,128)(2,1)S(1)}, u32[]{:S(2)}, u32[]{:S(2)}) collective-permute-start(bf16[128,256]{1,0:T(8,128)(2,1)S(1)} %get-tuple-element.37), channel_id=1, source_target_pairs={{0,24},{8,16},{16,8},{24,0},{1,25},{9,17},{17,9},{25,1},{2,26},{10... | collective-permute-start | bytes 196616 | tf_op jit(solution)/shard_map/ppermute | solution.py:294
  38.7 0.8 %collective-permute-done.13.refs_1_ = bf16[128,256]{1,0:T(8,128)(2,1)S(1)} collective-permute-done((bf16[128,256]{1,0:T(8,128)(2,1)S(1)}, bf16[128,256]{1,0:T(8,128)(2,1)S(1)}, u32[]{:S(2)}, u32[]{:S(2)}) %collective-permute-start.13) | collective-permute-done | bytes 65568 | tf_op jit(solution)/shard_map/ppermute | solution.py:294
  40.0 2.4 %collective-permute-done.15.refs_3_ = bf16[128,256]{1,0:T(8,128)(2,1)S(1)} collective-permute-done((bf16[128,256]{1,0:T(8,128)(2,1)S(1)}, bf16[128,256]{1,0:T(8,128)(2,1)S(1)}, u32[]{:S(2)}, u32[]{:S(2)}) %collective-permute-start.15) | collective-permute-done | bytes 65568 | tf_op jit(solution)/shard_map/ppermute | solution.py:294
  42.4 1.2 %shard_map.60 = bf16[4,64,512]{2,1,0:T(8,128)(2,1)S(1)} custom-call(bf16[128,256]{1,0:T(8,128)(2,1)S(1)} %get-tuple-element.34.refs_0_, bf16[128,256]{1,0:T(8,128)(2,1)S(1)} %collective-permute-done.13.refs_1_, bf16[128,256]{1,0:T(8,128)(2,1)S(1)} %collective-permute-done.14.refs_2_, bf16[128,256]{1,0:T(8,128)(2,1)S(1)} %collective-permute-done.15.refs_3_, ...), custom_call_target="tpu_custom_call" | custom-call | bytes 6291456 | tf_op jit(solution)/shard_map/pallas_call | solution.py:368
  43.6 1.2 %shard_map.59.keep_ref = f32[4,64,512]{2,1,0:T(8,128)S(1)} custom-call(bf16[128,256]{1,0:T(8,128)(2,1)S(1)} %get-tuple-element.34.refs_0_, bf16[128,256]{1,0:T(8,128)(2,1)S(1)} %collective-permute-done.13.refs_1_, bf16[128,256]{1,0:T(8,128)(2,1)S(1)} %collective-permute-done.14.refs_2_, bf16[128,256]{1,0:T(8,128)(2,1)S(1)} %collective-permute-done.15.refs_3_, ...), custom_call_target="tpu_custom_call" | custom-call | bytes 6291456 | tf_op jit(solution)/shard_map/pallas_call | solution.py:368
  45.2 0.8 %collective-permute-start.17 = (bf16[64,512]{1,0:T(8,128)(2,1)S(1)}, bf16[64,512]{1,0:T(8,128)(2,1)S(1)}, u32[]{:S(2)}, u32[]{:S(2)}) collective-permute-start(bf16[64,512]{1,0:T(8,128)(2,1)S(1)} %get-tuple-element.39), channel_id=1, source_target_pairs={{0,2},{1,3},{2,0},{3,1},{4,6},{5,7},{6,4},{7,5},{8,10},{9,11},{10,... | collective-permute-start | bytes 196616 | tf_op jit(solution)/shard_map/ppermute | solution.py:294
  46.0 2.3 %collective-permute-start.18 = (bf16[64,512]{1,0:T(8,128)(2,1)S(1)}, bf16[64,512]{1,0:T(8,128)(2,1)S(1)}, u32[]{:S(2)}, u32[]{:S(2)}) collective-permute-start(bf16[64,512]{1,0:T(8,128)(2,1)S(1)} %get-tuple-element.40), channel_id=1, source_target_pairs={{0,4},{1,5},{2,6},{3,7},{4,0},{5,1},{6,2},{7,3},{8,12},{9,13},{10,... | collective-permute-start | bytes 196616 | tf_op jit(solution)/shard_map/ppermute | solution.py:294
  48.3 1.3 %collective-permute-start.19 = (bf16[64,512]{1,0:T(8,128)(2,1)S(1)}, bf16[64,512]{1,0:T(8,128)(2,1)S(1)}, u32[]{:S(2)}, u32[]{:S(2)}) collective-permute-start(bf16[64,512]{1,0:T(8,128)(2,1)S(1)} %get-tuple-element.41), channel_id=1, source_target_pairs={{0,6},{1,7},{2,4},{3,5},{4,2},{5,3},{6,0},{7,1},{8,14},{9,15},{10,... | collective-permute-start | bytes 196616 | tf_op jit(solution)/shard_map/ppermute | solution.py:294
  50.2 3.5 %collective-permute-done.18.refs_2_ = bf16[64,512]{1,0:T(8,128)(2,1)S(1)} collective-permute-done((bf16[64,512]{1,0:T(8,128)(2,1)S(1)}, bf16[64,512]{1,0:T(8,128)(2,1)S(1)}, u32[]{:S(2)}, u32[]{:S(2)}) %collective-permute-start.18) | collective-permute-done | bytes 65568 | tf_op jit(solution)/shard_map/ppermute | solution.py:294
  53.7 0.8 %collective-permute-done.19.refs_3_ = bf16[64,512]{1,0:T(8,128)(2,1)S(1)} collective-permute-done((bf16[64,512]{1,0:T(8,128)(2,1)S(1)}, bf16[64,512]{1,0:T(8,128)(2,1)S(1)}, u32[]{:S(2)}, u32[]{:S(2)}) %collective-permute-start.19) | collective-permute-done | bytes 65568 | tf_op jit(solution)/shard_map/ppermute | solution.py:294
  54.5 3.0 %shard_map.62 = bf16[64,8,2,512]{3,2,1,0:T(2,128)(2,1)} custom-call(f32[64,512]{1,0:T(8,128)S(1)} %get-tuple-element.38.refs_0_, bf16[64,512]{1,0:T(8,128)(2,1)S(1)} %collective-permute-done.17.refs_1_, bf16[64,512]{1,0:T(8,128)(2,1)S(1)} %collective-permute-done.18.refs_2_, bf16[64,512]{1,0:T(8,128)(2,1)S(1)} %collective-permute-done.19.refs_3_, ...), custom_call_target="tpu_custom_call" | custom-call | bytes 4194304 | tf_op jit(solution)/shard_map/pallas_call | solution.py:384
  (30 shorter events, 3.2 us)
Async XLA Ops:
  0.0 22.8 %copy-start.3 = (bf16[256,128]{1,0:T(8,128)(2,1)S(1)}, bf16[256,128]{1,0:T(8,128)(2,1)}, u32[]{:S(2)}) copy-start(bf16[256,128]{1,0:T(8,128)(2,1)} %constant.6.clone.refs_9_) | copy-start | bytes 196612
  0.0 34.5 %copy-start.5 = (bf16[64,128]{1,0:T(8,128)(2,1)S(1)}, bf16[64,128]{1,0:T(8,128)(2,1)}, u32[]{:S(2)}) copy-start(bf16[64,128]{1,0:T(8,128)(2,1)} %constant.8.clone.refs_9_) | copy-start | bytes 49156
  0.0 34.5 %copy-start.6 = (bf16[64,128]{1,0:T(8,128)(2,1)S(1)}, bf16[64,128]{1,0:T(8,128)(2,1)}, u32[]{:S(2)}) copy-start(bf16[64,128]{1,0:T(8,128)(2,1)} %constant.7.clone.refs_8_) | copy-start | bytes 49156
  0.0 10.3 %copy-start.2 = (bf16[8,32,256]{2,1,0:T(8,128)(2,1)S(1)}, bf16[8,32,256]{2,1,0:T(8,128)(2,1)}, u32[]{:S(2)}) copy-start(bf16[8,32,256]{2,1,0:T(8,128)(2,1)} %coulomb_ref.1) | copy-start | bytes 393220
  4.5 5.9 %collective-permute-start = (bf16[64,512]{1,0:T(8,128)(2,1)}, bf16[64,512]{1,0:T(8,128)(2,1)S(1)}, u32[]{:S(2)}, u32[]{:S(2)}) collective-permute-start(bf16[64,512]{1,0:T(8,128)(2,1)} %get-tuple-element.24.refs_0_), channel_id=1, source_target_pairs={{0,1},{1,0},{2,3},{3,2},{4,5},{5,4},{6,7},{7,6},{8,9},{9,8},{10,11... | collective-permute-start | bytes 196616 | tf_op jit(solution)/shard_map/ppermute | solution.py:294
  5.0 7.7 %collective-permute-start.5 = (bf16[64,512]{1,0:T(8,128)(2,1)}, bf16[64,512]{1,0:T(8,128)(2,1)S(1)}, u32[]{:S(2)}, u32[]{:S(2)}) collective-permute-start(bf16[64,512]{1,0:T(8,128)(2,1)} %get-tuple-element.24.refs_0_), channel_id=1, source_target_pairs={{0,6},{1,7},{2,4},{3,5},{4,2},{5,3},{6,0},{7,1},{8,14},{9,15},{10,... | collective-permute-start | bytes 196616 | tf_op jit(solution)/shard_map/ppermute | solution.py:294
  9.7 6.3 %collective-permute-start.3 = (bf16[64,512]{1,0:T(8,128)(2,1)}, bf16[64,512]{1,0:T(8,128)(2,1)S(1)}, u32[]{:S(2)}, u32[]{:S(2)}) collective-permute-start(bf16[64,512]{1,0:T(8,128)(2,1)} %get-tuple-element.24.refs_0_), channel_id=1, source_target_pairs={{0,4},{1,5},{2,6},{3,7},{4,0},{5,1},{6,2},{7,3},{8,12},{9,13},{10,... | collective-permute-start | bytes 196616 | tf_op jit(solution)/shard_map/ppermute | solution.py:294
  9.7 6.3 %collective-permute-start.1 = (bf16[64,512]{1,0:T(8,128)(2,1)}, bf16[64,512]{1,0:T(8,128)(2,1)S(1)}, u32[]{:S(2)}, u32[]{:S(2)}) collective-permute-start(bf16[64,512]{1,0:T(8,128)(2,1)} %get-tuple-element.24.refs_0_), channel_id=1, source_target_pairs={{0,2},{1,3},{2,0},{3,1},{4,6},{5,7},{6,4},{7,5},{8,10},{9,11},{10,... | collective-permute-start | bytes 196616 | tf_op jit(solution)/shard_map/ppermute | solution.py:294
  10.4 7.6 %collective-permute-start.7 = (bf16[8,8,256]{2,1,0:T(8,128)(2,1)S(1)}, bf16[8,8,256]{2,1,0:T(8,128)(2,1)S(1)}, u32[]{:S(2)}, u32[]{:S(2)}) collective-permute-start(bf16[8,8,256]{2,1,0:T(8,128)(2,1)S(1)} %get-tuple-element.26), channel_id=1, source_target_pairs={{0,8},{8,0},{16,24},{24,16},{1,9},{9,1},{17,25},{25,17},{2,10},{10... | collective-permute-start | bytes 98312 | tf_op jit(solution)/shard_map/ppermute | solution.py:294
  12.8 10.1 %collective-permute-start.6 = (bf16[64,512]{1,0:T(8,128)(2,1)S(1)}, bf16[64,512]{1,0:T(8,128)(2,1)S(1)}, u32[]{:S(2)}, u32[]{:S(2)}) collective-permute-start(bf16[64,512]{1,0:T(8,128)(2,1)S(1)} %collective-permute-done.5.refs_6_), channel_id=1, source_target_pairs={{0,1},{1,0},{2,3},{3,2},{4,5},{5,4},{6,7},{7,6},{8,9},{9,8},{10,11... | collective-permute-start | bytes 196616 | tf_op jit(solution)/shard_map/ppermute | solution.py:294
  16.0 6.9 %collective-permute-start.4 = (bf16[64,512]{1,0:T(8,128)(2,1)S(1)}, bf16[64,512]{1,0:T(8,128)(2,1)S(1)}, u32[]{:S(2)}, u32[]{:S(2)}) collective-permute-start(bf16[64,512]{1,0:T(8,128)(2,1)S(1)} %collective-permute-done.3.refs_4_), channel_id=1, source_target_pairs={{0,1},{1,0},{2,3},{3,2},{4,5},{5,4},{6,7},{7,6},{8,9},{9,8},{10,11... | collective-permute-start | bytes 196616 | tf_op jit(solution)/shard_map/ppermute | solution.py:294
  16.0 6.9 %collective-permute-start.2 = (bf16[64,512]{1,0:T(8,128)(2,1)S(1)}, bf16[64,512]{1,0:T(8,128)(2,1)S(1)}, u32[]{:S(2)}, u32[]{:S(2)}) collective-permute-start(bf16[64,512]{1,0:T(8,128)(2,1)S(1)} %collective-permute-done.1.refs_2_), channel_id=1, source_target_pairs={{0,1},{1,0},{2,3},{3,2},{4,5},{5,4},{6,7},{7,6},{8,9},{9,8},{10,11... | collective-permute-start | bytes 196616 | tf_op jit(solution)/shard_map/ppermute | solution.py:294
  16.5 3.9 %collective-permute-start.8 = (bf16[8,8,256]{2,1,0:T(8,128)(2,1)S(1)}, bf16[8,8,256]{2,1,0:T(8,128)(2,1)S(1)}, u32[]{:S(2)}, u32[]{:S(2)}) collective-permute-start(bf16[8,8,256]{2,1,0:T(8,128)(2,1)S(1)} %get-tuple-element.27), channel_id=1, source_target_pairs={{0,16},{8,24},{16,0},{24,8},{1,17},{9,25},{17,1},{25,9},{2,18},{10... | collective-permute-start | bytes 98312 | tf_op jit(solution)/shard_map/ppermute | solution.py:294
  18.0 4.8 %collective-permute-start.9 = (bf16[8,8,256]{2,1,0:T(8,128)(2,1)S(1)}, bf16[8,8,256]{2,1,0:T(8,128)(2,1)S(1)}, u32[]{:S(2)}, u32[]{:S(2)}) collective-permute-start(bf16[8,8,256]{2,1,0:T(8,128)(2,1)S(1)} %get-tuple-element.28), channel_id=1, source_target_pairs={{0,24},{8,16},{16,8},{24,0},{1,25},{9,17},{17,9},{25,1},{2,26},{10... | collective-permute-start | bytes 98312 | tf_op jit(solution)/shard_map/ppermute | solution.py:294
  22.8 2.2 %copy-start = (bf16[8,2,512,256]{3,2,1,0:T(8,128)(2,1)S(1)}, bf16[8,2,512,256]{3,2,1,0:T(8,128)(2,1)}, u32[]{:S(2)}) copy-start(bf16[8,2,512,256]{3,2,1,0:T(8,128)(2,1)} %get-tuple-element.25.refs_8_.refs_4_) | copy-start | bytes 12582916
  25.0 0.8 %copy-start.4 = (bf16[64,512]{1,0:T(8,128)(2,1)S(1)}, bf16[64,512]{1,0:T(8,128)(2,1)}, u32[]{:S(2)}) copy-start(bf16[64,512]{1,0:T(8,128)(2,1)} %get-tuple-element.24.refs_0_) | copy-start | bytes 196612
  25.9 16.5 %copy-start.1 = (bf16[8,2,512,256]{3,2,1,0:T(8,128)(2,1)S(1)}, bf16[8,2,512,256]{3,2,1,0:T(8,128)(2,1)}, u32[]{:S(2)}) copy-start(bf16[8,2,512,256]{3,2,1,0:T(8,128)(2,1)} %get-tuple-element.25.refs_8_.refs_4_) | copy-start | bytes 12582916
  27.3 5.0 %collective-permute-start.10 = (bf16[128,256]{1,0:T(8,128)(2,1)S(1)}, bf16[128,256]{1,0:T(8,128)(2,1)S(1)}, u32[]{:S(2)}, u32[]{:S(2)}) collective-permute-start(bf16[128,256]{1,0:T(8,128)(2,1)S(1)} %get-tuple-element.30), channel_id=1, source_target_pairs={{0,8},{8,0},{16,24},{24,16},{1,9},{9,1},{17,25},{25,17},{2,10},{10... | collective-permute-start | bytes 196616 | tf_op jit(solution)/shard_map/ppermute | solution.py:294
  28.8 4.3 %collective-permute-start.11 = (bf16[128,256]{1,0:T(8,128)(2,1)S(1)}, bf16[128,256]{1,0:T(8,128)(2,1)S(1)}, u32[]{:S(2)}, u32[]{:S(2)}) collective-permute-start(bf16[128,256]{1,0:T(8,128)(2,1)S(1)} %get-tuple-element.31), channel_id=1, source_target_pairs={{0,16},{8,24},{16,0},{24,8},{1,17},{9,25},{17,1},{25,9},{2,18},{10... | collective-permute-start | bytes 196616 | tf_op jit(solution)/shard_map/ppermute | solution.py:294
  29.3 5.2 %collective-permute-start.12 = (bf16[128,256]{1,0:T(8,128)(2,1)S(1)}, bf16[128,256]{1,0:T(8,128)(2,1)S(1)}, u32[]{:S(2)}, u32[]{:S(2)}) collective-permute-start(bf16[128,256]{1,0:T(8,128)(2,1)S(1)} %get-tuple-element.32), channel_id=1, source_target_pairs={{0,24},{8,16},{16,8},{24,0},{1,25},{9,17},{17,9},{25,1},{2,26},{10... | collective-permute-start | bytes 196616 | tf_op jit(solution)/shard_map/ppermute | solution.py:294
  35.1 4.3 %collective-permute-start.13 = (bf16[128,256]{1,0:T(8,128)(2,1)S(1)}, bf16[128,256]{1,0:T(8,128)(2,1)S(1)}, u32[]{:S(2)}, u32[]{:S(2)}) collective-permute-start(bf16[128,256]{1,0:T(8,128)(2,1)S(1)} %get-tuple-element.35), channel_id=1, source_target_pairs={{0,8},{8,0},{16,24},{24,16},{1,9},{9,1},{17,25},{25,17},{2,10},{10... | collective-permute-start | bytes 196616 | tf_op jit(solution)/shard_map/ppermute | solution.py:294
  35.7 4.3 %collective-permute-start.14 = (bf16[128,256]{1,0:T(8,128)(2,1)S(1)}, bf16[128,256]{1,0:T(8,128)(2,1)S(1)}, u32[]{:S(2)}, u32[]{:S(2)}) collective-permute-start(bf16[128,256]{1,0:T(8,128)(2,1)S(1)} %get-tuple-element.36), channel_id=1, source_target_pairs={{0,16},{8,24},{16,0},{24,8},{1,17},{9,25},{17,1},{25,9},{2,18},{10... | collective-permute-start | bytes 196616 | tf_op jit(solution)/shard_map/ppermute | solution.py:294
  37.2 5.2 %collective-permute-start.15 = (bf16[128,256]{1,0:T(8,128)(2,1)S(1)}, bf16[128,256]{1,0:T(8,128)(2,1)S(1)}, u32[]{:S(2)}, u32[]{:S(2)}) collective-permute-start(bf16[128,256]{1,0:T(8,128)(2,1)S(1)} %get-tuple-element.37), channel_id=1, source_target_pairs={{0,24},{8,16},{16,8},{24,0},{1,25},{9,17},{17,9},{25,1},{2,26},{10... | collective-permute-start | bytes 196616 | tf_op jit(solution)/shard_map/ppermute | solution.py:294
  43.6 1.6 %collective-permute-start.16 = (bf16[4,64,512]{2,1,0:T(8,128)(2,1)S(1)}, bf16[4,64,512]{2,1,0:T(8,128)(2,1)S(1)}, u32[]{:S(2)}, u32[]{:S(2)}) collective-permute-start(bf16[4,64,512]{2,1,0:T(8,128)(2,1)S(1)} %shard_map.60), channel_id=1, source_target_pairs={{0,1},{1,0},{2,3},{3,2},{4,5},{5,4},{6,7},{7,6},{8,9},{9,8},{10,11... | collective-permute-start | bytes 786440 | tf_op jit(solution)/shard_map/ppermute | solution.py:294
  45.2 5.0 %collective-permute-start.17 = (bf16[64,512]{1,0:T(8,128)(2,1)S(1)}, bf16[64,512]{1,0:T(8,128)(2,1)S(1)}, u32[]{:S(2)}, u32[]{:S(2)}) collective-permute-start(bf16[64,512]{1,0:T(8,128)(2,1)S(1)} %get-tuple-element.39), channel_id=1, source_target_pairs={{0,2},{1,3},{2,0},{3,1},{4,6},{5,7},{6,4},{7,5},{8,10},{9,11},{10,... | collective-permute-start | bytes 196616 | tf_op jit(solution)/shard_map/ppermute | solution.py:294
  46.0 7.7 %collective-permute-start.18 = (bf16[64,512]{1,0:T(8,128)(2,1)S(1)}, bf16[64,512]{1,0:T(8,128)(2,1)S(1)}, u32[]{:S(2)}, u32[]{:S(2)}) collective-permute-start(bf16[64,512]{1,0:T(8,128)(2,1)S(1)} %get-tuple-element.40), channel_id=1, source_target_pairs={{0,4},{1,5},{2,6},{3,7},{4,0},{5,1},{6,2},{7,3},{8,12},{9,13},{10,... | collective-permute-start | bytes 196616 | tf_op jit(solution)/shard_map/ppermute | solution.py:294
  48.3 6.2 %collective-permute-start.19 = (bf16[64,512]{1,0:T(8,128)(2,1)S(1)}, bf16[64,512]{1,0:T(8,128)(2,1)S(1)}, u32[]{:S(2)}, u32[]{:S(2)}) collective-permute-start(bf16[64,512]{1,0:T(8,128)(2,1)S(1)} %get-tuple-element.41), channel_id=1, source_target_pairs={{0,6},{1,7},{2,4},{3,5},{4,2},{5,3},{6,0},{7,1},{8,14},{9,15},{10,... | collective-permute-start | bytes 196616 | tf_op jit(solution)/shard_map/ppermute | solution.py:294

commit v3 on v1

--- a/solution.py
+++ b/solution.py
@@ -89,37 +89,27 @@
     )
 
 
-def edge_kernel(per_block, orb_ref, out_ref):
-    group = orb_ref.shape[0]
+def edge_kernel(per_block, orb_ref, edge_ref):
+    local_k = orb_ref.shape[0]
     row = lax.broadcasted_iota(jnp.int32, (2 * per_block, LANES), 0)
     lane = lax.broadcasted_iota(jnp.int32, (2 * per_block, LANES), 1)
-    first = jnp.where(row < per_block, (row == lane).astype(F32), 0.0).astype(BF16)
-    second = jnp.where(row >= per_block, (row - per_block == lane).astype(F32), 0.0).astype(BF16)
-    rows = []
-    for k in range(group):
-        rows.append(
-            dot(first, orb_ref[k, 0], ((1,), (1,))) + dot(second, orb_ref[k, 1], ((1,), (1,)))
-        )
-    out_ref[...] = jnp.concatenate(rows, axis=0).astype(BF16)
-
-
-def coulomb_kernel(shares, coulomb_ref, *refs):
-    outs, wide = refs[:shares], refs[shares]
-    cells, columns, points = coulomb_ref.shape
-    share = columns // shares
-    me = lax.axis_index("ka")
-    wide[...] = coulomb_ref[...].astype(F32)
-    for s in range(shares):
-        dest = jnp.bitwise_xor(me, s)
-        start = pl.multiple_of(dest * share, share)
-        for r in range(cells):
-            outs[s][r] = wide[r, pl.ds(start, share), :].astype(BF16)
+    one, zero = jnp.ones(row.shape, F32), jnp.zeros(row.shape, F32)
+    first = jnp.where((row < per_block) & (row == lane), one, zero).astype(BF16)
+    second = jnp.where((row >= per_block) & (row == lane + per_block), one, zero).astype(BF16)
+    group = ROWS // (2 * per_block)
+    for g in range(local_k // group):
+        rows = []
+        for k in range(g * group, (g + 1) * group):
+            rows.append(
+                dot(first, orb_ref[k, 0, :, :LANES], ((1,), (1,)))
+                + dot(second, orb_ref[k, 1, :, :LANES], ((1,), (1,)))
+            )
+        edge_ref[g * ROWS : (g + 1) * ROWS] = jnp.concatenate(rows, axis=0).astype(BF16)
 
 
 def tile_kernel(shares, blocks, per_block, *refs):
-    edges, orb_ref, sel_ref = refs[:blocks], refs[blocks], refs[blocks + 1]
-    outs = refs[blocks + 2 : blocks + 2 + shares]
-    form_ref, gathered, wide = refs[blocks + 2 + shares :]
+    edges, orb_ref, sel_ref, coulomb_ref = refs[:blocks], refs[blocks], refs[blocks + 1], refs[blocks + 2]
+    outs, (form_ref, gathered, wide, cells) = refs[blocks + 3 : blocks + 3 + shares], refs[blocks + 3 + shares :]
     local_k, _, norb, points = orb_ref.shape
     group = ROWS // (2 * per_block)
     total = blocks * per_block
@@ -127,6 +117,7 @@
     rows = 2 * total
     me = lax.axis_index("ka")
     block = lax.axis_index("pts")
+    cells[...] = coulomb_ref[...].astype(F32)
     for s in range(blocks):
         gathered[jnp.bitwise_xor(block, s)] = edges[s][...]
     for g in range(local_k // group):
@@ -149,21 +140,24 @@
     size = share * 2 * local_k
     for s in range(shares):
         dest = jnp.bitwise_xor(me, s)
-        outs[s][...] = take(wide, pl.multiple_of(dest * size, size), size).astype(BF16)
+        outs[s][:size] = take(wide, pl.multiple_of(dest * size, size), size).astype(BF16)
+        start = pl.multiple_of(dest * share, share)
+        pair = [cells[r, pl.ds(start, share), :] for r in range(local_k)]
+        outs[s][size:] = jnp.concatenate(pair, axis=0).astype(BF16)
 
 
 def transform_kernel(shares, total, share, *refs):
-    tiles, coulombs = refs[:shares], refs[shares : 2 * shares]
-    fwd_ref, bwd_ref = refs[2 * shares : 2 * shares + 2]
-    outs = refs[2 * shares + 2 : 3 * shares + 2]
-    gathered, weight, wide = refs[3 * shares + 2 :]
+    tiles, (fwd_ref, bwd_ref) = refs[:shares][::-1], refs[shares : shares + 2]
+    outs, (gathered, weight, wide) = refs[shares + 2 : 2 * shares + 2], refs[2 * shares + 2 :]
     local_k = total // shares
+    size = 2 * local_k * share
     me = lax.axis_index("ka")
     for s in range(shares):
         src = jnp.bitwise_xor(me, s)
-        gathered[src] = tiles[s][...].astype(gathered.dtype)
+        gathered[src] = tiles[s][:size].astype(gathered.dtype)
+        cells = tiles[s][size:].astype(F32)
         for r in range(local_k):
-            spread(weight, src * local_k + r, total, coulombs[s][r].astype(F32))
+            spread(weight, src * local_k + r, total, cells[r * share : (r + 1) * share])
     rows = 2 * local_k
     columns = []
     for c in range(share):
@@ -178,14 +172,13 @@
     points = kernel.shape[1] // share
     for c in range(share):
         spread(wide, c, share, kernel[:, c * points : (c + 1) * points])
-    size = 2 * local_k * share
     for s in range(shares):
         dest = jnp.bitwise_xor(me, s)
         outs[s][...] = take(wide, pl.multiple_of(dest * size, size), size).astype(BF16)
 
 
 def weight_kernel(shares, flip, out_rows, *refs):
-    pieces, orb_ref, out_ref, gathered = refs[:shares], refs[shares], refs[shares + 1], refs[shares + 2]
+    pieces, orb_ref, out_ref, gathered = refs[:shares][::-1], refs[shares], refs[shares + 1], refs[shares + 2]
     local_k, _, norb, points = orb_ref.shape
     total_rows = gathered.shape[1]
     half = total_rows // local_k // 2
@@ -235,9 +228,10 @@
 
 
 def exchange_kernel(chunks, scale, *refs):
-    pieces, form_ref, out_ref, wide = refs[:chunks], refs[chunks], refs[chunks + 1], refs[chunks + 2]
+    pieces, form_ref, out_ref, wide = refs[:chunks][::-1], refs[chunks], refs[chunks + 1], refs[chunks + 2]
     local_k, lanes, twice = form_ref.shape
     norb = twice // 2
+    spans = norb // LANES
     out_rows = pieces[0].shape[0]
     total = pieces[0][...]
     for s in range(1, chunks):
@@ -263,16 +257,21 @@
         for kk in range(group):
             k = g * group + kk
             for part in range(2):
-                value = result[kk * out_rows : (kk + 1) * out_rows, part * norb : (part + 1) * norb]
-                spread(wide, 2 * k + part, 2 * local_k, value)
-    for t in range(norb // LANES):
-        value = wide[t].astype(BF16).reshape(out_rows, local_k, 2, LANES)
-        out_ref[:, :, :, t * LANES : (t + 1) * LANES] = value
+                for t in range(spans):
+                    lane_start = part * norb + t * LANES
+                    value = result[kk * out_rows : (kk + 1) * out_rows, lane_start : lane_start + LANES]
+                    start = (k * spans + t) * 2 + part
+                    wide[pl.ds(start, out_rows, stride=2 * spans * local_k), :] = value
+    out_ref[...] = wide[...].astype(BF16)
 
 
 def swap(value, axis, mask):
     size = lax.axis_size(axis)
     return lax.ppermute(value, axis, [(i, i ^ mask) for i in range(size)])
+
+
+def trade(pieces, axis, step):
+    return [swap(pieces[s], axis, s * step) for s in reversed(range(1, len(pieces)))] + [pieces[0]]
 
 
 def body(orbitals, coulomb):
@@ -287,13 +286,11 @@
     group = ROWS // (2 * per_block)
     shape = jax.ShapeDtypeStruct
 
-    edge = pl.pallas_call(
+    edge = call(
         functools.partial(edge_kernel, per_block),
-        out_shape=shape((local_k * 2 * per_block, norb), BF16),
-        grid=(local_k // group,),
-        in_specs=[pl.BlockSpec((group, 2, norb, LANES), lambda g: (g, 0, 0, 0))],
-        out_specs=pl.BlockSpec((ROWS, norb), lambda g: (g, 0)),
-        cost_estimate=pl.CostEstimate(flops=0, bytes_accessed=2 * MIB, transcendentals=0),
+        shape((local_k * 2 * per_block, norb), BF16),
+        1,
+        size=4 * MIB,
     )(orbitals)
     edges = [edge] + [None] * (blocks - 1)
     for s in range(1, chunks):
@@ -301,42 +298,35 @@
     for s in range(chunks):
         edges[2 * s + 1] = swap(edges[2 * s], "pts", 1)
 
-    own = call(
-        functools.partial(coulomb_kernel, shares),
-        [shape((local_k, share, points), BF16)] * shares,
-        1,
-        [pltpu.VMEM((local_k, columns, points), F32)],
-        size=2 * MIB,
-    )(coulomb)
-    coulombs = [own[0]] + [swap(own[s], "ka", s) for s in range(1, shares)]
-
     selector = jnp.asarray(column_selector(group, blocks, per_block, shares))
     piece = shape((share * 2 * local_k, points), BF16)
+    both = shape((share * 3 * local_k, points), BF16)
     *tiles, forms = call(
         functools.partial(tile_kernel, shares, blocks, per_block),
-        [piece] * shares + [shape((local_k, 2 * columns, 2 * norb), BF16)],
-        blocks + 2,
+        [both] * shares + [shape((local_k, 2 * columns, 2 * norb), BF16)],
+        blocks + 3,
         [
             pltpu.VMEM((blocks, local_k * 2 * per_block, norb), BF16),
             tiled(columns * 2 * local_k, points),
+            pltpu.VMEM((local_k, columns, points), F32),
         ],
         size=8 * MIB,
-    )(*edges, orbitals, selector)
-    tiles = [tiles[0]] + [swap(tiles[s], "ka", s) for s in range(1, shares)]
+    )(*edges, orbitals, selector, coulomb)
+    tiles = trade(tiles, "ka", 1)
 
     forward, backward = phase_tables(total)
     kernels = call(
         functools.partial(transform_kernel, shares, total, share),
         [piece] * shares,
-        2 * shares + 2,
+        shares + 2,
         [
             pltpu.VMEM((shares, share * 2 * local_k, points), BF16 if local_k % 8 == 0 else F32),
             tiled(share * total, points),
             tiled(2 * total * share, points),
         ],
         size=2 * MIB,
-    )(*tiles, *coulombs, jnp.asarray(forward), jnp.asarray(backward))
-    kernels = [kernels[0]] + [swap(kernels[s], "ka", s) for s in range(1, shares)]
+    )(*tiles, jnp.asarray(forward), jnp.asarray(backward))
+    kernels = trade(kernels, "ka", 1)
 
     lanes = local_k * 2 * columns
     halves = []
@@ -357,14 +347,18 @@
         2,
         size=1 * MIB,
     )(halves[1], came)
-    sums = [own_sum] + [swap(sums[s - 1], "pts", 2 * s) for s in range(1, chunks)]
-    return call(
+    sums = trade([own_sum, *sums], "pts", 2)
+    spans = norb // LANES
+    rows = out_rows * local_k * spans * 2
+    result = call(
         functools.partial(exchange_kernel, chunks, 1.0 / math.sqrt(points * blocks)),
-        shape((out_rows, local_k, 2, norb), BF16),
+        shape((rows, LANES), BF16),
         chunks + 1,
-        [tiled(out_rows * 2 * local_k, norb)],
+        [pltpu.VMEM((rows, LANES), F32)],
         size=4 * MIB,
     )(*sums, forms)
+    result = result.reshape(out_rows, local_k, spans, 2, LANES)
+    return result.transpose(0, 1, 3, 2, 4).reshape(out_rows, local_k, 2, norb)
 
 
 def solution(mesh):

time: 53.7 us -> 47.8 us (0.89)
  starting transfers between devices: 21.6 us -> 17.8 us
  Pallas kernels: 11.1 us -> 7.6 us
  waiting for transfers between devices: 17.7 us -> 19.1 us
    ppermute x20 -> x17, starting transfers between devices: 21.6 us -> 17.8 us  [swap(): return lax.ppermute(value, axis, [(i, i ^ mask) for i in range(size)])]
    pallas_call x3 -> x2, Pallas kernels: 5.31 us -> 2.04 us  [the longest x1 1.4 us: body(): call(functools.partial(tile_kernel, shares, blocks, per_block), [both] *...]
    ppermute x20 -> x17, waiting for transfers between devices: 17.7 us -> 19.1 us  [swap(): return lax.ppermute(value, axis, [(i, i ^ mask) for i in range(size)])]
    unnamed x14 -> x12, local copies, waits for them, and re-layouts: 3.04 us -> 3.11 us
  transfers between devices with their start and end apart: 20 -> 17, of which waited for: 10 -> 13; matrix products, arithmetic and copies ran while one was open for 0% -> 0% of each run, Pallas kernels for 5% -> 2%
where the time goes in v3:
time: 47.8 us; the launch traced here: 47.6 us
  waiting for transfers between devices  19.1 us (40%)
  starting transfers between devices  17.8 us (37%)
  Pallas kernels  7.6 us (16%)
  local copies, waits for them, and re-layouts  3.11 us (7%)
    ppermute x17, waiting for transfers between devices, swap(): return lax.ppermute(value, axis, [(i, i ^ mask) for i in range(size)])  19.1 us
    ppermute x17, starting transfers between devices, swap(): return lax.ppermute(value, axis, [(i, i ^ mask) for i in range(size)])  17.8 us
    unnamed x12, local copies, waits for them, and re-layouts  3.11 us
    pallas_call x1, Pallas kernels, body(): call(functools.partial(exchange_kernel, chunks, 1.0 / math.sqrt(points *...  2.61 us
    pallas_call x2, Pallas kernels, body(): call(functools.partial(weight_kernel, shares, flip, out_rows), shape((chu...  2.33 us
    pallas_call x1, Pallas kernels, body(): call(functools.partial(tile_kernel, shares, blocks, per_block), [both] *...  1.4 us
  transfers between devices with their start and end apart: 17, of which 13 were waited for; matrix products, arithmetic and copies ran while one was open for 0% of the time, Pallas kernels for 2%

profile of v3, /device:TPU:0, one launch (start us, length us, event | category | flops | bytes accessed | tf_op | source)
XLA Modules:
  0.0 47.6 jit_solution(8599324346260997702)
XLA Ops:
  0.0 2.2 %copy-done = bf16[8,2,512,256]{3,2,1,0:T(8,128)(2,1)S(1)} copy-done((bf16[8,2,512,256]{3,2,1,0:T(8,128)(2,1)S(1)}, bf16[8,2,512,256]{3,2,1,0:T(8,128)(2,1)}, u32[]{:S(2)}) %copy-start) | copy-done | bytes 4194328
  2.2 0.6 %shard_map.55.refs_0_ = bf16[64,512]{1,0:T(8,128)(2,1)S(1)} custom-call(bf16[8,2,512,256]{3,2,1,0:T(8,128)(2,1)S(1)} %copy-done), custom_call_target="tpu_custom_call" | custom-call | bytes 4194304 | tf_op jit(solution)/shard_map/pallas_call | solution.py:289
  2.8 5.1 %collective-permute-start.5 = (bf16[64,512]{1,0:T(8,128)(2,1)S(1)}, bf16[64,512]{1,0:T(8,128)(2,1)S(1)}, u32[]{:S(2)}, u32[]{:S(2)}) collective-permute-start(bf16[64,512]{1,0:T(8,128)(2,1)S(1)} %shard_map.55.refs_0_), channel_id=1, source_target_pairs={{0,6},{1,7},{2,4},{3,5},{4,2},{5,3},{6,0},{7,1},{8,14},{9,15},{10,... | collective-permute-start | bytes 196616 | tf_op jit(solution)/shard_map/ppermute | solution.py:270
  7.9 0.6 %collective-permute-start.1 = (bf16[64,512]{1,0:T(8,128)(2,1)S(1)}, bf16[64,512]{1,0:T(8,128)(2,1)S(1)}, u32[]{:S(2)}, u32[]{:S(2)}) collective-permute-start(bf16[64,512]{1,0:T(8,128)(2,1)S(1)} %shard_map.55.refs_0_), channel_id=1, source_target_pairs={{0,2},{1,3},{2,0},{3,1},{4,6},{5,7},{6,4},{7,5},{8,10},{9,11},{10,... | collective-permute-start | bytes 196616 | tf_op jit(solution)/shard_map/ppermute | solution.py:270
  8.5 2.0 %collective-permute-done.5.refs_6_ = bf16[64,512]{1,0:T(8,128)(2,1)S(1)} collective-permute-done((bf16[64,512]{1,0:T(8,128)(2,1)S(1)}, bf16[64,512]{1,0:T(8,128)(2,1)S(1)}, u32[]{:S(2)}, u32[]{:S(2)}) %collective-permute-start.5) | collective-permute-done | bytes 65568 | tf_op jit(solution)/shard_map/ppermute | solution.py:270
  10.5 3.0 %collective-permute-done.3.refs_4_ = bf16[64,512]{1,0:T(8,128)(2,1)S(1)} collective-permute-done((bf16[64,512]{1,0:T(8,128)(2,1)S(1)}, bf16[64,512]{1,0:T(8,128)(2,1)S(1)}, u32[]{:S(2)}, u32[]{:S(2)}) %collective-permute-start.3) | collective-permute-done | bytes 65568 | tf_op jit(solution)/shard_map/ppermute | solution.py:270
  13.5 0.5 %collective-permute-start.2 = (bf16[64,512]{1,0:T(8,128)(2,1)S(1)}, bf16[64,512]{1,0:T(8,128)(2,1)S(1)}, u32[]{:S(2)}, u32[]{:S(2)}) collective-permute-start(bf16[64,512]{1,0:T(8,128)(2,1)S(1)} %collective-permute-done.1.refs_2_), channel_id=1, source_target_pairs={{0,1},{1,0},{2,3},{3,2},{4,5},{5,4},{6,7},{7,6},{8,9},{9,8},{10,11... | collective-permute-start | bytes 196616 | tf_op jit(solution)/shard_map/ppermute | solution.py:270
  14.0 0.7 %collective-permute-done.4.refs_5_ = bf16[64,512]{1,0:T(8,128)(2,1)S(1)} collective-permute-done((bf16[64,512]{1,0:T(8,128)(2,1)S(1)}, bf16[64,512]{1,0:T(8,128)(2,1)S(1)}, u32[]{:S(2)}, u32[]{:S(2)}) %collective-permute-start.4) | collective-permute-done | bytes 65568 | tf_op jit(solution)/shard_map/ppermute | solution.py:270
  14.8 0.2 collective-permute-done.2.refs_3_
  14.9 0.9 %copy-done.2 = bf16[8,32,256]{2,1,0:T(8,128)(2,1)S(1)} copy-done((bf16[8,32,256]{2,1,0:T(8,128)(2,1)S(1)}, bf16[8,32,256]{2,1,0:T(8,128)(2,1)}, u32[]{:S(2)}) %copy-start.2) | copy-done | bytes 131096
  15.8 1.4 %shard_map.56 = (bf16[192,256]{1,0:T(8,128)(2,1)S(1)}, bf16[192,256]{1,0:T(8,128)(2,1)S(1)}, bf16[192,256]{1,0:T(8,128)(2,1)S(1)}, bf16[192,256]{1,0:T(8,128)(2,1)S(1)}, bf16[8,64,1024]{2,1,0:T(8,128)(2,1)S(1)}) custom-call(bf16[64,512]{1,0:T(8,128)(2,1)S(1)} %shard_map.55.refs_0_, bf16[64,512]{1,0:T(8,128)(2,1)S(1)} %collective-permute-done.refs_1_, ...), custom_call_target="tpu_custom_call" | custom-call | bytes 8388608 | tf_op jit(solution)/shard_map/pallas_call | solution.py:304
  17.2 2.5 %collective-permute-start.7 = (bf16[192,256]{1,0:T(8,128)(2,1)S(1)}, bf16[192,256]{1,0:T(8,128)(2,1)S(1)}, u32[]{:S(2)}, u32[]{:S(2)}) collective-permute-start(bf16[192,256]{1,0:T(8,128)(2,1)S(1)} %get-tuple-element.18), channel_id=1, source_target_pairs={{0,24},{8,16},{16,8},{24,0},{1,25},{9,17},{17,9},{25,1},{2,26},{10... | collective-permute-start | bytes 294920 | tf_op jit(solution)/shard_map/ppermute | solution.py:270
  19.8 0.5 %collective-permute-start.8 = (bf16[192,256]{1,0:T(8,128)(2,1)S(1)}, bf16[192,256]{1,0:T(8,128)(2,1)S(1)}, u32[]{:S(2)}, u32[]{:S(2)}) collective-permute-start(bf16[192,256]{1,0:T(8,128)(2,1)S(1)} %get-tuple-element.19), channel_id=1, source_target_pairs={{0,16},{8,24},{16,0},{24,8},{1,17},{9,25},{17,1},{25,9},{2,18},{10... | collective-permute-start | bytes 294920 | tf_op jit(solution)/shard_map/ppermute | solution.py:270
  20.3 0.5 %collective-permute-start.9 = (bf16[192,256]{1,0:T(8,128)(2,1)S(1)}, bf16[192,256]{1,0:T(8,128)(2,1)S(1)}, u32[]{:S(2)}, u32[]{:S(2)}) collective-permute-start(bf16[192,256]{1,0:T(8,128)(2,1)S(1)} %get-tuple-element.20), channel_id=1, source_target_pairs={{0,8},{8,0},{16,24},{24,16},{1,9},{9,1},{17,25},{25,17},{2,10},{10... | collective-permute-start | bytes 294920 | tf_op jit(solution)/shard_map/ppermute | solution.py:270
  20.8 2.5 %collective-permute-done.7.refs_0_ = bf16[192,256]{1,0:T(8,128)(2,1)S(1)} collective-permute-done((bf16[192,256]{1,0:T(8,128)(2,1)S(1)}, bf16[192,256]{1,0:T(8,128)(2,1)S(1)}, u32[]{:S(2)}, u32[]{:S(2)}) %collective-permute-start.7) | collective-permute-done | bytes 98336 | tf_op jit(solution)/shard_map/ppermute | solution.py:270
  23.3 2.0 %collective-permute-done.8.refs_1_ = bf16[192,256]{1,0:T(8,128)(2,1)S(1)} collective-permute-done((bf16[192,256]{1,0:T(8,128)(2,1)S(1)}, bf16[192,256]{1,0:T(8,128)(2,1)S(1)}, u32[]{:S(2)}, u32[]{:S(2)}) %collective-permute-start.8) | collective-permute-done | bytes 98336 | tf_op jit(solution)/shard_map/ppermute | solution.py:270
  25.4 0.6 %shard_map.57 = (bf16[128,256]{1,0:T(8,128)(2,1)S(1)}, bf16[128,256]{1,0:T(8,128)(2,1)S(1)}, bf16[128,256]{1,0:T(8,128)(2,1)S(1)}, bf16[128,256]{1,0:T(8,128)(2,1)S(1)}) custom-call(bf16[192,256]{1,0:T(8,128)(2,1)S(1)} %collective-permute-done.7.refs_0_, bf16[192,256]{1,0:T(8,128)(2,1)S(1)} %collective-permute-done.8.refs_1_, ...), custom_call_target="tpu_custom_call" | custom-call | bytes 2097152 | tf_op jit(solution)/shard_map/pallas_call | solution.py:318
  26.0 1.8 %collective-permute-start.10 = (bf16[128,256]{1,0:T(8,128)(2,1)S(1)}, bf16[128,256]{1,0:T(8,128)(2,1)S(1)}, u32[]{:S(2)}, u32[]{:S(2)}) collective-permute-start(bf16[128,256]{1,0:T(8,128)(2,1)S(1)} %get-tuple-element.22), channel_id=1, source_target_pairs={{0,24},{8,16},{16,8},{24,0},{1,25},{9,17},{17,9},{25,1},{2,26},{10... | collective-permute-start | bytes 196616 | tf_op jit(solution)/shard_map/ppermute | solution.py:270
  27.8 1.3 %collective-permute-start.11 = (bf16[128,256]{1,0:T(8,128)(2,1)S(1)}, bf16[128,256]{1,0:T(8,128)(2,1)S(1)}, u32[]{:S(2)}, u32[]{:S(2)}) collective-permute-start(bf16[128,256]{1,0:T(8,128)(2,1)S(1)} %get-tuple-element.23), channel_id=1, source_target_pairs={{0,16},{8,24},{16,0},{24,8},{1,17},{9,25},{17,1},{25,9},{2,18},{10... | collective-permute-start | bytes 196616 | tf_op jit(solution)/shard_map/ppermute | solution.py:270
  29.1 0.5 %collective-permute-start.12 = (bf16[128,256]{1,0:T(8,128)(2,1)S(1)}, bf16[128,256]{1,0:T(8,128)(2,1)S(1)}, u32[]{:S(2)}, u32[]{:S(2)}) collective-permute-start(bf16[128,256]{1,0:T(8,128)(2,1)S(1)} %get-tuple-element.24), channel_id=1, source_target_pairs={{0,8},{8,0},{16,24},{24,16},{1,9},{9,1},{17,25},{25,17},{2,10},{10... | collective-permute-start | bytes 196616 | tf_op jit(solution)/shard_map/ppermute | solution.py:270
  29.6 2.1 %collective-permute-done.10.refs_0_ = bf16[128,256]{1,0:T(8,128)(2,1)S(1)} collective-permute-done((bf16[128,256]{1,0:T(8,128)(2,1)S(1)}, bf16[128,256]{1,0:T(8,128)(2,1)S(1)}, u32[]{:S(2)}, u32[]{:S(2)}) %collective-permute-start.10) | collective-permute-done | bytes 65568 | tf_op jit(solution)/shard_map/ppermute | solution.py:270
  31.7 0.7 %collective-permute-done.11.refs_1_ = bf16[128,256]{1,0:T(8,128)(2,1)S(1)} collective-permute-done((bf16[128,256]{1,0:T(8,128)(2,1)S(1)}, bf16[128,256]{1,0:T(8,128)(2,1)S(1)}, u32[]{:S(2)}, u32[]{:S(2)}) %collective-permute-start.11) | collective-permute-done | bytes 65568 | tf_op jit(solution)/shard_map/ppermute | solution.py:270
  32.4 1.0 %collective-permute-done.12.refs_2_ = bf16[128,256]{1,0:T(8,128)(2,1)S(1)} collective-permute-done((bf16[128,256]{1,0:T(8,128)(2,1)S(1)}, bf16[128,256]{1,0:T(8,128)(2,1)S(1)}, u32[]{:S(2)}, u32[]{:S(2)}) %collective-permute-start.12) | collective-permute-done | bytes 65568 | tf_op jit(solution)/shard_map/ppermute | solution.py:270
  33.4 1.2 %shard_map.59 = bf16[4,64,512]{2,1,0:T(8,128)(2,1)S(1)} custom-call(bf16[128,256]{1,0:T(8,128)(2,1)S(1)} %collective-permute-done.10.refs_0_, bf16[128,256]{1,0:T(8,128)(2,1)S(1)} %collective-permute-done.11.refs_1_, bf16[128,256]{1,0:T(8,128)(2,1)S(1)} %collective-permute-done.12.refs_2_, bf16[128,256]{1,0:T(8,128)(2,1)S(1)} %get-tuple-element.25.refs_3_, ...), custom_call_target="tpu_custom_call" | custom-call | bytes 6291456 | tf_op jit(solution)/shard_map/pallas_call | solution.py:335
  34.5 0.1 collective-permute-start.13
  34.6 1.2 %shard_map.58.keep_ref = f32[4,64,512]{2,1,0:T(8,128)S(1)} custom-call(bf16[128,256]{1,0:T(8,128)(2,1)S(1)} %collective-permute-done.10.refs_0_, bf16[128,256]{1,0:T(8,128)(2,1)S(1)} %collective-permute-done.11.refs_1_, bf16[128,256]{1,0:T(8,128)(2,1)S(1)} %collective-permute-done.12.refs_2_, bf16[128,256]{1,0:T(8,128)(2,1)S(1)} %get-tuple-element.25.refs_3_, ...), custom_call_target="tpu_custom_call" | custom-call | bytes 6291456 | tf_op jit(solution)/shard_map/pallas_call | solution.py:335
  35.8 0.4 collective-permute-done.13.came_ref
  36.2 2.7 %collective-permute-start.14 = (bf16[64,512]{1,0:T(8,128)(2,1)S(1)}, bf16[64,512]{1,0:T(8,128)(2,1)S(1)}, u32[]{:S(2)}, u32[]{:S(2)}) collective-permute-start(bf16[64,512]{1,0:T(8,128)(2,1)S(1)} %get-tuple-element.26), channel_id=1, source_target_pairs={{0,6},{1,7},{2,4},{3,5},{4,2},{5,3},{6,0},{7,1},{8,14},{9,15},{10,... | collective-permute-start | bytes 196616 | tf_op jit(solution)/shard_map/ppermute | solution.py:270
  38.9 1.7 %collective-permute-start.16 = (bf16[64,512]{1,0:T(8,128)(2,1)S(1)}, bf16[64,512]{1,0:T(8,128)(2,1)S(1)}, u32[]{:S(2)}, u32[]{:S(2)}) collective-permute-start(bf16[64,512]{1,0:T(8,128)(2,1)S(1)} %get-tuple-element.28), channel_id=1, source_target_pairs={{0,2},{1,3},{2,0},{3,1},{4,6},{5,7},{6,4},{7,5},{8,10},{9,11},{10,... | collective-permute-start | bytes 196616 | tf_op jit(solution)/shard_map/ppermute | solution.py:270
  40.6 2.3 %collective-permute-done.14.refs_0_ = bf16[64,512]{1,0:T(8,128)(2,1)S(1)} collective-permute-done((bf16[64,512]{1,0:T(8,128)(2,1)S(1)}, bf16[64,512]{1,0:T(8,128)(2,1)S(1)}, u32[]{:S(2)}, u32[]{:S(2)}) %collective-permute-start.14) | collective-permute-done | bytes 65568 | tf_op jit(solution)/shard_map/ppermute | solution.py:270
  43.0 2.0 %collective-permute-done.15.refs_1_ = bf16[64,512]{1,0:T(8,128)(2,1)S(1)} collective-permute-done((bf16[64,512]{1,0:T(8,128)(2,1)S(1)}, bf16[64,512]{1,0:T(8,128)(2,1)S(1)}, u32[]{:S(2)}, u32[]{:S(2)}) %collective-permute-start.15) | collective-permute-done | bytes 65568 | tf_op jit(solution)/shard_map/ppermute | solution.py:270
  45.0 2.6 %shard_map.61 = bf16[4096,128]{1,0:T(8,128)(2,1)} custom-call(bf16[64,512]{1,0:T(8,128)(2,1)S(1)} %collective-permute-done.14.refs_0_, bf16[64,512]{1,0:T(8,128)(2,1)S(1)} %collective-permute-done.15.refs_1_, bf16[64,512]{1,0:T(8,128)(2,1)S(1)} %collective-permute-done.16.refs_2_, f32[64,512]{1,0:T(8,128)S(1)} %get-tuple-element.29.refs_3_, ...), custom_call_target="tpu_custom_call" | custom-call | bytes 4194304 | tf_op jit(solution)/shard_map/pallas_call | solution.py:353
  (21 shorter events, 0.1 us)
Async XLA Ops:
  0.0 2.2 %copy-start = (bf16[8,2,512,256]{3,2,1,0:T(8,128)(2,1)S(1)}, bf16[8,2,512,256]{3,2,1,0:T(8,128)(2,1)}, u32[]{:S(2)}) copy-start(bf16[8,2,512,256]{3,2,1,0:T(8,128)(2,1)} %refs_4_.4) | copy-start | bytes 12582916
  2.2 12.7 %copy-start.3 = (bf16[256,128]{1,0:T(8,128)(2,1)S(1)}, bf16[256,128]{1,0:T(8,128)(2,1)}, u32[]{:S(2)}) copy-start(bf16[256,128]{1,0:T(8,128)(2,1)} %constant.6.clone.refs_9_) | copy-start | bytes 196612
  2.2 31.2 %copy-start.1 = (bf16[8,2,512,256]{3,2,1,0:T(8,128)(2,1)S(1)}, bf16[8,2,512,256]{3,2,1,0:T(8,128)(2,1)}, u32[]{:S(2)}) copy-start(bf16[8,2,512,256]{3,2,1,0:T(8,128)(2,1)} %refs_4_.4) | copy-start | bytes 12582916
  2.8 7.6 %collective-permute-start.5 = (bf16[64,512]{1,0:T(8,128)(2,1)S(1)}, bf16[64,512]{1,0:T(8,128)(2,1)S(1)}, u32[]{:S(2)}, u32[]{:S(2)}) collective-permute-start(bf16[64,512]{1,0:T(8,128)(2,1)S(1)} %shard_map.55.refs_0_), channel_id=1, source_target_pairs={{0,6},{1,7},{2,4},{3,5},{4,2},{5,3},{6,0},{7,1},{8,14},{9,15},{10,... | collective-permute-start | bytes 196616 | tf_op jit(solution)/shard_map/ppermute | solution.py:270
  7.9 5.6 %collective-permute-start.3 = (bf16[64,512]{1,0:T(8,128)(2,1)S(1)}, bf16[64,512]{1,0:T(8,128)(2,1)S(1)}, u32[]{:S(2)}, u32[]{:S(2)}) collective-permute-start(bf16[64,512]{1,0:T(8,128)(2,1)S(1)} %shard_map.55.refs_0_), channel_id=1, source_target_pairs={{0,4},{1,5},{2,6},{3,7},{4,0},{5,1},{6,2},{7,3},{8,12},{9,13},{10,... | collective-permute-start | bytes 196616 | tf_op jit(solution)/shard_map/ppermute | solution.py:270
  7.9 5.6 %collective-permute-start.1 = (bf16[64,512]{1,0:T(8,128)(2,1)S(1)}, bf16[64,512]{1,0:T(8,128)(2,1)S(1)}, u32[]{:S(2)}, u32[]{:S(2)}) collective-permute-start(bf16[64,512]{1,0:T(8,128)(2,1)S(1)} %shard_map.55.refs_0_), channel_id=1, source_target_pairs={{0,2},{1,3},{2,0},{3,1},{4,6},{5,7},{6,4},{7,5},{8,10},{9,11},{10,... | collective-permute-start | bytes 196616 | tf_op jit(solution)/shard_map/ppermute | solution.py:270
  8.5 5.5 %collective-permute-start = (bf16[64,512]{1,0:T(8,128)(2,1)S(1)}, bf16[64,512]{1,0:T(8,128)(2,1)S(1)}, u32[]{:S(2)}, u32[]{:S(2)}) collective-permute-start(bf16[64,512]{1,0:T(8,128)(2,1)S(1)} %shard_map.55.refs_0_), channel_id=1, source_target_pairs={{0,1},{1,0},{2,3},{3,2},{4,5},{5,4},{6,7},{7,6},{8,9},{9,8},{10,11... | collective-permute-start | bytes 196616 | tf_op jit(solution)/shard_map/ppermute | solution.py:270
  10.5 3.6 %collective-permute-start.6 = (bf16[64,512]{1,0:T(8,128)(2,1)S(1)}, bf16[64,512]{1,0:T(8,128)(2,1)S(1)}, u32[]{:S(2)}, u32[]{:S(2)}) collective-permute-start(bf16[64,512]{1,0:T(8,128)(2,1)S(1)} %collective-permute-done.5.refs_6_), channel_id=1, source_target_pairs={{0,1},{1,0},{2,3},{3,2},{4,5},{5,4},{6,7},{7,6},{8,9},{9,8},{10,11... | collective-permute-start | bytes 196616 | tf_op jit(solution)/shard_map/ppermute | solution.py:270
  13.5 1.3 %collective-permute-start.4 = (bf16[64,512]{1,0:T(8,128)(2,1)S(1)}, bf16[64,512]{1,0:T(8,128)(2,1)S(1)}, u32[]{:S(2)}, u32[]{:S(2)}) collective-permute-start(bf16[64,512]{1,0:T(8,128)(2,1)S(1)} %collective-permute-done.3.refs_4_), channel_id=1, source_target_pairs={{0,1},{1,0},{2,3},{3,2},{4,5},{5,4},{6,7},{7,6},{8,9},{9,8},{10,11... | collective-permute-start | bytes 196616 | tf_op jit(solution)/shard_map/ppermute | solution.py:270
  13.5 1.4 %collective-permute-start.2 = (bf16[64,512]{1,0:T(8,128)(2,1)S(1)}, bf16[64,512]{1,0:T(8,128)(2,1)S(1)}, u32[]{:S(2)}, u32[]{:S(2)}) collective-permute-start(bf16[64,512]{1,0:T(8,128)(2,1)S(1)} %collective-permute-done.1.refs_2_), channel_id=1, source_target_pairs={{0,1},{1,0},{2,3},{3,2},{4,5},{5,4},{6,7},{7,6},{8,9},{9,8},{10,11... | collective-permute-start | bytes 196616 | tf_op jit(solution)/shard_map/ppermute | solution.py:270
  14.9 0.9 %copy-start.2 = (bf16[8,32,256]{2,1,0:T(8,128)(2,1)S(1)}, bf16[8,32,256]{2,1,0:T(8,128)(2,1)}, u32[]{:S(2)}) copy-start(bf16[8,32,256]{2,1,0:T(8,128)(2,1)} %refs_10_.1) | copy-start | bytes 393220
  15.8 9.6 %copy-start.4 = (bf16[64,128]{1,0:T(8,128)(2,1)S(1)}, bf16[64,128]{1,0:T(8,128)(2,1)}, u32[]{:S(2)}) copy-start(bf16[64,128]{1,0:T(8,128)(2,1)} %constant.8.clone.refs_5_) | copy-start | bytes 49156
  15.8 9.6 %copy-start.5 = (bf16[64,128]{1,0:T(8,128)(2,1)S(1)}, bf16[64,128]{1,0:T(8,128)(2,1)}, u32[]{:S(2)}) copy-start(bf16[64,128]{1,0:T(8,128)(2,1)} %constant.7.clone.refs_4_) | copy-start | bytes 49156
  17.2 6.1 %collective-permute-start.7 = (bf16[192,256]{1,0:T(8,128)(2,1)S(1)}, bf16[192,256]{1,0:T(8,128)(2,1)S(1)}, u32[]{:S(2)}, u32[]{:S(2)}) collective-permute-start(bf16[192,256]{1,0:T(8,128)(2,1)S(1)} %get-tuple-element.18), channel_id=1, source_target_pairs={{0,24},{8,16},{16,8},{24,0},{1,25},{9,17},{17,9},{25,1},{2,26},{10... | collective-permute-start | bytes 294920 | tf_op jit(solution)/shard_map/ppermute | solution.py:270
  19.8 5.6 %collective-permute-start.8 = (bf16[192,256]{1,0:T(8,128)(2,1)S(1)}, bf16[192,256]{1,0:T(8,128)(2,1)S(1)}, u32[]{:S(2)}, u32[]{:S(2)}) collective-permute-start(bf16[192,256]{1,0:T(8,128)(2,1)S(1)} %get-tuple-element.19), channel_id=1, source_target_pairs={{0,16},{8,24},{16,0},{24,8},{1,17},{9,25},{17,1},{25,9},{2,18},{10... | collective-permute-start | bytes 294920 | tf_op jit(solution)/shard_map/ppermute | solution.py:270
  20.3 5.2 %collective-permute-start.9 = (bf16[192,256]{1,0:T(8,128)(2,1)S(1)}, bf16[192,256]{1,0:T(8,128)(2,1)S(1)}, u32[]{:S(2)}, u32[]{:S(2)}) collective-permute-start(bf16[192,256]{1,0:T(8,128)(2,1)S(1)} %get-tuple-element.20), channel_id=1, source_target_pairs={{0,8},{8,0},{16,24},{24,16},{1,9},{9,1},{17,25},{25,17},{2,10},{10... | collective-permute-start | bytes 294920 | tf_op jit(solution)/shard_map/ppermute | solution.py:270
  26.0 5.7 %collective-permute-start.10 = (bf16[128,256]{1,0:T(8,128)(2,1)S(1)}, bf16[128,256]{1,0:T(8,128)(2,1)S(1)}, u32[]{:S(2)}, u32[]{:S(2)}) collective-permute-start(bf16[128,256]{1,0:T(8,128)(2,1)S(1)} %get-tuple-element.22), channel_id=1, source_target_pairs={{0,24},{8,16},{16,8},{24,0},{1,25},{9,17},{17,9},{25,1},{2,26},{10... | collective-permute-start | bytes 196616 | tf_op jit(solution)/shard_map/ppermute | solution.py:270
  27.8 4.6 %collective-permute-start.11 = (bf16[128,256]{1,0:T(8,128)(2,1)S(1)}, bf16[128,256]{1,0:T(8,128)(2,1)S(1)}, u32[]{:S(2)}, u32[]{:S(2)}) collective-permute-start(bf16[128,256]{1,0:T(8,128)(2,1)S(1)} %get-tuple-element.23), channel_id=1, source_target_pairs={{0,16},{8,24},{16,0},{24,8},{1,17},{9,25},{17,1},{25,9},{2,18},{10... | collective-permute-start | bytes 196616 | tf_op jit(solution)/shard_map/ppermute | solution.py:270
  29.1 4.3 %collective-permute-start.12 = (bf16[128,256]{1,0:T(8,128)(2,1)S(1)}, bf16[128,256]{1,0:T(8,128)(2,1)S(1)}, u32[]{:S(2)}, u32[]{:S(2)}) collective-permute-start(bf16[128,256]{1,0:T(8,128)(2,1)S(1)} %get-tuple-element.24), channel_id=1, source_target_pairs={{0,8},{8,0},{16,24},{24,16},{1,9},{9,1},{17,25},{25,17},{2,10},{10... | collective-permute-start | bytes 196616 | tf_op jit(solution)/shard_map/ppermute | solution.py:270
  34.5 1.6 %collective-permute-start.13 = (bf16[4,64,512]{2,1,0:T(8,128)(2,1)S(1)}, bf16[4,64,512]{2,1,0:T(8,128)(2,1)S(1)}, u32[]{:S(2)}, u32[]{:S(2)}) collective-permute-start(bf16[4,64,512]{2,1,0:T(8,128)(2,1)S(1)} %shard_map.59), channel_id=1, source_target_pairs={{0,1},{1,0},{2,3},{3,2},{4,5},{5,4},{6,7},{7,6},{8,9},{9,8},{10,11... | collective-permute-start | bytes 786440 | tf_op jit(solution)/shard_map/ppermute | solution.py:270
  36.2 6.8 %collective-permute-start.14 = (bf16[64,512]{1,0:T(8,128)(2,1)S(1)}, bf16[64,512]{1,0:T(8,128)(2,1)S(1)}, u32[]{:S(2)}, u32[]{:S(2)}) collective-permute-start(bf16[64,512]{1,0:T(8,128)(2,1)S(1)} %get-tuple-element.26), channel_id=1, source_target_pairs={{0,6},{1,7},{2,4},{3,5},{4,2},{5,3},{6,0},{7,1},{8,14},{9,15},{10,... | collective-permute-start | bytes 196616 | tf_op jit(solution)/shard_map/ppermute | solution.py:270
  38.9 6.1 %collective-permute-start.15 = (bf16[64,512]{1,0:T(8,128)(2,1)S(1)}, bf16[64,512]{1,0:T(8,128)(2,1)S(1)}, u32[]{:S(2)}, u32[]{:S(2)}) collective-permute-start(bf16[64,512]{1,0:T(8,128)(2,1)S(1)} %get-tuple-element.27), channel_id=1, source_target_pairs={{0,4},{1,5},{2,6},{3,7},{4,0},{5,1},{6,2},{7,3},{8,12},{9,13},{10,... | collective-permute-start | bytes 196616 | tf_op jit(solution)/shard_map/ppermute | solution.py:270
  38.9 6.1 %collective-permute-start.16 = (bf16[64,512]{1,0:T(8,128)(2,1)S(1)}, bf16[64,512]{1,0:T(8,128)(2,1)S(1)}, u32[]{:S(2)}, u32[]{:S(2)}) collective-permute-start(bf16[64,512]{1,0:T(8,128)(2,1)S(1)} %get-tuple-element.28), channel_id=1, source_target_pairs={{0,2},{1,3},{2,0},{3,1},{4,6},{5,7},{6,4},{7,5},{8,10},{9,11},{10,... | collective-permute-start | bytes 196616 | tf_op jit(solution)/shard_map/ppermute | solution.py:270

commit v4 on v3

--- a/solution.py
+++ b/solution.py
@@ -76,21 +76,24 @@
     return pltpu.VMEM((lanes // LANES, rows, LANES), F32)
 
 
-def call(kernel, out_shape, n_in, scratch=(), limit=24, flops=0, size=0):
+def call(kernel, out_shape, n_in, scratch=(), limit=24, flops=0, size=0, more=(), result=pltpu.VMEM):
     whole = pl.BlockSpec(memory_space=pltpu.VMEM)
     return pl.pallas_call(
         kernel,
         out_shape=out_shape,
-        in_specs=[whole] * n_in,
-        out_specs=jax.tree.map(lambda _: whole, out_shape),
+        in_specs=[whole] * n_in + [pl.BlockSpec(memory_space=place) for place in more],
+        out_specs=jax.tree.map(lambda _: pl.BlockSpec(memory_space=result), out_shape),
         scratch_shapes=list(scratch),
         compiler_params=pltpu.CompilerParams(vmem_limit_bytes=limit * MIB),
         cost_estimate=pl.CostEstimate(flops=flops, bytes_accessed=size, transcendentals=0),
     )
 
 
-def edge_kernel(per_block, orb_ref, edge_ref):
-    local_k = orb_ref.shape[0]
+def edge_kernel(per_block, orb_hbm, edge_ref, orb_ref, sems):
+    local_k = orb_hbm.shape[0]
+    copies = [pltpu.make_async_copy(orb_hbm.at[k], orb_ref.at[k], sems.at[k]) for k in range(local_k)]
+    for copy in copies:
+        copy.start()
     row = lax.broadcasted_iota(jnp.int32, (2 * per_block, LANES), 0)
     lane = lax.broadcasted_iota(jnp.int32, (2 * per_block, LANES), 1)
     one, zero = jnp.ones(row.shape, F32), jnp.zeros(row.shape, F32)
@@ -100,6 +103,7 @@
     for g in range(local_k // group):
         rows = []
         for k in range(g * group, (g + 1) * group):
+            copies[k].wait()
             rows.append(
                 dot(first, orb_ref[k, 0, :, :LANES], ((1,), (1,)))
                 + dot(second, orb_ref[k, 1, :, :LANES], ((1,), (1,)))
@@ -107,9 +111,21 @@
         edge_ref[g * ROWS : (g + 1) * ROWS] = jnp.concatenate(rows, axis=0).astype(BF16)
 
 
+def coulomb_kernel(shares, coulomb_ref, edge_ref, _, out_ref, own_ref, wide):
+    cells, columns, points = coulomb_ref.shape
+    share = columns // shares
+    me = lax.axis_index("ka")
+    own_ref[...] = edge_ref[...]
+    wide[...] = coulomb_ref[...].astype(F32)
+    for s in range(shares):
+        start = pl.multiple_of(jnp.bitwise_xor(me, s) * share, share)
+        pieces = [wide[r, pl.ds(start, share), :] for r in range(cells)]
+        out_ref[s] = jnp.concatenate(pieces, axis=0).astype(BF16)
+
+
 def tile_kernel(shares, blocks, per_block, *refs):
     edges, orb_ref, sel_ref, coulomb_ref = refs[:blocks], refs[blocks], refs[blocks + 1], refs[blocks + 2]
-    outs, (form_ref, gathered, wide, cells) = refs[blocks + 3 : blocks + 3 + shares], refs[blocks + 3 + shares :]
+    outs, (form_ref, gathered, wide) = refs[blocks + 3 : blocks + 3 + shares], refs[blocks + 3 + shares :]
     local_k, _, norb, points = orb_ref.shape
     group = ROWS // (2 * per_block)
     total = blocks * per_block
@@ -117,7 +133,6 @@
     rows = 2 * total
     me = lax.axis_index("ka")
     block = lax.axis_index("pts")
-    cells[...] = coulomb_ref[...].astype(F32)
     for s in range(blocks):
         gathered[jnp.bitwise_xor(block, s)] = edges[s][...]
     for g in range(local_k // group):
@@ -141,9 +156,7 @@
     for s in range(shares):
         dest = jnp.bitwise_xor(me, s)
         outs[s][:size] = take(wide, pl.multiple_of(dest * size, size), size).astype(BF16)
-        start = pl.multiple_of(dest * share, share)
-        pair = [cells[r, pl.ds(start, share), :] for r in range(local_k)]
-        outs[s][size:] = jnp.concatenate(pair, axis=0).astype(BF16)
+        outs[s][size:] = coulomb_ref[s]
 
 
 def transform_kernel(shares, total, share, *refs):
@@ -228,7 +241,8 @@
 
 
 def exchange_kernel(chunks, scale, *refs):
-    pieces, form_ref, out_ref, wide = refs[:chunks][::-1], refs[chunks], refs[chunks + 1], refs[chunks + 2]
+    pieces, form_ref, out_hbm = refs[:chunks][::-1], refs[chunks], refs[chunks + 1]
+    wide, out_ref, sems = refs[chunks + 2 :]
     local_k, lanes, twice = form_ref.shape
     norb = twice // 2
     spans = norb // LANES
@@ -243,6 +257,7 @@
     width = group * lanes
     lane = lax.broadcasted_iota(jnp.int32, (out_rows, width), 1)
     zero = jnp.zeros((out_rows, width), BF16)
+    copies = []
     for g in range(local_k // group):
         high_g = high[:, g * width : (g + 1) * width]
         low_g = low[:, g * width : (g + 1) * width]
@@ -255,14 +270,17 @@
         forms = [form_ref[g * group + kk] for kk in range(group)]
         result = dot(jnp.concatenate(left, axis=0), jnp.concatenate(forms + forms, axis=0))
         for kk in range(group):
-            k = g * group + kk
             for part in range(2):
                 for t in range(spans):
                     lane_start = part * norb + t * LANES
                     value = result[kk * out_rows : (kk + 1) * out_rows, lane_start : lane_start + LANES]
-                    start = (k * spans + t) * 2 + part
-                    wide[pl.ds(start, out_rows, stride=2 * spans * local_k), :] = value
-    out_ref[...] = wide[...].astype(BF16)
+                    start = (kk * spans + t) * 2 + part
+                    wide[g, pl.ds(start, out_rows, stride=2 * spans * group), :] = value
+        out_ref[g] = wide[g].astype(BF16).reshape(out_ref.shape[1:])
+        copies.append(pltpu.make_async_copy(out_ref.at[g], out_hbm.at[:, g], sems.at[g]))
+        copies[-1].start()
+    for copy in copies:
+        copy.wait()
 
 
 def swap(value, axis, mask):
@@ -289,14 +307,26 @@
     edge = call(
         functools.partial(edge_kernel, per_block),
         shape((local_k * 2 * per_block, norb), BF16),
-        1,
+        0,
+        [pltpu.VMEM(orbitals.shape, BF16), pltpu.SemaphoreType.DMA((local_k,))],
+        limit=57,
         size=4 * MIB,
+        more=[pltpu.HBM],
     )(orbitals)
     edges = [edge] + [None] * (blocks - 1)
     for s in range(1, chunks):
         edges[2 * s] = swap(edge, "pts", 2 * s)
     for s in range(chunks):
         edges[2 * s + 1] = swap(edges[2 * s], "pts", 1)
+
+    coulombs, edges[0] = call(
+        functools.partial(coulomb_kernel, shares),
+        [shape((shares, local_k * share, points), BF16), shape(edge.shape, BF16)],
+        2,
+        [pltpu.VMEM(coulomb.shape, F32)],
+        size=1 * MIB,
+        more=[pl.ANY],
+    )(coulomb, edge, edges[1])
 
     selector = jnp.asarray(column_selector(group, blocks, per_block, shares))
     piece = shape((share * 2 * local_k, points), BF16)
@@ -308,10 +338,9 @@
         [
             pltpu.VMEM((blocks, local_k * 2 * per_block, norb), BF16),
             tiled(columns * 2 * local_k, points),
-            pltpu.VMEM((local_k, columns, points), F32),
         ],
         size=8 * MIB,
-    )(*edges, orbitals, selector, coulomb)
+    )(*edges, orbitals, selector, coulombs)
     tiles = trade(tiles, "ka", 1)
 
     forward, backward = phase_tables(total)
@@ -349,13 +378,19 @@
     )(halves[1], came)
     sums = trade([own_sum, *sums], "pts", 2)
     spans = norb // LANES
-    rows = out_rows * local_k * spans * 2
+    pair = max(1, LANES // (2 * columns))
+    rows = pair * spans * 2
     result = call(
         functools.partial(exchange_kernel, chunks, 1.0 / math.sqrt(points * blocks)),
-        shape((rows, LANES), BF16),
+        shape((out_rows, local_k // pair, rows, LANES), BF16),
         chunks + 1,
-        [pltpu.VMEM((rows, LANES), F32)],
+        [
+            pltpu.VMEM((local_k // pair, out_rows * rows, LANES), F32),
+            pltpu.VMEM((local_k // pair, out_rows, rows, LANES), BF16),
+            pltpu.SemaphoreType.DMA((local_k // pair,)),
+        ],
         size=4 * MIB,
+        result=pltpu.HBM,
     )(*sums, forms)
     result = result.reshape(out_rows, local_k, spans, 2, LANES)
     return result.transpose(0, 1, 3, 2, 4).reshape(out_rows, local_k, 2, norb)

time: 47.8 us -> 47.6 us (level)
  Pallas kernels: 7.6 us -> 9.42 us
  local copies, waits for them, and re-layouts: 3.11 us -> 1.76 us
  waiting for transfers between devices: 19.1 us -> 18.2 us
    pallas_call x1, Pallas kernels: 0.64 us -> 3.37 us  [body(): call(functools.partial(edge_kernel, per_block), shape((local_k * 2 * per_...]
    unnamed x12, local copies, waits for them, and re-layouts: 3.11 us -> 1.76 us
    pallas_call x1, Pallas kernels: 2.61 us -> 1.66 us  [body(): call(functools.partial(exchange_kernel, chunks, 1.0 / math.sqrt(points *...]
    ppermute x17, waiting for transfers between devices: 19.1 us -> 18.2 us  [swap(): return lax.ppermute(value, axis, [(i, i ^ mask) for i in range(size)])]
  transfers between devices with their start and end apart: 17 -> 17, of which waited for: 13 -> 11; matrix products, arithmetic and copies ran while one was open for 0% -> 0% of each run, Pallas kernels for 2% -> 3%
where the time goes in v4:
time: 47.6 us; the launch traced here: 47.4 us
  waiting for transfers between devices  18.2 us (38%)
  starting transfers between devices  17.9 us (38%)
  Pallas kernels  9.42 us (20%)
  local copies, waits for them, and re-layouts  1.76 us (4%)
    ppermute x17, waiting for transfers between devices, swap(): return lax.ppermute(value, axis, [(i, i ^ mask) for i in range(size)])  18.2 us
    ppermute x17, starting transfers between devices, swap(): return lax.ppermute(value, axis, [(i, i ^ mask) for i in range(size)])  17.9 us
    pallas_call x1, Pallas kernels, body(): call(functools.partial(edge_kernel, per_block), shape((local_k * 2 * per_...  3.37 us
    pallas_call x2, Pallas kernels, body(): call(functools.partial(weight_kernel, shares, flip, out_rows), shape((chu...  2.33 us
    unnamed x12, local copies, waits for them, and re-layouts  1.76 us
    pallas_call x1, Pallas kernels, body(): call(functools.partial(exchange_kernel, chunks, 1.0 / math.sqrt(points *...  1.66 us
    pallas_call x1, Pallas kernels, body(): call(functools.partial(tile_kernel, shares, blocks, per_block), [both] *...  1.39 us
  transfers between devices with their start and end apart: 17, of which 11 were waited for; matrix products, arithmetic and copies ran while one was open for 0% of the time, Pallas kernels for 3%

profile of v4, /device:TPU:0, one launch (start us, length us, event | category | flops | bytes accessed | tf_op | source)
XLA Modules:
  0.0 47.4 jit_solution(6806910317143803390)
XLA Ops:
  0.0 3.4 %shard_map.55.edge_ref = bf16[64,512]{1,0:T(8,128)(2,1)} custom-call(bf16[8,2,512,256]{3,2,1,0:T(8,128)(2,1)} %refs_4_.4), custom_call_target="tpu_custom_call" | custom-call | bytes 4194304 | tf_op jit(solution)/shard_map/pallas_call | solution.py:307
  3.4 5.1 %collective-permute-start.5 = (bf16[64,512]{1,0:T(8,128)(2,1)}, bf16[64,512]{1,0:T(8,128)(2,1)S(1)}, u32[]{:S(2)}, u32[]{:S(2)}) collective-permute-start(bf16[64,512]{1,0:T(8,128)(2,1)} %shard_map.55.edge_ref), channel_id=1, source_target_pairs={{0,6},{1,7},{2,4},{3,5},{4,2},{5,3},{6,0},{7,1},{8,14},{9,15},{10,... | collective-permute-start | bytes 196616 | tf_op jit(solution)/shard_map/ppermute | solution.py:288
  8.5 0.6 %collective-permute-start.1 = (bf16[64,512]{1,0:T(8,128)(2,1)}, bf16[64,512]{1,0:T(8,128)(2,1)S(1)}, u32[]{:S(2)}, u32[]{:S(2)}) collective-permute-start(bf16[64,512]{1,0:T(8,128)(2,1)} %shard_map.55.edge_ref), channel_id=1, source_target_pairs={{0,2},{1,3},{2,0},{3,1},{4,6},{5,7},{6,4},{7,5},{8,10},{9,11},{10,... | collective-permute-start | bytes 196616 | tf_op jit(solution)/shard_map/ppermute | solution.py:288
  9.1 0.0 collective-permute-start
  9.1 2.2 %collective-permute-done.5.refs_6_ = bf16[64,512]{1,0:T(8,128)(2,1)S(1)} collective-permute-done((bf16[64,512]{1,0:T(8,128)(2,1)}, bf16[64,512]{1,0:T(8,128)(2,1)S(1)}, u32[]{:S(2)}, u32[]{:S(2)}) %collective-permute-start.5) | collective-permute-done | bytes 65568 | tf_op jit(solution)/shard_map/ppermute | solution.py:288
  11.3 3.0 %collective-permute-done.3.refs_4_ = bf16[64,512]{1,0:T(8,128)(2,1)S(1)} collective-permute-done((bf16[64,512]{1,0:T(8,128)(2,1)}, bf16[64,512]{1,0:T(8,128)(2,1)S(1)}, u32[]{:S(2)}, u32[]{:S(2)}) %collective-permute-start.3) | collective-permute-done | bytes 65568 | tf_op jit(solution)/shard_map/ppermute | solution.py:288
  14.3 0.5 %collective-permute-start.2 = (bf16[64,512]{1,0:T(8,128)(2,1)S(1)}, bf16[64,512]{1,0:T(8,128)(2,1)S(1)}, u32[]{:S(2)}, u32[]{:S(2)}) collective-permute-start(bf16[64,512]{1,0:T(8,128)(2,1)S(1)} %collective-permute-done.1.refs_2_), channel_id=1, source_target_pairs={{0,1},{1,0},{2,3},{3,2},{4,5},{5,4},{6,7},{7,6},{8,9},{9,8},{10,11... | collective-permute-start | bytes 196616 | tf_op jit(solution)/shard_map/ppermute | solution.py:288
  14.8 0.8 %copy-done.1 = bf16[64,512]{1,0:T(8,128)(2,1)S(1)} copy-done((bf16[64,512]{1,0:T(8,128)(2,1)S(1)}, bf16[64,512]{1,0:T(8,128)(2,1)}, u32[]{:S(2)}) %copy-start.1) | copy-done | bytes 65560
  15.7 0.9 %copy-done.2 = bf16[8,32,256]{2,1,0:T(8,128)(2,1)S(1)} copy-done((bf16[8,32,256]{2,1,0:T(8,128)(2,1)S(1)}, bf16[8,32,256]{2,1,0:T(8,128)(2,1)}, u32[]{:S(2)}) %copy-start.2) | copy-done | bytes 131096
  16.7 1.4 %shard_map.57 = (bf16[192,256]{1,0:T(8,128)(2,1)S(1)}, bf16[192,256]{1,0:T(8,128)(2,1)S(1)}, bf16[192,256]{1,0:T(8,128)(2,1)S(1)}, bf16[192,256]{1,0:T(8,128)(2,1)S(1)}, bf16[8,64,1024]{2,1,0:T(8,128)(2,1)S(1)}) custom-call(bf16[64,512]{1,0:T(8,128)(2,1)S(1)} %get-tuple-element.20.refs_0_, bf16[64,512]{1,0:T(8,128)(2,1)S(1)} %collective-permute-done._.refs_1_, ...), custom_call_target="tpu_custom_call" | custom-call | bytes 8388608 | tf_op jit(solution)/shard_map/pallas_call | solution.py:334
  18.1 2.5 %collective-permute-start.7 = (bf16[192,256]{1,0:T(8,128)(2,1)S(1)}, bf16[192,256]{1,0:T(8,128)(2,1)S(1)}, u32[]{:S(2)}, u32[]{:S(2)}) collective-permute-start(bf16[192,256]{1,0:T(8,128)(2,1)S(1)} %get-tuple-element.22), channel_id=1, source_target_pairs={{0,24},{8,16},{16,8},{24,0},{1,25},{9,17},{17,9},{25,1},{2,26},{10... | collective-permute-start | bytes 294920 | tf_op jit(solution)/shard_map/ppermute | solution.py:288
  20.6 0.5 %collective-permute-start.8 = (bf16[192,256]{1,0:T(8,128)(2,1)S(1)}, bf16[192,256]{1,0:T(8,128)(2,1)S(1)}, u32[]{:S(2)}, u32[]{:S(2)}) collective-permute-start(bf16[192,256]{1,0:T(8,128)(2,1)S(1)} %get-tuple-element.23), channel_id=1, source_target_pairs={{0,16},{8,24},{16,0},{24,8},{1,17},{9,25},{17,1},{25,9},{2,18},{10... | collective-permute-start | bytes 294920 | tf_op jit(solution)/shard_map/ppermute | solution.py:288
  21.1 0.5 %collective-permute-start.9 = (bf16[192,256]{1,0:T(8,128)(2,1)S(1)}, bf16[192,256]{1,0:T(8,128)(2,1)S(1)}, u32[]{:S(2)}, u32[]{:S(2)}) collective-permute-start(bf16[192,256]{1,0:T(8,128)(2,1)S(1)} %get-tuple-element.24), channel_id=1, source_target_pairs={{0,8},{8,0},{16,24},{24,16},{1,9},{9,1},{17,25},{25,17},{2,10},{10... | collective-permute-start | bytes 294920 | tf_op jit(solution)/shard_map/ppermute | solution.py:288
  21.6 2.2 %collective-permute-done.7.refs_0_ = bf16[192,256]{1,0:T(8,128)(2,1)S(1)} collective-permute-done((bf16[192,256]{1,0:T(8,128)(2,1)S(1)}, bf16[192,256]{1,0:T(8,128)(2,1)S(1)}, u32[]{:S(2)}, u32[]{:S(2)}) %collective-permute-start.7) | collective-permute-done | bytes 98336 | tf_op jit(solution)/shard_map/ppermute | solution.py:288
  23.8 2.0 %collective-permute-done.8.refs_1_ = bf16[192,256]{1,0:T(8,128)(2,1)S(1)} collective-permute-done((bf16[192,256]{1,0:T(8,128)(2,1)S(1)}, bf16[192,256]{1,0:T(8,128)(2,1)S(1)}, u32[]{:S(2)}, u32[]{:S(2)}) %collective-permute-start.8) | collective-permute-done | bytes 98336 | tf_op jit(solution)/shard_map/ppermute | solution.py:288
  25.8 0.1 collective-permute-done.9.refs_2_
  25.9 0.6 %shard_map.58 = (bf16[128,256]{1,0:T(8,128)(2,1)S(1)}, bf16[128,256]{1,0:T(8,128)(2,1)S(1)}, bf16[128,256]{1,0:T(8,128)(2,1)S(1)}, bf16[128,256]{1,0:T(8,128)(2,1)S(1)}) custom-call(bf16[192,256]{1,0:T(8,128)(2,1)S(1)} %collective-permute-done.7.refs_0_, bf16[192,256]{1,0:T(8,128)(2,1)S(1)} %collective-permute-done.8.refs_1_, ...), custom_call_target="tpu_custom_call" | custom-call | bytes 2097152 | tf_op jit(solution)/shard_map/pallas_call | solution.py:347
  26.5 1.8 %collective-permute-start.10 = (bf16[128,256]{1,0:T(8,128)(2,1)S(1)}, bf16[128,256]{1,0:T(8,128)(2,1)S(1)}, u32[]{:S(2)}, u32[]{:S(2)}) collective-permute-start(bf16[128,256]{1,0:T(8,128)(2,1)S(1)} %get-tuple-element.26), channel_id=1, source_target_pairs={{0,24},{8,16},{16,8},{24,0},{1,25},{9,17},{17,9},{25,1},{2,26},{10... | collective-permute-start | bytes 196616 | tf_op jit(solution)/shard_map/ppermute | solution.py:288
  28.3 1.3 %collective-permute-start.11 = (bf16[128,256]{1,0:T(8,128)(2,1)S(1)}, bf16[128,256]{1,0:T(8,128)(2,1)S(1)}, u32[]{:S(2)}, u32[]{:S(2)}) collective-permute-start(bf16[128,256]{1,0:T(8,128)(2,1)S(1)} %get-tuple-element.27), channel_id=1, source_target_pairs={{0,16},{8,24},{16,0},{24,8},{1,17},{9,25},{17,1},{25,9},{2,18},{10... | collective-permute-start | bytes 196616 | tf_op jit(solution)/shard_map/ppermute | solution.py:288
  29.6 0.5 %collective-permute-start.12 = (bf16[128,256]{1,0:T(8,128)(2,1)S(1)}, bf16[128,256]{1,0:T(8,128)(2,1)S(1)}, u32[]{:S(2)}, u32[]{:S(2)}) collective-permute-start(bf16[128,256]{1,0:T(8,128)(2,1)S(1)} %get-tuple-element.28), channel_id=1, source_target_pairs={{0,8},{8,0},{16,24},{24,16},{1,9},{9,1},{17,25},{25,17},{2,10},{10... | collective-permute-start | bytes 196616 | tf_op jit(solution)/shard_map/ppermute | solution.py:288
  30.1 2.1 %collective-permute-done.10.refs_0_ = bf16[128,256]{1,0:T(8,128)(2,1)S(1)} collective-permute-done((bf16[128,256]{1,0:T(8,128)(2,1)S(1)}, bf16[128,256]{1,0:T(8,128)(2,1)S(1)}, u32[]{:S(2)}, u32[]{:S(2)}) %collective-permute-start.10) | collective-permute-done | bytes 65568 | tf_op jit(solution)/shard_map/ppermute | solution.py:288
  32.2 0.5 %collective-permute-done.11.refs_1_ = bf16[128,256]{1,0:T(8,128)(2,1)S(1)} collective-permute-done((bf16[128,256]{1,0:T(8,128)(2,1)S(1)}, bf16[128,256]{1,0:T(8,128)(2,1)S(1)}, u32[]{:S(2)}, u32[]{:S(2)}) %collective-permute-start.11) | collective-permute-done | bytes 65568 | tf_op jit(solution)/shard_map/ppermute | solution.py:288
  32.7 1.1 %collective-permute-done.12.refs_2_ = bf16[128,256]{1,0:T(8,128)(2,1)S(1)} collective-permute-done((bf16[128,256]{1,0:T(8,128)(2,1)S(1)}, bf16[128,256]{1,0:T(8,128)(2,1)S(1)}, u32[]{:S(2)}, u32[]{:S(2)}) %collective-permute-start.12) | collective-permute-done | bytes 65568 | tf_op jit(solution)/shard_map/ppermute | solution.py:288
  33.8 1.2 %shard_map.60 = bf16[4,64,512]{2,1,0:T(8,128)(2,1)S(1)} custom-call(bf16[128,256]{1,0:T(8,128)(2,1)S(1)} %collective-permute-done.10.refs_0_, bf16[128,256]{1,0:T(8,128)(2,1)S(1)} %collective-permute-done.11.refs_1_, bf16[128,256]{1,0:T(8,128)(2,1)S(1)} %collective-permute-done.12.refs_2_, bf16[128,256]{1,0:T(8,128)(2,1)S(1)} %get-tuple-element.29.refs_3_, ...), custom_call_target="tpu_custom_call" | custom-call | bytes 6291456 | tf_op jit(solution)/shard_map/pallas_call | solution.py:364
  35.0 0.1 collective-permute-start.13
  35.1 1.2 %shard_map.59.keep_ref = f32[4,64,512]{2,1,0:T(8,128)S(1)} custom-call(bf16[128,256]{1,0:T(8,128)(2,1)S(1)} %collective-permute-done.10.refs_0_, bf16[128,256]{1,0:T(8,128)(2,1)S(1)} %collective-permute-done.11.refs_1_, bf16[128,256]{1,0:T(8,128)(2,1)S(1)} %collective-permute-done.12.refs_2_, bf16[128,256]{1,0:T(8,128)(2,1)S(1)} %get-tuple-element.29.refs_3_, ...), custom_call_target="tpu_custom_call" | custom-call | bytes 6291456 | tf_op jit(solution)/shard_map/pallas_call | solution.py:364
  36.3 0.4 collective-permute-done.13.came_ref
  36.7 2.8 %collective-permute-start.14 = (bf16[64,512]{1,0:T(8,128)(2,1)S(1)}, bf16[64,512]{1,0:T(8,128)(2,1)S(1)}, u32[]{:S(2)}, u32[]{:S(2)}) collective-permute-start(bf16[64,512]{1,0:T(8,128)(2,1)S(1)} %get-tuple-element.30), channel_id=1, source_target_pairs={{0,6},{1,7},{2,4},{3,5},{4,2},{5,3},{6,0},{7,1},{8,14},{9,15},{10,... | collective-permute-start | bytes 196616 | tf_op jit(solution)/shard_map/ppermute | solution.py:288
  39.5 1.7 %collective-permute-start.16 = (bf16[64,512]{1,0:T(8,128)(2,1)S(1)}, bf16[64,512]{1,0:T(8,128)(2,1)S(1)}, u32[]{:S(2)}, u32[]{:S(2)}) collective-permute-start(bf16[64,512]{1,0:T(8,128)(2,1)S(1)} %get-tuple-element.32), channel_id=1, source_target_pairs={{0,2},{1,3},{2,0},{3,1},{4,6},{5,7},{6,4},{7,5},{8,10},{9,11},{10,... | collective-permute-start | bytes 196616 | tf_op jit(solution)/shard_map/ppermute | solution.py:288
  41.1 2.4 %collective-permute-done.14.refs_0_ = bf16[64,512]{1,0:T(8,128)(2,1)S(1)} collective-permute-done((bf16[64,512]{1,0:T(8,128)(2,1)S(1)}, bf16[64,512]{1,0:T(8,128)(2,1)S(1)}, u32[]{:S(2)}, u32[]{:S(2)}) %collective-permute-start.14) | collective-permute-done | bytes 65568 | tf_op jit(solution)/shard_map/ppermute | solution.py:288
  43.5 2.2 %collective-permute-done.15.refs_1_ = bf16[64,512]{1,0:T(8,128)(2,1)S(1)} collective-permute-done((bf16[64,512]{1,0:T(8,128)(2,1)S(1)}, bf16[64,512]{1,0:T(8,128)(2,1)S(1)}, u32[]{:S(2)}, u32[]{:S(2)}) %collective-permute-start.15) | collective-permute-done | bytes 65568 | tf_op jit(solution)/shard_map/ppermute | solution.py:288
  45.7 1.7 %shard_map.62 = bf16[64,4,16,128]{3,2,1,0:T(8,128)(2,1)} custom-call(bf16[64,512]{1,0:T(8,128)(2,1)S(1)} %collective-permute-done.14.refs_0_, bf16[64,512]{1,0:T(8,128)(2,1)S(1)} %collective-permute-done.15.refs_1_, bf16[64,512]{1,0:T(8,128)(2,1)S(1)} %collective-permute-done.16.refs_2_, f32[64,512]{1,0:T(8,128)S(1)} %get-tuple-element.33.refs_3_, ...), custom_call_target="tpu_custom_call" | custom-call | bytes 4194304 | tf_op jit(solution)/shard_map/pallas_call | solution.py:383
  (22 shorter events, 0.1 us)
Async XLA Ops:
  0.0 16.7 %copy-start.3 = (bf16[256,128]{1,0:T(8,128)(2,1)S(1)}, bf16[256,128]{1,0:T(8,128)(2,1)}, u32[]{:S(2)}) copy-start(bf16[256,128]{1,0:T(8,128)(2,1)} %constant.6.clone.refs_9_) | copy-start | bytes 196612
  0.0 16.7 %copy-start = (bf16[8,2,512,256]{3,2,1,0:T(8,128)(2,1)S(1)}, bf16[8,2,512,256]{3,2,1,0:T(8,128)(2,1)}, u32[]{:S(2)}) copy-start(bf16[8,2,512,256]{3,2,1,0:T(8,128)(2,1)} %refs_4_.4) | copy-start | bytes 12582916
  3.4 7.9 %collective-permute-start.5 = (bf16[64,512]{1,0:T(8,128)(2,1)}, bf16[64,512]{1,0:T(8,128)(2,1)S(1)}, u32[]{:S(2)}, u32[]{:S(2)}) collective-permute-start(bf16[64,512]{1,0:T(8,128)(2,1)} %shard_map.55.edge_ref), channel_id=1, source_target_pairs={{0,6},{1,7},{2,4},{3,5},{4,2},{5,3},{6,0},{7,1},{8,14},{9,15},{10,... | collective-permute-start | bytes 196616 | tf_op jit(solution)/shard_map/ppermute | solution.py:288
  8.5 5.8 %collective-permute-start.3 = (bf16[64,512]{1,0:T(8,128)(2,1)}, bf16[64,512]{1,0:T(8,128)(2,1)S(1)}, u32[]{:S(2)}, u32[]{:S(2)}) collective-permute-start(bf16[64,512]{1,0:T(8,128)(2,1)} %shard_map.55.edge_ref), channel_id=1, source_target_pairs={{0,4},{1,5},{2,6},{3,7},{4,0},{5,1},{6,2},{7,3},{8,12},{9,13},{10,... | collective-permute-start | bytes 196616 | tf_op jit(solution)/shard_map/ppermute | solution.py:288
  8.5 5.8 %collective-permute-start.1 = (bf16[64,512]{1,0:T(8,128)(2,1)}, bf16[64,512]{1,0:T(8,128)(2,1)S(1)}, u32[]{:S(2)}, u32[]{:S(2)}) collective-permute-start(bf16[64,512]{1,0:T(8,128)(2,1)} %shard_map.55.edge_ref), channel_id=1, source_target_pairs={{0,2},{1,3},{2,0},{3,1},{4,6},{5,7},{6,4},{7,5},{8,10},{9,11},{10,... | collective-permute-start | bytes 196616 | tf_op jit(solution)/shard_map/ppermute | solution.py:288
  9.1 5.7 %collective-permute-start = (bf16[64,512]{1,0:T(8,128)(2,1)}, bf16[64,512]{1,0:T(8,128)(2,1)S(1)}, u32[]{:S(2)}, u32[]{:S(2)}) collective-permute-start(bf16[64,512]{1,0:T(8,128)(2,1)} %shard_map.55.edge_ref), channel_id=1, source_target_pairs={{0,1},{1,0},{2,3},{3,2},{4,5},{5,4},{6,7},{7,6},{8,9},{9,8},{10,11... | collective-permute-start | bytes 196616 | tf_op jit(solution)/shard_map/ppermute | solution.py:288
  11.3 5.3 %collective-permute-start.6 = (bf16[64,512]{1,0:T(8,128)(2,1)S(1)}, bf16[64,512]{1,0:T(8,128)(2,1)S(1)}, u32[]{:S(2)}, u32[]{:S(2)}) collective-permute-start(bf16[64,512]{1,0:T(8,128)(2,1)S(1)} %collective-permute-done.5.refs_6_), channel_id=1, source_target_pairs={{0,1},{1,0},{2,3},{3,2},{4,5},{5,4},{6,7},{7,6},{8,9},{9,8},{10,11... | collective-permute-start | bytes 196616 | tf_op jit(solution)/shard_map/ppermute | solution.py:288
  14.3 2.3 %collective-permute-start.4 = (bf16[64,512]{1,0:T(8,128)(2,1)S(1)}, bf16[64,512]{1,0:T(8,128)(2,1)S(1)}, u32[]{:S(2)}, u32[]{:S(2)}) collective-permute-start(bf16[64,512]{1,0:T(8,128)(2,1)S(1)} %collective-permute-done.3.refs_4_), channel_id=1, source_target_pairs={{0,1},{1,0},{2,3},{3,2},{4,5},{5,4},{6,7},{7,6},{8,9},{9,8},{10,11... | collective-permute-start | bytes 196616 | tf_op jit(solution)/shard_map/ppermute | solution.py:288
  14.3 2.3 %collective-permute-start.2 = (bf16[64,512]{1,0:T(8,128)(2,1)S(1)}, bf16[64,512]{1,0:T(8,128)(2,1)S(1)}, u32[]{:S(2)}, u32[]{:S(2)}) collective-permute-start(bf16[64,512]{1,0:T(8,128)(2,1)S(1)} %collective-permute-done.1.refs_2_), channel_id=1, source_target_pairs={{0,1},{1,0},{2,3},{3,2},{4,5},{5,4},{6,7},{7,6},{8,9},{9,8},{10,11... | collective-permute-start | bytes 196616 | tf_op jit(solution)/shard_map/ppermute | solution.py:288
  14.8 0.8 %copy-start.1 = (bf16[64,512]{1,0:T(8,128)(2,1)S(1)}, bf16[64,512]{1,0:T(8,128)(2,1)}, u32[]{:S(2)}) copy-start(bf16[64,512]{1,0:T(8,128)(2,1)} %shard_map.55.edge_ref) | copy-start | bytes 196612
  15.7 0.9 %copy-start.2 = (bf16[8,32,256]{2,1,0:T(8,128)(2,1)S(1)}, bf16[8,32,256]{2,1,0:T(8,128)(2,1)}, u32[]{:S(2)}) copy-start(bf16[8,32,256]{2,1,0:T(8,128)(2,1)} %coulomb_ref.1) | copy-start | bytes 393220
  16.6 9.3 %copy-start.4 = (bf16[64,128]{1,0:T(8,128)(2,1)S(1)}, bf16[64,128]{1,0:T(8,128)(2,1)}, u32[]{:S(2)}) copy-start(bf16[64,128]{1,0:T(8,128)(2,1)} %constant.8.clone.refs_5_) | copy-start | bytes 49156
  16.6 9.3 %copy-start.5 = (bf16[64,128]{1,0:T(8,128)(2,1)S(1)}, bf16[64,128]{1,0:T(8,128)(2,1)}, u32[]{:S(2)}) copy-start(bf16[64,128]{1,0:T(8,128)(2,1)} %constant.7.clone.refs_4_) | copy-start | bytes 49156
  18.1 5.8 %collective-permute-start.7 = (bf16[192,256]{1,0:T(8,128)(2,1)S(1)}, bf16[192,256]{1,0:T(8,128)(2,1)S(1)}, u32[]{:S(2)}, u32[]{:S(2)}) collective-permute-start(bf16[192,256]{1,0:T(8,128)(2,1)S(1)} %get-tuple-element.22), channel_id=1, source_target_pairs={{0,24},{8,16},{16,8},{24,0},{1,25},{9,17},{17,9},{25,1},{2,26},{10... | collective-permute-start | bytes 294920 | tf_op jit(solution)/shard_map/ppermute | solution.py:288
  20.6 5.3 %collective-permute-start.8 = (bf16[192,256]{1,0:T(8,128)(2,1)S(1)}, bf16[192,256]{1,0:T(8,128)(2,1)S(1)}, u32[]{:S(2)}, u32[]{:S(2)}) collective-permute-start(bf16[192,256]{1,0:T(8,128)(2,1)S(1)} %get-tuple-element.23), channel_id=1, source_target_pairs={{0,16},{8,24},{16,0},{24,8},{1,17},{9,25},{17,1},{25,9},{2,18},{10... | collective-permute-start | bytes 294920 | tf_op jit(solution)/shard_map/ppermute | solution.py:288
  21.1 4.8 %collective-permute-start.9 = (bf16[192,256]{1,0:T(8,128)(2,1)S(1)}, bf16[192,256]{1,0:T(8,128)(2,1)S(1)}, u32[]{:S(2)}, u32[]{:S(2)}) collective-permute-start(bf16[192,256]{1,0:T(8,128)(2,1)S(1)} %get-tuple-element.24), channel_id=1, source_target_pairs={{0,8},{8,0},{16,24},{24,16},{1,9},{9,1},{17,25},{25,17},{2,10},{10... | collective-permute-start | bytes 294920 | tf_op jit(solution)/shard_map/ppermute | solution.py:288
  26.5 5.7 %collective-permute-start.10 = (bf16[128,256]{1,0:T(8,128)(2,1)S(1)}, bf16[128,256]{1,0:T(8,128)(2,1)S(1)}, u32[]{:S(2)}, u32[]{:S(2)}) collective-permute-start(bf16[128,256]{1,0:T(8,128)(2,1)S(1)} %get-tuple-element.26), channel_id=1, source_target_pairs={{0,24},{8,16},{16,8},{24,0},{1,25},{9,17},{17,9},{25,1},{2,26},{10... | collective-permute-start | bytes 196616 | tf_op jit(solution)/shard_map/ppermute | solution.py:288
  28.3 4.4 %collective-permute-start.11 = (bf16[128,256]{1,0:T(8,128)(2,1)S(1)}, bf16[128,256]{1,0:T(8,128)(2,1)S(1)}, u32[]{:S(2)}, u32[]{:S(2)}) collective-permute-start(bf16[128,256]{1,0:T(8,128)(2,1)S(1)} %get-tuple-element.27), channel_id=1, source_target_pairs={{0,16},{8,24},{16,0},{24,8},{1,17},{9,25},{17,1},{25,9},{2,18},{10... | collective-permute-start | bytes 196616 | tf_op jit(solution)/shard_map/ppermute | solution.py:288
  29.6 4.3 %collective-permute-start.12 = (bf16[128,256]{1,0:T(8,128)(2,1)S(1)}, bf16[128,256]{1,0:T(8,128)(2,1)S(1)}, u32[]{:S(2)}, u32[]{:S(2)}) collective-permute-start(bf16[128,256]{1,0:T(8,128)(2,1)S(1)} %get-tuple-element.28), channel_id=1, source_target_pairs={{0,8},{8,0},{16,24},{24,16},{1,9},{9,1},{17,25},{25,17},{2,10},{10... | collective-permute-start | bytes 196616 | tf_op jit(solution)/shard_map/ppermute | solution.py:288
  35.0 1.6 %collective-permute-start.13 = (bf16[4,64,512]{2,1,0:T(8,128)(2,1)S(1)}, bf16[4,64,512]{2,1,0:T(8,128)(2,1)S(1)}, u32[]{:S(2)}, u32[]{:S(2)}) collective-permute-start(bf16[4,64,512]{2,1,0:T(8,128)(2,1)S(1)} %shard_map.60), channel_id=1, source_target_pairs={{0,1},{1,0},{2,3},{3,2},{4,5},{5,4},{6,7},{7,6},{8,9},{9,8},{10,11... | collective-permute-start | bytes 786440 | tf_op jit(solution)/shard_map/ppermute | solution.py:288
  36.7 6.8 %collective-permute-start.14 = (bf16[64,512]{1,0:T(8,128)(2,1)S(1)}, bf16[64,512]{1,0:T(8,128)(2,1)S(1)}, u32[]{:S(2)}, u32[]{:S(2)}) collective-permute-start(bf16[64,512]{1,0:T(8,128)(2,1)S(1)} %get-tuple-element.30), channel_id=1, source_target_pairs={{0,6},{1,7},{2,4},{3,5},{4,2},{5,3},{6,0},{7,1},{8,14},{9,15},{10,... | collective-permute-start | bytes 196616 | tf_op jit(solution)/shard_map/ppermute | solution.py:288
  39.5 6.3 %collective-permute-start.15 = (bf16[64,512]{1,0:T(8,128)(2,1)S(1)}, bf16[64,512]{1,0:T(8,128)(2,1)S(1)}, u32[]{:S(2)}, u32[]{:S(2)}) collective-permute-start(bf16[64,512]{1,0:T(8,128)(2,1)S(1)} %get-tuple-element.31), channel_id=1, source_target_pairs={{0,4},{1,5},{2,6},{3,7},{4,0},{5,1},{6,2},{7,3},{8,12},{9,13},{10,... | collective-permute-start | bytes 196616 | tf_op jit(solution)/shard_map/ppermute | solution.py:288
  39.5 6.3 %collective-permute-start.16 = (bf16[64,512]{1,0:T(8,128)(2,1)S(1)}, bf16[64,512]{1,0:T(8,128)(2,1)S(1)}, u32[]{:S(2)}, u32[]{:S(2)}) collective-permute-start(bf16[64,512]{1,0:T(8,128)(2,1)S(1)} %get-tuple-element.32), channel_id=1, source_target_pairs={{0,2},{1,3},{2,0},{3,1},{4,6},{5,7},{6,4},{7,5},{8,10},{9,11},{10,... | collective-permute-start | bytes 196616 | tf_op jit(solution)/shard_map/ppermute | solution.py:288

commit v5 on v4

--- a/solution.py
+++ b/solution.py
@@ -76,12 +76,12 @@
     return pltpu.VMEM((lanes // LANES, rows, LANES), F32)
 
 
-def call(kernel, out_shape, n_in, scratch=(), limit=24, flops=0, size=0, more=(), result=pltpu.VMEM):
+def call(kernel, out_shape, n_in, scratch=(), limit=24, flops=0, size=0, result=pltpu.VMEM):
     whole = pl.BlockSpec(memory_space=pltpu.VMEM)
     return pl.pallas_call(
         kernel,
         out_shape=out_shape,
-        in_specs=[whole] * n_in + [pl.BlockSpec(memory_space=place) for place in more],
+        in_specs=[whole] * n_in,
         out_specs=jax.tree.map(lambda _: pl.BlockSpec(memory_space=result), out_shape),
         scratch_shapes=list(scratch),
         compiler_params=pltpu.CompilerParams(vmem_limit_bytes=limit * MIB),
@@ -89,11 +89,10 @@
     )
 
 
-def edge_kernel(per_block, orb_hbm, edge_ref, orb_ref, sems):
-    local_k = orb_hbm.shape[0]
-    copies = [pltpu.make_async_copy(orb_hbm.at[k], orb_ref.at[k], sems.at[k]) for k in range(local_k)]
-    for copy in copies:
-        copy.start()
+def edge_kernel(per_block, shares, orb_ref, coulomb_ref, edge_ref, piece_ref, wide):
+    local_k = orb_ref.shape[0]
+    share = coulomb_ref.shape[1] // shares
+    me = lax.axis_index("ka")
     row = lax.broadcasted_iota(jnp.int32, (2 * per_block, LANES), 0)
     lane = lax.broadcasted_iota(jnp.int32, (2 * per_block, LANES), 1)
     one, zero = jnp.ones(row.shape, F32), jnp.zeros(row.shape, F32)
@@ -103,24 +102,16 @@
     for g in range(local_k // group):
         rows = []
         for k in range(g * group, (g + 1) * group):
-            copies[k].wait()
             rows.append(
                 dot(first, orb_ref[k, 0, :, :LANES], ((1,), (1,)))
                 + dot(second, orb_ref[k, 1, :, :LANES], ((1,), (1,)))
             )
         edge_ref[g * ROWS : (g + 1) * ROWS] = jnp.concatenate(rows, axis=0).astype(BF16)
-
-
-def coulomb_kernel(shares, coulomb_ref, edge_ref, _, out_ref, own_ref, wide):
-    cells, columns, points = coulomb_ref.shape
-    share = columns // shares
-    me = lax.axis_index("ka")
-    own_ref[...] = edge_ref[...]
     wide[...] = coulomb_ref[...].astype(F32)
     for s in range(shares):
         start = pl.multiple_of(jnp.bitwise_xor(me, s) * share, share)
-        pieces = [wide[r, pl.ds(start, share), :] for r in range(cells)]
-        out_ref[s] = jnp.concatenate(pieces, axis=0).astype(BF16)
+        pieces = [wide[r, pl.ds(start, share), :] for r in range(local_k)]
+        piece_ref[s] = jnp.concatenate(pieces, axis=0).astype(BF16)
 
 
 def tile_kernel(shares, blocks, per_block, *refs):
@@ -304,29 +295,21 @@
     group = ROWS // (2 * per_block)
     shape = jax.ShapeDtypeStruct
 
-    edge = call(
-        functools.partial(edge_kernel, per_block),
-        shape((local_k * 2 * per_block, norb), BF16),
-        0,
-        [pltpu.VMEM(orbitals.shape, BF16), pltpu.SemaphoreType.DMA((local_k,))],
-        limit=57,
+    edge, coulombs = call(
+        functools.partial(edge_kernel, per_block, shares),
+        [
+            shape((local_k * 2 * per_block, norb), BF16),
+            shape((shares, local_k * share, points), BF16),
+        ],
+        2,
+        [pltpu.VMEM(coulomb.shape, F32)],
         size=4 * MIB,
-        more=[pltpu.HBM],
-    )(orbitals)
+    )(orbitals, coulomb)
     edges = [edge] + [None] * (blocks - 1)
     for s in range(1, chunks):
         edges[2 * s] = swap(edge, "pts", 2 * s)
     for s in range(chunks):
         edges[2 * s + 1] = swap(edges[2 * s], "pts", 1)
-
-    coulombs, edges[0] = call(
-        functools.partial(coulomb_kernel, shares),
-        [shape((shares, local_k * share, points), BF16), shape(edge.shape, BF16)],
-        2,
-        [pltpu.VMEM(coulomb.shape, F32)],
-        size=1 * MIB,
-        more=[pl.ANY],
-    )(coulomb, edge, edges[1])
 
     selector = jnp.asarray(column_selector(group, blocks, per_block, shares))
     piece = shape((share * 2 * local_k, points), BF16)

time: 47.6 us -> 46.9 us (0.985)
  Pallas kernels: 9.42 us -> 6.67 us
  local copies, waits for them, and re-layouts: 1.76 us -> 3.11 us
  waiting for transfers between devices: 18.2 us -> 19 us
    pallas_call x2 -> x1, Pallas kernels: 3.41 us -> 0.66 us  [body(): call(functools.partial(edge_kernel, per_block, shares), [shape((local_k *...]
    unnamed x12, local copies, waits for them, and re-layouts: 1.76 us -> 3.11 us
    ppermute x17, waiting for transfers between devices: 18.2 us -> 19 us  [swap(): return lax.ppermute(value, axis, [(i, i ^ mask) for i in range(size)])]
  transfers between devices with their start and end apart: 17 -> 17, of which waited for: 11 -> 13; matrix products, arithmetic and copies ran while one was open for 0% -> 0% of each run, Pallas kernels for 3% -> 2%
where the time goes in v5:
time: 46.9 us; the launch traced here: 46.7 us
  waiting for transfers between devices  19 us (41%)
  starting transfers between devices  17.9 us (38%)
  Pallas kernels  6.67 us (14%)
  local copies, waits for them, and re-layouts  3.11 us (7%)
    ppermute x17, waiting for transfers between devices, swap(): return lax.ppermute(value, axis, [(i, i ^ mask) for i in range(size)])  19 us
    ppermute x17, starting transfers between devices, swap(): return lax.ppermute(value, axis, [(i, i ^ mask) for i in range(size)])  17.9 us
    unnamed x12, local copies, waits for them, and re-layouts  3.11 us
    pallas_call x2, Pallas kernels, body(): call(functools.partial(weight_kernel, shares, flip, out_rows), shape((chu...  2.33 us
    pallas_call x1, Pallas kernels, body(): call(functools.partial(exchange_kernel, chunks, 1.0 / math.sqrt(points *...  1.66 us
    pallas_call x1, Pallas kernels, body(): call(functools.partial(tile_kernel, shares, blocks, per_block), [both] *...  1.39 us
  transfers between devices with their start and end apart: 17, of which 13 were waited for; matrix products, arithmetic and copies ran while one was open for 0% of the time, Pallas kernels for 2%

profile of v5, /device:TPU:0, one launch (start us, length us, event | category | flops | bytes accessed | tf_op | source)
XLA Modules:
  0.0 46.7 jit_solution(8044003047579318651)
XLA Ops:
  0.0 2.2 %copy-done = bf16[8,2,512,256]{3,2,1,0:T(8,128)(2,1)S(1)} copy-done((bf16[8,2,512,256]{3,2,1,0:T(8,128)(2,1)S(1)}, bf16[8,2,512,256]{3,2,1,0:T(8,128)(2,1)}, u32[]{:S(2)}) %copy-start) | copy-done | bytes 4194328
  2.2 0.9 %copy-done.2 = bf16[8,32,256]{2,1,0:T(8,128)(2,1)S(1)} copy-done((bf16[8,32,256]{2,1,0:T(8,128)(2,1)S(1)}, bf16[8,32,256]{2,1,0:T(8,128)(2,1)}, u32[]{:S(2)}) %copy-start.2) | copy-done | bytes 131096
  3.1 0.7 %shard_map.55 = (bf16[64,512]{1,0:T(8,128)(2,1)S(1)}, bf16[4,64,256]{2,1,0:T(8,128)(2,1)S(1)}) custom-call(bf16[8,2,512,256]{3,2,1,0:T(8,128)(2,1)S(1)} %copy-done, bf16[8,32,256]{2,1,0:T(8,128)(2,1)S(1)} %copy-done.2), custom_call_target="tpu_custom_call" | custom-call | bytes 4194304 | tf_op jit(solution)/shard_map/pallas_call | solution.py:298
  3.8 5.1 %collective-permute-start.5 = (bf16[64,512]{1,0:T(8,128)(2,1)S(1)}, bf16[64,512]{1,0:T(8,128)(2,1)S(1)}, u32[]{:S(2)}, u32[]{:S(2)}) collective-permute-start(bf16[64,512]{1,0:T(8,128)(2,1)S(1)} %get-tuple-element.20.refs_0_), channel_id=1, source_target_pairs={{0,6},{1,7},{2,4},{3,5},{4,2},{5,3},{6,0},{7,1},{8,14},{9,15},{10,... | collective-permute-start | bytes 196616 | tf_op jit(solution)/shard_map/ppermute | solution.py:279
  8.8 0.6 %collective-permute-start.1 = (bf16[64,512]{1,0:T(8,128)(2,1)S(1)}, bf16[64,512]{1,0:T(8,128)(2,1)S(1)}, u32[]{:S(2)}, u32[]{:S(2)}) collective-permute-start(bf16[64,512]{1,0:T(8,128)(2,1)S(1)} %get-tuple-element.20.refs_0_), channel_id=1, source_target_pairs={{0,2},{1,3},{2,0},{3,1},{4,6},{5,7},{6,4},{7,5},{8,10},{9,11},{10,... | collective-permute-start | bytes 196616 | tf_op jit(solution)/shard_map/ppermute | solution.py:279
  9.5 1.9 %collective-permute-done.5.refs_6_ = bf16[64,512]{1,0:T(8,128)(2,1)S(1)} collective-permute-done((bf16[64,512]{1,0:T(8,128)(2,1)S(1)}, bf16[64,512]{1,0:T(8,128)(2,1)S(1)}, u32[]{:S(2)}, u32[]{:S(2)}) %collective-permute-start.5) | collective-permute-done | bytes 65568 | tf_op jit(solution)/shard_map/ppermute | solution.py:279
  11.4 3.0 %collective-permute-done.3.refs_4_ = bf16[64,512]{1,0:T(8,128)(2,1)S(1)} collective-permute-done((bf16[64,512]{1,0:T(8,128)(2,1)S(1)}, bf16[64,512]{1,0:T(8,128)(2,1)S(1)}, u32[]{:S(2)}, u32[]{:S(2)}) %collective-permute-start.3) | collective-permute-done | bytes 65568 | tf_op jit(solution)/shard_map/ppermute | solution.py:279
  14.4 0.5 %collective-permute-start.2 = (bf16[64,512]{1,0:T(8,128)(2,1)S(1)}, bf16[64,512]{1,0:T(8,128)(2,1)S(1)}, u32[]{:S(2)}, u32[]{:S(2)}) collective-permute-start(bf16[64,512]{1,0:T(8,128)(2,1)S(1)} %collective-permute-done.1.refs_2_), channel_id=1, source_target_pairs={{0,1},{1,0},{2,3},{3,2},{4,5},{5,4},{6,7},{7,6},{8,9},{9,8},{10,11... | collective-permute-start | bytes 196616 | tf_op jit(solution)/shard_map/ppermute | solution.py:279
  15.0 0.7 %collective-permute-done.4.refs_5_ = bf16[64,512]{1,0:T(8,128)(2,1)S(1)} collective-permute-done((bf16[64,512]{1,0:T(8,128)(2,1)S(1)}, bf16[64,512]{1,0:T(8,128)(2,1)S(1)}, u32[]{:S(2)}, u32[]{:S(2)}) %collective-permute-start.4) | collective-permute-done | bytes 65568 | tf_op jit(solution)/shard_map/ppermute | solution.py:279
  15.7 0.2 collective-permute-done.2.refs_3_
  15.9 1.4 %shard_map.56 = (bf16[192,256]{1,0:T(8,128)(2,1)S(1)}, bf16[192,256]{1,0:T(8,128)(2,1)S(1)}, bf16[192,256]{1,0:T(8,128)(2,1)S(1)}, bf16[192,256]{1,0:T(8,128)(2,1)S(1)}, bf16[8,64,1024]{2,1,0:T(8,128)(2,1)S(1)}) custom-call(bf16[64,512]{1,0:T(8,128)(2,1)S(1)} %get-tuple-element.20.refs_0_, bf16[64,512]{1,0:T(8,128)(2,1)S(1)} %collective-permute-done.refs_1_, ...), custom_call_target="tpu_custom_call" | custom-call | bytes 8388608 | tf_op jit(solution)/shard_map/pallas_call | solution.py:317
  17.3 2.5 %collective-permute-start.7 = (bf16[192,256]{1,0:T(8,128)(2,1)S(1)}, bf16[192,256]{1,0:T(8,128)(2,1)S(1)}, u32[]{:S(2)}, u32[]{:S(2)}) collective-permute-start(bf16[192,256]{1,0:T(8,128)(2,1)S(1)} %get-tuple-element.22), channel_id=1, source_target_pairs={{0,24},{8,16},{16,8},{24,0},{1,25},{9,17},{17,9},{25,1},{2,26},{10... | collective-permute-start | bytes 294920 | tf_op jit(solution)/shard_map/ppermute | solution.py:279
  19.8 0.5 %collective-permute-start.8 = (bf16[192,256]{1,0:T(8,128)(2,1)S(1)}, bf16[192,256]{1,0:T(8,128)(2,1)S(1)}, u32[]{:S(2)}, u32[]{:S(2)}) collective-permute-start(bf16[192,256]{1,0:T(8,128)(2,1)S(1)} %get-tuple-element.23), channel_id=1, source_target_pairs={{0,16},{8,24},{16,0},{24,8},{1,17},{9,25},{17,1},{25,9},{2,18},{10... | collective-permute-start | bytes 294920 | tf_op jit(solution)/shard_map/ppermute | solution.py:279
  20.3 0.5 %collective-permute-start.9 = (bf16[192,256]{1,0:T(8,128)(2,1)S(1)}, bf16[192,256]{1,0:T(8,128)(2,1)S(1)}, u32[]{:S(2)}, u32[]{:S(2)}) collective-permute-start(bf16[192,256]{1,0:T(8,128)(2,1)S(1)} %get-tuple-element.24), channel_id=1, source_target_pairs={{0,8},{8,0},{16,24},{24,16},{1,9},{9,1},{17,25},{25,17},{2,10},{10... | collective-permute-start | bytes 294920 | tf_op jit(solution)/shard_map/ppermute | solution.py:279
  20.8 2.5 %collective-permute-done.7.refs_0_ = bf16[192,256]{1,0:T(8,128)(2,1)S(1)} collective-permute-done((bf16[192,256]{1,0:T(8,128)(2,1)S(1)}, bf16[192,256]{1,0:T(8,128)(2,1)S(1)}, u32[]{:S(2)}, u32[]{:S(2)}) %collective-permute-start.7) | collective-permute-done | bytes 98336 | tf_op jit(solution)/shard_map/ppermute | solution.py:279
  23.4 2.0 %collective-permute-done.8.refs_1_ = bf16[192,256]{1,0:T(8,128)(2,1)S(1)} collective-permute-done((bf16[192,256]{1,0:T(8,128)(2,1)S(1)}, bf16[192,256]{1,0:T(8,128)(2,1)S(1)}, u32[]{:S(2)}, u32[]{:S(2)}) %collective-permute-start.8) | collective-permute-done | bytes 98336 | tf_op jit(solution)/shard_map/ppermute | solution.py:279
  25.4 0.6 %shard_map.57 = (bf16[128,256]{1,0:T(8,128)(2,1)S(1)}, bf16[128,256]{1,0:T(8,128)(2,1)S(1)}, bf16[128,256]{1,0:T(8,128)(2,1)S(1)}, bf16[128,256]{1,0:T(8,128)(2,1)S(1)}) custom-call(bf16[192,256]{1,0:T(8,128)(2,1)S(1)} %collective-permute-done.7.refs_0_, bf16[192,256]{1,0:T(8,128)(2,1)S(1)} %collective-permute-done.8.refs_1_, ...), custom_call_target="tpu_custom_call" | custom-call | bytes 2097152 | tf_op jit(solution)/shard_map/pallas_call | solution.py:330
  26.0 1.8 %collective-permute-start.10 = (bf16[128,256]{1,0:T(8,128)(2,1)S(1)}, bf16[128,256]{1,0:T(8,128)(2,1)S(1)}, u32[]{:S(2)}, u32[]{:S(2)}) collective-permute-start(bf16[128,256]{1,0:T(8,128)(2,1)S(1)} %get-tuple-element.26), channel_id=1, source_target_pairs={{0,24},{8,16},{16,8},{24,0},{1,25},{9,17},{17,9},{25,1},{2,26},{10... | collective-permute-start | bytes 196616 | tf_op jit(solution)/shard_map/ppermute | solution.py:279
  27.8 1.3 %collective-permute-start.11 = (bf16[128,256]{1,0:T(8,128)(2,1)S(1)}, bf16[128,256]{1,0:T(8,128)(2,1)S(1)}, u32[]{:S(2)}, u32[]{:S(2)}) collective-permute-start(bf16[128,256]{1,0:T(8,128)(2,1)S(1)} %get-tuple-element.27), channel_id=1, source_target_pairs={{0,16},{8,24},{16,0},{24,8},{1,17},{9,25},{17,1},{25,9},{2,18},{10... | collective-permute-start | bytes 196616 | tf_op jit(solution)/shard_map/ppermute | solution.py:279
  29.1 0.5 %collective-permute-start.12 = (bf16[128,256]{1,0:T(8,128)(2,1)S(1)}, bf16[128,256]{1,0:T(8,128)(2,1)S(1)}, u32[]{:S(2)}, u32[]{:S(2)}) collective-permute-start(bf16[128,256]{1,0:T(8,128)(2,1)S(1)} %get-tuple-element.28), channel_id=1, source_target_pairs={{0,8},{8,0},{16,24},{24,16},{1,9},{9,1},{17,25},{25,17},{2,10},{10... | collective-permute-start | bytes 196616 | tf_op jit(solution)/shard_map/ppermute | solution.py:279
  29.6 2.1 %collective-permute-done.10.refs_0_ = bf16[128,256]{1,0:T(8,128)(2,1)S(1)} collective-permute-done((bf16[128,256]{1,0:T(8,128)(2,1)S(1)}, bf16[128,256]{1,0:T(8,128)(2,1)S(1)}, u32[]{:S(2)}, u32[]{:S(2)}) %collective-permute-start.10) | collective-permute-done | bytes 65568 | tf_op jit(solution)/shard_map/ppermute | solution.py:279
  31.7 0.7 %collective-permute-done.11.refs_1_ = bf16[128,256]{1,0:T(8,128)(2,1)S(1)} collective-permute-done((bf16[128,256]{1,0:T(8,128)(2,1)S(1)}, bf16[128,256]{1,0:T(8,128)(2,1)S(1)}, u32[]{:S(2)}, u32[]{:S(2)}) %collective-permute-start.11) | collective-permute-done | bytes 65568 | tf_op jit(solution)/shard_map/ppermute | solution.py:279
  32.4 1.0 %collective-permute-done.12.refs_2_ = bf16[128,256]{1,0:T(8,128)(2,1)S(1)} collective-permute-done((bf16[128,256]{1,0:T(8,128)(2,1)S(1)}, bf16[128,256]{1,0:T(8,128)(2,1)S(1)}, u32[]{:S(2)}, u32[]{:S(2)}) %collective-permute-start.12) | collective-permute-done | bytes 65568 | tf_op jit(solution)/shard_map/ppermute | solution.py:279
  33.4 1.2 %shard_map.59 = bf16[4,64,512]{2,1,0:T(8,128)(2,1)S(1)} custom-call(bf16[128,256]{1,0:T(8,128)(2,1)S(1)} %collective-permute-done.10.refs_0_, bf16[128,256]{1,0:T(8,128)(2,1)S(1)} %collective-permute-done.11.refs_1_, bf16[128,256]{1,0:T(8,128)(2,1)S(1)} %collective-permute-done.12.refs_2_, bf16[128,256]{1,0:T(8,128)(2,1)S(1)} %get-tuple-element.29.refs_3_, ...), custom_call_target="tpu_custom_call" | custom-call | bytes 6291456 | tf_op jit(solution)/shard_map/pallas_call | solution.py:347
  34.6 0.1 collective-permute-start.13
  34.6 1.2 %shard_map.58.keep_ref = f32[4,64,512]{2,1,0:T(8,128)S(1)} custom-call(bf16[128,256]{1,0:T(8,128)(2,1)S(1)} %collective-permute-done.10.refs_0_, bf16[128,256]{1,0:T(8,128)(2,1)S(1)} %collective-permute-done.11.refs_1_, bf16[128,256]{1,0:T(8,128)(2,1)S(1)} %collective-permute-done.12.refs_2_, bf16[128,256]{1,0:T(8,128)(2,1)S(1)} %get-tuple-element.29.refs_3_, ...), custom_call_target="tpu_custom_call" | custom-call | bytes 6291456 | tf_op jit(solution)/shard_map/pallas_call | solution.py:347
  35.8 0.4 collective-permute-done.13.came_ref
  36.2 2.8 %collective-permute-start.14 = (bf16[64,512]{1,0:T(8,128)(2,1)S(1)}, bf16[64,512]{1,0:T(8,128)(2,1)S(1)}, u32[]{:S(2)}, u32[]{:S(2)}) collective-permute-start(bf16[64,512]{1,0:T(8,128)(2,1)S(1)} %get-tuple-element.30), channel_id=1, source_target_pairs={{0,6},{1,7},{2,4},{3,5},{4,2},{5,3},{6,0},{7,1},{8,14},{9,15},{10,... | collective-permute-start | bytes 196616 | tf_op jit(solution)/shard_map/ppermute | solution.py:279
  39.0 1.7 %collective-permute-start.16 = (bf16[64,512]{1,0:T(8,128)(2,1)S(1)}, bf16[64,512]{1,0:T(8,128)(2,1)S(1)}, u32[]{:S(2)}, u32[]{:S(2)}) collective-permute-start(bf16[64,512]{1,0:T(8,128)(2,1)S(1)} %get-tuple-element.32), channel_id=1, source_target_pairs={{0,2},{1,3},{2,0},{3,1},{4,6},{5,7},{6,4},{7,5},{8,10},{9,11},{10,... | collective-permute-start | bytes 196616 | tf_op jit(solution)/shard_map/ppermute | solution.py:279
  40.7 2.3 %collective-permute-done.14.refs_0_ = bf16[64,512]{1,0:T(8,128)(2,1)S(1)} collective-permute-done((bf16[64,512]{1,0:T(8,128)(2,1)S(1)}, bf16[64,512]{1,0:T(8,128)(2,1)S(1)}, u32[]{:S(2)}, u32[]{:S(2)}) %collective-permute-start.14) | collective-permute-done | bytes 65568 | tf_op jit(solution)/shard_map/ppermute | solution.py:279
  43.0 2.0 %collective-permute-done.15.refs_1_ = bf16[64,512]{1,0:T(8,128)(2,1)S(1)} collective-permute-done((bf16[64,512]{1,0:T(8,128)(2,1)S(1)}, bf16[64,512]{1,0:T(8,128)(2,1)S(1)}, u32[]{:S(2)}, u32[]{:S(2)}) %collective-permute-start.15) | collective-permute-done | bytes 65568 | tf_op jit(solution)/shard_map/ppermute | solution.py:279
  45.1 1.7 %shard_map.61 = bf16[64,4,16,128]{3,2,1,0:T(8,128)(2,1)} custom-call(bf16[64,512]{1,0:T(8,128)(2,1)S(1)} %collective-permute-done.14.refs_0_, bf16[64,512]{1,0:T(8,128)(2,1)S(1)} %collective-permute-done.15.refs_1_, bf16[64,512]{1,0:T(8,128)(2,1)S(1)} %collective-permute-done.16.refs_2_, f32[64,512]{1,0:T(8,128)S(1)} %get-tuple-element.33.refs_3_, ...), custom_call_target="tpu_custom_call" | custom-call | bytes 4194304 | tf_op jit(solution)/shard_map/pallas_call | solution.py:366
  (21 shorter events, 0.1 us)
Async XLA Ops:
  0.0 2.2 %copy-start = (bf16[8,2,512,256]{3,2,1,0:T(8,128)(2,1)S(1)}, bf16[8,2,512,256]{3,2,1,0:T(8,128)(2,1)}, u32[]{:S(2)}) copy-start(bf16[8,2,512,256]{3,2,1,0:T(8,128)(2,1)} %refs_4_.4) | copy-start | bytes 12582916
  2.2 0.9 %copy-start.2 = (bf16[8,32,256]{2,1,0:T(8,128)(2,1)S(1)}, bf16[8,32,256]{2,1,0:T(8,128)(2,1)}, u32[]{:S(2)}) copy-start(bf16[8,32,256]{2,1,0:T(8,128)(2,1)} %coulomb_ref.1) | copy-start | bytes 393220
  3.1 12.8 %copy-start.3 = (bf16[256,128]{1,0:T(8,128)(2,1)S(1)}, bf16[256,128]{1,0:T(8,128)(2,1)}, u32[]{:S(2)}) copy-start(bf16[256,128]{1,0:T(8,128)(2,1)} %constant.6.clone.refs_9_) | copy-start | bytes 196612
  3.1 22.3 %copy-start.4 = (bf16[64,128]{1,0:T(8,128)(2,1)S(1)}, bf16[64,128]{1,0:T(8,128)(2,1)}, u32[]{:S(2)}) copy-start(bf16[64,128]{1,0:T(8,128)(2,1)} %constant.8.clone.refs_5_) | copy-start | bytes 49156
  3.1 22.3 %copy-start.5 = (bf16[64,128]{1,0:T(8,128)(2,1)S(1)}, bf16[64,128]{1,0:T(8,128)(2,1)}, u32[]{:S(2)}) copy-start(bf16[64,128]{1,0:T(8,128)(2,1)} %constant.7.clone.refs_4_) | copy-start | bytes 49156
  3.1 30.3 %copy-start.1 = (bf16[8,2,512,256]{3,2,1,0:T(8,128)(2,1)S(1)}, bf16[8,2,512,256]{3,2,1,0:T(8,128)(2,1)}, u32[]{:S(2)}) copy-start(bf16[8,2,512,256]{3,2,1,0:T(8,128)(2,1)} %refs_4_.4) | copy-start | bytes 12582916
  3.8 7.7 %collective-permute-start.5 = (bf16[64,512]{1,0:T(8,128)(2,1)S(1)}, bf16[64,512]{1,0:T(8,128)(2,1)S(1)}, u32[]{:S(2)}, u32[]{:S(2)}) collective-permute-start(bf16[64,512]{1,0:T(8,128)(2,1)S(1)} %get-tuple-element.20.refs_0_), channel_id=1, source_target_pairs={{0,6},{1,7},{2,4},{3,5},{4,2},{5,3},{6,0},{7,1},{8,14},{9,15},{10,... | collective-permute-start | bytes 196616 | tf_op jit(solution)/shard_map/ppermute | solution.py:279
  8.8 5.6 %collective-permute-start.3 = (bf16[64,512]{1,0:T(8,128)(2,1)S(1)}, bf16[64,512]{1,0:T(8,128)(2,1)S(1)}, u32[]{:S(2)}, u32[]{:S(2)}) collective-permute-start(bf16[64,512]{1,0:T(8,128)(2,1)S(1)} %get-tuple-element.20.refs_0_), channel_id=1, source_target_pairs={{0,4},{1,5},{2,6},{3,7},{4,0},{5,1},{6,2},{7,3},{8,12},{9,13},{10,... | collective-permute-start | bytes 196616 | tf_op jit(solution)/shard_map/ppermute | solution.py:279
  8.8 5.6 %collective-permute-start.1 = (bf16[64,512]{1,0:T(8,128)(2,1)S(1)}, bf16[64,512]{1,0:T(8,128)(2,1)S(1)}, u32[]{:S(2)}, u32[]{:S(2)}) collective-permute-start(bf16[64,512]{1,0:T(8,128)(2,1)S(1)} %get-tuple-element.20.refs_0_), channel_id=1, source_target_pairs={{0,2},{1,3},{2,0},{3,1},{4,6},{5,7},{6,4},{7,5},{8,10},{9,11},{10,... | collective-permute-start | bytes 196616 | tf_op jit(solution)/shard_map/ppermute | solution.py:279
  9.5 5.5 %collective-permute-start = (bf16[64,512]{1,0:T(8,128)(2,1)S(1)}, bf16[64,512]{1,0:T(8,128)(2,1)S(1)}, u32[]{:S(2)}, u32[]{:S(2)}) collective-permute-start(bf16[64,512]{1,0:T(8,128)(2,1)S(1)} %get-tuple-element.20.refs_0_), channel_id=1, source_target_pairs={{0,1},{1,0},{2,3},{3,2},{4,5},{5,4},{6,7},{7,6},{8,9},{9,8},{10,11... | collective-permute-start | bytes 196616 | tf_op jit(solution)/shard_map/ppermute | solution.py:279
  11.4 3.5 %collective-permute-start.6 = (bf16[64,512]{1,0:T(8,128)(2,1)S(1)}, bf16[64,512]{1,0:T(8,128)(2,1)S(1)}, u32[]{:S(2)}, u32[]{:S(2)}) collective-permute-start(bf16[64,512]{1,0:T(8,128)(2,1)S(1)} %collective-permute-done.5.refs_6_), channel_id=1, source_target_pairs={{0,1},{1,0},{2,3},{3,2},{4,5},{5,4},{6,7},{7,6},{8,9},{9,8},{10,11... | collective-permute-start | bytes 196616 | tf_op jit(solution)/shard_map/ppermute | solution.py:279
  14.4 1.3 %collective-permute-start.4 = (bf16[64,512]{1,0:T(8,128)(2,1)S(1)}, bf16[64,512]{1,0:T(8,128)(2,1)S(1)}, u32[]{:S(2)}, u32[]{:S(2)}) collective-permute-start(bf16[64,512]{1,0:T(8,128)(2,1)S(1)} %collective-permute-done.3.refs_4_), channel_id=1, source_target_pairs={{0,1},{1,0},{2,3},{3,2},{4,5},{5,4},{6,7},{7,6},{8,9},{9,8},{10,11... | collective-permute-start | bytes 196616 | tf_op jit(solution)/shard_map/ppermute | solution.py:279
  14.4 1.4 %collective-permute-start.2 = (bf16[64,512]{1,0:T(8,128)(2,1)S(1)}, bf16[64,512]{1,0:T(8,128)(2,1)S(1)}, u32[]{:S(2)}, u32[]{:S(2)}) collective-permute-start(bf16[64,512]{1,0:T(8,128)(2,1)S(1)} %collective-permute-done.1.refs_2_), channel_id=1, source_target_pairs={{0,1},{1,0},{2,3},{3,2},{4,5},{5,4},{6,7},{7,6},{8,9},{9,8},{10,11... | collective-permute-start | bytes 196616 | tf_op jit(solution)/shard_map/ppermute | solution.py:279
  17.3 6.1 %collective-permute-start.7 = (bf16[192,256]{1,0:T(8,128)(2,1)S(1)}, bf16[192,256]{1,0:T(8,128)(2,1)S(1)}, u32[]{:S(2)}, u32[]{:S(2)}) collective-permute-start(bf16[192,256]{1,0:T(8,128)(2,1)S(1)} %get-tuple-element.22), channel_id=1, source_target_pairs={{0,24},{8,16},{16,8},{24,0},{1,25},{9,17},{17,9},{25,1},{2,26},{10... | collective-permute-start | bytes 294920 | tf_op jit(solution)/shard_map/ppermute | solution.py:279
  19.8 5.6 %collective-permute-start.8 = (bf16[192,256]{1,0:T(8,128)(2,1)S(1)}, bf16[192,256]{1,0:T(8,128)(2,1)S(1)}, u32[]{:S(2)}, u32[]{:S(2)}) collective-permute-start(bf16[192,256]{1,0:T(8,128)(2,1)S(1)} %get-tuple-element.23), channel_id=1, source_target_pairs={{0,16},{8,24},{16,0},{24,8},{1,17},{9,25},{17,1},{25,9},{2,18},{10... | collective-permute-start | bytes 294920 | tf_op jit(solution)/shard_map/ppermute | solution.py:279
  20.3 5.2 %collective-permute-start.9 = (bf16[192,256]{1,0:T(8,128)(2,1)S(1)}, bf16[192,256]{1,0:T(8,128)(2,1)S(1)}, u32[]{:S(2)}, u32[]{:S(2)}) collective-permute-start(bf16[192,256]{1,0:T(8,128)(2,1)S(1)} %get-tuple-element.24), channel_id=1, source_target_pairs={{0,8},{8,0},{16,24},{24,16},{1,9},{9,1},{17,25},{25,17},{2,10},{10... | collective-permute-start | bytes 294920 | tf_op jit(solution)/shard_map/ppermute | solution.py:279
  26.0 5.7 %collective-permute-start.10 = (bf16[128,256]{1,0:T(8,128)(2,1)S(1)}, bf16[128,256]{1,0:T(8,128)(2,1)S(1)}, u32[]{:S(2)}, u32[]{:S(2)}) collective-permute-start(bf16[128,256]{1,0:T(8,128)(2,1)S(1)} %get-tuple-element.26), channel_id=1, source_target_pairs={{0,24},{8,16},{16,8},{24,0},{1,25},{9,17},{17,9},{25,1},{2,26},{10... | collective-permute-start | bytes 196616 | tf_op jit(solution)/shard_map/ppermute | solution.py:279
  27.8 4.6 %collective-permute-start.11 = (bf16[128,256]{1,0:T(8,128)(2,1)S(1)}, bf16[128,256]{1,0:T(8,128)(2,1)S(1)}, u32[]{:S(2)}, u32[]{:S(2)}) collective-permute-start(bf16[128,256]{1,0:T(8,128)(2,1)S(1)} %get-tuple-element.27), channel_id=1, source_target_pairs={{0,16},{8,24},{16,0},{24,8},{1,17},{9,25},{17,1},{25,9},{2,18},{10... | collective-permute-start | bytes 196616 | tf_op jit(solution)/shard_map/ppermute | solution.py:279
  29.1 4.3 %collective-permute-start.12 = (bf16[128,256]{1,0:T(8,128)(2,1)S(1)}, bf16[128,256]{1,0:T(8,128)(2,1)S(1)}, u32[]{:S(2)}, u32[]{:S(2)}) collective-permute-start(bf16[128,256]{1,0:T(8,128)(2,1)S(1)} %get-tuple-element.28), channel_id=1, source_target_pairs={{0,8},{8,0},{16,24},{24,16},{1,9},{9,1},{17,25},{25,17},{2,10},{10... | collective-permute-start | bytes 196616 | tf_op jit(solution)/shard_map/ppermute | solution.py:279
  34.6 1.6 %collective-permute-start.13 = (bf16[4,64,512]{2,1,0:T(8,128)(2,1)S(1)}, bf16[4,64,512]{2,1,0:T(8,128)(2,1)S(1)}, u32[]{:S(2)}, u32[]{:S(2)}) collective-permute-start(bf16[4,64,512]{2,1,0:T(8,128)(2,1)S(1)} %shard_map.59), channel_id=1, source_target_pairs={{0,1},{1,0},{2,3},{3,2},{4,5},{5,4},{6,7},{7,6},{8,9},{9,8},{10,11... | collective-permute-start | bytes 786440 | tf_op jit(solution)/shard_map/ppermute | solution.py:279
  36.2 6.8 %collective-permute-start.14 = (bf16[64,512]{1,0:T(8,128)(2,1)S(1)}, bf16[64,512]{1,0:T(8,128)(2,1)S(1)}, u32[]{:S(2)}, u32[]{:S(2)}) collective-permute-start(bf16[64,512]{1,0:T(8,128)(2,1)S(1)} %get-tuple-element.30), channel_id=1, source_target_pairs={{0,6},{1,7},{2,4},{3,5},{4,2},{5,3},{6,0},{7,1},{8,14},{9,15},{10,... | collective-permute-start | bytes 196616 | tf_op jit(solution)/shard_map/ppermute | solution.py:279
  39.0 6.1 %collective-permute-start.15 = (bf16[64,512]{1,0:T(8,128)(2,1)S(1)}, bf16[64,512]{1,0:T(8,128)(2,1)S(1)}, u32[]{:S(2)}, u32[]{:S(2)}) collective-permute-start(bf16[64,512]{1,0:T(8,128)(2,1)S(1)} %get-tuple-element.31), channel_id=1, source_target_pairs={{0,4},{1,5},{2,6},{3,7},{4,0},{5,1},{6,2},{7,3},{8,12},{9,13},{10,... | collective-permute-start | bytes 196616 | tf_op jit(solution)/shard_map/ppermute | solution.py:279
  39.0 6.1 %collective-permute-start.16 = (bf16[64,512]{1,0:T(8,128)(2,1)S(1)}, bf16[64,512]{1,0:T(8,128)(2,1)S(1)}, u32[]{:S(2)}, u32[]{:S(2)}) collective-permute-start(bf16[64,512]{1,0:T(8,128)(2,1)S(1)} %get-tuple-element.32), channel_id=1, source_target_pairs={{0,2},{1,3},{2,0},{3,1},{4,6},{5,7},{6,4},{7,5},{8,10},{9,11},{10,... | collective-permute-start | bytes 196616 | tf_op jit(solution)/shard_map/ppermute | solution.py:279

commit v6 on v4

--- a/solution.py
+++ b/solution.py
@@ -76,12 +76,12 @@
     return pltpu.VMEM((lanes // LANES, rows, LANES), F32)
 
 
-def call(kernel, out_shape, n_in, scratch=(), limit=24, flops=0, size=0, more=(), result=pltpu.VMEM):
+def call(kernel, out_shape, n_in, scratch=(), limit=24, flops=0, size=0, unread=0, result=pltpu.VMEM):
     whole = pl.BlockSpec(memory_space=pltpu.VMEM)
     return pl.pallas_call(
         kernel,
         out_shape=out_shape,
-        in_specs=[whole] * n_in + [pl.BlockSpec(memory_space=place) for place in more],
+        in_specs=[whole] * n_in + [pl.BlockSpec(memory_space=pl.ANY)] * unread,
         out_specs=jax.tree.map(lambda _: pl.BlockSpec(memory_space=result), out_shape),
         scratch_shapes=list(scratch),
         compiler_params=pltpu.CompilerParams(vmem_limit_bytes=limit * MIB),
@@ -89,11 +89,8 @@
     )
 
 
-def edge_kernel(per_block, orb_hbm, edge_ref, orb_ref, sems):
-    local_k = orb_hbm.shape[0]
-    copies = [pltpu.make_async_copy(orb_hbm.at[k], orb_ref.at[k], sems.at[k]) for k in range(local_k)]
-    for copy in copies:
-        copy.start()
+def edge_kernel(per_block, orb_ref, edge_ref):
+    local_k = orb_ref.shape[0]
     row = lax.broadcasted_iota(jnp.int32, (2 * per_block, LANES), 0)
     lane = lax.broadcasted_iota(jnp.int32, (2 * per_block, LANES), 1)
     one, zero = jnp.ones(row.shape, F32), jnp.zeros(row.shape, F32)
@@ -103,7 +100,6 @@
     for g in range(local_k // group):
         rows = []
         for k in range(g * group, (g + 1) * group):
-            copies[k].wait()
             rows.append(
                 dot(first, orb_ref[k, 0, :, :LANES], ((1,), (1,)))
                 + dot(second, orb_ref[k, 1, :, :LANES], ((1,), (1,)))
@@ -111,21 +107,34 @@
         edge_ref[g * ROWS : (g + 1) * ROWS] = jnp.concatenate(rows, axis=0).astype(BF16)
 
 
-def coulomb_kernel(shares, coulomb_ref, edge_ref, _, out_ref, own_ref, wide):
+def coulomb_kernel(shares, coulomb_ref, _, *refs):
+    outs, wide = refs[:shares], refs[shares]
     cells, columns, points = coulomb_ref.shape
     share = columns // shares
     me = lax.axis_index("ka")
-    own_ref[...] = edge_ref[...]
     wide[...] = coulomb_ref[...].astype(F32)
     for s in range(shares):
         start = pl.multiple_of(jnp.bitwise_xor(me, s) * share, share)
         pieces = [wide[r, pl.ds(start, share), :] for r in range(cells)]
-        out_ref[s] = jnp.concatenate(pieces, axis=0).astype(BF16)
+        outs[s][...] = jnp.concatenate(pieces, axis=0).astype(BF16)
+
+
+def cell_kernel(shares, total, *refs):
+    pieces, edge_ref, weight, pass_ref = refs[:shares][::-1], refs[shares], refs[shares + 1], refs[shares + 2]
+    local_k = total // shares
+    share = pieces[0].shape[0] // local_k
+    me = lax.axis_index("ka")
+    pass_ref[...] = edge_ref[...]
+    for s in range(shares):
+        src = jnp.bitwise_xor(me, s)
+        cells = pieces[s][...].astype(F32)
+        for r in range(local_k):
+            spread(weight, src * local_k + r, total, cells[r * share : (r + 1) * share])
 
 
 def tile_kernel(shares, blocks, per_block, *refs):
-    edges, orb_ref, sel_ref, coulomb_ref = refs[:blocks], refs[blocks], refs[blocks + 1], refs[blocks + 2]
-    outs, (form_ref, gathered, wide) = refs[blocks + 3 : blocks + 3 + shares], refs[blocks + 3 + shares :]
+    edges, orb_ref, sel_ref = refs[:blocks], refs[blocks], refs[blocks + 1]
+    outs, (form_ref, gathered, wide) = refs[blocks + 2 : blocks + 2 + shares], refs[blocks + 2 + shares :]
     local_k, _, norb, points = orb_ref.shape
     group = ROWS // (2 * per_block)
     total = blocks * per_block
@@ -155,22 +164,18 @@
     size = share * 2 * local_k
     for s in range(shares):
         dest = jnp.bitwise_xor(me, s)
-        outs[s][:size] = take(wide, pl.multiple_of(dest * size, size), size).astype(BF16)
-        outs[s][size:] = coulomb_ref[s]
+        outs[s][...] = take(wide, pl.multiple_of(dest * size, size), size).astype(BF16)
 
 
 def transform_kernel(shares, total, share, *refs):
-    tiles, (fwd_ref, bwd_ref) = refs[:shares][::-1], refs[shares : shares + 2]
-    outs, (gathered, weight, wide) = refs[shares + 2 : 2 * shares + 2], refs[2 * shares + 2 :]
+    tiles, (fwd_ref, bwd_ref, weight) = refs[:shares][::-1], refs[shares : shares + 3]
+    outs, (gathered, wide) = refs[shares + 3 : 2 * shares + 3], refs[2 * shares + 3 :]
     local_k = total // shares
     size = 2 * local_k * share
     me = lax.axis_index("ka")
     for s in range(shares):
         src = jnp.bitwise_xor(me, s)
-        gathered[src] = tiles[s][:size].astype(gathered.dtype)
-        cells = tiles[s][size:].astype(F32)
-        for r in range(local_k):
-            spread(weight, src * local_k + r, total, cells[r * share : (r + 1) * share])
+        gathered[src] = tiles[s][...].astype(gathered.dtype)
     rows = 2 * local_k
     columns = []
     for c in range(share):
@@ -307,54 +312,57 @@
     edge = call(
         functools.partial(edge_kernel, per_block),
         shape((local_k * 2 * per_block, norb), BF16),
-        0,
-        [pltpu.VMEM(orbitals.shape, BF16), pltpu.SemaphoreType.DMA((local_k,))],
-        limit=57,
+        1,
         size=4 * MIB,
-        more=[pltpu.HBM],
     )(orbitals)
     edges = [edge] + [None] * (blocks - 1)
     for s in range(1, chunks):
         edges[2 * s] = swap(edge, "pts", 2 * s)
-    for s in range(chunks):
-        edges[2 * s + 1] = swap(edges[2 * s], "pts", 1)
-
-    coulombs, edges[0] = call(
+    edges[1] = swap(edge, "pts", 1)
+
+    cells = call(
         functools.partial(coulomb_kernel, shares),
-        [shape((shares, local_k * share, points), BF16), shape(edge.shape, BF16)],
-        2,
+        [shape((local_k * share, points), BF16)] * shares,
+        1,
         [pltpu.VMEM(coulomb.shape, F32)],
         size=1 * MIB,
-        more=[pl.ANY],
-    )(coulomb, edge, edges[1])
+        unread=1,
+    )(coulomb, edges[1])
+    last = chunks // 2
+    weight, passed = call(
+        functools.partial(cell_kernel, shares, total),
+        [shape((points // LANES, share * total, LANES), F32), shape(edge.shape, BF16)],
+        shares + 1,
+        size=1 * MIB,
+    )(*trade(cells, "ka", 1), edges[2 * last])
+    for s in range(1, chunks):
+        edges[2 * s + 1] = swap(passed if s == last else edges[2 * s], "pts", 1)
 
     selector = jnp.asarray(column_selector(group, blocks, per_block, shares))
     piece = shape((share * 2 * local_k, points), BF16)
-    both = shape((share * 3 * local_k, points), BF16)
     *tiles, forms = call(
         functools.partial(tile_kernel, shares, blocks, per_block),
-        [both] * shares + [shape((local_k, 2 * columns, 2 * norb), BF16)],
-        blocks + 3,
+        [piece] * shares + [shape((local_k, 2 * columns, 2 * norb), BF16)],
+        blocks + 2,
         [
             pltpu.VMEM((blocks, local_k * 2 * per_block, norb), BF16),
             tiled(columns * 2 * local_k, points),
         ],
         size=8 * MIB,
-    )(*edges, orbitals, selector, coulombs)
+    )(*edges, orbitals, selector)
     tiles = trade(tiles, "ka", 1)
 
     forward, backward = phase_tables(total)
     kernels = call(
         functools.partial(transform_kernel, shares, total, share),
         [piece] * shares,
-        shares + 2,
+        shares + 3,
         [
             pltpu.VMEM((shares, share * 2 * local_k, points), BF16 if local_k % 8 == 0 else F32),
-            tiled(share * total, points),
             tiled(2 * total * share, points),
         ],
         size=2 * MIB,
-    )(*tiles, jnp.asarray(forward), jnp.asarray(backward))
+    )(*tiles, jnp.asarray(forward), jnp.asarray(backward), weight)
     kernels = trade(kernels, "ka", 1)
 
     lanes = local_k * 2 * columns

time: 47.6 us -> 47.6 us (level)
  starting transfers between devices: 17.9 us -> 21.5 us
  Pallas kernels: 9.42 us -> 6.74 us
  waiting for transfers between devices: 18.2 us -> 16 us
  local copies, waits for them, and re-layouts: 1.76 us -> 3.11 us
    ppermute x17 -> x20, starting transfers between devices: 17.9 us -> 21.5 us  [swap(): return lax.ppermute(value, axis, [(i, i ^ mask) for i in range(size)])]
    pallas_call x1, Pallas kernels: 3.37 us -> 0.64 us  [body(): call(functools.partial(edge_kernel, per_block), shape((local_k * 2 * per_...]
    ppermute x17 -> x20, waiting for transfers between devices: 18.2 us -> 16 us  [swap(): return lax.ppermute(value, axis, [(i, i ^ mask) for i in range(size)])]
    unnamed x12, local copies, waits for them, and re-layouts: 1.76 us -> 3.11 us
    pallas_call x2 -> x3, Pallas kernels: 1.43 us -> 1.61 us  [the longest x1 1.38 us: body(): call(functools.partial(tile_kernel, shares, blocks, per_block), [piece] *...]
  transfers between devices with their start and end apart: 17 -> 20, of which waited for: 11 -> 13; matrix products, arithmetic and copies ran while one was open for 0% -> 0% of each run, Pallas kernels for 3% -> 3%
where the time goes in v6:
time: 47.6 us; the launch traced here: 47.5 us
  starting transfers between devices  21.5 us (45%)
  waiting for transfers between devices  16 us (34%)
  Pallas kernels  6.74 us (14%)
  local copies, waits for them, and re-layouts  3.11 us (7%)
    ppermute x20, starting transfers between devices, swap(): return lax.ppermute(value, axis, [(i, i ^ mask) for i in range(size)])  21.5 us
    ppermute x20, waiting for transfers between devices, swap(): return lax.ppermute(value, axis, [(i, i ^ mask) for i in range(size)])  16 us
    unnamed x12, local copies, waits for them, and re-layouts  3.11 us
    pallas_call x2, Pallas kernels, body(): call(functools.partial(weight_kernel, shares, flip, out_rows), shape((chu...  2.33 us
    pallas_call x1, Pallas kernels, body(): call(functools.partial(exchange_kernel, chunks, 1.0 / math.sqrt(points *...  1.66 us
    pallas_call x1, Pallas kernels, body(): call(functools.partial(tile_kernel, shares, blocks, per_block), [piece] *...  1.38 us
  transfers between devices with their start and end apart: 20, of which 13 were waited for; matrix products, arithmetic and copies ran while one was open for 0% of the time, Pallas kernels for 3%

profile of v6, /device:TPU:0, one launch (start us, length us, event | category | flops | bytes accessed | tf_op | source)
XLA Modules:
  0.0 47.5 jit_solution(4038084894125481799)
XLA Ops:
  0.0 2.2 %copy-done = bf16[8,2,512,256]{3,2,1,0:T(8,128)(2,1)S(1)} copy-done((bf16[8,2,512,256]{3,2,1,0:T(8,128)(2,1)S(1)}, bf16[8,2,512,256]{3,2,1,0:T(8,128)(2,1)}, u32[]{:S(2)}) %copy-start) | copy-done | bytes 4194328
  2.2 0.6 %shard_map.55.refs_0_ = bf16[64,512]{1,0:T(8,128)(2,1)S(1)} custom-call(bf16[8,2,512,256]{3,2,1,0:T(8,128)(2,1)S(1)} %copy-done), custom_call_target="tpu_custom_call" | custom-call | bytes 4194304 | tf_op jit(solution)/shard_map/pallas_call | solution.py:312
  2.8 0.5 collective-permute-start
  3.3 4.6 %collective-permute-start.8 = (bf16[64,512]{1,0:T(8,128)(2,1)S(1)}, bf16[64,512]{1,0:T(8,128)(2,1)S(1)}, u32[]{:S(2)}, u32[]{:S(2)}) collective-permute-start(bf16[64,512]{1,0:T(8,128)(2,1)S(1)} %shard_map.55.refs_0_), channel_id=1, source_target_pairs={{0,6},{1,7},{2,4},{3,5},{4,2},{5,3},{6,0},{7,1},{8,14},{9,15},{10,... | collective-permute-start | bytes 196616 | tf_op jit(solution)/shard_map/ppermute | solution.py:293
  7.9 0.6 %collective-permute-start.1 = (bf16[64,512]{1,0:T(8,128)(2,1)S(1)}, bf16[64,512]{1,0:T(8,128)(2,1)S(1)}, u32[]{:S(2)}, u32[]{:S(2)}) collective-permute-start(bf16[64,512]{1,0:T(8,128)(2,1)S(1)} %shard_map.55.refs_0_), channel_id=1, source_target_pairs={{0,2},{1,3},{2,0},{3,1},{4,6},{5,7},{6,4},{7,5},{8,10},{9,11},{10,... | collective-permute-start | bytes 196616 | tf_op jit(solution)/shard_map/ppermute | solution.py:293
  8.6 0.9 %copy-done.2 = bf16[8,32,256]{2,1,0:T(8,128)(2,1)S(1)} copy-done((bf16[8,32,256]{2,1,0:T(8,128)(2,1)S(1)}, bf16[8,32,256]{2,1,0:T(8,128)(2,1)}, u32[]{:S(2)}) %copy-start.2) | copy-done | bytes 131096
  9.5 2.7 %collective-permute-start.4 = (bf16[64,256]{1,0:T(8,128)(2,1)S(1)}, bf16[64,256]{1,0:T(8,128)(2,1)S(1)}, u32[]{:S(2)}, u32[]{:S(2)}) collective-permute-start(bf16[64,256]{1,0:T(8,128)(2,1)S(1)} %get-tuple-element.24), channel_id=1, source_target_pairs={{0,24},{8,16},{16,8},{24,0},{1,25},{9,17},{17,9},{25,1},{2,26},{10... | collective-permute-start | bytes 98312 | tf_op jit(solution)/shard_map/ppermute | solution.py:293
  12.2 0.5 %collective-permute-start.5 = (bf16[64,256]{1,0:T(8,128)(2,1)S(1)}, bf16[64,256]{1,0:T(8,128)(2,1)S(1)}, u32[]{:S(2)}, u32[]{:S(2)}) collective-permute-start(bf16[64,256]{1,0:T(8,128)(2,1)S(1)} %get-tuple-element.25), channel_id=1, source_target_pairs={{0,16},{8,24},{16,0},{24,8},{1,17},{9,25},{17,1},{25,9},{2,18},{10... | collective-permute-start | bytes 98312 | tf_op jit(solution)/shard_map/ppermute | solution.py:293
  13.1 0.9 %collective-permute-done.3.refs_4_ = bf16[64,512]{1,0:T(8,128)(2,1)S(1)} collective-permute-done((bf16[64,512]{1,0:T(8,128)(2,1)S(1)}, bf16[64,512]{1,0:T(8,128)(2,1)S(1)}, u32[]{:S(2)}, u32[]{:S(2)}) %collective-permute-start.3) | collective-permute-done | bytes 65568 | tf_op jit(solution)/shard_map/ppermute | solution.py:293
  14.0 0.5 %collective-permute-start.2 = (bf16[64,512]{1,0:T(8,128)(2,1)S(1)}, bf16[64,512]{1,0:T(8,128)(2,1)S(1)}, u32[]{:S(2)}, u32[]{:S(2)}) collective-permute-start(bf16[64,512]{1,0:T(8,128)(2,1)S(1)} %collective-permute-done.1.refs_2_), channel_id=1, source_target_pairs={{0,1},{1,0},{2,3},{3,2},{4,5},{5,4},{6,7},{7,6},{8,9},{9,8},{10,11... | collective-permute-start | bytes 196616 | tf_op jit(solution)/shard_map/ppermute | solution.py:293
  14.6 1.6 %collective-permute-done.5.refs_1_ = bf16[64,256]{1,0:T(8,128)(2,1)S(1)} collective-permute-done((bf16[64,256]{1,0:T(8,128)(2,1)S(1)}, bf16[64,256]{1,0:T(8,128)(2,1)S(1)}, u32[]{:S(2)}, u32[]{:S(2)}) %collective-permute-start.5) | collective-permute-done | bytes 32800 | tf_op jit(solution)/shard_map/ppermute | solution.py:293
  16.1 0.5 %collective-permute-done.6.refs_2_ = bf16[64,256]{1,0:T(8,128)(2,1)S(1)} collective-permute-done((bf16[64,256]{1,0:T(8,128)(2,1)S(1)}, bf16[64,256]{1,0:T(8,128)(2,1)S(1)}, u32[]{:S(2)}, u32[]{:S(2)}) %collective-permute-start.6) | collective-permute-done | bytes 32800 | tf_op jit(solution)/shard_map/ppermute | solution.py:293
  16.9 1.2 %collective-permute-done.7.refs_5_ = bf16[64,512]{1,0:T(8,128)(2,1)S(1)} collective-permute-done((bf16[64,512]{1,0:T(8,128)(2,1)S(1)}, bf16[64,512]{1,0:T(8,128)(2,1)S(1)}, u32[]{:S(2)}, u32[]{:S(2)}) %collective-permute-start.7) | collective-permute-done | bytes 65568 | tf_op jit(solution)/shard_map/ppermute | solution.py:293
  18.1 1.4 %shard_map.58 = (bf16[128,256]{1,0:T(8,128)(2,1)S(1)}, bf16[128,256]{1,0:T(8,128)(2,1)S(1)}, bf16[128,256]{1,0:T(8,128)(2,1)S(1)}, bf16[128,256]{1,0:T(8,128)(2,1)S(1)}, bf16[8,64,1024]{2,1,0:T(8,128)(2,1)S(1)}) custom-call(bf16[64,512]{1,0:T(8,128)(2,1)S(1)} %shard_map.55.refs_0_, bf16[64,512]{1,0:T(8,128)(2,1)S(1)} %collective-permute-done._.refs_1_, ...), custom_call_target="tpu_custom_call" | custom-call | bytes 8388608 | tf_op jit(solution)/shard_map/pallas_call | solution.py:343
  19.5 1.6 %collective-permute-start.10 = (bf16[128,256]{1,0:T(8,128)(2,1)S(1)}, bf16[128,256]{1,0:T(8,128)(2,1)S(1)}, u32[]{:S(2)}, u32[]{:S(2)}) collective-permute-start(bf16[128,256]{1,0:T(8,128)(2,1)S(1)} %get-tuple-element.29), channel_id=1, source_target_pairs={{0,24},{8,16},{16,8},{24,0},{1,25},{9,17},{17,9},{25,1},{2,26},{10... | collective-permute-start | bytes 196616 | tf_op jit(solution)/shard_map/ppermute | solution.py:293
  21.5 1.6 %collective-permute-start.12 = (bf16[128,256]{1,0:T(8,128)(2,1)S(1)}, bf16[128,256]{1,0:T(8,128)(2,1)S(1)}, u32[]{:S(2)}, u32[]{:S(2)}) collective-permute-start(bf16[128,256]{1,0:T(8,128)(2,1)S(1)} %get-tuple-element.31), channel_id=1, source_target_pairs={{0,8},{8,0},{16,24},{24,16},{1,9},{9,1},{17,25},{25,17},{2,10},{10... | collective-permute-start | bytes 196616 | tf_op jit(solution)/shard_map/ppermute | solution.py:293
  23.1 1.7 %collective-permute-done.10.refs_0_ = bf16[128,256]{1,0:T(8,128)(2,1)S(1)} collective-permute-done((bf16[128,256]{1,0:T(8,128)(2,1)S(1)}, bf16[128,256]{1,0:T(8,128)(2,1)S(1)}, u32[]{:S(2)}, u32[]{:S(2)}) %collective-permute-start.10) | collective-permute-done | bytes 65568 | tf_op jit(solution)/shard_map/ppermute | solution.py:293
  24.8 1.2 %collective-permute-done.11.refs_1_ = bf16[128,256]{1,0:T(8,128)(2,1)S(1)} collective-permute-done((bf16[128,256]{1,0:T(8,128)(2,1)S(1)}, bf16[128,256]{1,0:T(8,128)(2,1)S(1)}, u32[]{:S(2)}, u32[]{:S(2)}) %collective-permute-start.11) | collective-permute-done | bytes 65568 | tf_op jit(solution)/shard_map/ppermute | solution.py:293
  26.1 0.5 shard_map.59
  26.6 2.3 %collective-permute-start.13 = (bf16[128,256]{1,0:T(8,128)(2,1)S(1)}, bf16[128,256]{1,0:T(8,128)(2,1)S(1)}, u32[]{:S(2)}, u32[]{:S(2)}) collective-permute-start(bf16[128,256]{1,0:T(8,128)(2,1)S(1)} %get-tuple-element.34), channel_id=1, source_target_pairs={{0,24},{8,16},{16,8},{24,0},{1,25},{9,17},{17,9},{25,1},{2,26},{10... | collective-permute-start | bytes 196616 | tf_op jit(solution)/shard_map/ppermute | solution.py:293
  28.8 0.5 %collective-permute-start.14 = (bf16[128,256]{1,0:T(8,128)(2,1)S(1)}, bf16[128,256]{1,0:T(8,128)(2,1)S(1)}, u32[]{:S(2)}, u32[]{:S(2)}) collective-permute-start(bf16[128,256]{1,0:T(8,128)(2,1)S(1)} %get-tuple-element.35), channel_id=1, source_target_pairs={{0,16},{8,24},{16,0},{24,8},{1,17},{9,25},{17,1},{25,9},{2,18},{10... | collective-permute-start | bytes 196616 | tf_op jit(solution)/shard_map/ppermute | solution.py:293
  29.3 0.8 %collective-permute-start.15 = (bf16[128,256]{1,0:T(8,128)(2,1)S(1)}, bf16[128,256]{1,0:T(8,128)(2,1)S(1)}, u32[]{:S(2)}, u32[]{:S(2)}) collective-permute-start(bf16[128,256]{1,0:T(8,128)(2,1)S(1)} %get-tuple-element.36), channel_id=1, source_target_pairs={{0,8},{8,0},{16,24},{24,16},{1,9},{9,1},{17,25},{25,17},{2,10},{10... | collective-permute-start | bytes 196616 | tf_op jit(solution)/shard_map/ppermute | solution.py:293
  30.1 2.0 %collective-permute-done.13.refs_0_ = bf16[128,256]{1,0:T(8,128)(2,1)S(1)} collective-permute-done((bf16[128,256]{1,0:T(8,128)(2,1)S(1)}, bf16[128,256]{1,0:T(8,128)(2,1)S(1)}, u32[]{:S(2)}, u32[]{:S(2)}) %collective-permute-start.13) | collective-permute-done | bytes 65568 | tf_op jit(solution)/shard_map/ppermute | solution.py:293
  32.2 0.9 %collective-permute-done.14.refs_1_ = bf16[128,256]{1,0:T(8,128)(2,1)S(1)} collective-permute-done((bf16[128,256]{1,0:T(8,128)(2,1)S(1)}, bf16[128,256]{1,0:T(8,128)(2,1)S(1)}, u32[]{:S(2)}, u32[]{:S(2)}) %collective-permute-start.14) | collective-permute-done | bytes 65568 | tf_op jit(solution)/shard_map/ppermute | solution.py:293
  33.1 0.5 %collective-permute-done.15.refs_2_ = bf16[128,256]{1,0:T(8,128)(2,1)S(1)} collective-permute-done((bf16[128,256]{1,0:T(8,128)(2,1)S(1)}, bf16[128,256]{1,0:T(8,128)(2,1)S(1)}, u32[]{:S(2)}, u32[]{:S(2)}) %collective-permute-start.15) | collective-permute-done | bytes 65568 | tf_op jit(solution)/shard_map/ppermute | solution.py:293
  33.6 1.2 %shard_map.61 = bf16[4,64,512]{2,1,0:T(8,128)(2,1)S(1)} custom-call(bf16[128,256]{1,0:T(8,128)(2,1)S(1)} %collective-permute-done.13.refs_0_, bf16[128,256]{1,0:T(8,128)(2,1)S(1)} %collective-permute-done.14.refs_1_, bf16[128,256]{1,0:T(8,128)(2,1)S(1)} %collective-permute-done.15.refs_2_, bf16[128,256]{1,0:T(8,128)(2,1)S(1)} %get-tuple-element.37.refs_3_, ...), custom_call_target="tpu_custom_call" | custom-call | bytes 6291456 | tf_op jit(solution)/shard_map/pallas_call | solution.py:372
  34.9 1.2 %shard_map.60.keep_ref = f32[4,64,512]{2,1,0:T(8,128)S(1)} custom-call(bf16[128,256]{1,0:T(8,128)(2,1)S(1)} %collective-permute-done.13.refs_0_, bf16[128,256]{1,0:T(8,128)(2,1)S(1)} %collective-permute-done.14.refs_1_, bf16[128,256]{1,0:T(8,128)(2,1)S(1)} %collective-permute-done.15.refs_2_, bf16[128,256]{1,0:T(8,128)(2,1)S(1)} %get-tuple-element.37.refs_3_, ...), custom_call_target="tpu_custom_call" | custom-call | bytes 6291456 | tf_op jit(solution)/shard_map/pallas_call | solution.py:372
  36.4 3.7 %collective-permute-start.17 = (bf16[64,512]{1,0:T(8,128)(2,1)S(1)}, bf16[64,512]{1,0:T(8,128)(2,1)S(1)}, u32[]{:S(2)}, u32[]{:S(2)}) collective-permute-start(bf16[64,512]{1,0:T(8,128)(2,1)S(1)} %get-tuple-element.38), channel_id=1, source_target_pairs={{0,6},{1,7},{2,4},{3,5},{4,2},{5,3},{6,0},{7,1},{8,14},{9,15},{10,... | collective-permute-start | bytes 196616 | tf_op jit(solution)/shard_map/ppermute | solution.py:293
  40.1 0.8 %collective-permute-start.19 = (bf16[64,512]{1,0:T(8,128)(2,1)S(1)}, bf16[64,512]{1,0:T(8,128)(2,1)S(1)}, u32[]{:S(2)}, u32[]{:S(2)}) collective-permute-start(bf16[64,512]{1,0:T(8,128)(2,1)S(1)} %get-tuple-element.40), channel_id=1, source_target_pairs={{0,2},{1,3},{2,0},{3,1},{4,6},{5,7},{6,4},{7,5},{8,10},{9,11},{10,... | collective-permute-start | bytes 196616 | tf_op jit(solution)/shard_map/ppermute | solution.py:293
  40.9 2.3 %collective-permute-done.17.refs_0_ = bf16[64,512]{1,0:T(8,128)(2,1)S(1)} collective-permute-done((bf16[64,512]{1,0:T(8,128)(2,1)S(1)}, bf16[64,512]{1,0:T(8,128)(2,1)S(1)}, u32[]{:S(2)}, u32[]{:S(2)}) %collective-permute-start.17) | collective-permute-done | bytes 65568 | tf_op jit(solution)/shard_map/ppermute | solution.py:293
  43.2 2.6 %collective-permute-done.18.refs_1_ = bf16[64,512]{1,0:T(8,128)(2,1)S(1)} collective-permute-done((bf16[64,512]{1,0:T(8,128)(2,1)S(1)}, bf16[64,512]{1,0:T(8,128)(2,1)S(1)}, u32[]{:S(2)}, u32[]{:S(2)}) %collective-permute-start.18) | collective-permute-done | bytes 65568 | tf_op jit(solution)/shard_map/ppermute | solution.py:293
  45.8 1.7 %shard_map.63 = bf16[64,4,16,128]{3,2,1,0:T(8,128)(2,1)} custom-call(bf16[64,512]{1,0:T(8,128)(2,1)S(1)} %collective-permute-done.17.refs_0_, bf16[64,512]{1,0:T(8,128)(2,1)S(1)} %collective-permute-done.18.refs_1_, bf16[64,512]{1,0:T(8,128)(2,1)S(1)} %collective-permute-done.19.refs_2_, f32[64,512]{1,0:T(8,128)S(1)} %get-tuple-element.41.refs_3_, ...), custom_call_target="tpu_custom_call" | custom-call | bytes 4194304 | tf_op jit(solution)/shard_map/pallas_call | solution.py:391
  (29 shorter events, 1.6 us)
Async XLA Ops:
  0.0 2.2 %copy-start = (bf16[8,2,512,256]{3,2,1,0:T(8,128)(2,1)S(1)}, bf16[8,2,512,256]{3,2,1,0:T(8,128)(2,1)}, u32[]{:S(2)}) copy-start(bf16[8,2,512,256]{3,2,1,0:T(8,128)(2,1)} %refs_4_.4) | copy-start | bytes 12582916
  2.2 15.9 %copy-start.1 = (bf16[8,2,512,256]{3,2,1,0:T(8,128)(2,1)S(1)}, bf16[8,2,512,256]{3,2,1,0:T(8,128)(2,1)}, u32[]{:S(2)}) copy-start(bf16[8,2,512,256]{3,2,1,0:T(8,128)(2,1)} %refs_4_.4) | copy-start | bytes 12582916
  2.2 15.9 %copy-start.3 = (bf16[256,128]{1,0:T(8,128)(2,1)S(1)}, bf16[256,128]{1,0:T(8,128)(2,1)}, u32[]{:S(2)}) copy-start(bf16[256,128]{1,0:T(8,128)(2,1)} %constant.6.clone.refs_9_) | copy-start | bytes 196612
  2.8 5.7 %collective-permute-start = (bf16[64,512]{1,0:T(8,128)(2,1)S(1)}, bf16[64,512]{1,0:T(8,128)(2,1)S(1)}, u32[]{:S(2)}, u32[]{:S(2)}) collective-permute-start(bf16[64,512]{1,0:T(8,128)(2,1)S(1)} %shard_map.55.refs_0_), channel_id=1, source_target_pairs={{0,1},{1,0},{2,3},{3,2},{4,5},{5,4},{6,7},{7,6},{8,9},{9,8},{10,11... | collective-permute-start | bytes 196616 | tf_op jit(solution)/shard_map/ppermute | solution.py:293
  3.3 9.4 %collective-permute-start.8 = (bf16[64,512]{1,0:T(8,128)(2,1)S(1)}, bf16[64,512]{1,0:T(8,128)(2,1)S(1)}, u32[]{:S(2)}, u32[]{:S(2)}) collective-permute-start(bf16[64,512]{1,0:T(8,128)(2,1)S(1)} %shard_map.55.refs_0_), channel_id=1, source_target_pairs={{0,6},{1,7},{2,4},{3,5},{4,2},{5,3},{6,0},{7,1},{8,14},{9,15},{10,... | collective-permute-start | bytes 196616 | tf_op jit(solution)/shard_map/ppermute | solution.py:293
  7.9 6.1 %collective-permute-start.3 = (bf16[64,512]{1,0:T(8,128)(2,1)S(1)}, bf16[64,512]{1,0:T(8,128)(2,1)S(1)}, u32[]{:S(2)}, u32[]{:S(2)}) collective-permute-start(bf16[64,512]{1,0:T(8,128)(2,1)S(1)} %shard_map.55.refs_0_), channel_id=1, source_target_pairs={{0,4},{1,5},{2,6},{3,7},{4,0},{5,1},{6,2},{7,3},{8,12},{9,13},{10,... | collective-permute-start | bytes 196616 | tf_op jit(solution)/shard_map/ppermute | solution.py:293
  7.9 6.1 %collective-permute-start.1 = (bf16[64,512]{1,0:T(8,128)(2,1)S(1)}, bf16[64,512]{1,0:T(8,128)(2,1)S(1)}, u32[]{:S(2)}, u32[]{:S(2)}) collective-permute-start(bf16[64,512]{1,0:T(8,128)(2,1)S(1)} %shard_map.55.refs_0_), channel_id=1, source_target_pairs={{0,2},{1,3},{2,0},{3,1},{4,6},{5,7},{6,4},{7,5},{8,10},{9,11},{10,... | collective-permute-start | bytes 196616 | tf_op jit(solution)/shard_map/ppermute | solution.py:293
  8.6 0.9 %copy-start.2 = (bf16[8,32,256]{2,1,0:T(8,128)(2,1)S(1)}, bf16[8,32,256]{2,1,0:T(8,128)(2,1)}, u32[]{:S(2)}) copy-start(bf16[8,32,256]{2,1,0:T(8,128)(2,1)} %coulomb_ref.1) | copy-start | bytes 393220
  9.5 16.6 %copy-start.4 = (bf16[64,128]{1,0:T(8,128)(2,1)S(1)}, bf16[64,128]{1,0:T(8,128)(2,1)}, u32[]{:S(2)}) copy-start(bf16[64,128]{1,0:T(8,128)(2,1)} %constant.8.clone.refs_5_) | copy-start | bytes 49156
  9.5 16.6 %copy-start.5 = (bf16[64,128]{1,0:T(8,128)(2,1)S(1)}, bf16[64,128]{1,0:T(8,128)(2,1)}, u32[]{:S(2)}) copy-start(bf16[64,128]{1,0:T(8,128)(2,1)} %constant.7.clone.refs_4_) | copy-start | bytes 49156
  9.5 5.0 %collective-permute-start.4 = (bf16[64,256]{1,0:T(8,128)(2,1)S(1)}, bf16[64,256]{1,0:T(8,128)(2,1)S(1)}, u32[]{:S(2)}, u32[]{:S(2)}) collective-permute-start(bf16[64,256]{1,0:T(8,128)(2,1)S(1)} %get-tuple-element.24), channel_id=1, source_target_pairs={{0,24},{8,16},{16,8},{24,0},{1,25},{9,17},{17,9},{25,1},{2,26},{10... | collective-permute-start | bytes 98312 | tf_op jit(solution)/shard_map/ppermute | solution.py:293
  12.2 3.9 %collective-permute-start.5 = (bf16[64,256]{1,0:T(8,128)(2,1)S(1)}, bf16[64,256]{1,0:T(8,128)(2,1)S(1)}, u32[]{:S(2)}, u32[]{:S(2)}) collective-permute-start(bf16[64,256]{1,0:T(8,128)(2,1)S(1)} %get-tuple-element.25), channel_id=1, source_target_pairs={{0,16},{8,24},{16,0},{24,8},{1,17},{9,25},{17,1},{25,9},{2,18},{10... | collective-permute-start | bytes 98312 | tf_op jit(solution)/shard_map/ppermute | solution.py:293
  12.7 3.9 %collective-permute-start.6 = (bf16[64,256]{1,0:T(8,128)(2,1)S(1)}, bf16[64,256]{1,0:T(8,128)(2,1)S(1)}, u32[]{:S(2)}, u32[]{:S(2)}) collective-permute-start(bf16[64,256]{1,0:T(8,128)(2,1)S(1)} %get-tuple-element.26), channel_id=1, source_target_pairs={{0,8},{8,0},{16,24},{24,16},{1,9},{9,1},{17,25},{25,17},{2,10},{10... | collective-permute-start | bytes 98312 | tf_op jit(solution)/shard_map/ppermute | solution.py:293
  14.0 2.9 %collective-permute-start.9 = (bf16[64,512]{1,0:T(8,128)(2,1)S(1)}, bf16[64,512]{1,0:T(8,128)(2,1)S(1)}, u32[]{:S(2)}, u32[]{:S(2)}) collective-permute-start(bf16[64,512]{1,0:T(8,128)(2,1)S(1)} %collective-permute-done.8.refs_6_), channel_id=1, source_target_pairs={{0,1},{1,0},{2,3},{3,2},{4,5},{5,4},{6,7},{7,6},{8,9},{9,8},{10,11... | collective-permute-start | bytes 196616 | tf_op jit(solution)/shard_map/ppermute | solution.py:293
  14.0 2.9 %collective-permute-start.2 = (bf16[64,512]{1,0:T(8,128)(2,1)S(1)}, bf16[64,512]{1,0:T(8,128)(2,1)S(1)}, u32[]{:S(2)}, u32[]{:S(2)}) collective-permute-start(bf16[64,512]{1,0:T(8,128)(2,1)S(1)} %collective-permute-done.1.refs_2_), channel_id=1, source_target_pairs={{0,1},{1,0},{2,3},{3,2},{4,5},{5,4},{6,7},{7,6},{8,9},{9,8},{10,11... | collective-permute-start | bytes 196616 | tf_op jit(solution)/shard_map/ppermute | solution.py:293
  16.8 1.3 %collective-permute-start.7 = (bf16[64,512]{1,0:T(8,128)(2,1)S(1)}, bf16[64,512]{1,0:T(8,128)(2,1)S(1)}, u32[]{:S(2)}, u32[]{:S(2)}) collective-permute-start(bf16[64,512]{1,0:T(8,128)(2,1)S(1)} %get-tuple-element.28), channel_id=1, source_target_pairs={{0,1},{1,0},{2,3},{3,2},{4,5},{5,4},{6,7},{7,6},{8,9},{9,8},{10,11... | collective-permute-start | bytes 196616 | tf_op jit(solution)/shard_map/ppermute | solution.py:293
  19.5 5.3 %collective-permute-start.10 = (bf16[128,256]{1,0:T(8,128)(2,1)S(1)}, bf16[128,256]{1,0:T(8,128)(2,1)S(1)}, u32[]{:S(2)}, u32[]{:S(2)}) collective-permute-start(bf16[128,256]{1,0:T(8,128)(2,1)S(1)} %get-tuple-element.29), channel_id=1, source_target_pairs={{0,24},{8,16},{16,8},{24,0},{1,25},{9,17},{17,9},{25,1},{2,26},{10... | collective-permute-start | bytes 196616 | tf_op jit(solution)/shard_map/ppermute | solution.py:293
  21.1 5.0 %collective-permute-start.11 = (bf16[128,256]{1,0:T(8,128)(2,1)S(1)}, bf16[128,256]{1,0:T(8,128)(2,1)S(1)}, u32[]{:S(2)}, u32[]{:S(2)}) collective-permute-start(bf16[128,256]{1,0:T(8,128)(2,1)S(1)} %get-tuple-element.30), channel_id=1, source_target_pairs={{0,16},{8,24},{16,0},{24,8},{1,17},{9,25},{17,1},{25,9},{2,18},{10... | collective-permute-start | bytes 196616 | tf_op jit(solution)/shard_map/ppermute | solution.py:293
  21.5 4.7 %collective-permute-start.12 = (bf16[128,256]{1,0:T(8,128)(2,1)S(1)}, bf16[128,256]{1,0:T(8,128)(2,1)S(1)}, u32[]{:S(2)}, u32[]{:S(2)}) collective-permute-start(bf16[128,256]{1,0:T(8,128)(2,1)S(1)} %get-tuple-element.31), channel_id=1, source_target_pairs={{0,8},{8,0},{16,24},{24,16},{1,9},{9,1},{17,25},{25,17},{2,10},{10... | collective-permute-start | bytes 196616 | tf_op jit(solution)/shard_map/ppermute | solution.py:293
  26.6 5.6 %collective-permute-start.13 = (bf16[128,256]{1,0:T(8,128)(2,1)S(1)}, bf16[128,256]{1,0:T(8,128)(2,1)S(1)}, u32[]{:S(2)}, u32[]{:S(2)}) collective-permute-start(bf16[128,256]{1,0:T(8,128)(2,1)S(1)} %get-tuple-element.34), channel_id=1, source_target_pairs={{0,24},{8,16},{16,8},{24,0},{1,25},{9,17},{17,9},{25,1},{2,26},{10... | collective-permute-start | bytes 196616 | tf_op jit(solution)/shard_map/ppermute | solution.py:293
  28.8 4.3 %collective-permute-start.14 = (bf16[128,256]{1,0:T(8,128)(2,1)S(1)}, bf16[128,256]{1,0:T(8,128)(2,1)S(1)}, u32[]{:S(2)}, u32[]{:S(2)}) collective-permute-start(bf16[128,256]{1,0:T(8,128)(2,1)S(1)} %get-tuple-element.35), channel_id=1, source_target_pairs={{0,16},{8,24},{16,0},{24,8},{1,17},{9,25},{17,1},{25,9},{2,18},{10... | collective-permute-start | bytes 196616 | tf_op jit(solution)/shard_map/ppermute | solution.py:293
  29.3 4.3 %collective-permute-start.15 = (bf16[128,256]{1,0:T(8,128)(2,1)S(1)}, bf16[128,256]{1,0:T(8,128)(2,1)S(1)}, u32[]{:S(2)}, u32[]{:S(2)}) collective-permute-start(bf16[128,256]{1,0:T(8,128)(2,1)S(1)} %get-tuple-element.36), channel_id=1, source_target_pairs={{0,8},{8,0},{16,24},{24,16},{1,9},{9,1},{17,25},{25,17},{2,10},{10... | collective-permute-start | bytes 196616 | tf_op jit(solution)/shard_map/ppermute | solution.py:293
  34.8 1.6 %collective-permute-start.16 = (bf16[4,64,512]{2,1,0:T(8,128)(2,1)S(1)}, bf16[4,64,512]{2,1,0:T(8,128)(2,1)S(1)}, u32[]{:S(2)}, u32[]{:S(2)}) collective-permute-start(bf16[4,64,512]{2,1,0:T(8,128)(2,1)S(1)} %shard_map.61), channel_id=1, source_target_pairs={{0,1},{1,0},{2,3},{3,2},{4,5},{5,4},{6,7},{7,6},{8,9},{9,8},{10,11... | collective-permute-start | bytes 786440 | tf_op jit(solution)/shard_map/ppermute | solution.py:293
  36.4 6.7 %collective-permute-start.17 = (bf16[64,512]{1,0:T(8,128)(2,1)S(1)}, bf16[64,512]{1,0:T(8,128)(2,1)S(1)}, u32[]{:S(2)}, u32[]{:S(2)}) collective-permute-start(bf16[64,512]{1,0:T(8,128)(2,1)S(1)} %get-tuple-element.38), channel_id=1, source_target_pairs={{0,6},{1,7},{2,4},{3,5},{4,2},{5,3},{6,0},{7,1},{8,14},{9,15},{10,... | collective-permute-start | bytes 196616 | tf_op jit(solution)/shard_map/ppermute | solution.py:293
  40.1 5.7 %collective-permute-start.18 = (bf16[64,512]{1,0:T(8,128)(2,1)S(1)}, bf16[64,512]{1,0:T(8,128)(2,1)S(1)}, u32[]{:S(2)}, u32[]{:S(2)}) collective-permute-start(bf16[64,512]{1,0:T(8,128)(2,1)S(1)} %get-tuple-element.39), channel_id=1, source_target_pairs={{0,4},{1,5},{2,6},{3,7},{4,0},{5,1},{6,2},{7,3},{8,12},{9,13},{10,... | collective-permute-start | bytes 196616 | tf_op jit(solution)/shard_map/ppermute | solution.py:293
  40.1 5.7 %collective-permute-start.19 = (bf16[64,512]{1,0:T(8,128)(2,1)S(1)}, bf16[64,512]{1,0:T(8,128)(2,1)S(1)}, u32[]{:S(2)}, u32[]{:S(2)}) collective-permute-start(bf16[64,512]{1,0:T(8,128)(2,1)S(1)} %get-tuple-element.40), channel_id=1, source_target_pairs={{0,2},{1,3},{2,0},{3,1},{4,6},{5,7},{6,4},{7,5},{8,10},{9,11},{10,... | collective-permute-start | bytes 196616 | tf_op jit(solution)/shard_map/ppermute | solution.py:293

commit v7 on v5

--- a/solution.py
+++ b/solution.py
@@ -76,12 +76,12 @@
     return pltpu.VMEM((lanes // LANES, rows, LANES), F32)
 
 
-def call(kernel, out_shape, n_in, scratch=(), limit=24, flops=0, size=0, result=pltpu.VMEM):
+def call(kernel, out_shape, n_in, scratch=(), limit=24, flops=0, size=0, unread=0, result=pltpu.VMEM):
     whole = pl.BlockSpec(memory_space=pltpu.VMEM)
     return pl.pallas_call(
         kernel,
         out_shape=out_shape,
-        in_specs=[whole] * n_in,
+        in_specs=[whole] * n_in + [pl.BlockSpec(memory_space=pl.ANY)] * unread,
         out_specs=jax.tree.map(lambda _: pl.BlockSpec(memory_space=result), out_shape),
         scratch_shapes=list(scratch),
         compiler_params=pltpu.CompilerParams(vmem_limit_bytes=limit * MIB),
@@ -89,10 +89,8 @@
     )
 
 
-def edge_kernel(per_block, shares, orb_ref, coulomb_ref, edge_ref, piece_ref, wide):
+def edge_kernel(per_block, orb_ref, edge_ref):
     local_k = orb_ref.shape[0]
-    share = coulomb_ref.shape[1] // shares
-    me = lax.axis_index("ka")
     row = lax.broadcasted_iota(jnp.int32, (2 * per_block, LANES), 0)
     lane = lax.broadcasted_iota(jnp.int32, (2 * per_block, LANES), 1)
     one, zero = jnp.ones(row.shape, F32), jnp.zeros(row.shape, F32)
@@ -107,30 +105,54 @@
                 + dot(second, orb_ref[k, 1, :, :LANES], ((1,), (1,)))
             )
         edge_ref[g * ROWS : (g + 1) * ROWS] = jnp.concatenate(rows, axis=0).astype(BF16)
-    wide[...] = coulomb_ref[...].astype(F32)
-    for s in range(shares):
-        start = pl.multiple_of(jnp.bitwise_xor(me, s) * share, share)
-        pieces = [wide[r, pl.ds(start, share), :] for r in range(local_k)]
-        piece_ref[s] = jnp.concatenate(pieces, axis=0).astype(BF16)
-
-
-def tile_kernel(shares, blocks, per_block, *refs):
-    edges, orb_ref, sel_ref, coulomb_ref = refs[:blocks], refs[blocks], refs[blocks + 1], refs[blocks + 2]
-    outs, (form_ref, gathered, wide) = refs[blocks + 3 : blocks + 3 + shares], refs[blocks + 3 + shares :]
+
+
+def orders(shares):
+    return [[a ^ j for j in reversed(range(shares)) if a ^ j] for a in range(shares)]
+
+
+def pick(table, index):
+    value = jnp.int32(table[0])
+    for i in range(1, len(table)):
+        value = jnp.where(index == i, jnp.int32(table[i]), value)
+    return value
+
+
+def steps_for(j, shares):
+    order = orders(shares)
+    return sorted({order[a].index(a ^ j) for a in range(shares) if a ^ j})
+
+
+def plane_of(shares):
+    return lax.div(lax.axis_index("pts"), lax.axis_size("pts") // shares)
+
+
+def tile_kernel(j, shares, per_share, per_block, *refs):
+    steps = steps_for(j, shares)
+    n = per_share * (1 + len(steps))
+    blocks, (orb_ref, sel_ref, coulomb_ref) = refs[:n], refs[n : n + 3]
+    out_ref, form_ref, gathered, wide, cells = refs[-5:]
     local_k, _, norb, points = orb_ref.shape
     group = ROWS // (2 * per_block)
-    total = blocks * per_block
-    share = total // shares
-    rows = 2 * total
-    me = lax.axis_index("ka")
-    block = lax.axis_index("pts")
-    for s in range(blocks):
-        gathered[jnp.bitwise_xor(block, s)] = edges[s][...]
+    share = per_share * per_block
+    me, block = lax.axis_index("ka"), lax.axis_index("pts")
+    offset = jnp.bitwise_xor(me, j)
+    order = orders(shares)
+    for i, t in enumerate([None] + steps):
+        here = 0 if t is None else pick([order[a][t] for a in range(shares)], me)
+
+        @pl.when(offset == here)
+        def _(i=i):
+            for e in range(per_share):
+                place = jnp.bitwise_xor(jnp.bitwise_and(block, per_share - 1), e)
+                gathered[place] = blocks[i * per_share + e][...]
+
     for g in range(local_k // group):
         stacked = jnp.concatenate(
-            [gathered[b, g * ROWS : (g + 1) * ROWS] for b in range(blocks)], axis=0
+            [gathered[b, g * ROWS : (g + 1) * ROWS] for b in range(per_share)], axis=0
         )
         forms = dot(sel_ref[...], stacked).astype(BF16)
+        rows = 2 * share
         for kk in range(group):
             k = g * group + kk
             left = forms[2 * kk * rows : (2 * kk + 1) * rows]
@@ -138,16 +160,14 @@
             form = jnp.concatenate([left, right], axis=1)
             form_ref[k] = form
             tile = dot(form, orb_ref[k].reshape(2 * norb, points))
-            for d in range(shares):
-                for part in range(2):
-                    low = (2 * d + part) * share
-                    start = d * share * 2 * local_k + 2 * k + part
-                    spread(wide, start, 2 * local_k, tile[low : low + share])
+            for part in range(2):
+                spread(wide, 2 * k + part, 2 * local_k, tile[part * share : (part + 1) * share])
     size = share * 2 * local_k
-    for s in range(shares):
-        dest = jnp.bitwise_xor(me, s)
-        outs[s][:size] = take(wide, pl.multiple_of(dest * size, size), size).astype(BF16)
-        outs[s][size:] = coulomb_ref[s]
+    out_ref[:size] = take(wide, 0, size).astype(BF16)
+    start = pl.multiple_of(jnp.bitwise_xor(offset, plane_of(shares)) * share, share)
+    cells[...] = coulomb_ref[...].astype(F32)
+    pieces = [cells[r, pl.ds(start, share), :] for r in range(local_k)]
+    out_ref[size:] = jnp.concatenate(pieces, axis=0).astype(BF16)
 
 
 def transform_kernel(shares, total, share, *refs):
@@ -188,8 +208,9 @@
     half = total_rows // local_k // 2
     me = lax.axis_index("ka")
     core = jnp.bitwise_xor(jnp.bitwise_and(lax.axis_index("pts"), 1), flip)
+    plane = plane_of(shares)
     for s in range(shares):
-        gathered[jnp.bitwise_xor(me, s)] = pieces[s][...]
+        gathered[jnp.bitwise_xor(jnp.bitwise_xor(me, s), plane)] = pieces[s][...]
     lanes = 2 * half * shares
     group = max(1, LANES // lanes)
     chunks = norb // out_rows // 2
@@ -231,10 +252,14 @@
             outs[s - 1][...] = value.astype(BF16)
 
 
-def exchange_kernel(chunks, scale, *refs):
-    pieces, form_ref, out_hbm = refs[:chunks][::-1], refs[chunks], refs[chunks + 1]
-    wide, out_ref, sems = refs[chunks + 2 :]
-    local_k, lanes, twice = form_ref.shape
+def exchange_kernel(chunks, shares, scale, *refs):
+    pieces, form_refs, out_hbm = refs[:chunks][::-1], refs[chunks : chunks + shares], refs[chunks + shares]
+    wide, out_ref, form_ref, sems = refs[chunks + shares + 1 :]
+    owner = jnp.bitwise_xor(lax.axis_index("ka"), plane_of(shares))
+    for j in range(shares):
+        form_ref[jnp.bitwise_xor(owner, j)] = form_refs[j][...]
+    _, local_k, part_lanes, twice = form_ref.shape
+    lanes = shares * part_lanes
     norb = twice // 2
     spans = norb // LANES
     out_rows = pieces[0].shape[0]
@@ -258,7 +283,7 @@
             left.append(
                 jnp.concatenate([jnp.where(keep, high_g, zero), jnp.where(keep, low_g, zero)], axis=1)
             )
-        forms = [form_ref[g * group + kk] for kk in range(group)]
+        forms = [form_ref[d, g * group + kk] for kk in range(group) for d in range(shares)]
         result = dot(jnp.concatenate(left, axis=0), jnp.concatenate(forms + forms, axis=0))
         for kk in range(group):
             for part in range(2):
@@ -295,35 +320,48 @@
     group = ROWS // (2 * per_block)
     shape = jax.ShapeDtypeStruct
 
-    edge, coulombs = call(
-        functools.partial(edge_kernel, per_block, shares),
-        [
-            shape((local_k * 2 * per_block, norb), BF16),
-            shape((shares, local_k * share, points), BF16),
-        ],
-        2,
-        [pltpu.VMEM(coulomb.shape, F32)],
+    edge = call(
+        functools.partial(edge_kernel, per_block),
+        shape((local_k * 2 * per_block, norb), BF16),
+        1,
         size=4 * MIB,
-    )(orbitals, coulomb)
-    edges = [edge] + [None] * (blocks - 1)
-    for s in range(1, chunks):
-        edges[2 * s] = swap(edge, "pts", 2 * s)
-    for s in range(chunks):
-        edges[2 * s + 1] = swap(edges[2 * s], "pts", 1)
-
-    selector = jnp.asarray(column_selector(group, blocks, per_block, shares))
+    )(orbitals)
+    per_share = blocks // shares
+    order = orders(shares)
+    partner = swap(edge, "pts", 1)
+    near = [edge, partner] + [swap(edge, "pts", 2 * e + c) for e in range(1, per_share // 2) for c in range(2)]
+    came = []
+    for t in range(shares - 1):
+        step = []
+        for e in range(per_share // 2):
+            pairs = [
+                (a * blocks + i, a * blocks + (i ^ (order[a][t] * per_share + 2 * e)))
+                for a in range(shares)
+                for i in range(blocks)
+            ]
+            block = lax.ppermute(edge, ("ka", "pts"), pairs)
+            step += [block, swap(block, "pts", 1)]
+        came.append(step)
+
+    selector = jnp.asarray(column_selector(group, per_share, per_block, 1))
     piece = shape((share * 2 * local_k, points), BF16)
     both = shape((share * 3 * local_k, points), BF16)
-    *tiles, forms = call(
-        functools.partial(tile_kernel, shares, blocks, per_block),
-        [both] * shares + [shape((local_k, 2 * columns, 2 * norb), BF16)],
-        blocks + 3,
-        [
-            pltpu.VMEM((blocks, local_k * 2 * per_block, norb), BF16),
-            tiled(columns * 2 * local_k, points),
-        ],
-        size=8 * MIB,
-    )(*edges, orbitals, selector, coulombs)
+    tiles, forms, before = [None] * shares, [None] * shares, []
+    for j in reversed(range(shares)):
+        taken = [block for t in steps_for(j, shares) for block in came[t]]
+        tiles[j], forms[j] = call(
+            functools.partial(tile_kernel, j, shares, per_share, per_block),
+            [both, shape((local_k, 2 * share, 2 * norb), BF16)],
+            len(near) + len(taken) + 3,
+            [
+                pltpu.VMEM((per_share, local_k * 2 * per_block, norb), BF16),
+                tiled(share * 2 * local_k, points),
+                pltpu.VMEM(coulomb.shape, F32),
+            ],
+            size=6 * MIB,
+            unread=len(before),
+        )(*near, *taken, orbitals, selector, coulomb, *before)
+        before = [forms[j]]
     tiles = trade(tiles, "ka", 1)
 
     forward, backward = phase_tables(total)
@@ -364,17 +402,18 @@
     pair = max(1, LANES // (2 * columns))
     rows = pair * spans * 2
     result = call(
-        functools.partial(exchange_kernel, chunks, 1.0 / math.sqrt(points * blocks)),
+        functools.partial(exchange_kernel, chunks, shares, 1.0 / math.sqrt(points * blocks)),
         shape((out_rows, local_k // pair, rows, LANES), BF16),
-        chunks + 1,
+        chunks + shares,
         [
             pltpu.VMEM((local_k // pair, out_rows * rows, LANES), F32),
             pltpu.VMEM((local_k // pair, out_rows, rows, LANES), BF16),
+            pltpu.VMEM((shares, local_k, 2 * share, 2 * norb), BF16),
             pltpu.SemaphoreType.DMA((local_k // pair,)),
         ],
         size=4 * MIB,
         result=pltpu.HBM,
-    )(*sums, forms)
+    )(*sums, *forms)
     result = result.reshape(out_rows, local_k, spans, 2, LANES)
     return result.transpose(0, 1, 3, 2, 4).reshape(out_rows, local_k, 2, norb)
 

time: 46.9 us -> 46.3 us (0.987)
  waiting for transfers between devices: 19 us -> 15.8 us
  Pallas kernels: 6.67 us -> 9.74 us
  local copies, waits for them, and re-layouts: 3.11 us -> 2.21 us
    ppermute x17 -> x14, waiting for transfers between devices: 19 us -> 10.8 us  [swap(): return lax.ppermute(value, axis, [(i, i ^ mask) for i in range(size)])]
    ppermute x0 -> x3, starting transfers between devices: none -> 5.67 us  [body(): block = lax.ppermute(edge, ('ka', 'pts'), pairs)]
    ppermute x17 -> x14, starting transfers between devices: 17.9 us -> 12.6 us  [swap(): return lax.ppermute(value, axis, [(i, i ^ mask) for i in range(size)])]
    ppermute x0 -> x3, waiting for transfers between devices: none -> 5 us  [body(): block = lax.ppermute(edge, ('ka', 'pts'), pairs)]
    pallas_call x3 -> x6, Pallas kernels: 3.71 us -> 6.78 us  [the longest x4 4.38 us: body(): call(functools.partial(tile_kernel, j, shares, per_share, per_block), [bo...]
    unnamed x12, local copies, waits for them, and re-layouts: 3.11 us -> 2.21 us
  transfers between devices with their start and end apart: 17 -> 17, of which waited for: 13 -> 10; matrix products, arithmetic and copies ran while one was open for 0% -> 0% of each run, Pallas kernels for 2% -> 12%
where the time goes in v7:
time: 46.3 us; the launch traced here: 46.1 us
  starting transfers between devices  18.2 us (39%)
  waiting for transfers between devices  15.8 us (34%)
  Pallas kernels  9.74 us (21%)
  local copies, waits for them, and re-layouts  2.21 us (5%)
    ppermute x14, starting transfers between devices, swap(): return lax.ppermute(value, axis, [(i, i ^ mask) for i in range(size)])  12.6 us
    ppermute x14, waiting for transfers between devices, swap(): return lax.ppermute(value, axis, [(i, i ^ mask) for i in range(size)])  10.8 us
    ppermute x3, starting transfers between devices, body(): block = lax.ppermute(edge, ('ka', 'pts'), pairs)  5.67 us
    ppermute x3, waiting for transfers between devices, body(): block = lax.ppermute(edge, ('ka', 'pts'), pairs)  5 us
    pallas_call x4, Pallas kernels, body(): call(functools.partial(tile_kernel, j, shares, per_share, per_block), [bo...  4.38 us
    pallas_call x2, Pallas kernels, body(): call(functools.partial(weight_kernel, shares, flip, out_rows), shape((chu...  2.33 us
    unnamed x12, local copies, waits for them, and re-layouts  2.21 us
    pallas_call x1, Pallas kernels, body(): call(functools.partial(exchange_kernel, chunks, shares, 1.0 / math.sqrt(p...  1.75 us
  transfers between devices with their start and end apart: 17, of which 10 were waited for; matrix products, arithmetic and copies ran while one was open for 0% of the time, Pallas kernels for 12%

profile of v7, /device:TPU:0, one launch (start us, length us, event | category | flops | bytes accessed | tf_op | source)
XLA Modules:
  0.0 46.1 jit_solution(3460973873916236921)
XLA Ops:
  0.0 2.2 %copy-done = bf16[8,2,512,256]{3,2,1,0:T(8,128)(2,1)S(1)} copy-done((bf16[8,2,512,256]{3,2,1,0:T(8,128)(2,1)S(1)}, bf16[8,2,512,256]{3,2,1,0:T(8,128)(2,1)}, u32[]{:S(2)}) %copy-start) | copy-done | bytes 4194328
  2.2 0.6 %shard_map.55.refs_0_ = bf16[64,512]{1,0:T(8,128)(2,1)S(1)} custom-call(bf16[8,2,512,256]{3,2,1,0:T(8,128)(2,1)S(1)} %copy-done), custom_call_target="tpu_custom_call" | custom-call | bytes 4194304 | tf_op jit(solution)/shard_map/pallas_call | solution.py:323
  2.8 5.1 %collective-permute-start.1 = (bf16[64,512]{1,0:T(8,128)(2,1)S(1)}, bf16[64,512]{1,0:T(8,128)(2,1)S(1)}, u32[]{:S(2)}, u32[]{:S(2)}) collective-permute-start(bf16[64,512]{1,0:T(8,128)(2,1)S(1)} %shard_map.55.refs_0_), channel_id=1, source_target_pairs={{0,6},{1,7},{2,4},{3,5},{4,2},{5,3},{6,0},{7,1},{8,12},{9,13},{10,... | collective-permute-start | bytes 196616 | tf_op jit(solution)/shard_map/ppermute | solution.py:342
  7.9 0.6 %collective-permute-start.7 = (bf16[64,512]{1,0:T(8,128)(2,1)S(1)}, bf16[64,512]{1,0:T(8,128)(2,1)S(1)}, u32[]{:S(2)}, u32[]{:S(2)}) collective-permute-start(bf16[64,512]{1,0:T(8,128)(2,1)S(1)} %shard_map.55.refs_0_), channel_id=1, source_target_pairs={{0,2},{1,3},{2,0},{3,1},{4,6},{5,7},{6,4},{7,5},{8,10},{9,11},{10,... | collective-permute-start | bytes 196616 | tf_op jit(solution)/shard_map/ppermute | solution.py:342
  8.5 2.0 %collective-permute-done.1.refs_2_ = bf16[64,512]{1,0:T(8,128)(2,1)S(1)} collective-permute-done((bf16[64,512]{1,0:T(8,128)(2,1)S(1)}, bf16[64,512]{1,0:T(8,128)(2,1)S(1)}, u32[]{:S(2)}, u32[]{:S(2)}) %collective-permute-start.1) | collective-permute-done | bytes 65568 | tf_op jit(solution)/shard_map/ppermute | solution.py:342
  10.5 3.0 %collective-permute-done.4.refs_4_.refs_2_ = bf16[64,512]{1,0:T(8,128)(2,1)S(1)} collective-permute-done((bf16[64,512]{1,0:T(8,128)(2,1)S(1)}, bf16[64,512]{1,0:T(8,128)(2,1)S(1)}, u32[]{:S(2)}, u32[]{:S(2)}) %collective-permute-start.4) | collective-permute-done | bytes 65568 | tf_op jit(solution)/shard_map/ppermute | solution.py:342
  13.5 0.5 %collective-permute-start.8 = (bf16[64,512]{1,0:T(8,128)(2,1)S(1)}, bf16[64,512]{1,0:T(8,128)(2,1)S(1)}, u32[]{:S(2)}, u32[]{:S(2)}) collective-permute-start(bf16[64,512]{1,0:T(8,128)(2,1)S(1)} %collective-permute-done.7.refs_4_.refs_2_), channel_id=1, source_target_pairs={{0,1},{1,0},{2,3},{3,2},{4,5},{5,4},{6,7},{7,6},{8,9},{9,8},{10,11... | collective-permute-start | bytes 196616 | tf_op jit(solution)/shard_map/ppermute | solution.py:304
  14.0 1.1 %shard_map.56 = (bf16[192,256]{1,0:T(8,128)(2,1)S(1)}, bf16[8,16,1024]{2,1,0:T(8,128)(2,1)S(1)}) custom-call(bf16[64,512]{1,0:T(8,128)(2,1)S(1)} %shard_map.55.refs_0_, bf16[64,512]{1,0:T(8,128)(2,1)S(1)} %collective-permute-done.refs_1_, bf16[64,512]{1,0:T(8,128)(2,1)S(1)} %collective-permute-done.1.refs_2_, ...), custom_call_target="tpu_custom_call" | custom-call | bytes 6291456 | tf_op jit(solution)/shard_map/pallas_call | solution.py:352
  15.2 3.0 %collective-permute-start.3 = (bf16[192,256]{1,0:T(8,128)(2,1)S(1)}, bf16[192,256]{1,0:T(8,128)(2,1)S(1)}, u32[]{:S(2)}, u32[]{:S(2)}) collective-permute-start(bf16[192,256]{1,0:T(8,128)(2,1)S(1)} %get-tuple-element.21), channel_id=1, source_target_pairs={{0,24},{8,16},{16,8},{24,0},{1,25},{9,17},{17,9},{25,1},{2,26},{10... | collective-permute-start | bytes 294920 | tf_op jit(solution)/shard_map/ppermute | solution.py:304
  18.2 1.1 %shard_map.57 = (bf16[192,256]{1,0:T(8,128)(2,1)S(1)}, bf16[8,16,1024]{2,1,0:T(8,128)(2,1)S(1)}) custom-call(bf16[64,512]{1,0:T(8,128)(2,1)S(1)} %shard_map.55.refs_0_, bf16[64,512]{1,0:T(8,128)(2,1)S(1)} %collective-permute-done.refs_1_, bf16[64,512]{1,0:T(8,128)(2,1)S(1)} %collective-permute-done.1.refs_2_, ...), custom_call_target="tpu_custom_call" | custom-call | bytes 6291456 | tf_op jit(solution)/shard_map/pallas_call | solution.py:352
  19.3 0.1 collective-permute-start.6
  19.4 1.1 %shard_map.58 = (bf16[192,256]{1,0:T(8,128)(2,1)S(1)}, bf16[8,16,1024]{2,1,0:T(8,128)(2,1)S(1)}) custom-call(bf16[64,512]{1,0:T(8,128)(2,1)S(1)} %shard_map.55.refs_0_, bf16[64,512]{1,0:T(8,128)(2,1)S(1)} %collective-permute-done.refs_1_, bf16[64,512]{1,0:T(8,128)(2,1)S(1)} %collective-permute-done.4.refs_4_.refs_2_, ...), custom_call_target="tpu_custom_call" | custom-call | bytes 6291456 | tf_op jit(solution)/shard_map/pallas_call | solution.py:352
  20.5 0.9 %collective-permute-start.9 = (bf16[192,256]{1,0:T(8,128)(2,1)S(1)}, bf16[192,256]{1,0:T(8,128)(2,1)S(1)}, u32[]{:S(2)}, u32[]{:S(2)}) collective-permute-start(bf16[192,256]{1,0:T(8,128)(2,1)S(1)} %get-tuple-element.25), channel_id=1, source_target_pairs={{0,8},{8,0},{16,24},{24,16},{1,9},{9,1},{17,25},{25,17},{2,10},{10... | collective-permute-start | bytes 294920 | tf_op jit(solution)/shard_map/ppermute | solution.py:304
  21.4 1.1 %shard_map.59 = (bf16[192,256]{1,0:T(8,128)(2,1)S(1)}, bf16[8,16,1024]{2,1,0:T(8,128)(2,1)S(1)}) custom-call(bf16[64,512]{1,0:T(8,128)(2,1)S(1)} %shard_map.55.refs_0_, bf16[64,512]{1,0:T(8,128)(2,1)S(1)} %collective-permute-done.refs_1_, bf16[64,512]{1,0:T(8,128)(2,1)S(1)} %collective-permute-done.7.refs_4_.refs_2_, ...), custom_call_target="tpu_custom_call" | custom-call | bytes 6291456 | tf_op jit(solution)/shard_map/pallas_call | solution.py:352
  22.5 1.8 %collective-permute-done.6.refs_1_ = bf16[192,256]{1,0:T(8,128)(2,1)S(1)} collective-permute-done((bf16[192,256]{1,0:T(8,128)(2,1)S(1)}, bf16[192,256]{1,0:T(8,128)(2,1)S(1)}, u32[]{:S(2)}, u32[]{:S(2)}) %collective-permute-start.6) | collective-permute-done | bytes 98336 | tf_op jit(solution)/shard_map/ppermute | solution.py:304
  24.3 1.2 %collective-permute-done.9.refs_2_ = bf16[192,256]{1,0:T(8,128)(2,1)S(1)} collective-permute-done((bf16[192,256]{1,0:T(8,128)(2,1)S(1)}, bf16[192,256]{1,0:T(8,128)(2,1)S(1)}, u32[]{:S(2)}, u32[]{:S(2)}) %collective-permute-start.9) | collective-permute-done | bytes 98336 | tf_op jit(solution)/shard_map/ppermute | solution.py:304
  25.5 0.6 %shard_map.60 = (bf16[128,256]{1,0:T(8,128)(2,1)S(1)}, bf16[128,256]{1,0:T(8,128)(2,1)S(1)}, bf16[128,256]{1,0:T(8,128)(2,1)S(1)}, bf16[128,256]{1,0:T(8,128)(2,1)S(1)}) custom-call(bf16[192,256]{1,0:T(8,128)(2,1)S(1)} %collective-permute-done.3.refs_0_, bf16[192,256]{1,0:T(8,128)(2,1)S(1)} %collective-permute-done.6.refs_1_, ...), custom_call_target="tpu_custom_call" | custom-call | bytes 2097152 | tf_op jit(solution)/shard_map/pallas_call | solution.py:368
  26.1 2.0 %collective-permute-start.10 = (bf16[128,256]{1,0:T(8,128)(2,1)S(1)}, bf16[128,256]{1,0:T(8,128)(2,1)S(1)}, u32[]{:S(2)}, u32[]{:S(2)}) collective-permute-start(bf16[128,256]{1,0:T(8,128)(2,1)S(1)} %get-tuple-element.28), channel_id=1, source_target_pairs={{0,24},{8,16},{16,8},{24,0},{1,25},{9,17},{17,9},{25,1},{2,26},{10... | collective-permute-start | bytes 196616 | tf_op jit(solution)/shard_map/ppermute | solution.py:304
  28.1 0.3 collective-permute-start.11
  28.4 1.2 %collective-permute-start.12 = (bf16[128,256]{1,0:T(8,128)(2,1)S(1)}, bf16[128,256]{1,0:T(8,128)(2,1)S(1)}, u32[]{:S(2)}, u32[]{:S(2)}) collective-permute-start(bf16[128,256]{1,0:T(8,128)(2,1)S(1)} %get-tuple-element.30), channel_id=1, source_target_pairs={{0,8},{8,0},{16,24},{24,16},{1,9},{9,1},{17,25},{25,17},{2,10},{10... | collective-permute-start | bytes 196616 | tf_op jit(solution)/shard_map/ppermute | solution.py:304
  29.7 2.3 %collective-permute-done.10.refs_0_ = bf16[128,256]{1,0:T(8,128)(2,1)S(1)} collective-permute-done((bf16[128,256]{1,0:T(8,128)(2,1)S(1)}, bf16[128,256]{1,0:T(8,128)(2,1)S(1)}, u32[]{:S(2)}, u32[]{:S(2)}) %collective-permute-start.10) | collective-permute-done | bytes 65568 | tf_op jit(solution)/shard_map/ppermute | solution.py:304
  32.0 0.5 %collective-permute-done.11.refs_1_ = bf16[128,256]{1,0:T(8,128)(2,1)S(1)} collective-permute-done((bf16[128,256]{1,0:T(8,128)(2,1)S(1)}, bf16[128,256]{1,0:T(8,128)(2,1)S(1)}, u32[]{:S(2)}, u32[]{:S(2)}) %collective-permute-start.11) | collective-permute-done | bytes 65568 | tf_op jit(solution)/shard_map/ppermute | solution.py:304
  32.5 0.2 collective-permute-done.12.refs_2_
  32.7 1.2 %shard_map.62 = bf16[4,64,512]{2,1,0:T(8,128)(2,1)S(1)} custom-call(bf16[128,256]{1,0:T(8,128)(2,1)S(1)} %collective-permute-done.10.refs_0_, bf16[128,256]{1,0:T(8,128)(2,1)S(1)} %collective-permute-done.11.refs_1_, bf16[128,256]{1,0:T(8,128)(2,1)S(1)} %collective-permute-done.12.refs_2_, bf16[128,256]{1,0:T(8,128)(2,1)S(1)} %get-tuple-element.31.refs_3_, ...), custom_call_target="tpu_custom_call" | custom-call | bytes 6291456 | tf_op jit(solution)/shard_map/pallas_call | solution.py:385
  33.9 0.1 collective-permute-start.13
  34.0 1.2 %shard_map.61.keep_ref = f32[4,64,512]{2,1,0:T(8,128)S(1)} custom-call(bf16[128,256]{1,0:T(8,128)(2,1)S(1)} %collective-permute-done.10.refs_0_, bf16[128,256]{1,0:T(8,128)(2,1)S(1)} %collective-permute-done.11.refs_1_, bf16[128,256]{1,0:T(8,128)(2,1)S(1)} %collective-permute-done.12.refs_2_, bf16[128,256]{1,0:T(8,128)(2,1)S(1)} %get-tuple-element.31.refs_3_, ...), custom_call_target="tpu_custom_call" | custom-call | bytes 6291456 | tf_op jit(solution)/shard_map/pallas_call | solution.py:385
  35.1 0.4 collective-permute-done.13.came_ref
  35.5 2.5 %collective-permute-start.14 = (bf16[64,512]{1,0:T(8,128)(2,1)S(1)}, bf16[64,512]{1,0:T(8,128)(2,1)S(1)}, u32[]{:S(2)}, u32[]{:S(2)}) collective-permute-start(bf16[64,512]{1,0:T(8,128)(2,1)S(1)} %get-tuple-element.32), channel_id=1, source_target_pairs={{0,6},{1,7},{2,4},{3,5},{4,2},{5,3},{6,0},{7,1},{8,14},{9,15},{10,... | collective-permute-start | bytes 196616 | tf_op jit(solution)/shard_map/ppermute | solution.py:304
  38.0 2.0 %collective-permute-start.16 = (bf16[64,512]{1,0:T(8,128)(2,1)S(1)}, bf16[64,512]{1,0:T(8,128)(2,1)S(1)}, u32[]{:S(2)}, u32[]{:S(2)}) collective-permute-start(bf16[64,512]{1,0:T(8,128)(2,1)S(1)} %get-tuple-element.34), channel_id=1, source_target_pairs={{0,2},{1,3},{2,0},{3,1},{4,6},{5,7},{6,4},{7,5},{8,10},{9,11},{10,... | collective-permute-start | bytes 196616 | tf_op jit(solution)/shard_map/ppermute | solution.py:304
  40.0 2.4 %collective-permute-done.14.refs_0_ = bf16[64,512]{1,0:T(8,128)(2,1)S(1)} collective-permute-done((bf16[64,512]{1,0:T(8,128)(2,1)S(1)}, bf16[64,512]{1,0:T(8,128)(2,1)S(1)}, u32[]{:S(2)}, u32[]{:S(2)}) %collective-permute-start.14) | collective-permute-done | bytes 65568 | tf_op jit(solution)/shard_map/ppermute | solution.py:304
  42.4 2.0 %collective-permute-done.15.refs_1_ = bf16[64,512]{1,0:T(8,128)(2,1)S(1)} collective-permute-done((bf16[64,512]{1,0:T(8,128)(2,1)S(1)}, bf16[64,512]{1,0:T(8,128)(2,1)S(1)}, u32[]{:S(2)}, u32[]{:S(2)}) %collective-permute-start.15) | collective-permute-done | bytes 65568 | tf_op jit(solution)/shard_map/ppermute | solution.py:304
  44.4 1.8 %shard_map.64 = bf16[64,4,16,128]{3,2,1,0:T(8,128)(2,1)} custom-call(bf16[64,512]{1,0:T(8,128)(2,1)S(1)} %collective-permute-done.14.refs_0_, bf16[64,512]{1,0:T(8,128)(2,1)S(1)} %collective-permute-done.15.refs_1_, bf16[64,512]{1,0:T(8,128)(2,1)S(1)} %collective-permute-done.16.refs_2_, f32[64,512]{1,0:T(8,128)S(1)} %get-tuple-element.35.refs_3_, ...), custom_call_target="tpu_custom_call" | custom-call | bytes 4194304 | tf_op jit(solution)/shard_map/pallas_call | solution.py:404
  (24 shorter events, 0.1 us)
Async XLA Ops:
  0.0 2.2 %copy-start = (bf16[8,2,512,256]{3,2,1,0:T(8,128)(2,1)S(1)}, bf16[8,2,512,256]{3,2,1,0:T(8,128)(2,1)}, u32[]{:S(2)}) copy-start(bf16[8,2,512,256]{3,2,1,0:T(8,128)(2,1)} %refs_4_.8) | copy-start | bytes 12582916
  2.2 11.8 %copy-start.2 = (bf16[8,32,256]{2,1,0:T(8,128)(2,1)S(1)}, bf16[8,32,256]{2,1,0:T(8,128)(2,1)}, u32[]{:S(2)}) copy-start(bf16[8,32,256]{2,1,0:T(8,128)(2,1)} %refs_6_.7) | copy-start | bytes 393220
  2.2 11.8 %copy-start.3 = (bf16[64,32]{1,0:T(8,128)(2,1)S(1)}, bf16[64,32]{1,0:T(8,128)(2,1)}, u32[]{:S(2)}) copy-start(bf16[64,32]{1,0:T(8,128)(2,1)} %constant.6.clone.refs_5_.refs_7_) | copy-start | bytes 12292
  2.8 7.6 %collective-permute-start.1 = (bf16[64,512]{1,0:T(8,128)(2,1)S(1)}, bf16[64,512]{1,0:T(8,128)(2,1)S(1)}, u32[]{:S(2)}, u32[]{:S(2)}) collective-permute-start(bf16[64,512]{1,0:T(8,128)(2,1)S(1)} %shard_map.55.refs_0_), channel_id=1, source_target_pairs={{0,6},{1,7},{2,4},{3,5},{4,2},{5,3},{6,0},{7,1},{8,12},{9,13},{10,... | collective-permute-start | bytes 196616 | tf_op jit(solution)/shard_map/ppermute | solution.py:342
  7.9 5.6 %collective-permute-start.4 = (bf16[64,512]{1,0:T(8,128)(2,1)S(1)}, bf16[64,512]{1,0:T(8,128)(2,1)S(1)}, u32[]{:S(2)}, u32[]{:S(2)}) collective-permute-start(bf16[64,512]{1,0:T(8,128)(2,1)S(1)} %shard_map.55.refs_0_), channel_id=1, source_target_pairs={{0,4},{1,5},{2,6},{3,7},{4,0},{5,1},{6,2},{7,3},{8,14},{9,15},{10,... | collective-permute-start | bytes 196616 | tf_op jit(solution)/shard_map/ppermute | solution.py:342
  7.9 5.6 %collective-permute-start.7 = (bf16[64,512]{1,0:T(8,128)(2,1)S(1)}, bf16[64,512]{1,0:T(8,128)(2,1)S(1)}, u32[]{:S(2)}, u32[]{:S(2)}) collective-permute-start(bf16[64,512]{1,0:T(8,128)(2,1)S(1)} %shard_map.55.refs_0_), channel_id=1, source_target_pairs={{0,2},{1,3},{2,0},{3,1},{4,6},{5,7},{6,4},{7,5},{8,10},{9,11},{10,... | collective-permute-start | bytes 196616 | tf_op jit(solution)/shard_map/ppermute | solution.py:342
  8.5 5.5 %collective-permute-start = (bf16[64,512]{1,0:T(8,128)(2,1)S(1)}, bf16[64,512]{1,0:T(8,128)(2,1)S(1)}, u32[]{:S(2)}, u32[]{:S(2)}) collective-permute-start(bf16[64,512]{1,0:T(8,128)(2,1)S(1)} %shard_map.55.refs_0_), channel_id=1, source_target_pairs={{0,1},{1,0},{2,3},{3,2},{4,5},{5,4},{6,7},{7,6},{8,9},{9,8},{10,11... | collective-permute-start | bytes 196616 | tf_op jit(solution)/shard_map/ppermute | solution.py:304
  10.5 3.6 %collective-permute-start.2 = (bf16[64,512]{1,0:T(8,128)(2,1)S(1)}, bf16[64,512]{1,0:T(8,128)(2,1)S(1)}, u32[]{:S(2)}, u32[]{:S(2)}) collective-permute-start(bf16[64,512]{1,0:T(8,128)(2,1)S(1)} %collective-permute-done.1.refs_2_), channel_id=1, source_target_pairs={{0,1},{1,0},{2,3},{3,2},{4,5},{5,4},{6,7},{7,6},{8,9},{9,8},{10,11... | collective-permute-start | bytes 196616 | tf_op jit(solution)/shard_map/ppermute | solution.py:304
  13.5 4.7 %collective-permute-start.5 = (bf16[64,512]{1,0:T(8,128)(2,1)S(1)}, bf16[64,512]{1,0:T(8,128)(2,1)S(1)}, u32[]{:S(2)}, u32[]{:S(2)}) collective-permute-start(bf16[64,512]{1,0:T(8,128)(2,1)S(1)} %collective-permute-done.4.refs_4_.refs_2_), channel_id=1, source_target_pairs={{0,1},{1,0},{2,3},{3,2},{4,5},{5,4},{6,7},{7,6},{8,9},{9,8},{10,11... | collective-permute-start | bytes 196616 | tf_op jit(solution)/shard_map/ppermute | solution.py:304
  13.5 5.9 %collective-permute-start.8 = (bf16[64,512]{1,0:T(8,128)(2,1)S(1)}, bf16[64,512]{1,0:T(8,128)(2,1)S(1)}, u32[]{:S(2)}, u32[]{:S(2)}) collective-permute-start(bf16[64,512]{1,0:T(8,128)(2,1)S(1)} %collective-permute-done.7.refs_4_.refs_2_), channel_id=1, source_target_pairs={{0,1},{1,0},{2,3},{3,2},{4,5},{5,4},{6,7},{7,6},{8,9},{9,8},{10,11... | collective-permute-start | bytes 196616 | tf_op jit(solution)/shard_map/ppermute | solution.py:304
  15.2 7.3 %collective-permute-start.3 = (bf16[192,256]{1,0:T(8,128)(2,1)S(1)}, bf16[192,256]{1,0:T(8,128)(2,1)S(1)}, u32[]{:S(2)}, u32[]{:S(2)}) collective-permute-start(bf16[192,256]{1,0:T(8,128)(2,1)S(1)} %get-tuple-element.21), channel_id=1, source_target_pairs={{0,24},{8,16},{16,8},{24,0},{1,25},{9,17},{17,9},{25,1},{2,26},{10... | collective-permute-start | bytes 294920 | tf_op jit(solution)/shard_map/ppermute | solution.py:304
  19.3 5.0 %collective-permute-start.6 = (bf16[192,256]{1,0:T(8,128)(2,1)S(1)}, bf16[192,256]{1,0:T(8,128)(2,1)S(1)}, u32[]{:S(2)}, u32[]{:S(2)}) collective-permute-start(bf16[192,256]{1,0:T(8,128)(2,1)S(1)} %get-tuple-element.23), channel_id=1, source_target_pairs={{0,16},{8,24},{16,0},{24,8},{1,17},{9,25},{17,1},{25,9},{2,18},{10... | collective-permute-start | bytes 294920 | tf_op jit(solution)/shard_map/ppermute | solution.py:304
  19.4 6.1 %copy-start.4 = (bf16[64,128]{1,0:T(8,128)(2,1)S(1)}, bf16[64,128]{1,0:T(8,128)(2,1)}, u32[]{:S(2)}) copy-start(bf16[64,128]{1,0:T(8,128)(2,1)} %constant.8.clone.refs_5_) | copy-start | bytes 49156
  19.4 6.1 %copy-start.5 = (bf16[64,128]{1,0:T(8,128)(2,1)S(1)}, bf16[64,128]{1,0:T(8,128)(2,1)}, u32[]{:S(2)}) copy-start(bf16[64,128]{1,0:T(8,128)(2,1)} %constant.7.clone.refs_4_) | copy-start | bytes 49156
  19.4 13.3 %copy-start.1 = (bf16[8,2,512,256]{3,2,1,0:T(8,128)(2,1)S(1)}, bf16[8,2,512,256]{3,2,1,0:T(8,128)(2,1)}, u32[]{:S(2)}) copy-start(bf16[8,2,512,256]{3,2,1,0:T(8,128)(2,1)} %refs_4_.8) | copy-start | bytes 12582916
  20.5 5.0 %collective-permute-start.9 = (bf16[192,256]{1,0:T(8,128)(2,1)S(1)}, bf16[192,256]{1,0:T(8,128)(2,1)S(1)}, u32[]{:S(2)}, u32[]{:S(2)}) collective-permute-start(bf16[192,256]{1,0:T(8,128)(2,1)S(1)} %get-tuple-element.25), channel_id=1, source_target_pairs={{0,8},{8,0},{16,24},{24,16},{1,9},{9,1},{17,25},{25,17},{2,10},{10... | collective-permute-start | bytes 294920 | tf_op jit(solution)/shard_map/ppermute | solution.py:304
  26.1 5.9 %collective-permute-start.10 = (bf16[128,256]{1,0:T(8,128)(2,1)S(1)}, bf16[128,256]{1,0:T(8,128)(2,1)S(1)}, u32[]{:S(2)}, u32[]{:S(2)}) collective-permute-start(bf16[128,256]{1,0:T(8,128)(2,1)S(1)} %get-tuple-element.28), channel_id=1, source_target_pairs={{0,24},{8,16},{16,8},{24,0},{1,25},{9,17},{17,9},{25,1},{2,26},{10... | collective-permute-start | bytes 196616 | tf_op jit(solution)/shard_map/ppermute | solution.py:304
  28.1 4.4 %collective-permute-start.11 = (bf16[128,256]{1,0:T(8,128)(2,1)S(1)}, bf16[128,256]{1,0:T(8,128)(2,1)S(1)}, u32[]{:S(2)}, u32[]{:S(2)}) collective-permute-start(bf16[128,256]{1,0:T(8,128)(2,1)S(1)} %get-tuple-element.29), channel_id=1, source_target_pairs={{0,16},{8,24},{16,0},{24,8},{1,17},{9,25},{17,1},{25,9},{2,18},{10... | collective-permute-start | bytes 196616 | tf_op jit(solution)/shard_map/ppermute | solution.py:304
  28.4 4.3 %collective-permute-start.12 = (bf16[128,256]{1,0:T(8,128)(2,1)S(1)}, bf16[128,256]{1,0:T(8,128)(2,1)S(1)}, u32[]{:S(2)}, u32[]{:S(2)}) collective-permute-start(bf16[128,256]{1,0:T(8,128)(2,1)S(1)} %get-tuple-element.30), channel_id=1, source_target_pairs={{0,8},{8,0},{16,24},{24,16},{1,9},{9,1},{17,25},{25,17},{2,10},{10... | collective-permute-start | bytes 196616 | tf_op jit(solution)/shard_map/ppermute | solution.py:304
  33.9 1.6 %collective-permute-start.13 = (bf16[4,64,512]{2,1,0:T(8,128)(2,1)S(1)}, bf16[4,64,512]{2,1,0:T(8,128)(2,1)S(1)}, u32[]{:S(2)}, u32[]{:S(2)}) collective-permute-start(bf16[4,64,512]{2,1,0:T(8,128)(2,1)S(1)} %shard_map.62), channel_id=1, source_target_pairs={{0,1},{1,0},{2,3},{3,2},{4,5},{5,4},{6,7},{7,6},{8,9},{9,8},{10,11... | collective-permute-start | bytes 786440 | tf_op jit(solution)/shard_map/ppermute | solution.py:304
  35.5 6.8 %collective-permute-start.14 = (bf16[64,512]{1,0:T(8,128)(2,1)S(1)}, bf16[64,512]{1,0:T(8,128)(2,1)S(1)}, u32[]{:S(2)}, u32[]{:S(2)}) collective-permute-start(bf16[64,512]{1,0:T(8,128)(2,1)S(1)} %get-tuple-element.32), channel_id=1, source_target_pairs={{0,6},{1,7},{2,4},{3,5},{4,2},{5,3},{6,0},{7,1},{8,14},{9,15},{10,... | collective-permute-start | bytes 196616 | tf_op jit(solution)/shard_map/ppermute | solution.py:304
  38.0 6.4 %collective-permute-start.15 = (bf16[64,512]{1,0:T(8,128)(2,1)S(1)}, bf16[64,512]{1,0:T(8,128)(2,1)S(1)}, u32[]{:S(2)}, u32[]{:S(2)}) collective-permute-start(bf16[64,512]{1,0:T(8,128)(2,1)S(1)} %get-tuple-element.33), channel_id=1, source_target_pairs={{0,4},{1,5},{2,6},{3,7},{4,0},{5,1},{6,2},{7,3},{8,12},{9,13},{10,... | collective-permute-start | bytes 196616 | tf_op jit(solution)/shard_map/ppermute | solution.py:304
  38.0 6.4 %collective-permute-start.16 = (bf16[64,512]{1,0:T(8,128)(2,1)S(1)}, bf16[64,512]{1,0:T(8,128)(2,1)S(1)}, u32[]{:S(2)}, u32[]{:S(2)}) collective-permute-start(bf16[64,512]{1,0:T(8,128)(2,1)S(1)} %get-tuple-element.34), channel_id=1, source_target_pairs={{0,2},{1,3},{2,0},{3,1},{4,6},{5,7},{6,4},{7,5},{8,10},{9,11},{10,... | collective-permute-start | bytes 196616 | tf_op jit(solution)/shard_map/ppermute | solution.py:304

commit v8 on v7

--- a/solution.py
+++ b/solution.py
@@ -123,51 +123,66 @@
     return sorted({order[a].index(a ^ j) for a in range(shares) if a ^ j})
 
 
+def pieces_of(shares):
+    half = shares // 2
+    return [list(reversed(range(half, shares))), list(reversed(range(half)))]
+
+
 def plane_of(shares):
     return lax.div(lax.axis_index("pts"), lax.axis_size("pts") // shares)
 
 
-def tile_kernel(j, shares, per_share, per_block, *refs):
-    steps = steps_for(j, shares)
-    n = per_share * (1 + len(steps))
+def tile_kernel(targets, shares, per_share, per_block, *refs):
+    steps = sorted({t for j in targets for t in steps_for(j, shares)})
+    n, many = per_share * (1 + len(steps)), len(targets)
     blocks, (orb_ref, sel_ref, coulomb_ref) = refs[:n], refs[n : n + 3]
-    out_ref, form_ref, gathered, wide, cells = refs[-5:]
+    *refs, gathered, wide, cells = refs[-2 * many - 3 :]
+    outs, form_refs = refs[:many], refs[many:]
     local_k, _, norb, points = orb_ref.shape
     group = ROWS // (2 * per_block)
     share = per_share * per_block
+    rows = 2 * share
     me, block = lax.axis_index("ka"), lax.axis_index("pts")
-    offset = jnp.bitwise_xor(me, j)
     order = orders(shares)
     for i, t in enumerate([None] + steps):
         here = 0 if t is None else pick([order[a][t] for a in range(shares)], me)
-
-        @pl.when(offset == here)
-        def _(i=i):
-            for e in range(per_share):
-                place = jnp.bitwise_xor(jnp.bitwise_and(block, per_share - 1), e)
-                gathered[place] = blocks[i * per_share + e][...]
+        for slot, j in enumerate(targets):
+
+            @pl.when(jnp.bitwise_xor(me, j) == here)
+            def _(i=i, slot=slot):
+                for e in range(per_share):
+                    place = jnp.bitwise_xor(jnp.bitwise_and(block, per_share - 1), e)
+                    gathered[slot, place] = blocks[i * per_share + e][...]
 
     for g in range(local_k // group):
-        stacked = jnp.concatenate(
-            [gathered[b, g * ROWS : (g + 1) * ROWS] for b in range(per_share)], axis=0
-        )
-        forms = dot(sel_ref[...], stacked).astype(BF16)
-        rows = 2 * share
+        forms = []
+        for slot in range(many):
+            stacked = jnp.concatenate(
+                [gathered[slot, b, g * ROWS : (g + 1) * ROWS] for b in range(per_share)], axis=0
+            )
+            forms.append(dot(sel_ref[...], stacked).astype(BF16))
         for kk in range(group):
             k = g * group + kk
-            left = forms[2 * kk * rows : (2 * kk + 1) * rows]
-            right = forms[(2 * kk + 1) * rows : (2 * kk + 2) * rows]
-            form = jnp.concatenate([left, right], axis=1)
-            form_ref[k] = form
+            left = [form[2 * kk * rows : (2 * kk + 1) * rows] for form in forms]
+            right = [form[(2 * kk + 1) * rows : (2 * kk + 2) * rows] for form in forms]
+            form = jnp.concatenate(
+                [jnp.concatenate(left, axis=0), jnp.concatenate(right, axis=0)], axis=1
+            )
             tile = dot(form, orb_ref[k].reshape(2 * norb, points))
-            for part in range(2):
-                spread(wide, 2 * k + part, 2 * local_k, tile[part * share : (part + 1) * share])
+            for slot in range(many):
+                form_refs[slot][k] = form[slot * rows : (slot + 1) * rows]
+                for part in range(2):
+                    low = slot * rows + part * share
+                    start = slot * share * 2 * local_k + 2 * k + part
+                    spread(wide, start, 2 * local_k, tile[low : low + share])
     size = share * 2 * local_k
-    out_ref[:size] = take(wide, 0, size).astype(BF16)
-    start = pl.multiple_of(jnp.bitwise_xor(offset, plane_of(shares)) * share, share)
     cells[...] = coulomb_ref[...].astype(F32)
-    pieces = [cells[r, pl.ds(start, share), :] for r in range(local_k)]
-    out_ref[size:] = jnp.concatenate(pieces, axis=0).astype(BF16)
+    for slot, j in enumerate(targets):
+        outs[slot][:size] = take(wide, slot * size, size).astype(BF16)
+        owned = jnp.bitwise_xor(jnp.bitwise_xor(me, j), plane_of(shares))
+        start = pl.multiple_of(owned * share, share)
+        pieces = [cells[r, pl.ds(start, share), :] for r in range(local_k)]
+        outs[slot][size:] = jnp.concatenate(pieces, axis=0).astype(BF16)
 
 
 def transform_kernel(shares, total, share, *refs):
@@ -347,21 +362,25 @@
     piece = shape((share * 2 * local_k, points), BF16)
     both = shape((share * 3 * local_k, points), BF16)
     tiles, forms, before = [None] * shares, [None] * shares, []
-    for j in reversed(range(shares)):
-        taken = [block for t in steps_for(j, shares) for block in came[t]]
-        tiles[j], forms[j] = call(
-            functools.partial(tile_kernel, j, shares, per_share, per_block),
-            [both, shape((local_k, 2 * share, 2 * norb), BF16)],
+    for targets in pieces_of(shares):
+        many = len(targets)
+        steps = sorted({t for j in targets for t in steps_for(j, shares)})
+        taken = [block for t in steps for block in came[t]]
+        result = call(
+            functools.partial(tile_kernel, targets, shares, per_share, per_block),
+            [both] * many + [shape((local_k, 2 * share, 2 * norb), BF16)] * many,
             len(near) + len(taken) + 3,
             [
-                pltpu.VMEM((per_share, local_k * 2 * per_block, norb), BF16),
-                tiled(share * 2 * local_k, points),
+                pltpu.VMEM((many, per_share, local_k * 2 * per_block, norb), BF16),
+                tiled(many * share * 2 * local_k, points),
                 pltpu.VMEM(coulomb.shape, F32),
             ],
             size=6 * MIB,
             unread=len(before),
         )(*near, *taken, orbitals, selector, coulomb, *before)
-        before = [forms[j]]
+        for slot, j in enumerate(targets):
+            tiles[j], forms[j] = result[slot], result[many + slot]
+        before = [forms[targets[0]]]
     tiles = trade(tiles, "ka", 1)
 
     forward, backward = phase_tables(total)

time: 46.3 us -> 45.8 us (0.989)
  Pallas kernels: 9.74 us -> 7.69 us
  waiting for transfers between devices: 15.8 us -> 17.8 us
    ppermute x14, waiting for transfers between devices: 10.8 us -> 13.1 us  [swap(): return lax.ppermute(value, axis, [(i, i ^ mask) for i in range(size)])]
    pallas_call x4 -> x2, Pallas kernels: 4.38 us -> 2.34 us  [body(): call(functools.partial(tile_kernel, targets, shares, per_share, per_block...]
  transfers between devices with their start and end apart: 17 -> 17, of which waited for: 10 -> 13; matrix products, arithmetic and copies ran while one was open for 0% -> 0% of each run, Pallas kernels for 12% -> 8%
where the time goes in v8:
time: 45.8 us; the launch traced here: 45.6 us
  starting transfers between devices  17.8 us (39%)
  waiting for transfers between devices  17.8 us (39%)
  Pallas kernels  7.69 us (17%)
  local copies, waits for them, and re-layouts  2.21 us (5%)
    ppermute x14, waiting for transfers between devices, swap(): return lax.ppermute(value, axis, [(i, i ^ mask) for i in range(size)])  13.1 us
    ppermute x14, starting transfers between devices, swap(): return lax.ppermute(value, axis, [(i, i ^ mask) for i in range(size)])  12.1 us
    ppermute x3, starting transfers between devices, body(): block = lax.ppermute(edge, ('ka', 'pts'), pairs)  5.68 us
    ppermute x3, waiting for transfers between devices, body(): block = lax.ppermute(edge, ('ka', 'pts'), pairs)  4.73 us
    pallas_call x2, Pallas kernels, body(): call(functools.partial(tile_kernel, targets, shares, per_share, per_block...  2.34 us
    pallas_call x2, Pallas kernels, body(): call(functools.partial(weight_kernel, shares, flip, out_rows), shape((chu...  2.33 us
    unnamed x12, local copies, waits for them, and re-layouts  2.21 us
    pallas_call x1, Pallas kernels, body(): call(functools.partial(exchange_kernel, chunks, shares, 1.0 / math.sqrt(p...  1.76 us
  transfers between devices with their start and end apart: 17, of which 13 were waited for; matrix products, arithmetic and copies ran while one was open for 0% of the time, Pallas kernels for 8%

profile of v8, /device:TPU:0, one launch (start us, length us, event | category | flops | bytes accessed | tf_op | source)
XLA Modules:
  0.0 45.6 jit_solution(2134524981445843179)
XLA Ops:
  0.0 2.2 %copy-done = bf16[8,2,512,256]{3,2,1,0:T(8,128)(2,1)S(1)} copy-done((bf16[8,2,512,256]{3,2,1,0:T(8,128)(2,1)S(1)}, bf16[8,2,512,256]{3,2,1,0:T(8,128)(2,1)}, u32[]{:S(2)}) %copy-start) | copy-done | bytes 4194328
  2.2 0.6 %shard_map.55.refs_0_ = bf16[64,512]{1,0:T(8,128)(2,1)S(1)} custom-call(bf16[8,2,512,256]{3,2,1,0:T(8,128)(2,1)S(1)} %copy-done), custom_call_target="tpu_custom_call" | custom-call | bytes 4194304 | tf_op jit(solution)/shard_map/pallas_call | solution.py:338
  2.9 4.1 %collective-permute-start.3 = (bf16[64,512]{1,0:T(8,128)(2,1)S(1)}, bf16[64,512]{1,0:T(8,128)(2,1)S(1)}, u32[]{:S(2)}, u32[]{:S(2)}) collective-permute-start(bf16[64,512]{1,0:T(8,128)(2,1)S(1)} %shard_map.55.refs_0_), channel_id=1, source_target_pairs={{0,4},{1,5},{2,6},{3,7},{4,0},{5,1},{6,2},{7,3},{8,14},{9,15},{10,... | collective-permute-start | bytes 196616 | tf_op jit(solution)/shard_map/ppermute | solution.py:357
  7.0 1.3 %collective-permute-start.1 = (bf16[64,512]{1,0:T(8,128)(2,1)S(1)}, bf16[64,512]{1,0:T(8,128)(2,1)S(1)}, u32[]{:S(2)}, u32[]{:S(2)}) collective-permute-start(bf16[64,512]{1,0:T(8,128)(2,1)S(1)} %shard_map.55.refs_0_), channel_id=1, source_target_pairs={{0,6},{1,7},{2,4},{3,5},{4,2},{5,3},{6,0},{7,1},{8,12},{9,13},{10,... | collective-permute-start | bytes 196616 | tf_op jit(solution)/shard_map/ppermute | solution.py:357
  8.3 0.2 collective-permute-start.7
  8.5 2.2 %collective-permute-done.3.refs_4_.refs_2_ = bf16[64,512]{1,0:T(8,128)(2,1)S(1)} collective-permute-done((bf16[64,512]{1,0:T(8,128)(2,1)S(1)}, bf16[64,512]{1,0:T(8,128)(2,1)S(1)}, u32[]{:S(2)}, u32[]{:S(2)}) %collective-permute-start.3) | collective-permute-done | bytes 65568 | tf_op jit(solution)/shard_map/ppermute | solution.py:357
  10.7 2.5 %collective-permute-done.1.refs_2_ = bf16[64,512]{1,0:T(8,128)(2,1)S(1)} collective-permute-done((bf16[64,512]{1,0:T(8,128)(2,1)S(1)}, bf16[64,512]{1,0:T(8,128)(2,1)S(1)}, u32[]{:S(2)}, u32[]{:S(2)}) %collective-permute-start.1) | collective-permute-done | bytes 65568 | tf_op jit(solution)/shard_map/ppermute | solution.py:357
  13.3 0.4 collective-permute-start.8
  13.7 0.7 %collective-permute-done.2.refs_3_ = bf16[64,512]{1,0:T(8,128)(2,1)S(1)} collective-permute-done((bf16[64,512]{1,0:T(8,128)(2,1)S(1)}, bf16[64,512]{1,0:T(8,128)(2,1)S(1)}, u32[]{:S(2)}, u32[]{:S(2)}) %collective-permute-start.2) | collective-permute-done | bytes 65568 | tf_op jit(solution)/shard_map/ppermute | solution.py:319
  14.4 1.2 %shard_map.56 = (bf16[192,256]{1,0:T(8,128)(2,1)S(1)}, bf16[192,256]{1,0:T(8,128)(2,1)S(1)}, bf16[8,16,1024]{2,1,0:T(8,128)(2,1)S(1)}, bf16[8,16,1024]{2,1,0:T(8,128)(2,1)S(1)}) custom-call(bf16[64,512]{1,0:T(8,128)(2,1)S(1)} %shard_map.55.refs_0_, bf16[64,512]{1,0:T(8,128)(2,1)S(1)} %collective-permute-done.refs_1_, ...), custom_call_target="tpu_custom_call" | custom-call | bytes 6291456 | tf_op jit(solution)/shard_map/pallas_call | solution.py:369
  15.6 2.7 %collective-permute-start.5 = (bf16[192,256]{1,0:T(8,128)(2,1)S(1)}, bf16[192,256]{1,0:T(8,128)(2,1)S(1)}, u32[]{:S(2)}, u32[]{:S(2)}) collective-permute-start(bf16[192,256]{1,0:T(8,128)(2,1)S(1)} %get-tuple-element.21), channel_id=1, source_target_pairs={{0,24},{8,16},{16,8},{24,0},{1,25},{9,17},{17,9},{25,1},{2,26},{10... | collective-permute-start | bytes 294920 | tf_op jit(solution)/shard_map/ppermute | solution.py:319
  18.4 0.7 %collective-permute-start.6 = (bf16[192,256]{1,0:T(8,128)(2,1)S(1)}, bf16[192,256]{1,0:T(8,128)(2,1)S(1)}, u32[]{:S(2)}, u32[]{:S(2)}) collective-permute-start(bf16[192,256]{1,0:T(8,128)(2,1)S(1)} %get-tuple-element.22), channel_id=1, source_target_pairs={{0,16},{8,24},{16,0},{24,8},{1,17},{9,25},{17,1},{25,9},{2,18},{10... | collective-permute-start | bytes 294920 | tf_op jit(solution)/shard_map/ppermute | solution.py:319
  19.0 1.2 %shard_map.57 = (bf16[192,256]{1,0:T(8,128)(2,1)S(1)}, bf16[192,256]{1,0:T(8,128)(2,1)S(1)}, bf16[8,16,1024]{2,1,0:T(8,128)(2,1)S(1)}, bf16[8,16,1024]{2,1,0:T(8,128)(2,1)S(1)}) custom-call(bf16[64,512]{1,0:T(8,128)(2,1)S(1)} %shard_map.55.refs_0_, bf16[64,512]{1,0:T(8,128)(2,1)S(1)} %collective-permute-done.refs_1_, ...), custom_call_target="tpu_custom_call" | custom-call | bytes 6291456 | tf_op jit(solution)/shard_map/pallas_call | solution.py:369
  20.2 0.2 collective-permute-start.9
  20.4 1.5 %collective-permute-done.5.refs_0_ = bf16[192,256]{1,0:T(8,128)(2,1)S(1)} collective-permute-done((bf16[192,256]{1,0:T(8,128)(2,1)S(1)}, bf16[192,256]{1,0:T(8,128)(2,1)S(1)}, u32[]{:S(2)}, u32[]{:S(2)}) %collective-permute-start.5) | collective-permute-done | bytes 98336 | tf_op jit(solution)/shard_map/ppermute | solution.py:319
  21.9 2.0 %collective-permute-done.6.refs_1_ = bf16[192,256]{1,0:T(8,128)(2,1)S(1)} collective-permute-done((bf16[192,256]{1,0:T(8,128)(2,1)S(1)}, bf16[192,256]{1,0:T(8,128)(2,1)S(1)}, u32[]{:S(2)}, u32[]{:S(2)}) %collective-permute-start.6) | collective-permute-done | bytes 98336 | tf_op jit(solution)/shard_map/ppermute | solution.py:319
  23.9 1.0 %collective-permute-done.9.refs_2_ = bf16[192,256]{1,0:T(8,128)(2,1)S(1)} collective-permute-done((bf16[192,256]{1,0:T(8,128)(2,1)S(1)}, bf16[192,256]{1,0:T(8,128)(2,1)S(1)}, u32[]{:S(2)}, u32[]{:S(2)}) %collective-permute-start.9) | collective-permute-done | bytes 98336 | tf_op jit(solution)/shard_map/ppermute | solution.py:319
  24.9 0.6 %shard_map.58 = (bf16[128,256]{1,0:T(8,128)(2,1)S(1)}, bf16[128,256]{1,0:T(8,128)(2,1)S(1)}, bf16[128,256]{1,0:T(8,128)(2,1)S(1)}, bf16[128,256]{1,0:T(8,128)(2,1)S(1)}) custom-call(bf16[192,256]{1,0:T(8,128)(2,1)S(1)} %collective-permute-done.5.refs_0_, bf16[192,256]{1,0:T(8,128)(2,1)S(1)} %collective-permute-done.6.refs_1_, ...), custom_call_target="tpu_custom_call" | custom-call | bytes 2097152 | tf_op jit(solution)/shard_map/pallas_call | solution.py:387
  25.5 1.2 %collective-permute-start.10 = (bf16[128,256]{1,0:T(8,128)(2,1)S(1)}, bf16[128,256]{1,0:T(8,128)(2,1)S(1)}, u32[]{:S(2)}, u32[]{:S(2)}) collective-permute-start(bf16[128,256]{1,0:T(8,128)(2,1)S(1)} %get-tuple-element.26), channel_id=1, source_target_pairs={{0,24},{8,16},{16,8},{24,0},{1,25},{9,17},{17,9},{25,1},{2,26},{10... | collective-permute-start | bytes 196616 | tf_op jit(solution)/shard_map/ppermute | solution.py:319
  26.7 1.2 %collective-permute-start.11 = (bf16[128,256]{1,0:T(8,128)(2,1)S(1)}, bf16[128,256]{1,0:T(8,128)(2,1)S(1)}, u32[]{:S(2)}, u32[]{:S(2)}) collective-permute-start(bf16[128,256]{1,0:T(8,128)(2,1)S(1)} %get-tuple-element.27), channel_id=1, source_target_pairs={{0,16},{8,24},{16,0},{24,8},{1,17},{9,25},{17,1},{25,9},{2,18},{10... | collective-permute-start | bytes 196616 | tf_op jit(solution)/shard_map/ppermute | solution.py:319
  27.8 1.2 %collective-permute-start.12 = (bf16[128,256]{1,0:T(8,128)(2,1)S(1)}, bf16[128,256]{1,0:T(8,128)(2,1)S(1)}, u32[]{:S(2)}, u32[]{:S(2)}) collective-permute-start(bf16[128,256]{1,0:T(8,128)(2,1)S(1)} %get-tuple-element.28), channel_id=1, source_target_pairs={{0,8},{8,0},{16,24},{24,16},{1,9},{9,1},{17,25},{25,17},{2,10},{10... | collective-permute-start | bytes 196616 | tf_op jit(solution)/shard_map/ppermute | solution.py:319
  29.0 2.0 %collective-permute-done.10.refs_0_ = bf16[128,256]{1,0:T(8,128)(2,1)S(1)} collective-permute-done((bf16[128,256]{1,0:T(8,128)(2,1)S(1)}, bf16[128,256]{1,0:T(8,128)(2,1)S(1)}, u32[]{:S(2)}, u32[]{:S(2)}) %collective-permute-start.10) | collective-permute-done | bytes 65568 | tf_op jit(solution)/shard_map/ppermute | solution.py:319
  31.1 0.4 collective-permute-done.11.refs_1_
  31.5 0.6 %collective-permute-done.12.refs_2_ = bf16[128,256]{1,0:T(8,128)(2,1)S(1)} collective-permute-done((bf16[128,256]{1,0:T(8,128)(2,1)S(1)}, bf16[128,256]{1,0:T(8,128)(2,1)S(1)}, u32[]{:S(2)}, u32[]{:S(2)}) %collective-permute-start.12) | collective-permute-done | bytes 65568 | tf_op jit(solution)/shard_map/ppermute | solution.py:319
  32.1 1.2 %shard_map.60 = bf16[4,64,512]{2,1,0:T(8,128)(2,1)S(1)} custom-call(bf16[128,256]{1,0:T(8,128)(2,1)S(1)} %collective-permute-done.10.refs_0_, bf16[128,256]{1,0:T(8,128)(2,1)S(1)} %collective-permute-done.11.refs_1_, bf16[128,256]{1,0:T(8,128)(2,1)S(1)} %collective-permute-done.12.refs_2_, bf16[128,256]{1,0:T(8,128)(2,1)S(1)} %get-tuple-element.29.refs_3_, ...), custom_call_target="tpu_custom_call" | custom-call | bytes 6291456 | tf_op jit(solution)/shard_map/pallas_call | solution.py:404
  33.4 1.2 %shard_map.59.keep_ref = f32[4,64,512]{2,1,0:T(8,128)S(1)} custom-call(bf16[128,256]{1,0:T(8,128)(2,1)S(1)} %collective-permute-done.10.refs_0_, bf16[128,256]{1,0:T(8,128)(2,1)S(1)} %collective-permute-done.11.refs_1_, bf16[128,256]{1,0:T(8,128)(2,1)S(1)} %collective-permute-done.12.refs_2_, bf16[128,256]{1,0:T(8,128)(2,1)S(1)} %get-tuple-element.29.refs_3_, ...), custom_call_target="tpu_custom_call" | custom-call | bytes 6291456 | tf_op jit(solution)/shard_map/pallas_call | solution.py:404
  34.5 0.4 collective-permute-done.13.came_ref
  34.9 2.5 %collective-permute-start.14 = (bf16[64,512]{1,0:T(8,128)(2,1)S(1)}, bf16[64,512]{1,0:T(8,128)(2,1)S(1)}, u32[]{:S(2)}, u32[]{:S(2)}) collective-permute-start(bf16[64,512]{1,0:T(8,128)(2,1)S(1)} %get-tuple-element.30), channel_id=1, source_target_pairs={{0,6},{1,7},{2,4},{3,5},{4,2},{5,3},{6,0},{7,1},{8,14},{9,15},{10,... | collective-permute-start | bytes 196616 | tf_op jit(solution)/shard_map/ppermute | solution.py:319
  37.5 1.9 %collective-permute-start.16 = (bf16[64,512]{1,0:T(8,128)(2,1)S(1)}, bf16[64,512]{1,0:T(8,128)(2,1)S(1)}, u32[]{:S(2)}, u32[]{:S(2)}) collective-permute-start(bf16[64,512]{1,0:T(8,128)(2,1)S(1)} %get-tuple-element.32), channel_id=1, source_target_pairs={{0,2},{1,3},{2,0},{3,1},{4,6},{5,7},{6,4},{7,5},{8,10},{9,11},{10,... | collective-permute-start | bytes 196616 | tf_op jit(solution)/shard_map/ppermute | solution.py:319
  39.4 2.3 %collective-permute-done.14.refs_0_ = bf16[64,512]{1,0:T(8,128)(2,1)S(1)} collective-permute-done((bf16[64,512]{1,0:T(8,128)(2,1)S(1)}, bf16[64,512]{1,0:T(8,128)(2,1)S(1)}, u32[]{:S(2)}, u32[]{:S(2)}) %collective-permute-start.14) | collective-permute-done | bytes 65568 | tf_op jit(solution)/shard_map/ppermute | solution.py:319
  41.7 2.1 %collective-permute-done.15.refs_1_ = bf16[64,512]{1,0:T(8,128)(2,1)S(1)} collective-permute-done((bf16[64,512]{1,0:T(8,128)(2,1)S(1)}, bf16[64,512]{1,0:T(8,128)(2,1)S(1)}, u32[]{:S(2)}, u32[]{:S(2)}) %collective-permute-start.15) | collective-permute-done | bytes 65568 | tf_op jit(solution)/shard_map/ppermute | solution.py:319
  43.9 1.8 %shard_map.62 = bf16[64,4,16,128]{3,2,1,0:T(8,128)(2,1)} custom-call(bf16[64,512]{1,0:T(8,128)(2,1)S(1)} %collective-permute-done.14.refs_0_, bf16[64,512]{1,0:T(8,128)(2,1)S(1)} %collective-permute-done.15.refs_1_, bf16[64,512]{1,0:T(8,128)(2,1)S(1)} %collective-permute-done.16.refs_2_, f32[64,512]{1,0:T(8,128)S(1)} %get-tuple-element.33.refs_3_, ...), custom_call_target="tpu_custom_call" | custom-call | bytes 4194304 | tf_op jit(solution)/shard_map/pallas_call | solution.py:423
  (22 shorter events, 0.2 us)
Async XLA Ops:
  0.0 2.2 %copy-start = (bf16[8,2,512,256]{3,2,1,0:T(8,128)(2,1)S(1)}, bf16[8,2,512,256]{3,2,1,0:T(8,128)(2,1)}, u32[]{:S(2)}) copy-start(bf16[8,2,512,256]{3,2,1,0:T(8,128)(2,1)} %refs_4_.4) | copy-start | bytes 12582916
  2.2 12.2 %copy-start.2 = (bf16[8,32,256]{2,1,0:T(8,128)(2,1)S(1)}, bf16[8,32,256]{2,1,0:T(8,128)(2,1)}, u32[]{:S(2)}) copy-start(bf16[8,32,256]{2,1,0:T(8,128)(2,1)} %refs_8_.3) | copy-start | bytes 393220
  2.2 12.3 %copy-start.3 = (bf16[64,32]{1,0:T(8,128)(2,1)S(1)}, bf16[64,32]{1,0:T(8,128)(2,1)}, u32[]{:S(2)}) copy-start(bf16[64,32]{1,0:T(8,128)(2,1)} %constant.6.clone.refs_7_) | copy-start | bytes 12292
  2.8 22.1 %copy-start.4 = (bf16[64,128]{1,0:T(8,128)(2,1)S(1)}, bf16[64,128]{1,0:T(8,128)(2,1)}, u32[]{:S(2)}) copy-start(bf16[64,128]{1,0:T(8,128)(2,1)} %constant.8.clone.refs_5_) | copy-start | bytes 49156
  2.8 22.1 %copy-start.5 = (bf16[64,128]{1,0:T(8,128)(2,1)S(1)}, bf16[64,128]{1,0:T(8,128)(2,1)}, u32[]{:S(2)}) copy-start(bf16[64,128]{1,0:T(8,128)(2,1)} %constant.7.clone.refs_4_) | copy-start | bytes 49156
  2.8 29.3 %copy-start.1 = (bf16[8,2,512,256]{3,2,1,0:T(8,128)(2,1)S(1)}, bf16[8,2,512,256]{3,2,1,0:T(8,128)(2,1)}, u32[]{:S(2)}) copy-start(bf16[8,2,512,256]{3,2,1,0:T(8,128)(2,1)} %refs_4_.4) | copy-start | bytes 12582916
  2.9 7.9 %collective-permute-start.3 = (bf16[64,512]{1,0:T(8,128)(2,1)S(1)}, bf16[64,512]{1,0:T(8,128)(2,1)S(1)}, u32[]{:S(2)}, u32[]{:S(2)}) collective-permute-start(bf16[64,512]{1,0:T(8,128)(2,1)S(1)} %shard_map.55.refs_0_), channel_id=1, source_target_pairs={{0,4},{1,5},{2,6},{3,7},{4,0},{5,1},{6,2},{7,3},{8,14},{9,15},{10,... | collective-permute-start | bytes 196616 | tf_op jit(solution)/shard_map/ppermute | solution.py:357
  7.0 6.2 %collective-permute-start.1 = (bf16[64,512]{1,0:T(8,128)(2,1)S(1)}, bf16[64,512]{1,0:T(8,128)(2,1)S(1)}, u32[]{:S(2)}, u32[]{:S(2)}) collective-permute-start(bf16[64,512]{1,0:T(8,128)(2,1)S(1)} %shard_map.55.refs_0_), channel_id=1, source_target_pairs={{0,6},{1,7},{2,4},{3,5},{4,2},{5,3},{6,0},{7,1},{8,12},{9,13},{10,... | collective-permute-start | bytes 196616 | tf_op jit(solution)/shard_map/ppermute | solution.py:357
  8.3 5.0 %collective-permute-start.7 = (bf16[64,512]{1,0:T(8,128)(2,1)S(1)}, bf16[64,512]{1,0:T(8,128)(2,1)S(1)}, u32[]{:S(2)}, u32[]{:S(2)}) collective-permute-start(bf16[64,512]{1,0:T(8,128)(2,1)S(1)} %shard_map.55.refs_0_), channel_id=1, source_target_pairs={{0,2},{1,3},{2,0},{3,1},{4,6},{5,7},{6,4},{7,5},{8,10},{9,11},{10,... | collective-permute-start | bytes 196616 | tf_op jit(solution)/shard_map/ppermute | solution.py:357
  8.5 5.2 %collective-permute-start = (bf16[64,512]{1,0:T(8,128)(2,1)S(1)}, bf16[64,512]{1,0:T(8,128)(2,1)S(1)}, u32[]{:S(2)}, u32[]{:S(2)}) collective-permute-start(bf16[64,512]{1,0:T(8,128)(2,1)S(1)} %shard_map.55.refs_0_), channel_id=1, source_target_pairs={{0,1},{1,0},{2,3},{3,2},{4,5},{5,4},{6,7},{7,6},{8,9},{9,8},{10,11... | collective-permute-start | bytes 196616 | tf_op jit(solution)/shard_map/ppermute | solution.py:319
  10.7 3.0 %collective-permute-start.4 = (bf16[64,512]{1,0:T(8,128)(2,1)S(1)}, bf16[64,512]{1,0:T(8,128)(2,1)S(1)}, u32[]{:S(2)}, u32[]{:S(2)}) collective-permute-start(bf16[64,512]{1,0:T(8,128)(2,1)S(1)} %collective-permute-done.3.refs_4_.refs_2_), channel_id=1, source_target_pairs={{0,1},{1,0},{2,3},{3,2},{4,5},{5,4},{6,7},{7,6},{8,9},{9,8},{10,11... | collective-permute-start | bytes 196616 | tf_op jit(solution)/shard_map/ppermute | solution.py:319
  13.2 1.3 %collective-permute-start.2 = (bf16[64,512]{1,0:T(8,128)(2,1)S(1)}, bf16[64,512]{1,0:T(8,128)(2,1)S(1)}, u32[]{:S(2)}, u32[]{:S(2)}) collective-permute-start(bf16[64,512]{1,0:T(8,128)(2,1)S(1)} %collective-permute-done.1.refs_2_), channel_id=1, source_target_pairs={{0,1},{1,0},{2,3},{3,2},{4,5},{5,4},{6,7},{7,6},{8,9},{9,8},{10,11... | collective-permute-start | bytes 196616 | tf_op jit(solution)/shard_map/ppermute | solution.py:319
  13.3 5.8 %collective-permute-start.8 = (bf16[64,512]{1,0:T(8,128)(2,1)S(1)}, bf16[64,512]{1,0:T(8,128)(2,1)S(1)}, u32[]{:S(2)}, u32[]{:S(2)}) collective-permute-start(bf16[64,512]{1,0:T(8,128)(2,1)S(1)} %collective-permute-done.7.refs_4_), channel_id=1, source_target_pairs={{0,1},{1,0},{2,3},{3,2},{4,5},{5,4},{6,7},{7,6},{8,9},{9,8},{10,11... | collective-permute-start | bytes 196616 | tf_op jit(solution)/shard_map/ppermute | solution.py:319
  15.6 6.3 %collective-permute-start.5 = (bf16[192,256]{1,0:T(8,128)(2,1)S(1)}, bf16[192,256]{1,0:T(8,128)(2,1)S(1)}, u32[]{:S(2)}, u32[]{:S(2)}) collective-permute-start(bf16[192,256]{1,0:T(8,128)(2,1)S(1)} %get-tuple-element.21), channel_id=1, source_target_pairs={{0,24},{8,16},{16,8},{24,0},{1,25},{9,17},{17,9},{25,1},{2,26},{10... | collective-permute-start | bytes 294920 | tf_op jit(solution)/shard_map/ppermute | solution.py:319
  18.4 5.6 %collective-permute-start.6 = (bf16[192,256]{1,0:T(8,128)(2,1)S(1)}, bf16[192,256]{1,0:T(8,128)(2,1)S(1)}, u32[]{:S(2)}, u32[]{:S(2)}) collective-permute-start(bf16[192,256]{1,0:T(8,128)(2,1)S(1)} %get-tuple-element.22), channel_id=1, source_target_pairs={{0,16},{8,24},{16,0},{24,8},{1,17},{9,25},{17,1},{25,9},{2,18},{10... | collective-permute-start | bytes 294920 | tf_op jit(solution)/shard_map/ppermute | solution.py:319
  20.2 4.7 %collective-permute-start.9 = (bf16[192,256]{1,0:T(8,128)(2,1)S(1)}, bf16[192,256]{1,0:T(8,128)(2,1)S(1)}, u32[]{:S(2)}, u32[]{:S(2)}) collective-permute-start(bf16[192,256]{1,0:T(8,128)(2,1)S(1)} %get-tuple-element.24), channel_id=1, source_target_pairs={{0,8},{8,0},{16,24},{24,16},{1,9},{9,1},{17,25},{25,17},{2,10},{10... | collective-permute-start | bytes 294920 | tf_op jit(solution)/shard_map/ppermute | solution.py:319
  25.5 5.6 %collective-permute-start.10 = (bf16[128,256]{1,0:T(8,128)(2,1)S(1)}, bf16[128,256]{1,0:T(8,128)(2,1)S(1)}, u32[]{:S(2)}, u32[]{:S(2)}) collective-permute-start(bf16[128,256]{1,0:T(8,128)(2,1)S(1)} %get-tuple-element.26), channel_id=1, source_target_pairs={{0,24},{8,16},{16,8},{24,0},{1,25},{9,17},{17,9},{25,1},{2,26},{10... | collective-permute-start | bytes 196616 | tf_op jit(solution)/shard_map/ppermute | solution.py:319
  26.7 4.8 %collective-permute-start.11 = (bf16[128,256]{1,0:T(8,128)(2,1)S(1)}, bf16[128,256]{1,0:T(8,128)(2,1)S(1)}, u32[]{:S(2)}, u32[]{:S(2)}) collective-permute-start(bf16[128,256]{1,0:T(8,128)(2,1)S(1)} %get-tuple-element.27), channel_id=1, source_target_pairs={{0,16},{8,24},{16,0},{24,8},{1,17},{9,25},{17,1},{25,9},{2,18},{10... | collective-permute-start | bytes 196616 | tf_op jit(solution)/shard_map/ppermute | solution.py:319
  27.8 4.3 %collective-permute-start.12 = (bf16[128,256]{1,0:T(8,128)(2,1)S(1)}, bf16[128,256]{1,0:T(8,128)(2,1)S(1)}, u32[]{:S(2)}, u32[]{:S(2)}) collective-permute-start(bf16[128,256]{1,0:T(8,128)(2,1)S(1)} %get-tuple-element.28), channel_id=1, source_target_pairs={{0,8},{8,0},{16,24},{24,16},{1,9},{9,1},{17,25},{25,17},{2,10},{10... | collective-permute-start | bytes 196616 | tf_op jit(solution)/shard_map/ppermute | solution.py:319
  33.3 1.6 %collective-permute-start.13 = (bf16[4,64,512]{2,1,0:T(8,128)(2,1)S(1)}, bf16[4,64,512]{2,1,0:T(8,128)(2,1)S(1)}, u32[]{:S(2)}, u32[]{:S(2)}) collective-permute-start(bf16[4,64,512]{2,1,0:T(8,128)(2,1)S(1)} %shard_map.60), channel_id=1, source_target_pairs={{0,1},{1,0},{2,3},{3,2},{4,5},{5,4},{6,7},{7,6},{8,9},{9,8},{10,11... | collective-permute-start | bytes 786440 | tf_op jit(solution)/shard_map/ppermute | solution.py:319
  34.9 6.8 %collective-permute-start.14 = (bf16[64,512]{1,0:T(8,128)(2,1)S(1)}, bf16[64,512]{1,0:T(8,128)(2,1)S(1)}, u32[]{:S(2)}, u32[]{:S(2)}) collective-permute-start(bf16[64,512]{1,0:T(8,128)(2,1)S(1)} %get-tuple-element.30), channel_id=1, source_target_pairs={{0,6},{1,7},{2,4},{3,5},{4,2},{5,3},{6,0},{7,1},{8,14},{9,15},{10,... | collective-permute-start | bytes 196616 | tf_op jit(solution)/shard_map/ppermute | solution.py:319
  37.5 6.4 %collective-permute-start.15 = (bf16[64,512]{1,0:T(8,128)(2,1)S(1)}, bf16[64,512]{1,0:T(8,128)(2,1)S(1)}, u32[]{:S(2)}, u32[]{:S(2)}) collective-permute-start(bf16[64,512]{1,0:T(8,128)(2,1)S(1)} %get-tuple-element.31), channel_id=1, source_target_pairs={{0,4},{1,5},{2,6},{3,7},{4,0},{5,1},{6,2},{7,3},{8,12},{9,13},{10,... | collective-permute-start | bytes 196616 | tf_op jit(solution)/shard_map/ppermute | solution.py:319
  37.5 6.4 %collective-permute-start.16 = (bf16[64,512]{1,0:T(8,128)(2,1)S(1)}, bf16[64,512]{1,0:T(8,128)(2,1)S(1)}, u32[]{:S(2)}, u32[]{:S(2)}) collective-permute-start(bf16[64,512]{1,0:T(8,128)(2,1)S(1)} %get-tuple-element.32), channel_id=1, source_target_pairs={{0,2},{1,3},{2,0},{3,1},{4,6},{5,7},{6,4},{7,5},{8,10},{9,11},{10,... | collective-permute-start | bytes 196616 | tf_op jit(solution)/shard_map/ppermute | solution.py:319

commit v9 on v8

--- a/solution.py
+++ b/solution.py
@@ -89,8 +89,11 @@
     )
 
 
-def edge_kernel(per_block, orb_ref, edge_ref):
-    local_k = orb_ref.shape[0]
+def edge_kernel(per_block, orb_hbm, edge_ref, orb_ref, sems):
+    local_k = orb_hbm.shape[0]
+    copies = [pltpu.make_async_copy(orb_hbm.at[k], orb_ref.at[k], sems.at[k]) for k in range(local_k)]
+    for copy in copies:
+        copy.start()
     row = lax.broadcasted_iota(jnp.int32, (2 * per_block, LANES), 0)
     lane = lax.broadcasted_iota(jnp.int32, (2 * per_block, LANES), 1)
     one, zero = jnp.ones(row.shape, F32), jnp.zeros(row.shape, F32)
@@ -100,6 +103,7 @@
     for g in range(local_k // group):
         rows = []
         for k in range(g * group, (g + 1) * group):
+            copies[k].wait()
             rows.append(
                 dot(first, orb_ref[k, 0, :, :LANES], ((1,), (1,)))
                 + dot(second, orb_ref[k, 1, :, :LANES], ((1,), (1,)))
@@ -335,11 +339,14 @@
     group = ROWS // (2 * per_block)
     shape = jax.ShapeDtypeStruct
 
-    edge = call(
+    edge, orbitals = call(
         functools.partial(edge_kernel, per_block),
-        shape((local_k * 2 * per_block, norb), BF16),
-        1,
-        size=4 * MIB,
+        [shape((local_k * 2 * per_block, norb), BF16), shape(orbitals.shape, BF16)],
+        0,
+        [pltpu.SemaphoreType.DMA((local_k,))],
+        limit=47,
+        size=8 * MIB,
+        unread=1,
     )(orbitals)
     per_share = blocks // shares
     order = orders(shares)

time: 45.8 us -> 45.6 us (level)
  local copies, waits for them, and re-layouts: 2.21 us -> 0.01 us
  Pallas kernels: 7.69 us -> 9.72 us
    unnamed x12 -> x8, local copies, waits for them, and re-layouts: 2.21 us -> 0.01 us
    pallas_call x1, Pallas kernels: 0.64 us -> 2.63 us  [body(): call(functools.partial(edge_kernel, per_block), [shape((local_k * 2 * per...]
where the time goes in v9:
time: 45.6 us; the launch traced here: 45.4 us
  starting transfers between devices  17.8 us (39%)
  waiting for transfers between devices  17.8 us (39%)
  Pallas kernels  9.72 us (21%)
    ppermute x14, waiting for transfers between devices, swap(): return lax.ppermute(value, axis, [(i, i ^ mask) for i in range(size)])  13.1 us
    ppermute x14, starting transfers between devices, swap(): return lax.ppermute(value, axis, [(i, i ^ mask) for i in range(size)])  12.1 us
    ppermute x3, starting transfers between devices, body(): block = lax.ppermute(edge, ('ka', 'pts'), pairs)  5.68 us
    ppermute x3, waiting for transfers between devices, body(): block = lax.ppermute(edge, ('ka', 'pts'), pairs)  4.73 us
    pallas_call x1, Pallas kernels, body(): call(functools.partial(edge_kernel, per_block), [shape((local_k * 2 * per...  2.63 us
    pallas_call x2, Pallas kernels, body(): call(functools.partial(tile_kernel, targets, shares, per_share, per_block...  2.38 us
    pallas_call x2, Pallas kernels, body(): call(functools.partial(weight_kernel, shares, flip, out_rows), shape((chu...  2.33 us
    pallas_call x1, Pallas kernels, body(): call(functools.partial(exchange_kernel, chunks, shares, 1.0 / math.sqrt(p...  1.76 us
  transfers between devices with their start and end apart: 17, of which 13 were waited for; matrix products, arithmetic and copies ran while one was open for 0% of the time, Pallas kernels for 8%

profile of v9, /device:TPU:0, one launch (start us, length us, event | category | flops | bytes accessed | tf_op | source)
XLA Modules:
  0.0 45.4 jit_solution(2460898580721954882)
XLA Ops:
  0.0 2.6 %shard_map.55 = (bf16[64,512]{1,0:T(8,128)(2,1)S(1)}, bf16[8,2,512,256]{3,2,1,0:T(8,128)(2,1)S(1)}) custom-call(bf16[8,2,512,256]{3,2,1,0:T(8,128)(2,1)} %orb_hbm.1), custom_call_target="tpu_custom_call" | custom-call | bytes 8388608 | tf_op jit(solution)/shard_map/pallas_call | solution.py:342
  2.6 4.1 %collective-permute-start.3 = (bf16[64,512]{1,0:T(8,128)(2,1)S(1)}, bf16[64,512]{1,0:T(8,128)(2,1)S(1)}, u32[]{:S(2)}, u32[]{:S(2)}) collective-permute-start(bf16[64,512]{1,0:T(8,128)(2,1)S(1)} %get-tuple-element.23.refs_0_), channel_id=1, source_target_pairs={{0,4},{1,5},{2,6},{3,7},{4,0},{5,1},{6,2},{7,3},{8,14},{9,15},{10,... | collective-permute-start | bytes 196616 | tf_op jit(solution)/shard_map/ppermute | solution.py:364
  6.7 1.3 %collective-permute-start.1 = (bf16[64,512]{1,0:T(8,128)(2,1)S(1)}, bf16[64,512]{1,0:T(8,128)(2,1)S(1)}, u32[]{:S(2)}, u32[]{:S(2)}) collective-permute-start(bf16[64,512]{1,0:T(8,128)(2,1)S(1)} %get-tuple-element.23.refs_0_), channel_id=1, source_target_pairs={{0,6},{1,7},{2,4},{3,5},{4,2},{5,3},{6,0},{7,1},{8,12},{9,13},{10,... | collective-permute-start | bytes 196616 | tf_op jit(solution)/shard_map/ppermute | solution.py:364
  8.1 0.2 collective-permute-start.7
  8.3 2.2 %collective-permute-done.3.refs_4_.refs_2_ = bf16[64,512]{1,0:T(8,128)(2,1)S(1)} collective-permute-done((bf16[64,512]{1,0:T(8,128)(2,1)S(1)}, bf16[64,512]{1,0:T(8,128)(2,1)S(1)}, u32[]{:S(2)}, u32[]{:S(2)}) %collective-permute-start.3) | collective-permute-done | bytes 65568 | tf_op jit(solution)/shard_map/ppermute | solution.py:364
  10.5 2.5 %collective-permute-done.1.refs_2_ = bf16[64,512]{1,0:T(8,128)(2,1)S(1)} collective-permute-done((bf16[64,512]{1,0:T(8,128)(2,1)S(1)}, bf16[64,512]{1,0:T(8,128)(2,1)S(1)}, u32[]{:S(2)}, u32[]{:S(2)}) %collective-permute-start.1) | collective-permute-done | bytes 65568 | tf_op jit(solution)/shard_map/ppermute | solution.py:364
  13.0 0.1 collective-permute-done.7.refs_4_
  13.1 0.4 collective-permute-start.8
  13.5 0.7 %collective-permute-done.2.refs_3_ = bf16[64,512]{1,0:T(8,128)(2,1)S(1)} collective-permute-done((bf16[64,512]{1,0:T(8,128)(2,1)S(1)}, bf16[64,512]{1,0:T(8,128)(2,1)S(1)}, u32[]{:S(2)}, u32[]{:S(2)}) %collective-permute-start.2) | collective-permute-done | bytes 65568 | tf_op jit(solution)/shard_map/ppermute | solution.py:323
  14.2 1.2 %shard_map.56 = (bf16[192,256]{1,0:T(8,128)(2,1)S(1)}, bf16[192,256]{1,0:T(8,128)(2,1)S(1)}, bf16[8,16,1024]{2,1,0:T(8,128)(2,1)S(1)}, bf16[8,16,1024]{2,1,0:T(8,128)(2,1)S(1)}) custom-call(bf16[64,512]{1,0:T(8,128)(2,1)S(1)} %get-tuple-element.23.refs_0_, bf16[64,512]{1,0:T(8,128)(2,1)S(1)} %collective-permute-done.refs_1_, ...), custom_call_target="tpu_custom_call" | custom-call | bytes 6291456 | tf_op jit(solution)/shard_map/pallas_call | solution.py:376
  15.4 2.7 %collective-permute-start.5 = (bf16[192,256]{1,0:T(8,128)(2,1)S(1)}, bf16[192,256]{1,0:T(8,128)(2,1)S(1)}, u32[]{:S(2)}, u32[]{:S(2)}) collective-permute-start(bf16[192,256]{1,0:T(8,128)(2,1)S(1)} %get-tuple-element.25), channel_id=1, source_target_pairs={{0,24},{8,16},{16,8},{24,0},{1,25},{9,17},{17,9},{25,1},{2,26},{10... | collective-permute-start | bytes 294920 | tf_op jit(solution)/shard_map/ppermute | solution.py:323
  18.2 0.7 %collective-permute-start.6 = (bf16[192,256]{1,0:T(8,128)(2,1)S(1)}, bf16[192,256]{1,0:T(8,128)(2,1)S(1)}, u32[]{:S(2)}, u32[]{:S(2)}) collective-permute-start(bf16[192,256]{1,0:T(8,128)(2,1)S(1)} %get-tuple-element.26), channel_id=1, source_target_pairs={{0,16},{8,24},{16,0},{24,8},{1,17},{9,25},{17,1},{25,9},{2,18},{10... | collective-permute-start | bytes 294920 | tf_op jit(solution)/shard_map/ppermute | solution.py:323
  18.9 1.2 %shard_map.57 = (bf16[192,256]{1,0:T(8,128)(2,1)S(1)}, bf16[192,256]{1,0:T(8,128)(2,1)S(1)}, bf16[8,16,1024]{2,1,0:T(8,128)(2,1)S(1)}, bf16[8,16,1024]{2,1,0:T(8,128)(2,1)S(1)}) custom-call(bf16[64,512]{1,0:T(8,128)(2,1)S(1)} %get-tuple-element.23.refs_0_, bf16[64,512]{1,0:T(8,128)(2,1)S(1)} %collective-permute-done.refs_1_, ...), custom_call_target="tpu_custom_call" | custom-call | bytes 6291456 | tf_op jit(solution)/shard_map/pallas_call | solution.py:376
  20.0 0.2 collective-permute-start.9
  20.3 1.4 %collective-permute-done.5.refs_0_ = bf16[192,256]{1,0:T(8,128)(2,1)S(1)} collective-permute-done((bf16[192,256]{1,0:T(8,128)(2,1)S(1)}, bf16[192,256]{1,0:T(8,128)(2,1)S(1)}, u32[]{:S(2)}, u32[]{:S(2)}) %collective-permute-start.5) | collective-permute-done | bytes 98336 | tf_op jit(solution)/shard_map/ppermute | solution.py:323
  21.7 2.0 %collective-permute-done.6.refs_1_ = bf16[192,256]{1,0:T(8,128)(2,1)S(1)} collective-permute-done((bf16[192,256]{1,0:T(8,128)(2,1)S(1)}, bf16[192,256]{1,0:T(8,128)(2,1)S(1)}, u32[]{:S(2)}, u32[]{:S(2)}) %collective-permute-start.6) | collective-permute-done | bytes 98336 | tf_op jit(solution)/shard_map/ppermute | solution.py:323
  23.7 1.0 %collective-permute-done.9.refs_2_ = bf16[192,256]{1,0:T(8,128)(2,1)S(1)} collective-permute-done((bf16[192,256]{1,0:T(8,128)(2,1)S(1)}, bf16[192,256]{1,0:T(8,128)(2,1)S(1)}, u32[]{:S(2)}, u32[]{:S(2)}) %collective-permute-start.9) | collective-permute-done | bytes 98336 | tf_op jit(solution)/shard_map/ppermute | solution.py:323
  24.7 0.6 %shard_map.58 = (bf16[128,256]{1,0:T(8,128)(2,1)S(1)}, bf16[128,256]{1,0:T(8,128)(2,1)S(1)}, bf16[128,256]{1,0:T(8,128)(2,1)S(1)}, bf16[128,256]{1,0:T(8,128)(2,1)S(1)}) custom-call(bf16[192,256]{1,0:T(8,128)(2,1)S(1)} %collective-permute-done.5.refs_0_, bf16[192,256]{1,0:T(8,128)(2,1)S(1)} %collective-permute-done.6.refs_1_, ...), custom_call_target="tpu_custom_call" | custom-call | bytes 2097152 | tf_op jit(solution)/shard_map/pallas_call | solution.py:394
  25.3 1.2 %collective-permute-start.10 = (bf16[128,256]{1,0:T(8,128)(2,1)S(1)}, bf16[128,256]{1,0:T(8,128)(2,1)S(1)}, u32[]{:S(2)}, u32[]{:S(2)}) collective-permute-start(bf16[128,256]{1,0:T(8,128)(2,1)S(1)} %get-tuple-element.30), channel_id=1, source_target_pairs={{0,24},{8,16},{16,8},{24,0},{1,25},{9,17},{17,9},{25,1},{2,26},{10... | collective-permute-start | bytes 196616 | tf_op jit(solution)/shard_map/ppermute | solution.py:323
  26.5 1.2 %collective-permute-start.11 = (bf16[128,256]{1,0:T(8,128)(2,1)S(1)}, bf16[128,256]{1,0:T(8,128)(2,1)S(1)}, u32[]{:S(2)}, u32[]{:S(2)}) collective-permute-start(bf16[128,256]{1,0:T(8,128)(2,1)S(1)} %get-tuple-element.31), channel_id=1, source_target_pairs={{0,16},{8,24},{16,0},{24,8},{1,17},{9,25},{17,1},{25,9},{2,18},{10... | collective-permute-start | bytes 196616 | tf_op jit(solution)/shard_map/ppermute | solution.py:323
  27.6 1.2 %collective-permute-start.12 = (bf16[128,256]{1,0:T(8,128)(2,1)S(1)}, bf16[128,256]{1,0:T(8,128)(2,1)S(1)}, u32[]{:S(2)}, u32[]{:S(2)}) collective-permute-start(bf16[128,256]{1,0:T(8,128)(2,1)S(1)} %get-tuple-element.32), channel_id=1, source_target_pairs={{0,8},{8,0},{16,24},{24,16},{1,9},{9,1},{17,25},{25,17},{2,10},{10... | collective-permute-start | bytes 196616 | tf_op jit(solution)/shard_map/ppermute | solution.py:323
  28.9 2.0 %collective-permute-done.10.refs_0_ = bf16[128,256]{1,0:T(8,128)(2,1)S(1)} collective-permute-done((bf16[128,256]{1,0:T(8,128)(2,1)S(1)}, bf16[128,256]{1,0:T(8,128)(2,1)S(1)}, u32[]{:S(2)}, u32[]{:S(2)}) %collective-permute-start.10) | collective-permute-done | bytes 65568 | tf_op jit(solution)/shard_map/ppermute | solution.py:323
  30.9 0.4 collective-permute-done.11.refs_1_
  31.3 0.6 %collective-permute-done.12.refs_2_ = bf16[128,256]{1,0:T(8,128)(2,1)S(1)} collective-permute-done((bf16[128,256]{1,0:T(8,128)(2,1)S(1)}, bf16[128,256]{1,0:T(8,128)(2,1)S(1)}, u32[]{:S(2)}, u32[]{:S(2)}) %collective-permute-start.12) | collective-permute-done | bytes 65568 | tf_op jit(solution)/shard_map/ppermute | solution.py:323
  31.9 1.2 %shard_map.60 = bf16[4,64,512]{2,1,0:T(8,128)(2,1)S(1)} custom-call(bf16[128,256]{1,0:T(8,128)(2,1)S(1)} %collective-permute-done.10.refs_0_, bf16[128,256]{1,0:T(8,128)(2,1)S(1)} %collective-permute-done.11.refs_1_, bf16[128,256]{1,0:T(8,128)(2,1)S(1)} %collective-permute-done.12.refs_2_, bf16[128,256]{1,0:T(8,128)(2,1)S(1)} %get-tuple-element.33.refs_3_, ...), custom_call_target="tpu_custom_call" | custom-call | bytes 6291456 | tf_op jit(solution)/shard_map/pallas_call | solution.py:411
  33.2 1.2 %shard_map.59.keep_ref = f32[4,64,512]{2,1,0:T(8,128)S(1)} custom-call(bf16[128,256]{1,0:T(8,128)(2,1)S(1)} %collective-permute-done.10.refs_0_, bf16[128,256]{1,0:T(8,128)(2,1)S(1)} %collective-permute-done.11.refs_1_, bf16[128,256]{1,0:T(8,128)(2,1)S(1)} %collective-permute-done.12.refs_2_, bf16[128,256]{1,0:T(8,128)(2,1)S(1)} %get-tuple-element.33.refs_3_, ...), custom_call_target="tpu_custom_call" | custom-call | bytes 6291456 | tf_op jit(solution)/shard_map/pallas_call | solution.py:411
  34.3 0.4 collective-permute-done.13.came_ref
  34.7 2.5 %collective-permute-start.14 = (bf16[64,512]{1,0:T(8,128)(2,1)S(1)}, bf16[64,512]{1,0:T(8,128)(2,1)S(1)}, u32[]{:S(2)}, u32[]{:S(2)}) collective-permute-start(bf16[64,512]{1,0:T(8,128)(2,1)S(1)} %get-tuple-element.34), channel_id=1, source_target_pairs={{0,6},{1,7},{2,4},{3,5},{4,2},{5,3},{6,0},{7,1},{8,14},{9,15},{10,... | collective-permute-start | bytes 196616 | tf_op jit(solution)/shard_map/ppermute | solution.py:323
  37.3 1.9 %collective-permute-start.16 = (bf16[64,512]{1,0:T(8,128)(2,1)S(1)}, bf16[64,512]{1,0:T(8,128)(2,1)S(1)}, u32[]{:S(2)}, u32[]{:S(2)}) collective-permute-start(bf16[64,512]{1,0:T(8,128)(2,1)S(1)} %get-tuple-element.36), channel_id=1, source_target_pairs={{0,2},{1,3},{2,0},{3,1},{4,6},{5,7},{6,4},{7,5},{8,10},{9,11},{10,... | collective-permute-start | bytes 196616 | tf_op jit(solution)/shard_map/ppermute | solution.py:323
  39.2 2.3 %collective-permute-done.14.refs_0_ = bf16[64,512]{1,0:T(8,128)(2,1)S(1)} collective-permute-done((bf16[64,512]{1,0:T(8,128)(2,1)S(1)}, bf16[64,512]{1,0:T(8,128)(2,1)S(1)}, u32[]{:S(2)}, u32[]{:S(2)}) %collective-permute-start.14) | collective-permute-done | bytes 65568 | tf_op jit(solution)/shard_map/ppermute | solution.py:323
  41.5 2.2 %collective-permute-done.15.refs_1_ = bf16[64,512]{1,0:T(8,128)(2,1)S(1)} collective-permute-done((bf16[64,512]{1,0:T(8,128)(2,1)S(1)}, bf16[64,512]{1,0:T(8,128)(2,1)S(1)}, u32[]{:S(2)}, u32[]{:S(2)}) %collective-permute-start.15) | collective-permute-done | bytes 65568 | tf_op jit(solution)/shard_map/ppermute | solution.py:323
  43.7 1.8 %shard_map.62 = bf16[64,4,16,128]{3,2,1,0:T(8,128)(2,1)} custom-call(bf16[64,512]{1,0:T(8,128)(2,1)S(1)} %collective-permute-done.14.refs_0_, bf16[64,512]{1,0:T(8,128)(2,1)S(1)} %collective-permute-done.15.refs_1_, bf16[64,512]{1,0:T(8,128)(2,1)S(1)} %collective-permute-done.16.refs_2_, f32[64,512]{1,0:T(8,128)S(1)} %get-tuple-element.37.refs_3_, ...), custom_call_target="tpu_custom_call" | custom-call | bytes 4194304 | tf_op jit(solution)/shard_map/pallas_call | solution.py:430
  (18 shorter events, 0.2 us)
Async XLA Ops:
  0.0 14.2 %copy-start.1 = (bf16[64,32]{1,0:T(8,128)(2,1)S(1)}, bf16[64,32]{1,0:T(8,128)(2,1)}, u32[]{:S(2)}) copy-start(bf16[64,32]{1,0:T(8,128)(2,1)} %constant.6.clone.refs_7_) | copy-start | bytes 12292
  0.0 14.2 %copy-start = (bf16[8,32,256]{2,1,0:T(8,128)(2,1)S(1)}, bf16[8,32,256]{2,1,0:T(8,128)(2,1)}, u32[]{:S(2)}) copy-start(bf16[8,32,256]{2,1,0:T(8,128)(2,1)} %refs_8_.3) | copy-start | bytes 393220
  2.6 7.9 %collective-permute-start.3 = (bf16[64,512]{1,0:T(8,128)(2,1)S(1)}, bf16[64,512]{1,0:T(8,128)(2,1)S(1)}, u32[]{:S(2)}, u32[]{:S(2)}) collective-permute-start(bf16[64,512]{1,0:T(8,128)(2,1)S(1)} %get-tuple-element.23.refs_0_), channel_id=1, source_target_pairs={{0,4},{1,5},{2,6},{3,7},{4,0},{5,1},{6,2},{7,3},{8,14},{9,15},{10,... | collective-permute-start | bytes 196616 | tf_op jit(solution)/shard_map/ppermute | solution.py:364
  6.7 6.2 %collective-permute-start.1 = (bf16[64,512]{1,0:T(8,128)(2,1)S(1)}, bf16[64,512]{1,0:T(8,128)(2,1)S(1)}, u32[]{:S(2)}, u32[]{:S(2)}) collective-permute-start(bf16[64,512]{1,0:T(8,128)(2,1)S(1)} %get-tuple-element.23.refs_0_), channel_id=1, source_target_pairs={{0,6},{1,7},{2,4},{3,5},{4,2},{5,3},{6,0},{7,1},{8,12},{9,13},{10,... | collective-permute-start | bytes 196616 | tf_op jit(solution)/shard_map/ppermute | solution.py:364
  8.1 5.0 %collective-permute-start.7 = (bf16[64,512]{1,0:T(8,128)(2,1)S(1)}, bf16[64,512]{1,0:T(8,128)(2,1)S(1)}, u32[]{:S(2)}, u32[]{:S(2)}) collective-permute-start(bf16[64,512]{1,0:T(8,128)(2,1)S(1)} %get-tuple-element.23.refs_0_), channel_id=1, source_target_pairs={{0,2},{1,3},{2,0},{3,1},{4,6},{5,7},{6,4},{7,5},{8,10},{9,11},{10,... | collective-permute-start | bytes 196616 | tf_op jit(solution)/shard_map/ppermute | solution.py:364
  8.3 5.2 %collective-permute-start = (bf16[64,512]{1,0:T(8,128)(2,1)S(1)}, bf16[64,512]{1,0:T(8,128)(2,1)S(1)}, u32[]{:S(2)}, u32[]{:S(2)}) collective-permute-start(bf16[64,512]{1,0:T(8,128)(2,1)S(1)} %get-tuple-element.23.refs_0_), channel_id=1, source_target_pairs={{0,1},{1,0},{2,3},{3,2},{4,5},{5,4},{6,7},{7,6},{8,9},{9,8},{10,11... | collective-permute-start | bytes 196616 | tf_op jit(solution)/shard_map/ppermute | solution.py:323
  10.5 3.0 %collective-permute-start.4 = (bf16[64,512]{1,0:T(8,128)(2,1)S(1)}, bf16[64,512]{1,0:T(8,128)(2,1)S(1)}, u32[]{:S(2)}, u32[]{:S(2)}) collective-permute-start(bf16[64,512]{1,0:T(8,128)(2,1)S(1)} %collective-permute-done.3.refs_4_.refs_2_), channel_id=1, source_target_pairs={{0,1},{1,0},{2,3},{3,2},{4,5},{5,4},{6,7},{7,6},{8,9},{9,8},{10,11... | collective-permute-start | bytes 196616 | tf_op jit(solution)/shard_map/ppermute | solution.py:323
  13.0 1.3 %collective-permute-start.2 = (bf16[64,512]{1,0:T(8,128)(2,1)S(1)}, bf16[64,512]{1,0:T(8,128)(2,1)S(1)}, u32[]{:S(2)}, u32[]{:S(2)}) collective-permute-start(bf16[64,512]{1,0:T(8,128)(2,1)S(1)} %collective-permute-done.1.refs_2_), channel_id=1, source_target_pairs={{0,1},{1,0},{2,3},{3,2},{4,5},{5,4},{6,7},{7,6},{8,9},{9,8},{10,11... | collective-permute-start | bytes 196616 | tf_op jit(solution)/shard_map/ppermute | solution.py:323
  13.1 5.8 %collective-permute-start.8 = (bf16[64,512]{1,0:T(8,128)(2,1)S(1)}, bf16[64,512]{1,0:T(8,128)(2,1)S(1)}, u32[]{:S(2)}, u32[]{:S(2)}) collective-permute-start(bf16[64,512]{1,0:T(8,128)(2,1)S(1)} %collective-permute-done.7.refs_4_), channel_id=1, source_target_pairs={{0,1},{1,0},{2,3},{3,2},{4,5},{5,4},{6,7},{7,6},{8,9},{9,8},{10,11... | collective-permute-start | bytes 196616 | tf_op jit(solution)/shard_map/ppermute | solution.py:323
  14.2 10.5 %copy-start.2 = (bf16[64,128]{1,0:T(8,128)(2,1)S(1)}, bf16[64,128]{1,0:T(8,128)(2,1)}, u32[]{:S(2)}) copy-start(bf16[64,128]{1,0:T(8,128)(2,1)} %constant.8.clone.refs_5_) | copy-start | bytes 49156
  14.2 10.5 %copy-start.3 = (bf16[64,128]{1,0:T(8,128)(2,1)S(1)}, bf16[64,128]{1,0:T(8,128)(2,1)}, u32[]{:S(2)}) copy-start(bf16[64,128]{1,0:T(8,128)(2,1)} %constant.7.clone.refs_4_) | copy-start | bytes 49156
  15.4 6.2 %collective-permute-start.5 = (bf16[192,256]{1,0:T(8,128)(2,1)S(1)}, bf16[192,256]{1,0:T(8,128)(2,1)S(1)}, u32[]{:S(2)}, u32[]{:S(2)}) collective-permute-start(bf16[192,256]{1,0:T(8,128)(2,1)S(1)} %get-tuple-element.25), channel_id=1, source_target_pairs={{0,24},{8,16},{16,8},{24,0},{1,25},{9,17},{17,9},{25,1},{2,26},{10... | collective-permute-start | bytes 294920 | tf_op jit(solution)/shard_map/ppermute | solution.py:323
  18.2 5.6 %collective-permute-start.6 = (bf16[192,256]{1,0:T(8,128)(2,1)S(1)}, bf16[192,256]{1,0:T(8,128)(2,1)S(1)}, u32[]{:S(2)}, u32[]{:S(2)}) collective-permute-start(bf16[192,256]{1,0:T(8,128)(2,1)S(1)} %get-tuple-element.26), channel_id=1, source_target_pairs={{0,16},{8,24},{16,0},{24,8},{1,17},{9,25},{17,1},{25,9},{2,18},{10... | collective-permute-start | bytes 294920 | tf_op jit(solution)/shard_map/ppermute | solution.py:323
  20.0 4.7 %collective-permute-start.9 = (bf16[192,256]{1,0:T(8,128)(2,1)S(1)}, bf16[192,256]{1,0:T(8,128)(2,1)S(1)}, u32[]{:S(2)}, u32[]{:S(2)}) collective-permute-start(bf16[192,256]{1,0:T(8,128)(2,1)S(1)} %get-tuple-element.28), channel_id=1, source_target_pairs={{0,8},{8,0},{16,24},{24,16},{1,9},{9,1},{17,25},{25,17},{2,10},{10... | collective-permute-start | bytes 294920 | tf_op jit(solution)/shard_map/ppermute | solution.py:323
  25.3 5.6 %collective-permute-start.10 = (bf16[128,256]{1,0:T(8,128)(2,1)S(1)}, bf16[128,256]{1,0:T(8,128)(2,1)S(1)}, u32[]{:S(2)}, u32[]{:S(2)}) collective-permute-start(bf16[128,256]{1,0:T(8,128)(2,1)S(1)} %get-tuple-element.30), channel_id=1, source_target_pairs={{0,24},{8,16},{16,8},{24,0},{1,25},{9,17},{17,9},{25,1},{2,26},{10... | collective-permute-start | bytes 196616 | tf_op jit(solution)/shard_map/ppermute | solution.py:323
  26.5 4.8 %collective-permute-start.11 = (bf16[128,256]{1,0:T(8,128)(2,1)S(1)}, bf16[128,256]{1,0:T(8,128)(2,1)S(1)}, u32[]{:S(2)}, u32[]{:S(2)}) collective-permute-start(bf16[128,256]{1,0:T(8,128)(2,1)S(1)} %get-tuple-element.31), channel_id=1, source_target_pairs={{0,16},{8,24},{16,0},{24,8},{1,17},{9,25},{17,1},{25,9},{2,18},{10... | collective-permute-start | bytes 196616 | tf_op jit(solution)/shard_map/ppermute | solution.py:323
  27.6 4.3 %collective-permute-start.12 = (bf16[128,256]{1,0:T(8,128)(2,1)S(1)}, bf16[128,256]{1,0:T(8,128)(2,1)S(1)}, u32[]{:S(2)}, u32[]{:S(2)}) collective-permute-start(bf16[128,256]{1,0:T(8,128)(2,1)S(1)} %get-tuple-element.32), channel_id=1, source_target_pairs={{0,8},{8,0},{16,24},{24,16},{1,9},{9,1},{17,25},{25,17},{2,10},{10... | collective-permute-start | bytes 196616 | tf_op jit(solution)/shard_map/ppermute | solution.py:323
  33.1 1.6 %collective-permute-start.13 = (bf16[4,64,512]{2,1,0:T(8,128)(2,1)S(1)}, bf16[4,64,512]{2,1,0:T(8,128)(2,1)S(1)}, u32[]{:S(2)}, u32[]{:S(2)}) collective-permute-start(bf16[4,64,512]{2,1,0:T(8,128)(2,1)S(1)} %shard_map.60), channel_id=1, source_target_pairs={{0,1},{1,0},{2,3},{3,2},{4,5},{5,4},{6,7},{7,6},{8,9},{9,8},{10,11... | collective-permute-start | bytes 786440 | tf_op jit(solution)/shard_map/ppermute | solution.py:323
  34.7 6.8 %collective-permute-start.14 = (bf16[64,512]{1,0:T(8,128)(2,1)S(1)}, bf16[64,512]{1,0:T(8,128)(2,1)S(1)}, u32[]{:S(2)}, u32[]{:S(2)}) collective-permute-start(bf16[64,512]{1,0:T(8,128)(2,1)S(1)} %get-tuple-element.34), channel_id=1, source_target_pairs={{0,6},{1,7},{2,4},{3,5},{4,2},{5,3},{6,0},{7,1},{8,14},{9,15},{10,... | collective-permute-start | bytes 196616 | tf_op jit(solution)/shard_map/ppermute | solution.py:323
  37.3 6.4 %collective-permute-start.15 = (bf16[64,512]{1,0:T(8,128)(2,1)S(1)}, bf16[64,512]{1,0:T(8,128)(2,1)S(1)}, u32[]{:S(2)}, u32[]{:S(2)}) collective-permute-start(bf16[64,512]{1,0:T(8,128)(2,1)S(1)} %get-tuple-element.35), channel_id=1, source_target_pairs={{0,4},{1,5},{2,6},{3,7},{4,0},{5,1},{6,2},{7,3},{8,12},{9,13},{10,... | collective-permute-start | bytes 196616 | tf_op jit(solution)/shard_map/ppermute | solution.py:323
  37.3 6.4 %collective-permute-start.16 = (bf16[64,512]{1,0:T(8,128)(2,1)S(1)}, bf16[64,512]{1,0:T(8,128)(2,1)S(1)}, u32[]{:S(2)}, u32[]{:S(2)}) collective-permute-start(bf16[64,512]{1,0:T(8,128)(2,1)S(1)} %get-tuple-element.36), channel_id=1, source_target_pairs={{0,2},{1,3},{2,0},{3,1},{4,6},{5,7},{6,4},{7,5},{8,10},{9,11},{10,... | collective-permute-start | bytes 196616 | tf_op jit(solution)/shard_map/ppermute | solution.py:323

commit v10 on v9

--- a/solution.py
+++ b/solution.py
@@ -112,7 +112,7 @@
 
 
 def orders(shares):
-    return [[a ^ j for j in reversed(range(shares)) if a ^ j] for a in range(shares)]
+    return [list(reversed(range(1, shares)))] * shares
 
 
 def pick(table, index):
@@ -128,8 +128,7 @@
 
 
 def pieces_of(shares):
-    half = shares // 2
-    return [list(reversed(range(half, shares))), list(reversed(range(half)))]
+    return [list(reversed(range(shares)))]
 
 
 def plane_of(shares):

time: 45.6 us -> 46.7 us (1.024)
  waiting for transfers between devices: 17.8 us -> 19.8 us
  Pallas kernels: 9.72 us -> 8.8 us
    ppermute x14, waiting for transfers between devices: 13.1 us -> 14.2 us  [swap(): return lax.ppermute(value, axis, [(i, i ^ mask) for i in range(size)])]
    pallas_call x2 -> x1, Pallas kernels: 2.38 us -> 1.46 us  [body(): call(functools.partial(tile_kernel, targets, shares, per_share, per_block...]
    ppermute x3, waiting for transfers between devices: 4.73 us -> 5.56 us  [body(): block = lax.ppermute(edge, ('ka', 'pts'), pairs)]
  transfers between devices with their start and end apart: 17 -> 17, of which waited for: 13 -> 12; matrix products, arithmetic and copies ran while one was open for 0% -> 0% of each run, Pallas kernels for 8% -> 2%
where the time goes in v10:
time: 46.7 us; the launch traced here: 46.5 us
  waiting for transfers between devices  19.8 us (42%)
  starting transfers between devices  17.9 us (38%)
  Pallas kernels  8.8 us (19%)
    ppermute x14, waiting for transfers between devices, swap(): return lax.ppermute(value, axis, [(i, i ^ mask) for i in range(size)])  14.2 us
    ppermute x14, starting transfers between devices, swap(): return lax.ppermute(value, axis, [(i, i ^ mask) for i in range(size)])  12.1 us
    ppermute x3, starting transfers between devices, body(): block = lax.ppermute(edge, ('ka', 'pts'), pairs)  5.71 us
    ppermute x3, waiting for transfers between devices, body(): block = lax.ppermute(edge, ('ka', 'pts'), pairs)  5.56 us
    pallas_call x1, Pallas kernels, body(): call(functools.partial(edge_kernel, per_block), [shape((local_k * 2 * per...  2.63 us
    pallas_call x2, Pallas kernels, body(): call(functools.partial(weight_kernel, shares, flip, out_rows), shape((chu...  2.33 us
    pallas_call x1, Pallas kernels, body(): call(functools.partial(exchange_kernel, chunks, shares, 1.0 / math.sqrt(p...  1.75 us
    pallas_call x1, Pallas kernels, body(): call(functools.partial(tile_kernel, targets, shares, per_share, per_block...  1.46 us
  transfers between devices with their start and end apart: 17, of which 12 were waited for; matrix products, arithmetic and copies ran while one was open for 0% of the time, Pallas kernels for 2%

profile of v10, /device:TPU:0, one launch (start us, length us, event | category | flops | bytes accessed | tf_op | source)
XLA Modules:
  0.0 46.5 jit_solution(7406629957291964138)
XLA Ops:
  0.0 2.6 %shard_map.55 = (bf16[64,512]{1,0:T(8,128)(2,1)S(1)}, bf16[8,2,512,256]{3,2,1,0:T(8,128)(2,1)S(1)}) custom-call(bf16[8,2,512,256]{3,2,1,0:T(8,128)(2,1)} %orb_hbm.1), custom_call_target="tpu_custom_call" | custom-call | bytes 8388608 | tf_op jit(solution)/shard_map/pallas_call | solution.py:341
  2.6 3.1 %collective-permute-start.5 = (bf16[64,512]{1,0:T(8,128)(2,1)S(1)}, bf16[64,512]{1,0:T(8,128)(2,1)S(1)}, u32[]{:S(2)}, u32[]{:S(2)}) collective-permute-start(bf16[64,512]{1,0:T(8,128)(2,1)S(1)} %get-tuple-element.23.refs_0_), channel_id=1, source_target_pairs={{0,2},{1,3},{2,0},{3,1},{4,6},{5,7},{6,4},{7,5},{8,10},{9,11},{10,... | collective-permute-start | bytes 196616 | tf_op jit(solution)/shard_map/ppermute | solution.py:363
  5.8 2.6 %collective-permute-start.3 = (bf16[64,512]{1,0:T(8,128)(2,1)S(1)}, bf16[64,512]{1,0:T(8,128)(2,1)S(1)}, u32[]{:S(2)}, u32[]{:S(2)}) collective-permute-start(bf16[64,512]{1,0:T(8,128)(2,1)S(1)} %get-tuple-element.23.refs_0_), channel_id=1, source_target_pairs={{0,4},{1,5},{2,6},{3,7},{4,0},{5,1},{6,2},{7,3},{8,12},{9,13},{10,... | collective-permute-start | bytes 196616 | tf_op jit(solution)/shard_map/ppermute | solution.py:363
  8.4 0.0 collective-permute-start.1
  8.4 0.0 collective-permute-start
  8.4 0.5 %collective-permute-start.6 = (bf16[64,512]{1,0:T(8,128)(2,1)S(1)}, bf16[64,512]{1,0:T(8,128)(2,1)S(1)}, u32[]{:S(2)}, u32[]{:S(2)}) collective-permute-start(bf16[64,512]{1,0:T(8,128)(2,1)S(1)} %collective-permute-done.5.refs_6_), channel_id=1, source_target_pairs={{0,1},{1,0},{2,3},{3,2},{4,5},{5,4},{6,7},{7,6},{8,9},{9,8},{10,11... | collective-permute-start | bytes 196616 | tf_op jit(solution)/shard_map/ppermute | solution.py:322
  8.9 4.2 %collective-permute-done.3.refs_4_ = bf16[64,512]{1,0:T(8,128)(2,1)S(1)} collective-permute-done((bf16[64,512]{1,0:T(8,128)(2,1)S(1)}, bf16[64,512]{1,0:T(8,128)(2,1)S(1)}, u32[]{:S(2)}, u32[]{:S(2)}) %collective-permute-start.3) | collective-permute-done | bytes 65568 | tf_op jit(solution)/shard_map/ppermute | solution.py:363
  13.0 1.4 %collective-permute-done.1.refs_2_ = bf16[64,512]{1,0:T(8,128)(2,1)S(1)} collective-permute-done((bf16[64,512]{1,0:T(8,128)(2,1)S(1)}, bf16[64,512]{1,0:T(8,128)(2,1)S(1)}, u32[]{:S(2)}, u32[]{:S(2)}) %collective-permute-start.1) | collective-permute-done | bytes 65568 | tf_op jit(solution)/shard_map/ppermute | solution.py:363
  14.5 1.2 %collective-permute-done.2.refs_3_ = bf16[64,512]{1,0:T(8,128)(2,1)S(1)} collective-permute-done((bf16[64,512]{1,0:T(8,128)(2,1)S(1)}, bf16[64,512]{1,0:T(8,128)(2,1)S(1)}, u32[]{:S(2)}, u32[]{:S(2)}) %collective-permute-start.2) | collective-permute-done | bytes 65568 | tf_op jit(solution)/shard_map/ppermute | solution.py:322
  15.7 1.5 %shard_map.56 = (bf16[192,256]{1,0:T(8,128)(2,1)S(1)}, bf16[192,256]{1,0:T(8,128)(2,1)S(1)}, bf16[192,256]{1,0:T(8,128)(2,1)S(1)}, bf16[192,256]{1,0:T(8,128)(2,...) custom-call(bf16[64,512]{1,0:T(8,128)(2,1)S(1)} %get-tuple-element.2, ...), custom_call_target="tpu_custom_call" | custom-call | bytes 6291456 | tf_op jit(solution)/shard_map/pallas_call | solution.py:375
  17.2 2.5 %collective-permute-start.7 = (bf16[192,256]{1,0:T(8,128)(2,1)S(1)}, bf16[192,256]{1,0:T(8,128)(2,1)S(1)}, u32[]{:S(2)}, u32[]{:S(2)}) collective-permute-start(bf16[192,256]{1,0:T(8,128)(2,1)S(1)} %get-tuple-element.25), channel_id=1, source_target_pairs={{0,24},{8,16},{16,8},{24,0},{1,25},{9,17},{17,9},{25,1},{2,26},{10... | collective-permute-start | bytes 294920 | tf_op jit(solution)/shard_map/ppermute | solution.py:322
  19.7 0.5 %collective-permute-start.8 = (bf16[192,256]{1,0:T(8,128)(2,1)S(1)}, bf16[192,256]{1,0:T(8,128)(2,1)S(1)}, u32[]{:S(2)}, u32[]{:S(2)}) collective-permute-start(bf16[192,256]{1,0:T(8,128)(2,1)S(1)} %get-tuple-element.26), channel_id=1, source_target_pairs={{0,16},{8,24},{16,0},{24,8},{1,17},{9,25},{17,1},{25,9},{2,18},{10... | collective-permute-start | bytes 294920 | tf_op jit(solution)/shard_map/ppermute | solution.py:322
  20.2 0.5 %collective-permute-start.9 = (bf16[192,256]{1,0:T(8,128)(2,1)S(1)}, bf16[192,256]{1,0:T(8,128)(2,1)S(1)}, u32[]{:S(2)}, u32[]{:S(2)}) collective-permute-start(bf16[192,256]{1,0:T(8,128)(2,1)S(1)} %get-tuple-element.27), channel_id=1, source_target_pairs={{0,8},{8,0},{16,24},{24,16},{1,9},{9,1},{17,25},{25,17},{2,10},{10... | collective-permute-start | bytes 294920 | tf_op jit(solution)/shard_map/ppermute | solution.py:322
  20.7 2.4 %collective-permute-done.7.refs_0_ = bf16[192,256]{1,0:T(8,128)(2,1)S(1)} collective-permute-done((bf16[192,256]{1,0:T(8,128)(2,1)S(1)}, bf16[192,256]{1,0:T(8,128)(2,1)S(1)}, u32[]{:S(2)}, u32[]{:S(2)}) %collective-permute-start.7) | collective-permute-done | bytes 98336 | tf_op jit(solution)/shard_map/ppermute | solution.py:322
  23.1 2.0 %collective-permute-done.8.refs_1_ = bf16[192,256]{1,0:T(8,128)(2,1)S(1)} collective-permute-done((bf16[192,256]{1,0:T(8,128)(2,1)S(1)}, bf16[192,256]{1,0:T(8,128)(2,1)S(1)}, u32[]{:S(2)}, u32[]{:S(2)}) %collective-permute-start.8) | collective-permute-done | bytes 98336 | tf_op jit(solution)/shard_map/ppermute | solution.py:322
  25.1 0.1 collective-permute-done.9.refs_2_
  25.2 0.6 %shard_map.57 = (bf16[128,256]{1,0:T(8,128)(2,1)S(1)}, bf16[128,256]{1,0:T(8,128)(2,1)S(1)}, bf16[128,256]{1,0:T(8,128)(2,1)S(1)}, bf16[128,256]{1,0:T(8,128)(2,1)S(1)}) custom-call(bf16[192,256]{1,0:T(8,128)(2,1)S(1)} %collective-permute-done.7.refs_0_, bf16[192,256]{1,0:T(8,128)(2,1)S(1)} %collective-permute-done.8.refs_1_, ...), custom_call_target="tpu_custom_call" | custom-call | bytes 2097152 | tf_op jit(solution)/shard_map/pallas_call | solution.py:393
  25.8 1.8 %collective-permute-start.10 = (bf16[128,256]{1,0:T(8,128)(2,1)S(1)}, bf16[128,256]{1,0:T(8,128)(2,1)S(1)}, u32[]{:S(2)}, u32[]{:S(2)}) collective-permute-start(bf16[128,256]{1,0:T(8,128)(2,1)S(1)} %get-tuple-element.29), channel_id=1, source_target_pairs={{0,24},{8,16},{16,8},{24,0},{1,25},{9,17},{17,9},{25,1},{2,26},{10... | collective-permute-start | bytes 196616 | tf_op jit(solution)/shard_map/ppermute | solution.py:322
  27.5 1.3 %collective-permute-start.11 = (bf16[128,256]{1,0:T(8,128)(2,1)S(1)}, bf16[128,256]{1,0:T(8,128)(2,1)S(1)}, u32[]{:S(2)}, u32[]{:S(2)}) collective-permute-start(bf16[128,256]{1,0:T(8,128)(2,1)S(1)} %get-tuple-element.30), channel_id=1, source_target_pairs={{0,16},{8,24},{16,0},{24,8},{1,17},{9,25},{17,1},{25,9},{2,18},{10... | collective-permute-start | bytes 196616 | tf_op jit(solution)/shard_map/ppermute | solution.py:322
  28.8 0.5 %collective-permute-start.12 = (bf16[128,256]{1,0:T(8,128)(2,1)S(1)}, bf16[128,256]{1,0:T(8,128)(2,1)S(1)}, u32[]{:S(2)}, u32[]{:S(2)}) collective-permute-start(bf16[128,256]{1,0:T(8,128)(2,1)S(1)} %get-tuple-element.31), channel_id=1, source_target_pairs={{0,8},{8,0},{16,24},{24,16},{1,9},{9,1},{17,25},{25,17},{2,10},{10... | collective-permute-start | bytes 196616 | tf_op jit(solution)/shard_map/ppermute | solution.py:322
  29.3 2.1 %collective-permute-done.10.refs_0_ = bf16[128,256]{1,0:T(8,128)(2,1)S(1)} collective-permute-done((bf16[128,256]{1,0:T(8,128)(2,1)S(1)}, bf16[128,256]{1,0:T(8,128)(2,1)S(1)}, u32[]{:S(2)}, u32[]{:S(2)}) %collective-permute-start.10) | collective-permute-done | bytes 65568 | tf_op jit(solution)/shard_map/ppermute | solution.py:322
  31.4 0.5 %collective-permute-done.11.refs_1_ = bf16[128,256]{1,0:T(8,128)(2,1)S(1)} collective-permute-done((bf16[128,256]{1,0:T(8,128)(2,1)S(1)}, bf16[128,256]{1,0:T(8,128)(2,1)S(1)}, u32[]{:S(2)}, u32[]{:S(2)}) %collective-permute-start.11) | collective-permute-done | bytes 65568 | tf_op jit(solution)/shard_map/ppermute | solution.py:322
  32.0 1.1 %collective-permute-done.12.refs_2_ = bf16[128,256]{1,0:T(8,128)(2,1)S(1)} collective-permute-done((bf16[128,256]{1,0:T(8,128)(2,1)S(1)}, bf16[128,256]{1,0:T(8,128)(2,1)S(1)}, u32[]{:S(2)}, u32[]{:S(2)}) %collective-permute-start.12) | collective-permute-done | bytes 65568 | tf_op jit(solution)/shard_map/ppermute | solution.py:322
  33.1 1.2 %shard_map.59 = bf16[4,64,512]{2,1,0:T(8,128)(2,1)S(1)} custom-call(bf16[128,256]{1,0:T(8,128)(2,1)S(1)} %collective-permute-done.10.refs_0_, bf16[128,256]{1,0:T(8,128)(2,1)S(1)} %collective-permute-done.11.refs_1_, bf16[128,256]{1,0:T(8,128)(2,1)S(1)} %collective-permute-done.12.refs_2_, bf16[128,256]{1,0:T(8,128)(2,1)S(1)} %get-tuple-element.32.refs_3_, ...), custom_call_target="tpu_custom_call" | custom-call | bytes 6291456 | tf_op jit(solution)/shard_map/pallas_call | solution.py:410
  34.3 0.1 collective-permute-start.13
  34.4 1.2 %shard_map.58.keep_ref = f32[4,64,512]{2,1,0:T(8,128)S(1)} custom-call(bf16[128,256]{1,0:T(8,128)(2,1)S(1)} %collective-permute-done.10.refs_0_, bf16[128,256]{1,0:T(8,128)(2,1)S(1)} %collective-permute-done.11.refs_1_, bf16[128,256]{1,0:T(8,128)(2,1)S(1)} %collective-permute-done.12.refs_2_, bf16[128,256]{1,0:T(8,128)(2,1)S(1)} %get-tuple-element.32.refs_3_, ...), custom_call_target="tpu_custom_call" | custom-call | bytes 6291456 | tf_op jit(solution)/shard_map/pallas_call | solution.py:410
  35.5 0.4 collective-permute-done.13.came_ref
  35.9 2.2 %collective-permute-start.14 = (bf16[64,512]{1,0:T(8,128)(2,1)S(1)}, bf16[64,512]{1,0:T(8,128)(2,1)S(1)}, u32[]{:S(2)}, u32[]{:S(2)}) collective-permute-start(bf16[64,512]{1,0:T(8,128)(2,1)S(1)} %get-tuple-element.33), channel_id=1, source_target_pairs={{0,6},{1,7},{2,4},{3,5},{4,2},{5,3},{6,0},{7,1},{8,14},{9,15},{10,... | collective-permute-start | bytes 196616 | tf_op jit(solution)/shard_map/ppermute | solution.py:322
  38.1 2.3 %collective-permute-start.16 = (bf16[64,512]{1,0:T(8,128)(2,1)S(1)}, bf16[64,512]{1,0:T(8,128)(2,1)S(1)}, u32[]{:S(2)}, u32[]{:S(2)}) collective-permute-start(bf16[64,512]{1,0:T(8,128)(2,1)S(1)} %get-tuple-element.35), channel_id=1, source_target_pairs={{0,2},{1,3},{2,0},{3,1},{4,6},{5,7},{6,4},{7,5},{8,10},{9,11},{10,... | collective-permute-start | bytes 196616 | tf_op jit(solution)/shard_map/ppermute | solution.py:322
  40.4 2.4 %collective-permute-done.14.refs_0_ = bf16[64,512]{1,0:T(8,128)(2,1)S(1)} collective-permute-done((bf16[64,512]{1,0:T(8,128)(2,1)S(1)}, bf16[64,512]{1,0:T(8,128)(2,1)S(1)}, u32[]{:S(2)}, u32[]{:S(2)}) %collective-permute-start.14) | collective-permute-done | bytes 65568 | tf_op jit(solution)/shard_map/ppermute | solution.py:322
  42.8 2.0 %collective-permute-done.15.refs_1_ = bf16[64,512]{1,0:T(8,128)(2,1)S(1)} collective-permute-done((bf16[64,512]{1,0:T(8,128)(2,1)S(1)}, bf16[64,512]{1,0:T(8,128)(2,1)S(1)}, u32[]{:S(2)}, u32[]{:S(2)}) %collective-permute-start.15) | collective-permute-done | bytes 65568 | tf_op jit(solution)/shard_map/ppermute | solution.py:322
  44.8 1.8 %shard_map.61 = bf16[64,4,16,128]{3,2,1,0:T(8,128)(2,1)} custom-call(bf16[64,512]{1,0:T(8,128)(2,1)S(1)} %collective-permute-done.14.refs_0_, bf16[64,512]{1,0:T(8,128)(2,1)S(1)} %collective-permute-done.15.refs_1_, bf16[64,512]{1,0:T(8,128)(2,1)S(1)} %collective-permute-done.16.refs_2_, f32[64,512]{1,0:T(8,128)S(1)} %get-tuple-element.36.refs_3_, ...), custom_call_target="tpu_custom_call" | custom-call | bytes 4194304 | tf_op jit(solution)/shard_map/pallas_call | solution.py:429
  (17 shorter events, 0.1 us)
Async XLA Ops:
  0.0 15.7 %copy-start.1 = (bf16[64,32]{1,0:T(8,128)(2,1)S(1)}, bf16[64,32]{1,0:T(8,128)(2,1)}, u32[]{:S(2)}) copy-start(bf16[64,32]{1,0:T(8,128)(2,1)} %constant.6.clone.refs_9_) | copy-start | bytes 12292
  0.0 25.2 %copy-start.2 = (bf16[64,128]{1,0:T(8,128)(2,1)S(1)}, bf16[64,128]{1,0:T(8,128)(2,1)}, u32[]{:S(2)}) copy-start(bf16[64,128]{1,0:T(8,128)(2,1)} %constant.8.clone.refs_5_) | copy-start | bytes 49156
  0.0 25.2 %copy-start.3 = (bf16[64,128]{1,0:T(8,128)(2,1)S(1)}, bf16[64,128]{1,0:T(8,128)(2,1)}, u32[]{:S(2)}) copy-start(bf16[64,128]{1,0:T(8,128)(2,1)} %constant.7.clone.refs_4_) | copy-start | bytes 49156
  0.0 15.7 %copy-start = (bf16[8,32,256]{2,1,0:T(8,128)(2,1)S(1)}, bf16[8,32,256]{2,1,0:T(8,128)(2,1)}, u32[]{:S(2)}) copy-start(bf16[8,32,256]{2,1,0:T(8,128)(2,1)} %refs_10_.1) | copy-start | bytes 393220
  2.6 5.7 %collective-permute-start.5 = (bf16[64,512]{1,0:T(8,128)(2,1)S(1)}, bf16[64,512]{1,0:T(8,128)(2,1)S(1)}, u32[]{:S(2)}, u32[]{:S(2)}) collective-permute-start(bf16[64,512]{1,0:T(8,128)(2,1)S(1)} %get-tuple-element.23.refs_0_), channel_id=1, source_target_pairs={{0,2},{1,3},{2,0},{3,1},{4,6},{5,7},{6,4},{7,5},{8,10},{9,11},{10,... | collective-permute-start | bytes 196616 | tf_op jit(solution)/shard_map/ppermute | solution.py:363
  5.8 7.3 %collective-permute-start.3 = (bf16[64,512]{1,0:T(8,128)(2,1)S(1)}, bf16[64,512]{1,0:T(8,128)(2,1)S(1)}, u32[]{:S(2)}, u32[]{:S(2)}) collective-permute-start(bf16[64,512]{1,0:T(8,128)(2,1)S(1)} %get-tuple-element.23.refs_0_), channel_id=1, source_target_pairs={{0,4},{1,5},{2,6},{3,7},{4,0},{5,1},{6,2},{7,3},{8,12},{9,13},{10,... | collective-permute-start | bytes 196616 | tf_op jit(solution)/shard_map/ppermute | solution.py:363
  8.4 6.1 %collective-permute-start.1 = (bf16[64,512]{1,0:T(8,128)(2,1)S(1)}, bf16[64,512]{1,0:T(8,128)(2,1)S(1)}, u32[]{:S(2)}, u32[]{:S(2)}) collective-permute-start(bf16[64,512]{1,0:T(8,128)(2,1)S(1)} %get-tuple-element.23.refs_0_), channel_id=1, source_target_pairs={{0,6},{1,7},{2,4},{3,5},{4,2},{5,3},{6,0},{7,1},{8,14},{9,15},{10,... | collective-permute-start | bytes 196616 | tf_op jit(solution)/shard_map/ppermute | solution.py:363
  8.4 6.1 %collective-permute-start = (bf16[64,512]{1,0:T(8,128)(2,1)S(1)}, bf16[64,512]{1,0:T(8,128)(2,1)S(1)}, u32[]{:S(2)}, u32[]{:S(2)}) collective-permute-start(bf16[64,512]{1,0:T(8,128)(2,1)S(1)} %get-tuple-element.23.refs_0_), channel_id=1, source_target_pairs={{0,1},{1,0},{2,3},{3,2},{4,5},{5,4},{6,7},{7,6},{8,9},{9,8},{10,11... | collective-permute-start | bytes 196616 | tf_op jit(solution)/shard_map/ppermute | solution.py:322
  8.4 6.1 %collective-permute-start.6 = (bf16[64,512]{1,0:T(8,128)(2,1)S(1)}, bf16[64,512]{1,0:T(8,128)(2,1)S(1)}, u32[]{:S(2)}, u32[]{:S(2)}) collective-permute-start(bf16[64,512]{1,0:T(8,128)(2,1)S(1)} %collective-permute-done.5.refs_6_), channel_id=1, source_target_pairs={{0,1},{1,0},{2,3},{3,2},{4,5},{5,4},{6,7},{7,6},{8,9},{9,8},{10,11... | collective-permute-start | bytes 196616 | tf_op jit(solution)/shard_map/ppermute | solution.py:322
  13.0 1.4 %collective-permute-start.4 = (bf16[64,512]{1,0:T(8,128)(2,1)S(1)}, bf16[64,512]{1,0:T(8,128)(2,1)S(1)}, u32[]{:S(2)}, u32[]{:S(2)}) collective-permute-start(bf16[64,512]{1,0:T(8,128)(2,1)S(1)} %collective-permute-done.3.refs_4_), channel_id=1, source_target_pairs={{0,1},{1,0},{2,3},{3,2},{4,5},{5,4},{6,7},{7,6},{8,9},{9,8},{10,11... | collective-permute-start | bytes 196616 | tf_op jit(solution)/shard_map/ppermute | solution.py:322
  14.4 1.3 %collective-permute-start.2 = (bf16[64,512]{1,0:T(8,128)(2,1)S(1)}, bf16[64,512]{1,0:T(8,128)(2,1)S(1)}, u32[]{:S(2)}, u32[]{:S(2)}) collective-permute-start(bf16[64,512]{1,0:T(8,128)(2,1)S(1)} %collective-permute-done.1.refs_2_), channel_id=1, source_target_pairs={{0,1},{1,0},{2,3},{3,2},{4,5},{5,4},{6,7},{7,6},{8,9},{9,8},{10,11... | collective-permute-start | bytes 196616 | tf_op jit(solution)/shard_map/ppermute | solution.py:322
  17.2 5.9 %collective-permute-start.7 = (bf16[192,256]{1,0:T(8,128)(2,1)S(1)}, bf16[192,256]{1,0:T(8,128)(2,1)S(1)}, u32[]{:S(2)}, u32[]{:S(2)}) collective-permute-start(bf16[192,256]{1,0:T(8,128)(2,1)S(1)} %get-tuple-element.25), channel_id=1, source_target_pairs={{0,24},{8,16},{16,8},{24,0},{1,25},{9,17},{17,9},{25,1},{2,26},{10... | collective-permute-start | bytes 294920 | tf_op jit(solution)/shard_map/ppermute | solution.py:322
  19.7 5.4 %collective-permute-start.8 = (bf16[192,256]{1,0:T(8,128)(2,1)S(1)}, bf16[192,256]{1,0:T(8,128)(2,1)S(1)}, u32[]{:S(2)}, u32[]{:S(2)}) collective-permute-start(bf16[192,256]{1,0:T(8,128)(2,1)S(1)} %get-tuple-element.26), channel_id=1, source_target_pairs={{0,16},{8,24},{16,0},{24,8},{1,17},{9,25},{17,1},{25,9},{2,18},{10... | collective-permute-start | bytes 294920 | tf_op jit(solution)/shard_map/ppermute | solution.py:322
  20.2 5.0 %collective-permute-start.9 = (bf16[192,256]{1,0:T(8,128)(2,1)S(1)}, bf16[192,256]{1,0:T(8,128)(2,1)S(1)}, u32[]{:S(2)}, u32[]{:S(2)}) collective-permute-start(bf16[192,256]{1,0:T(8,128)(2,1)S(1)} %get-tuple-element.27), channel_id=1, source_target_pairs={{0,8},{8,0},{16,24},{24,16},{1,9},{9,1},{17,25},{25,17},{2,10},{10... | collective-permute-start | bytes 294920 | tf_op jit(solution)/shard_map/ppermute | solution.py:322
  25.8 5.7 %collective-permute-start.10 = (bf16[128,256]{1,0:T(8,128)(2,1)S(1)}, bf16[128,256]{1,0:T(8,128)(2,1)S(1)}, u32[]{:S(2)}, u32[]{:S(2)}) collective-permute-start(bf16[128,256]{1,0:T(8,128)(2,1)S(1)} %get-tuple-element.29), channel_id=1, source_target_pairs={{0,24},{8,16},{16,8},{24,0},{1,25},{9,17},{17,9},{25,1},{2,26},{10... | collective-permute-start | bytes 196616 | tf_op jit(solution)/shard_map/ppermute | solution.py:322
  27.5 4.5 %collective-permute-start.11 = (bf16[128,256]{1,0:T(8,128)(2,1)S(1)}, bf16[128,256]{1,0:T(8,128)(2,1)S(1)}, u32[]{:S(2)}, u32[]{:S(2)}) collective-permute-start(bf16[128,256]{1,0:T(8,128)(2,1)S(1)} %get-tuple-element.30), channel_id=1, source_target_pairs={{0,16},{8,24},{16,0},{24,8},{1,17},{9,25},{17,1},{25,9},{2,18},{10... | collective-permute-start | bytes 196616 | tf_op jit(solution)/shard_map/ppermute | solution.py:322
  28.8 4.3 %collective-permute-start.12 = (bf16[128,256]{1,0:T(8,128)(2,1)S(1)}, bf16[128,256]{1,0:T(8,128)(2,1)S(1)}, u32[]{:S(2)}, u32[]{:S(2)}) collective-permute-start(bf16[128,256]{1,0:T(8,128)(2,1)S(1)} %get-tuple-element.31), channel_id=1, source_target_pairs={{0,8},{8,0},{16,24},{24,16},{1,9},{9,1},{17,25},{25,17},{2,10},{10... | collective-permute-start | bytes 196616 | tf_op jit(solution)/shard_map/ppermute | solution.py:322
  34.3 1.6 %collective-permute-start.13 = (bf16[4,64,512]{2,1,0:T(8,128)(2,1)S(1)}, bf16[4,64,512]{2,1,0:T(8,128)(2,1)S(1)}, u32[]{:S(2)}, u32[]{:S(2)}) collective-permute-start(bf16[4,64,512]{2,1,0:T(8,128)(2,1)S(1)} %shard_map.59), channel_id=1, source_target_pairs={{0,1},{1,0},{2,3},{3,2},{4,5},{5,4},{6,7},{7,6},{8,9},{9,8},{10,11... | collective-permute-start | bytes 786440 | tf_op jit(solution)/shard_map/ppermute | solution.py:322
  35.9 6.8 %collective-permute-start.14 = (bf16[64,512]{1,0:T(8,128)(2,1)S(1)}, bf16[64,512]{1,0:T(8,128)(2,1)S(1)}, u32[]{:S(2)}, u32[]{:S(2)}) collective-permute-start(bf16[64,512]{1,0:T(8,128)(2,1)S(1)} %get-tuple-element.33), channel_id=1, source_target_pairs={{0,6},{1,7},{2,4},{3,5},{4,2},{5,3},{6,0},{7,1},{8,14},{9,15},{10,... | collective-permute-start | bytes 196616 | tf_op jit(solution)/shard_map/ppermute | solution.py:322
  38.1 6.6 %collective-permute-start.15 = (bf16[64,512]{1,0:T(8,128)(2,1)S(1)}, bf16[64,512]{1,0:T(8,128)(2,1)S(1)}, u32[]{:S(2)}, u32[]{:S(2)}) collective-permute-start(bf16[64,512]{1,0:T(8,128)(2,1)S(1)} %get-tuple-element.34), channel_id=1, source_target_pairs={{0,4},{1,5},{2,6},{3,7},{4,0},{5,1},{6,2},{7,3},{8,12},{9,13},{10,... | collective-permute-start | bytes 196616 | tf_op jit(solution)/shard_map/ppermute | solution.py:322
  38.1 6.6 %collective-permute-start.16 = (bf16[64,512]{1,0:T(8,128)(2,1)S(1)}, bf16[64,512]{1,0:T(8,128)(2,1)S(1)}, u32[]{:S(2)}, u32[]{:S(2)}) collective-permute-start(bf16[64,512]{1,0:T(8,128)(2,1)S(1)} %get-tuple-element.35), channel_id=1, source_target_pairs={{0,2},{1,3},{2,0},{3,1},{4,6},{5,7},{6,4},{7,5},{8,10},{9,11},{10,... | collective-permute-start | bytes 196616 | tf_op jit(solution)/shard_map/ppermute | solution.py:322

commit v11 on v10

--- a/solution.py
+++ b/solution.py
@@ -112,7 +112,7 @@
 
 
 def orders(shares):
-    return [list(reversed(range(1, shares)))] * shares
+    return [list(range(1, shares))] * shares
 
 
 def pick(table, index):

time: 46.7 us -> 46 us (0.985)
  waiting for transfers between devices: 19.8 us -> 19 us
    ppermute x3, waiting for transfers between devices: 5.56 us -> 4.96 us  [body(): block = lax.ppermute(edge, ('ka', 'pts'), pairs)]
  transfers between devices with their start and end apart: 17 -> 17, of which waited for: 12 -> 13; matrix products, arithmetic and copies ran while one was open for 0% -> 0% of each run, Pallas kernels for 2% -> 3%
where the time goes in v11:
time: 46 us; the launch traced here: 45.8 us
  waiting for transfers between devices  19 us (41%)
  starting transfers between devices  17.9 us (39%)
  Pallas kernels  8.8 us (19%)
    ppermute x14, waiting for transfers between devices, swap(): return lax.ppermute(value, axis, [(i, i ^ mask) for i in range(size)])  14.1 us
    ppermute x14, starting transfers between devices, swap(): return lax.ppermute(value, axis, [(i, i ^ mask) for i in range(size)])  12.1 us
    ppermute x3, starting transfers between devices, body(): block = lax.ppermute(edge, ('ka', 'pts'), pairs)  5.79 us
    ppermute x3, waiting for transfers between devices, body(): block = lax.ppermute(edge, ('ka', 'pts'), pairs)  4.96 us
    pallas_call x1, Pallas kernels, body(): call(functools.partial(edge_kernel, per_block), [shape((local_k * 2 * per...  2.63 us
    pallas_call x2, Pallas kernels, body(): call(functools.partial(weight_kernel, shares, flip, out_rows), shape((chu...  2.33 us
    pallas_call x1, Pallas kernels, body(): call(functools.partial(exchange_kernel, chunks, shares, 1.0 / math.sqrt(p...  1.75 us
    pallas_call x1, Pallas kernels, body(): call(functools.partial(tile_kernel, targets, shares, per_share, per_block...  1.46 us
  transfers between devices with their start and end apart: 17, of which 13 were waited for; matrix products, arithmetic and copies ran while one was open for 0% of the time, Pallas kernels for 3%

profile of v11, /device:TPU:0, one launch (start us, length us, event | category | flops | bytes accessed | tf_op | source)
XLA Modules:
  0.0 45.8 jit_solution(977453796313450683)
XLA Ops:
  0.0 2.6 %shard_map.55 = (bf16[64,512]{1,0:T(8,128)(2,1)S(1)}, bf16[8,2,512,256]{3,2,1,0:T(8,128)(2,1)S(1)}) custom-call(bf16[8,2,512,256]{3,2,1,0:T(8,128)(2,1)} %orb_hbm.1), custom_call_target="tpu_custom_call" | custom-call | bytes 8388608 | tf_op jit(solution)/shard_map/pallas_call | solution.py:341
  2.6 5.1 %collective-permute-start.5 = (bf16[64,512]{1,0:T(8,128)(2,1)S(1)}, bf16[64,512]{1,0:T(8,128)(2,1)S(1)}, u32[]{:S(2)}, u32[]{:S(2)}) collective-permute-start(bf16[64,512]{1,0:T(8,128)(2,1)S(1)} %get-tuple-element.23.refs_0_), channel_id=1, source_target_pairs={{0,6},{1,7},{2,4},{3,5},{4,2},{5,3},{6,0},{7,1},{8,14},{9,15},{10,... | collective-permute-start | bytes 196616 | tf_op jit(solution)/shard_map/ppermute | solution.py:363
  7.8 0.0 collective-permute-start.3
  7.8 0.6 %collective-permute-start.1 = (bf16[64,512]{1,0:T(8,128)(2,1)S(1)}, bf16[64,512]{1,0:T(8,128)(2,1)S(1)}, u32[]{:S(2)}, u32[]{:S(2)}) collective-permute-start(bf16[64,512]{1,0:T(8,128)(2,1)S(1)} %get-tuple-element.23.refs_0_), channel_id=1, source_target_pairs={{0,2},{1,3},{2,0},{3,1},{4,6},{5,7},{6,4},{7,5},{8,10},{9,11},{10,... | collective-permute-start | bytes 196616 | tf_op jit(solution)/shard_map/ppermute | solution.py:363
  8.4 1.9 %collective-permute-done.5.refs_6_ = bf16[64,512]{1,0:T(8,128)(2,1)S(1)} collective-permute-done((bf16[64,512]{1,0:T(8,128)(2,1)S(1)}, bf16[64,512]{1,0:T(8,128)(2,1)S(1)}, u32[]{:S(2)}, u32[]{:S(2)}) %collective-permute-start.5) | collective-permute-done | bytes 65568 | tf_op jit(solution)/shard_map/ppermute | solution.py:363
  10.4 3.0 %collective-permute-done.3.refs_4_ = bf16[64,512]{1,0:T(8,128)(2,1)S(1)} collective-permute-done((bf16[64,512]{1,0:T(8,128)(2,1)S(1)}, bf16[64,512]{1,0:T(8,128)(2,1)S(1)}, u32[]{:S(2)}, u32[]{:S(2)}) %collective-permute-start.3) | collective-permute-done | bytes 65568 | tf_op jit(solution)/shard_map/ppermute | solution.py:363
  13.4 0.5 %collective-permute-start.2 = (bf16[64,512]{1,0:T(8,128)(2,1)S(1)}, bf16[64,512]{1,0:T(8,128)(2,1)S(1)}, u32[]{:S(2)}, u32[]{:S(2)}) collective-permute-start(bf16[64,512]{1,0:T(8,128)(2,1)S(1)} %collective-permute-done.1.refs_2_), channel_id=1, source_target_pairs={{0,1},{1,0},{2,3},{3,2},{4,5},{5,4},{6,7},{7,6},{8,9},{9,8},{10,11... | collective-permute-start | bytes 196616 | tf_op jit(solution)/shard_map/ppermute | solution.py:322
  13.9 0.7 %collective-permute-done.4.refs_5_ = bf16[64,512]{1,0:T(8,128)(2,1)S(1)} collective-permute-done((bf16[64,512]{1,0:T(8,128)(2,1)S(1)}, bf16[64,512]{1,0:T(8,128)(2,1)S(1)}, u32[]{:S(2)}, u32[]{:S(2)}) %collective-permute-start.4) | collective-permute-done | bytes 65568 | tf_op jit(solution)/shard_map/ppermute | solution.py:322
  14.6 0.2 collective-permute-done.2.refs_3_
  14.8 1.5 %shard_map.56 = (bf16[192,256]{1,0:T(8,128)(2,1)S(1)}, bf16[192,256]{1,0:T(8,128)(2,1)S(1)}, bf16[192,256]{1,0:T(8,128)(2,1)S(1)}, bf16[192,256]{1,0:T(8,128)(2,...) custom-call(bf16[64,512]{1,0:T(8,128)(2,1)S(1)} %get-tuple-element.2, ...), custom_call_target="tpu_custom_call" | custom-call | bytes 6291456 | tf_op jit(solution)/shard_map/pallas_call | solution.py:375
  16.3 2.5 %collective-permute-start.7 = (bf16[192,256]{1,0:T(8,128)(2,1)S(1)}, bf16[192,256]{1,0:T(8,128)(2,1)S(1)}, u32[]{:S(2)}, u32[]{:S(2)}) collective-permute-start(bf16[192,256]{1,0:T(8,128)(2,1)S(1)} %get-tuple-element.25), channel_id=1, source_target_pairs={{0,24},{8,16},{16,8},{24,0},{1,25},{9,17},{17,9},{25,1},{2,26},{10... | collective-permute-start | bytes 294920 | tf_op jit(solution)/shard_map/ppermute | solution.py:322
  18.8 0.5 %collective-permute-start.8 = (bf16[192,256]{1,0:T(8,128)(2,1)S(1)}, bf16[192,256]{1,0:T(8,128)(2,1)S(1)}, u32[]{:S(2)}, u32[]{:S(2)}) collective-permute-start(bf16[192,256]{1,0:T(8,128)(2,1)S(1)} %get-tuple-element.26), channel_id=1, source_target_pairs={{0,16},{8,24},{16,0},{24,8},{1,17},{9,25},{17,1},{25,9},{2,18},{10... | collective-permute-start | bytes 294920 | tf_op jit(solution)/shard_map/ppermute | solution.py:322
  19.3 0.5 %collective-permute-start.9 = (bf16[192,256]{1,0:T(8,128)(2,1)S(1)}, bf16[192,256]{1,0:T(8,128)(2,1)S(1)}, u32[]{:S(2)}, u32[]{:S(2)}) collective-permute-start(bf16[192,256]{1,0:T(8,128)(2,1)S(1)} %get-tuple-element.27), channel_id=1, source_target_pairs={{0,8},{8,0},{16,24},{24,16},{1,9},{9,1},{17,25},{25,17},{2,10},{10... | collective-permute-start | bytes 294920 | tf_op jit(solution)/shard_map/ppermute | solution.py:322
  19.8 2.6 %collective-permute-done.7.refs_0_ = bf16[192,256]{1,0:T(8,128)(2,1)S(1)} collective-permute-done((bf16[192,256]{1,0:T(8,128)(2,1)S(1)}, bf16[192,256]{1,0:T(8,128)(2,1)S(1)}, u32[]{:S(2)}, u32[]{:S(2)}) %collective-permute-start.7) | collective-permute-done | bytes 98336 | tf_op jit(solution)/shard_map/ppermute | solution.py:322
  22.4 2.0 %collective-permute-done.8.refs_1_ = bf16[192,256]{1,0:T(8,128)(2,1)S(1)} collective-permute-done((bf16[192,256]{1,0:T(8,128)(2,1)S(1)}, bf16[192,256]{1,0:T(8,128)(2,1)S(1)}, u32[]{:S(2)}, u32[]{:S(2)}) %collective-permute-start.8) | collective-permute-done | bytes 98336 | tf_op jit(solution)/shard_map/ppermute | solution.py:322
  24.4 0.1 collective-permute-done.9.refs_2_
  24.5 0.6 %shard_map.57 = (bf16[128,256]{1,0:T(8,128)(2,1)S(1)}, bf16[128,256]{1,0:T(8,128)(2,1)S(1)}, bf16[128,256]{1,0:T(8,128)(2,1)S(1)}, bf16[128,256]{1,0:T(8,128)(2,1)S(1)}) custom-call(bf16[192,256]{1,0:T(8,128)(2,1)S(1)} %collective-permute-done.7.refs_0_, bf16[192,256]{1,0:T(8,128)(2,1)S(1)} %collective-permute-done.8.refs_1_, ...), custom_call_target="tpu_custom_call" | custom-call | bytes 2097152 | tf_op jit(solution)/shard_map/pallas_call | solution.py:393
  25.1 1.8 %collective-permute-start.10 = (bf16[128,256]{1,0:T(8,128)(2,1)S(1)}, bf16[128,256]{1,0:T(8,128)(2,1)S(1)}, u32[]{:S(2)}, u32[]{:S(2)}) collective-permute-start(bf16[128,256]{1,0:T(8,128)(2,1)S(1)} %get-tuple-element.29), channel_id=1, source_target_pairs={{0,24},{8,16},{16,8},{24,0},{1,25},{9,17},{17,9},{25,1},{2,26},{10... | collective-permute-start | bytes 196616 | tf_op jit(solution)/shard_map/ppermute | solution.py:322
  26.8 1.3 %collective-permute-start.11 = (bf16[128,256]{1,0:T(8,128)(2,1)S(1)}, bf16[128,256]{1,0:T(8,128)(2,1)S(1)}, u32[]{:S(2)}, u32[]{:S(2)}) collective-permute-start(bf16[128,256]{1,0:T(8,128)(2,1)S(1)} %get-tuple-element.30), channel_id=1, source_target_pairs={{0,16},{8,24},{16,0},{24,8},{1,17},{9,25},{17,1},{25,9},{2,18},{10... | collective-permute-start | bytes 196616 | tf_op jit(solution)/shard_map/ppermute | solution.py:322
  28.1 0.5 %collective-permute-start.12 = (bf16[128,256]{1,0:T(8,128)(2,1)S(1)}, bf16[128,256]{1,0:T(8,128)(2,1)S(1)}, u32[]{:S(2)}, u32[]{:S(2)}) collective-permute-start(bf16[128,256]{1,0:T(8,128)(2,1)S(1)} %get-tuple-element.31), channel_id=1, source_target_pairs={{0,8},{8,0},{16,24},{24,16},{1,9},{9,1},{17,25},{25,17},{2,10},{10... | collective-permute-start | bytes 196616 | tf_op jit(solution)/shard_map/ppermute | solution.py:322
  28.6 2.1 %collective-permute-done.10.refs_0_ = bf16[128,256]{1,0:T(8,128)(2,1)S(1)} collective-permute-done((bf16[128,256]{1,0:T(8,128)(2,1)S(1)}, bf16[128,256]{1,0:T(8,128)(2,1)S(1)}, u32[]{:S(2)}, u32[]{:S(2)}) %collective-permute-start.10) | collective-permute-done | bytes 65568 | tf_op jit(solution)/shard_map/ppermute | solution.py:322
  30.7 0.7 %collective-permute-done.11.refs_1_ = bf16[128,256]{1,0:T(8,128)(2,1)S(1)} collective-permute-done((bf16[128,256]{1,0:T(8,128)(2,1)S(1)}, bf16[128,256]{1,0:T(8,128)(2,1)S(1)}, u32[]{:S(2)}, u32[]{:S(2)}) %collective-permute-start.11) | collective-permute-done | bytes 65568 | tf_op jit(solution)/shard_map/ppermute | solution.py:322
  31.4 1.0 %collective-permute-done.12.refs_2_ = bf16[128,256]{1,0:T(8,128)(2,1)S(1)} collective-permute-done((bf16[128,256]{1,0:T(8,128)(2,1)S(1)}, bf16[128,256]{1,0:T(8,128)(2,1)S(1)}, u32[]{:S(2)}, u32[]{:S(2)}) %collective-permute-start.12) | collective-permute-done | bytes 65568 | tf_op jit(solution)/shard_map/ppermute | solution.py:322
  32.4 1.2 %shard_map.59 = bf16[4,64,512]{2,1,0:T(8,128)(2,1)S(1)} custom-call(bf16[128,256]{1,0:T(8,128)(2,1)S(1)} %collective-permute-done.10.refs_0_, bf16[128,256]{1,0:T(8,128)(2,1)S(1)} %collective-permute-done.11.refs_1_, bf16[128,256]{1,0:T(8,128)(2,1)S(1)} %collective-permute-done.12.refs_2_, bf16[128,256]{1,0:T(8,128)(2,1)S(1)} %get-tuple-element.32.refs_3_, ...), custom_call_target="tpu_custom_call" | custom-call | bytes 6291456 | tf_op jit(solution)/shard_map/pallas_call | solution.py:410
  33.6 0.1 collective-permute-start.13
  33.7 1.2 %shard_map.58.keep_ref = f32[4,64,512]{2,1,0:T(8,128)S(1)} custom-call(bf16[128,256]{1,0:T(8,128)(2,1)S(1)} %collective-permute-done.10.refs_0_, bf16[128,256]{1,0:T(8,128)(2,1)S(1)} %collective-permute-done.11.refs_1_, bf16[128,256]{1,0:T(8,128)(2,1)S(1)} %collective-permute-done.12.refs_2_, bf16[128,256]{1,0:T(8,128)(2,1)S(1)} %get-tuple-element.32.refs_3_, ...), custom_call_target="tpu_custom_call" | custom-call | bytes 6291456 | tf_op jit(solution)/shard_map/pallas_call | solution.py:410
  34.8 0.4 collective-permute-done.13.came_ref
  35.2 2.8 %collective-permute-start.14 = (bf16[64,512]{1,0:T(8,128)(2,1)S(1)}, bf16[64,512]{1,0:T(8,128)(2,1)S(1)}, u32[]{:S(2)}, u32[]{:S(2)}) collective-permute-start(bf16[64,512]{1,0:T(8,128)(2,1)S(1)} %get-tuple-element.33), channel_id=1, source_target_pairs={{0,6},{1,7},{2,4},{3,5},{4,2},{5,3},{6,0},{7,1},{8,14},{9,15},{10,... | collective-permute-start | bytes 196616 | tf_op jit(solution)/shard_map/ppermute | solution.py:322
  38.0 1.7 %collective-permute-start.16 = (bf16[64,512]{1,0:T(8,128)(2,1)S(1)}, bf16[64,512]{1,0:T(8,128)(2,1)S(1)}, u32[]{:S(2)}, u32[]{:S(2)}) collective-permute-start(bf16[64,512]{1,0:T(8,128)(2,1)S(1)} %get-tuple-element.35), channel_id=1, source_target_pairs={{0,2},{1,3},{2,0},{3,1},{4,6},{5,7},{6,4},{7,5},{8,10},{9,11},{10,... | collective-permute-start | bytes 196616 | tf_op jit(solution)/shard_map/ppermute | solution.py:322
  39.7 2.3 %collective-permute-done.14.refs_0_ = bf16[64,512]{1,0:T(8,128)(2,1)S(1)} collective-permute-done((bf16[64,512]{1,0:T(8,128)(2,1)S(1)}, bf16[64,512]{1,0:T(8,128)(2,1)S(1)}, u32[]{:S(2)}, u32[]{:S(2)}) %collective-permute-start.14) | collective-permute-done | bytes 65568 | tf_op jit(solution)/shard_map/ppermute | solution.py:322
  42.0 2.0 %collective-permute-done.15.refs_1_ = bf16[64,512]{1,0:T(8,128)(2,1)S(1)} collective-permute-done((bf16[64,512]{1,0:T(8,128)(2,1)S(1)}, bf16[64,512]{1,0:T(8,128)(2,1)S(1)}, u32[]{:S(2)}, u32[]{:S(2)}) %collective-permute-start.15) | collective-permute-done | bytes 65568 | tf_op jit(solution)/shard_map/ppermute | solution.py:322
  44.1 1.8 %shard_map.61 = bf16[64,4,16,128]{3,2,1,0:T(8,128)(2,1)} custom-call(bf16[64,512]{1,0:T(8,128)(2,1)S(1)} %collective-permute-done.14.refs_0_, bf16[64,512]{1,0:T(8,128)(2,1)S(1)} %collective-permute-done.15.refs_1_, bf16[64,512]{1,0:T(8,128)(2,1)S(1)} %collective-permute-done.16.refs_2_, f32[64,512]{1,0:T(8,128)S(1)} %get-tuple-element.36.refs_3_, ...), custom_call_target="tpu_custom_call" | custom-call | bytes 4194304 | tf_op jit(solution)/shard_map/pallas_call | solution.py:429
  (17 shorter events, 0.1 us)
Async XLA Ops:
  0.0 14.8 %copy-start.1 = (bf16[64,32]{1,0:T(8,128)(2,1)S(1)}, bf16[64,32]{1,0:T(8,128)(2,1)}, u32[]{:S(2)}) copy-start(bf16[64,32]{1,0:T(8,128)(2,1)} %constant.6.clone.refs_9_) | copy-start | bytes 12292
  0.0 24.5 %copy-start.2 = (bf16[64,128]{1,0:T(8,128)(2,1)S(1)}, bf16[64,128]{1,0:T(8,128)(2,1)}, u32[]{:S(2)}) copy-start(bf16[64,128]{1,0:T(8,128)(2,1)} %constant.8.clone.refs_5_) | copy-start | bytes 49156
  0.0 24.5 %copy-start.3 = (bf16[64,128]{1,0:T(8,128)(2,1)S(1)}, bf16[64,128]{1,0:T(8,128)(2,1)}, u32[]{:S(2)}) copy-start(bf16[64,128]{1,0:T(8,128)(2,1)} %constant.7.clone.refs_4_) | copy-start | bytes 49156
  0.0 14.8 %copy-start = (bf16[8,32,256]{2,1,0:T(8,128)(2,1)S(1)}, bf16[8,32,256]{2,1,0:T(8,128)(2,1)}, u32[]{:S(2)}) copy-start(bf16[8,32,256]{2,1,0:T(8,128)(2,1)} %refs_10_.1) | copy-start | bytes 393220
  2.6 7.7 %collective-permute-start.5 = (bf16[64,512]{1,0:T(8,128)(2,1)S(1)}, bf16[64,512]{1,0:T(8,128)(2,1)S(1)}, u32[]{:S(2)}, u32[]{:S(2)}) collective-permute-start(bf16[64,512]{1,0:T(8,128)(2,1)S(1)} %get-tuple-element.23.refs_0_), channel_id=1, source_target_pairs={{0,6},{1,7},{2,4},{3,5},{4,2},{5,3},{6,0},{7,1},{8,14},{9,15},{10,... | collective-permute-start | bytes 196616 | tf_op jit(solution)/shard_map/ppermute | solution.py:363
  7.8 5.6 %collective-permute-start.3 = (bf16[64,512]{1,0:T(8,128)(2,1)S(1)}, bf16[64,512]{1,0:T(8,128)(2,1)S(1)}, u32[]{:S(2)}, u32[]{:S(2)}) collective-permute-start(bf16[64,512]{1,0:T(8,128)(2,1)S(1)} %get-tuple-element.23.refs_0_), channel_id=1, source_target_pairs={{0,4},{1,5},{2,6},{3,7},{4,0},{5,1},{6,2},{7,3},{8,12},{9,13},{10,... | collective-permute-start | bytes 196616 | tf_op jit(solution)/shard_map/ppermute | solution.py:363
  7.8 5.6 %collective-permute-start.1 = (bf16[64,512]{1,0:T(8,128)(2,1)S(1)}, bf16[64,512]{1,0:T(8,128)(2,1)S(1)}, u32[]{:S(2)}, u32[]{:S(2)}) collective-permute-start(bf16[64,512]{1,0:T(8,128)(2,1)S(1)} %get-tuple-element.23.refs_0_), channel_id=1, source_target_pairs={{0,2},{1,3},{2,0},{3,1},{4,6},{5,7},{6,4},{7,5},{8,10},{9,11},{10,... | collective-permute-start | bytes 196616 | tf_op jit(solution)/shard_map/ppermute | solution.py:363
  8.4 5.5 %collective-permute-start = (bf16[64,512]{1,0:T(8,128)(2,1)S(1)}, bf16[64,512]{1,0:T(8,128)(2,1)S(1)}, u32[]{:S(2)}, u32[]{:S(2)}) collective-permute-start(bf16[64,512]{1,0:T(8,128)(2,1)S(1)} %get-tuple-element.23.refs_0_), channel_id=1, source_target_pairs={{0,1},{1,0},{2,3},{3,2},{4,5},{5,4},{6,7},{7,6},{8,9},{9,8},{10,11... | collective-permute-start | bytes 196616 | tf_op jit(solution)/shard_map/ppermute | solution.py:322
  10.4 3.5 %collective-permute-start.6 = (bf16[64,512]{1,0:T(8,128)(2,1)S(1)}, bf16[64,512]{1,0:T(8,128)(2,1)S(1)}, u32[]{:S(2)}, u32[]{:S(2)}) collective-permute-start(bf16[64,512]{1,0:T(8,128)(2,1)S(1)} %collective-permute-done.5.refs_6_), channel_id=1, source_target_pairs={{0,1},{1,0},{2,3},{3,2},{4,5},{5,4},{6,7},{7,6},{8,9},{9,8},{10,11... | collective-permute-start | bytes 196616 | tf_op jit(solution)/shard_map/ppermute | solution.py:322
  13.4 1.3 %collective-permute-start.4 = (bf16[64,512]{1,0:T(8,128)(2,1)S(1)}, bf16[64,512]{1,0:T(8,128)(2,1)S(1)}, u32[]{:S(2)}, u32[]{:S(2)}) collective-permute-start(bf16[64,512]{1,0:T(8,128)(2,1)S(1)} %collective-permute-done.3.refs_4_), channel_id=1, source_target_pairs={{0,1},{1,0},{2,3},{3,2},{4,5},{5,4},{6,7},{7,6},{8,9},{9,8},{10,11... | collective-permute-start | bytes 196616 | tf_op jit(solution)/shard_map/ppermute | solution.py:322
  13.4 1.4 %collective-permute-start.2 = (bf16[64,512]{1,0:T(8,128)(2,1)S(1)}, bf16[64,512]{1,0:T(8,128)(2,1)S(1)}, u32[]{:S(2)}, u32[]{:S(2)}) collective-permute-start(bf16[64,512]{1,0:T(8,128)(2,1)S(1)} %collective-permute-done.1.refs_2_), channel_id=1, source_target_pairs={{0,1},{1,0},{2,3},{3,2},{4,5},{5,4},{6,7},{7,6},{8,9},{9,8},{10,11... | collective-permute-start | bytes 196616 | tf_op jit(solution)/shard_map/ppermute | solution.py:322
  16.3 6.1 %collective-permute-start.7 = (bf16[192,256]{1,0:T(8,128)(2,1)S(1)}, bf16[192,256]{1,0:T(8,128)(2,1)S(1)}, u32[]{:S(2)}, u32[]{:S(2)}) collective-permute-start(bf16[192,256]{1,0:T(8,128)(2,1)S(1)} %get-tuple-element.25), channel_id=1, source_target_pairs={{0,24},{8,16},{16,8},{24,0},{1,25},{9,17},{17,9},{25,1},{2,26},{10... | collective-permute-start | bytes 294920 | tf_op jit(solution)/shard_map/ppermute | solution.py:322
  18.8 5.6 %collective-permute-start.8 = (bf16[192,256]{1,0:T(8,128)(2,1)S(1)}, bf16[192,256]{1,0:T(8,128)(2,1)S(1)}, u32[]{:S(2)}, u32[]{:S(2)}) collective-permute-start(bf16[192,256]{1,0:T(8,128)(2,1)S(1)} %get-tuple-element.26), channel_id=1, source_target_pairs={{0,16},{8,24},{16,0},{24,8},{1,17},{9,25},{17,1},{25,9},{2,18},{10... | collective-permute-start | bytes 294920 | tf_op jit(solution)/shard_map/ppermute | solution.py:322
  19.3 5.2 %collective-permute-start.9 = (bf16[192,256]{1,0:T(8,128)(2,1)S(1)}, bf16[192,256]{1,0:T(8,128)(2,1)S(1)}, u32[]{:S(2)}, u32[]{:S(2)}) collective-permute-start(bf16[192,256]{1,0:T(8,128)(2,1)S(1)} %get-tuple-element.27), channel_id=1, source_target_pairs={{0,8},{8,0},{16,24},{24,16},{1,9},{9,1},{17,25},{25,17},{2,10},{10... | collective-permute-start | bytes 294920 | tf_op jit(solution)/shard_map/ppermute | solution.py:322
  25.1 5.7 %collective-permute-start.10 = (bf16[128,256]{1,0:T(8,128)(2,1)S(1)}, bf16[128,256]{1,0:T(8,128)(2,1)S(1)}, u32[]{:S(2)}, u32[]{:S(2)}) collective-permute-start(bf16[128,256]{1,0:T(8,128)(2,1)S(1)} %get-tuple-element.29), channel_id=1, source_target_pairs={{0,24},{8,16},{16,8},{24,0},{1,25},{9,17},{17,9},{25,1},{2,26},{10... | collective-permute-start | bytes 196616 | tf_op jit(solution)/shard_map/ppermute | solution.py:322
  26.8 4.6 %collective-permute-start.11 = (bf16[128,256]{1,0:T(8,128)(2,1)S(1)}, bf16[128,256]{1,0:T(8,128)(2,1)S(1)}, u32[]{:S(2)}, u32[]{:S(2)}) collective-permute-start(bf16[128,256]{1,0:T(8,128)(2,1)S(1)} %get-tuple-element.30), channel_id=1, source_target_pairs={{0,16},{8,24},{16,0},{24,8},{1,17},{9,25},{17,1},{25,9},{2,18},{10... | collective-permute-start | bytes 196616 | tf_op jit(solution)/shard_map/ppermute | solution.py:322
  28.1 4.3 %collective-permute-start.12 = (bf16[128,256]{1,0:T(8,128)(2,1)S(1)}, bf16[128,256]{1,0:T(8,128)(2,1)S(1)}, u32[]{:S(2)}, u32[]{:S(2)}) collective-permute-start(bf16[128,256]{1,0:T(8,128)(2,1)S(1)} %get-tuple-element.31), channel_id=1, source_target_pairs={{0,8},{8,0},{16,24},{24,16},{1,9},{9,1},{17,25},{25,17},{2,10},{10... | collective-permute-start | bytes 196616 | tf_op jit(solution)/shard_map/ppermute | solution.py:322
  33.6 1.6 %collective-permute-start.13 = (bf16[4,64,512]{2,1,0:T(8,128)(2,1)S(1)}, bf16[4,64,512]{2,1,0:T(8,128)(2,1)S(1)}, u32[]{:S(2)}, u32[]{:S(2)}) collective-permute-start(bf16[4,64,512]{2,1,0:T(8,128)(2,1)S(1)} %shard_map.59), channel_id=1, source_target_pairs={{0,1},{1,0},{2,3},{3,2},{4,5},{5,4},{6,7},{7,6},{8,9},{9,8},{10,11... | collective-permute-start | bytes 786440 | tf_op jit(solution)/shard_map/ppermute | solution.py:322
  35.2 6.8 %collective-permute-start.14 = (bf16[64,512]{1,0:T(8,128)(2,1)S(1)}, bf16[64,512]{1,0:T(8,128)(2,1)S(1)}, u32[]{:S(2)}, u32[]{:S(2)}) collective-permute-start(bf16[64,512]{1,0:T(8,128)(2,1)S(1)} %get-tuple-element.33), channel_id=1, source_target_pairs={{0,6},{1,7},{2,4},{3,5},{4,2},{5,3},{6,0},{7,1},{8,14},{9,15},{10,... | collective-permute-start | bytes 196616 | tf_op jit(solution)/shard_map/ppermute | solution.py:322
  38.0 6.0 %collective-permute-start.15 = (bf16[64,512]{1,0:T(8,128)(2,1)S(1)}, bf16[64,512]{1,0:T(8,128)(2,1)S(1)}, u32[]{:S(2)}, u32[]{:S(2)}) collective-permute-start(bf16[64,512]{1,0:T(8,128)(2,1)S(1)} %get-tuple-element.34), channel_id=1, source_target_pairs={{0,4},{1,5},{2,6},{3,7},{4,0},{5,1},{6,2},{7,3},{8,12},{9,13},{10,... | collective-permute-start | bytes 196616 | tf_op jit(solution)/shard_map/ppermute | solution.py:322
  38.0 6.0 %collective-permute-start.16 = (bf16[64,512]{1,0:T(8,128)(2,1)S(1)}, bf16[64,512]{1,0:T(8,128)(2,1)S(1)}, u32[]{:S(2)}, u32[]{:S(2)}) collective-permute-start(bf16[64,512]{1,0:T(8,128)(2,1)S(1)} %get-tuple-element.35), channel_id=1, source_target_pairs={{0,2},{1,3},{2,0},{3,1},{4,6},{5,7},{6,4},{7,5},{8,10},{9,11},{10,... | collective-permute-start | bytes 196616 | tf_op jit(solution)/shard_map/ppermute | solution.py:322

commit v12 on v11

--- a/solution.py
+++ b/solution.py
@@ -89,11 +89,28 @@
     )
 
 
+def load_copies(orb_hbm, orb_ref, sems, start):
+    lanes = pl.ds(start, orb_ref.shape[3])
+    copies = [
+        pltpu.make_async_copy(orb_hbm.at[k, :, :, lanes], orb_ref.at[k], sems.at[k])
+        for k in range(orb_ref.shape[0])
+    ]
+    for copy in copies:
+        copy.start()
+    return copies
+
+
+def rest_kernel(orb_hbm, edge_hbm, pass_ref, orb_ref, sems, pass_sem):
+    copies = load_copies(orb_hbm, orb_ref, sems, LANES)
+    copies.append(pltpu.make_async_copy(edge_hbm, pass_ref, pass_sem))
+    copies[-1].start()
+    for copy in copies:
+        copy.wait()
+
+
 def edge_kernel(per_block, orb_hbm, edge_ref, orb_ref, sems):
     local_k = orb_hbm.shape[0]
-    copies = [pltpu.make_async_copy(orb_hbm.at[k], orb_ref.at[k], sems.at[k]) for k in range(local_k)]
-    for copy in copies:
-        copy.start()
+    copies = load_copies(orb_hbm, orb_ref, sems, 0)
     row = lax.broadcasted_iota(jnp.int32, (2 * per_block, LANES), 0)
     lane = lax.broadcasted_iota(jnp.int32, (2 * per_block, LANES), 1)
     one, zero = jnp.ones(row.shape, F32), jnp.zeros(row.shape, F32)
@@ -105,8 +122,8 @@
         for k in range(g * group, (g + 1) * group):
             copies[k].wait()
             rows.append(
-                dot(first, orb_ref[k, 0, :, :LANES], ((1,), (1,)))
-                + dot(second, orb_ref[k, 1, :, :LANES], ((1,), (1,)))
+                dot(first, orb_ref[k, 0], ((1,), (1,)))
+                + dot(second, orb_ref[k, 1], ((1,), (1,)))
             )
         edge_ref[g * ROWS : (g + 1) * ROWS] = jnp.concatenate(rows, axis=0).astype(BF16)
 
@@ -138,10 +155,10 @@
 def tile_kernel(targets, shares, per_share, per_block, *refs):
     steps = sorted({t for j in targets for t in steps_for(j, shares)})
     n, many = per_share * (1 + len(steps)), len(targets)
-    blocks, (orb_ref, sel_ref, coulomb_ref) = refs[:n], refs[n : n + 3]
+    blocks, (orb_ref, rest_ref, sel_ref, coulomb_ref) = refs[:n], refs[n : n + 4]
     *refs, gathered, wide, cells = refs[-2 * many - 3 :]
     outs, form_refs = refs[:many], refs[many:]
-    local_k, _, norb, points = orb_ref.shape
+    local_k, _, norb, _ = orb_ref.shape
     group = ROWS // (2 * per_block)
     share = per_share * per_block
     rows = 2 * share
@@ -171,7 +188,8 @@
             form = jnp.concatenate(
                 [jnp.concatenate(left, axis=0), jnp.concatenate(right, axis=0)], axis=1
             )
-            tile = dot(form, orb_ref[k].reshape(2 * norb, points))
+            halves = [ref[k].reshape(2 * norb, ref.shape[3]) for ref in (orb_ref, rest_ref)]
+            tile = dot(form, jnp.concatenate(halves, axis=1))
             for slot in range(many):
                 form_refs[slot][k] = form[slot * rows : (slot + 1) * rows]
                 for part in range(2):
@@ -220,8 +238,8 @@
 
 
 def weight_kernel(shares, flip, out_rows, *refs):
-    pieces, orb_ref, out_ref, gathered = refs[:shares][::-1], refs[shares], refs[shares + 1], refs[shares + 2]
-    local_k, _, norb, points = orb_ref.shape
+    pieces, (orb_ref, rest_ref, out_ref, gathered) = refs[:shares][::-1], refs[shares:]
+    local_k, _, norb, _ = orb_ref.shape
     total_rows = gathered.shape[1]
     half = total_rows // local_k // 2
     me = lax.axis_index("ka")
@@ -252,7 +270,13 @@
         for z in range(chunks):
             start = pl.multiple_of((2 * z + core) * out_rows, out_rows)
             rows = jnp.concatenate(
-                [orb_ref[k, part, pl.ds(start, out_rows), :] for k in left for part in range(2)], axis=1
+                [
+                    ref[k, part, pl.ds(start, out_rows), :]
+                    for k in left
+                    for part in range(2)
+                    for ref in (orb_ref, rest_ref)
+                ],
+                axis=1,
             )
             out_ref[z, :, g * group * lanes : (g + 1) * group * lanes] = dot(
                 rows, right, ((1,), (1,))
@@ -338,18 +362,30 @@
     group = ROWS // (2 * per_block)
     shape = jax.ShapeDtypeStruct
 
-    edge, orbitals = call(
+    edge, first = call(
         functools.partial(edge_kernel, per_block),
-        [shape((local_k * 2 * per_block, norb), BF16), shape(orbitals.shape, BF16)],
+        [
+            shape((local_k * 2 * per_block, norb), BF16),
+            shape((local_k, 2, norb, LANES), BF16),
+        ],
         0,
         [pltpu.SemaphoreType.DMA((local_k,))],
-        limit=47,
-        size=8 * MIB,
+        limit=50,
+        size=4 * MIB,
         unread=1,
     )(orbitals)
+    passed_edge, rest = call(
+        rest_kernel,
+        [shape(edge.shape, BF16), shape((local_k, 2, norb, points - LANES), BF16)],
+        0,
+        [pltpu.SemaphoreType.DMA((local_k,)), pltpu.SemaphoreType.DMA],
+        limit=49,
+        size=4 * MIB,
+        unread=2,
+    )(orbitals, edge)
     per_share = blocks // shares
     order = orders(shares)
-    partner = swap(edge, "pts", 1)
+    partner = swap(passed_edge, "pts", 1)
     near = [edge, partner] + [swap(edge, "pts", 2 * e + c) for e in range(1, per_share // 2) for c in range(2)]
     came = []
     for t in range(shares - 1):
@@ -375,7 +411,7 @@
         result = call(
             functools.partial(tile_kernel, targets, shares, per_share, per_block),
             [both] * many + [shape((local_k, 2 * share, 2 * norb), BF16)] * many,
-            len(near) + len(taken) + 3,
+            len(near) + len(taken) + 4,
             [
                 pltpu.VMEM((many, per_share, local_k * 2 * per_block, norb), BF16),
                 tiled(many * share * 2 * local_k, points),
@@ -383,7 +419,7 @@
             ],
             size=6 * MIB,
             unread=len(before),
-        )(*near, *taken, orbitals, selector, coulomb, *before)
+        )(*near, *taken, first, rest, selector, coulomb, *before)
         for slot, j in enumerate(targets):
             tiles[j], forms[j] = result[slot], result[many + slot]
         before = [forms[targets[0]]]
@@ -410,10 +446,10 @@
             call(
                 functools.partial(weight_kernel, shares, flip, out_rows),
                 shape((chunks, out_rows, lanes), kind),
-                shares + 1,
+                shares + 2,
                 [pltpu.VMEM((shares, share * 2 * local_k, points), BF16)],
                 size=6 * MIB,
-            )(*kernels, orbitals)
+            )(*kernels, first, rest)
         )
     came = swap(halves[0], "pts", 1)
     own_sum, *sums = call(

time: 46 us -> 45.9 us (level)
  waiting for transfers between devices: 19 us -> 17.1 us
  Pallas kernels: 8.8 us -> 10.3 us
    ppermute x3, waiting for transfers between devices: 4.96 us -> 3.06 us  [body(): block = lax.ppermute(edge, ('ka', 'pts'), pairs)]
    pallas_call x0 -> x1, Pallas kernels: none -> 1.58 us  [body(): call(rest_kernel, [shape(edge.shape, BF16), shape((local_k, 2, norb, poin...]
  transfers between devices with their start and end apart: 17 -> 17, of which waited for: 13 -> 12; matrix products, arithmetic and copies ran while one was open for 0% -> 0% of each run, Pallas kernels for 3% -> 6%
where the time goes in v12:
time: 45.9 us; the launch traced here: 45.7 us
  starting transfers between devices  18.2 us (40%)
  waiting for transfers between devices  17.1 us (37%)
  Pallas kernels  10.3 us (22%)
    ppermute x14, waiting for transfers between devices, swap(): return lax.ppermute(value, axis, [(i, i ^ mask) for i in range(size)])  14 us
    ppermute x14, starting transfers between devices, swap(): return lax.ppermute(value, axis, [(i, i ^ mask) for i in range(size)])  12.5 us
    ppermute x3, starting transfers between devices, body(): block = lax.ppermute(edge, ('ka', 'pts'), pairs)  5.76 us
    ppermute x3, waiting for transfers between devices, body(): block = lax.ppermute(edge, ('ka', 'pts'), pairs)  3.06 us
    pallas_call x1, Pallas kernels, body(): call(functools.partial(edge_kernel, per_block), [shape((local_k * 2 * per...  2.5 us
    pallas_call x2, Pallas kernels, body(): call(functools.partial(weight_kernel, shares, flip, out_rows), shape((chu...  2.33 us
    pallas_call x1, Pallas kernels, body(): call(functools.partial(exchange_kernel, chunks, shares, 1.0 / math.sqrt(p...  1.75 us
    pallas_call x1, Pallas kernels, body(): call(rest_kernel, [shape(edge.shape, BF16), shape((local_k, 2, norb, poin...  1.58 us
  transfers between devices with their start and end apart: 17, of which 12 were waited for; matrix products, arithmetic and copies ran while one was open for 0% of the time, Pallas kernels for 6%

profile of v12, /device:TPU:0, one launch (start us, length us, event | category | flops | bytes accessed | tf_op | source)
XLA Modules:
  0.0 45.7 jit_solution(17025448326662877312)
XLA Ops:
  0.0 2.5 %shard_map.55 = (bf16[64,512]{1,0:T(8,128)(2,1)S(1)}, bf16[8,2,512,128]{3,2,1,0:T(8,128)(2,1)S(1)}) custom-call(bf16[8,2,512,256]{3,2,1,0:T(8,128)(2,1)} %orb_hbm.3), custom_call_target="tpu_custom_call" | custom-call | bytes 4194304 | tf_op jit(solution)/shard_map/pallas_call | solution.py:365
  2.5 5.1 %collective-permute-start.5 = (bf16[64,512]{1,0:T(8,128)(2,1)S(1)}, bf16[64,512]{1,0:T(8,128)(2,1)S(1)}, u32[]{:S(2)}, u32[]{:S(2)}) collective-permute-start(bf16[64,512]{1,0:T(8,128)(2,1)S(1)} %get-tuple-element.25.edge_hbm.refs_0_), channel_id=1, source_target_pairs={{0,6},{1,7},{2,4},{3,5},{4,2},{5,3},{6,0},{7,1},{8,14},{9,15},{10,... | collective-permute-start | bytes 196616 | tf_op jit(solution)/shard_map/ppermute | solution.py:399
  7.7 0.6 %collective-permute-start.1 = (bf16[64,512]{1,0:T(8,128)(2,1)S(1)}, bf16[64,512]{1,0:T(8,128)(2,1)S(1)}, u32[]{:S(2)}, u32[]{:S(2)}) collective-permute-start(bf16[64,512]{1,0:T(8,128)(2,1)S(1)} %get-tuple-element.25.edge_hbm.refs_0_), channel_id=1, source_target_pairs={{0,2},{1,3},{2,0},{3,1},{4,6},{5,7},{6,4},{7,5},{8,10},{9,11},{10,... | collective-permute-start | bytes 196616 | tf_op jit(solution)/shard_map/ppermute | solution.py:399
  8.3 1.6 %shard_map.56 = (bf16[64,512]{1,0:T(8,128)(2,1)S(1)}, bf16[8,2,512,128]{3,2,1,0:T(8,128)(2,1)S(1)}) custom-call(bf16[8,2,512,256]{3,2,1,0:T(8,128)(2,1)} %orb_hbm.3, bf16[64,512]{1,0:T(8,128)(2,1)S(1)} %get-tuple-element.25.edge_hbm.refs_0_), custom_call_target="tpu_custom_call" | custom-call | bytes 4194304 | tf_op jit(solution)/shard_map/pallas_call | solution.py:377
  10.0 0.3 collective-permute-done.5.refs_6_
  10.2 0.2 collective-permute-start.6
  10.5 2.8 %collective-permute-done.3.refs_4_ = bf16[64,512]{1,0:T(8,128)(2,1)S(1)} collective-permute-done((bf16[64,512]{1,0:T(8,128)(2,1)S(1)}, bf16[64,512]{1,0:T(8,128)(2,1)S(1)}, u32[]{:S(2)}, u32[]{:S(2)}) %collective-permute-start.3) | collective-permute-done | bytes 65568 | tf_op jit(solution)/shard_map/ppermute | solution.py:399
  13.3 0.5 %collective-permute-start.2 = (bf16[64,512]{1,0:T(8,128)(2,1)S(1)}, bf16[64,512]{1,0:T(8,128)(2,1)S(1)}, u32[]{:S(2)}, u32[]{:S(2)}) collective-permute-start(bf16[64,512]{1,0:T(8,128)(2,1)S(1)} %collective-permute-done.1.refs_2_), channel_id=1, source_target_pairs={{0,1},{1,0},{2,3},{3,2},{4,5},{5,4},{6,7},{7,6},{8,9},{9,8},{10,11... | collective-permute-start | bytes 196616 | tf_op jit(solution)/shard_map/ppermute | solution.py:346
  13.8 0.7 %collective-permute-done.4.refs_5_ = bf16[64,512]{1,0:T(8,128)(2,1)S(1)} collective-permute-done((bf16[64,512]{1,0:T(8,128)(2,1)S(1)}, bf16[64,512]{1,0:T(8,128)(2,1)S(1)}, u32[]{:S(2)}, u32[]{:S(2)}) %collective-permute-start.4) | collective-permute-done | bytes 65568 | tf_op jit(solution)/shard_map/ppermute | solution.py:346
  14.5 0.2 collective-permute-done.2.refs_3_
  14.7 1.5 %shard_map.57 = (bf16[192,256]{1,0:T(8,128)(2,1)S(1)}, bf16[192,256]{1,0:T(8,128)(2,1)S(1)}, bf16[192,256]{1,0:T(8,128)(2,1)S(1)}, bf16[192,256]{1,0:T(8,128)(2,...) custom-call(bf16[64,512]{1,0:T(8,128)(2,1)S(1)} %get-tuple-element.2, ...), custom_call_target="tpu_custom_call" | custom-call | bytes 6291456 | tf_op jit(solution)/shard_map/pallas_call | solution.py:411
  16.2 2.5 %collective-permute-start.7 = (bf16[192,256]{1,0:T(8,128)(2,1)S(1)}, bf16[192,256]{1,0:T(8,128)(2,1)S(1)}, u32[]{:S(2)}, u32[]{:S(2)}) collective-permute-start(bf16[192,256]{1,0:T(8,128)(2,1)S(1)} %get-tuple-element.29), channel_id=1, source_target_pairs={{0,24},{8,16},{16,8},{24,0},{1,25},{9,17},{17,9},{25,1},{2,26},{10... | collective-permute-start | bytes 294920 | tf_op jit(solution)/shard_map/ppermute | solution.py:346
  18.7 0.5 %collective-permute-start.8 = (bf16[192,256]{1,0:T(8,128)(2,1)S(1)}, bf16[192,256]{1,0:T(8,128)(2,1)S(1)}, u32[]{:S(2)}, u32[]{:S(2)}) collective-permute-start(bf16[192,256]{1,0:T(8,128)(2,1)S(1)} %get-tuple-element.30), channel_id=1, source_target_pairs={{0,16},{8,24},{16,0},{24,8},{1,17},{9,25},{17,1},{25,9},{2,18},{10... | collective-permute-start | bytes 294920 | tf_op jit(solution)/shard_map/ppermute | solution.py:346
  19.2 0.5 %collective-permute-start.9 = (bf16[192,256]{1,0:T(8,128)(2,1)S(1)}, bf16[192,256]{1,0:T(8,128)(2,1)S(1)}, u32[]{:S(2)}, u32[]{:S(2)}) collective-permute-start(bf16[192,256]{1,0:T(8,128)(2,1)S(1)} %get-tuple-element.31), channel_id=1, source_target_pairs={{0,8},{8,0},{16,24},{24,16},{1,9},{9,1},{17,25},{25,17},{2,10},{10... | collective-permute-start | bytes 294920 | tf_op jit(solution)/shard_map/ppermute | solution.py:346
  19.7 2.5 %collective-permute-done.7.refs_0_ = bf16[192,256]{1,0:T(8,128)(2,1)S(1)} collective-permute-done((bf16[192,256]{1,0:T(8,128)(2,1)S(1)}, bf16[192,256]{1,0:T(8,128)(2,1)S(1)}, u32[]{:S(2)}, u32[]{:S(2)}) %collective-permute-start.7) | collective-permute-done | bytes 98336 | tf_op jit(solution)/shard_map/ppermute | solution.py:346
  22.3 2.0 %collective-permute-done.8.refs_1_ = bf16[192,256]{1,0:T(8,128)(2,1)S(1)} collective-permute-done((bf16[192,256]{1,0:T(8,128)(2,1)S(1)}, bf16[192,256]{1,0:T(8,128)(2,1)S(1)}, u32[]{:S(2)}, u32[]{:S(2)}) %collective-permute-start.8) | collective-permute-done | bytes 98336 | tf_op jit(solution)/shard_map/ppermute | solution.py:346
  24.4 0.6 %shard_map.58 = (bf16[128,256]{1,0:T(8,128)(2,1)S(1)}, bf16[128,256]{1,0:T(8,128)(2,1)S(1)}, bf16[128,256]{1,0:T(8,128)(2,1)S(1)}, bf16[128,256]{1,0:T(8,128)(2,1)S(1)}) custom-call(bf16[192,256]{1,0:T(8,128)(2,1)S(1)} %collective-permute-done.7.refs_0_, bf16[192,256]{1,0:T(8,128)(2,1)S(1)} %collective-permute-done.8.refs_1_, ...), custom_call_target="tpu_custom_call" | custom-call | bytes 2097152 | tf_op jit(solution)/shard_map/pallas_call | solution.py:429
  25.0 1.8 %collective-permute-start.10 = (bf16[128,256]{1,0:T(8,128)(2,1)S(1)}, bf16[128,256]{1,0:T(8,128)(2,1)S(1)}, u32[]{:S(2)}, u32[]{:S(2)}) collective-permute-start(bf16[128,256]{1,0:T(8,128)(2,1)S(1)} %get-tuple-element.33), channel_id=1, source_target_pairs={{0,24},{8,16},{16,8},{24,0},{1,25},{9,17},{17,9},{25,1},{2,26},{10... | collective-permute-start | bytes 196616 | tf_op jit(solution)/shard_map/ppermute | solution.py:346
  26.7 1.3 %collective-permute-start.11 = (bf16[128,256]{1,0:T(8,128)(2,1)S(1)}, bf16[128,256]{1,0:T(8,128)(2,1)S(1)}, u32[]{:S(2)}, u32[]{:S(2)}) collective-permute-start(bf16[128,256]{1,0:T(8,128)(2,1)S(1)} %get-tuple-element.34), channel_id=1, source_target_pairs={{0,16},{8,24},{16,0},{24,8},{1,17},{9,25},{17,1},{25,9},{2,18},{10... | collective-permute-start | bytes 196616 | tf_op jit(solution)/shard_map/ppermute | solution.py:346
  28.0 0.5 %collective-permute-start.12 = (bf16[128,256]{1,0:T(8,128)(2,1)S(1)}, bf16[128,256]{1,0:T(8,128)(2,1)S(1)}, u32[]{:S(2)}, u32[]{:S(2)}) collective-permute-start(bf16[128,256]{1,0:T(8,128)(2,1)S(1)} %get-tuple-element.35), channel_id=1, source_target_pairs={{0,8},{8,0},{16,24},{24,16},{1,9},{9,1},{17,25},{25,17},{2,10},{10... | collective-permute-start | bytes 196616 | tf_op jit(solution)/shard_map/ppermute | solution.py:346
  28.5 2.1 %collective-permute-done.10.refs_0_ = bf16[128,256]{1,0:T(8,128)(2,1)S(1)} collective-permute-done((bf16[128,256]{1,0:T(8,128)(2,1)S(1)}, bf16[128,256]{1,0:T(8,128)(2,1)S(1)}, u32[]{:S(2)}, u32[]{:S(2)}) %collective-permute-start.10) | collective-permute-done | bytes 65568 | tf_op jit(solution)/shard_map/ppermute | solution.py:346
  30.6 0.7 %collective-permute-done.11.refs_1_ = bf16[128,256]{1,0:T(8,128)(2,1)S(1)} collective-permute-done((bf16[128,256]{1,0:T(8,128)(2,1)S(1)}, bf16[128,256]{1,0:T(8,128)(2,1)S(1)}, u32[]{:S(2)}, u32[]{:S(2)}) %collective-permute-start.11) | collective-permute-done | bytes 65568 | tf_op jit(solution)/shard_map/ppermute | solution.py:346
  31.3 1.0 %collective-permute-done.12.refs_2_ = bf16[128,256]{1,0:T(8,128)(2,1)S(1)} collective-permute-done((bf16[128,256]{1,0:T(8,128)(2,1)S(1)}, bf16[128,256]{1,0:T(8,128)(2,1)S(1)}, u32[]{:S(2)}, u32[]{:S(2)}) %collective-permute-start.12) | collective-permute-done | bytes 65568 | tf_op jit(solution)/shard_map/ppermute | solution.py:346
  32.3 1.2 %shard_map.60 = bf16[4,64,512]{2,1,0:T(8,128)(2,1)S(1)} custom-call(bf16[128,256]{1,0:T(8,128)(2,1)S(1)} %collective-permute-done.10.refs_0_, bf16[128,256]{1,0:T(8,128)(2,1)S(1)} %collective-permute-done.11.refs_1_, bf16[128,256]{1,0:T(8,128)(2,1)S(1)} %collective-permute-done.12.refs_2_, bf16[128,256]{1,0:T(8,128)(2,1)S(1)} %get-tuple-element.36.refs_3_, ...), custom_call_target="tpu_custom_call" | custom-call | bytes 6291456 | tf_op jit(solution)/shard_map/pallas_call | solution.py:446
  33.5 0.1 collective-permute-start.13
  33.5 1.2 %shard_map.59.keep_ref = f32[4,64,512]{2,1,0:T(8,128)S(1)} custom-call(bf16[128,256]{1,0:T(8,128)(2,1)S(1)} %collective-permute-done.10.refs_0_, bf16[128,256]{1,0:T(8,128)(2,1)S(1)} %collective-permute-done.11.refs_1_, bf16[128,256]{1,0:T(8,128)(2,1)S(1)} %collective-permute-done.12.refs_2_, bf16[128,256]{1,0:T(8,128)(2,1)S(1)} %get-tuple-element.36.refs_3_, ...), custom_call_target="tpu_custom_call" | custom-call | bytes 6291456 | tf_op jit(solution)/shard_map/pallas_call | solution.py:446
  34.7 0.4 collective-permute-done.13.came_ref
  35.1 2.8 %collective-permute-start.14 = (bf16[64,512]{1,0:T(8,128)(2,1)S(1)}, bf16[64,512]{1,0:T(8,128)(2,1)S(1)}, u32[]{:S(2)}, u32[]{:S(2)}) collective-permute-start(bf16[64,512]{1,0:T(8,128)(2,1)S(1)} %get-tuple-element.37), channel_id=1, source_target_pairs={{0,6},{1,7},{2,4},{3,5},{4,2},{5,3},{6,0},{7,1},{8,14},{9,15},{10,... | collective-permute-start | bytes 196616 | tf_op jit(solution)/shard_map/ppermute | solution.py:346
  37.9 1.7 %collective-permute-start.16 = (bf16[64,512]{1,0:T(8,128)(2,1)S(1)}, bf16[64,512]{1,0:T(8,128)(2,1)S(1)}, u32[]{:S(2)}, u32[]{:S(2)}) collective-permute-start(bf16[64,512]{1,0:T(8,128)(2,1)S(1)} %get-tuple-element.39), channel_id=1, source_target_pairs={{0,2},{1,3},{2,0},{3,1},{4,6},{5,7},{6,4},{7,5},{8,10},{9,11},{10,... | collective-permute-start | bytes 196616 | tf_op jit(solution)/shard_map/ppermute | solution.py:346
  39.6 2.3 %collective-permute-done.14.refs_0_ = bf16[64,512]{1,0:T(8,128)(2,1)S(1)} collective-permute-done((bf16[64,512]{1,0:T(8,128)(2,1)S(1)}, bf16[64,512]{1,0:T(8,128)(2,1)S(1)}, u32[]{:S(2)}, u32[]{:S(2)}) %collective-permute-start.14) | collective-permute-done | bytes 65568 | tf_op jit(solution)/shard_map/ppermute | solution.py:346
  41.9 2.0 %collective-permute-done.15.refs_1_ = bf16[64,512]{1,0:T(8,128)(2,1)S(1)} collective-permute-done((bf16[64,512]{1,0:T(8,128)(2,1)S(1)}, bf16[64,512]{1,0:T(8,128)(2,1)S(1)}, u32[]{:S(2)}, u32[]{:S(2)}) %collective-permute-start.15) | collective-permute-done | bytes 65568 | tf_op jit(solution)/shard_map/ppermute | solution.py:346
  44.0 1.8 %shard_map.62 = bf16[64,4,16,128]{3,2,1,0:T(8,128)(2,1)} custom-call(bf16[64,512]{1,0:T(8,128)(2,1)S(1)} %collective-permute-done.14.refs_0_, bf16[64,512]{1,0:T(8,128)(2,1)S(1)} %collective-permute-done.15.refs_1_, bf16[64,512]{1,0:T(8,128)(2,1)S(1)} %collective-permute-done.16.refs_2_, f32[64,512]{1,0:T(8,128)S(1)} %get-tuple-element.40.refs_3_, ...), custom_call_target="tpu_custom_call" | custom-call | bytes 4194304 | tf_op jit(solution)/shard_map/pallas_call | solution.py:465
  (18 shorter events, 0.2 us)
Async XLA Ops:
  2.5 12.2 %copy-start = (bf16[8,32,256]{2,1,0:T(8,128)(2,1)S(1)}, bf16[8,32,256]{2,1,0:T(8,128)(2,1)}, u32[]{:S(2)}) copy-start(bf16[8,32,256]{2,1,0:T(8,128)(2,1)} %refs_11_.1) | copy-start | bytes 393220
  2.5 12.2 %copy-start.1 = (bf16[64,32]{1,0:T(8,128)(2,1)S(1)}, bf16[64,32]{1,0:T(8,128)(2,1)}, u32[]{:S(2)}) copy-start(bf16[64,32]{1,0:T(8,128)(2,1)} %constant.6.clone.refs_10_) | copy-start | bytes 12292
  2.5 7.7 %collective-permute-start.5 = (bf16[64,512]{1,0:T(8,128)(2,1)S(1)}, bf16[64,512]{1,0:T(8,128)(2,1)S(1)}, u32[]{:S(2)}, u32[]{:S(2)}) collective-permute-start(bf16[64,512]{1,0:T(8,128)(2,1)S(1)} %get-tuple-element.25.edge_hbm.refs_0_), channel_id=1, source_target_pairs={{0,6},{1,7},{2,4},{3,5},{4,2},{5,3},{6,0},{7,1},{8,14},{9,15},{10,... | collective-permute-start | bytes 196616 | tf_op jit(solution)/shard_map/ppermute | solution.py:399
  7.6 5.6 %collective-permute-start.3 = (bf16[64,512]{1,0:T(8,128)(2,1)S(1)}, bf16[64,512]{1,0:T(8,128)(2,1)S(1)}, u32[]{:S(2)}, u32[]{:S(2)}) collective-permute-start(bf16[64,512]{1,0:T(8,128)(2,1)S(1)} %get-tuple-element.25.edge_hbm.refs_0_), channel_id=1, source_target_pairs={{0,4},{1,5},{2,6},{3,7},{4,0},{5,1},{6,2},{7,3},{8,12},{9,13},{10,... | collective-permute-start | bytes 196616 | tf_op jit(solution)/shard_map/ppermute | solution.py:399
  7.7 5.6 %collective-permute-start.1 = (bf16[64,512]{1,0:T(8,128)(2,1)S(1)}, bf16[64,512]{1,0:T(8,128)(2,1)S(1)}, u32[]{:S(2)}, u32[]{:S(2)}) collective-permute-start(bf16[64,512]{1,0:T(8,128)(2,1)S(1)} %get-tuple-element.25.edge_hbm.refs_0_), channel_id=1, source_target_pairs={{0,2},{1,3},{2,0},{3,1},{4,6},{5,7},{6,4},{7,5},{8,10},{9,11},{10,... | collective-permute-start | bytes 196616 | tf_op jit(solution)/shard_map/ppermute | solution.py:399
  9.9 3.9 %collective-permute-start = (bf16[64,512]{1,0:T(8,128)(2,1)S(1)}, bf16[64,512]{1,0:T(8,128)(2,1)S(1)}, u32[]{:S(2)}, u32[]{:S(2)}) collective-permute-start(bf16[64,512]{1,0:T(8,128)(2,1)S(1)} %get-tuple-element.26), channel_id=1, source_target_pairs={{0,1},{1,0},{2,3},{3,2},{4,5},{5,4},{6,7},{7,6},{8,9},{9,8},{10,11... | collective-permute-start | bytes 196616 | tf_op jit(solution)/shard_map/ppermute | solution.py:346
  10.2 3.5 %collective-permute-start.6 = (bf16[64,512]{1,0:T(8,128)(2,1)S(1)}, bf16[64,512]{1,0:T(8,128)(2,1)S(1)}, u32[]{:S(2)}, u32[]{:S(2)}) collective-permute-start(bf16[64,512]{1,0:T(8,128)(2,1)S(1)} %collective-permute-done.5.refs_6_), channel_id=1, source_target_pairs={{0,1},{1,0},{2,3},{3,2},{4,5},{5,4},{6,7},{7,6},{8,9},{9,8},{10,11... | collective-permute-start | bytes 196616 | tf_op jit(solution)/shard_map/ppermute | solution.py:346
  13.3 1.3 %collective-permute-start.4 = (bf16[64,512]{1,0:T(8,128)(2,1)S(1)}, bf16[64,512]{1,0:T(8,128)(2,1)S(1)}, u32[]{:S(2)}, u32[]{:S(2)}) collective-permute-start(bf16[64,512]{1,0:T(8,128)(2,1)S(1)} %collective-permute-done.3.refs_4_), channel_id=1, source_target_pairs={{0,1},{1,0},{2,3},{3,2},{4,5},{5,4},{6,7},{7,6},{8,9},{9,8},{10,11... | collective-permute-start | bytes 196616 | tf_op jit(solution)/shard_map/ppermute | solution.py:346
  13.3 1.4 %collective-permute-start.2 = (bf16[64,512]{1,0:T(8,128)(2,1)S(1)}, bf16[64,512]{1,0:T(8,128)(2,1)S(1)}, u32[]{:S(2)}, u32[]{:S(2)}) collective-permute-start(bf16[64,512]{1,0:T(8,128)(2,1)S(1)} %collective-permute-done.1.refs_2_), channel_id=1, source_target_pairs={{0,1},{1,0},{2,3},{3,2},{4,5},{5,4},{6,7},{7,6},{8,9},{9,8},{10,11... | collective-permute-start | bytes 196616 | tf_op jit(solution)/shard_map/ppermute | solution.py:346
  14.7 9.7 %copy-start.2 = (bf16[64,128]{1,0:T(8,128)(2,1)S(1)}, bf16[64,128]{1,0:T(8,128)(2,1)}, u32[]{:S(2)}) copy-start(bf16[64,128]{1,0:T(8,128)(2,1)} %constant.8.clone.refs_5_) | copy-start | bytes 49156
  14.7 9.7 %copy-start.3 = (bf16[64,128]{1,0:T(8,128)(2,1)S(1)}, bf16[64,128]{1,0:T(8,128)(2,1)}, u32[]{:S(2)}) copy-start(bf16[64,128]{1,0:T(8,128)(2,1)} %constant.7.clone.refs_4_) | copy-start | bytes 49156
  16.2 6.1 %collective-permute-start.7 = (bf16[192,256]{1,0:T(8,128)(2,1)S(1)}, bf16[192,256]{1,0:T(8,128)(2,1)S(1)}, u32[]{:S(2)}, u32[]{:S(2)}) collective-permute-start(bf16[192,256]{1,0:T(8,128)(2,1)S(1)} %get-tuple-element.29), channel_id=1, source_target_pairs={{0,24},{8,16},{16,8},{24,0},{1,25},{9,17},{17,9},{25,1},{2,26},{10... | collective-permute-start | bytes 294920 | tf_op jit(solution)/shard_map/ppermute | solution.py:346
  18.7 5.6 %collective-permute-start.8 = (bf16[192,256]{1,0:T(8,128)(2,1)S(1)}, bf16[192,256]{1,0:T(8,128)(2,1)S(1)}, u32[]{:S(2)}, u32[]{:S(2)}) collective-permute-start(bf16[192,256]{1,0:T(8,128)(2,1)S(1)} %get-tuple-element.30), channel_id=1, source_target_pairs={{0,16},{8,24},{16,0},{24,8},{1,17},{9,25},{17,1},{25,9},{2,18},{10... | collective-permute-start | bytes 294920 | tf_op jit(solution)/shard_map/ppermute | solution.py:346
  19.2 5.2 %collective-permute-start.9 = (bf16[192,256]{1,0:T(8,128)(2,1)S(1)}, bf16[192,256]{1,0:T(8,128)(2,1)S(1)}, u32[]{:S(2)}, u32[]{:S(2)}) collective-permute-start(bf16[192,256]{1,0:T(8,128)(2,1)S(1)} %get-tuple-element.31), channel_id=1, source_target_pairs={{0,8},{8,0},{16,24},{24,16},{1,9},{9,1},{17,25},{25,17},{2,10},{10... | collective-permute-start | bytes 294920 | tf_op jit(solution)/shard_map/ppermute | solution.py:346
  25.0 5.7 %collective-permute-start.10 = (bf16[128,256]{1,0:T(8,128)(2,1)S(1)}, bf16[128,256]{1,0:T(8,128)(2,1)S(1)}, u32[]{:S(2)}, u32[]{:S(2)}) collective-permute-start(bf16[128,256]{1,0:T(8,128)(2,1)S(1)} %get-tuple-element.33), channel_id=1, source_target_pairs={{0,24},{8,16},{16,8},{24,0},{1,25},{9,17},{17,9},{25,1},{2,26},{10... | collective-permute-start | bytes 196616 | tf_op jit(solution)/shard_map/ppermute | solution.py:346
  26.7 4.6 %collective-permute-start.11 = (bf16[128,256]{1,0:T(8,128)(2,1)S(1)}, bf16[128,256]{1,0:T(8,128)(2,1)S(1)}, u32[]{:S(2)}, u32[]{:S(2)}) collective-permute-start(bf16[128,256]{1,0:T(8,128)(2,1)S(1)} %get-tuple-element.34), channel_id=1, source_target_pairs={{0,16},{8,24},{16,0},{24,8},{1,17},{9,25},{17,1},{25,9},{2,18},{10... | collective-permute-start | bytes 196616 | tf_op jit(solution)/shard_map/ppermute | solution.py:346
  28.0 4.3 %collective-permute-start.12 = (bf16[128,256]{1,0:T(8,128)(2,1)S(1)}, bf16[128,256]{1,0:T(8,128)(2,1)S(1)}, u32[]{:S(2)}, u32[]{:S(2)}) collective-permute-start(bf16[128,256]{1,0:T(8,128)(2,1)S(1)} %get-tuple-element.35), channel_id=1, source_target_pairs={{0,8},{8,0},{16,24},{24,16},{1,9},{9,1},{17,25},{25,17},{2,10},{10... | collective-permute-start | bytes 196616 | tf_op jit(solution)/shard_map/ppermute | solution.py:346
  33.5 1.6 %collective-permute-start.13 = (bf16[4,64,512]{2,1,0:T(8,128)(2,1)S(1)}, bf16[4,64,512]{2,1,0:T(8,128)(2,1)S(1)}, u32[]{:S(2)}, u32[]{:S(2)}) collective-permute-start(bf16[4,64,512]{2,1,0:T(8,128)(2,1)S(1)} %shard_map.60), channel_id=1, source_target_pairs={{0,1},{1,0},{2,3},{3,2},{4,5},{5,4},{6,7},{7,6},{8,9},{9,8},{10,11... | collective-permute-start | bytes 786440 | tf_op jit(solution)/shard_map/ppermute | solution.py:346
  35.1 6.8 %collective-permute-start.14 = (bf16[64,512]{1,0:T(8,128)(2,1)S(1)}, bf16[64,512]{1,0:T(8,128)(2,1)S(1)}, u32[]{:S(2)}, u32[]{:S(2)}) collective-permute-start(bf16[64,512]{1,0:T(8,128)(2,1)S(1)} %get-tuple-element.37), channel_id=1, source_target_pairs={{0,6},{1,7},{2,4},{3,5},{4,2},{5,3},{6,0},{7,1},{8,14},{9,15},{10,... | collective-permute-start | bytes 196616 | tf_op jit(solution)/shard_map/ppermute | solution.py:346
  37.9 6.0 %collective-permute-start.15 = (bf16[64,512]{1,0:T(8,128)(2,1)S(1)}, bf16[64,512]{1,0:T(8,128)(2,1)S(1)}, u32[]{:S(2)}, u32[]{:S(2)}) collective-permute-start(bf16[64,512]{1,0:T(8,128)(2,1)S(1)} %get-tuple-element.38), channel_id=1, source_target_pairs={{0,4},{1,5},{2,6},{3,7},{4,0},{5,1},{6,2},{7,3},{8,12},{9,13},{10,... | collective-permute-start | bytes 196616 | tf_op jit(solution)/shard_map/ppermute | solution.py:346
  37.9 6.0 %collective-permute-start.16 = (bf16[64,512]{1,0:T(8,128)(2,1)S(1)}, bf16[64,512]{1,0:T(8,128)(2,1)S(1)}, u32[]{:S(2)}, u32[]{:S(2)}) collective-permute-start(bf16[64,512]{1,0:T(8,128)(2,1)S(1)} %get-tuple-element.39), channel_id=1, source_target_pairs={{0,2},{1,3},{2,0},{3,1},{4,6},{5,7},{6,4},{7,5},{8,10},{9,11},{10,... | collective-permute-start | bytes 196616 | tf_op jit(solution)/shard_map/ppermute | solution.py:346

commit v13 on v11

--- a/solution.py
+++ b/solution.py
@@ -131,6 +131,14 @@
     return [list(reversed(range(shares)))]
 
 
+def crossed(s):
+    return (s & ~3) | ((s & 1) << 1) | ((s >> 1) & 1)
+
+
+def turn(s):
+    return jnp.where(jnp.bitwise_and(lax.axis_index("pts"), 1) == 0, jnp.int32(s), jnp.int32(crossed(s)))
+
+
 def plane_of(shares):
     return lax.div(lax.axis_index("pts"), lax.axis_size("pts") // shares)
 
@@ -151,7 +159,7 @@
         here = 0 if t is None else pick([order[a][t] for a in range(shares)], me)
         for slot, j in enumerate(targets):
 
-            @pl.when(jnp.bitwise_xor(me, j) == here)
+            @pl.when(jnp.bitwise_xor(me, turn(j)) == here)
             def _(i=i, slot=slot):
                 for e in range(per_share):
                     place = jnp.bitwise_xor(jnp.bitwise_and(block, per_share - 1), e)
@@ -182,7 +190,7 @@
     cells[...] = coulomb_ref[...].astype(F32)
     for slot, j in enumerate(targets):
         outs[slot][:size] = take(wide, slot * size, size).astype(BF16)
-        owned = jnp.bitwise_xor(jnp.bitwise_xor(me, j), plane_of(shares))
+        owned = jnp.bitwise_xor(jnp.bitwise_xor(me, turn(j)), plane_of(shares))
         start = pl.multiple_of(owned * share, share)
         pieces = [cells[r, pl.ds(start, share), :] for r in range(local_k)]
         outs[slot][size:] = jnp.concatenate(pieces, axis=0).astype(BF16)
@@ -195,7 +203,7 @@
     size = 2 * local_k * share
     me = lax.axis_index("ka")
     for s in range(shares):
-        src = jnp.bitwise_xor(me, s)
+        src = jnp.bitwise_xor(me, turn(s))
         gathered[src] = tiles[s][:size].astype(gathered.dtype)
         cells = tiles[s][size:].astype(F32)
         for r in range(local_k):
@@ -215,7 +223,7 @@
     for c in range(share):
         spread(wide, c, share, kernel[:, c * points : (c + 1) * points])
     for s in range(shares):
-        dest = jnp.bitwise_xor(me, s)
+        dest = jnp.bitwise_xor(me, turn(s))
         outs[s][...] = take(wide, pl.multiple_of(dest * size, size), size).astype(BF16)
 
 
@@ -228,7 +236,7 @@
     core = jnp.bitwise_xor(jnp.bitwise_and(lax.axis_index("pts"), 1), flip)
     plane = plane_of(shares)
     for s in range(shares):
-        gathered[jnp.bitwise_xor(jnp.bitwise_xor(me, s), plane)] = pieces[s][...]
+        gathered[jnp.bitwise_xor(jnp.bitwise_xor(me, turn(s)), plane)] = pieces[s][...]
     lanes = 2 * half * shares
     group = max(1, LANES // lanes)
     chunks = norb // out_rows // 2
@@ -275,7 +283,7 @@
     wide, out_ref, form_ref, sems = refs[chunks + shares + 1 :]
     owner = jnp.bitwise_xor(lax.axis_index("ka"), plane_of(shares))
     for j in range(shares):
-        form_ref[jnp.bitwise_xor(owner, j)] = form_refs[j][...]
+        form_ref[jnp.bitwise_xor(owner, turn(j))] = form_refs[j][...]
     _, local_k, part_lanes, twice = form_ref.shape
     lanes = shares * part_lanes
     norb = twice // 2
@@ -322,8 +330,21 @@
     return lax.ppermute(value, axis, [(i, i ^ mask) for i in range(size)])
 
 
-def trade(pieces, axis, step):
-    return [swap(pieces[s], axis, s * step) for s in reversed(range(1, len(pieces)))] + [pieces[0]]
+def trade(pieces):
+    shares, blocks = lax.axis_size("ka"), lax.axis_size("pts")
+    came = []
+    for s in reversed(range(1, shares)):
+        pairs = [
+            (a * blocks + i, (a ^ (crossed(s) if i & 1 else s)) * blocks + i)
+            for a in range(shares)
+            for i in range(blocks)
+        ]
+        came.append(lax.ppermute(pieces[s], ("ka", "pts"), pairs))
+    return came + [pieces[0]]
+
+
+def trade_sums(pieces):
+    return [swap(pieces[s], "pts", 2 * s) for s in reversed(range(1, len(pieces)))] + [pieces[0]]
 
 
 def body(orbitals, coulomb):
@@ -387,7 +408,7 @@
         for slot, j in enumerate(targets):
             tiles[j], forms[j] = result[slot], result[many + slot]
         before = [forms[targets[0]]]
-    tiles = trade(tiles, "ka", 1)
+    tiles = trade(tiles)
 
     forward, backward = phase_tables(total)
     kernels = call(
@@ -401,7 +422,7 @@
         ],
         size=2 * MIB,
     )(*tiles, jnp.asarray(forward), jnp.asarray(backward))
-    kernels = trade(kernels, "ka", 1)
+    kernels = trade(kernels)
 
     lanes = local_k * 2 * columns
     halves = []
@@ -422,7 +443,7 @@
         2,
         size=1 * MIB,
     )(halves[1], came)
-    sums = trade([own_sum, *sums], "pts", 2)
+    sums = trade_sums([own_sum, *sums])
     spans = norb // LANES
     pair = max(1, LANES // (2 * columns))
     rows = pair * spans * 2

time: 46 us -> 45.9 us (level)
    ppermute x14 -> x8, waiting for transfers between devices: 14.1 us -> 5.64 us  [swap(): return lax.ppermute(value, axis, [(i, i ^ mask) for i in range(size)])]
    ppermute x0 -> x6, waiting for transfers between devices: none -> 8.37 us  [trade(): came.append(lax.ppermute(pieces[s], ('ka', 'pts'), pairs))]
    ppermute x0 -> x6, starting transfers between devices: none -> 7.11 us  [trade(): came.append(lax.ppermute(pieces[s], ('ka', 'pts'), pairs))]
    ppermute x14 -> x8, starting transfers between devices: 12.1 us -> 5.04 us  [swap(): return lax.ppermute(value, axis, [(i, i ^ mask) for i in range(size)])]
where the time goes in v13:
time: 45.9 us; the launch traced here: 45.8 us
  waiting for transfers between devices  19 us (41%)
  starting transfers between devices  17.9 us (39%)
  Pallas kernels  8.81 us (19%)
    ppermute x6, waiting for transfers between devices, trade(): came.append(lax.ppermute(pieces[s], ('ka', 'pts'), pairs))  8.37 us
    ppermute x6, starting transfers between devices, trade(): came.append(lax.ppermute(pieces[s], ('ka', 'pts'), pairs))  7.11 us
    ppermute x3, starting transfers between devices, body(): block = lax.ppermute(edge, ('ka', 'pts'), pairs)  5.79 us
    ppermute x8, waiting for transfers between devices, swap(): return lax.ppermute(value, axis, [(i, i ^ mask) for i in range(size)])  5.64 us
    ppermute x8, starting transfers between devices, swap(): return lax.ppermute(value, axis, [(i, i ^ mask) for i in range(size)])  5.04 us
    ppermute x3, waiting for transfers between devices, body(): block = lax.ppermute(edge, ('ka', 'pts'), pairs)  4.96 us
    pallas_call x1, Pallas kernels, body(): call(functools.partial(edge_kernel, per_block), [shape((local_k * 2 * per...  2.63 us
    pallas_call x2, Pallas kernels, body(): call(functools.partial(weight_kernel, shares, flip, out_rows), shape((chu...  2.33 us
  transfers between devices with their start and end apart: 17, of which 13 were waited for; matrix products, arithmetic and copies ran while one was open for 0% of the time, Pallas kernels for 3%

profile of v13, /device:TPU:0, one launch (start us, length us, event | category | flops | bytes accessed | tf_op | source)
XLA Modules:
  0.0 45.8 jit_solution(4914902787003879231)
XLA Ops:
  0.0 2.6 %shard_map.55 = (bf16[64,512]{1,0:T(8,128)(2,1)S(1)}, bf16[8,2,512,256]{3,2,1,0:T(8,128)(2,1)S(1)}) custom-call(bf16[8,2,512,256]{3,2,1,0:T(8,128)(2,1)} %orb_hbm.1), custom_call_target="tpu_custom_call" | custom-call | bytes 8388608 | tf_op jit(solution)/shard_map/pallas_call | solution.py:362
  2.6 5.1 %collective-permute-start.5 = (bf16[64,512]{1,0:T(8,128)(2,1)S(1)}, bf16[64,512]{1,0:T(8,128)(2,1)S(1)}, u32[]{:S(2)}, u32[]{:S(2)}) collective-permute-start(bf16[64,512]{1,0:T(8,128)(2,1)S(1)} %get-tuple-element.23.refs_0_), channel_id=1, source_target_pairs={{0,6},{1,7},{2,4},{3,5},{4,2},{5,3},{6,0},{7,1},{8,14},{9,15},{10,... | collective-permute-start | bytes 196616 | tf_op jit(solution)/shard_map/ppermute | solution.py:384
  7.8 0.0 collective-permute-start.3
  7.8 0.6 %collective-permute-start.1 = (bf16[64,512]{1,0:T(8,128)(2,1)S(1)}, bf16[64,512]{1,0:T(8,128)(2,1)S(1)}, u32[]{:S(2)}, u32[]{:S(2)}) collective-permute-start(bf16[64,512]{1,0:T(8,128)(2,1)S(1)} %get-tuple-element.23.refs_0_), channel_id=1, source_target_pairs={{0,2},{1,3},{2,0},{3,1},{4,6},{5,7},{6,4},{7,5},{8,10},{9,11},{10,... | collective-permute-start | bytes 196616 | tf_op jit(solution)/shard_map/ppermute | solution.py:384
  8.4 1.9 %collective-permute-done.5.refs_6_ = bf16[64,512]{1,0:T(8,128)(2,1)S(1)} collective-permute-done((bf16[64,512]{1,0:T(8,128)(2,1)S(1)}, bf16[64,512]{1,0:T(8,128)(2,1)S(1)}, u32[]{:S(2)}, u32[]{:S(2)}) %collective-permute-start.5) | collective-permute-done | bytes 65568 | tf_op jit(solution)/shard_map/ppermute | solution.py:384
  10.4 3.0 %collective-permute-done.3.refs_4_ = bf16[64,512]{1,0:T(8,128)(2,1)S(1)} collective-permute-done((bf16[64,512]{1,0:T(8,128)(2,1)S(1)}, bf16[64,512]{1,0:T(8,128)(2,1)S(1)}, u32[]{:S(2)}, u32[]{:S(2)}) %collective-permute-start.3) | collective-permute-done | bytes 65568 | tf_op jit(solution)/shard_map/ppermute | solution.py:384
  13.4 0.5 %collective-permute-start.2 = (bf16[64,512]{1,0:T(8,128)(2,1)S(1)}, bf16[64,512]{1,0:T(8,128)(2,1)S(1)}, u32[]{:S(2)}, u32[]{:S(2)}) collective-permute-start(bf16[64,512]{1,0:T(8,128)(2,1)S(1)} %collective-permute-done.1.refs_2_), channel_id=1, source_target_pairs={{0,1},{1,0},{2,3},{3,2},{4,5},{5,4},{6,7},{7,6},{8,9},{9,8},{10,11... | collective-permute-start | bytes 196616 | tf_op jit(solution)/shard_map/ppermute | solution.py:330
  13.9 0.7 %collective-permute-done.4.refs_5_ = bf16[64,512]{1,0:T(8,128)(2,1)S(1)} collective-permute-done((bf16[64,512]{1,0:T(8,128)(2,1)S(1)}, bf16[64,512]{1,0:T(8,128)(2,1)S(1)}, u32[]{:S(2)}, u32[]{:S(2)}) %collective-permute-start.4) | collective-permute-done | bytes 65568 | tf_op jit(solution)/shard_map/ppermute | solution.py:330
  14.6 0.2 collective-permute-done.2.refs_3_
  14.8 1.5 %shard_map.56 = (bf16[192,256]{1,0:T(8,128)(2,1)S(1)}, bf16[192,256]{1,0:T(8,128)(2,1)S(1)}, bf16[192,256]{1,0:T(8,128)(2,1)S(1)}, bf16[192,256]{1,0:T(8,128)(2,...) custom-call(bf16[64,512]{1,0:T(8,128)(2,1)S(1)} %get-tuple-element.2, ...), custom_call_target="tpu_custom_call" | custom-call | bytes 6291456 | tf_op jit(solution)/shard_map/pallas_call | solution.py:396
  16.3 2.5 %collective-permute-start.7 = (bf16[192,256]{1,0:T(8,128)(2,1)S(1)}, bf16[192,256]{1,0:T(8,128)(2,1)S(1)}, u32[]{:S(2)}, u32[]{:S(2)}) collective-permute-start(bf16[192,256]{1,0:T(8,128)(2,1)S(1)} %get-tuple-element.25), channel_id=1, source_target_pairs={{0,24},{1,25},{2,26},{3,27},{4,28},{5,29},{6,30},{7,31},{8,16},{9,... | collective-permute-start | bytes 294920 | tf_op jit(solution)/shard_map/ppermute | solution.py:342
  18.8 0.5 %collective-permute-start.8 = (bf16[192,256]{1,0:T(8,128)(2,1)S(1)}, bf16[192,256]{1,0:T(8,128)(2,1)S(1)}, u32[]{:S(2)}, u32[]{:S(2)}) collective-permute-start(bf16[192,256]{1,0:T(8,128)(2,1)S(1)} %get-tuple-element.26), channel_id=1, source_target_pairs={{0,16},{1,9},{2,18},{3,11},{4,20},{5,13},{6,22},{7,15},{8,24},{9,1... | collective-permute-start | bytes 294920 | tf_op jit(solution)/shard_map/ppermute | solution.py:342
  19.3 0.5 %collective-permute-start.9 = (bf16[192,256]{1,0:T(8,128)(2,1)S(1)}, bf16[192,256]{1,0:T(8,128)(2,1)S(1)}, u32[]{:S(2)}, u32[]{:S(2)}) collective-permute-start(bf16[192,256]{1,0:T(8,128)(2,1)S(1)} %get-tuple-element.27), channel_id=1, source_target_pairs={{0,8},{1,17},{2,10},{3,19},{4,12},{5,21},{6,14},{7,23},{8,0},{9,25... | collective-permute-start | bytes 294920 | tf_op jit(solution)/shard_map/ppermute | solution.py:342
  19.8 3.0 %collective-permute-done.7.refs_0_ = bf16[192,256]{1,0:T(8,128)(2,1)S(1)} collective-permute-done((bf16[192,256]{1,0:T(8,128)(2,1)S(1)}, bf16[192,256]{1,0:T(8,128)(2,1)S(1)}, u32[]{:S(2)}, u32[]{:S(2)}) %collective-permute-start.7) | collective-permute-done | bytes 98336 | tf_op jit(solution)/shard_map/ppermute | solution.py:342
  22.9 1.6 %collective-permute-done.8.refs_1_ = bf16[192,256]{1,0:T(8,128)(2,1)S(1)} collective-permute-done((bf16[192,256]{1,0:T(8,128)(2,1)S(1)}, bf16[192,256]{1,0:T(8,128)(2,1)S(1)}, u32[]{:S(2)}, u32[]{:S(2)}) %collective-permute-start.8) | collective-permute-done | bytes 98336 | tf_op jit(solution)/shard_map/ppermute | solution.py:342
  24.4 0.1 collective-permute-done.9.refs_2_
  24.5 0.6 %shard_map.57 = (bf16[128,256]{1,0:T(8,128)(2,1)S(1)}, bf16[128,256]{1,0:T(8,128)(2,1)S(1)}, bf16[128,256]{1,0:T(8,128)(2,1)S(1)}, bf16[128,256]{1,0:T(8,128)(2,1)S(1)}) custom-call(bf16[192,256]{1,0:T(8,128)(2,1)S(1)} %collective-permute-done.7.refs_0_, bf16[192,256]{1,0:T(8,128)(2,1)S(1)} %collective-permute-done.8.refs_1_, ...), custom_call_target="tpu_custom_call" | custom-call | bytes 2097152 | tf_op jit(solution)/shard_map/pallas_call | solution.py:414
  25.1 2.5 %collective-permute-start.10 = (bf16[128,256]{1,0:T(8,128)(2,1)S(1)}, bf16[128,256]{1,0:T(8,128)(2,1)S(1)}, u32[]{:S(2)}, u32[]{:S(2)}) collective-permute-start(bf16[128,256]{1,0:T(8,128)(2,1)S(1)} %get-tuple-element.29), channel_id=1, source_target_pairs={{0,24},{1,25},{2,26},{3,27},{4,28},{5,29},{6,30},{7,31},{8,16},{9,... | collective-permute-start | bytes 196616 | tf_op jit(solution)/shard_map/ppermute | solution.py:342
  27.5 0.6 %collective-permute-start.11 = (bf16[128,256]{1,0:T(8,128)(2,1)S(1)}, bf16[128,256]{1,0:T(8,128)(2,1)S(1)}, u32[]{:S(2)}, u32[]{:S(2)}) collective-permute-start(bf16[128,256]{1,0:T(8,128)(2,1)S(1)} %get-tuple-element.30), channel_id=1, source_target_pairs={{0,16},{1,9},{2,18},{3,11},{4,20},{5,13},{6,22},{7,15},{8,24},{9,1... | collective-permute-start | bytes 196616 | tf_op jit(solution)/shard_map/ppermute | solution.py:342
  28.1 0.5 %collective-permute-start.12 = (bf16[128,256]{1,0:T(8,128)(2,1)S(1)}, bf16[128,256]{1,0:T(8,128)(2,1)S(1)}, u32[]{:S(2)}, u32[]{:S(2)}) collective-permute-start(bf16[128,256]{1,0:T(8,128)(2,1)S(1)} %get-tuple-element.31), channel_id=1, source_target_pairs={{0,8},{1,17},{2,10},{3,19},{4,12},{5,21},{6,14},{7,23},{8,0},{9,25... | collective-permute-start | bytes 196616 | tf_op jit(solution)/shard_map/ppermute | solution.py:342
  28.6 2.1 %collective-permute-done.10.refs_0_ = bf16[128,256]{1,0:T(8,128)(2,1)S(1)} collective-permute-done((bf16[128,256]{1,0:T(8,128)(2,1)S(1)}, bf16[128,256]{1,0:T(8,128)(2,1)S(1)}, u32[]{:S(2)}, u32[]{:S(2)}) %collective-permute-start.10) | collective-permute-done | bytes 65568 | tf_op jit(solution)/shard_map/ppermute | solution.py:342
  30.7 1.1 %collective-permute-done.11.refs_1_ = bf16[128,256]{1,0:T(8,128)(2,1)S(1)} collective-permute-done((bf16[128,256]{1,0:T(8,128)(2,1)S(1)}, bf16[128,256]{1,0:T(8,128)(2,1)S(1)}, u32[]{:S(2)}, u32[]{:S(2)}) %collective-permute-start.11) | collective-permute-done | bytes 65568 | tf_op jit(solution)/shard_map/ppermute | solution.py:342
  31.8 0.5 %collective-permute-done.12.refs_2_ = bf16[128,256]{1,0:T(8,128)(2,1)S(1)} collective-permute-done((bf16[128,256]{1,0:T(8,128)(2,1)S(1)}, bf16[128,256]{1,0:T(8,128)(2,1)S(1)}, u32[]{:S(2)}, u32[]{:S(2)}) %collective-permute-start.12) | collective-permute-done | bytes 65568 | tf_op jit(solution)/shard_map/ppermute | solution.py:342
  32.4 1.2 %shard_map.59 = bf16[4,64,512]{2,1,0:T(8,128)(2,1)S(1)} custom-call(bf16[128,256]{1,0:T(8,128)(2,1)S(1)} %collective-permute-done.10.refs_0_, bf16[128,256]{1,0:T(8,128)(2,1)S(1)} %collective-permute-done.11.refs_1_, bf16[128,256]{1,0:T(8,128)(2,1)S(1)} %collective-permute-done.12.refs_2_, bf16[128,256]{1,0:T(8,128)(2,1)S(1)} %get-tuple-element.32.refs_3_, ...), custom_call_target="tpu_custom_call" | custom-call | bytes 6291456 | tf_op jit(solution)/shard_map/pallas_call | solution.py:431
  33.5 0.1 collective-permute-start.13
  33.6 1.2 %shard_map.58.keep_ref = f32[4,64,512]{2,1,0:T(8,128)S(1)} custom-call(bf16[128,256]{1,0:T(8,128)(2,1)S(1)} %collective-permute-done.10.refs_0_, bf16[128,256]{1,0:T(8,128)(2,1)S(1)} %collective-permute-done.11.refs_1_, bf16[128,256]{1,0:T(8,128)(2,1)S(1)} %collective-permute-done.12.refs_2_, bf16[128,256]{1,0:T(8,128)(2,1)S(1)} %get-tuple-element.32.refs_3_, ...), custom_call_target="tpu_custom_call" | custom-call | bytes 6291456 | tf_op jit(solution)/shard_map/pallas_call | solution.py:431
  34.8 0.4 collective-permute-done.13.came_ref
  35.2 2.8 %collective-permute-start.14 = (bf16[64,512]{1,0:T(8,128)(2,1)S(1)}, bf16[64,512]{1,0:T(8,128)(2,1)S(1)}, u32[]{:S(2)}, u32[]{:S(2)}) collective-permute-start(bf16[64,512]{1,0:T(8,128)(2,1)S(1)} %get-tuple-element.33), channel_id=1, source_target_pairs={{0,6},{1,7},{2,4},{3,5},{4,2},{5,3},{6,0},{7,1},{8,14},{9,15},{10,... | collective-permute-start | bytes 196616 | tf_op jit(solution)/shard_map/ppermute | solution.py:330
  38.0 1.7 %collective-permute-start.16 = (bf16[64,512]{1,0:T(8,128)(2,1)S(1)}, bf16[64,512]{1,0:T(8,128)(2,1)S(1)}, u32[]{:S(2)}, u32[]{:S(2)}) collective-permute-start(bf16[64,512]{1,0:T(8,128)(2,1)S(1)} %get-tuple-element.35), channel_id=1, source_target_pairs={{0,2},{1,3},{2,0},{3,1},{4,6},{5,7},{6,4},{7,5},{8,10},{9,11},{10,... | collective-permute-start | bytes 196616 | tf_op jit(solution)/shard_map/ppermute | solution.py:330
  39.7 2.3 %collective-permute-done.14.refs_0_ = bf16[64,512]{1,0:T(8,128)(2,1)S(1)} collective-permute-done((bf16[64,512]{1,0:T(8,128)(2,1)S(1)}, bf16[64,512]{1,0:T(8,128)(2,1)S(1)}, u32[]{:S(2)}, u32[]{:S(2)}) %collective-permute-start.14) | collective-permute-done | bytes 65568 | tf_op jit(solution)/shard_map/ppermute | solution.py:330
  42.0 2.0 %collective-permute-done.15.refs_1_ = bf16[64,512]{1,0:T(8,128)(2,1)S(1)} collective-permute-done((bf16[64,512]{1,0:T(8,128)(2,1)S(1)}, bf16[64,512]{1,0:T(8,128)(2,1)S(1)}, u32[]{:S(2)}, u32[]{:S(2)}) %collective-permute-start.15) | collective-permute-done | bytes 65568 | tf_op jit(solution)/shard_map/ppermute | solution.py:330
  44.0 1.8 %shard_map.61 = bf16[64,4,16,128]{3,2,1,0:T(8,128)(2,1)} custom-call(bf16[64,512]{1,0:T(8,128)(2,1)S(1)} %collective-permute-done.14.refs_0_, bf16[64,512]{1,0:T(8,128)(2,1)S(1)} %collective-permute-done.15.refs_1_, bf16[64,512]{1,0:T(8,128)(2,1)S(1)} %collective-permute-done.16.refs_2_, f32[64,512]{1,0:T(8,128)S(1)} %get-tuple-element.36.refs_3_, ...), custom_call_target="tpu_custom_call" | custom-call | bytes 4194304 | tf_op jit(solution)/shard_map/pallas_call | solution.py:450
  (17 shorter events, 0.1 us)
Async XLA Ops:
  0.0 14.8 %copy-start.1 = (bf16[64,32]{1,0:T(8,128)(2,1)S(1)}, bf16[64,32]{1,0:T(8,128)(2,1)}, u32[]{:S(2)}) copy-start(bf16[64,32]{1,0:T(8,128)(2,1)} %constant.6.clone.refs_9_) | copy-start | bytes 12292
  0.0 24.5 %copy-start.2 = (bf16[64,128]{1,0:T(8,128)(2,1)S(1)}, bf16[64,128]{1,0:T(8,128)(2,1)}, u32[]{:S(2)}) copy-start(bf16[64,128]{1,0:T(8,128)(2,1)} %constant.8.clone.refs_5_) | copy-start | bytes 49156
  0.0 24.5 %copy-start.3 = (bf16[64,128]{1,0:T(8,128)(2,1)S(1)}, bf16[64,128]{1,0:T(8,128)(2,1)}, u32[]{:S(2)}) copy-start(bf16[64,128]{1,0:T(8,128)(2,1)} %constant.7.clone.refs_4_) | copy-start | bytes 49156
  0.0 14.8 %copy-start = (bf16[8,32,256]{2,1,0:T(8,128)(2,1)S(1)}, bf16[8,32,256]{2,1,0:T(8,128)(2,1)}, u32[]{:S(2)}) copy-start(bf16[8,32,256]{2,1,0:T(8,128)(2,1)} %refs_10_.1) | copy-start | bytes 393220
  2.6 7.7 %collective-permute-start.5 = (bf16[64,512]{1,0:T(8,128)(2,1)S(1)}, bf16[64,512]{1,0:T(8,128)(2,1)S(1)}, u32[]{:S(2)}, u32[]{:S(2)}) collective-permute-start(bf16[64,512]{1,0:T(8,128)(2,1)S(1)} %get-tuple-element.23.refs_0_), channel_id=1, source_target_pairs={{0,6},{1,7},{2,4},{3,5},{4,2},{5,3},{6,0},{7,1},{8,14},{9,15},{10,... | collective-permute-start | bytes 196616 | tf_op jit(solution)/shard_map/ppermute | solution.py:384
  7.8 5.6 %collective-permute-start.3 = (bf16[64,512]{1,0:T(8,128)(2,1)S(1)}, bf16[64,512]{1,0:T(8,128)(2,1)S(1)}, u32[]{:S(2)}, u32[]{:S(2)}) collective-permute-start(bf16[64,512]{1,0:T(8,128)(2,1)S(1)} %get-tuple-element.23.refs_0_), channel_id=1, source_target_pairs={{0,4},{1,5},{2,6},{3,7},{4,0},{5,1},{6,2},{7,3},{8,12},{9,13},{10,... | collective-permute-start | bytes 196616 | tf_op jit(solution)/shard_map/ppermute | solution.py:384
  7.8 5.6 %collective-permute-start.1 = (bf16[64,512]{1,0:T(8,128)(2,1)S(1)}, bf16[64,512]{1,0:T(8,128)(2,1)S(1)}, u32[]{:S(2)}, u32[]{:S(2)}) collective-permute-start(bf16[64,512]{1,0:T(8,128)(2,1)S(1)} %get-tuple-element.23.refs_0_), channel_id=1, source_target_pairs={{0,2},{1,3},{2,0},{3,1},{4,6},{5,7},{6,4},{7,5},{8,10},{9,11},{10,... | collective-permute-start | bytes 196616 | tf_op jit(solution)/shard_map/ppermute | solution.py:384
  8.4 5.5 %collective-permute-start = (bf16[64,512]{1,0:T(8,128)(2,1)S(1)}, bf16[64,512]{1,0:T(8,128)(2,1)S(1)}, u32[]{:S(2)}, u32[]{:S(2)}) collective-permute-start(bf16[64,512]{1,0:T(8,128)(2,1)S(1)} %get-tuple-element.23.refs_0_), channel_id=1, source_target_pairs={{0,1},{1,0},{2,3},{3,2},{4,5},{5,4},{6,7},{7,6},{8,9},{9,8},{10,11... | collective-permute-start | bytes 196616 | tf_op jit(solution)/shard_map/ppermute | solution.py:330
  10.4 3.5 %collective-permute-start.6 = (bf16[64,512]{1,0:T(8,128)(2,1)S(1)}, bf16[64,512]{1,0:T(8,128)(2,1)S(1)}, u32[]{:S(2)}, u32[]{:S(2)}) collective-permute-start(bf16[64,512]{1,0:T(8,128)(2,1)S(1)} %collective-permute-done.5.refs_6_), channel_id=1, source_target_pairs={{0,1},{1,0},{2,3},{3,2},{4,5},{5,4},{6,7},{7,6},{8,9},{9,8},{10,11... | collective-permute-start | bytes 196616 | tf_op jit(solution)/shard_map/ppermute | solution.py:330
  13.4 1.3 %collective-permute-start.4 = (bf16[64,512]{1,0:T(8,128)(2,1)S(1)}, bf16[64,512]{1,0:T(8,128)(2,1)S(1)}, u32[]{:S(2)}, u32[]{:S(2)}) collective-permute-start(bf16[64,512]{1,0:T(8,128)(2,1)S(1)} %collective-permute-done.3.refs_4_), channel_id=1, source_target_pairs={{0,1},{1,0},{2,3},{3,2},{4,5},{5,4},{6,7},{7,6},{8,9},{9,8},{10,11... | collective-permute-start | bytes 196616 | tf_op jit(solution)/shard_map/ppermute | solution.py:330
  13.4 1.4 %collective-permute-start.2 = (bf16[64,512]{1,0:T(8,128)(2,1)S(1)}, bf16[64,512]{1,0:T(8,128)(2,1)S(1)}, u32[]{:S(2)}, u32[]{:S(2)}) collective-permute-start(bf16[64,512]{1,0:T(8,128)(2,1)S(1)} %collective-permute-done.1.refs_2_), channel_id=1, source_target_pairs={{0,1},{1,0},{2,3},{3,2},{4,5},{5,4},{6,7},{7,6},{8,9},{9,8},{10,11... | collective-permute-start | bytes 196616 | tf_op jit(solution)/shard_map/ppermute | solution.py:330
  16.3 6.6 %collective-permute-start.7 = (bf16[192,256]{1,0:T(8,128)(2,1)S(1)}, bf16[192,256]{1,0:T(8,128)(2,1)S(1)}, u32[]{:S(2)}, u32[]{:S(2)}) collective-permute-start(bf16[192,256]{1,0:T(8,128)(2,1)S(1)} %get-tuple-element.25), channel_id=1, source_target_pairs={{0,24},{1,25},{2,26},{3,27},{4,28},{5,29},{6,30},{7,31},{8,16},{9,... | collective-permute-start | bytes 294920 | tf_op jit(solution)/shard_map/ppermute | solution.py:342
  18.8 5.6 %collective-permute-start.8 = (bf16[192,256]{1,0:T(8,128)(2,1)S(1)}, bf16[192,256]{1,0:T(8,128)(2,1)S(1)}, u32[]{:S(2)}, u32[]{:S(2)}) collective-permute-start(bf16[192,256]{1,0:T(8,128)(2,1)S(1)} %get-tuple-element.26), channel_id=1, source_target_pairs={{0,16},{1,9},{2,18},{3,11},{4,20},{5,13},{6,22},{7,15},{8,24},{9,1... | collective-permute-start | bytes 294920 | tf_op jit(solution)/shard_map/ppermute | solution.py:342
  19.3 5.1 %collective-permute-start.9 = (bf16[192,256]{1,0:T(8,128)(2,1)S(1)}, bf16[192,256]{1,0:T(8,128)(2,1)S(1)}, u32[]{:S(2)}, u32[]{:S(2)}) collective-permute-start(bf16[192,256]{1,0:T(8,128)(2,1)S(1)} %get-tuple-element.27), channel_id=1, source_target_pairs={{0,8},{1,17},{2,10},{3,19},{4,12},{5,21},{6,14},{7,23},{8,0},{9,25... | collective-permute-start | bytes 294920 | tf_op jit(solution)/shard_map/ppermute | solution.py:342
  25.1 5.6 %collective-permute-start.10 = (bf16[128,256]{1,0:T(8,128)(2,1)S(1)}, bf16[128,256]{1,0:T(8,128)(2,1)S(1)}, u32[]{:S(2)}, u32[]{:S(2)}) collective-permute-start(bf16[128,256]{1,0:T(8,128)(2,1)S(1)} %get-tuple-element.29), channel_id=1, source_target_pairs={{0,24},{1,25},{2,26},{3,27},{4,28},{5,29},{6,30},{7,31},{8,16},{9,... | collective-permute-start | bytes 196616 | tf_op jit(solution)/shard_map/ppermute | solution.py:342
  27.5 4.3 %collective-permute-start.11 = (bf16[128,256]{1,0:T(8,128)(2,1)S(1)}, bf16[128,256]{1,0:T(8,128)(2,1)S(1)}, u32[]{:S(2)}, u32[]{:S(2)}) collective-permute-start(bf16[128,256]{1,0:T(8,128)(2,1)S(1)} %get-tuple-element.30), channel_id=1, source_target_pairs={{0,16},{1,9},{2,18},{3,11},{4,20},{5,13},{6,22},{7,15},{8,24},{9,1... | collective-permute-start | bytes 196616 | tf_op jit(solution)/shard_map/ppermute | solution.py:342
  28.1 4.3 %collective-permute-start.12 = (bf16[128,256]{1,0:T(8,128)(2,1)S(1)}, bf16[128,256]{1,0:T(8,128)(2,1)S(1)}, u32[]{:S(2)}, u32[]{:S(2)}) collective-permute-start(bf16[128,256]{1,0:T(8,128)(2,1)S(1)} %get-tuple-element.31), channel_id=1, source_target_pairs={{0,8},{1,17},{2,10},{3,19},{4,12},{5,21},{6,14},{7,23},{8,0},{9,25... | collective-permute-start | bytes 196616 | tf_op jit(solution)/shard_map/ppermute | solution.py:342
  33.5 1.6 %collective-permute-start.13 = (bf16[4,64,512]{2,1,0:T(8,128)(2,1)S(1)}, bf16[4,64,512]{2,1,0:T(8,128)(2,1)S(1)}, u32[]{:S(2)}, u32[]{:S(2)}) collective-permute-start(bf16[4,64,512]{2,1,0:T(8,128)(2,1)S(1)} %shard_map.59), channel_id=1, source_target_pairs={{0,1},{1,0},{2,3},{3,2},{4,5},{5,4},{6,7},{7,6},{8,9},{9,8},{10,11... | collective-permute-start | bytes 786440 | tf_op jit(solution)/shard_map/ppermute | solution.py:330
  35.2 6.8 %collective-permute-start.14 = (bf16[64,512]{1,0:T(8,128)(2,1)S(1)}, bf16[64,512]{1,0:T(8,128)(2,1)S(1)}, u32[]{:S(2)}, u32[]{:S(2)}) collective-permute-start(bf16[64,512]{1,0:T(8,128)(2,1)S(1)} %get-tuple-element.33), channel_id=1, source_target_pairs={{0,6},{1,7},{2,4},{3,5},{4,2},{5,3},{6,0},{7,1},{8,14},{9,15},{10,... | collective-permute-start | bytes 196616 | tf_op jit(solution)/shard_map/ppermute | solution.py:330
  38.0 6.1 %collective-permute-start.15 = (bf16[64,512]{1,0:T(8,128)(2,1)S(1)}, bf16[64,512]{1,0:T(8,128)(2,1)S(1)}, u32[]{:S(2)}, u32[]{:S(2)}) collective-permute-start(bf16[64,512]{1,0:T(8,128)(2,1)S(1)} %get-tuple-element.34), channel_id=1, source_target_pairs={{0,4},{1,5},{2,6},{3,7},{4,0},{5,1},{6,2},{7,3},{8,12},{9,13},{10,... | collective-permute-start | bytes 196616 | tf_op jit(solution)/shard_map/ppermute | solution.py:330
  38.0 6.1 %collective-permute-start.16 = (bf16[64,512]{1,0:T(8,128)(2,1)S(1)}, bf16[64,512]{1,0:T(8,128)(2,1)S(1)}, u32[]{:S(2)}, u32[]{:S(2)}) collective-permute-start(bf16[64,512]{1,0:T(8,128)(2,1)S(1)} %get-tuple-element.35), channel_id=1, source_target_pairs={{0,2},{1,3},{2,0},{3,1},{4,6},{5,7},{6,4},{7,5},{8,10},{9,11},{10,... | collective-permute-start | bytes 196616 | tf_op jit(solution)/shard_map/ppermute | solution.py:330

commit v14 on v11

--- a/solution.py
+++ b/solution.py
@@ -111,59 +111,36 @@
         edge_ref[g * ROWS : (g + 1) * ROWS] = jnp.concatenate(rows, axis=0).astype(BF16)
 
 
-def orders(shares):
-    return [list(range(1, shares))] * shares
-
-
-def pick(table, index):
-    value = jnp.int32(table[0])
-    for i in range(1, len(table)):
-        value = jnp.where(index == i, jnp.int32(table[i]), value)
-    return value
-
-
-def steps_for(j, shares):
-    order = orders(shares)
-    return sorted({order[a].index(a ^ j) for a in range(shares) if a ^ j})
-
-
-def pieces_of(shares):
-    return [list(reversed(range(shares)))]
+def asked(shares):
+    return [2, 1, *range(3, shares)]
 
 
 def plane_of(shares):
     return lax.div(lax.axis_index("pts"), lax.axis_size("pts") // shares)
 
 
-def tile_kernel(targets, shares, per_share, per_block, *refs):
-    steps = sorted({t for j in targets for t in steps_for(j, shares)})
-    n, many = per_share * (1 + len(steps)), len(targets)
-    blocks, (orb_ref, sel_ref, coulomb_ref) = refs[:n], refs[n : n + 3]
-    *refs, gathered, wide, cells = refs[-2 * many - 3 :]
-    outs, form_refs = refs[:many], refs[many:]
+def tile_kernel(shares, per_share, per_block, *refs):
+    blocks, (orb_ref, sel_ref, coulomb_ref) = refs[: shares * per_share], refs[shares * per_share :][:3]
+    *outs, form_ref, wide, cells = refs[shares * per_share + 3 :]
     local_k, _, norb, points = orb_ref.shape
     group = ROWS // (2 * per_block)
     share = per_share * per_block
     rows = 2 * share
     me, block = lax.axis_index("ka"), lax.axis_index("pts")
-    order = orders(shares)
-    for i, t in enumerate([None] + steps):
-        here = 0 if t is None else pick([order[a][t] for a in range(shares)], me)
-        for slot, j in enumerate(targets):
-
-            @pl.when(jnp.bitwise_xor(me, j) == here)
-            def _(i=i, slot=slot):
-                for e in range(per_share):
-                    place = jnp.bitwise_xor(jnp.bitwise_and(block, per_share - 1), e)
-                    gathered[slot, place] = blocks[i * per_share + e][...]
-
+    plane = plane_of(shares)
+    selector = sel_ref[jnp.bitwise_and(block, per_share - 1)]
+    order = [0, *asked(shares)]
     for g in range(local_k // group):
         forms = []
-        for slot in range(many):
+        for offset in range(shares):
             stacked = jnp.concatenate(
-                [gathered[slot, b, g * ROWS : (g + 1) * ROWS] for b in range(per_share)], axis=0
+                [
+                    blocks[order.index(offset) * per_share + e][g * ROWS : (g + 1) * ROWS]
+                    for e in range(per_share)
+                ],
+                axis=0,
             )
-            forms.append(dot(sel_ref[...], stacked).astype(BF16))
+            forms.append(dot(selector, stacked).astype(BF16))
         for kk in range(group):
             k = g * group + kk
             left = [form[2 * kk * rows : (2 * kk + 1) * rows] for form in forms]
@@ -172,20 +149,20 @@
                 [jnp.concatenate(left, axis=0), jnp.concatenate(right, axis=0)], axis=1
             )
             tile = dot(form, orb_ref[k].reshape(2 * norb, points))
-            for slot in range(many):
-                form_refs[slot][k] = form[slot * rows : (slot + 1) * rows]
+            for offset in range(shares):
+                form_ref[jnp.bitwise_xor(plane, offset), k] = form[offset * rows : (offset + 1) * rows]
                 for part in range(2):
-                    low = slot * rows + part * share
-                    start = slot * share * 2 * local_k + 2 * k + part
+                    low = offset * rows + part * share
+                    start = offset * share * 2 * local_k + 2 * k + part
                     spread(wide, start, 2 * local_k, tile[low : low + share])
     size = share * 2 * local_k
     cells[...] = coulomb_ref[...].astype(F32)
-    for slot, j in enumerate(targets):
-        outs[slot][:size] = take(wide, slot * size, size).astype(BF16)
-        owned = jnp.bitwise_xor(jnp.bitwise_xor(me, j), plane_of(shares))
-        start = pl.multiple_of(owned * share, share)
+    for s in range(shares):
+        offset = jnp.bitwise_xor(me, s)
+        outs[s][:size] = take(wide, pl.multiple_of(offset * size, size), size).astype(BF16)
+        start = pl.multiple_of(jnp.bitwise_xor(offset, plane) * share, share)
         pieces = [cells[r, pl.ds(start, share), :] for r in range(local_k)]
-        outs[slot][size:] = jnp.concatenate(pieces, axis=0).astype(BF16)
+        outs[s][size:] = jnp.concatenate(pieces, axis=0).astype(BF16)
 
 
 def transform_kernel(shares, total, share, *refs):
@@ -270,13 +247,9 @@
             outs[s - 1][...] = value.astype(BF16)
 
 
-def exchange_kernel(chunks, shares, scale, *refs):
-    pieces, form_refs, out_hbm = refs[:chunks][::-1], refs[chunks : chunks + shares], refs[chunks + shares]
-    wide, out_ref, form_ref, sems = refs[chunks + shares + 1 :]
-    owner = jnp.bitwise_xor(lax.axis_index("ka"), plane_of(shares))
-    for j in range(shares):
-        form_ref[jnp.bitwise_xor(owner, j)] = form_refs[j][...]
-    _, local_k, part_lanes, twice = form_ref.shape
+def exchange_kernel(chunks, scale, *refs):
+    pieces, (form_ref, out_hbm, wide, out_ref, sems) = refs[:chunks][::-1], refs[chunks:]
+    shares, local_k, part_lanes, twice = form_ref.shape
     lanes = shares * part_lanes
     norb = twice // 2
     spans = norb // LANES
@@ -348,45 +321,29 @@
         unread=1,
     )(orbitals)
     per_share = blocks // shares
-    order = orders(shares)
     partner = swap(edge, "pts", 1)
-    near = [edge, partner] + [swap(edge, "pts", 2 * e + c) for e in range(1, per_share // 2) for c in range(2)]
-    came = []
-    for t in range(shares - 1):
-        step = []
+    came = [edge, partner] + [swap(edge, "pts", 2 * e + c) for e in range(1, per_share // 2) for c in range(2)]
+    came = {0: came}
+    for offset in asked(shares):
+        came[offset] = []
         for e in range(per_share // 2):
-            pairs = [
-                (a * blocks + i, a * blocks + (i ^ (order[a][t] * per_share + 2 * e)))
-                for a in range(shares)
-                for i in range(blocks)
-            ]
-            block = lax.ppermute(edge, ("ka", "pts"), pairs)
-            step += [block, swap(block, "pts", 1)]
-        came.append(step)
-
-    selector = jnp.asarray(column_selector(group, per_share, per_block, 1))
+            block = swap(edge, "pts", offset * per_share + 2 * e)
+            came[offset] += [block, swap(block, "pts", 1)]
+    table = column_selector(group, per_share, per_block, 1).reshape(-1, per_share, ROWS)
+    places = [[place ^ e for e in range(per_share)] for place in range(per_share)]
+    selector = jnp.asarray(np.stack([table[:, place].reshape(table.shape[0], -1) for place in places]))
     piece = shape((share * 2 * local_k, points), BF16)
     both = shape((share * 3 * local_k, points), BF16)
-    tiles, forms, before = [None] * shares, [None] * shares, []
-    for targets in pieces_of(shares):
-        many = len(targets)
-        steps = sorted({t for j in targets for t in steps_for(j, shares)})
-        taken = [block for t in steps for block in came[t]]
-        result = call(
-            functools.partial(tile_kernel, targets, shares, per_share, per_block),
-            [both] * many + [shape((local_k, 2 * share, 2 * norb), BF16)] * many,
-            len(near) + len(taken) + 3,
-            [
-                pltpu.VMEM((many, per_share, local_k * 2 * per_block, norb), BF16),
-                tiled(many * share * 2 * local_k, points),
-                pltpu.VMEM(coulomb.shape, F32),
-            ],
-            size=6 * MIB,
-            unread=len(before),
-        )(*near, *taken, orbitals, selector, coulomb, *before)
-        for slot, j in enumerate(targets):
-            tiles[j], forms[j] = result[slot], result[many + slot]
-        before = [forms[targets[0]]]
+    *tiles, forms = call(
+        functools.partial(tile_kernel, shares, per_share, per_block),
+        [both] * shares + [shape((shares, local_k, 2 * share, 2 * norb), BF16)],
+        blocks + 3,
+        [
+            tiled(shares * share * 2 * local_k, points),
+            pltpu.VMEM(coulomb.shape, F32),
+        ],
+        size=6 * MIB,
+    )(*[block for offset in [0, *asked(shares)] for block in came[offset]], orbitals, selector, coulomb)
     tiles = trade(tiles, "ka", 1)
 
     forward, backward = phase_tables(total)
@@ -427,18 +384,17 @@
     pair = max(1, LANES // (2 * columns))
     rows = pair * spans * 2
     result = call(
-        functools.partial(exchange_kernel, chunks, shares, 1.0 / math.sqrt(points * blocks)),
+        functools.partial(exchange_kernel, chunks, 1.0 / math.sqrt(points * blocks)),
         shape((out_rows, local_k // pair, rows, LANES), BF16),
-        chunks + shares,
+        chunks + 1,
         [
             pltpu.VMEM((local_k // pair, out_rows * rows, LANES), F32),
             pltpu.VMEM((local_k // pair, out_rows, rows, LANES), BF16),
-            pltpu.VMEM((shares, local_k, 2 * share, 2 * norb), BF16),
             pltpu.SemaphoreType.DMA((local_k // pair,)),
         ],
         size=4 * MIB,
         result=pltpu.HBM,
-    )(*sums, *forms)
+    )(*sums, forms)
     result = result.reshape(out_rows, local_k, spans, 2, LANES)
     return result.transpose(0, 1, 3, 2, 4).reshape(out_rows, local_k, 2, norb)
 

time: 46 us -> 46.2 us (level)
  waiting for transfers between devices: 19 us -> 19.9 us
  starting transfers between devices: 17.9 us -> 17.4 us
    ppermute x14 -> x17, waiting for transfers between devices: 14.1 us -> 19.9 us  [swap(): return lax.ppermute(value, axis, [(i, i ^ mask) for i in range(size)])]
    ppermute x3 -> x0, starting transfers between devices: 5.79 us -> none  [body(): block = lax.ppermute(edge, ('ka', 'pts'), pairs)]
    ppermute x14 -> x17, starting transfers between devices: 12.1 us -> 17.4 us  [swap(): return lax.ppermute(value, axis, [(i, i ^ mask) for i in range(size)])]
    ppermute x3 -> x0, waiting for transfers between devices: 4.96 us -> none  [body(): block = lax.ppermute(edge, ('ka', 'pts'), pairs)]
  transfers between devices with their start and end apart: 17 -> 17, of which waited for: 13 -> 14; matrix products, arithmetic and copies ran while one was open for 0% -> 0% of each run, Pallas kernels for 3% -> 3%
where the time goes in v14:
time: 46.2 us; the launch traced here: 46 us
  waiting for transfers between devices  19.9 us (43%)
  starting transfers between devices  17.4 us (38%)
  Pallas kernels  8.62 us (19%)
    ppermute x17, waiting for transfers between devices, swap(): return lax.ppermute(value, axis, [(i, i ^ mask) for i in range(size)])  19.9 us
    ppermute x17, starting transfers between devices, swap(): return lax.ppermute(value, axis, [(i, i ^ mask) for i in range(size)])  17.4 us
    pallas_call x1, Pallas kernels, body(): call(functools.partial(edge_kernel, per_block), [shape((local_k * 2 * per...  2.63 us
    pallas_call x2, Pallas kernels, body(): call(functools.partial(weight_kernel, shares, flip, out_rows), shape((chu...  2.33 us
    pallas_call x1, Pallas kernels, body(): call(functools.partial(exchange_kernel, chunks, 1.0 / math.sqrt(points *...  1.66 us
    pallas_call x1, Pallas kernels, body(): call(functools.partial(tile_kernel, shares, per_share, per_block), [both]...  1.38 us
  transfers between devices with their start and end apart: 17, of which 14 were waited for; matrix products, arithmetic and copies ran while one was open for 0% of the time, Pallas kernels for 3%

profile of v14, /device:TPU:0, one launch (start us, length us, event | category | flops | bytes accessed | tf_op | source)
XLA Modules:
  0.0 46.0 jit_solution(6630685399082591044)
XLA Ops:
  0.0 2.6 %shard_map.55 = (bf16[64,512]{1,0:T(8,128)(2,1)S(1)}, bf16[8,2,512,256]{3,2,1,0:T(8,128)(2,1)S(1)}) custom-call(bf16[8,2,512,256]{3,2,1,0:T(8,128)(2,1)} %orb_hbm.1), custom_call_target="tpu_custom_call" | custom-call | bytes 8388608 | tf_op jit(solution)/shard_map/pallas_call | solution.py:314
  2.6 5.1 %collective-permute-start.5 = (bf16[64,512]{1,0:T(8,128)(2,1)S(1)}, bf16[64,512]{1,0:T(8,128)(2,1)S(1)}, u32[]{:S(2)}, u32[]{:S(2)}) collective-permute-start(bf16[64,512]{1,0:T(8,128)(2,1)S(1)} %get-tuple-element.20.refs_0_), channel_id=1, source_target_pairs={{0,6},{1,7},{2,4},{3,5},{4,2},{5,3},{6,0},{7,1},{8,14},{9,15},{10,... | collective-permute-start | bytes 196616 | tf_op jit(solution)/shard_map/ppermute | solution.py:295
  7.8 0.6 %collective-permute-start.1 = (bf16[64,512]{1,0:T(8,128)(2,1)S(1)}, bf16[64,512]{1,0:T(8,128)(2,1)S(1)}, u32[]{:S(2)}, u32[]{:S(2)}) collective-permute-start(bf16[64,512]{1,0:T(8,128)(2,1)S(1)} %get-tuple-element.20.refs_0_), channel_id=1, source_target_pairs={{0,4},{1,5},{2,6},{3,7},{4,0},{5,1},{6,2},{7,3},{8,12},{9,13},{10,... | collective-permute-start | bytes 196616 | tf_op jit(solution)/shard_map/ppermute | solution.py:295
  8.4 2.3 %collective-permute-done.5.refs_6_ = bf16[64,512]{1,0:T(8,128)(2,1)S(1)} collective-permute-done((bf16[64,512]{1,0:T(8,128)(2,1)S(1)}, bf16[64,512]{1,0:T(8,128)(2,1)S(1)}, u32[]{:S(2)}, u32[]{:S(2)}) %collective-permute-start.5) | collective-permute-done | bytes 65568 | tf_op jit(solution)/shard_map/ppermute | solution.py:295
  10.7 1.8 %collective-permute-done.3.refs_4_ = bf16[64,512]{1,0:T(8,128)(2,1)S(1)} collective-permute-done((bf16[64,512]{1,0:T(8,128)(2,1)S(1)}, bf16[64,512]{1,0:T(8,128)(2,1)S(1)}, u32[]{:S(2)}, u32[]{:S(2)}) %collective-permute-start.3) | collective-permute-done | bytes 65568 | tf_op jit(solution)/shard_map/ppermute | solution.py:295
  12.4 1.0 %collective-permute-done.1.refs_2_ = bf16[64,512]{1,0:T(8,128)(2,1)S(1)} collective-permute-done((bf16[64,512]{1,0:T(8,128)(2,1)S(1)}, bf16[64,512]{1,0:T(8,128)(2,1)S(1)}, u32[]{:S(2)}, u32[]{:S(2)}) %collective-permute-start.1) | collective-permute-done | bytes 65568 | tf_op jit(solution)/shard_map/ppermute | solution.py:295
  13.4 0.3 collective-permute-done.4.refs_5_
  13.7 1.0 %collective-permute-done.2.refs_3_ = bf16[64,512]{1,0:T(8,128)(2,1)S(1)} collective-permute-done((bf16[64,512]{1,0:T(8,128)(2,1)S(1)}, bf16[64,512]{1,0:T(8,128)(2,1)S(1)}, u32[]{:S(2)}, u32[]{:S(2)}) %collective-permute-start.2) | collective-permute-done | bytes 65568 | tf_op jit(solution)/shard_map/ppermute | solution.py:295
  14.7 1.4 %shard_map.56 = (bf16[192,256]{1,0:T(8,128)(2,1)S(1)}, bf16[192,256]{1,0:T(8,128)(2,1)S(1)}, bf16[192,256]{1,0:T(8,128)(2,1)S(1)}, bf16[192,256]{1,0:T(8,128)(2,1)S(1)}, bf16[4,8,16,1024]{3,2,1,0:T(8,128)(2,1)S(1)}) custom-call(bf16[64,512]{1,0:T(8,128)(2,1)S(1)} %get-tuple-element.20.refs_0_, bf16[64,512]{1,0:T(8,128)(2,1)S(1)} %collective-permute-done.refs_1_, ...), custom_call_target="tpu_custom_call" | custom-call | bytes 6291456 | tf_op jit(solution)/shard_map/pallas_call | solution.py:337
  16.1 2.5 %collective-permute-start.7 = (bf16[192,256]{1,0:T(8,128)(2,1)S(1)}, bf16[192,256]{1,0:T(8,128)(2,1)S(1)}, u32[]{:S(2)}, u32[]{:S(2)}) collective-permute-start(bf16[192,256]{1,0:T(8,128)(2,1)S(1)} %get-tuple-element.22), channel_id=1, source_target_pairs={{0,24},{8,16},{16,8},{24,0},{1,25},{9,17},{17,9},{25,1},{2,26},{10... | collective-permute-start | bytes 294920 | tf_op jit(solution)/shard_map/ppermute | solution.py:295
  18.6 0.5 %collective-permute-start.8 = (bf16[192,256]{1,0:T(8,128)(2,1)S(1)}, bf16[192,256]{1,0:T(8,128)(2,1)S(1)}, u32[]{:S(2)}, u32[]{:S(2)}) collective-permute-start(bf16[192,256]{1,0:T(8,128)(2,1)S(1)} %get-tuple-element.23), channel_id=1, source_target_pairs={{0,16},{8,24},{16,0},{24,8},{1,17},{9,25},{17,1},{25,9},{2,18},{10... | collective-permute-start | bytes 294920 | tf_op jit(solution)/shard_map/ppermute | solution.py:295
  19.1 0.5 %collective-permute-start.9 = (bf16[192,256]{1,0:T(8,128)(2,1)S(1)}, bf16[192,256]{1,0:T(8,128)(2,1)S(1)}, u32[]{:S(2)}, u32[]{:S(2)}) collective-permute-start(bf16[192,256]{1,0:T(8,128)(2,1)S(1)} %get-tuple-element.24), channel_id=1, source_target_pairs={{0,8},{8,0},{16,24},{24,16},{1,9},{9,1},{17,25},{25,17},{2,10},{10... | collective-permute-start | bytes 294920 | tf_op jit(solution)/shard_map/ppermute | solution.py:295
  19.6 2.4 %collective-permute-done.7.refs_0_ = bf16[192,256]{1,0:T(8,128)(2,1)S(1)} collective-permute-done((bf16[192,256]{1,0:T(8,128)(2,1)S(1)}, bf16[192,256]{1,0:T(8,128)(2,1)S(1)}, u32[]{:S(2)}, u32[]{:S(2)}) %collective-permute-start.7) | collective-permute-done | bytes 98336 | tf_op jit(solution)/shard_map/ppermute | solution.py:295
  22.0 2.0 %collective-permute-done.8.refs_1_ = bf16[192,256]{1,0:T(8,128)(2,1)S(1)} collective-permute-done((bf16[192,256]{1,0:T(8,128)(2,1)S(1)}, bf16[192,256]{1,0:T(8,128)(2,1)S(1)}, u32[]{:S(2)}, u32[]{:S(2)}) %collective-permute-start.8) | collective-permute-done | bytes 98336 | tf_op jit(solution)/shard_map/ppermute | solution.py:295
  24.0 0.1 collective-permute-done.9.refs_2_
  24.1 0.6 %shard_map.57 = (bf16[128,256]{1,0:T(8,128)(2,1)S(1)}, bf16[128,256]{1,0:T(8,128)(2,1)S(1)}, bf16[128,256]{1,0:T(8,128)(2,1)S(1)}, bf16[128,256]{1,0:T(8,128)(2,1)S(1)}) custom-call(bf16[192,256]{1,0:T(8,128)(2,1)S(1)} %collective-permute-done.7.refs_0_, bf16[192,256]{1,0:T(8,128)(2,1)S(1)} %collective-permute-done.8.refs_1_, ...), custom_call_target="tpu_custom_call" | custom-call | bytes 2097152 | tf_op jit(solution)/shard_map/pallas_call | solution.py:350
  24.6 1.8 %collective-permute-start.10 = (bf16[128,256]{1,0:T(8,128)(2,1)S(1)}, bf16[128,256]{1,0:T(8,128)(2,1)S(1)}, u32[]{:S(2)}, u32[]{:S(2)}) collective-permute-start(bf16[128,256]{1,0:T(8,128)(2,1)S(1)} %get-tuple-element.26), channel_id=1, source_target_pairs={{0,24},{8,16},{16,8},{24,0},{1,25},{9,17},{17,9},{25,1},{2,26},{10... | collective-permute-start | bytes 196616 | tf_op jit(solution)/shard_map/ppermute | solution.py:295
  26.4 1.3 %collective-permute-start.11 = (bf16[128,256]{1,0:T(8,128)(2,1)S(1)}, bf16[128,256]{1,0:T(8,128)(2,1)S(1)}, u32[]{:S(2)}, u32[]{:S(2)}) collective-permute-start(bf16[128,256]{1,0:T(8,128)(2,1)S(1)} %get-tuple-element.27), channel_id=1, source_target_pairs={{0,16},{8,24},{16,0},{24,8},{1,17},{9,25},{17,1},{25,9},{2,18},{10... | collective-permute-start | bytes 196616 | tf_op jit(solution)/shard_map/ppermute | solution.py:295
  27.7 0.5 %collective-permute-start.12 = (bf16[128,256]{1,0:T(8,128)(2,1)S(1)}, bf16[128,256]{1,0:T(8,128)(2,1)S(1)}, u32[]{:S(2)}, u32[]{:S(2)}) collective-permute-start(bf16[128,256]{1,0:T(8,128)(2,1)S(1)} %get-tuple-element.28), channel_id=1, source_target_pairs={{0,8},{8,0},{16,24},{24,16},{1,9},{9,1},{17,25},{25,17},{2,10},{10... | collective-permute-start | bytes 196616 | tf_op jit(solution)/shard_map/ppermute | solution.py:295
  28.2 2.1 %collective-permute-done.10.refs_0_ = bf16[128,256]{1,0:T(8,128)(2,1)S(1)} collective-permute-done((bf16[128,256]{1,0:T(8,128)(2,1)S(1)}, bf16[128,256]{1,0:T(8,128)(2,1)S(1)}, u32[]{:S(2)}, u32[]{:S(2)}) %collective-permute-start.10) | collective-permute-done | bytes 65568 | tf_op jit(solution)/shard_map/ppermute | solution.py:295
  30.3 0.5 %collective-permute-done.11.refs_1_ = bf16[128,256]{1,0:T(8,128)(2,1)S(1)} collective-permute-done((bf16[128,256]{1,0:T(8,128)(2,1)S(1)}, bf16[128,256]{1,0:T(8,128)(2,1)S(1)}, u32[]{:S(2)}, u32[]{:S(2)}) %collective-permute-start.11) | collective-permute-done | bytes 65568 | tf_op jit(solution)/shard_map/ppermute | solution.py:295
  30.9 1.1 %collective-permute-done.12.refs_2_ = bf16[128,256]{1,0:T(8,128)(2,1)S(1)} collective-permute-done((bf16[128,256]{1,0:T(8,128)(2,1)S(1)}, bf16[128,256]{1,0:T(8,128)(2,1)S(1)}, u32[]{:S(2)}, u32[]{:S(2)}) %collective-permute-start.12) | collective-permute-done | bytes 65568 | tf_op jit(solution)/shard_map/ppermute | solution.py:295
  32.0 1.2 %shard_map.59 = bf16[4,64,512]{2,1,0:T(8,128)(2,1)S(1)} custom-call(bf16[128,256]{1,0:T(8,128)(2,1)S(1)} %collective-permute-done.10.refs_0_, bf16[128,256]{1,0:T(8,128)(2,1)S(1)} %collective-permute-done.11.refs_1_, bf16[128,256]{1,0:T(8,128)(2,1)S(1)} %collective-permute-done.12.refs_2_, bf16[128,256]{1,0:T(8,128)(2,1)S(1)} %get-tuple-element.29.refs_3_, ...), custom_call_target="tpu_custom_call" | custom-call | bytes 6291456 | tf_op jit(solution)/shard_map/pallas_call | solution.py:367
  33.2 0.1 collective-permute-start.13
  33.2 1.2 %shard_map.58.keep_ref = f32[4,64,512]{2,1,0:T(8,128)S(1)} custom-call(bf16[128,256]{1,0:T(8,128)(2,1)S(1)} %collective-permute-done.10.refs_0_, bf16[128,256]{1,0:T(8,128)(2,1)S(1)} %collective-permute-done.11.refs_1_, bf16[128,256]{1,0:T(8,128)(2,1)S(1)} %collective-permute-done.12.refs_2_, bf16[128,256]{1,0:T(8,128)(2,1)S(1)} %get-tuple-element.29.refs_3_, ...), custom_call_target="tpu_custom_call" | custom-call | bytes 6291456 | tf_op jit(solution)/shard_map/pallas_call | solution.py:367
  34.4 0.4 collective-permute-done.13.came_ref
  34.8 2.2 %collective-permute-start.14 = (bf16[64,512]{1,0:T(8,128)(2,1)S(1)}, bf16[64,512]{1,0:T(8,128)(2,1)S(1)}, u32[]{:S(2)}, u32[]{:S(2)}) collective-permute-start(bf16[64,512]{1,0:T(8,128)(2,1)S(1)} %get-tuple-element.30), channel_id=1, source_target_pairs={{0,6},{1,7},{2,4},{3,5},{4,2},{5,3},{6,0},{7,1},{8,14},{9,15},{10,... | collective-permute-start | bytes 196616 | tf_op jit(solution)/shard_map/ppermute | solution.py:295
  37.0 0.9 %collective-permute-start.15 = (bf16[64,512]{1,0:T(8,128)(2,1)S(1)}, bf16[64,512]{1,0:T(8,128)(2,1)S(1)}, u32[]{:S(2)}, u32[]{:S(2)}) collective-permute-start(bf16[64,512]{1,0:T(8,128)(2,1)S(1)} %get-tuple-element.31), channel_id=1, source_target_pairs={{0,4},{1,5},{2,6},{3,7},{4,0},{5,1},{6,2},{7,3},{8,12},{9,13},{10,... | collective-permute-start | bytes 196616 | tf_op jit(solution)/shard_map/ppermute | solution.py:295
  37.9 1.4 %collective-permute-start.16 = (bf16[64,512]{1,0:T(8,128)(2,1)S(1)}, bf16[64,512]{1,0:T(8,128)(2,1)S(1)}, u32[]{:S(2)}, u32[]{:S(2)}) collective-permute-start(bf16[64,512]{1,0:T(8,128)(2,1)S(1)} %get-tuple-element.32), channel_id=1, source_target_pairs={{0,2},{1,3},{2,0},{3,1},{4,6},{5,7},{6,4},{7,5},{8,10},{9,11},{10,... | collective-permute-start | bytes 196616 | tf_op jit(solution)/shard_map/ppermute | solution.py:295
  39.3 2.4 %collective-permute-done.14.refs_0_ = bf16[64,512]{1,0:T(8,128)(2,1)S(1)} collective-permute-done((bf16[64,512]{1,0:T(8,128)(2,1)S(1)}, bf16[64,512]{1,0:T(8,128)(2,1)S(1)}, u32[]{:S(2)}, u32[]{:S(2)}) %collective-permute-start.14) | collective-permute-done | bytes 65568 | tf_op jit(solution)/shard_map/ppermute | solution.py:295
  41.6 2.7 %collective-permute-done.15.refs_1_ = bf16[64,512]{1,0:T(8,128)(2,1)S(1)} collective-permute-done((bf16[64,512]{1,0:T(8,128)(2,1)S(1)}, bf16[64,512]{1,0:T(8,128)(2,1)S(1)}, u32[]{:S(2)}, u32[]{:S(2)}) %collective-permute-start.15) | collective-permute-done | bytes 65568 | tf_op jit(solution)/shard_map/ppermute | solution.py:295
  44.3 1.7 %shard_map.61 = bf16[64,4,16,128]{3,2,1,0:T(8,128)(2,1)} custom-call(bf16[64,512]{1,0:T(8,128)(2,1)S(1)} %collective-permute-done.14.refs_0_, bf16[64,512]{1,0:T(8,128)(2,1)S(1)} %collective-permute-done.15.refs_1_, bf16[64,512]{1,0:T(8,128)(2,1)S(1)} %collective-permute-done.16.refs_2_, f32[64,512]{1,0:T(8,128)S(1)} %get-tuple-element.33.refs_3_, ...), custom_call_target="tpu_custom_call" | custom-call | bytes 4194304 | tf_op jit(solution)/shard_map/pallas_call | solution.py:386
  (17 shorter events, 0.1 us)
Async XLA Ops:
  0.0 14.7 %copy-start.1 = (bf16[2,64,32]{2,1,0:T(8,128)(2,1)S(1)}, bf16[2,64,32]{2,1,0:T(8,128)(2,1)}, u32[]{:S(2)}) copy-start(bf16[2,64,32]{2,1,0:T(8,128)(2,1)} %constant.6.clone.refs_9_) | copy-start | bytes 24580
  0.0 24.0 %copy-start.2 = (bf16[64,128]{1,0:T(8,128)(2,1)S(1)}, bf16[64,128]{1,0:T(8,128)(2,1)}, u32[]{:S(2)}) copy-start(bf16[64,128]{1,0:T(8,128)(2,1)} %constant.8.clone.refs_5_) | copy-start | bytes 49156
  0.0 24.0 %copy-start.3 = (bf16[64,128]{1,0:T(8,128)(2,1)S(1)}, bf16[64,128]{1,0:T(8,128)(2,1)}, u32[]{:S(2)}) copy-start(bf16[64,128]{1,0:T(8,128)(2,1)} %constant.7.clone.refs_4_) | copy-start | bytes 49156
  0.0 14.7 %copy-start = (bf16[8,32,256]{2,1,0:T(8,128)(2,1)S(1)}, bf16[8,32,256]{2,1,0:T(8,128)(2,1)}, u32[]{:S(2)}) copy-start(bf16[8,32,256]{2,1,0:T(8,128)(2,1)} %refs_10_.1) | copy-start | bytes 393220
  2.6 8.0 %collective-permute-start.5 = (bf16[64,512]{1,0:T(8,128)(2,1)S(1)}, bf16[64,512]{1,0:T(8,128)(2,1)S(1)}, u32[]{:S(2)}, u32[]{:S(2)}) collective-permute-start(bf16[64,512]{1,0:T(8,128)(2,1)S(1)} %get-tuple-element.20.refs_0_), channel_id=1, source_target_pairs={{0,6},{1,7},{2,4},{3,5},{4,2},{5,3},{6,0},{7,1},{8,14},{9,15},{10,... | collective-permute-start | bytes 196616 | tf_op jit(solution)/shard_map/ppermute | solution.py:295
  7.8 4.7 %collective-permute-start.3 = (bf16[64,512]{1,0:T(8,128)(2,1)S(1)}, bf16[64,512]{1,0:T(8,128)(2,1)S(1)}, u32[]{:S(2)}, u32[]{:S(2)}) collective-permute-start(bf16[64,512]{1,0:T(8,128)(2,1)S(1)} %get-tuple-element.20.refs_0_), channel_id=1, source_target_pairs={{0,2},{1,3},{2,0},{3,1},{4,6},{5,7},{6,4},{7,5},{8,10},{9,11},{10,... | collective-permute-start | bytes 196616 | tf_op jit(solution)/shard_map/ppermute | solution.py:295
  7.8 5.6 %collective-permute-start.1 = (bf16[64,512]{1,0:T(8,128)(2,1)S(1)}, bf16[64,512]{1,0:T(8,128)(2,1)S(1)}, u32[]{:S(2)}, u32[]{:S(2)}) collective-permute-start(bf16[64,512]{1,0:T(8,128)(2,1)S(1)} %get-tuple-element.20.refs_0_), channel_id=1, source_target_pairs={{0,4},{1,5},{2,6},{3,7},{4,0},{5,1},{6,2},{7,3},{8,12},{9,13},{10,... | collective-permute-start | bytes 196616 | tf_op jit(solution)/shard_map/ppermute | solution.py:295
  8.4 5.0 %collective-permute-start = (bf16[64,512]{1,0:T(8,128)(2,1)S(1)}, bf16[64,512]{1,0:T(8,128)(2,1)S(1)}, u32[]{:S(2)}, u32[]{:S(2)}) collective-permute-start(bf16[64,512]{1,0:T(8,128)(2,1)S(1)} %get-tuple-element.20.refs_0_), channel_id=1, source_target_pairs={{0,1},{1,0},{2,3},{3,2},{4,5},{5,4},{6,7},{7,6},{8,9},{9,8},{10,11... | collective-permute-start | bytes 196616 | tf_op jit(solution)/shard_map/ppermute | solution.py:295
  10.7 2.7 %collective-permute-start.6 = (bf16[64,512]{1,0:T(8,128)(2,1)S(1)}, bf16[64,512]{1,0:T(8,128)(2,1)S(1)}, u32[]{:S(2)}, u32[]{:S(2)}) collective-permute-start(bf16[64,512]{1,0:T(8,128)(2,1)S(1)} %collective-permute-done.5.refs_6_), channel_id=1, source_target_pairs={{0,1},{1,0},{2,3},{3,2},{4,5},{5,4},{6,7},{7,6},{8,9},{9,8},{10,11... | collective-permute-start | bytes 196616 | tf_op jit(solution)/shard_map/ppermute | solution.py:295
  12.4 1.3 %collective-permute-start.4 = (bf16[64,512]{1,0:T(8,128)(2,1)S(1)}, bf16[64,512]{1,0:T(8,128)(2,1)S(1)}, u32[]{:S(2)}, u32[]{:S(2)}) collective-permute-start(bf16[64,512]{1,0:T(8,128)(2,1)S(1)} %collective-permute-done.3.refs_4_), channel_id=1, source_target_pairs={{0,1},{1,0},{2,3},{3,2},{4,5},{5,4},{6,7},{7,6},{8,9},{9,8},{10,11... | collective-permute-start | bytes 196616 | tf_op jit(solution)/shard_map/ppermute | solution.py:295
  13.4 1.3 %collective-permute-start.2 = (bf16[64,512]{1,0:T(8,128)(2,1)S(1)}, bf16[64,512]{1,0:T(8,128)(2,1)S(1)}, u32[]{:S(2)}, u32[]{:S(2)}) collective-permute-start(bf16[64,512]{1,0:T(8,128)(2,1)S(1)} %collective-permute-done.1.refs_2_), channel_id=1, source_target_pairs={{0,1},{1,0},{2,3},{3,2},{4,5},{5,4},{6,7},{7,6},{8,9},{9,8},{10,11... | collective-permute-start | bytes 196616 | tf_op jit(solution)/shard_map/ppermute | solution.py:295
  16.1 5.9 %collective-permute-start.7 = (bf16[192,256]{1,0:T(8,128)(2,1)S(1)}, bf16[192,256]{1,0:T(8,128)(2,1)S(1)}, u32[]{:S(2)}, u32[]{:S(2)}) collective-permute-start(bf16[192,256]{1,0:T(8,128)(2,1)S(1)} %get-tuple-element.22), channel_id=1, source_target_pairs={{0,24},{8,16},{16,8},{24,0},{1,25},{9,17},{17,9},{25,1},{2,26},{10... | collective-permute-start | bytes 294920 | tf_op jit(solution)/shard_map/ppermute | solution.py:295
  18.6 5.4 %collective-permute-start.8 = (bf16[192,256]{1,0:T(8,128)(2,1)S(1)}, bf16[192,256]{1,0:T(8,128)(2,1)S(1)}, u32[]{:S(2)}, u32[]{:S(2)}) collective-permute-start(bf16[192,256]{1,0:T(8,128)(2,1)S(1)} %get-tuple-element.23), channel_id=1, source_target_pairs={{0,16},{8,24},{16,0},{24,8},{1,17},{9,25},{17,1},{25,9},{2,18},{10... | collective-permute-start | bytes 294920 | tf_op jit(solution)/shard_map/ppermute | solution.py:295
  19.1 5.0 %collective-permute-start.9 = (bf16[192,256]{1,0:T(8,128)(2,1)S(1)}, bf16[192,256]{1,0:T(8,128)(2,1)S(1)}, u32[]{:S(2)}, u32[]{:S(2)}) collective-permute-start(bf16[192,256]{1,0:T(8,128)(2,1)S(1)} %get-tuple-element.24), channel_id=1, source_target_pairs={{0,8},{8,0},{16,24},{24,16},{1,9},{9,1},{17,25},{25,17},{2,10},{10... | collective-permute-start | bytes 294920 | tf_op jit(solution)/shard_map/ppermute | solution.py:295
  24.6 5.7 %collective-permute-start.10 = (bf16[128,256]{1,0:T(8,128)(2,1)S(1)}, bf16[128,256]{1,0:T(8,128)(2,1)S(1)}, u32[]{:S(2)}, u32[]{:S(2)}) collective-permute-start(bf16[128,256]{1,0:T(8,128)(2,1)S(1)} %get-tuple-element.26), channel_id=1, source_target_pairs={{0,24},{8,16},{16,8},{24,0},{1,25},{9,17},{17,9},{25,1},{2,26},{10... | collective-permute-start | bytes 196616 | tf_op jit(solution)/shard_map/ppermute | solution.py:295
  26.4 4.5 %collective-permute-start.11 = (bf16[128,256]{1,0:T(8,128)(2,1)S(1)}, bf16[128,256]{1,0:T(8,128)(2,1)S(1)}, u32[]{:S(2)}, u32[]{:S(2)}) collective-permute-start(bf16[128,256]{1,0:T(8,128)(2,1)S(1)} %get-tuple-element.27), channel_id=1, source_target_pairs={{0,16},{8,24},{16,0},{24,8},{1,17},{9,25},{17,1},{25,9},{2,18},{10... | collective-permute-start | bytes 196616 | tf_op jit(solution)/shard_map/ppermute | solution.py:295
  27.7 4.3 %collective-permute-start.12 = (bf16[128,256]{1,0:T(8,128)(2,1)S(1)}, bf16[128,256]{1,0:T(8,128)(2,1)S(1)}, u32[]{:S(2)}, u32[]{:S(2)}) collective-permute-start(bf16[128,256]{1,0:T(8,128)(2,1)S(1)} %get-tuple-element.28), channel_id=1, source_target_pairs={{0,8},{8,0},{16,24},{24,16},{1,9},{9,1},{17,25},{25,17},{2,10},{10... | collective-permute-start | bytes 196616 | tf_op jit(solution)/shard_map/ppermute | solution.py:295
  33.2 1.6 %collective-permute-start.13 = (bf16[4,64,512]{2,1,0:T(8,128)(2,1)S(1)}, bf16[4,64,512]{2,1,0:T(8,128)(2,1)S(1)}, u32[]{:S(2)}, u32[]{:S(2)}) collective-permute-start(bf16[4,64,512]{2,1,0:T(8,128)(2,1)S(1)} %shard_map.59), channel_id=1, source_target_pairs={{0,1},{1,0},{2,3},{3,2},{4,5},{5,4},{6,7},{7,6},{8,9},{9,8},{10,11... | collective-permute-start | bytes 786440 | tf_op jit(solution)/shard_map/ppermute | solution.py:295
  34.8 6.8 %collective-permute-start.14 = (bf16[64,512]{1,0:T(8,128)(2,1)S(1)}, bf16[64,512]{1,0:T(8,128)(2,1)S(1)}, u32[]{:S(2)}, u32[]{:S(2)}) collective-permute-start(bf16[64,512]{1,0:T(8,128)(2,1)S(1)} %get-tuple-element.30), channel_id=1, source_target_pairs={{0,6},{1,7},{2,4},{3,5},{4,2},{5,3},{6,0},{7,1},{8,14},{9,15},{10,... | collective-permute-start | bytes 196616 | tf_op jit(solution)/shard_map/ppermute | solution.py:295
  37.0 7.3 %collective-permute-start.15 = (bf16[64,512]{1,0:T(8,128)(2,1)S(1)}, bf16[64,512]{1,0:T(8,128)(2,1)S(1)}, u32[]{:S(2)}, u32[]{:S(2)}) collective-permute-start(bf16[64,512]{1,0:T(8,128)(2,1)S(1)} %get-tuple-element.31), channel_id=1, source_target_pairs={{0,4},{1,5},{2,6},{3,7},{4,0},{5,1},{6,2},{7,3},{8,12},{9,13},{10,... | collective-permute-start | bytes 196616 | tf_op jit(solution)/shard_map/ppermute | solution.py:295
  37.9 6.5 %collective-permute-start.16 = (bf16[64,512]{1,0:T(8,128)(2,1)S(1)}, bf16[64,512]{1,0:T(8,128)(2,1)S(1)}, u32[]{:S(2)}, u32[]{:S(2)}) collective-permute-start(bf16[64,512]{1,0:T(8,128)(2,1)S(1)} %get-tuple-element.32), channel_id=1, source_target_pairs={{0,2},{1,3},{2,0},{3,1},{4,6},{5,7},{6,4},{7,5},{8,10},{9,11},{10,... | collective-permute-start | bytes 196616 | tf_op jit(solution)/shard_map/ppermute | solution.py:295

commit v15 on v14

--- a/solution.py
+++ b/solution.py
@@ -239,7 +239,7 @@
 def pair_kernel(chunks, keep_ref, came_ref, own_ref, *outs):
     z = lax.shift_right_logical(lax.axis_index("pts"), 1)
     for s in range(chunks):
-        dest = jnp.bitwise_xor(z, s)
+        dest = lax.rem(z + s, chunks)
         value = keep_ref[dest] + came_ref[dest].astype(F32)
         if s == 0:
             own_ref[...] = value
@@ -299,6 +299,15 @@
     return [swap(pieces[s], axis, s * step) for s in reversed(range(1, len(pieces)))] + [pieces[0]]
 
 
+def shift_along(pieces):
+    chunks = len(pieces)
+    came = []
+    for s in range(1, chunks):
+        pairs = [(2 * z + core, 2 * ((z + s) % chunks) + core) for z in range(chunks) for core in range(2)]
+        came.append(lax.ppermute(pieces[s], "pts", pairs))
+    return came + [pieces[0]]
+
+
 def body(orbitals, coulomb):
     shares, blocks = lax.axis_size("ka"), lax.axis_size("pts")
     local_k, _, norb, points = orbitals.shape
@@ -379,7 +388,7 @@
         2,
         size=1 * MIB,
     )(halves[1], came)
-    sums = trade([own_sum, *sums], "pts", 2)
+    sums = shift_along([own_sum, *sums])
     spans = norb // LANES
     pair = max(1, LANES // (2 * columns))
     rows = pair * spans * 2

time: 46.2 us -> 45.5 us (0.985)
  waiting for transfers between devices: 19.9 us -> 18.8 us
  starting transfers between devices: 17.4 us -> 17.9 us
    ppermute x17 -> x14, waiting for transfers between devices: 19.9 us -> 14.8 us  [swap(): return lax.ppermute(value, axis, [(i, i ^ mask) for i in range(size)])]
    ppermute x0 -> x3, starting transfers between devices: none -> 4.92 us  [shift_along(): came.append(lax.ppermute(pieces[s], 'pts', pairs))]
    ppermute x17 -> x14, starting transfers between devices: 17.4 us -> 13 us  [swap(): return lax.ppermute(value, axis, [(i, i ^ mask) for i in range(size)])]
    ppermute x0 -> x3, waiting for transfers between devices: none -> 4 us  [shift_along(): came.append(lax.ppermute(pieces[s], 'pts', pairs))]
where the time goes in v15:
time: 45.5 us; the launch traced here: 45.4 us
  waiting for transfers between devices  18.8 us (41%)
  starting transfers between devices  17.9 us (39%)
  Pallas kernels  8.62 us (19%)
    ppermute x14, waiting for transfers between devices, swap(): return lax.ppermute(value, axis, [(i, i ^ mask) for i in range(size)])  14.8 us
    ppermute x14, starting transfers between devices, swap(): return lax.ppermute(value, axis, [(i, i ^ mask) for i in range(size)])  13 us
    ppermute x3, starting transfers between devices, shift_along(): came.append(lax.ppermute(pieces[s], 'pts', pairs))  4.92 us
    ppermute x3, waiting for transfers between devices, shift_along(): came.append(lax.ppermute(pieces[s], 'pts', pairs))  4 us
    pallas_call x1, Pallas kernels, body(): call(functools.partial(edge_kernel, per_block), [shape((local_k * 2 * per...  2.63 us
    pallas_call x2, Pallas kernels, body(): call(functools.partial(weight_kernel, shares, flip, out_rows), shape((chu...  2.33 us
    pallas_call x1, Pallas kernels, body(): call(functools.partial(exchange_kernel, chunks, 1.0 / math.sqrt(points *...  1.66 us
    pallas_call x1, Pallas kernels, body(): call(functools.partial(tile_kernel, shares, per_share, per_block), [both]...  1.38 us
  transfers between devices with their start and end apart: 17, of which 14 were waited for; matrix products, arithmetic and copies ran while one was open for 0% of the time, Pallas kernels for 3%

profile of v15, /device:TPU:0, one launch (start us, length us, event | category | flops | bytes accessed | tf_op | source)
XLA Modules:
  0.0 45.4 jit_solution(12166443762559764409)
XLA Ops:
  0.0 2.6 %shard_map.55 = (bf16[64,512]{1,0:T(8,128)(2,1)S(1)}, bf16[8,2,512,256]{3,2,1,0:T(8,128)(2,1)S(1)}) custom-call(bf16[8,2,512,256]{3,2,1,0:T(8,128)(2,1)} %orb_hbm.1), custom_call_target="tpu_custom_call" | custom-call | bytes 8388608 | tf_op jit(solution)/shard_map/pallas_call | solution.py:323
  2.6 5.1 %collective-permute-start.5 = (bf16[64,512]{1,0:T(8,128)(2,1)S(1)}, bf16[64,512]{1,0:T(8,128)(2,1)S(1)}, u32[]{:S(2)}, u32[]{:S(2)}) collective-permute-start(bf16[64,512]{1,0:T(8,128)(2,1)S(1)} %get-tuple-element.20.refs_0_), channel_id=1, source_target_pairs={{0,6},{1,7},{2,4},{3,5},{4,2},{5,3},{6,0},{7,1},{8,14},{9,15},{10,... | collective-permute-start | bytes 196616 | tf_op jit(solution)/shard_map/ppermute | solution.py:295
  7.8 0.6 %collective-permute-start.1 = (bf16[64,512]{1,0:T(8,128)(2,1)S(1)}, bf16[64,512]{1,0:T(8,128)(2,1)S(1)}, u32[]{:S(2)}, u32[]{:S(2)}) collective-permute-start(bf16[64,512]{1,0:T(8,128)(2,1)S(1)} %get-tuple-element.20.refs_0_), channel_id=1, source_target_pairs={{0,4},{1,5},{2,6},{3,7},{4,0},{5,1},{6,2},{7,3},{8,12},{9,13},{10,... | collective-permute-start | bytes 196616 | tf_op jit(solution)/shard_map/ppermute | solution.py:295
  8.4 2.3 %collective-permute-done.5.refs_6_ = bf16[64,512]{1,0:T(8,128)(2,1)S(1)} collective-permute-done((bf16[64,512]{1,0:T(8,128)(2,1)S(1)}, bf16[64,512]{1,0:T(8,128)(2,1)S(1)}, u32[]{:S(2)}, u32[]{:S(2)}) %collective-permute-start.5) | collective-permute-done | bytes 65568 | tf_op jit(solution)/shard_map/ppermute | solution.py:295
  10.7 1.8 %collective-permute-done.3.refs_4_ = bf16[64,512]{1,0:T(8,128)(2,1)S(1)} collective-permute-done((bf16[64,512]{1,0:T(8,128)(2,1)S(1)}, bf16[64,512]{1,0:T(8,128)(2,1)S(1)}, u32[]{:S(2)}, u32[]{:S(2)}) %collective-permute-start.3) | collective-permute-done | bytes 65568 | tf_op jit(solution)/shard_map/ppermute | solution.py:295
  12.4 1.0 %collective-permute-done.1.refs_2_ = bf16[64,512]{1,0:T(8,128)(2,1)S(1)} collective-permute-done((bf16[64,512]{1,0:T(8,128)(2,1)S(1)}, bf16[64,512]{1,0:T(8,128)(2,1)S(1)}, u32[]{:S(2)}, u32[]{:S(2)}) %collective-permute-start.1) | collective-permute-done | bytes 65568 | tf_op jit(solution)/shard_map/ppermute | solution.py:295
  13.4 0.3 collective-permute-done.4.refs_5_
  13.7 1.0 %collective-permute-done.2.refs_3_ = bf16[64,512]{1,0:T(8,128)(2,1)S(1)} collective-permute-done((bf16[64,512]{1,0:T(8,128)(2,1)S(1)}, bf16[64,512]{1,0:T(8,128)(2,1)S(1)}, u32[]{:S(2)}, u32[]{:S(2)}) %collective-permute-start.2) | collective-permute-done | bytes 65568 | tf_op jit(solution)/shard_map/ppermute | solution.py:295
  14.7 1.4 %shard_map.56 = (bf16[192,256]{1,0:T(8,128)(2,1)S(1)}, bf16[192,256]{1,0:T(8,128)(2,1)S(1)}, bf16[192,256]{1,0:T(8,128)(2,1)S(1)}, bf16[192,256]{1,0:T(8,128)(2,1)S(1)}, bf16[4,8,16,1024]{3,2,1,0:T(8,128)(2,1)S(1)}) custom-call(bf16[64,512]{1,0:T(8,128)(2,1)S(1)} %get-tuple-element.20.refs_0_, bf16[64,512]{1,0:T(8,128)(2,1)S(1)} %collective-permute-done.refs_1_, ...), custom_call_target="tpu_custom_call" | custom-call | bytes 6291456 | tf_op jit(solution)/shard_map/pallas_call | solution.py:346
  16.1 2.5 %collective-permute-start.7 = (bf16[192,256]{1,0:T(8,128)(2,1)S(1)}, bf16[192,256]{1,0:T(8,128)(2,1)S(1)}, u32[]{:S(2)}, u32[]{:S(2)}) collective-permute-start(bf16[192,256]{1,0:T(8,128)(2,1)S(1)} %get-tuple-element.22), channel_id=1, source_target_pairs={{0,24},{8,16},{16,8},{24,0},{1,25},{9,17},{17,9},{25,1},{2,26},{10... | collective-permute-start | bytes 294920 | tf_op jit(solution)/shard_map/ppermute | solution.py:295
  18.6 0.5 %collective-permute-start.8 = (bf16[192,256]{1,0:T(8,128)(2,1)S(1)}, bf16[192,256]{1,0:T(8,128)(2,1)S(1)}, u32[]{:S(2)}, u32[]{:S(2)}) collective-permute-start(bf16[192,256]{1,0:T(8,128)(2,1)S(1)} %get-tuple-element.23), channel_id=1, source_target_pairs={{0,16},{8,24},{16,0},{24,8},{1,17},{9,25},{17,1},{25,9},{2,18},{10... | collective-permute-start | bytes 294920 | tf_op jit(solution)/shard_map/ppermute | solution.py:295
  19.1 0.5 %collective-permute-start.9 = (bf16[192,256]{1,0:T(8,128)(2,1)S(1)}, bf16[192,256]{1,0:T(8,128)(2,1)S(1)}, u32[]{:S(2)}, u32[]{:S(2)}) collective-permute-start(bf16[192,256]{1,0:T(8,128)(2,1)S(1)} %get-tuple-element.24), channel_id=1, source_target_pairs={{0,8},{8,0},{16,24},{24,16},{1,9},{9,1},{17,25},{25,17},{2,10},{10... | collective-permute-start | bytes 294920 | tf_op jit(solution)/shard_map/ppermute | solution.py:295
  19.6 2.4 %collective-permute-done.7.refs_0_ = bf16[192,256]{1,0:T(8,128)(2,1)S(1)} collective-permute-done((bf16[192,256]{1,0:T(8,128)(2,1)S(1)}, bf16[192,256]{1,0:T(8,128)(2,1)S(1)}, u32[]{:S(2)}, u32[]{:S(2)}) %collective-permute-start.7) | collective-permute-done | bytes 98336 | tf_op jit(solution)/shard_map/ppermute | solution.py:295
  22.0 2.0 %collective-permute-done.8.refs_1_ = bf16[192,256]{1,0:T(8,128)(2,1)S(1)} collective-permute-done((bf16[192,256]{1,0:T(8,128)(2,1)S(1)}, bf16[192,256]{1,0:T(8,128)(2,1)S(1)}, u32[]{:S(2)}, u32[]{:S(2)}) %collective-permute-start.8) | collective-permute-done | bytes 98336 | tf_op jit(solution)/shard_map/ppermute | solution.py:295
  24.0 0.1 collective-permute-done.9.refs_2_
  24.1 0.6 %shard_map.57 = (bf16[128,256]{1,0:T(8,128)(2,1)S(1)}, bf16[128,256]{1,0:T(8,128)(2,1)S(1)}, bf16[128,256]{1,0:T(8,128)(2,1)S(1)}, bf16[128,256]{1,0:T(8,128)(2,1)S(1)}) custom-call(bf16[192,256]{1,0:T(8,128)(2,1)S(1)} %collective-permute-done.7.refs_0_, bf16[192,256]{1,0:T(8,128)(2,1)S(1)} %collective-permute-done.8.refs_1_, ...), custom_call_target="tpu_custom_call" | custom-call | bytes 2097152 | tf_op jit(solution)/shard_map/pallas_call | solution.py:359
  24.6 1.8 %collective-permute-start.10 = (bf16[128,256]{1,0:T(8,128)(2,1)S(1)}, bf16[128,256]{1,0:T(8,128)(2,1)S(1)}, u32[]{:S(2)}, u32[]{:S(2)}) collective-permute-start(bf16[128,256]{1,0:T(8,128)(2,1)S(1)} %get-tuple-element.26), channel_id=1, source_target_pairs={{0,24},{8,16},{16,8},{24,0},{1,25},{9,17},{17,9},{25,1},{2,26},{10... | collective-permute-start | bytes 196616 | tf_op jit(solution)/shard_map/ppermute | solution.py:295
  26.4 1.3 %collective-permute-start.11 = (bf16[128,256]{1,0:T(8,128)(2,1)S(1)}, bf16[128,256]{1,0:T(8,128)(2,1)S(1)}, u32[]{:S(2)}, u32[]{:S(2)}) collective-permute-start(bf16[128,256]{1,0:T(8,128)(2,1)S(1)} %get-tuple-element.27), channel_id=1, source_target_pairs={{0,16},{8,24},{16,0},{24,8},{1,17},{9,25},{17,1},{25,9},{2,18},{10... | collective-permute-start | bytes 196616 | tf_op jit(solution)/shard_map/ppermute | solution.py:295
  27.7 0.5 %collective-permute-start.12 = (bf16[128,256]{1,0:T(8,128)(2,1)S(1)}, bf16[128,256]{1,0:T(8,128)(2,1)S(1)}, u32[]{:S(2)}, u32[]{:S(2)}) collective-permute-start(bf16[128,256]{1,0:T(8,128)(2,1)S(1)} %get-tuple-element.28), channel_id=1, source_target_pairs={{0,8},{8,0},{16,24},{24,16},{1,9},{9,1},{17,25},{25,17},{2,10},{10... | collective-permute-start | bytes 196616 | tf_op jit(solution)/shard_map/ppermute | solution.py:295
  28.2 2.1 %collective-permute-done.10.refs_0_ = bf16[128,256]{1,0:T(8,128)(2,1)S(1)} collective-permute-done((bf16[128,256]{1,0:T(8,128)(2,1)S(1)}, bf16[128,256]{1,0:T(8,128)(2,1)S(1)}, u32[]{:S(2)}, u32[]{:S(2)}) %collective-permute-start.10) | collective-permute-done | bytes 65568 | tf_op jit(solution)/shard_map/ppermute | solution.py:295
  30.3 0.5 %collective-permute-done.11.refs_1_ = bf16[128,256]{1,0:T(8,128)(2,1)S(1)} collective-permute-done((bf16[128,256]{1,0:T(8,128)(2,1)S(1)}, bf16[128,256]{1,0:T(8,128)(2,1)S(1)}, u32[]{:S(2)}, u32[]{:S(2)}) %collective-permute-start.11) | collective-permute-done | bytes 65568 | tf_op jit(solution)/shard_map/ppermute | solution.py:295
  30.9 1.1 %collective-permute-done.12.refs_2_ = bf16[128,256]{1,0:T(8,128)(2,1)S(1)} collective-permute-done((bf16[128,256]{1,0:T(8,128)(2,1)S(1)}, bf16[128,256]{1,0:T(8,128)(2,1)S(1)}, u32[]{:S(2)}, u32[]{:S(2)}) %collective-permute-start.12) | collective-permute-done | bytes 65568 | tf_op jit(solution)/shard_map/ppermute | solution.py:295
  32.0 1.2 %shard_map.59 = bf16[4,64,512]{2,1,0:T(8,128)(2,1)S(1)} custom-call(bf16[128,256]{1,0:T(8,128)(2,1)S(1)} %collective-permute-done.10.refs_0_, bf16[128,256]{1,0:T(8,128)(2,1)S(1)} %collective-permute-done.11.refs_1_, bf16[128,256]{1,0:T(8,128)(2,1)S(1)} %collective-permute-done.12.refs_2_, bf16[128,256]{1,0:T(8,128)(2,1)S(1)} %get-tuple-element.29.refs_3_, ...), custom_call_target="tpu_custom_call" | custom-call | bytes 6291456 | tf_op jit(solution)/shard_map/pallas_call | solution.py:376
  33.2 0.1 collective-permute-start.13
  33.2 1.2 %shard_map.58.keep_ref = f32[4,64,512]{2,1,0:T(8,128)S(1)} custom-call(bf16[128,256]{1,0:T(8,128)(2,1)S(1)} %collective-permute-done.10.refs_0_, bf16[128,256]{1,0:T(8,128)(2,1)S(1)} %collective-permute-done.11.refs_1_, bf16[128,256]{1,0:T(8,128)(2,1)S(1)} %collective-permute-done.12.refs_2_, bf16[128,256]{1,0:T(8,128)(2,1)S(1)} %get-tuple-element.29.refs_3_, ...), custom_call_target="tpu_custom_call" | custom-call | bytes 6291456 | tf_op jit(solution)/shard_map/pallas_call | solution.py:376
  34.4 0.4 collective-permute-done.13.came_ref
  34.8 1.6 %collective-permute-start.14 = (bf16[64,512]{1,0:T(8,128)(2,1)S(1)}, bf16[64,512]{1,0:T(8,128)(2,1)S(1)}, u32[]{:S(2)}, u32[]{:S(2)}) collective-permute-start(bf16[64,512]{1,0:T(8,128)(2,1)S(1)} %get-tuple-element.30), channel_id=1, source_target_pairs={{0,2},{1,3},{2,4},{3,5},{4,6},{5,7},{6,0},{7,1},{8,10},{9,11},{10,... | collective-permute-start | bytes 196616 | tf_op jit(solution)/shard_map/ppermute | solution.py:307
  36.4 1.2 %collective-permute-start.15 = (bf16[64,512]{1,0:T(8,128)(2,1)S(1)}, bf16[64,512]{1,0:T(8,128)(2,1)S(1)}, u32[]{:S(2)}, u32[]{:S(2)}) collective-permute-start(bf16[64,512]{1,0:T(8,128)(2,1)S(1)} %get-tuple-element.31), channel_id=1, source_target_pairs={{0,4},{1,5},{2,6},{3,7},{4,0},{5,1},{6,2},{7,3},{8,12},{9,13},{10,... | collective-permute-start | bytes 196616 | tf_op jit(solution)/shard_map/ppermute | solution.py:307
  37.6 2.1 %collective-permute-start.16 = (bf16[64,512]{1,0:T(8,128)(2,1)S(1)}, bf16[64,512]{1,0:T(8,128)(2,1)S(1)}, u32[]{:S(2)}, u32[]{:S(2)}) collective-permute-start(bf16[64,512]{1,0:T(8,128)(2,1)S(1)} %get-tuple-element.32), channel_id=1, source_target_pairs={{0,6},{1,7},{2,0},{3,1},{4,2},{5,3},{6,4},{7,5},{8,14},{9,15},{10,... | collective-permute-start | bytes 196616 | tf_op jit(solution)/shard_map/ppermute | solution.py:307
  39.7 1.9 %collective-permute-done.14.refs_0_ = bf16[64,512]{1,0:T(8,128)(2,1)S(1)} collective-permute-done((bf16[64,512]{1,0:T(8,128)(2,1)S(1)}, bf16[64,512]{1,0:T(8,128)(2,1)S(1)}, u32[]{:S(2)}, u32[]{:S(2)}) %collective-permute-start.14) | collective-permute-done | bytes 65568 | tf_op jit(solution)/shard_map/ppermute | solution.py:307
  41.6 2.1 %collective-permute-done.15.refs_1_ = bf16[64,512]{1,0:T(8,128)(2,1)S(1)} collective-permute-done((bf16[64,512]{1,0:T(8,128)(2,1)S(1)}, bf16[64,512]{1,0:T(8,128)(2,1)S(1)}, u32[]{:S(2)}, u32[]{:S(2)}) %collective-permute-start.15) | collective-permute-done | bytes 65568 | tf_op jit(solution)/shard_map/ppermute | solution.py:307
  43.7 1.7 %shard_map.61 = bf16[64,4,16,128]{3,2,1,0:T(8,128)(2,1)} custom-call(bf16[64,512]{1,0:T(8,128)(2,1)S(1)} %collective-permute-done.14.refs_0_, bf16[64,512]{1,0:T(8,128)(2,1)S(1)} %collective-permute-done.15.refs_1_, bf16[64,512]{1,0:T(8,128)(2,1)S(1)} %collective-permute-done.16.refs_2_, f32[64,512]{1,0:T(8,128)S(1)} %get-tuple-element.33.refs_3_, ...), custom_call_target="tpu_custom_call" | custom-call | bytes 4194304 | tf_op jit(solution)/shard_map/pallas_call | solution.py:395
  (17 shorter events, 0.1 us)
Async XLA Ops:
  0.0 14.7 %copy-start.1 = (bf16[2,64,32]{2,1,0:T(8,128)(2,1)S(1)}, bf16[2,64,32]{2,1,0:T(8,128)(2,1)}, u32[]{:S(2)}) copy-start(bf16[2,64,32]{2,1,0:T(8,128)(2,1)} %constant.6.clone.refs_9_) | copy-start | bytes 24580
  0.0 24.0 %copy-start.2 = (bf16[64,128]{1,0:T(8,128)(2,1)S(1)}, bf16[64,128]{1,0:T(8,128)(2,1)}, u32[]{:S(2)}) copy-start(bf16[64,128]{1,0:T(8,128)(2,1)} %constant.8.clone.refs_5_) | copy-start | bytes 49156
  0.0 24.0 %copy-start.3 = (bf16[64,128]{1,0:T(8,128)(2,1)S(1)}, bf16[64,128]{1,0:T(8,128)(2,1)}, u32[]{:S(2)}) copy-start(bf16[64,128]{1,0:T(8,128)(2,1)} %constant.7.clone.refs_4_) | copy-start | bytes 49156
  0.0 14.7 %copy-start = (bf16[8,32,256]{2,1,0:T(8,128)(2,1)S(1)}, bf16[8,32,256]{2,1,0:T(8,128)(2,1)}, u32[]{:S(2)}) copy-start(bf16[8,32,256]{2,1,0:T(8,128)(2,1)} %refs_10_.1) | copy-start | bytes 393220
  2.6 8.0 %collective-permute-start.5 = (bf16[64,512]{1,0:T(8,128)(2,1)S(1)}, bf16[64,512]{1,0:T(8,128)(2,1)S(1)}, u32[]{:S(2)}, u32[]{:S(2)}) collective-permute-start(bf16[64,512]{1,0:T(8,128)(2,1)S(1)} %get-tuple-element.20.refs_0_), channel_id=1, source_target_pairs={{0,6},{1,7},{2,4},{3,5},{4,2},{5,3},{6,0},{7,1},{8,14},{9,15},{10,... | collective-permute-start | bytes 196616 | tf_op jit(solution)/shard_map/ppermute | solution.py:295
  7.8 4.7 %collective-permute-start.3 = (bf16[64,512]{1,0:T(8,128)(2,1)S(1)}, bf16[64,512]{1,0:T(8,128)(2,1)S(1)}, u32[]{:S(2)}, u32[]{:S(2)}) collective-permute-start(bf16[64,512]{1,0:T(8,128)(2,1)S(1)} %get-tuple-element.20.refs_0_), channel_id=1, source_target_pairs={{0,2},{1,3},{2,0},{3,1},{4,6},{5,7},{6,4},{7,5},{8,10},{9,11},{10,... | collective-permute-start | bytes 196616 | tf_op jit(solution)/shard_map/ppermute | solution.py:295
  7.8 5.6 %collective-permute-start.1 = (bf16[64,512]{1,0:T(8,128)(2,1)S(1)}, bf16[64,512]{1,0:T(8,128)(2,1)S(1)}, u32[]{:S(2)}, u32[]{:S(2)}) collective-permute-start(bf16[64,512]{1,0:T(8,128)(2,1)S(1)} %get-tuple-element.20.refs_0_), channel_id=1, source_target_pairs={{0,4},{1,5},{2,6},{3,7},{4,0},{5,1},{6,2},{7,3},{8,12},{9,13},{10,... | collective-permute-start | bytes 196616 | tf_op jit(solution)/shard_map/ppermute | solution.py:295
  8.4 5.0 %collective-permute-start = (bf16[64,512]{1,0:T(8,128)(2,1)S(1)}, bf16[64,512]{1,0:T(8,128)(2,1)S(1)}, u32[]{:S(2)}, u32[]{:S(2)}) collective-permute-start(bf16[64,512]{1,0:T(8,128)(2,1)S(1)} %get-tuple-element.20.refs_0_), channel_id=1, source_target_pairs={{0,1},{1,0},{2,3},{3,2},{4,5},{5,4},{6,7},{7,6},{8,9},{9,8},{10,11... | collective-permute-start | bytes 196616 | tf_op jit(solution)/shard_map/ppermute | solution.py:295
  10.7 2.7 %collective-permute-start.6 = (bf16[64,512]{1,0:T(8,128)(2,1)S(1)}, bf16[64,512]{1,0:T(8,128)(2,1)S(1)}, u32[]{:S(2)}, u32[]{:S(2)}) collective-permute-start(bf16[64,512]{1,0:T(8,128)(2,1)S(1)} %collective-permute-done.5.refs_6_), channel_id=1, source_target_pairs={{0,1},{1,0},{2,3},{3,2},{4,5},{5,4},{6,7},{7,6},{8,9},{9,8},{10,11... | collective-permute-start | bytes 196616 | tf_op jit(solution)/shard_map/ppermute | solution.py:295
  12.4 1.3 %collective-permute-start.4 = (bf16[64,512]{1,0:T(8,128)(2,1)S(1)}, bf16[64,512]{1,0:T(8,128)(2,1)S(1)}, u32[]{:S(2)}, u32[]{:S(2)}) collective-permute-start(bf16[64,512]{1,0:T(8,128)(2,1)S(1)} %collective-permute-done.3.refs_4_), channel_id=1, source_target_pairs={{0,1},{1,0},{2,3},{3,2},{4,5},{5,4},{6,7},{7,6},{8,9},{9,8},{10,11... | collective-permute-start | bytes 196616 | tf_op jit(solution)/shard_map/ppermute | solution.py:295
  13.4 1.3 %collective-permute-start.2 = (bf16[64,512]{1,0:T(8,128)(2,1)S(1)}, bf16[64,512]{1,0:T(8,128)(2,1)S(1)}, u32[]{:S(2)}, u32[]{:S(2)}) collective-permute-start(bf16[64,512]{1,0:T(8,128)(2,1)S(1)} %collective-permute-done.1.refs_2_), channel_id=1, source_target_pairs={{0,1},{1,0},{2,3},{3,2},{4,5},{5,4},{6,7},{7,6},{8,9},{9,8},{10,11... | collective-permute-start | bytes 196616 | tf_op jit(solution)/shard_map/ppermute | solution.py:295
  16.1 5.9 %collective-permute-start.7 = (bf16[192,256]{1,0:T(8,128)(2,1)S(1)}, bf16[192,256]{1,0:T(8,128)(2,1)S(1)}, u32[]{:S(2)}, u32[]{:S(2)}) collective-permute-start(bf16[192,256]{1,0:T(8,128)(2,1)S(1)} %get-tuple-element.22), channel_id=1, source_target_pairs={{0,24},{8,16},{16,8},{24,0},{1,25},{9,17},{17,9},{25,1},{2,26},{10... | collective-permute-start | bytes 294920 | tf_op jit(solution)/shard_map/ppermute | solution.py:295
  18.6 5.4 %collective-permute-start.8 = (bf16[192,256]{1,0:T(8,128)(2,1)S(1)}, bf16[192,256]{1,0:T(8,128)(2,1)S(1)}, u32[]{:S(2)}, u32[]{:S(2)}) collective-permute-start(bf16[192,256]{1,0:T(8,128)(2,1)S(1)} %get-tuple-element.23), channel_id=1, source_target_pairs={{0,16},{8,24},{16,0},{24,8},{1,17},{9,25},{17,1},{25,9},{2,18},{10... | collective-permute-start | bytes 294920 | tf_op jit(solution)/shard_map/ppermute | solution.py:295
  19.1 5.0 %collective-permute-start.9 = (bf16[192,256]{1,0:T(8,128)(2,1)S(1)}, bf16[192,256]{1,0:T(8,128)(2,1)S(1)}, u32[]{:S(2)}, u32[]{:S(2)}) collective-permute-start(bf16[192,256]{1,0:T(8,128)(2,1)S(1)} %get-tuple-element.24), channel_id=1, source_target_pairs={{0,8},{8,0},{16,24},{24,16},{1,9},{9,1},{17,25},{25,17},{2,10},{10... | collective-permute-start | bytes 294920 | tf_op jit(solution)/shard_map/ppermute | solution.py:295
  24.6 5.7 %collective-permute-start.10 = (bf16[128,256]{1,0:T(8,128)(2,1)S(1)}, bf16[128,256]{1,0:T(8,128)(2,1)S(1)}, u32[]{:S(2)}, u32[]{:S(2)}) collective-permute-start(bf16[128,256]{1,0:T(8,128)(2,1)S(1)} %get-tuple-element.26), channel_id=1, source_target_pairs={{0,24},{8,16},{16,8},{24,0},{1,25},{9,17},{17,9},{25,1},{2,26},{10... | collective-permute-start | bytes 196616 | tf_op jit(solution)/shard_map/ppermute | solution.py:295
  26.4 4.5 %collective-permute-start.11 = (bf16[128,256]{1,0:T(8,128)(2,1)S(1)}, bf16[128,256]{1,0:T(8,128)(2,1)S(1)}, u32[]{:S(2)}, u32[]{:S(2)}) collective-permute-start(bf16[128,256]{1,0:T(8,128)(2,1)S(1)} %get-tuple-element.27), channel_id=1, source_target_pairs={{0,16},{8,24},{16,0},{24,8},{1,17},{9,25},{17,1},{25,9},{2,18},{10... | collective-permute-start | bytes 196616 | tf_op jit(solution)/shard_map/ppermute | solution.py:295
  27.7 4.3 %collective-permute-start.12 = (bf16[128,256]{1,0:T(8,128)(2,1)S(1)}, bf16[128,256]{1,0:T(8,128)(2,1)S(1)}, u32[]{:S(2)}, u32[]{:S(2)}) collective-permute-start(bf16[128,256]{1,0:T(8,128)(2,1)S(1)} %get-tuple-element.28), channel_id=1, source_target_pairs={{0,8},{8,0},{16,24},{24,16},{1,9},{9,1},{17,25},{25,17},{2,10},{10... | collective-permute-start | bytes 196616 | tf_op jit(solution)/shard_map/ppermute | solution.py:295
  33.2 1.6 %collective-permute-start.13 = (bf16[4,64,512]{2,1,0:T(8,128)(2,1)S(1)}, bf16[4,64,512]{2,1,0:T(8,128)(2,1)S(1)}, u32[]{:S(2)}, u32[]{:S(2)}) collective-permute-start(bf16[4,64,512]{2,1,0:T(8,128)(2,1)S(1)} %shard_map.59), channel_id=1, source_target_pairs={{0,1},{1,0},{2,3},{3,2},{4,5},{5,4},{6,7},{7,6},{8,9},{9,8},{10,11... | collective-permute-start | bytes 786440 | tf_op jit(solution)/shard_map/ppermute | solution.py:295
  34.8 6.8 %collective-permute-start.14 = (bf16[64,512]{1,0:T(8,128)(2,1)S(1)}, bf16[64,512]{1,0:T(8,128)(2,1)S(1)}, u32[]{:S(2)}, u32[]{:S(2)}) collective-permute-start(bf16[64,512]{1,0:T(8,128)(2,1)S(1)} %get-tuple-element.30), channel_id=1, source_target_pairs={{0,2},{1,3},{2,4},{3,5},{4,6},{5,7},{6,0},{7,1},{8,10},{9,11},{10,... | collective-permute-start | bytes 196616 | tf_op jit(solution)/shard_map/ppermute | solution.py:307
  36.4 7.3 %collective-permute-start.15 = (bf16[64,512]{1,0:T(8,128)(2,1)S(1)}, bf16[64,512]{1,0:T(8,128)(2,1)S(1)}, u32[]{:S(2)}, u32[]{:S(2)}) collective-permute-start(bf16[64,512]{1,0:T(8,128)(2,1)S(1)} %get-tuple-element.31), channel_id=1, source_target_pairs={{0,4},{1,5},{2,6},{3,7},{4,0},{5,1},{6,2},{7,3},{8,12},{9,13},{10,... | collective-permute-start | bytes 196616 | tf_op jit(solution)/shard_map/ppermute | solution.py:307
  37.6 6.1 %collective-permute-start.16 = (bf16[64,512]{1,0:T(8,128)(2,1)S(1)}, bf16[64,512]{1,0:T(8,128)(2,1)S(1)}, u32[]{:S(2)}, u32[]{:S(2)}) collective-permute-start(bf16[64,512]{1,0:T(8,128)(2,1)S(1)} %get-tuple-element.32), channel_id=1, source_target_pairs={{0,6},{1,7},{2,0},{3,1},{4,2},{5,3},{6,4},{7,5},{8,14},{9,15},{10,... | collective-permute-start | bytes 196616 | tf_op jit(solution)/shard_map/ppermute | solution.py:307

commit v16 on v15

--- a/solution.py
+++ b/solution.py
@@ -89,25 +89,39 @@
     )
 
 
+def load_copies(orb_hbm, orb_ref, sems, start):
+    lanes = pl.ds(start, orb_ref.shape[3])
+    copies = [
+        pltpu.make_async_copy(orb_hbm.at[k, :, :, lanes], orb_ref.at[k], sems.at[k])
+        for k in range(orb_ref.shape[0])
+    ]
+    for copy in copies:
+        copy.start()
+    return copies
+
+
+def rest_kernel(orb_hbm, edge_hbm, pass_ref, orb_ref, sems, pass_sem):
+    copies = load_copies(orb_hbm, orb_ref, sems, LANES)
+    copies.append(pltpu.make_async_copy(edge_hbm, pass_ref, pass_sem))
+    copies[-1].start()
+    for copy in copies:
+        copy.wait()
+
+
 def edge_kernel(per_block, orb_hbm, edge_ref, orb_ref, sems):
     local_k = orb_hbm.shape[0]
-    copies = [pltpu.make_async_copy(orb_hbm.at[k], orb_ref.at[k], sems.at[k]) for k in range(local_k)]
-    for copy in copies:
-        copy.start()
-    row = lax.broadcasted_iota(jnp.int32, (2 * per_block, LANES), 0)
-    lane = lax.broadcasted_iota(jnp.int32, (2 * per_block, LANES), 1)
-    one, zero = jnp.ones(row.shape, F32), jnp.zeros(row.shape, F32)
-    first = jnp.where((row < per_block) & (row == lane), one, zero).astype(BF16)
-    second = jnp.where((row >= per_block) & (row == lane + per_block), one, zero).astype(BF16)
+    copies = load_copies(orb_hbm, orb_ref, sems, 0)
+    row = lax.broadcasted_iota(jnp.int32, (2 * per_block, 2 * LANES), 0)
+    lane = lax.broadcasted_iota(jnp.int32, (2 * per_block, 2 * LANES), 1)
+    column = jnp.where(row < per_block, row, row - per_block + LANES)
+    chosen = jnp.where(lane == column, jnp.ones(row.shape, F32), jnp.zeros(row.shape, F32)).astype(BF16)
     group = ROWS // (2 * per_block)
     for g in range(local_k // group):
         rows = []
         for k in range(g * group, (g + 1) * group):
             copies[k].wait()
-            rows.append(
-                dot(first, orb_ref[k, 0, :, :LANES], ((1,), (1,)))
-                + dot(second, orb_ref[k, 1, :, :LANES], ((1,), (1,)))
-            )
+            both = jnp.concatenate([orb_ref[k, 0], orb_ref[k, 1]], axis=1)
+            rows.append(dot(chosen, both, ((1,), (1,))))
         edge_ref[g * ROWS : (g + 1) * ROWS] = jnp.concatenate(rows, axis=0).astype(BF16)
 
 
@@ -120,9 +134,9 @@
 
 
 def tile_kernel(shares, per_share, per_block, *refs):
-    blocks, (orb_ref, sel_ref, coulomb_ref) = refs[: shares * per_share], refs[shares * per_share :][:3]
-    *outs, form_ref, wide, cells = refs[shares * per_share + 3 :]
-    local_k, _, norb, points = orb_ref.shape
+    blocks, (orb_ref, rest_ref, sel_ref, coulomb_ref) = refs[: shares * per_share], refs[shares * per_share :][:4]
+    *outs, form_ref, wide, cells = refs[shares * per_share + 4 :]
+    local_k, _, norb, _ = orb_ref.shape
     group = ROWS // (2 * per_block)
     share = per_share * per_block
     rows = 2 * share
@@ -148,7 +162,8 @@
             form = jnp.concatenate(
                 [jnp.concatenate(left, axis=0), jnp.concatenate(right, axis=0)], axis=1
             )
-            tile = dot(form, orb_ref[k].reshape(2 * norb, points))
+            halves = [ref[k].reshape(2 * norb, ref.shape[3]) for ref in (orb_ref, rest_ref)]
+            tile = dot(form, jnp.concatenate(halves, axis=1))
             for offset in range(shares):
                 form_ref[jnp.bitwise_xor(plane, offset), k] = form[offset * rows : (offset + 1) * rows]
                 for part in range(2):
@@ -197,8 +212,8 @@
 
 
 def weight_kernel(shares, flip, out_rows, *refs):
-    pieces, orb_ref, out_ref, gathered = refs[:shares][::-1], refs[shares], refs[shares + 1], refs[shares + 2]
-    local_k, _, norb, points = orb_ref.shape
+    pieces, (orb_ref, rest_ref, out_ref, gathered) = refs[:shares][::-1], refs[shares:]
+    local_k, _, norb, _ = orb_ref.shape
     total_rows = gathered.shape[1]
     half = total_rows // local_k // 2
     me = lax.axis_index("ka")
@@ -229,7 +244,13 @@
         for z in range(chunks):
             start = pl.multiple_of((2 * z + core) * out_rows, out_rows)
             rows = jnp.concatenate(
-                [orb_ref[k, part, pl.ds(start, out_rows), :] for k in left for part in range(2)], axis=1
+                [
+                    ref[k, part, pl.ds(start, out_rows), :]
+                    for k in left
+                    for part in range(2)
+                    for ref in (orb_ref, rest_ref)
+                ],
+                axis=1,
             )
             out_ref[z, :, g * group * lanes : (g + 1) * group * lanes] = dot(
                 rows, right, ((1,), (1,))
@@ -320,17 +341,29 @@
     group = ROWS // (2 * per_block)
     shape = jax.ShapeDtypeStruct
 
-    edge, orbitals = call(
+    edge, first = call(
         functools.partial(edge_kernel, per_block),
-        [shape((local_k * 2 * per_block, norb), BF16), shape(orbitals.shape, BF16)],
+        [
+            shape((local_k * 2 * per_block, norb), BF16),
+            shape((local_k, 2, norb, LANES), BF16),
+        ],
         0,
         [pltpu.SemaphoreType.DMA((local_k,))],
-        limit=47,
-        size=8 * MIB,
+        limit=50,
+        size=4 * MIB,
         unread=1,
     )(orbitals)
+    passed_edge, rest = call(
+        rest_kernel,
+        [shape(edge.shape, BF16), shape((local_k, 2, norb, points - LANES), BF16)],
+        0,
+        [pltpu.SemaphoreType.DMA((local_k,)), pltpu.SemaphoreType.DMA],
+        limit=49,
+        size=4 * MIB,
+        unread=2,
+    )(orbitals, edge)
     per_share = blocks // shares
-    partner = swap(edge, "pts", 1)
+    partner = swap(passed_edge, "pts", 1)
     came = [edge, partner] + [swap(edge, "pts", 2 * e + c) for e in range(1, per_share // 2) for c in range(2)]
     came = {0: came}
     for offset in asked(shares):
@@ -346,13 +379,13 @@
     *tiles, forms = call(
         functools.partial(tile_kernel, shares, per_share, per_block),
         [both] * shares + [shape((shares, local_k, 2 * share, 2 * norb), BF16)],
-        blocks + 3,
+        blocks + 4,
         [
             tiled(shares * share * 2 * local_k, points),
             pltpu.VMEM(coulomb.shape, F32),
         ],
         size=6 * MIB,
-    )(*[block for offset in [0, *asked(shares)] for block in came[offset]], orbitals, selector, coulomb)
+    )(*[block for offset in [0, *asked(shares)] for block in came[offset]], first, rest, selector, coulomb)
     tiles = trade(tiles, "ka", 1)
 
     forward, backward = phase_tables(total)
@@ -376,10 +409,10 @@
             call(
                 functools.partial(weight_kernel, shares, flip, out_rows),
                 shape((chunks, out_rows, lanes), kind),
-                shares + 1,
+                shares + 2,
                 [pltpu.VMEM((shares, share * 2 * local_k, points), BF16)],
                 size=6 * MIB,
-            )(*kernels, orbitals)
+            )(*kernels, first, rest)
         )
     came = swap(halves[0], "pts", 1)
     own_sum, *sums = call(

time: 45.5 us -> 45.4 us (level)
  waiting for transfers between devices: 18.8 us -> 17.1 us
  Pallas kernels: 8.62 us -> 10.1 us
    ppermute x14, waiting for transfers between devices: 14.8 us -> 13.1 us  [swap(): return lax.ppermute(value, axis, [(i, i ^ mask) for i in range(size)])]
    pallas_call x0 -> x1, Pallas kernels: none -> 1.58 us  [body(): call(rest_kernel, [shape(edge.shape, BF16), shape((local_k, 2, norb, poin...]
  transfers between devices with their start and end apart: 17 -> 17, of which waited for: 14 -> 14; matrix products, arithmetic and copies ran while one was open for 0% -> 0% of each run, Pallas kernels for 3% -> 6%
where the time goes in v16:
time: 45.4 us; the launch traced here: 45.3 us
  starting transfers between devices  18 us (40%)
  waiting for transfers between devices  17.1 us (38%)
  Pallas kernels  10.1 us (22%)
    ppermute x14, waiting for transfers between devices, swap(): return lax.ppermute(value, axis, [(i, i ^ mask) for i in range(size)])  13.1 us
    ppermute x14, starting transfers between devices, swap(): return lax.ppermute(value, axis, [(i, i ^ mask) for i in range(size)])  13 us
    ppermute x3, starting transfers between devices, shift_along(): came.append(lax.ppermute(pieces[s], 'pts', pairs))  4.94 us
    ppermute x3, waiting for transfers between devices, shift_along(): came.append(lax.ppermute(pieces[s], 'pts', pairs))  3.98 us
    pallas_call x1, Pallas kernels, body(): call(functools.partial(edge_kernel, per_block), [shape((local_k * 2 * per...  2.5 us
    pallas_call x2, Pallas kernels, body(): call(functools.partial(weight_kernel, shares, flip, out_rows), shape((chu...  2.33 us
    pallas_call x1, Pallas kernels, body(): call(functools.partial(exchange_kernel, chunks, 1.0 / math.sqrt(points *...  1.66 us
    pallas_call x1, Pallas kernels, body(): call(rest_kernel, [shape(edge.shape, BF16), shape((local_k, 2, norb, poin...  1.58 us
  transfers between devices with their start and end apart: 17, of which 14 were waited for; matrix products, arithmetic and copies ran while one was open for 0% of the time, Pallas kernels for 6%

profile of v16, /device:TPU:0, one launch (start us, length us, event | category | flops | bytes accessed | tf_op | source)
XLA Modules:
  0.0 45.3 jit_solution(10462728562787843414)
XLA Ops:
  0.0 2.5 %shard_map.55 = (bf16[64,512]{1,0:T(8,128)(2,1)S(1)}, bf16[8,2,512,128]{3,2,1,0:T(8,128)(2,1)S(1)}) custom-call(bf16[8,2,512,256]{3,2,1,0:T(8,128)(2,1)} %orb_hbm.3), custom_call_target="tpu_custom_call" | custom-call | bytes 4194304 | tf_op jit(solution)/shard_map/pallas_call | solution.py:344
  2.5 5.1 %collective-permute-start.5 = (bf16[64,512]{1,0:T(8,128)(2,1)S(1)}, bf16[64,512]{1,0:T(8,128)(2,1)S(1)}, u32[]{:S(2)}, u32[]{:S(2)}) collective-permute-start(bf16[64,512]{1,0:T(8,128)(2,1)S(1)} %get-tuple-element.22.edge_hbm.refs_0_), channel_id=1, source_target_pairs={{0,6},{1,7},{2,4},{3,5},{4,2},{5,3},{6,0},{7,1},{8,14},{9,15},{10,... | collective-permute-start | bytes 196616 | tf_op jit(solution)/shard_map/ppermute | solution.py:316
  7.7 0.6 %collective-permute-start.1 = (bf16[64,512]{1,0:T(8,128)(2,1)S(1)}, bf16[64,512]{1,0:T(8,128)(2,1)S(1)}, u32[]{:S(2)}, u32[]{:S(2)}) collective-permute-start(bf16[64,512]{1,0:T(8,128)(2,1)S(1)} %get-tuple-element.22.edge_hbm.refs_0_), channel_id=1, source_target_pairs={{0,4},{1,5},{2,6},{3,7},{4,0},{5,1},{6,2},{7,3},{8,12},{9,13},{10,... | collective-permute-start | bytes 196616 | tf_op jit(solution)/shard_map/ppermute | solution.py:316
  8.3 1.6 %shard_map.56 = (bf16[64,512]{1,0:T(8,128)(2,1)S(1)}, bf16[8,2,512,128]{3,2,1,0:T(8,128)(2,1)S(1)}) custom-call(bf16[8,2,512,256]{3,2,1,0:T(8,128)(2,1)} %orb_hbm.3, bf16[64,512]{1,0:T(8,128)(2,1)S(1)} %get-tuple-element.22.edge_hbm.refs_0_), custom_call_target="tpu_custom_call" | custom-call | bytes 4194304 | tf_op jit(solution)/shard_map/pallas_call | solution.py:356
  9.9 0.1 collective-permute-start
  10.0 0.6 %collective-permute-done.5.refs_6_ = bf16[64,512]{1,0:T(8,128)(2,1)S(1)} collective-permute-done((bf16[64,512]{1,0:T(8,128)(2,1)S(1)}, bf16[64,512]{1,0:T(8,128)(2,1)S(1)}, u32[]{:S(2)}, u32[]{:S(2)}) %collective-permute-start.5) | collective-permute-done | bytes 65568 | tf_op jit(solution)/shard_map/ppermute | solution.py:316
  10.6 1.8 %collective-permute-done.3.refs_4_ = bf16[64,512]{1,0:T(8,128)(2,1)S(1)} collective-permute-done((bf16[64,512]{1,0:T(8,128)(2,1)S(1)}, bf16[64,512]{1,0:T(8,128)(2,1)S(1)}, u32[]{:S(2)}, u32[]{:S(2)}) %collective-permute-start.3) | collective-permute-done | bytes 65568 | tf_op jit(solution)/shard_map/ppermute | solution.py:316
  12.3 1.0 %collective-permute-done.1.refs_2_ = bf16[64,512]{1,0:T(8,128)(2,1)S(1)} collective-permute-done((bf16[64,512]{1,0:T(8,128)(2,1)S(1)}, bf16[64,512]{1,0:T(8,128)(2,1)S(1)}, u32[]{:S(2)}, u32[]{:S(2)}) %collective-permute-start.1) | collective-permute-done | bytes 65568 | tf_op jit(solution)/shard_map/ppermute | solution.py:316
  13.3 0.3 collective-permute-done.4.refs_5_
  13.6 1.0 %collective-permute-done.2.refs_3_ = bf16[64,512]{1,0:T(8,128)(2,1)S(1)} collective-permute-done((bf16[64,512]{1,0:T(8,128)(2,1)S(1)}, bf16[64,512]{1,0:T(8,128)(2,1)S(1)}, u32[]{:S(2)}, u32[]{:S(2)}) %collective-permute-start.2) | collective-permute-done | bytes 65568 | tf_op jit(solution)/shard_map/ppermute | solution.py:316
  14.6 1.4 %shard_map.57 = (bf16[192,256]{1,0:T(8,128)(2,1)S(1)}, bf16[192,256]{1,0:T(8,128)(2,1)S(1)}, bf16[192,256]{1,0:T(8,128)(2,1)S(1)}, bf16[192,256]{1,0:T(8,128)(2,1)S(1)}, bf16[4,8,16,1024]{3,2,1,0:T(8,128)(2,1)S(1)}) custom-call(bf16[64,512]{1,0:T(8,128)(2,1)S(1)} %get-tuple-element.22.edge_hbm.refs_0_, bf16[64,512]{1,0:T(8,128)(2,1)S(1)} %collective-permute-done.refs_1_, ...), custom_call_target="tpu_custom_call" | custom-call | bytes 6291456 | tf_op jit(solution)/shard_map/pallas_call | solution.py:379
  15.9 2.5 %collective-permute-start.7 = (bf16[192,256]{1,0:T(8,128)(2,1)S(1)}, bf16[192,256]{1,0:T(8,128)(2,1)S(1)}, u32[]{:S(2)}, u32[]{:S(2)}) collective-permute-start(bf16[192,256]{1,0:T(8,128)(2,1)S(1)} %get-tuple-element.26), channel_id=1, source_target_pairs={{0,24},{8,16},{16,8},{24,0},{1,25},{9,17},{17,9},{25,1},{2,26},{10... | collective-permute-start | bytes 294920 | tf_op jit(solution)/shard_map/ppermute | solution.py:316
  18.5 0.5 %collective-permute-start.8 = (bf16[192,256]{1,0:T(8,128)(2,1)S(1)}, bf16[192,256]{1,0:T(8,128)(2,1)S(1)}, u32[]{:S(2)}, u32[]{:S(2)}) collective-permute-start(bf16[192,256]{1,0:T(8,128)(2,1)S(1)} %get-tuple-element.27), channel_id=1, source_target_pairs={{0,16},{8,24},{16,0},{24,8},{1,17},{9,25},{17,1},{25,9},{2,18},{10... | collective-permute-start | bytes 294920 | tf_op jit(solution)/shard_map/ppermute | solution.py:316
  19.0 0.5 %collective-permute-start.9 = (bf16[192,256]{1,0:T(8,128)(2,1)S(1)}, bf16[192,256]{1,0:T(8,128)(2,1)S(1)}, u32[]{:S(2)}, u32[]{:S(2)}) collective-permute-start(bf16[192,256]{1,0:T(8,128)(2,1)S(1)} %get-tuple-element.28), channel_id=1, source_target_pairs={{0,8},{8,0},{16,24},{24,16},{1,9},{9,1},{17,25},{25,17},{2,10},{10... | collective-permute-start | bytes 294920 | tf_op jit(solution)/shard_map/ppermute | solution.py:316
  19.5 2.3 %collective-permute-done.7.refs_0_ = bf16[192,256]{1,0:T(8,128)(2,1)S(1)} collective-permute-done((bf16[192,256]{1,0:T(8,128)(2,1)S(1)}, bf16[192,256]{1,0:T(8,128)(2,1)S(1)}, u32[]{:S(2)}, u32[]{:S(2)}) %collective-permute-start.7) | collective-permute-done | bytes 98336 | tf_op jit(solution)/shard_map/ppermute | solution.py:316
  21.8 2.0 %collective-permute-done.8.refs_1_ = bf16[192,256]{1,0:T(8,128)(2,1)S(1)} collective-permute-done((bf16[192,256]{1,0:T(8,128)(2,1)S(1)}, bf16[192,256]{1,0:T(8,128)(2,1)S(1)}, u32[]{:S(2)}, u32[]{:S(2)}) %collective-permute-start.8) | collective-permute-done | bytes 98336 | tf_op jit(solution)/shard_map/ppermute | solution.py:316
  23.9 0.6 %shard_map.58 = (bf16[128,256]{1,0:T(8,128)(2,1)S(1)}, bf16[128,256]{1,0:T(8,128)(2,1)S(1)}, bf16[128,256]{1,0:T(8,128)(2,1)S(1)}, bf16[128,256]{1,0:T(8,128)(2,1)S(1)}) custom-call(bf16[192,256]{1,0:T(8,128)(2,1)S(1)} %collective-permute-done.7.refs_0_, bf16[192,256]{1,0:T(8,128)(2,1)S(1)} %collective-permute-done.8.refs_1_, ...), custom_call_target="tpu_custom_call" | custom-call | bytes 2097152 | tf_op jit(solution)/shard_map/pallas_call | solution.py:392
  24.5 1.8 %collective-permute-start.10 = (bf16[128,256]{1,0:T(8,128)(2,1)S(1)}, bf16[128,256]{1,0:T(8,128)(2,1)S(1)}, u32[]{:S(2)}, u32[]{:S(2)}) collective-permute-start(bf16[128,256]{1,0:T(8,128)(2,1)S(1)} %get-tuple-element.30), channel_id=1, source_target_pairs={{0,24},{8,16},{16,8},{24,0},{1,25},{9,17},{17,9},{25,1},{2,26},{10... | collective-permute-start | bytes 196616 | tf_op jit(solution)/shard_map/ppermute | solution.py:316
  26.3 1.3 %collective-permute-start.11 = (bf16[128,256]{1,0:T(8,128)(2,1)S(1)}, bf16[128,256]{1,0:T(8,128)(2,1)S(1)}, u32[]{:S(2)}, u32[]{:S(2)}) collective-permute-start(bf16[128,256]{1,0:T(8,128)(2,1)S(1)} %get-tuple-element.31), channel_id=1, source_target_pairs={{0,16},{8,24},{16,0},{24,8},{1,17},{9,25},{17,1},{25,9},{2,18},{10... | collective-permute-start | bytes 196616 | tf_op jit(solution)/shard_map/ppermute | solution.py:316
  27.6 0.5 %collective-permute-start.12 = (bf16[128,256]{1,0:T(8,128)(2,1)S(1)}, bf16[128,256]{1,0:T(8,128)(2,1)S(1)}, u32[]{:S(2)}, u32[]{:S(2)}) collective-permute-start(bf16[128,256]{1,0:T(8,128)(2,1)S(1)} %get-tuple-element.32), channel_id=1, source_target_pairs={{0,8},{8,0},{16,24},{24,16},{1,9},{9,1},{17,25},{25,17},{2,10},{10... | collective-permute-start | bytes 196616 | tf_op jit(solution)/shard_map/ppermute | solution.py:316
  28.1 2.1 %collective-permute-done.10.refs_0_ = bf16[128,256]{1,0:T(8,128)(2,1)S(1)} collective-permute-done((bf16[128,256]{1,0:T(8,128)(2,1)S(1)}, bf16[128,256]{1,0:T(8,128)(2,1)S(1)}, u32[]{:S(2)}, u32[]{:S(2)}) %collective-permute-start.10) | collective-permute-done | bytes 65568 | tf_op jit(solution)/shard_map/ppermute | solution.py:316
  30.2 0.5 %collective-permute-done.11.refs_1_ = bf16[128,256]{1,0:T(8,128)(2,1)S(1)} collective-permute-done((bf16[128,256]{1,0:T(8,128)(2,1)S(1)}, bf16[128,256]{1,0:T(8,128)(2,1)S(1)}, u32[]{:S(2)}, u32[]{:S(2)}) %collective-permute-start.11) | collective-permute-done | bytes 65568 | tf_op jit(solution)/shard_map/ppermute | solution.py:316
  30.7 1.1 %collective-permute-done.12.refs_2_ = bf16[128,256]{1,0:T(8,128)(2,1)S(1)} collective-permute-done((bf16[128,256]{1,0:T(8,128)(2,1)S(1)}, bf16[128,256]{1,0:T(8,128)(2,1)S(1)}, u32[]{:S(2)}, u32[]{:S(2)}) %collective-permute-start.12) | collective-permute-done | bytes 65568 | tf_op jit(solution)/shard_map/ppermute | solution.py:316
  31.9 1.2 %shard_map.60 = bf16[4,64,512]{2,1,0:T(8,128)(2,1)S(1)} custom-call(bf16[128,256]{1,0:T(8,128)(2,1)S(1)} %collective-permute-done.10.refs_0_, bf16[128,256]{1,0:T(8,128)(2,1)S(1)} %collective-permute-done.11.refs_1_, bf16[128,256]{1,0:T(8,128)(2,1)S(1)} %collective-permute-done.12.refs_2_, bf16[128,256]{1,0:T(8,128)(2,1)S(1)} %get-tuple-element.33.refs_3_, ...), custom_call_target="tpu_custom_call" | custom-call | bytes 6291456 | tf_op jit(solution)/shard_map/pallas_call | solution.py:409
  33.1 1.2 %shard_map.59.keep_ref = f32[4,64,512]{2,1,0:T(8,128)S(1)} custom-call(bf16[128,256]{1,0:T(8,128)(2,1)S(1)} %collective-permute-done.10.refs_0_, bf16[128,256]{1,0:T(8,128)(2,1)S(1)} %collective-permute-done.11.refs_1_, bf16[128,256]{1,0:T(8,128)(2,1)S(1)} %collective-permute-done.12.refs_2_, bf16[128,256]{1,0:T(8,128)(2,1)S(1)} %get-tuple-element.33.refs_3_, ...), custom_call_target="tpu_custom_call" | custom-call | bytes 6291456 | tf_op jit(solution)/shard_map/pallas_call | solution.py:409
  34.3 0.4 collective-permute-done.13.came_ref
  34.7 1.6 %collective-permute-start.14 = (bf16[64,512]{1,0:T(8,128)(2,1)S(1)}, bf16[64,512]{1,0:T(8,128)(2,1)S(1)}, u32[]{:S(2)}, u32[]{:S(2)}) collective-permute-start(bf16[64,512]{1,0:T(8,128)(2,1)S(1)} %get-tuple-element.34), channel_id=1, source_target_pairs={{0,2},{1,3},{2,4},{3,5},{4,6},{5,7},{6,0},{7,1},{8,10},{9,11},{10,... | collective-permute-start | bytes 196616 | tf_op jit(solution)/shard_map/ppermute | solution.py:328
  36.3 1.2 %collective-permute-start.15 = (bf16[64,512]{1,0:T(8,128)(2,1)S(1)}, bf16[64,512]{1,0:T(8,128)(2,1)S(1)}, u32[]{:S(2)}, u32[]{:S(2)}) collective-permute-start(bf16[64,512]{1,0:T(8,128)(2,1)S(1)} %get-tuple-element.35), channel_id=1, source_target_pairs={{0,4},{1,5},{2,6},{3,7},{4,0},{5,1},{6,2},{7,3},{8,12},{9,13},{10,... | collective-permute-start | bytes 196616 | tf_op jit(solution)/shard_map/ppermute | solution.py:328
  37.5 2.2 %collective-permute-start.16 = (bf16[64,512]{1,0:T(8,128)(2,1)S(1)}, bf16[64,512]{1,0:T(8,128)(2,1)S(1)}, u32[]{:S(2)}, u32[]{:S(2)}) collective-permute-start(bf16[64,512]{1,0:T(8,128)(2,1)S(1)} %get-tuple-element.36), channel_id=1, source_target_pairs={{0,6},{1,7},{2,0},{3,1},{4,2},{5,3},{6,4},{7,5},{8,14},{9,15},{10,... | collective-permute-start | bytes 196616 | tf_op jit(solution)/shard_map/ppermute | solution.py:328
  39.6 1.9 %collective-permute-done.14.refs_0_ = bf16[64,512]{1,0:T(8,128)(2,1)S(1)} collective-permute-done((bf16[64,512]{1,0:T(8,128)(2,1)S(1)}, bf16[64,512]{1,0:T(8,128)(2,1)S(1)}, u32[]{:S(2)}, u32[]{:S(2)}) %collective-permute-start.14) | collective-permute-done | bytes 65568 | tf_op jit(solution)/shard_map/ppermute | solution.py:328
  41.5 2.1 %collective-permute-done.15.refs_1_ = bf16[64,512]{1,0:T(8,128)(2,1)S(1)} collective-permute-done((bf16[64,512]{1,0:T(8,128)(2,1)S(1)}, bf16[64,512]{1,0:T(8,128)(2,1)S(1)}, u32[]{:S(2)}, u32[]{:S(2)}) %collective-permute-start.15) | collective-permute-done | bytes 65568 | tf_op jit(solution)/shard_map/ppermute | solution.py:328
  43.6 1.7 %shard_map.62 = bf16[64,4,16,128]{3,2,1,0:T(8,128)(2,1)} custom-call(bf16[64,512]{1,0:T(8,128)(2,1)S(1)} %collective-permute-done.14.refs_0_, bf16[64,512]{1,0:T(8,128)(2,1)S(1)} %collective-permute-done.15.refs_1_, bf16[64,512]{1,0:T(8,128)(2,1)S(1)} %collective-permute-done.16.refs_2_, f32[64,512]{1,0:T(8,128)S(1)} %get-tuple-element.37.refs_3_, ...), custom_call_target="tpu_custom_call" | custom-call | bytes 4194304 | tf_op jit(solution)/shard_map/pallas_call | solution.py:428
  (18 shorter events, 0.2 us)
Async XLA Ops:
  2.5 12.0 %copy-start = (bf16[8,32,256]{2,1,0:T(8,128)(2,1)S(1)}, bf16[8,32,256]{2,1,0:T(8,128)(2,1)}, u32[]{:S(2)}) copy-start(bf16[8,32,256]{2,1,0:T(8,128)(2,1)} %refs_11_.1) | copy-start | bytes 393220
  2.5 12.0 %copy-start.1 = (bf16[2,64,32]{2,1,0:T(8,128)(2,1)S(1)}, bf16[2,64,32]{2,1,0:T(8,128)(2,1)}, u32[]{:S(2)}) copy-start(bf16[2,64,32]{2,1,0:T(8,128)(2,1)} %constant.6.clone.refs_10_) | copy-start | bytes 24580
  2.5 8.0 %collective-permute-start.5 = (bf16[64,512]{1,0:T(8,128)(2,1)S(1)}, bf16[64,512]{1,0:T(8,128)(2,1)S(1)}, u32[]{:S(2)}, u32[]{:S(2)}) collective-permute-start(bf16[64,512]{1,0:T(8,128)(2,1)S(1)} %get-tuple-element.22.edge_hbm.refs_0_), channel_id=1, source_target_pairs={{0,6},{1,7},{2,4},{3,5},{4,2},{5,3},{6,0},{7,1},{8,14},{9,15},{10,... | collective-permute-start | bytes 196616 | tf_op jit(solution)/shard_map/ppermute | solution.py:316
  7.6 4.7 %collective-permute-start.3 = (bf16[64,512]{1,0:T(8,128)(2,1)S(1)}, bf16[64,512]{1,0:T(8,128)(2,1)S(1)}, u32[]{:S(2)}, u32[]{:S(2)}) collective-permute-start(bf16[64,512]{1,0:T(8,128)(2,1)S(1)} %get-tuple-element.22.edge_hbm.refs_0_), channel_id=1, source_target_pairs={{0,2},{1,3},{2,0},{3,1},{4,6},{5,7},{6,4},{7,5},{8,10},{9,11},{10,... | collective-permute-start | bytes 196616 | tf_op jit(solution)/shard_map/ppermute | solution.py:316
  7.7 5.6 %collective-permute-start.1 = (bf16[64,512]{1,0:T(8,128)(2,1)S(1)}, bf16[64,512]{1,0:T(8,128)(2,1)S(1)}, u32[]{:S(2)}, u32[]{:S(2)}) collective-permute-start(bf16[64,512]{1,0:T(8,128)(2,1)S(1)} %get-tuple-element.22.edge_hbm.refs_0_), channel_id=1, source_target_pairs={{0,4},{1,5},{2,6},{3,7},{4,0},{5,1},{6,2},{7,3},{8,12},{9,13},{10,... | collective-permute-start | bytes 196616 | tf_op jit(solution)/shard_map/ppermute | solution.py:316
  9.9 3.4 %collective-permute-start = (bf16[64,512]{1,0:T(8,128)(2,1)S(1)}, bf16[64,512]{1,0:T(8,128)(2,1)S(1)}, u32[]{:S(2)}, u32[]{:S(2)}) collective-permute-start(bf16[64,512]{1,0:T(8,128)(2,1)S(1)} %get-tuple-element.23), channel_id=1, source_target_pairs={{0,1},{1,0},{2,3},{3,2},{4,5},{5,4},{6,7},{7,6},{8,9},{9,8},{10,11... | collective-permute-start | bytes 196616 | tf_op jit(solution)/shard_map/ppermute | solution.py:316
  10.5 2.7 %collective-permute-start.6 = (bf16[64,512]{1,0:T(8,128)(2,1)S(1)}, bf16[64,512]{1,0:T(8,128)(2,1)S(1)}, u32[]{:S(2)}, u32[]{:S(2)}) collective-permute-start(bf16[64,512]{1,0:T(8,128)(2,1)S(1)} %collective-permute-done.5.refs_6_), channel_id=1, source_target_pairs={{0,1},{1,0},{2,3},{3,2},{4,5},{5,4},{6,7},{7,6},{8,9},{9,8},{10,11... | collective-permute-start | bytes 196616 | tf_op jit(solution)/shard_map/ppermute | solution.py:316
  12.3 1.3 %collective-permute-start.4 = (bf16[64,512]{1,0:T(8,128)(2,1)S(1)}, bf16[64,512]{1,0:T(8,128)(2,1)S(1)}, u32[]{:S(2)}, u32[]{:S(2)}) collective-permute-start(bf16[64,512]{1,0:T(8,128)(2,1)S(1)} %collective-permute-done.3.refs_4_), channel_id=1, source_target_pairs={{0,1},{1,0},{2,3},{3,2},{4,5},{5,4},{6,7},{7,6},{8,9},{9,8},{10,11... | collective-permute-start | bytes 196616 | tf_op jit(solution)/shard_map/ppermute | solution.py:316
  13.3 1.3 %collective-permute-start.2 = (bf16[64,512]{1,0:T(8,128)(2,1)S(1)}, bf16[64,512]{1,0:T(8,128)(2,1)S(1)}, u32[]{:S(2)}, u32[]{:S(2)}) collective-permute-start(bf16[64,512]{1,0:T(8,128)(2,1)S(1)} %collective-permute-done.1.refs_2_), channel_id=1, source_target_pairs={{0,1},{1,0},{2,3},{3,2},{4,5},{5,4},{6,7},{7,6},{8,9},{9,8},{10,11... | collective-permute-start | bytes 196616 | tf_op jit(solution)/shard_map/ppermute | solution.py:316
  14.5 9.4 %copy-start.2 = (bf16[64,128]{1,0:T(8,128)(2,1)S(1)}, bf16[64,128]{1,0:T(8,128)(2,1)}, u32[]{:S(2)}) copy-start(bf16[64,128]{1,0:T(8,128)(2,1)} %constant.8.clone.refs_5_) | copy-start | bytes 49156
  14.5 9.4 %copy-start.3 = (bf16[64,128]{1,0:T(8,128)(2,1)S(1)}, bf16[64,128]{1,0:T(8,128)(2,1)}, u32[]{:S(2)}) copy-start(bf16[64,128]{1,0:T(8,128)(2,1)} %constant.7.clone.refs_4_) | copy-start | bytes 49156
  15.9 5.9 %collective-permute-start.7 = (bf16[192,256]{1,0:T(8,128)(2,1)S(1)}, bf16[192,256]{1,0:T(8,128)(2,1)S(1)}, u32[]{:S(2)}, u32[]{:S(2)}) collective-permute-start(bf16[192,256]{1,0:T(8,128)(2,1)S(1)} %get-tuple-element.26), channel_id=1, source_target_pairs={{0,24},{8,16},{16,8},{24,0},{1,25},{9,17},{17,9},{25,1},{2,26},{10... | collective-permute-start | bytes 294920 | tf_op jit(solution)/shard_map/ppermute | solution.py:316
  18.5 5.4 %collective-permute-start.8 = (bf16[192,256]{1,0:T(8,128)(2,1)S(1)}, bf16[192,256]{1,0:T(8,128)(2,1)S(1)}, u32[]{:S(2)}, u32[]{:S(2)}) collective-permute-start(bf16[192,256]{1,0:T(8,128)(2,1)S(1)} %get-tuple-element.27), channel_id=1, source_target_pairs={{0,16},{8,24},{16,0},{24,8},{1,17},{9,25},{17,1},{25,9},{2,18},{10... | collective-permute-start | bytes 294920 | tf_op jit(solution)/shard_map/ppermute | solution.py:316
  19.0 5.0 %collective-permute-start.9 = (bf16[192,256]{1,0:T(8,128)(2,1)S(1)}, bf16[192,256]{1,0:T(8,128)(2,1)S(1)}, u32[]{:S(2)}, u32[]{:S(2)}) collective-permute-start(bf16[192,256]{1,0:T(8,128)(2,1)S(1)} %get-tuple-element.28), channel_id=1, source_target_pairs={{0,8},{8,0},{16,24},{24,16},{1,9},{9,1},{17,25},{25,17},{2,10},{10... | collective-permute-start | bytes 294920 | tf_op jit(solution)/shard_map/ppermute | solution.py:316
  24.5 5.7 %collective-permute-start.10 = (bf16[128,256]{1,0:T(8,128)(2,1)S(1)}, bf16[128,256]{1,0:T(8,128)(2,1)S(1)}, u32[]{:S(2)}, u32[]{:S(2)}) collective-permute-start(bf16[128,256]{1,0:T(8,128)(2,1)S(1)} %get-tuple-element.30), channel_id=1, source_target_pairs={{0,24},{8,16},{16,8},{24,0},{1,25},{9,17},{17,9},{25,1},{2,26},{10... | collective-permute-start | bytes 196616 | tf_op jit(solution)/shard_map/ppermute | solution.py:316
  26.3 4.5 %collective-permute-start.11 = (bf16[128,256]{1,0:T(8,128)(2,1)S(1)}, bf16[128,256]{1,0:T(8,128)(2,1)S(1)}, u32[]{:S(2)}, u32[]{:S(2)}) collective-permute-start(bf16[128,256]{1,0:T(8,128)(2,1)S(1)} %get-tuple-element.31), channel_id=1, source_target_pairs={{0,16},{8,24},{16,0},{24,8},{1,17},{9,25},{17,1},{25,9},{2,18},{10... | collective-permute-start | bytes 196616 | tf_op jit(solution)/shard_map/ppermute | solution.py:316
  27.6 4.3 %collective-permute-start.12 = (bf16[128,256]{1,0:T(8,128)(2,1)S(1)}, bf16[128,256]{1,0:T(8,128)(2,1)S(1)}, u32[]{:S(2)}, u32[]{:S(2)}) collective-permute-start(bf16[128,256]{1,0:T(8,128)(2,1)S(1)} %get-tuple-element.32), channel_id=1, source_target_pairs={{0,8},{8,0},{16,24},{24,16},{1,9},{9,1},{17,25},{25,17},{2,10},{10... | collective-permute-start | bytes 196616 | tf_op jit(solution)/shard_map/ppermute | solution.py:316
  33.0 1.6 %collective-permute-start.13 = (bf16[4,64,512]{2,1,0:T(8,128)(2,1)S(1)}, bf16[4,64,512]{2,1,0:T(8,128)(2,1)S(1)}, u32[]{:S(2)}, u32[]{:S(2)}) collective-permute-start(bf16[4,64,512]{2,1,0:T(8,128)(2,1)S(1)} %shard_map.60), channel_id=1, source_target_pairs={{0,1},{1,0},{2,3},{3,2},{4,5},{5,4},{6,7},{7,6},{8,9},{9,8},{10,11... | collective-permute-start | bytes 786440 | tf_op jit(solution)/shard_map/ppermute | solution.py:316
  34.7 6.8 %collective-permute-start.14 = (bf16[64,512]{1,0:T(8,128)(2,1)S(1)}, bf16[64,512]{1,0:T(8,128)(2,1)S(1)}, u32[]{:S(2)}, u32[]{:S(2)}) collective-permute-start(bf16[64,512]{1,0:T(8,128)(2,1)S(1)} %get-tuple-element.34), channel_id=1, source_target_pairs={{0,2},{1,3},{2,4},{3,5},{4,6},{5,7},{6,0},{7,1},{8,10},{9,11},{10,... | collective-permute-start | bytes 196616 | tf_op jit(solution)/shard_map/ppermute | solution.py:328
  36.3 7.3 %collective-permute-start.15 = (bf16[64,512]{1,0:T(8,128)(2,1)S(1)}, bf16[64,512]{1,0:T(8,128)(2,1)S(1)}, u32[]{:S(2)}, u32[]{:S(2)}) collective-permute-start(bf16[64,512]{1,0:T(8,128)(2,1)S(1)} %get-tuple-element.35), channel_id=1, source_target_pairs={{0,4},{1,5},{2,6},{3,7},{4,0},{5,1},{6,2},{7,3},{8,12},{9,13},{10,... | collective-permute-start | bytes 196616 | tf_op jit(solution)/shard_map/ppermute | solution.py:328
  37.5 6.1 %collective-permute-start.16 = (bf16[64,512]{1,0:T(8,128)(2,1)S(1)}, bf16[64,512]{1,0:T(8,128)(2,1)S(1)}, u32[]{:S(2)}, u32[]{:S(2)}) collective-permute-start(bf16[64,512]{1,0:T(8,128)(2,1)S(1)} %get-tuple-element.36), channel_id=1, source_target_pairs={{0,6},{1,7},{2,0},{3,1},{4,2},{5,3},{6,4},{7,5},{8,14},{9,15},{10,... | collective-permute-start | bytes 196616 | tf_op jit(solution)/shard_map/ppermute | solution.py:328

commit v17 on v16

--- a/solution.py
+++ b/solution.py
@@ -211,21 +211,16 @@
         outs[s][...] = take(wide, pl.multiple_of(dest * size, size), size).astype(BF16)
 
 
-def weight_kernel(shares, flip, out_rows, *refs):
-    pieces, (orb_ref, rest_ref, out_ref, gathered) = refs[:shares][::-1], refs[shares:]
-    local_k, _, norb, _ = orb_ref.shape
-    total_rows = gathered.shape[1]
-    half = total_rows // local_k // 2
-    me = lax.axis_index("ka")
-    core = jnp.bitwise_xor(jnp.bitwise_and(lax.axis_index("pts"), 1), flip)
-    plane = plane_of(shares)
+def weight_operands(pieces, right_ref, gathered):
+    shares = len(pieces)
+    groups, lanes, depth = right_ref.shape
+    me, plane = lax.axis_index("ka"), plane_of(shares)
     for s in range(shares):
         gathered[jnp.bitwise_xor(jnp.bitwise_xor(me, s), plane)] = pieces[s][...]
-    lanes = 2 * half * shares
-    group = max(1, LANES // lanes)
-    chunks = norb // out_rows // 2
-    for g in range(local_k // group):
-        right, left = [], []
+    group = depth // (2 * gathered.shape[2])
+    half = gathered.shape[1] // (groups * group) // 2
+    for g in range(groups):
+        right = []
         for kk in range(group):
             k = g * group + kk
             first, second = [], []
@@ -235,37 +230,50 @@
                 second.extend([piece[half:], -piece[:half]])
             first = jnp.concatenate(first, axis=0).astype(BF16)
             second = jnp.concatenate(second, axis=0).astype(BF16)
-            zero = jnp.zeros_like(first)
-            parts = [zero] * (2 * group)
+            parts = [jnp.zeros_like(first)] * (2 * group)
             parts[2 * kk], parts[2 * kk + 1] = first, second
             right.append(jnp.concatenate(parts, axis=1))
-            left.append(k)
-        right = jnp.concatenate(right, axis=0)
-        for z in range(chunks):
-            start = pl.multiple_of((2 * z + core) * out_rows, out_rows)
+        right_ref[g] = jnp.concatenate(right, axis=0)
+
+
+def weight_rows(offsets, flip, out_rows, right_ref, orb_ref, rest_ref, out_ref):
+    groups, lanes, _ = right_ref.shape
+    local_k, _, norb, _ = orb_ref.shape
+    group = local_k // groups
+    block = lax.axis_index("pts")
+    core = jnp.bitwise_xor(jnp.bitwise_and(block, 1), flip)
+    z = lax.shift_right_logical(block, 1)
+    chunks = norb // out_rows // 2
+    for g in range(groups):
+        for i, offset in enumerate(offsets):
+            start = pl.multiple_of((2 * lax.rem(z + offset, chunks) + core) * out_rows, out_rows)
             rows = jnp.concatenate(
                 [
                     ref[k, part, pl.ds(start, out_rows), :]
-                    for k in left
+                    for k in range(g * group, (g + 1) * group)
                     for part in range(2)
                     for ref in (orb_ref, rest_ref)
                 ],
                 axis=1,
             )
-            out_ref[z, :, g * group * lanes : (g + 1) * group * lanes] = dot(
-                rows, right, ((1,), (1,))
-            ).astype(out_ref.dtype)
-
-
-def pair_kernel(chunks, keep_ref, came_ref, own_ref, *outs):
-    z = lax.shift_right_logical(lax.axis_index("pts"), 1)
-    for s in range(chunks):
-        dest = lax.rem(z + s, chunks)
-        value = keep_ref[dest] + came_ref[dest].astype(F32)
-        if s == 0:
-            own_ref[...] = value
-        else:
-            outs[s - 1][...] = value.astype(BF16)
+            out_ref[i, :, g * lanes : (g + 1) * lanes] = dot(rows, right_ref[g], ((1,), (1,))).astype(
+                out_ref.dtype
+            )
+
+
+def first_weight_kernel(shares, offsets, out_rows, *refs):
+    pieces, (orb_ref, rest_ref, out_ref, right_ref, gathered) = refs[:shares][::-1], refs[shares:]
+    weight_operands(pieces, right_ref, gathered)
+    weight_rows(offsets, 1, out_rows, right_ref, orb_ref, rest_ref, out_ref)
+
+
+def next_weight_kernel(offsets, flip, out_rows, right_ref, orb_ref, rest_ref, *refs):
+    weight_rows(offsets, flip, out_rows, right_ref, orb_ref, rest_ref, refs[-1])
+
+
+def pair_kernel(keep_ref, came_ref, *outs):
+    for i, out_ref in enumerate(outs):
+        out_ref[...] = (keep_ref[i] + came_ref[i].astype(F32)).astype(out_ref.dtype)
 
 
 def exchange_kernel(chunks, scale, *refs):
@@ -324,9 +332,9 @@
     chunks = len(pieces)
     came = []
     for s in range(1, chunks):
-        pairs = [(2 * z + core, 2 * ((z + s) % chunks) + core) for z in range(chunks) for core in range(2)]
+        pairs = [(2 * z + core, 2 * ((z - s) % chunks) + core) for z in range(chunks) for core in range(2)]
         came.append(lax.ppermute(pieces[s], "pts", pairs))
-    return came + [pieces[0]]
+    return came[::-1] + [pieces[0]]
 
 
 def body(orbitals, coulomb):
@@ -403,27 +411,36 @@
     kernels = trade(kernels, "ka", 1)
 
     lanes = local_k * 2 * columns
-    halves = []
-    for flip, kind in ((1, BF16), (0, F32)):
-        halves.append(
-            call(
-                functools.partial(weight_kernel, shares, flip, out_rows),
-                shape((chunks, out_rows, lanes), kind),
-                shares + 2,
-                [pltpu.VMEM((shares, share * 2 * local_k, points), BF16)],
-                size=6 * MIB,
-            )(*kernels, first, rest)
-        )
-    came = swap(halves[0], "pts", 1)
-    own_sum, *sums = call(
-        functools.partial(pair_kernel, chunks),
-        [shape((out_rows, lanes), F32)] + [shape((out_rows, lanes), BF16)] * (chunks - 1),
-        2,
-        size=1 * MIB,
-    )(halves[1], came)
-    sums = shift_along([own_sum, *sums])
+    pair = max(1, LANES // (2 * columns))
+    early, late = list(reversed(range(1, chunks))), [0]
+    sent, right = call(
+        functools.partial(first_weight_kernel, shares, early, out_rows),
+        [
+            shape((len(early), out_rows, lanes), BF16),
+            shape((local_k // pair, pair * 2 * columns, pair * 2 * points), BF16),
+        ],
+        shares + 2,
+        [pltpu.VMEM((shares, share * 2 * local_k, points), BF16)],
+    )(*kernels, first, rest)
+
+    def rows_of(offsets, flip, kind, before):
+        return call(
+            functools.partial(next_weight_kernel, offsets, flip, out_rows),
+            shape((len(offsets), out_rows, lanes), kind),
+            3,
+            unread=1,
+        )(right, first, rest, before)
+
+    def summed(offsets, keep, came):
+        kinds = [shape((out_rows, lanes), BF16 if offset else F32) for offset in offsets]
+        return call(pair_kernel, kinds, 2)(keep, came)
+
+    sent_late = rows_of(late, 1, BF16, sent)
+    early_sums = summed(early, rows_of(early, 0, F32, sent_late), swap(sent, "pts", 1))
+    late_sums = summed(late, rows_of(late, 0, F32, early_sums[0]), swap(sent_late, "pts", 1))
+    sums = [*late_sums, *early_sums]
+    sums = shift_along(sums)
     spans = norb // LANES
-    pair = max(1, LANES // (2 * columns))
     rows = pair * spans * 2
     result = call(
         functools.partial(exchange_kernel, chunks, 1.0 / math.sqrt(points * blocks)),

time: 45.4 us -> 46.1 us (1.015)
  Pallas kernels: 10.1 us -> 11.1 us
  waiting for transfers between devices: 17.1 us -> 16.1 us
  starting transfers between devices: 18 us -> 18.5 us
    pallas_call x3 -> x6, Pallas kernels: 2.38 us -> 3.39 us  [the longest x3 2.11 us: rows_of(): call(functools.partial(next_weight_kernel, offsets, flip, out_rows), shap...]
    ppermute x3, waiting for transfers between devices: 3.98 us -> 3.32 us  [shift_along(): came.append(lax.ppermute(pieces[s], 'pts', pairs))]
    ppermute x14 -> x15, starting transfers between devices: 13 us -> 13.6 us  [swap(): return lax.ppermute(value, axis, [(i, i ^ mask) for i in range(size)])]
    ppermute x14 -> x15, waiting for transfers between devices: 13.1 us -> 12.8 us  [swap(): return lax.ppermute(value, axis, [(i, i ^ mask) for i in range(size)])]
  transfers between devices with their start and end apart: 17 -> 18, of which waited for: 14 -> 13; matrix products, arithmetic and copies ran while one was open for 0% -> 0% of each run, Pallas kernels for 6% -> 8%
where the time goes in v17:
time: 46.1 us; the launch traced here: 45.9 us
  starting transfers between devices  18.5 us (40%)
  waiting for transfers between devices  16.1 us (35%)
  Pallas kernels  11.1 us (24%)
    ppermute x15, starting transfers between devices, swap(): return lax.ppermute(value, axis, [(i, i ^ mask) for i in range(size)])  13.6 us
    ppermute x15, waiting for transfers between devices, swap(): return lax.ppermute(value, axis, [(i, i ^ mask) for i in range(size)])  12.8 us
    ppermute x3, starting transfers between devices, shift_along(): came.append(lax.ppermute(pieces[s], 'pts', pairs))  4.94 us
    ppermute x3, waiting for transfers between devices, shift_along(): came.append(lax.ppermute(pieces[s], 'pts', pairs))  3.32 us
    pallas_call x1, Pallas kernels, body(): call(functools.partial(edge_kernel, per_block), [shape((local_k * 2 * per...  2.5 us
    pallas_call x3, Pallas kernels, rows_of(): call(functools.partial(next_weight_kernel, offsets, flip, out_rows), shap...  2.11 us
    pallas_call x1, Pallas kernels, body(): call(functools.partial(exchange_kernel, chunks, 1.0 / math.sqrt(points *...  1.66 us
    pallas_call x1, Pallas kernels, body(): call(rest_kernel, [shape(edge.shape, BF16), shape((local_k, 2, norb, poin...  1.58 us
  transfers between devices with their start and end apart: 18, of which 13 were waited for; matrix products, arithmetic and copies ran while one was open for 0% of the time, Pallas kernels for 8%

profile of v17, /device:TPU:0, one launch (start us, length us, event | category | flops | bytes accessed | tf_op | source)
XLA Modules:
  0.0 45.9 jit_solution(6363942627621558138)
XLA Ops:
  0.0 2.5 %shard_map.55 = (bf16[64,512]{1,0:T(8,128)(2,1)S(1)}, bf16[8,2,512,128]{3,2,1,0:T(8,128)(2,1)S(1)}) custom-call(bf16[8,2,512,256]{3,2,1,0:T(8,128)(2,1)} %orb_hbm.3), custom_call_target="tpu_custom_call" | custom-call | bytes 4194304 | tf_op jit(solution)/shard_map/pallas_call | solution.py:352
  2.5 5.1 %collective-permute-start.5 = (bf16[64,512]{1,0:T(8,128)(2,1)S(1)}, bf16[64,512]{1,0:T(8,128)(2,1)S(1)}, u32[]{:S(2)}, u32[]{:S(2)}) collective-permute-start(bf16[64,512]{1,0:T(8,128)(2,1)S(1)} %get-tuple-element.23.edge_hbm.refs_0_), channel_id=1, source_target_pairs={{0,6},{1,7},{2,4},{3,5},{4,2},{5,3},{6,0},{7,1},{8,14},{9,15},{10,... | collective-permute-start | bytes 196616 | tf_op jit(solution)/shard_map/ppermute | solution.py:324
  7.7 0.6 %collective-permute-start.1 = (bf16[64,512]{1,0:T(8,128)(2,1)S(1)}, bf16[64,512]{1,0:T(8,128)(2,1)S(1)}, u32[]{:S(2)}, u32[]{:S(2)}) collective-permute-start(bf16[64,512]{1,0:T(8,128)(2,1)S(1)} %get-tuple-element.23.edge_hbm.refs_0_), channel_id=1, source_target_pairs={{0,4},{1,5},{2,6},{3,7},{4,0},{5,1},{6,2},{7,3},{8,12},{9,13},{10,... | collective-permute-start | bytes 196616 | tf_op jit(solution)/shard_map/ppermute | solution.py:324
  8.3 1.6 %shard_map.56 = (bf16[64,512]{1,0:T(8,128)(2,1)S(1)}, bf16[8,2,512,128]{3,2,1,0:T(8,128)(2,1)S(1)}) custom-call(bf16[8,2,512,256]{3,2,1,0:T(8,128)(2,1)} %orb_hbm.3, bf16[64,512]{1,0:T(8,128)(2,1)S(1)} %get-tuple-element.23.edge_hbm.refs_0_), custom_call_target="tpu_custom_call" | custom-call | bytes 4194304 | tf_op jit(solution)/shard_map/pallas_call | solution.py:364
  10.0 0.6 %collective-permute-done.5.refs_6_ = bf16[64,512]{1,0:T(8,128)(2,1)S(1)} collective-permute-done((bf16[64,512]{1,0:T(8,128)(2,1)S(1)}, bf16[64,512]{1,0:T(8,128)(2,1)S(1)}, u32[]{:S(2)}, u32[]{:S(2)}) %collective-permute-start.5) | collective-permute-done | bytes 65568 | tf_op jit(solution)/shard_map/ppermute | solution.py:324
  10.6 1.8 %collective-permute-done.3.refs_4_ = bf16[64,512]{1,0:T(8,128)(2,1)S(1)} collective-permute-done((bf16[64,512]{1,0:T(8,128)(2,1)S(1)}, bf16[64,512]{1,0:T(8,128)(2,1)S(1)}, u32[]{:S(2)}, u32[]{:S(2)}) %collective-permute-start.3) | collective-permute-done | bytes 65568 | tf_op jit(solution)/shard_map/ppermute | solution.py:324
  12.3 1.0 %collective-permute-done.1.refs_2_ = bf16[64,512]{1,0:T(8,128)(2,1)S(1)} collective-permute-done((bf16[64,512]{1,0:T(8,128)(2,1)S(1)}, bf16[64,512]{1,0:T(8,128)(2,1)S(1)}, u32[]{:S(2)}, u32[]{:S(2)}) %collective-permute-start.1) | collective-permute-done | bytes 65568 | tf_op jit(solution)/shard_map/ppermute | solution.py:324
  13.6 1.0 %collective-permute-done.2.refs_3_ = bf16[64,512]{1,0:T(8,128)(2,1)S(1)} collective-permute-done((bf16[64,512]{1,0:T(8,128)(2,1)S(1)}, bf16[64,512]{1,0:T(8,128)(2,1)S(1)}, u32[]{:S(2)}, u32[]{:S(2)}) %collective-permute-start.2) | collective-permute-done | bytes 65568 | tf_op jit(solution)/shard_map/ppermute | solution.py:324
  14.6 1.4 %shard_map.57 = (bf16[192,256]{1,0:T(8,128)(2,1)S(1)}, bf16[192,256]{1,0:T(8,128)(2,1)S(1)}, bf16[192,256]{1,0:T(8,128)(2,1)S(1)}, bf16[192,256]{1,0:T(8,128)(2,1)S(1)}, bf16[4,8,16,1024]{3,2,1,0:T(8,128)(2,1)S(1)}) custom-call(bf16[64,512]{1,0:T(8,128)(2,1)S(1)} %get-tuple-element.23.edge_hbm.refs_0_, bf16[64,512]{1,0:T(8,128)(2,1)S(1)} %collective-permute-done.refs_1_, ...), custom_call_target="tpu_custom_call" | custom-call | bytes 6291456 | tf_op jit(solution)/shard_map/pallas_call | solution.py:387
  15.9 2.5 %collective-permute-start.7 = (bf16[192,256]{1,0:T(8,128)(2,1)S(1)}, bf16[192,256]{1,0:T(8,128)(2,1)S(1)}, u32[]{:S(2)}, u32[]{:S(2)}) collective-permute-start(bf16[192,256]{1,0:T(8,128)(2,1)S(1)} %get-tuple-element.27), channel_id=1, source_target_pairs={{0,24},{8,16},{16,8},{24,0},{1,25},{9,17},{17,9},{25,1},{2,26},{10... | collective-permute-start | bytes 294920 | tf_op jit(solution)/shard_map/ppermute | solution.py:324
  18.5 0.5 %collective-permute-start.8 = (bf16[192,256]{1,0:T(8,128)(2,1)S(1)}, bf16[192,256]{1,0:T(8,128)(2,1)S(1)}, u32[]{:S(2)}, u32[]{:S(2)}) collective-permute-start(bf16[192,256]{1,0:T(8,128)(2,1)S(1)} %get-tuple-element.28), channel_id=1, source_target_pairs={{0,16},{8,24},{16,0},{24,8},{1,17},{9,25},{17,1},{25,9},{2,18},{10... | collective-permute-start | bytes 294920 | tf_op jit(solution)/shard_map/ppermute | solution.py:324
  19.0 0.5 %collective-permute-start.9 = (bf16[192,256]{1,0:T(8,128)(2,1)S(1)}, bf16[192,256]{1,0:T(8,128)(2,1)S(1)}, u32[]{:S(2)}, u32[]{:S(2)}) collective-permute-start(bf16[192,256]{1,0:T(8,128)(2,1)S(1)} %get-tuple-element.29), channel_id=1, source_target_pairs={{0,8},{8,0},{16,24},{24,16},{1,9},{9,1},{17,25},{25,17},{2,10},{10... | collective-permute-start | bytes 294920 | tf_op jit(solution)/shard_map/ppermute | solution.py:324
  19.5 2.3 %collective-permute-done.7.refs_0_ = bf16[192,256]{1,0:T(8,128)(2,1)S(1)} collective-permute-done((bf16[192,256]{1,0:T(8,128)(2,1)S(1)}, bf16[192,256]{1,0:T(8,128)(2,1)S(1)}, u32[]{:S(2)}, u32[]{:S(2)}) %collective-permute-start.7) | collective-permute-done | bytes 98336 | tf_op jit(solution)/shard_map/ppermute | solution.py:324
  21.8 2.0 %collective-permute-done.8.refs_1_ = bf16[192,256]{1,0:T(8,128)(2,1)S(1)} collective-permute-done((bf16[192,256]{1,0:T(8,128)(2,1)S(1)}, bf16[192,256]{1,0:T(8,128)(2,1)S(1)}, u32[]{:S(2)}, u32[]{:S(2)}) %collective-permute-start.8) | collective-permute-done | bytes 98336 | tf_op jit(solution)/shard_map/ppermute | solution.py:324
  23.9 0.6 %shard_map.58 = (bf16[128,256]{1,0:T(8,128)(2,1)S(1)}, bf16[128,256]{1,0:T(8,128)(2,1)S(1)}, bf16[128,256]{1,0:T(8,128)(2,1)S(1)}, bf16[128,256]{1,0:T(8,128)(2,1)S(1)}) custom-call(bf16[192,256]{1,0:T(8,128)(2,1)S(1)} %collective-permute-done.7.refs_0_, bf16[192,256]{1,0:T(8,128)(2,1)S(1)} %collective-permute-done.8.refs_1_, ...), custom_call_target="tpu_custom_call" | custom-call | bytes 2097152 | tf_op jit(solution)/shard_map/pallas_call | solution.py:400
  24.5 1.8 %collective-permute-start.10 = (bf16[128,256]{1,0:T(8,128)(2,1)S(1)}, bf16[128,256]{1,0:T(8,128)(2,1)S(1)}, u32[]{:S(2)}, u32[]{:S(2)}) collective-permute-start(bf16[128,256]{1,0:T(8,128)(2,1)S(1)} %get-tuple-element.31), channel_id=1, source_target_pairs={{0,24},{8,16},{16,8},{24,0},{1,25},{9,17},{17,9},{25,1},{2,26},{10... | collective-permute-start | bytes 196616 | tf_op jit(solution)/shard_map/ppermute | solution.py:324
  26.3 1.3 %collective-permute-start.11 = (bf16[128,256]{1,0:T(8,128)(2,1)S(1)}, bf16[128,256]{1,0:T(8,128)(2,1)S(1)}, u32[]{:S(2)}, u32[]{:S(2)}) collective-permute-start(bf16[128,256]{1,0:T(8,128)(2,1)S(1)} %get-tuple-element.32), channel_id=1, source_target_pairs={{0,16},{8,24},{16,0},{24,8},{1,17},{9,25},{17,1},{25,9},{2,18},{10... | collective-permute-start | bytes 196616 | tf_op jit(solution)/shard_map/ppermute | solution.py:324
  27.6 0.5 %collective-permute-start.12 = (bf16[128,256]{1,0:T(8,128)(2,1)S(1)}, bf16[128,256]{1,0:T(8,128)(2,1)S(1)}, u32[]{:S(2)}, u32[]{:S(2)}) collective-permute-start(bf16[128,256]{1,0:T(8,128)(2,1)S(1)} %get-tuple-element.33), channel_id=1, source_target_pairs={{0,8},{8,0},{16,24},{24,16},{1,9},{9,1},{17,25},{25,17},{2,10},{10... | collective-permute-start | bytes 196616 | tf_op jit(solution)/shard_map/ppermute | solution.py:324
  28.1 2.1 %collective-permute-done.10.refs_0_ = bf16[128,256]{1,0:T(8,128)(2,1)S(1)} collective-permute-done((bf16[128,256]{1,0:T(8,128)(2,1)S(1)}, bf16[128,256]{1,0:T(8,128)(2,1)S(1)}, u32[]{:S(2)}, u32[]{:S(2)}) %collective-permute-start.10) | collective-permute-done | bytes 65568 | tf_op jit(solution)/shard_map/ppermute | solution.py:324
  30.2 0.5 %collective-permute-done.11.refs_1_ = bf16[128,256]{1,0:T(8,128)(2,1)S(1)} collective-permute-done((bf16[128,256]{1,0:T(8,128)(2,1)S(1)}, bf16[128,256]{1,0:T(8,128)(2,1)S(1)}, u32[]{:S(2)}, u32[]{:S(2)}) %collective-permute-start.11) | collective-permute-done | bytes 65568 | tf_op jit(solution)/shard_map/ppermute | solution.py:324
  30.7 1.1 %collective-permute-done.12.refs_2_ = bf16[128,256]{1,0:T(8,128)(2,1)S(1)} collective-permute-done((bf16[128,256]{1,0:T(8,128)(2,1)S(1)}, bf16[128,256]{1,0:T(8,128)(2,1)S(1)}, u32[]{:S(2)}, u32[]{:S(2)}) %collective-permute-start.12) | collective-permute-done | bytes 65568 | tf_op jit(solution)/shard_map/ppermute | solution.py:324
  31.9 1.2 %shard_map.59 = (bf16[3,64,512]{2,1,0:T(8,128)(2,1)S(1)}, bf16[4,128,1024]{2,1,0:T(8,128)(2,1)S(1)}) custom-call(bf16[128,256]{1,0:T(8,128)(2,1)S(1)} %collective-permute-done.10.refs_0_, bf16[128,256]{1,0:T(8,128)(2,1)S(1)} %collective-permute-done.11.refs_1_, bf16[128,256]{1,0:T(8,128)(2,1)S(1)} %collective-permute-done.12.refs_2_, ...), custom_call_target="tpu_custom_call" | custom-call | tf_op jit(solution)/shard_map/pallas_call | solution.py:416
  33.2 0.5 %shard_map.60.refs_0_ = bf16[1,64,512]{2,1,0:T(8,128)(2,1)S(1)} custom-call(bf16[4,128,1024]{2,1,0:T(8,128)(2,1)S(1)} %get-tuple-element.35.right_ref, bf16[8,2,512,128]{3,2,1,0:T(8,128)(2,1)S(1)} %get-tuple-element.25.refs_8_.refs_4_.orb_ref, bf16[8,2,512,128]{3,2,1,0:T(8,128)(2,1)S(1)} %get-tuple-element.26.refs_9_.refs_5_.rest_ref, ...), custom_call_target="tpu_custom_call" | custom-call | tf_op jit(solution)/shard_map/pallas_call | solution.py:427
  33.7 0.6 %collective-permute-start.17 = (bf16[1,64,512]{2,1,0:T(8,128)(2,1)S(1)}, bf16[1,64,512]{2,1,0:T(8,128)(2,1)S(1)}, u32[]{:S(2)}, u32[]{:S(2)}) collective-permute-start(bf16[1,64,512]{2,1,0:T(8,128)(2,1)S(1)} %shard_map.60.refs_0_), channel_id=1, source_target_pairs={{0,1},{1,0},{2,3},{3,2},{4,5},{5,4},{6,7},{7,6},{8,9},{9,8},{10,11... | collective-permute-start | bytes 196616 | tf_op jit(solution)/shard_map/ppermute | solution.py:324
  34.2 1.2 %shard_map.61.keep_ref = f32[3,64,512]{2,1,0:T(8,128)S(1)} custom-call(bf16[4,128,1024]{2,1,0:T(8,128)(2,1)S(1)} %get-tuple-element.35.right_ref, bf16[8,2,512,128]{3,2,1,0:T(8,128)(2,1)S(1)} %get-tuple-element.25.refs_8_.refs_4_.orb_ref, bf16[8,2,512,128]{3,2,1,0:T(8,128)(2,1)S(1)} %get-tuple-element.26.refs_9_.refs_5_.rest_ref, ...), custom_call_target="tpu_custom_call" | custom-call | tf_op jit(solution)/shard_map/pallas_call | solution.py:427
  35.5 1.6 %collective-permute-start.14 = (bf16[64,512]{1,0:T(8,128)(2,1)S(1)}, bf16[64,512]{1,0:T(8,128)(2,1)S(1)}, u32[]{:S(2)}, u32[]{:S(2)}) collective-permute-start(bf16[64,512]{1,0:T(8,128)(2,1)S(1)} %get-tuple-element.37), channel_id=1, source_target_pairs={{0,2},{1,3},{2,4},{3,5},{4,6},{5,7},{6,0},{7,1},{8,10},{9,11},{10,... | collective-permute-start | bytes 196616 | tf_op jit(solution)/shard_map/ppermute | solution.py:336
  37.1 1.2 %collective-permute-start.15 = (bf16[64,512]{1,0:T(8,128)(2,1)S(1)}, bf16[64,512]{1,0:T(8,128)(2,1)S(1)}, u32[]{:S(2)}, u32[]{:S(2)}) collective-permute-start(bf16[64,512]{1,0:T(8,128)(2,1)S(1)} %get-tuple-element.38), channel_id=1, source_target_pairs={{0,4},{1,5},{2,6},{3,7},{4,0},{5,1},{6,2},{7,3},{8,12},{9,13},{10,... | collective-permute-start | bytes 196616 | tf_op jit(solution)/shard_map/ppermute | solution.py:336
  38.2 2.2 %collective-permute-start.16 = (bf16[64,512]{1,0:T(8,128)(2,1)S(1)}, bf16[64,512]{1,0:T(8,128)(2,1)S(1)}, u32[]{:S(2)}, u32[]{:S(2)}) collective-permute-start(bf16[64,512]{1,0:T(8,128)(2,1)S(1)} %get-tuple-element.39.refs_0_), channel_id=1, source_target_pairs={{0,6},{1,7},{2,0},{3,1},{4,2},{5,3},{6,4},{7,5},{8,14},{9,15},{10,... | collective-permute-start | bytes 196616 | tf_op jit(solution)/shard_map/ppermute | solution.py:336
  40.4 0.5 %shard_map.63.keep_ref = f32[1,64,512]{2,1,0:T(8,128)S(1)} custom-call(bf16[4,128,1024]{2,1,0:T(8,128)(2,1)S(1)} %get-tuple-element.35.right_ref, bf16[8,2,512,128]{3,2,1,0:T(8,128)(2,1)S(1)} %get-tuple-element.25.refs_8_.refs_4_.orb_ref, bf16[8,2,512,128]{3,2,1,0:T(8,128)(2,1)S(1)} %get-tuple-element.26.refs_9_.refs_5_.rest_ref, ...), custom_call_target="tpu_custom_call" | custom-call | tf_op jit(solution)/shard_map/pallas_call | solution.py:427
  40.9 1.4 %collective-permute-done.14.refs_0_ = bf16[64,512]{1,0:T(8,128)(2,1)S(1)} collective-permute-done((bf16[64,512]{1,0:T(8,128)(2,1)S(1)}, bf16[64,512]{1,0:T(8,128)(2,1)S(1)}, u32[]{:S(2)}, u32[]{:S(2)}) %collective-permute-start.14) | collective-permute-done | bytes 65568 | tf_op jit(solution)/shard_map/ppermute | solution.py:336
  42.3 1.9 %collective-permute-done.15.refs_1_ = bf16[64,512]{1,0:T(8,128)(2,1)S(1)} collective-permute-done((bf16[64,512]{1,0:T(8,128)(2,1)S(1)}, bf16[64,512]{1,0:T(8,128)(2,1)S(1)}, u32[]{:S(2)}, u32[]{:S(2)}) %collective-permute-start.15) | collective-permute-done | bytes 65568 | tf_op jit(solution)/shard_map/ppermute | solution.py:336
  44.2 1.7 %shard_map.65 = bf16[64,4,16,128]{3,2,1,0:T(8,128)(2,1)} custom-call(bf16[64,512]{1,0:T(8,128)(2,1)S(1)} %collective-permute-done.14.refs_0_, bf16[64,512]{1,0:T(8,128)(2,1)S(1)} %collective-permute-done.15.refs_1_, bf16[64,512]{1,0:T(8,128)(2,1)S(1)} %collective-permute-done.16.refs_2_, f32[64,512]{1,0:T(8,128)S(1)} %shard_map.64.refs_3_, ...), custom_call_target="tpu_custom_call" | custom-call | bytes 4194304 | tf_op jit(solution)/shard_map/pallas_call | solution.py:445
  (23 shorter events, 0.6 us)
Async XLA Ops:
  2.5 12.0 %copy-start = (bf16[8,32,256]{2,1,0:T(8,128)(2,1)S(1)}, bf16[8,32,256]{2,1,0:T(8,128)(2,1)}, u32[]{:S(2)}) copy-start(bf16[8,32,256]{2,1,0:T(8,128)(2,1)} %refs_11_.1) | copy-start | bytes 393220
  2.5 12.0 %copy-start.1 = (bf16[2,64,32]{2,1,0:T(8,128)(2,1)S(1)}, bf16[2,64,32]{2,1,0:T(8,128)(2,1)}, u32[]{:S(2)}) copy-start(bf16[2,64,32]{2,1,0:T(8,128)(2,1)} %constant.6.clone.refs_10_) | copy-start | bytes 24580
  2.5 8.0 %collective-permute-start.5 = (bf16[64,512]{1,0:T(8,128)(2,1)S(1)}, bf16[64,512]{1,0:T(8,128)(2,1)S(1)}, u32[]{:S(2)}, u32[]{:S(2)}) collective-permute-start(bf16[64,512]{1,0:T(8,128)(2,1)S(1)} %get-tuple-element.23.edge_hbm.refs_0_), channel_id=1, source_target_pairs={{0,6},{1,7},{2,4},{3,5},{4,2},{5,3},{6,0},{7,1},{8,14},{9,15},{10,... | collective-permute-start | bytes 196616 | tf_op jit(solution)/shard_map/ppermute | solution.py:324
  7.6 4.7 %collective-permute-start.3 = (bf16[64,512]{1,0:T(8,128)(2,1)S(1)}, bf16[64,512]{1,0:T(8,128)(2,1)S(1)}, u32[]{:S(2)}, u32[]{:S(2)}) collective-permute-start(bf16[64,512]{1,0:T(8,128)(2,1)S(1)} %get-tuple-element.23.edge_hbm.refs_0_), channel_id=1, source_target_pairs={{0,2},{1,3},{2,0},{3,1},{4,6},{5,7},{6,4},{7,5},{8,10},{9,11},{10,... | collective-permute-start | bytes 196616 | tf_op jit(solution)/shard_map/ppermute | solution.py:324
  7.7 5.6 %collective-permute-start.1 = (bf16[64,512]{1,0:T(8,128)(2,1)S(1)}, bf16[64,512]{1,0:T(8,128)(2,1)S(1)}, u32[]{:S(2)}, u32[]{:S(2)}) collective-permute-start(bf16[64,512]{1,0:T(8,128)(2,1)S(1)} %get-tuple-element.23.edge_hbm.refs_0_), channel_id=1, source_target_pairs={{0,4},{1,5},{2,6},{3,7},{4,0},{5,1},{6,2},{7,3},{8,12},{9,13},{10,... | collective-permute-start | bytes 196616 | tf_op jit(solution)/shard_map/ppermute | solution.py:324
  9.9 3.4 %collective-permute-start = (bf16[64,512]{1,0:T(8,128)(2,1)S(1)}, bf16[64,512]{1,0:T(8,128)(2,1)S(1)}, u32[]{:S(2)}, u32[]{:S(2)}) collective-permute-start(bf16[64,512]{1,0:T(8,128)(2,1)S(1)} %get-tuple-element.24), channel_id=1, source_target_pairs={{0,1},{1,0},{2,3},{3,2},{4,5},{5,4},{6,7},{7,6},{8,9},{9,8},{10,11... | collective-permute-start | bytes 196616 | tf_op jit(solution)/shard_map/ppermute | solution.py:324
  10.5 2.7 %collective-permute-start.6 = (bf16[64,512]{1,0:T(8,128)(2,1)S(1)}, bf16[64,512]{1,0:T(8,128)(2,1)S(1)}, u32[]{:S(2)}, u32[]{:S(2)}) collective-permute-start(bf16[64,512]{1,0:T(8,128)(2,1)S(1)} %collective-permute-done.5.refs_6_), channel_id=1, source_target_pairs={{0,1},{1,0},{2,3},{3,2},{4,5},{5,4},{6,7},{7,6},{8,9},{9,8},{10,11... | collective-permute-start | bytes 196616 | tf_op jit(solution)/shard_map/ppermute | solution.py:324
  12.3 1.3 %collective-permute-start.4 = (bf16[64,512]{1,0:T(8,128)(2,1)S(1)}, bf16[64,512]{1,0:T(8,128)(2,1)S(1)}, u32[]{:S(2)}, u32[]{:S(2)}) collective-permute-start(bf16[64,512]{1,0:T(8,128)(2,1)S(1)} %collective-permute-done.3.refs_4_), channel_id=1, source_target_pairs={{0,1},{1,0},{2,3},{3,2},{4,5},{5,4},{6,7},{7,6},{8,9},{9,8},{10,11... | collective-permute-start | bytes 196616 | tf_op jit(solution)/shard_map/ppermute | solution.py:324
  13.3 1.3 %collective-permute-start.2 = (bf16[64,512]{1,0:T(8,128)(2,1)S(1)}, bf16[64,512]{1,0:T(8,128)(2,1)S(1)}, u32[]{:S(2)}, u32[]{:S(2)}) collective-permute-start(bf16[64,512]{1,0:T(8,128)(2,1)S(1)} %collective-permute-done.1.refs_2_), channel_id=1, source_target_pairs={{0,1},{1,0},{2,3},{3,2},{4,5},{5,4},{6,7},{7,6},{8,9},{9,8},{10,11... | collective-permute-start | bytes 196616 | tf_op jit(solution)/shard_map/ppermute | solution.py:324
  14.5 9.4 %copy-start.2 = (bf16[64,128]{1,0:T(8,128)(2,1)S(1)}, bf16[64,128]{1,0:T(8,128)(2,1)}, u32[]{:S(2)}) copy-start(bf16[64,128]{1,0:T(8,128)(2,1)} %constant.8.clone.refs_5_) | copy-start | bytes 49156
  14.5 9.4 %copy-start.3 = (bf16[64,128]{1,0:T(8,128)(2,1)S(1)}, bf16[64,128]{1,0:T(8,128)(2,1)}, u32[]{:S(2)}) copy-start(bf16[64,128]{1,0:T(8,128)(2,1)} %constant.7.clone.refs_4_) | copy-start | bytes 49156
  15.9 5.9 %collective-permute-start.7 = (bf16[192,256]{1,0:T(8,128)(2,1)S(1)}, bf16[192,256]{1,0:T(8,128)(2,1)S(1)}, u32[]{:S(2)}, u32[]{:S(2)}) collective-permute-start(bf16[192,256]{1,0:T(8,128)(2,1)S(1)} %get-tuple-element.27), channel_id=1, source_target_pairs={{0,24},{8,16},{16,8},{24,0},{1,25},{9,17},{17,9},{25,1},{2,26},{10... | collective-permute-start | bytes 294920 | tf_op jit(solution)/shard_map/ppermute | solution.py:324
  18.5 5.4 %collective-permute-start.8 = (bf16[192,256]{1,0:T(8,128)(2,1)S(1)}, bf16[192,256]{1,0:T(8,128)(2,1)S(1)}, u32[]{:S(2)}, u32[]{:S(2)}) collective-permute-start(bf16[192,256]{1,0:T(8,128)(2,1)S(1)} %get-tuple-element.28), channel_id=1, source_target_pairs={{0,16},{8,24},{16,0},{24,8},{1,17},{9,25},{17,1},{25,9},{2,18},{10... | collective-permute-start | bytes 294920 | tf_op jit(solution)/shard_map/ppermute | solution.py:324
  19.0 5.0 %collective-permute-start.9 = (bf16[192,256]{1,0:T(8,128)(2,1)S(1)}, bf16[192,256]{1,0:T(8,128)(2,1)S(1)}, u32[]{:S(2)}, u32[]{:S(2)}) collective-permute-start(bf16[192,256]{1,0:T(8,128)(2,1)S(1)} %get-tuple-element.29), channel_id=1, source_target_pairs={{0,8},{8,0},{16,24},{24,16},{1,9},{9,1},{17,25},{25,17},{2,10},{10... | collective-permute-start | bytes 294920 | tf_op jit(solution)/shard_map/ppermute | solution.py:324
  24.5 5.7 %collective-permute-start.10 = (bf16[128,256]{1,0:T(8,128)(2,1)S(1)}, bf16[128,256]{1,0:T(8,128)(2,1)S(1)}, u32[]{:S(2)}, u32[]{:S(2)}) collective-permute-start(bf16[128,256]{1,0:T(8,128)(2,1)S(1)} %get-tuple-element.31), channel_id=1, source_target_pairs={{0,24},{8,16},{16,8},{24,0},{1,25},{9,17},{17,9},{25,1},{2,26},{10... | collective-permute-start | bytes 196616 | tf_op jit(solution)/shard_map/ppermute | solution.py:324
  26.3 4.5 %collective-permute-start.11 = (bf16[128,256]{1,0:T(8,128)(2,1)S(1)}, bf16[128,256]{1,0:T(8,128)(2,1)S(1)}, u32[]{:S(2)}, u32[]{:S(2)}) collective-permute-start(bf16[128,256]{1,0:T(8,128)(2,1)S(1)} %get-tuple-element.32), channel_id=1, source_target_pairs={{0,16},{8,24},{16,0},{24,8},{1,17},{9,25},{17,1},{25,9},{2,18},{10... | collective-permute-start | bytes 196616 | tf_op jit(solution)/shard_map/ppermute | solution.py:324
  27.6 4.3 %collective-permute-start.12 = (bf16[128,256]{1,0:T(8,128)(2,1)S(1)}, bf16[128,256]{1,0:T(8,128)(2,1)S(1)}, u32[]{:S(2)}, u32[]{:S(2)}) collective-permute-start(bf16[128,256]{1,0:T(8,128)(2,1)S(1)} %get-tuple-element.33), channel_id=1, source_target_pairs={{0,8},{8,0},{16,24},{24,16},{1,9},{9,1},{17,25},{25,17},{2,10},{10... | collective-permute-start | bytes 196616 | tf_op jit(solution)/shard_map/ppermute | solution.py:324
  33.1 2.3 %collective-permute-start.13 = (bf16[3,64,512]{2,1,0:T(8,128)(2,1)S(1)}, bf16[3,64,512]{2,1,0:T(8,128)(2,1)S(1)}, u32[]{:S(2)}, u32[]{:S(2)}) collective-permute-start(bf16[3,64,512]{2,1,0:T(8,128)(2,1)S(1)} %get-tuple-element.36.refs_0_), channel_id=1, source_target_pairs={{0,1},{1,0},{2,3},{3,2},{4,5},{5,4},{6,7},{7,6},{8,9},{9,8},{10,11... | collective-permute-start | bytes 589832 | tf_op jit(solution)/shard_map/ppermute | solution.py:324
  33.7 7.2 %collective-permute-start.17 = (bf16[1,64,512]{2,1,0:T(8,128)(2,1)S(1)}, bf16[1,64,512]{2,1,0:T(8,128)(2,1)S(1)}, u32[]{:S(2)}, u32[]{:S(2)}) collective-permute-start(bf16[1,64,512]{2,1,0:T(8,128)(2,1)S(1)} %shard_map.60.refs_0_), channel_id=1, source_target_pairs={{0,1},{1,0},{2,3},{3,2},{4,5},{5,4},{6,7},{7,6},{8,9},{9,8},{10,11... | collective-permute-start | bytes 196616 | tf_op jit(solution)/shard_map/ppermute | solution.py:324
  35.5 6.9 %collective-permute-start.14 = (bf16[64,512]{1,0:T(8,128)(2,1)S(1)}, bf16[64,512]{1,0:T(8,128)(2,1)S(1)}, u32[]{:S(2)}, u32[]{:S(2)}) collective-permute-start(bf16[64,512]{1,0:T(8,128)(2,1)S(1)} %get-tuple-element.37), channel_id=1, source_target_pairs={{0,2},{1,3},{2,4},{3,5},{4,6},{5,7},{6,0},{7,1},{8,10},{9,11},{10,... | collective-permute-start | bytes 196616 | tf_op jit(solution)/shard_map/ppermute | solution.py:336
  37.1 7.2 %collective-permute-start.15 = (bf16[64,512]{1,0:T(8,128)(2,1)S(1)}, bf16[64,512]{1,0:T(8,128)(2,1)S(1)}, u32[]{:S(2)}, u32[]{:S(2)}) collective-permute-start(bf16[64,512]{1,0:T(8,128)(2,1)S(1)} %get-tuple-element.38), channel_id=1, source_target_pairs={{0,4},{1,5},{2,6},{3,7},{4,0},{5,1},{6,2},{7,3},{8,12},{9,13},{10,... | collective-permute-start | bytes 196616 | tf_op jit(solution)/shard_map/ppermute | solution.py:336
  38.2 6.0 %collective-permute-start.16 = (bf16[64,512]{1,0:T(8,128)(2,1)S(1)}, bf16[64,512]{1,0:T(8,128)(2,1)S(1)}, u32[]{:S(2)}, u32[]{:S(2)}) collective-permute-start(bf16[64,512]{1,0:T(8,128)(2,1)S(1)} %get-tuple-element.39.refs_0_), channel_id=1, source_target_pairs={{0,6},{1,7},{2,0},{3,1},{4,2},{5,3},{6,4},{7,5},{8,14},{9,15},{10,... | collective-permute-start | bytes 196616 | tf_op jit(solution)/shard_map/ppermute | solution.py:336

commit v18 on v17

--- a/solution.py
+++ b/solution.py
@@ -145,16 +145,17 @@
     selector = sel_ref[jnp.bitwise_and(block, per_share - 1)]
     order = [0, *asked(shares)]
     for g in range(local_k // group):
-        forms = []
-        for offset in range(shares):
-            stacked = jnp.concatenate(
-                [
-                    blocks[order.index(offset) * per_share + e][g * ROWS : (g + 1) * ROWS]
-                    for e in range(per_share)
-                ],
-                axis=0,
-            )
-            forms.append(dot(selector, stacked).astype(BF16))
+        stacked = jnp.concatenate(
+            [
+                blocks[order.index(offset) * per_share + e][g * ROWS : (g + 1) * ROWS]
+                for offset in range(shares)
+                for e in range(per_share)
+            ],
+            axis=0,
+        )
+        chosen = dot(selector, stacked).astype(BF16)
+        size = 2 * group * rows
+        forms = [chosen[offset * size : (offset + 1) * size] for offset in range(shares)]
         for kk in range(group):
             k = g * group + kk
             left = [form[2 * kk * rows : (2 * kk + 1) * rows] for form in forms]
@@ -245,20 +246,19 @@
     z = lax.shift_right_logical(block, 1)
     chunks = norb // out_rows // 2
     for g in range(groups):
-        for i, offset in enumerate(offsets):
+        rows = []
+        for offset in offsets:
             start = pl.multiple_of((2 * lax.rem(z + offset, chunks) + core) * out_rows, out_rows)
-            rows = jnp.concatenate(
-                [
-                    ref[k, part, pl.ds(start, out_rows), :]
-                    for k in range(g * group, (g + 1) * group)
-                    for part in range(2)
-                    for ref in (orb_ref, rest_ref)
-                ],
-                axis=1,
-            )
-            out_ref[i, :, g * lanes : (g + 1) * lanes] = dot(rows, right_ref[g], ((1,), (1,))).astype(
-                out_ref.dtype
-            )
+            parts = [
+                ref[k, part, pl.ds(start, out_rows), :]
+                for k in range(g * group, (g + 1) * group)
+                for part in range(2)
+                for ref in (orb_ref, rest_ref)
+            ]
+            rows.append(jnp.concatenate(parts, axis=1))
+        result = dot(jnp.concatenate(rows, axis=0), right_ref[g], ((1,), (1,))).astype(out_ref.dtype)
+        for i in range(len(offsets)):
+            out_ref[i, :, g * lanes : (g + 1) * lanes] = result[i * out_rows : (i + 1) * out_rows]
 
 
 def first_weight_kernel(shares, offsets, out_rows, *refs):
@@ -381,7 +381,8 @@
             came[offset] += [block, swap(block, "pts", 1)]
     table = column_selector(group, per_share, per_block, 1).reshape(-1, per_share, ROWS)
     places = [[place ^ e for e in range(per_share)] for place in range(per_share)]
-    selector = jnp.asarray(np.stack([table[:, place].reshape(table.shape[0], -1) for place in places]))
+    tables = [table[:, place].reshape(table.shape[0], -1).astype(np.float32) for place in places]
+    selector = jnp.asarray(np.stack([np.kron(np.eye(shares, dtype=np.float32), t) for t in tables]), BF16)
     piece = shape((share * 2 * local_k, points), BF16)
     both = shape((share * 3 * local_k, points), BF16)
     *tiles, forms = call(

time: 46.1 us -> 44.8 us (0.972)
  Pallas kernels: 11.1 us -> 9.88 us
    pallas_call x1, Pallas kernels: 1.23 us -> 0.62 us  [body(): call(functools.partial(first_weight_kernel, shares, early, out_rows), [sh...]
    pallas_call x3, Pallas kernels: 2.11 us -> 1.51 us  [rows_of(): call(functools.partial(next_weight_kernel, offsets, flip, out_rows), shap...]
  transfers between devices with their start and end apart: 18 -> 18, of which waited for: 13 -> 13; matrix products, arithmetic and copies ran while one was open for 0% -> 0% of each run, Pallas kernels for 8% -> 7%
where the time goes in v18:
time: 44.8 us; the launch traced here: 44.6 us
  starting transfers between devices  18.5 us (41%)
  waiting for transfers between devices  16.1 us (36%)
  Pallas kernels  9.88 us (22%)
    ppermute x15, starting transfers between devices, swap(): return lax.ppermute(value, axis, [(i, i ^ mask) for i in range(size)])  13.6 us
    ppermute x15, waiting for transfers between devices, swap(): return lax.ppermute(value, axis, [(i, i ^ mask) for i in range(size)])  12.8 us
    ppermute x3, starting transfers between devices, shift_along(): came.append(lax.ppermute(pieces[s], 'pts', pairs))  4.93 us
    ppermute x3, waiting for transfers between devices, shift_along(): came.append(lax.ppermute(pieces[s], 'pts', pairs))  3.32 us
    pallas_call x1, Pallas kernels, body(): call(functools.partial(edge_kernel, per_block), [shape((local_k * 2 * per...  2.5 us
    pallas_call x1, Pallas kernels, body(): call(functools.partial(exchange_kernel, chunks, 1.0 / math.sqrt(points *...  1.66 us
    pallas_call x1, Pallas kernels, body(): call(rest_kernel, [shape(edge.shape, BF16), shape((local_k, 2, norb, poin...  1.58 us
    pallas_call x3, Pallas kernels, rows_of(): call(functools.partial(next_weight_kernel, offsets, flip, out_rows), shap...  1.51 us
  transfers between devices with their start and end apart: 18, of which 13 were waited for; matrix products, arithmetic and copies ran while one was open for 0% of the time, Pallas kernels for 7%

profile of v18, /device:TPU:0, one launch (start us, length us, event | category | flops | bytes accessed | tf_op | source)
XLA Modules:
  0.0 44.6 jit_solution(2712726220616286018)
XLA Ops:
  0.0 2.5 %shard_map.55 = (bf16[64,512]{1,0:T(8,128)(2,1)S(1)}, bf16[8,2,512,128]{3,2,1,0:T(8,128)(2,1)S(1)}) custom-call(bf16[8,2,512,256]{3,2,1,0:T(8,128)(2,1)} %orb_hbm.3), custom_call_target="tpu_custom_call" | custom-call | bytes 4194304 | tf_op jit(solution)/shard_map/pallas_call | solution.py:352
  2.5 5.1 %collective-permute-start.5 = (bf16[64,512]{1,0:T(8,128)(2,1)S(1)}, bf16[64,512]{1,0:T(8,128)(2,1)S(1)}, u32[]{:S(2)}, u32[]{:S(2)}) collective-permute-start(bf16[64,512]{1,0:T(8,128)(2,1)S(1)} %get-tuple-element.23.edge_hbm.refs_0_), channel_id=1, source_target_pairs={{0,6},{1,7},{2,4},{3,5},{4,2},{5,3},{6,0},{7,1},{8,14},{9,15},{10,... | collective-permute-start | bytes 196616 | tf_op jit(solution)/shard_map/ppermute | solution.py:324
  7.7 0.6 %collective-permute-start.1 = (bf16[64,512]{1,0:T(8,128)(2,1)S(1)}, bf16[64,512]{1,0:T(8,128)(2,1)S(1)}, u32[]{:S(2)}, u32[]{:S(2)}) collective-permute-start(bf16[64,512]{1,0:T(8,128)(2,1)S(1)} %get-tuple-element.23.edge_hbm.refs_0_), channel_id=1, source_target_pairs={{0,4},{1,5},{2,6},{3,7},{4,0},{5,1},{6,2},{7,3},{8,12},{9,13},{10,... | collective-permute-start | bytes 196616 | tf_op jit(solution)/shard_map/ppermute | solution.py:324
  8.3 1.6 %shard_map.56 = (bf16[64,512]{1,0:T(8,128)(2,1)S(1)}, bf16[8,2,512,128]{3,2,1,0:T(8,128)(2,1)S(1)}) custom-call(bf16[8,2,512,256]{3,2,1,0:T(8,128)(2,1)} %orb_hbm.3, bf16[64,512]{1,0:T(8,128)(2,1)S(1)} %get-tuple-element.23.edge_hbm.refs_0_), custom_call_target="tpu_custom_call" | custom-call | bytes 4194304 | tf_op jit(solution)/shard_map/pallas_call | solution.py:364
  10.0 0.6 %collective-permute-done.5.refs_6_ = bf16[64,512]{1,0:T(8,128)(2,1)S(1)} collective-permute-done((bf16[64,512]{1,0:T(8,128)(2,1)S(1)}, bf16[64,512]{1,0:T(8,128)(2,1)S(1)}, u32[]{:S(2)}, u32[]{:S(2)}) %collective-permute-start.5) | collective-permute-done | bytes 65568 | tf_op jit(solution)/shard_map/ppermute | solution.py:324
  10.6 1.8 %collective-permute-done.3.refs_4_ = bf16[64,512]{1,0:T(8,128)(2,1)S(1)} collective-permute-done((bf16[64,512]{1,0:T(8,128)(2,1)S(1)}, bf16[64,512]{1,0:T(8,128)(2,1)S(1)}, u32[]{:S(2)}, u32[]{:S(2)}) %collective-permute-start.3) | collective-permute-done | bytes 65568 | tf_op jit(solution)/shard_map/ppermute | solution.py:324
  12.3 1.0 %collective-permute-done.1.refs_2_ = bf16[64,512]{1,0:T(8,128)(2,1)S(1)} collective-permute-done((bf16[64,512]{1,0:T(8,128)(2,1)S(1)}, bf16[64,512]{1,0:T(8,128)(2,1)S(1)}, u32[]{:S(2)}, u32[]{:S(2)}) %collective-permute-start.1) | collective-permute-done | bytes 65568 | tf_op jit(solution)/shard_map/ppermute | solution.py:324
  13.6 1.0 %collective-permute-done.2.refs_3_ = bf16[64,512]{1,0:T(8,128)(2,1)S(1)} collective-permute-done((bf16[64,512]{1,0:T(8,128)(2,1)S(1)}, bf16[64,512]{1,0:T(8,128)(2,1)S(1)}, u32[]{:S(2)}, u32[]{:S(2)}) %collective-permute-start.2) | collective-permute-done | bytes 65568 | tf_op jit(solution)/shard_map/ppermute | solution.py:324
  14.6 1.4 %shard_map.57 = (bf16[192,256]{1,0:T(8,128)(2,1)S(1)}, bf16[192,256]{1,0:T(8,128)(2,1)S(1)}, bf16[192,256]{1,0:T(8,128)(2,1)S(1)}, bf16[192,256]{1,0:T(8,128)(2,1)S(1)}, bf16[4,8,16,1024]{3,2,1,0:T(8,128)(2,1)S(1)}) custom-call(bf16[64,512]{1,0:T(8,128)(2,1)S(1)} %get-tuple-element.23.edge_hbm.refs_0_, bf16[64,512]{1,0:T(8,128)(2,1)S(1)} %collective-permute-done.refs_1_, ...), custom_call_target="tpu_custom_call" | custom-call | bytes 6291456 | tf_op jit(solution)/shard_map/pallas_call | solution.py:388
  15.9 2.5 %collective-permute-start.7 = (bf16[192,256]{1,0:T(8,128)(2,1)S(1)}, bf16[192,256]{1,0:T(8,128)(2,1)S(1)}, u32[]{:S(2)}, u32[]{:S(2)}) collective-permute-start(bf16[192,256]{1,0:T(8,128)(2,1)S(1)} %get-tuple-element.27), channel_id=1, source_target_pairs={{0,24},{8,16},{16,8},{24,0},{1,25},{9,17},{17,9},{25,1},{2,26},{10... | collective-permute-start | bytes 294920 | tf_op jit(solution)/shard_map/ppermute | solution.py:324
  18.4 0.5 %collective-permute-start.8 = (bf16[192,256]{1,0:T(8,128)(2,1)S(1)}, bf16[192,256]{1,0:T(8,128)(2,1)S(1)}, u32[]{:S(2)}, u32[]{:S(2)}) collective-permute-start(bf16[192,256]{1,0:T(8,128)(2,1)S(1)} %get-tuple-element.28), channel_id=1, source_target_pairs={{0,16},{8,24},{16,0},{24,8},{1,17},{9,25},{17,1},{25,9},{2,18},{10... | collective-permute-start | bytes 294920 | tf_op jit(solution)/shard_map/ppermute | solution.py:324
  18.9 0.5 %collective-permute-start.9 = (bf16[192,256]{1,0:T(8,128)(2,1)S(1)}, bf16[192,256]{1,0:T(8,128)(2,1)S(1)}, u32[]{:S(2)}, u32[]{:S(2)}) collective-permute-start(bf16[192,256]{1,0:T(8,128)(2,1)S(1)} %get-tuple-element.29), channel_id=1, source_target_pairs={{0,8},{8,0},{16,24},{24,16},{1,9},{9,1},{17,25},{25,17},{2,10},{10... | collective-permute-start | bytes 294920 | tf_op jit(solution)/shard_map/ppermute | solution.py:324
  19.5 2.4 %collective-permute-done.7.refs_0_ = bf16[192,256]{1,0:T(8,128)(2,1)S(1)} collective-permute-done((bf16[192,256]{1,0:T(8,128)(2,1)S(1)}, bf16[192,256]{1,0:T(8,128)(2,1)S(1)}, u32[]{:S(2)}, u32[]{:S(2)}) %collective-permute-start.7) | collective-permute-done | bytes 98336 | tf_op jit(solution)/shard_map/ppermute | solution.py:324
  21.8 2.0 %collective-permute-done.8.refs_1_ = bf16[192,256]{1,0:T(8,128)(2,1)S(1)} collective-permute-done((bf16[192,256]{1,0:T(8,128)(2,1)S(1)}, bf16[192,256]{1,0:T(8,128)(2,1)S(1)}, u32[]{:S(2)}, u32[]{:S(2)}) %collective-permute-start.8) | collective-permute-done | bytes 98336 | tf_op jit(solution)/shard_map/ppermute | solution.py:324
  23.9 0.6 %shard_map.58 = (bf16[128,256]{1,0:T(8,128)(2,1)S(1)}, bf16[128,256]{1,0:T(8,128)(2,1)S(1)}, bf16[128,256]{1,0:T(8,128)(2,1)S(1)}, bf16[128,256]{1,0:T(8,128)(2,1)S(1)}) custom-call(bf16[192,256]{1,0:T(8,128)(2,1)S(1)} %collective-permute-done.7.refs_0_, bf16[192,256]{1,0:T(8,128)(2,1)S(1)} %collective-permute-done.8.refs_1_, ...), custom_call_target="tpu_custom_call" | custom-call | bytes 2097152 | tf_op jit(solution)/shard_map/pallas_call | solution.py:401
  24.5 1.8 %collective-permute-start.10 = (bf16[128,256]{1,0:T(8,128)(2,1)S(1)}, bf16[128,256]{1,0:T(8,128)(2,1)S(1)}, u32[]{:S(2)}, u32[]{:S(2)}) collective-permute-start(bf16[128,256]{1,0:T(8,128)(2,1)S(1)} %get-tuple-element.31), channel_id=1, source_target_pairs={{0,24},{8,16},{16,8},{24,0},{1,25},{9,17},{17,9},{25,1},{2,26},{10... | collective-permute-start | bytes 196616 | tf_op jit(solution)/shard_map/ppermute | solution.py:324
  26.3 1.3 %collective-permute-start.11 = (bf16[128,256]{1,0:T(8,128)(2,1)S(1)}, bf16[128,256]{1,0:T(8,128)(2,1)S(1)}, u32[]{:S(2)}, u32[]{:S(2)}) collective-permute-start(bf16[128,256]{1,0:T(8,128)(2,1)S(1)} %get-tuple-element.32), channel_id=1, source_target_pairs={{0,16},{8,24},{16,0},{24,8},{1,17},{9,25},{17,1},{25,9},{2,18},{10... | collective-permute-start | bytes 196616 | tf_op jit(solution)/shard_map/ppermute | solution.py:324
  27.6 0.5 %collective-permute-start.12 = (bf16[128,256]{1,0:T(8,128)(2,1)S(1)}, bf16[128,256]{1,0:T(8,128)(2,1)S(1)}, u32[]{:S(2)}, u32[]{:S(2)}) collective-permute-start(bf16[128,256]{1,0:T(8,128)(2,1)S(1)} %get-tuple-element.33), channel_id=1, source_target_pairs={{0,8},{8,0},{16,24},{24,16},{1,9},{9,1},{17,25},{25,17},{2,10},{10... | collective-permute-start | bytes 196616 | tf_op jit(solution)/shard_map/ppermute | solution.py:324
  28.1 2.1 %collective-permute-done.10.refs_0_ = bf16[128,256]{1,0:T(8,128)(2,1)S(1)} collective-permute-done((bf16[128,256]{1,0:T(8,128)(2,1)S(1)}, bf16[128,256]{1,0:T(8,128)(2,1)S(1)}, u32[]{:S(2)}, u32[]{:S(2)}) %collective-permute-start.10) | collective-permute-done | bytes 65568 | tf_op jit(solution)/shard_map/ppermute | solution.py:324
  30.2 0.5 %collective-permute-done.11.refs_1_ = bf16[128,256]{1,0:T(8,128)(2,1)S(1)} collective-permute-done((bf16[128,256]{1,0:T(8,128)(2,1)S(1)}, bf16[128,256]{1,0:T(8,128)(2,1)S(1)}, u32[]{:S(2)}, u32[]{:S(2)}) %collective-permute-start.11) | collective-permute-done | bytes 65568 | tf_op jit(solution)/shard_map/ppermute | solution.py:324
  30.7 1.1 %collective-permute-done.12.refs_2_ = bf16[128,256]{1,0:T(8,128)(2,1)S(1)} collective-permute-done((bf16[128,256]{1,0:T(8,128)(2,1)S(1)}, bf16[128,256]{1,0:T(8,128)(2,1)S(1)}, u32[]{:S(2)}, u32[]{:S(2)}) %collective-permute-start.12) | collective-permute-done | bytes 65568 | tf_op jit(solution)/shard_map/ppermute | solution.py:324
  31.8 0.6 %shard_map.59 = (bf16[3,64,512]{2,1,0:T(8,128)(2,1)S(1)}, bf16[4,128,1024]{2,1,0:T(8,128)(2,1)S(1)}) custom-call(bf16[128,256]{1,0:T(8,128)(2,1)S(1)} %collective-permute-done.10.refs_0_, bf16[128,256]{1,0:T(8,128)(2,1)S(1)} %collective-permute-done.11.refs_1_, bf16[128,256]{1,0:T(8,128)(2,1)S(1)} %collective-permute-done.12.refs_2_, ...), custom_call_target="tpu_custom_call" | custom-call | tf_op jit(solution)/shard_map/pallas_call | solution.py:417
  32.5 0.5 %shard_map.60.refs_0_ = bf16[1,64,512]{2,1,0:T(8,128)(2,1)S(1)} custom-call(bf16[4,128,1024]{2,1,0:T(8,128)(2,1)S(1)} %get-tuple-element.35.right_ref, bf16[8,2,512,128]{3,2,1,0:T(8,128)(2,1)S(1)} %get-tuple-element.25.refs_8_.refs_4_.orb_ref, bf16[8,2,512,128]{3,2,1,0:T(8,128)(2,1)S(1)} %get-tuple-element.26.refs_9_.refs_5_.rest_ref, ...), custom_call_target="tpu_custom_call" | custom-call | tf_op jit(solution)/shard_map/pallas_call | solution.py:428
  33.0 0.6 %collective-permute-start.17 = (bf16[1,64,512]{2,1,0:T(8,128)(2,1)S(1)}, bf16[1,64,512]{2,1,0:T(8,128)(2,1)S(1)}, u32[]{:S(2)}, u32[]{:S(2)}) collective-permute-start(bf16[1,64,512]{2,1,0:T(8,128)(2,1)S(1)} %shard_map.60.refs_0_), channel_id=1, source_target_pairs={{0,1},{1,0},{2,3},{3,2},{4,5},{5,4},{6,7},{7,6},{8,9},{9,8},{10,11... | collective-permute-start | bytes 196616 | tf_op jit(solution)/shard_map/ppermute | solution.py:324
  33.6 0.6 %shard_map.61.keep_ref = f32[3,64,512]{2,1,0:T(8,128)S(1)} custom-call(bf16[4,128,1024]{2,1,0:T(8,128)(2,1)S(1)} %get-tuple-element.35.right_ref, bf16[8,2,512,128]{3,2,1,0:T(8,128)(2,1)S(1)} %get-tuple-element.25.refs_8_.refs_4_.orb_ref, bf16[8,2,512,128]{3,2,1,0:T(8,128)(2,1)S(1)} %get-tuple-element.26.refs_9_.refs_5_.rest_ref, ...), custom_call_target="tpu_custom_call" | custom-call | tf_op jit(solution)/shard_map/pallas_call | solution.py:428
  34.2 1.6 %collective-permute-start.14 = (bf16[64,512]{1,0:T(8,128)(2,1)S(1)}, bf16[64,512]{1,0:T(8,128)(2,1)S(1)}, u32[]{:S(2)}, u32[]{:S(2)}) collective-permute-start(bf16[64,512]{1,0:T(8,128)(2,1)S(1)} %get-tuple-element.37), channel_id=1, source_target_pairs={{0,2},{1,3},{2,4},{3,5},{4,6},{5,7},{6,0},{7,1},{8,10},{9,11},{10,... | collective-permute-start | bytes 196616 | tf_op jit(solution)/shard_map/ppermute | solution.py:336
  35.8 1.2 %collective-permute-start.15 = (bf16[64,512]{1,0:T(8,128)(2,1)S(1)}, bf16[64,512]{1,0:T(8,128)(2,1)S(1)}, u32[]{:S(2)}, u32[]{:S(2)}) collective-permute-start(bf16[64,512]{1,0:T(8,128)(2,1)S(1)} %get-tuple-element.38), channel_id=1, source_target_pairs={{0,4},{1,5},{2,6},{3,7},{4,0},{5,1},{6,2},{7,3},{8,12},{9,13},{10,... | collective-permute-start | bytes 196616 | tf_op jit(solution)/shard_map/ppermute | solution.py:336
  37.0 2.1 %collective-permute-start.16 = (bf16[64,512]{1,0:T(8,128)(2,1)S(1)}, bf16[64,512]{1,0:T(8,128)(2,1)S(1)}, u32[]{:S(2)}, u32[]{:S(2)}) collective-permute-start(bf16[64,512]{1,0:T(8,128)(2,1)S(1)} %get-tuple-element.39.refs_0_), channel_id=1, source_target_pairs={{0,6},{1,7},{2,0},{3,1},{4,2},{5,3},{6,4},{7,5},{8,14},{9,15},{10,... | collective-permute-start | bytes 196616 | tf_op jit(solution)/shard_map/ppermute | solution.py:336
  39.1 0.5 %shard_map.63.keep_ref = f32[1,64,512]{2,1,0:T(8,128)S(1)} custom-call(bf16[4,128,1024]{2,1,0:T(8,128)(2,1)S(1)} %get-tuple-element.35.right_ref, bf16[8,2,512,128]{3,2,1,0:T(8,128)(2,1)S(1)} %get-tuple-element.25.refs_8_.refs_4_.orb_ref, bf16[8,2,512,128]{3,2,1,0:T(8,128)(2,1)S(1)} %get-tuple-element.26.refs_9_.refs_5_.rest_ref, ...), custom_call_target="tpu_custom_call" | custom-call | tf_op jit(solution)/shard_map/pallas_call | solution.py:428
  39.7 1.4 %collective-permute-done.14.refs_0_ = bf16[64,512]{1,0:T(8,128)(2,1)S(1)} collective-permute-done((bf16[64,512]{1,0:T(8,128)(2,1)S(1)}, bf16[64,512]{1,0:T(8,128)(2,1)S(1)}, u32[]{:S(2)}, u32[]{:S(2)}) %collective-permute-start.14) | collective-permute-done | bytes 65568 | tf_op jit(solution)/shard_map/ppermute | solution.py:336
  41.1 1.9 %collective-permute-done.15.refs_1_ = bf16[64,512]{1,0:T(8,128)(2,1)S(1)} collective-permute-done((bf16[64,512]{1,0:T(8,128)(2,1)S(1)}, bf16[64,512]{1,0:T(8,128)(2,1)S(1)}, u32[]{:S(2)}, u32[]{:S(2)}) %collective-permute-start.15) | collective-permute-done | bytes 65568 | tf_op jit(solution)/shard_map/ppermute | solution.py:336
  43.0 1.7 %shard_map.65 = bf16[64,4,16,128]{3,2,1,0:T(8,128)(2,1)} custom-call(bf16[64,512]{1,0:T(8,128)(2,1)S(1)} %collective-permute-done.14.refs_0_, bf16[64,512]{1,0:T(8,128)(2,1)S(1)} %collective-permute-done.15.refs_1_, bf16[64,512]{1,0:T(8,128)(2,1)S(1)} %collective-permute-done.16.refs_2_, f32[64,512]{1,0:T(8,128)S(1)} %shard_map.64.refs_3_, ...), custom_call_target="tpu_custom_call" | custom-call | bytes 4194304 | tf_op jit(solution)/shard_map/pallas_call | solution.py:446
  (23 shorter events, 0.6 us)
Async XLA Ops:
  2.5 12.0 %copy-start = (bf16[8,32,256]{2,1,0:T(8,128)(2,1)S(1)}, bf16[8,32,256]{2,1,0:T(8,128)(2,1)}, u32[]{:S(2)}) copy-start(bf16[8,32,256]{2,1,0:T(8,128)(2,1)} %refs_11_.1) | copy-start | bytes 393220
  2.5 12.0 %copy-start.1 = (bf16[2,256,128]{2,1,0:T(8,128)(2,1)S(1)}, bf16[2,256,128]{2,1,0:T(8,128)(2,1)}, u32[]{:S(2)}) copy-start(bf16[2,256,128]{2,1,0:T(8,128)(2,1)} %constant.6.clone.refs_10_) | copy-start | bytes 393220
  2.5 8.0 %collective-permute-start.5 = (bf16[64,512]{1,0:T(8,128)(2,1)S(1)}, bf16[64,512]{1,0:T(8,128)(2,1)S(1)}, u32[]{:S(2)}, u32[]{:S(2)}) collective-permute-start(bf16[64,512]{1,0:T(8,128)(2,1)S(1)} %get-tuple-element.23.edge_hbm.refs_0_), channel_id=1, source_target_pairs={{0,6},{1,7},{2,4},{3,5},{4,2},{5,3},{6,0},{7,1},{8,14},{9,15},{10,... | collective-permute-start | bytes 196616 | tf_op jit(solution)/shard_map/ppermute | solution.py:324
  7.6 4.7 %collective-permute-start.3 = (bf16[64,512]{1,0:T(8,128)(2,1)S(1)}, bf16[64,512]{1,0:T(8,128)(2,1)S(1)}, u32[]{:S(2)}, u32[]{:S(2)}) collective-permute-start(bf16[64,512]{1,0:T(8,128)(2,1)S(1)} %get-tuple-element.23.edge_hbm.refs_0_), channel_id=1, source_target_pairs={{0,2},{1,3},{2,0},{3,1},{4,6},{5,7},{6,4},{7,5},{8,10},{9,11},{10,... | collective-permute-start | bytes 196616 | tf_op jit(solution)/shard_map/ppermute | solution.py:324
  7.7 5.6 %collective-permute-start.1 = (bf16[64,512]{1,0:T(8,128)(2,1)S(1)}, bf16[64,512]{1,0:T(8,128)(2,1)S(1)}, u32[]{:S(2)}, u32[]{:S(2)}) collective-permute-start(bf16[64,512]{1,0:T(8,128)(2,1)S(1)} %get-tuple-element.23.edge_hbm.refs_0_), channel_id=1, source_target_pairs={{0,4},{1,5},{2,6},{3,7},{4,0},{5,1},{6,2},{7,3},{8,12},{9,13},{10,... | collective-permute-start | bytes 196616 | tf_op jit(solution)/shard_map/ppermute | solution.py:324
  9.9 3.4 %collective-permute-start = (bf16[64,512]{1,0:T(8,128)(2,1)S(1)}, bf16[64,512]{1,0:T(8,128)(2,1)S(1)}, u32[]{:S(2)}, u32[]{:S(2)}) collective-permute-start(bf16[64,512]{1,0:T(8,128)(2,1)S(1)} %get-tuple-element.24), channel_id=1, source_target_pairs={{0,1},{1,0},{2,3},{3,2},{4,5},{5,4},{6,7},{7,6},{8,9},{9,8},{10,11... | collective-permute-start | bytes 196616 | tf_op jit(solution)/shard_map/ppermute | solution.py:324
  10.5 2.7 %collective-permute-start.6 = (bf16[64,512]{1,0:T(8,128)(2,1)S(1)}, bf16[64,512]{1,0:T(8,128)(2,1)S(1)}, u32[]{:S(2)}, u32[]{:S(2)}) collective-permute-start(bf16[64,512]{1,0:T(8,128)(2,1)S(1)} %collective-permute-done.5.refs_6_), channel_id=1, source_target_pairs={{0,1},{1,0},{2,3},{3,2},{4,5},{5,4},{6,7},{7,6},{8,9},{9,8},{10,11... | collective-permute-start | bytes 196616 | tf_op jit(solution)/shard_map/ppermute | solution.py:324
  12.3 1.3 %collective-permute-start.4 = (bf16[64,512]{1,0:T(8,128)(2,1)S(1)}, bf16[64,512]{1,0:T(8,128)(2,1)S(1)}, u32[]{:S(2)}, u32[]{:S(2)}) collective-permute-start(bf16[64,512]{1,0:T(8,128)(2,1)S(1)} %collective-permute-done.3.refs_4_), channel_id=1, source_target_pairs={{0,1},{1,0},{2,3},{3,2},{4,5},{5,4},{6,7},{7,6},{8,9},{9,8},{10,11... | collective-permute-start | bytes 196616 | tf_op jit(solution)/shard_map/ppermute | solution.py:324
  13.3 1.3 %collective-permute-start.2 = (bf16[64,512]{1,0:T(8,128)(2,1)S(1)}, bf16[64,512]{1,0:T(8,128)(2,1)S(1)}, u32[]{:S(2)}, u32[]{:S(2)}) collective-permute-start(bf16[64,512]{1,0:T(8,128)(2,1)S(1)} %collective-permute-done.1.refs_2_), channel_id=1, source_target_pairs={{0,1},{1,0},{2,3},{3,2},{4,5},{5,4},{6,7},{7,6},{8,9},{9,8},{10,11... | collective-permute-start | bytes 196616 | tf_op jit(solution)/shard_map/ppermute | solution.py:324
  14.5 9.4 %copy-start.2 = (bf16[64,128]{1,0:T(8,128)(2,1)S(1)}, bf16[64,128]{1,0:T(8,128)(2,1)}, u32[]{:S(2)}) copy-start(bf16[64,128]{1,0:T(8,128)(2,1)} %constant.8.clone.refs_5_) | copy-start | bytes 49156
  14.5 9.4 %copy-start.3 = (bf16[64,128]{1,0:T(8,128)(2,1)S(1)}, bf16[64,128]{1,0:T(8,128)(2,1)}, u32[]{:S(2)}) copy-start(bf16[64,128]{1,0:T(8,128)(2,1)} %constant.7.clone.refs_4_) | copy-start | bytes 49156
  15.9 5.9 %collective-permute-start.7 = (bf16[192,256]{1,0:T(8,128)(2,1)S(1)}, bf16[192,256]{1,0:T(8,128)(2,1)S(1)}, u32[]{:S(2)}, u32[]{:S(2)}) collective-permute-start(bf16[192,256]{1,0:T(8,128)(2,1)S(1)} %get-tuple-element.27), channel_id=1, source_target_pairs={{0,24},{8,16},{16,8},{24,0},{1,25},{9,17},{17,9},{25,1},{2,26},{10... | collective-permute-start | bytes 294920 | tf_op jit(solution)/shard_map/ppermute | solution.py:324
  18.4 5.4 %collective-permute-start.8 = (bf16[192,256]{1,0:T(8,128)(2,1)S(1)}, bf16[192,256]{1,0:T(8,128)(2,1)S(1)}, u32[]{:S(2)}, u32[]{:S(2)}) collective-permute-start(bf16[192,256]{1,0:T(8,128)(2,1)S(1)} %get-tuple-element.28), channel_id=1, source_target_pairs={{0,16},{8,24},{16,0},{24,8},{1,17},{9,25},{17,1},{25,9},{2,18},{10... | collective-permute-start | bytes 294920 | tf_op jit(solution)/shard_map/ppermute | solution.py:324
  18.9 5.0 %collective-permute-start.9 = (bf16[192,256]{1,0:T(8,128)(2,1)S(1)}, bf16[192,256]{1,0:T(8,128)(2,1)S(1)}, u32[]{:S(2)}, u32[]{:S(2)}) collective-permute-start(bf16[192,256]{1,0:T(8,128)(2,1)S(1)} %get-tuple-element.29), channel_id=1, source_target_pairs={{0,8},{8,0},{16,24},{24,16},{1,9},{9,1},{17,25},{25,17},{2,10},{10... | collective-permute-start | bytes 294920 | tf_op jit(solution)/shard_map/ppermute | solution.py:324
  24.5 5.7 %collective-permute-start.10 = (bf16[128,256]{1,0:T(8,128)(2,1)S(1)}, bf16[128,256]{1,0:T(8,128)(2,1)S(1)}, u32[]{:S(2)}, u32[]{:S(2)}) collective-permute-start(bf16[128,256]{1,0:T(8,128)(2,1)S(1)} %get-tuple-element.31), channel_id=1, source_target_pairs={{0,24},{8,16},{16,8},{24,0},{1,25},{9,17},{17,9},{25,1},{2,26},{10... | collective-permute-start | bytes 196616 | tf_op jit(solution)/shard_map/ppermute | solution.py:324
  26.3 4.5 %collective-permute-start.11 = (bf16[128,256]{1,0:T(8,128)(2,1)S(1)}, bf16[128,256]{1,0:T(8,128)(2,1)S(1)}, u32[]{:S(2)}, u32[]{:S(2)}) collective-permute-start(bf16[128,256]{1,0:T(8,128)(2,1)S(1)} %get-tuple-element.32), channel_id=1, source_target_pairs={{0,16},{8,24},{16,0},{24,8},{1,17},{9,25},{17,1},{25,9},{2,18},{10... | collective-permute-start | bytes 196616 | tf_op jit(solution)/shard_map/ppermute | solution.py:324
  27.6 4.3 %collective-permute-start.12 = (bf16[128,256]{1,0:T(8,128)(2,1)S(1)}, bf16[128,256]{1,0:T(8,128)(2,1)S(1)}, u32[]{:S(2)}, u32[]{:S(2)}) collective-permute-start(bf16[128,256]{1,0:T(8,128)(2,1)S(1)} %get-tuple-element.33), channel_id=1, source_target_pairs={{0,8},{8,0},{16,24},{24,16},{1,9},{9,1},{17,25},{25,17},{2,10},{10... | collective-permute-start | bytes 196616 | tf_op jit(solution)/shard_map/ppermute | solution.py:324
  32.5 1.7 %collective-permute-start.13 = (bf16[3,64,512]{2,1,0:T(8,128)(2,1)S(1)}, bf16[3,64,512]{2,1,0:T(8,128)(2,1)S(1)}, u32[]{:S(2)}, u32[]{:S(2)}) collective-permute-start(bf16[3,64,512]{2,1,0:T(8,128)(2,1)S(1)} %get-tuple-element.36.refs_0_), channel_id=1, source_target_pairs={{0,1},{1,0},{2,3},{3,2},{4,5},{5,4},{6,7},{7,6},{8,9},{9,8},{10,11... | collective-permute-start | bytes 589832 | tf_op jit(solution)/shard_map/ppermute | solution.py:324
  33.0 6.6 %collective-permute-start.17 = (bf16[1,64,512]{2,1,0:T(8,128)(2,1)S(1)}, bf16[1,64,512]{2,1,0:T(8,128)(2,1)S(1)}, u32[]{:S(2)}, u32[]{:S(2)}) collective-permute-start(bf16[1,64,512]{2,1,0:T(8,128)(2,1)S(1)} %shard_map.60.refs_0_), channel_id=1, source_target_pairs={{0,1},{1,0},{2,3},{3,2},{4,5},{5,4},{6,7},{7,6},{8,9},{9,8},{10,11... | collective-permute-start | bytes 196616 | tf_op jit(solution)/shard_map/ppermute | solution.py:324
  34.2 6.8 %collective-permute-start.14 = (bf16[64,512]{1,0:T(8,128)(2,1)S(1)}, bf16[64,512]{1,0:T(8,128)(2,1)S(1)}, u32[]{:S(2)}, u32[]{:S(2)}) collective-permute-start(bf16[64,512]{1,0:T(8,128)(2,1)S(1)} %get-tuple-element.37), channel_id=1, source_target_pairs={{0,2},{1,3},{2,4},{3,5},{4,6},{5,7},{6,0},{7,1},{8,10},{9,11},{10,... | collective-permute-start | bytes 196616 | tf_op jit(solution)/shard_map/ppermute | solution.py:336
  35.8 7.2 %collective-permute-start.15 = (bf16[64,512]{1,0:T(8,128)(2,1)S(1)}, bf16[64,512]{1,0:T(8,128)(2,1)S(1)}, u32[]{:S(2)}, u32[]{:S(2)}) collective-permute-start(bf16[64,512]{1,0:T(8,128)(2,1)S(1)} %get-tuple-element.38), channel_id=1, source_target_pairs={{0,4},{1,5},{2,6},{3,7},{4,0},{5,1},{6,2},{7,3},{8,12},{9,13},{10,... | collective-permute-start | bytes 196616 | tf_op jit(solution)/shard_map/ppermute | solution.py:336
  37.0 6.0 %collective-permute-start.16 = (bf16[64,512]{1,0:T(8,128)(2,1)S(1)}, bf16[64,512]{1,0:T(8,128)(2,1)S(1)}, u32[]{:S(2)}, u32[]{:S(2)}) collective-permute-start(bf16[64,512]{1,0:T(8,128)(2,1)S(1)} %get-tuple-element.39.refs_0_), channel_id=1, source_target_pairs={{0,6},{1,7},{2,0},{3,1},{4,2},{5,3},{6,4},{7,5},{8,14},{9,15},{10,... | collective-permute-start | bytes 196616 | tf_op jit(solution)/shard_map/ppermute | solution.py:336

commit v19 on v18

--- a/solution.py
+++ b/solution.py
@@ -286,35 +286,32 @@
     total = pieces[0][...]
     for s in range(1, chunks):
         total = total + pieces[s][...].astype(F32)
-    total = total * scale
-    high = total.astype(BF16)
-    low = (total - high.astype(F32)).astype(BF16)
-    group = max(1, LANES // lanes)
+    total = (total * scale).astype(BF16)
+    pair = max(1, LANES // lanes)
+    group = min(local_k, max(1, 2 * LANES // lanes))
     width = group * lanes
     lane = lax.broadcasted_iota(jnp.int32, (out_rows, width), 1)
     zero = jnp.zeros((out_rows, width), BF16)
     copies = []
     for g in range(local_k // group):
-        high_g = high[:, g * width : (g + 1) * width]
-        low_g = low[:, g * width : (g + 1) * width]
-        left = []
+        part_g = total[:, g * width : (g + 1) * width]
+        left = [
+            jnp.where((lane >= kk * lanes) & (lane < (kk + 1) * lanes), part_g, zero) for kk in range(group)
+        ]
+        forms = [form_ref[d, g * group + kk] for kk in range(group) for d in range(shares)]
+        result = dot(jnp.concatenate(left, axis=0), jnp.concatenate(forms, axis=0))
         for kk in range(group):
-            keep = (lane >= kk * lanes) & (lane < (kk + 1) * lanes)
-            left.append(
-                jnp.concatenate([jnp.where(keep, high_g, zero), jnp.where(keep, low_g, zero)], axis=1)
-            )
-        forms = [form_ref[d, g * group + kk] for kk in range(group) for d in range(shares)]
-        result = dot(jnp.concatenate(left, axis=0), jnp.concatenate(forms + forms, axis=0))
-        for kk in range(group):
+            place, slot = divmod(g * group + kk, pair)
             for part in range(2):
                 for t in range(spans):
                     lane_start = part * norb + t * LANES
                     value = result[kk * out_rows : (kk + 1) * out_rows, lane_start : lane_start + LANES]
-                    start = (kk * spans + t) * 2 + part
-                    wide[g, pl.ds(start, out_rows, stride=2 * spans * group), :] = value
-        out_ref[g] = wide[g].astype(BF16).reshape(out_ref.shape[1:])
-        copies.append(pltpu.make_async_copy(out_ref.at[g], out_hbm.at[:, g], sems.at[g]))
-        copies[-1].start()
+                    start = (slot * spans + t) * 2 + part
+                    wide[place, pl.ds(start, out_rows, stride=2 * spans * pair), :] = value
+            if slot == pair - 1:
+                out_ref[place] = wide[place].astype(BF16).reshape(out_ref.shape[1:])
+                copies.append(pltpu.make_async_copy(out_ref.at[place], out_hbm.at[:, place], sems.at[place]))
+                copies[-1].start()
     for copy in copies:
         copy.wait()
 
@@ -436,9 +433,9 @@
         kinds = [shape((out_rows, lanes), BF16 if offset else F32) for offset in offsets]
         return call(pair_kernel, kinds, 2)(keep, came)
 
-    sent_late = rows_of(late, 1, BF16, sent)
-    early_sums = summed(early, rows_of(early, 0, F32, sent_late), swap(sent, "pts", 1))
-    late_sums = summed(late, rows_of(late, 0, F32, early_sums[0]), swap(sent_late, "pts", 1))
+    early_sums = summed(early, rows_of(early, 0, F32, sent), swap(sent, "pts", 1))
+    sent_late = rows_of(late, 1, BF16, early_sums[0])
+    late_sums = summed(late, rows_of(late, 0, F32, sent_late), swap(sent_late, "pts", 1))
     sums = [*late_sums, *early_sums]
     sums = shift_along(sums)
     spans = norb // LANES

time: 44.8 us -> 45.5 us (1.016)
  waiting for transfers between devices: 16.1 us -> 17.3 us
    ppermute x15, waiting for transfers between devices: 12.8 us -> 13.6 us  [swap(): return lax.ppermute(value, axis, [(i, i ^ mask) for i in range(size)])]
  transfers between devices with their start and end apart: 18 -> 18, of which waited for: 13 -> 14; matrix products, arithmetic and copies ran while one was open for 0% -> 0% of each run, Pallas kernels for 7% -> 6%
where the time goes in v19:
time: 45.5 us; the launch traced here: 45.4 us
  starting transfers between devices  18.1 us (40%)
  waiting for transfers between devices  17.3 us (38%)
  Pallas kernels  9.81 us (22%)
    ppermute x15, waiting for transfers between devices, swap(): return lax.ppermute(value, axis, [(i, i ^ mask) for i in range(size)])  13.6 us
    ppermute x15, starting transfers between devices, swap(): return lax.ppermute(value, axis, [(i, i ^ mask) for i in range(size)])  13.2 us
    ppermute x3, starting transfers between devices, shift_along(): came.append(lax.ppermute(pieces[s], 'pts', pairs))  4.9 us
    ppermute x3, waiting for transfers between devices, shift_along(): came.append(lax.ppermute(pieces[s], 'pts', pairs))  3.65 us
    pallas_call x1, Pallas kernels, body(): call(functools.partial(edge_kernel, per_block), [shape((local_k * 2 * per...  2.5 us
    pallas_call x1, Pallas kernels, body(): call(functools.partial(exchange_kernel, chunks, 1.0 / math.sqrt(points *...  1.6 us
    pallas_call x1, Pallas kernels, body(): call(rest_kernel, [shape(edge.shape, BF16), shape((local_k, 2, norb, poin...  1.58 us
    pallas_call x3, Pallas kernels, rows_of(): call(functools.partial(next_weight_kernel, offsets, flip, out_rows), shap...  1.51 us
  transfers between devices with their start and end apart: 18, of which 14 were waited for; matrix products, arithmetic and copies ran while one was open for 0% of the time, Pallas kernels for 6%

profile of v19, /device:TPU:0, one launch (start us, length us, event | category | flops | bytes accessed | tf_op | source)
XLA Modules:
  0.0 45.4 jit_solution(8424546584218004192)
XLA Ops:
  0.0 2.5 %shard_map.55 = (bf16[64,512]{1,0:T(8,128)(2,1)S(1)}, bf16[8,2,512,128]{3,2,1,0:T(8,128)(2,1)S(1)}) custom-call(bf16[8,2,512,256]{3,2,1,0:T(8,128)(2,1)} %orb_hbm.3), custom_call_target="tpu_custom_call" | custom-call | bytes 4194304 | tf_op jit(solution)/shard_map/pallas_call | solution.py:349
  2.5 5.1 %collective-permute-start.5 = (bf16[64,512]{1,0:T(8,128)(2,1)S(1)}, bf16[64,512]{1,0:T(8,128)(2,1)S(1)}, u32[]{:S(2)}, u32[]{:S(2)}) collective-permute-start(bf16[64,512]{1,0:T(8,128)(2,1)S(1)} %get-tuple-element.23.edge_hbm.refs_0_), channel_id=1, source_target_pairs={{0,6},{1,7},{2,4},{3,5},{4,2},{5,3},{6,0},{7,1},{8,14},{9,15},{10,... | collective-permute-start | bytes 196616 | tf_op jit(solution)/shard_map/ppermute | solution.py:321
  7.7 0.6 %collective-permute-start.1 = (bf16[64,512]{1,0:T(8,128)(2,1)S(1)}, bf16[64,512]{1,0:T(8,128)(2,1)S(1)}, u32[]{:S(2)}, u32[]{:S(2)}) collective-permute-start(bf16[64,512]{1,0:T(8,128)(2,1)S(1)} %get-tuple-element.23.edge_hbm.refs_0_), channel_id=1, source_target_pairs={{0,4},{1,5},{2,6},{3,7},{4,0},{5,1},{6,2},{7,3},{8,12},{9,13},{10,... | collective-permute-start | bytes 196616 | tf_op jit(solution)/shard_map/ppermute | solution.py:321
  8.3 1.6 %shard_map.56 = (bf16[64,512]{1,0:T(8,128)(2,1)S(1)}, bf16[8,2,512,128]{3,2,1,0:T(8,128)(2,1)S(1)}) custom-call(bf16[8,2,512,256]{3,2,1,0:T(8,128)(2,1)} %orb_hbm.3, bf16[64,512]{1,0:T(8,128)(2,1)S(1)} %get-tuple-element.23.edge_hbm.refs_0_), custom_call_target="tpu_custom_call" | custom-call | bytes 4194304 | tf_op jit(solution)/shard_map/pallas_call | solution.py:361
  10.0 0.6 %collective-permute-done.5.refs_6_ = bf16[64,512]{1,0:T(8,128)(2,1)S(1)} collective-permute-done((bf16[64,512]{1,0:T(8,128)(2,1)S(1)}, bf16[64,512]{1,0:T(8,128)(2,1)S(1)}, u32[]{:S(2)}, u32[]{:S(2)}) %collective-permute-start.5) | collective-permute-done | bytes 65568 | tf_op jit(solution)/shard_map/ppermute | solution.py:321
  10.6 1.8 %collective-permute-done.3.refs_4_ = bf16[64,512]{1,0:T(8,128)(2,1)S(1)} collective-permute-done((bf16[64,512]{1,0:T(8,128)(2,1)S(1)}, bf16[64,512]{1,0:T(8,128)(2,1)S(1)}, u32[]{:S(2)}, u32[]{:S(2)}) %collective-permute-start.3) | collective-permute-done | bytes 65568 | tf_op jit(solution)/shard_map/ppermute | solution.py:321
  12.3 1.0 %collective-permute-done.1.refs_2_ = bf16[64,512]{1,0:T(8,128)(2,1)S(1)} collective-permute-done((bf16[64,512]{1,0:T(8,128)(2,1)S(1)}, bf16[64,512]{1,0:T(8,128)(2,1)S(1)}, u32[]{:S(2)}, u32[]{:S(2)}) %collective-permute-start.1) | collective-permute-done | bytes 65568 | tf_op jit(solution)/shard_map/ppermute | solution.py:321
  13.6 1.0 %collective-permute-done.2.refs_3_ = bf16[64,512]{1,0:T(8,128)(2,1)S(1)} collective-permute-done((bf16[64,512]{1,0:T(8,128)(2,1)S(1)}, bf16[64,512]{1,0:T(8,128)(2,1)S(1)}, u32[]{:S(2)}, u32[]{:S(2)}) %collective-permute-start.2) | collective-permute-done | bytes 65568 | tf_op jit(solution)/shard_map/ppermute | solution.py:321
  14.6 1.4 %shard_map.57 = (bf16[192,256]{1,0:T(8,128)(2,1)S(1)}, bf16[192,256]{1,0:T(8,128)(2,1)S(1)}, bf16[192,256]{1,0:T(8,128)(2,1)S(1)}, bf16[192,256]{1,0:T(8,128)(2,1)S(1)}, bf16[4,8,16,1024]{3,2,1,0:T(8,128)(2,1)S(1)}) custom-call(bf16[64,512]{1,0:T(8,128)(2,1)S(1)} %get-tuple-element.23.edge_hbm.refs_0_, bf16[64,512]{1,0:T(8,128)(2,1)S(1)} %collective-permute-done.refs_1_, ...), custom_call_target="tpu_custom_call" | custom-call | bytes 6291456 | tf_op jit(solution)/shard_map/pallas_call | solution.py:385
  15.9 2.5 %collective-permute-start.7 = (bf16[192,256]{1,0:T(8,128)(2,1)S(1)}, bf16[192,256]{1,0:T(8,128)(2,1)S(1)}, u32[]{:S(2)}, u32[]{:S(2)}) collective-permute-start(bf16[192,256]{1,0:T(8,128)(2,1)S(1)} %get-tuple-element.27), channel_id=1, source_target_pairs={{0,24},{8,16},{16,8},{24,0},{1,25},{9,17},{17,9},{25,1},{2,26},{10... | collective-permute-start | bytes 294920 | tf_op jit(solution)/shard_map/ppermute | solution.py:321
  18.4 0.5 %collective-permute-start.8 = (bf16[192,256]{1,0:T(8,128)(2,1)S(1)}, bf16[192,256]{1,0:T(8,128)(2,1)S(1)}, u32[]{:S(2)}, u32[]{:S(2)}) collective-permute-start(bf16[192,256]{1,0:T(8,128)(2,1)S(1)} %get-tuple-element.28), channel_id=1, source_target_pairs={{0,16},{8,24},{16,0},{24,8},{1,17},{9,25},{17,1},{25,9},{2,18},{10... | collective-permute-start | bytes 294920 | tf_op jit(solution)/shard_map/ppermute | solution.py:321
  18.9 0.5 %collective-permute-start.9 = (bf16[192,256]{1,0:T(8,128)(2,1)S(1)}, bf16[192,256]{1,0:T(8,128)(2,1)S(1)}, u32[]{:S(2)}, u32[]{:S(2)}) collective-permute-start(bf16[192,256]{1,0:T(8,128)(2,1)S(1)} %get-tuple-element.29), channel_id=1, source_target_pairs={{0,8},{8,0},{16,24},{24,16},{1,9},{9,1},{17,25},{25,17},{2,10},{10... | collective-permute-start | bytes 294920 | tf_op jit(solution)/shard_map/ppermute | solution.py:321
  19.5 2.4 %collective-permute-done.7.refs_0_ = bf16[192,256]{1,0:T(8,128)(2,1)S(1)} collective-permute-done((bf16[192,256]{1,0:T(8,128)(2,1)S(1)}, bf16[192,256]{1,0:T(8,128)(2,1)S(1)}, u32[]{:S(2)}, u32[]{:S(2)}) %collective-permute-start.7) | collective-permute-done | bytes 98336 | tf_op jit(solution)/shard_map/ppermute | solution.py:321
  21.8 2.0 %collective-permute-done.8.refs_1_ = bf16[192,256]{1,0:T(8,128)(2,1)S(1)} collective-permute-done((bf16[192,256]{1,0:T(8,128)(2,1)S(1)}, bf16[192,256]{1,0:T(8,128)(2,1)S(1)}, u32[]{:S(2)}, u32[]{:S(2)}) %collective-permute-start.8) | collective-permute-done | bytes 98336 | tf_op jit(solution)/shard_map/ppermute | solution.py:321
  23.9 0.6 %shard_map.58 = (bf16[128,256]{1,0:T(8,128)(2,1)S(1)}, bf16[128,256]{1,0:T(8,128)(2,1)S(1)}, bf16[128,256]{1,0:T(8,128)(2,1)S(1)}, bf16[128,256]{1,0:T(8,128)(2,1)S(1)}) custom-call(bf16[192,256]{1,0:T(8,128)(2,1)S(1)} %collective-permute-done.7.refs_0_, bf16[192,256]{1,0:T(8,128)(2,1)S(1)} %collective-permute-done.8.refs_1_, ...), custom_call_target="tpu_custom_call" | custom-call | bytes 2097152 | tf_op jit(solution)/shard_map/pallas_call | solution.py:398
  24.5 1.8 %collective-permute-start.10 = (bf16[128,256]{1,0:T(8,128)(2,1)S(1)}, bf16[128,256]{1,0:T(8,128)(2,1)S(1)}, u32[]{:S(2)}, u32[]{:S(2)}) collective-permute-start(bf16[128,256]{1,0:T(8,128)(2,1)S(1)} %get-tuple-element.31), channel_id=1, source_target_pairs={{0,24},{8,16},{16,8},{24,0},{1,25},{9,17},{17,9},{25,1},{2,26},{10... | collective-permute-start | bytes 196616 | tf_op jit(solution)/shard_map/ppermute | solution.py:321
  26.3 1.3 %collective-permute-start.11 = (bf16[128,256]{1,0:T(8,128)(2,1)S(1)}, bf16[128,256]{1,0:T(8,128)(2,1)S(1)}, u32[]{:S(2)}, u32[]{:S(2)}) collective-permute-start(bf16[128,256]{1,0:T(8,128)(2,1)S(1)} %get-tuple-element.32), channel_id=1, source_target_pairs={{0,16},{8,24},{16,0},{24,8},{1,17},{9,25},{17,1},{25,9},{2,18},{10... | collective-permute-start | bytes 196616 | tf_op jit(solution)/shard_map/ppermute | solution.py:321
  27.6 0.5 %collective-permute-start.12 = (bf16[128,256]{1,0:T(8,128)(2,1)S(1)}, bf16[128,256]{1,0:T(8,128)(2,1)S(1)}, u32[]{:S(2)}, u32[]{:S(2)}) collective-permute-start(bf16[128,256]{1,0:T(8,128)(2,1)S(1)} %get-tuple-element.33), channel_id=1, source_target_pairs={{0,8},{8,0},{16,24},{24,16},{1,9},{9,1},{17,25},{25,17},{2,10},{10... | collective-permute-start | bytes 196616 | tf_op jit(solution)/shard_map/ppermute | solution.py:321
  28.1 2.1 %collective-permute-done.10.refs_0_ = bf16[128,256]{1,0:T(8,128)(2,1)S(1)} collective-permute-done((bf16[128,256]{1,0:T(8,128)(2,1)S(1)}, bf16[128,256]{1,0:T(8,128)(2,1)S(1)}, u32[]{:S(2)}, u32[]{:S(2)}) %collective-permute-start.10) | collective-permute-done | bytes 65568 | tf_op jit(solution)/shard_map/ppermute | solution.py:321
  30.2 0.5 %collective-permute-done.11.refs_1_ = bf16[128,256]{1,0:T(8,128)(2,1)S(1)} collective-permute-done((bf16[128,256]{1,0:T(8,128)(2,1)S(1)}, bf16[128,256]{1,0:T(8,128)(2,1)S(1)}, u32[]{:S(2)}, u32[]{:S(2)}) %collective-permute-start.11) | collective-permute-done | bytes 65568 | tf_op jit(solution)/shard_map/ppermute | solution.py:321
  30.7 1.1 %collective-permute-done.12.refs_2_ = bf16[128,256]{1,0:T(8,128)(2,1)S(1)} collective-permute-done((bf16[128,256]{1,0:T(8,128)(2,1)S(1)}, bf16[128,256]{1,0:T(8,128)(2,1)S(1)}, u32[]{:S(2)}, u32[]{:S(2)}) %collective-permute-start.12) | collective-permute-done | bytes 65568 | tf_op jit(solution)/shard_map/ppermute | solution.py:321
  31.8 0.6 %shard_map.59 = (bf16[3,64,512]{2,1,0:T(8,128)(2,1)S(1)}, bf16[4,128,1024]{2,1,0:T(8,128)(2,1)S(1)}) custom-call(bf16[128,256]{1,0:T(8,128)(2,1)S(1)} %collective-permute-done.10.refs_0_, bf16[128,256]{1,0:T(8,128)(2,1)S(1)} %collective-permute-done.11.refs_1_, bf16[128,256]{1,0:T(8,128)(2,1)S(1)} %collective-permute-done.12.refs_2_, ...), custom_call_target="tpu_custom_call" | custom-call | tf_op jit(solution)/shard_map/pallas_call | solution.py:414
  32.5 0.6 %shard_map.60.keep_ref = f32[3,64,512]{2,1,0:T(8,128)S(1)} custom-call(bf16[4,128,1024]{2,1,0:T(8,128)(2,1)S(1)} %get-tuple-element.35.right_ref, bf16[8,2,512,128]{3,2,1,0:T(8,128)(2,1)S(1)} %get-tuple-element.25.refs_8_.refs_4_.orb_ref, bf16[8,2,512,128]{3,2,1,0:T(8,128)(2,1)S(1)} %get-tuple-element.26.refs_9_.refs_5_.rest_ref, ...), custom_call_target="tpu_custom_call" | custom-call | tf_op jit(solution)/shard_map/pallas_call | solution.py:425
  33.1 0.9 %collective-permute-done.13.came_ref = bf16[3,64,512]{2,1,0:T(8,128)(2,1)S(1)} collective-permute-done((bf16[3,64,512]{2,1,0:T(8,128)(2,1)S(1)}, bf16[3,64,512]{2,1,0:T(8,128)(2,1)S(1)}, u32[]{:S(2)}, u32[]{:S(2)}) %collective-permute-start.13) | collective-permute-done | bytes 196640 | tf_op jit(solution)/shard_map/ppermute | solution.py:321
  34.0 0.5 %shard_map.62.refs_0_ = bf16[1,64,512]{2,1,0:T(8,128)(2,1)S(1)} custom-call(bf16[4,128,1024]{2,1,0:T(8,128)(2,1)S(1)} %get-tuple-element.35.right_ref, bf16[8,2,512,128]{3,2,1,0:T(8,128)(2,1)S(1)} %get-tuple-element.25.refs_8_.refs_4_.orb_ref, bf16[8,2,512,128]{3,2,1,0:T(8,128)(2,1)S(1)} %get-tuple-element.26.refs_9_.refs_5_.rest_ref, ...), custom_call_target="tpu_custom_call" | custom-call | tf_op jit(solution)/shard_map/pallas_call | solution.py:425
  34.7 1.6 %collective-permute-start.14 = (bf16[64,512]{1,0:T(8,128)(2,1)S(1)}, bf16[64,512]{1,0:T(8,128)(2,1)S(1)}, u32[]{:S(2)}, u32[]{:S(2)}) collective-permute-start(bf16[64,512]{1,0:T(8,128)(2,1)S(1)} %get-tuple-element.37), channel_id=1, source_target_pairs={{0,2},{1,3},{2,4},{3,5},{4,6},{5,7},{6,0},{7,1},{8,10},{9,11},{10,... | collective-permute-start | bytes 196616 | tf_op jit(solution)/shard_map/ppermute | solution.py:333
  36.3 1.2 %collective-permute-start.15 = (bf16[64,512]{1,0:T(8,128)(2,1)S(1)}, bf16[64,512]{1,0:T(8,128)(2,1)S(1)}, u32[]{:S(2)}, u32[]{:S(2)}) collective-permute-start(bf16[64,512]{1,0:T(8,128)(2,1)S(1)} %get-tuple-element.38), channel_id=1, source_target_pairs={{0,4},{1,5},{2,6},{3,7},{4,0},{5,1},{6,2},{7,3},{8,12},{9,13},{10,... | collective-permute-start | bytes 196616 | tf_op jit(solution)/shard_map/ppermute | solution.py:333
  37.4 2.1 %collective-permute-start.16 = (bf16[64,512]{1,0:T(8,128)(2,1)S(1)}, bf16[64,512]{1,0:T(8,128)(2,1)S(1)}, u32[]{:S(2)}, u32[]{:S(2)}) collective-permute-start(bf16[64,512]{1,0:T(8,128)(2,1)S(1)} %get-tuple-element.39.refs_0_), channel_id=1, source_target_pairs={{0,6},{1,7},{2,0},{3,1},{4,2},{5,3},{6,4},{7,5},{8,14},{9,15},{10,... | collective-permute-start | bytes 196616 | tf_op jit(solution)/shard_map/ppermute | solution.py:333
  39.6 0.5 %shard_map.63.keep_ref = f32[1,64,512]{2,1,0:T(8,128)S(1)} custom-call(bf16[4,128,1024]{2,1,0:T(8,128)(2,1)S(1)} %get-tuple-element.35.right_ref, bf16[8,2,512,128]{3,2,1,0:T(8,128)(2,1)S(1)} %get-tuple-element.25.refs_8_.refs_4_.orb_ref, bf16[8,2,512,128]{3,2,1,0:T(8,128)(2,1)S(1)} %get-tuple-element.26.refs_9_.refs_5_.rest_ref, ...), custom_call_target="tpu_custom_call" | custom-call | tf_op jit(solution)/shard_map/pallas_call | solution.py:425
  40.1 1.4 %collective-permute-done.14.refs_0_ = bf16[64,512]{1,0:T(8,128)(2,1)S(1)} collective-permute-done((bf16[64,512]{1,0:T(8,128)(2,1)S(1)}, bf16[64,512]{1,0:T(8,128)(2,1)S(1)}, u32[]{:S(2)}, u32[]{:S(2)}) %collective-permute-start.14) | collective-permute-done | bytes 65568 | tf_op jit(solution)/shard_map/ppermute | solution.py:333
  41.5 2.2 %collective-permute-done.15.refs_1_ = bf16[64,512]{1,0:T(8,128)(2,1)S(1)} collective-permute-done((bf16[64,512]{1,0:T(8,128)(2,1)S(1)}, bf16[64,512]{1,0:T(8,128)(2,1)S(1)}, u32[]{:S(2)}, u32[]{:S(2)}) %collective-permute-start.15) | collective-permute-done | bytes 65568 | tf_op jit(solution)/shard_map/ppermute | solution.py:333
  43.8 1.6 %shard_map.65 = bf16[64,4,16,128]{3,2,1,0:T(8,128)(2,1)} custom-call(bf16[64,512]{1,0:T(8,128)(2,1)S(1)} %collective-permute-done.14.refs_0_, bf16[64,512]{1,0:T(8,128)(2,1)S(1)} %collective-permute-done.15.refs_1_, bf16[64,512]{1,0:T(8,128)(2,1)S(1)} %collective-permute-done.16.refs_2_, f32[64,512]{1,0:T(8,128)S(1)} %shard_map.64.refs_3_, ...), custom_call_target="tpu_custom_call" | custom-call | bytes 4194304 | tf_op jit(solution)/shard_map/pallas_call | solution.py:443
  (23 shorter events, 0.8 us)
Async XLA Ops:
  2.5 12.0 %copy-start = (bf16[8,32,256]{2,1,0:T(8,128)(2,1)S(1)}, bf16[8,32,256]{2,1,0:T(8,128)(2,1)}, u32[]{:S(2)}) copy-start(bf16[8,32,256]{2,1,0:T(8,128)(2,1)} %refs_11_.1) | copy-start | bytes 393220
  2.5 12.0 %copy-start.1 = (bf16[2,256,128]{2,1,0:T(8,128)(2,1)S(1)}, bf16[2,256,128]{2,1,0:T(8,128)(2,1)}, u32[]{:S(2)}) copy-start(bf16[2,256,128]{2,1,0:T(8,128)(2,1)} %constant.6.clone.refs_10_) | copy-start | bytes 393220
  2.5 8.0 %collective-permute-start.5 = (bf16[64,512]{1,0:T(8,128)(2,1)S(1)}, bf16[64,512]{1,0:T(8,128)(2,1)S(1)}, u32[]{:S(2)}, u32[]{:S(2)}) collective-permute-start(bf16[64,512]{1,0:T(8,128)(2,1)S(1)} %get-tuple-element.23.edge_hbm.refs_0_), channel_id=1, source_target_pairs={{0,6},{1,7},{2,4},{3,5},{4,2},{5,3},{6,0},{7,1},{8,14},{9,15},{10,... | collective-permute-start | bytes 196616 | tf_op jit(solution)/shard_map/ppermute | solution.py:321
  7.6 4.7 %collective-permute-start.3 = (bf16[64,512]{1,0:T(8,128)(2,1)S(1)}, bf16[64,512]{1,0:T(8,128)(2,1)S(1)}, u32[]{:S(2)}, u32[]{:S(2)}) collective-permute-start(bf16[64,512]{1,0:T(8,128)(2,1)S(1)} %get-tuple-element.23.edge_hbm.refs_0_), channel_id=1, source_target_pairs={{0,2},{1,3},{2,0},{3,1},{4,6},{5,7},{6,4},{7,5},{8,10},{9,11},{10,... | collective-permute-start | bytes 196616 | tf_op jit(solution)/shard_map/ppermute | solution.py:321
  7.7 5.6 %collective-permute-start.1 = (bf16[64,512]{1,0:T(8,128)(2,1)S(1)}, bf16[64,512]{1,0:T(8,128)(2,1)S(1)}, u32[]{:S(2)}, u32[]{:S(2)}) collective-permute-start(bf16[64,512]{1,0:T(8,128)(2,1)S(1)} %get-tuple-element.23.edge_hbm.refs_0_), channel_id=1, source_target_pairs={{0,4},{1,5},{2,6},{3,7},{4,0},{5,1},{6,2},{7,3},{8,12},{9,13},{10,... | collective-permute-start | bytes 196616 | tf_op jit(solution)/shard_map/ppermute | solution.py:321
  9.9 3.4 %collective-permute-start = (bf16[64,512]{1,0:T(8,128)(2,1)S(1)}, bf16[64,512]{1,0:T(8,128)(2,1)S(1)}, u32[]{:S(2)}, u32[]{:S(2)}) collective-permute-start(bf16[64,512]{1,0:T(8,128)(2,1)S(1)} %get-tuple-element.24), channel_id=1, source_target_pairs={{0,1},{1,0},{2,3},{3,2},{4,5},{5,4},{6,7},{7,6},{8,9},{9,8},{10,11... | collective-permute-start | bytes 196616 | tf_op jit(solution)/shard_map/ppermute | solution.py:321
  10.5 2.7 %collective-permute-start.6 = (bf16[64,512]{1,0:T(8,128)(2,1)S(1)}, bf16[64,512]{1,0:T(8,128)(2,1)S(1)}, u32[]{:S(2)}, u32[]{:S(2)}) collective-permute-start(bf16[64,512]{1,0:T(8,128)(2,1)S(1)} %collective-permute-done.5.refs_6_), channel_id=1, source_target_pairs={{0,1},{1,0},{2,3},{3,2},{4,5},{5,4},{6,7},{7,6},{8,9},{9,8},{10,11... | collective-permute-start | bytes 196616 | tf_op jit(solution)/shard_map/ppermute | solution.py:321
  12.3 1.3 %collective-permute-start.4 = (bf16[64,512]{1,0:T(8,128)(2,1)S(1)}, bf16[64,512]{1,0:T(8,128)(2,1)S(1)}, u32[]{:S(2)}, u32[]{:S(2)}) collective-permute-start(bf16[64,512]{1,0:T(8,128)(2,1)S(1)} %collective-permute-done.3.refs_4_), channel_id=1, source_target_pairs={{0,1},{1,0},{2,3},{3,2},{4,5},{5,4},{6,7},{7,6},{8,9},{9,8},{10,11... | collective-permute-start | bytes 196616 | tf_op jit(solution)/shard_map/ppermute | solution.py:321
  13.3 1.3 %collective-permute-start.2 = (bf16[64,512]{1,0:T(8,128)(2,1)S(1)}, bf16[64,512]{1,0:T(8,128)(2,1)S(1)}, u32[]{:S(2)}, u32[]{:S(2)}) collective-permute-start(bf16[64,512]{1,0:T(8,128)(2,1)S(1)} %collective-permute-done.1.refs_2_), channel_id=1, source_target_pairs={{0,1},{1,0},{2,3},{3,2},{4,5},{5,4},{6,7},{7,6},{8,9},{9,8},{10,11... | collective-permute-start | bytes 196616 | tf_op jit(solution)/shard_map/ppermute | solution.py:321
  14.5 9.4 %copy-start.2 = (bf16[64,128]{1,0:T(8,128)(2,1)S(1)}, bf16[64,128]{1,0:T(8,128)(2,1)}, u32[]{:S(2)}) copy-start(bf16[64,128]{1,0:T(8,128)(2,1)} %constant.8.clone.refs_5_) | copy-start | bytes 49156
  14.5 9.4 %copy-start.3 = (bf16[64,128]{1,0:T(8,128)(2,1)S(1)}, bf16[64,128]{1,0:T(8,128)(2,1)}, u32[]{:S(2)}) copy-start(bf16[64,128]{1,0:T(8,128)(2,1)} %constant.7.clone.refs_4_) | copy-start | bytes 49156
  15.9 5.9 %collective-permute-start.7 = (bf16[192,256]{1,0:T(8,128)(2,1)S(1)}, bf16[192,256]{1,0:T(8,128)(2,1)S(1)}, u32[]{:S(2)}, u32[]{:S(2)}) collective-permute-start(bf16[192,256]{1,0:T(8,128)(2,1)S(1)} %get-tuple-element.27), channel_id=1, source_target_pairs={{0,24},{8,16},{16,8},{24,0},{1,25},{9,17},{17,9},{25,1},{2,26},{10... | collective-permute-start | bytes 294920 | tf_op jit(solution)/shard_map/ppermute | solution.py:321
  18.4 5.4 %collective-permute-start.8 = (bf16[192,256]{1,0:T(8,128)(2,1)S(1)}, bf16[192,256]{1,0:T(8,128)(2,1)S(1)}, u32[]{:S(2)}, u32[]{:S(2)}) collective-permute-start(bf16[192,256]{1,0:T(8,128)(2,1)S(1)} %get-tuple-element.28), channel_id=1, source_target_pairs={{0,16},{8,24},{16,0},{24,8},{1,17},{9,25},{17,1},{25,9},{2,18},{10... | collective-permute-start | bytes 294920 | tf_op jit(solution)/shard_map/ppermute | solution.py:321
  18.9 5.0 %collective-permute-start.9 = (bf16[192,256]{1,0:T(8,128)(2,1)S(1)}, bf16[192,256]{1,0:T(8,128)(2,1)S(1)}, u32[]{:S(2)}, u32[]{:S(2)}) collective-permute-start(bf16[192,256]{1,0:T(8,128)(2,1)S(1)} %get-tuple-element.29), channel_id=1, source_target_pairs={{0,8},{8,0},{16,24},{24,16},{1,9},{9,1},{17,25},{25,17},{2,10},{10... | collective-permute-start | bytes 294920 | tf_op jit(solution)/shard_map/ppermute | solution.py:321
  24.5 5.7 %collective-permute-start.10 = (bf16[128,256]{1,0:T(8,128)(2,1)S(1)}, bf16[128,256]{1,0:T(8,128)(2,1)S(1)}, u32[]{:S(2)}, u32[]{:S(2)}) collective-permute-start(bf16[128,256]{1,0:T(8,128)(2,1)S(1)} %get-tuple-element.31), channel_id=1, source_target_pairs={{0,24},{8,16},{16,8},{24,0},{1,25},{9,17},{17,9},{25,1},{2,26},{10... | collective-permute-start | bytes 196616 | tf_op jit(solution)/shard_map/ppermute | solution.py:321
  26.3 4.5 %collective-permute-start.11 = (bf16[128,256]{1,0:T(8,128)(2,1)S(1)}, bf16[128,256]{1,0:T(8,128)(2,1)S(1)}, u32[]{:S(2)}, u32[]{:S(2)}) collective-permute-start(bf16[128,256]{1,0:T(8,128)(2,1)S(1)} %get-tuple-element.32), channel_id=1, source_target_pairs={{0,16},{8,24},{16,0},{24,8},{1,17},{9,25},{17,1},{25,9},{2,18},{10... | collective-permute-start | bytes 196616 | tf_op jit(solution)/shard_map/ppermute | solution.py:321
  27.6 4.3 %collective-permute-start.12 = (bf16[128,256]{1,0:T(8,128)(2,1)S(1)}, bf16[128,256]{1,0:T(8,128)(2,1)S(1)}, u32[]{:S(2)}, u32[]{:S(2)}) collective-permute-start(bf16[128,256]{1,0:T(8,128)(2,1)S(1)} %get-tuple-element.33), channel_id=1, source_target_pairs={{0,8},{8,0},{16,24},{24,16},{1,9},{9,1},{17,25},{25,17},{2,10},{10... | collective-permute-start | bytes 196616 | tf_op jit(solution)/shard_map/ppermute | solution.py:321
  32.5 1.5 %collective-permute-start.13 = (bf16[3,64,512]{2,1,0:T(8,128)(2,1)S(1)}, bf16[3,64,512]{2,1,0:T(8,128)(2,1)S(1)}, u32[]{:S(2)}, u32[]{:S(2)}) collective-permute-start(bf16[3,64,512]{2,1,0:T(8,128)(2,1)S(1)} %get-tuple-element.36.refs_0_), channel_id=1, source_target_pairs={{0,1},{1,0},{2,3},{3,2},{4,5},{5,4},{6,7},{7,6},{8,9},{9,8},{10,11... | collective-permute-start | bytes 589832 | tf_op jit(solution)/shard_map/ppermute | solution.py:321
  34.5 5.6 %collective-permute-start.17 = (bf16[1,64,512]{2,1,0:T(8,128)(2,1)S(1)}, bf16[1,64,512]{2,1,0:T(8,128)(2,1)S(1)}, u32[]{:S(2)}, u32[]{:S(2)}) collective-permute-start(bf16[1,64,512]{2,1,0:T(8,128)(2,1)S(1)} %shard_map.62.refs_0_), channel_id=1, source_target_pairs={{0,1},{1,0},{2,3},{3,2},{4,5},{5,4},{6,7},{7,6},{8,9},{9,8},{10,11... | collective-permute-start | bytes 196616 | tf_op jit(solution)/shard_map/ppermute | solution.py:321
  34.7 6.8 %collective-permute-start.14 = (bf16[64,512]{1,0:T(8,128)(2,1)S(1)}, bf16[64,512]{1,0:T(8,128)(2,1)S(1)}, u32[]{:S(2)}, u32[]{:S(2)}) collective-permute-start(bf16[64,512]{1,0:T(8,128)(2,1)S(1)} %get-tuple-element.37), channel_id=1, source_target_pairs={{0,2},{1,3},{2,4},{3,5},{4,6},{5,7},{6,0},{7,1},{8,10},{9,11},{10,... | collective-permute-start | bytes 196616 | tf_op jit(solution)/shard_map/ppermute | solution.py:333
  36.3 7.5 %collective-permute-start.15 = (bf16[64,512]{1,0:T(8,128)(2,1)S(1)}, bf16[64,512]{1,0:T(8,128)(2,1)S(1)}, u32[]{:S(2)}, u32[]{:S(2)}) collective-permute-start(bf16[64,512]{1,0:T(8,128)(2,1)S(1)} %get-tuple-element.38), channel_id=1, source_target_pairs={{0,4},{1,5},{2,6},{3,7},{4,0},{5,1},{6,2},{7,3},{8,12},{9,13},{10,... | collective-permute-start | bytes 196616 | tf_op jit(solution)/shard_map/ppermute | solution.py:333
  37.4 6.3 %collective-permute-start.16 = (bf16[64,512]{1,0:T(8,128)(2,1)S(1)}, bf16[64,512]{1,0:T(8,128)(2,1)S(1)}, u32[]{:S(2)}, u32[]{:S(2)}) collective-permute-start(bf16[64,512]{1,0:T(8,128)(2,1)S(1)} %get-tuple-element.39.refs_0_), channel_id=1, source_target_pairs={{0,6},{1,7},{2,0},{3,1},{4,2},{5,3},{6,4},{7,5},{8,14},{9,15},{10,... | collective-permute-start | bytes 196616 | tf_op jit(solution)/shard_map/ppermute | solution.py:333

commit v20 on v18

--- a/solution.py
+++ b/solution.py
@@ -89,28 +89,19 @@
     )
 
 
-def load_copies(orb_hbm, orb_ref, sems, start):
-    lanes = pl.ds(start, orb_ref.shape[3])
-    copies = [
-        pltpu.make_async_copy(orb_hbm.at[k, :, :, lanes], orb_ref.at[k], sems.at[k])
-        for k in range(orb_ref.shape[0])
-    ]
-    for copy in copies:
-        copy.start()
-    return copies
-
-
-def rest_kernel(orb_hbm, edge_hbm, pass_ref, orb_ref, sems, pass_sem):
-    copies = load_copies(orb_hbm, orb_ref, sems, LANES)
-    copies.append(pltpu.make_async_copy(edge_hbm, pass_ref, pass_sem))
-    copies[-1].start()
-    for copy in copies:
-        copy.wait()
-
-
-def edge_kernel(per_block, orb_hbm, edge_ref, orb_ref, sems):
-    local_k = orb_hbm.shape[0]
-    copies = load_copies(orb_hbm, orb_ref, sems, 0)
+def coulomb_kernel(shares, coulomb_ref, out_ref, wide):
+    cells, columns, points = coulomb_ref.shape
+    share = columns // shares
+    plane = plane_of(shares)
+    wide[...] = coulomb_ref[...].astype(F32)
+    for owner in range(shares):
+        start = pl.multiple_of(jnp.bitwise_xor(owner, plane) * share, share)
+        pieces = [wide[r, pl.ds(start, share), :] for r in range(cells)]
+        out_ref[owner] = jnp.concatenate(pieces, axis=0).astype(BF16)
+
+
+def edge_kernel(per_block, orb_ref, edge_ref):
+    local_k = orb_ref.shape[0]
     row = lax.broadcasted_iota(jnp.int32, (2 * per_block, 2 * LANES), 0)
     lane = lax.broadcasted_iota(jnp.int32, (2 * per_block, 2 * LANES), 1)
     column = jnp.where(row < per_block, row, row - per_block + LANES)
@@ -119,8 +110,7 @@
     for g in range(local_k // group):
         rows = []
         for k in range(g * group, (g + 1) * group):
-            copies[k].wait()
-            both = jnp.concatenate([orb_ref[k, 0], orb_ref[k, 1]], axis=1)
+            both = jnp.concatenate([orb_ref[k, 0, :, :LANES], orb_ref[k, 1, :, :LANES]], axis=1)
             rows.append(dot(chosen, both, ((1,), (1,))))
         edge_ref[g * ROWS : (g + 1) * ROWS] = jnp.concatenate(rows, axis=0).astype(BF16)
 
@@ -134,9 +124,9 @@
 
 
 def tile_kernel(shares, per_share, per_block, *refs):
-    blocks, (orb_ref, rest_ref, sel_ref, coulomb_ref) = refs[: shares * per_share], refs[shares * per_share :][:4]
-    *outs, form_ref, wide, cells = refs[shares * per_share + 4 :]
-    local_k, _, norb, _ = orb_ref.shape
+    blocks, (orb_ref, sel_ref) = refs[: shares * per_share], refs[shares * per_share :][:2]
+    *outs, form_ref, wide = refs[shares * per_share + 2 :]
+    local_k, _, norb, points = orb_ref.shape
     group = ROWS // (2 * per_block)
     share = per_share * per_block
     rows = 2 * share
@@ -163,8 +153,7 @@
             form = jnp.concatenate(
                 [jnp.concatenate(left, axis=0), jnp.concatenate(right, axis=0)], axis=1
             )
-            halves = [ref[k].reshape(2 * norb, ref.shape[3]) for ref in (orb_ref, rest_ref)]
-            tile = dot(form, jnp.concatenate(halves, axis=1))
+            tile = dot(form, orb_ref[k].reshape(2 * norb, points))
             for offset in range(shares):
                 form_ref[jnp.bitwise_xor(plane, offset), k] = form[offset * rows : (offset + 1) * rows]
                 for part in range(2):
@@ -172,27 +161,23 @@
                     start = offset * share * 2 * local_k + 2 * k + part
                     spread(wide, start, 2 * local_k, tile[low : low + share])
     size = share * 2 * local_k
-    cells[...] = coulomb_ref[...].astype(F32)
     for s in range(shares):
         offset = jnp.bitwise_xor(me, s)
-        outs[s][:size] = take(wide, pl.multiple_of(offset * size, size), size).astype(BF16)
-        start = pl.multiple_of(jnp.bitwise_xor(offset, plane) * share, share)
-        pieces = [cells[r, pl.ds(start, share), :] for r in range(local_k)]
-        outs[s][size:] = jnp.concatenate(pieces, axis=0).astype(BF16)
+        outs[s][...] = take(wide, pl.multiple_of(offset * size, size), size).astype(BF16)
 
 
 def transform_kernel(shares, total, share, *refs):
-    tiles, (fwd_ref, bwd_ref) = refs[:shares][::-1], refs[shares : shares + 2]
-    outs, (gathered, weight, wide) = refs[shares + 2 : 2 * shares + 2], refs[2 * shares + 2 :]
+    tiles, (fwd_ref, bwd_ref, cell_ref) = refs[:shares][::-1], refs[shares : shares + 3]
+    outs, (gathered, weight, wide) = refs[shares + 3 : 2 * shares + 3], refs[2 * shares + 3 :]
     local_k = total // shares
     size = 2 * local_k * share
     me = lax.axis_index("ka")
     for s in range(shares):
         src = jnp.bitwise_xor(me, s)
-        gathered[src] = tiles[s][:size].astype(gathered.dtype)
-        cells = tiles[s][size:].astype(F32)
+        gathered[src] = tiles[s][...].astype(gathered.dtype)
+        cells = cell_ref[s].astype(F32)
         for r in range(local_k):
-            spread(weight, src * local_k + r, total, cells[r * share : (r + 1) * share])
+            spread(weight, s * local_k + r, total, cells[r * share : (r + 1) * share])
     rows = 2 * local_k
     columns = []
     for c in range(share):
@@ -237,7 +222,7 @@
         right_ref[g] = jnp.concatenate(right, axis=0)
 
 
-def weight_rows(offsets, flip, out_rows, right_ref, orb_ref, rest_ref, out_ref):
+def weight_rows(offsets, flip, out_rows, right_ref, orb_ref, out_ref):
     groups, lanes, _ = right_ref.shape
     local_k, _, norb, _ = orb_ref.shape
     group = local_k // groups
@@ -250,10 +235,9 @@
         for offset in offsets:
             start = pl.multiple_of((2 * lax.rem(z + offset, chunks) + core) * out_rows, out_rows)
             parts = [
-                ref[k, part, pl.ds(start, out_rows), :]
+                orb_ref[k, part, pl.ds(start, out_rows), :]
                 for k in range(g * group, (g + 1) * group)
                 for part in range(2)
-                for ref in (orb_ref, rest_ref)
             ]
             rows.append(jnp.concatenate(parts, axis=1))
         result = dot(jnp.concatenate(rows, axis=0), right_ref[g], ((1,), (1,))).astype(out_ref.dtype)
@@ -262,13 +246,13 @@
 
 
 def first_weight_kernel(shares, offsets, out_rows, *refs):
-    pieces, (orb_ref, rest_ref, out_ref, right_ref, gathered) = refs[:shares][::-1], refs[shares:]
+    pieces, (orb_ref, out_ref, right_ref, gathered) = refs[:shares][::-1], refs[shares:]
     weight_operands(pieces, right_ref, gathered)
-    weight_rows(offsets, 1, out_rows, right_ref, orb_ref, rest_ref, out_ref)
-
-
-def next_weight_kernel(offsets, flip, out_rows, right_ref, orb_ref, rest_ref, *refs):
-    weight_rows(offsets, flip, out_rows, right_ref, orb_ref, rest_ref, refs[-1])
+    weight_rows(offsets, 1, out_rows, right_ref, orb_ref, out_ref)
+
+
+def next_weight_kernel(offsets, flip, out_rows, right_ref, orb_ref, *refs):
+    weight_rows(offsets, flip, out_rows, right_ref, orb_ref, refs[-1])
 
 
 def pair_kernel(keep_ref, came_ref, *outs):
@@ -349,29 +333,20 @@
     group = ROWS // (2 * per_block)
     shape = jax.ShapeDtypeStruct
 
-    edge, first = call(
+    cells = call(
+        functools.partial(coulomb_kernel, shares),
+        shape((shares, local_k * share, points), BF16),
+        1,
+        [pltpu.VMEM(coulomb.shape, F32)],
+    )(coulomb)
+    cells = lax.all_to_all(cells, "ka", split_axis=0, concat_axis=0, tiled=True)
+    edge = call(
         functools.partial(edge_kernel, per_block),
-        [
-            shape((local_k * 2 * per_block, norb), BF16),
-            shape((local_k, 2, norb, LANES), BF16),
-        ],
-        0,
-        [pltpu.SemaphoreType.DMA((local_k,))],
-        limit=50,
-        size=4 * MIB,
-        unread=1,
+        shape((local_k * 2 * per_block, norb), BF16),
+        1,
     )(orbitals)
-    passed_edge, rest = call(
-        rest_kernel,
-        [shape(edge.shape, BF16), shape((local_k, 2, norb, points - LANES), BF16)],
-        0,
-        [pltpu.SemaphoreType.DMA((local_k,)), pltpu.SemaphoreType.DMA],
-        limit=49,
-        size=4 * MIB,
-        unread=2,
-    )(orbitals, edge)
     per_share = blocks // shares
-    partner = swap(passed_edge, "pts", 1)
+    partner = swap(edge, "pts", 1)
     came = [edge, partner] + [swap(edge, "pts", 2 * e + c) for e in range(1, per_share // 2) for c in range(2)]
     came = {0: came}
     for offset in asked(shares):
@@ -384,31 +359,29 @@
     tables = [table[:, place].reshape(table.shape[0], -1).astype(np.float32) for place in places]
     selector = jnp.asarray(np.stack([np.kron(np.eye(shares, dtype=np.float32), t) for t in tables]), BF16)
     piece = shape((share * 2 * local_k, points), BF16)
-    both = shape((share * 3 * local_k, points), BF16)
     *tiles, forms = call(
         functools.partial(tile_kernel, shares, per_share, per_block),
-        [both] * shares + [shape((shares, local_k, 2 * share, 2 * norb), BF16)],
-        blocks + 4,
+        [piece] * shares + [shape((shares, local_k, 2 * share, 2 * norb), BF16)],
+        blocks + 2,
         [
             tiled(shares * share * 2 * local_k, points),
-            pltpu.VMEM(coulomb.shape, F32),
         ],
         size=6 * MIB,
-    )(*[block for offset in [0, *asked(shares)] for block in came[offset]], first, rest, selector, coulomb)
+    )(*[block for offset in [0, *asked(shares)] for block in came[offset]], orbitals, selector)
     tiles = trade(tiles, "ka", 1)
 
     forward, backward = phase_tables(total)
     kernels = call(
         functools.partial(transform_kernel, shares, total, share),
         [piece] * shares,
-        shares + 2,
+        shares + 3,
         [
             pltpu.VMEM((shares, share * 2 * local_k, points), BF16 if local_k % 8 == 0 else F32),
             tiled(share * total, points),
             tiled(2 * total * share, points),
         ],
         size=2 * MIB,
-    )(*tiles, jnp.asarray(forward), jnp.asarray(backward))
+    )(*tiles, jnp.asarray(forward), jnp.asarray(backward), cells)
     kernels = trade(kernels, "ka", 1)
 
     lanes = local_k * 2 * columns
@@ -420,17 +393,17 @@
             shape((len(early), out_rows, lanes), BF16),
             shape((local_k // pair, pair * 2 * columns, pair * 2 * points), BF16),
         ],
-        shares + 2,
+        shares + 1,
         [pltpu.VMEM((shares, share * 2 * local_k, points), BF16)],
-    )(*kernels, first, rest)
+    )(*kernels, orbitals)
 
     def rows_of(offsets, flip, kind, before):
         return call(
             functools.partial(next_weight_kernel, offsets, flip, out_rows),
             shape((len(offsets), out_rows, lanes), kind),
-            3,
+            2,
             unread=1,
-        )(right, first, rest, before)
+        )(right, orbitals, before)
 
     def summed(offsets, keep, came):
         kinds = [shape((out_rows, lanes), BF16 if offset else F32) for offset in offsets]

time: 44.8 us -> 51.6 us (1.15)
  local copies, waits for them, and re-layouts: 0.02 us -> 6.58 us
  starting transfers between devices: 18.5 us -> 22.1 us
  Pallas kernels: 9.88 us -> 7.07 us
  waiting for transfers between devices: 16.1 us -> 15.3 us
    unnamed x8 -> x16, local copies, waits for them, and re-layouts: 0.02 us -> 6.58 us
    all_to_all x0 -> x1, starting transfers between devices: none -> 3.72 us  [body(): cells = lax.all_to_all(cells, 'ka', split_axis=0, concat_axis=0, tiled=True)]
    pallas_call x3, Pallas kernels: 5.44 us -> 2.7 us  [the longest x1 1.36 us: body(): call(functools.partial(tile_kernel, shares, per_share, per_block), [piece...]
    ppermute x15, waiting for transfers between devices: 12.8 us -> 12 us  [swap(): return lax.ppermute(value, axis, [(i, i ^ mask) for i in range(size)])]
  transfers between devices with their start and end apart: 18 -> 19, of which waited for: 13 -> 11; matrix products, arithmetic and copies ran while one was open for 0% -> 0% of each run, Pallas kernels for 7% -> 7%
where the time goes in v20:
time: 51.6 us; the launch traced here: 51.3 us
  starting transfers between devices  22.1 us (43%)
  waiting for transfers between devices  15.3 us (30%)
  Pallas kernels  7.07 us (14%)
  local copies, waits for them, and re-layouts  6.58 us (13%)
    ppermute x15, starting transfers between devices, swap(): return lax.ppermute(value, axis, [(i, i ^ mask) for i in range(size)])  13.5 us
    ppermute x15, waiting for transfers between devices, swap(): return lax.ppermute(value, axis, [(i, i ^ mask) for i in range(size)])  12 us
    unnamed x16, local copies, waits for them, and re-layouts  6.58 us
    ppermute x3, starting transfers between devices, shift_along(): came.append(lax.ppermute(pieces[s], 'pts', pairs))  4.93 us
    all_to_all x1, starting transfers between devices, body(): cells = lax.all_to_all(cells, 'ka', split_axis=0, concat_axis=0, tiled=True)  3.72 us
    ppermute x3, waiting for transfers between devices, shift_along(): came.append(lax.ppermute(pieces[s], 'pts', pairs))  3.32 us
    pallas_call x1, Pallas kernels, body(): call(functools.partial(exchange_kernel, chunks, 1.0 / math.sqrt(points *...  1.66 us
    pallas_call x3, Pallas kernels, rows_of(): call(functools.partial(next_weight_kernel, offsets, flip, out_rows), shap...  1.51 us
  transfers between devices with their start and end apart: 19, of which 11 were waited for; matrix products, arithmetic and copies ran while one was open for 0% of the time, Pallas kernels for 7%

profile of v20, /device:TPU:0, one launch (start us, length us, event | category | flops | bytes accessed | tf_op | source)
XLA Modules:
  0.0 51.3 jit_solution(6165337421323326912)
XLA Ops:
  0.0 2.2 %copy-done = bf16[8,2,512,256]{3,2,1,0:T(8,128)(2,1)S(1)} copy-done((bf16[8,2,512,256]{3,2,1,0:T(8,128)(2,1)S(1)}, bf16[8,2,512,256]{3,2,1,0:T(8,128)(2,1)}, u32[]{:S(2)}) %copy-start) | copy-done | bytes 4194328
  2.2 0.6 %shard_map.55.refs_0_ = bf16[64,512]{1,0:T(8,128)(2,1)S(1)} custom-call(bf16[8,2,512,256]{3,2,1,0:T(8,128)(2,1)S(1)} %copy-done), custom_call_target="tpu_custom_call" | custom-call | tf_op jit(solution)/shard_map/pallas_call | solution.py:343
  2.8 5.1 %collective-permute-start.5 = (bf16[64,512]{1,0:T(8,128)(2,1)S(1)}, bf16[64,512]{1,0:T(8,128)(2,1)S(1)}, u32[]{:S(2)}, u32[]{:S(2)}) collective-permute-start(bf16[64,512]{1,0:T(8,128)(2,1)S(1)} %shard_map.55.refs_0_), channel_id=1, source_target_pairs={{0,6},{1,7},{2,4},{3,5},{4,2},{5,3},{6,0},{7,1},{8,14},{9,15},{10,... | collective-permute-start | bytes 196616 | tf_op jit(solution)/shard_map/ppermute | solution.py:308
  7.9 0.6 %collective-permute-start.1 = (bf16[64,512]{1,0:T(8,128)(2,1)S(1)}, bf16[64,512]{1,0:T(8,128)(2,1)S(1)}, u32[]{:S(2)}, u32[]{:S(2)}) collective-permute-start(bf16[64,512]{1,0:T(8,128)(2,1)S(1)} %shard_map.55.refs_0_), channel_id=1, source_target_pairs={{0,4},{1,5},{2,6},{3,7},{4,0},{5,1},{6,2},{7,3},{8,12},{9,13},{10,... | collective-permute-start | bytes 196616 | tf_op jit(solution)/shard_map/ppermute | solution.py:308
  8.5 2.3 %collective-permute-done.5.refs_6_ = bf16[64,512]{1,0:T(8,128)(2,1)S(1)} collective-permute-done((bf16[64,512]{1,0:T(8,128)(2,1)S(1)}, bf16[64,512]{1,0:T(8,128)(2,1)S(1)}, u32[]{:S(2)}, u32[]{:S(2)}) %collective-permute-start.5) | collective-permute-done | bytes 65568 | tf_op jit(solution)/shard_map/ppermute | solution.py:308
  10.8 1.8 %collective-permute-done.3.refs_4_ = bf16[64,512]{1,0:T(8,128)(2,1)S(1)} collective-permute-done((bf16[64,512]{1,0:T(8,128)(2,1)S(1)}, bf16[64,512]{1,0:T(8,128)(2,1)S(1)}, u32[]{:S(2)}, u32[]{:S(2)}) %collective-permute-start.3) | collective-permute-done | bytes 65568 | tf_op jit(solution)/shard_map/ppermute | solution.py:308
  12.6 1.0 %collective-permute-done.1.refs_2_ = bf16[64,512]{1,0:T(8,128)(2,1)S(1)} collective-permute-done((bf16[64,512]{1,0:T(8,128)(2,1)S(1)}, bf16[64,512]{1,0:T(8,128)(2,1)S(1)}, u32[]{:S(2)}, u32[]{:S(2)}) %collective-permute-start.1) | collective-permute-done | bytes 65568 | tf_op jit(solution)/shard_map/ppermute | solution.py:308
  13.6 0.7 %shard_map.57 = bf16[4,64,256]{2,1,0:T(8,128)(2,1)} custom-call(bf16[8,32,256]{2,1,0:T(8,128)(2,1)S(1)} %copy-done.5), custom_call_target="tpu_custom_call" | custom-call | tf_op jit(solution)/shard_map/pallas_call | solution.py:336
  14.2 3.7 %all-to-all-start = ((bf16[4,64,256]{2,1,0:T(8,128)(2,1)}), bf16[4,64,256]{2,1,0:T(8,128)(2,1)S(1)}, u32[]{:S(2)}, u32[]{:S(2)}) async-start(bf16[4,64,256]{2,1,0:T(8,128)(2,1)} %shard_map.57), calls=%async_computation | async-start | bytes 262144 | tf_op jit(solution)/shard_map/all_to_all | solution.py:342
  18.0 2.2 %copy-done.1 = bf16[8,2,512,256]{3,2,1,0:T(8,128)(2,1)S(1)} copy-done((bf16[8,2,512,256]{3,2,1,0:T(8,128)(2,1)S(1)}, bf16[8,2,512,256]{3,2,1,0:T(8,128)(2,1)}, u32[]{:S(2)}) %copy-start.1) | copy-done | bytes 4194328
  20.2 1.4 %shard_map.56 = (bf16[128,256]{1,0:T(8,128)(2,1)S(1)}, bf16[128,256]{1,0:T(8,128)(2,1)S(1)}, bf16[128,256]{1,0:T(8,128)(2,1)S(1)}, bf16[128,256]{1,0:T(8,128)(2,1)S(1)}, bf16[4,8,16,1024]{3,2,1,0:T(8,128)(2,1)S(1)}) custom-call(bf16[64,512]{1,0:T(8,128)(2,1)S(1)} %shard_map.55.refs_0_, bf16[64,512]{1,0:T(8,128)(2,1)S(1)} %collective-permute-done.refs_1_, ...), custom_call_target="tpu_custom_call" | custom-call | bytes 6291456 | tf_op jit(solution)/shard_map/pallas_call | solution.py:362
  21.6 3.0 %collective-permute-start.7 = (bf16[128,256]{1,0:T(8,128)(2,1)S(1)}, bf16[128,256]{1,0:T(8,128)(2,1)S(1)}, u32[]{:S(2)}, u32[]{:S(2)}) collective-permute-start(bf16[128,256]{1,0:T(8,128)(2,1)S(1)} %get-tuple-element.19), channel_id=1, source_target_pairs={{0,24},{8,16},{16,8},{24,0},{1,25},{9,17},{17,9},{25,1},{2,26},{10... | collective-permute-start | bytes 196616 | tf_op jit(solution)/shard_map/ppermute | solution.py:308
  24.5 0.6 %collective-permute-start.8 = (bf16[128,256]{1,0:T(8,128)(2,1)S(1)}, bf16[128,256]{1,0:T(8,128)(2,1)S(1)}, u32[]{:S(2)}, u32[]{:S(2)}) collective-permute-start(bf16[128,256]{1,0:T(8,128)(2,1)S(1)} %get-tuple-element.20), channel_id=1, source_target_pairs={{0,16},{8,24},{16,0},{24,8},{1,17},{9,25},{17,1},{25,9},{2,18},{10... | collective-permute-start | bytes 196616 | tf_op jit(solution)/shard_map/ppermute | solution.py:308
  25.2 1.6 %collective-permute-done.7.refs_0_ = bf16[128,256]{1,0:T(8,128)(2,1)S(1)} collective-permute-done((bf16[128,256]{1,0:T(8,128)(2,1)S(1)}, bf16[128,256]{1,0:T(8,128)(2,1)S(1)}, u32[]{:S(2)}, u32[]{:S(2)}) %collective-permute-start.7) | collective-permute-done | bytes 65568 | tf_op jit(solution)/shard_map/ppermute | solution.py:308
  26.8 2.0 %collective-permute-done.8.refs_1_ = bf16[128,256]{1,0:T(8,128)(2,1)S(1)} collective-permute-done((bf16[128,256]{1,0:T(8,128)(2,1)S(1)}, bf16[128,256]{1,0:T(8,128)(2,1)S(1)}, u32[]{:S(2)}, u32[]{:S(2)}) %collective-permute-start.8) | collective-permute-done | bytes 65568 | tf_op jit(solution)/shard_map/ppermute | solution.py:308
  28.8 0.6 %collective-permute-done.9.refs_2_ = bf16[128,256]{1,0:T(8,128)(2,1)S(1)} collective-permute-done((bf16[128,256]{1,0:T(8,128)(2,1)S(1)}, bf16[128,256]{1,0:T(8,128)(2,1)S(1)}, u32[]{:S(2)}, u32[]{:S(2)}) %collective-permute-start.9) | collective-permute-done | bytes 65568 | tf_op jit(solution)/shard_map/ppermute | solution.py:308
  29.4 0.5 %shard_map.58 = (bf16[128,256]{1,0:T(8,128)(2,1)S(1)}, bf16[128,256]{1,0:T(8,128)(2,1)S(1)}, bf16[128,256]{1,0:T(8,128)(2,1)S(1)}, bf16[128,256]{1,0:T(8,128)(2,1)S(1)}) custom-call(bf16[128,256]{1,0:T(8,128)(2,1)S(1)} %collective-permute-done.7.refs_0_, bf16[128,256]{1,0:T(8,128)(2,1)S(1)} %collective-permute-done.8.refs_1_, ...), custom_call_target="tpu_custom_call" | custom-call | bytes 2097152 | tf_op jit(solution)/shard_map/pallas_call | solution.py:374
  29.9 1.5 %collective-permute-start.10 = (bf16[128,256]{1,0:T(8,128)(2,1)S(1)}, bf16[128,256]{1,0:T(8,128)(2,1)S(1)}, u32[]{:S(2)}, u32[]{:S(2)}) collective-permute-start(bf16[128,256]{1,0:T(8,128)(2,1)S(1)} %get-tuple-element.23), channel_id=1, source_target_pairs={{0,24},{8,16},{16,8},{24,0},{1,25},{9,17},{17,9},{25,1},{2,26},{10... | collective-permute-start | bytes 196616 | tf_op jit(solution)/shard_map/ppermute | solution.py:308
  31.4 0.5 %collective-permute-start.11 = (bf16[128,256]{1,0:T(8,128)(2,1)S(1)}, bf16[128,256]{1,0:T(8,128)(2,1)S(1)}, u32[]{:S(2)}, u32[]{:S(2)}) collective-permute-start(bf16[128,256]{1,0:T(8,128)(2,1)S(1)} %get-tuple-element.24), channel_id=1, source_target_pairs={{0,16},{8,24},{16,0},{24,8},{1,17},{9,25},{17,1},{25,9},{2,18},{10... | collective-permute-start | bytes 196616 | tf_op jit(solution)/shard_map/ppermute | solution.py:308
  32.0 1.5 %collective-permute-start.12 = (bf16[128,256]{1,0:T(8,128)(2,1)S(1)}, bf16[128,256]{1,0:T(8,128)(2,1)S(1)}, u32[]{:S(2)}, u32[]{:S(2)}) collective-permute-start(bf16[128,256]{1,0:T(8,128)(2,1)S(1)} %get-tuple-element.25), channel_id=1, source_target_pairs={{0,8},{8,0},{16,24},{24,16},{1,9},{9,1},{17,25},{25,17},{2,10},{10... | collective-permute-start | bytes 196616 | tf_op jit(solution)/shard_map/ppermute | solution.py:308
  33.5 1.7 %collective-permute-done.10.refs_0_ = bf16[128,256]{1,0:T(8,128)(2,1)S(1)} collective-permute-done((bf16[128,256]{1,0:T(8,128)(2,1)S(1)}, bf16[128,256]{1,0:T(8,128)(2,1)S(1)}, u32[]{:S(2)}, u32[]{:S(2)}) %collective-permute-start.10) | collective-permute-done | bytes 65568 | tf_op jit(solution)/shard_map/ppermute | solution.py:308
  35.2 0.7 %collective-permute-done.11.refs_1_ = bf16[128,256]{1,0:T(8,128)(2,1)S(1)} collective-permute-done((bf16[128,256]{1,0:T(8,128)(2,1)S(1)}, bf16[128,256]{1,0:T(8,128)(2,1)S(1)}, u32[]{:S(2)}, u32[]{:S(2)}) %collective-permute-start.11) | collective-permute-done | bytes 65568 | tf_op jit(solution)/shard_map/ppermute | solution.py:308
  36.2 2.2 %copy-done.2 = bf16[8,2,512,256]{3,2,1,0:T(8,128)(2,1)S(1)} copy-done((bf16[8,2,512,256]{3,2,1,0:T(8,128)(2,1)S(1)}, bf16[8,2,512,256]{3,2,1,0:T(8,128)(2,1)}, u32[]{:S(2)}) %copy-start.2) | copy-done | bytes 4194328
  38.4 0.6 %shard_map.59 = (bf16[3,64,512]{2,1,0:T(8,128)(2,1)S(1)}, bf16[4,128,1024]{2,1,0:T(8,128)(2,1)S(1)}) custom-call(bf16[128,256]{1,0:T(8,128)(2,1)S(1)} %collective-permute-done.10.refs_0_, bf16[128,256]{1,0:T(8,128)(2,1)S(1)} %collective-permute-done.11.refs_1_, bf16[128,256]{1,0:T(8,128)(2,1)S(1)} %collective-permute-done.12.refs_2_, ...), custom_call_target="tpu_custom_call" | custom-call | tf_op jit(solution)/shard_map/pallas_call | solution.py:390
  39.6 0.6 %collective-permute-start.17 = (bf16[1,64,512]{2,1,0:T(8,128)(2,1)S(1)}, bf16[1,64,512]{2,1,0:T(8,128)(2,1)S(1)}, u32[]{:S(2)}, u32[]{:S(2)}) collective-permute-start(bf16[1,64,512]{2,1,0:T(8,128)(2,1)S(1)} %shard_map.60.refs_0_), channel_id=1, source_target_pairs={{0,1},{1,0},{2,3},{3,2},{4,5},{5,4},{6,7},{7,6},{8,9},{9,8},{10,11... | collective-permute-start | bytes 196616 | tf_op jit(solution)/shard_map/ppermute | solution.py:308
  40.2 0.6 %shard_map.61.keep_ref = f32[3,64,512]{2,1,0:T(8,128)S(1)} custom-call(bf16[4,128,1024]{2,1,0:T(8,128)(2,1)S(1)} %get-tuple-element.27.right_ref, bf16[8,2,512,256]{3,2,1,0:T(8,128)(2,1)S(1)} %copy-done.2, bf16[1,64,512]{2,1,0:T(8,128)(2,1)S(1)} %shard_map.60.refs_0_), custom_call_target="tpu_custom_call" | custom-call | tf_op jit(solution)/shard_map/pallas_call | solution.py:401
  40.8 1.6 %collective-permute-start.14 = (bf16[64,512]{1,0:T(8,128)(2,1)S(1)}, bf16[64,512]{1,0:T(8,128)(2,1)S(1)}, u32[]{:S(2)}, u32[]{:S(2)}) collective-permute-start(bf16[64,512]{1,0:T(8,128)(2,1)S(1)} %get-tuple-element.29), channel_id=1, source_target_pairs={{0,2},{1,3},{2,4},{3,5},{4,6},{5,7},{6,0},{7,1},{8,10},{9,11},{10,... | collective-permute-start | bytes 196616 | tf_op jit(solution)/shard_map/ppermute | solution.py:320
  42.4 1.2 %collective-permute-start.15 = (bf16[64,512]{1,0:T(8,128)(2,1)S(1)}, bf16[64,512]{1,0:T(8,128)(2,1)S(1)}, u32[]{:S(2)}, u32[]{:S(2)}) collective-permute-start(bf16[64,512]{1,0:T(8,128)(2,1)S(1)} %get-tuple-element.30), channel_id=1, source_target_pairs={{0,4},{1,5},{2,6},{3,7},{4,0},{5,1},{6,2},{7,3},{8,12},{9,13},{10,... | collective-permute-start | bytes 196616 | tf_op jit(solution)/shard_map/ppermute | solution.py:320
  43.6 2.1 %collective-permute-start.16 = (bf16[64,512]{1,0:T(8,128)(2,1)S(1)}, bf16[64,512]{1,0:T(8,128)(2,1)S(1)}, u32[]{:S(2)}, u32[]{:S(2)}) collective-permute-start(bf16[64,512]{1,0:T(8,128)(2,1)S(1)} %get-tuple-element.31.refs_0_), channel_id=1, source_target_pairs={{0,6},{1,7},{2,0},{3,1},{4,2},{5,3},{6,4},{7,5},{8,14},{9,15},{10,... | collective-permute-start | bytes 196616 | tf_op jit(solution)/shard_map/ppermute | solution.py:320
  46.3 1.4 %collective-permute-done.14.refs_0_ = bf16[64,512]{1,0:T(8,128)(2,1)S(1)} collective-permute-done((bf16[64,512]{1,0:T(8,128)(2,1)S(1)}, bf16[64,512]{1,0:T(8,128)(2,1)S(1)}, u32[]{:S(2)}, u32[]{:S(2)}) %collective-permute-start.14) | collective-permute-done | bytes 65568 | tf_op jit(solution)/shard_map/ppermute | solution.py:320
  47.7 1.9 %collective-permute-done.15.refs_1_ = bf16[64,512]{1,0:T(8,128)(2,1)S(1)} collective-permute-done((bf16[64,512]{1,0:T(8,128)(2,1)S(1)}, bf16[64,512]{1,0:T(8,128)(2,1)S(1)}, u32[]{:S(2)}, u32[]{:S(2)}) %collective-permute-start.15) | collective-permute-done | bytes 65568 | tf_op jit(solution)/shard_map/ppermute | solution.py:320
  49.6 1.7 %shard_map.65 = bf16[64,4,16,128]{3,2,1,0:T(8,128)(2,1)} custom-call(bf16[64,512]{1,0:T(8,128)(2,1)S(1)} %collective-permute-done.14.refs_0_, bf16[64,512]{1,0:T(8,128)(2,1)S(1)} %collective-permute-done.15.refs_1_, bf16[64,512]{1,0:T(8,128)(2,1)S(1)} %collective-permute-done.16.refs_2_, f32[64,512]{1,0:T(8,128)S(1)} %shard_map.64.refs_3_, ...), custom_call_target="tpu_custom_call" | custom-call | bytes 4194304 | tf_op jit(solution)/shard_map/pallas_call | solution.py:419
  (33 shorter events, 1.6 us)
Async XLA Ops:
  0.0 2.2 %copy-start = (bf16[8,2,512,256]{3,2,1,0:T(8,128)(2,1)S(1)}, bf16[8,2,512,256]{3,2,1,0:T(8,128)(2,1)}, u32[]{:S(2)}) copy-start(bf16[8,2,512,256]{3,2,1,0:T(8,128)(2,1)} %orb_ref.7) | copy-start | bytes 12582916
  2.2 11.4 %copy-start.5 = (bf16[8,32,256]{2,1,0:T(8,128)(2,1)S(1)}, bf16[8,32,256]{2,1,0:T(8,128)(2,1)}, u32[]{:S(2)}) copy-start(bf16[8,32,256]{2,1,0:T(8,128)(2,1)} %coulomb_ref.1) | copy-start | bytes 393220
  2.2 15.8 %copy-start.4 = (bf16[2,256,128]{2,1,0:T(8,128)(2,1)S(1)}, bf16[2,256,128]{2,1,0:T(8,128)(2,1)}, u32[]{:S(2)}) copy-start(bf16[2,256,128]{2,1,0:T(8,128)(2,1)} %constant.6.clone.refs_9_) | copy-start | bytes 393220
  2.2 27.2 %copy-start.6 = (bf16[64,128]{1,0:T(8,128)(2,1)S(1)}, bf16[64,128]{1,0:T(8,128)(2,1)}, u32[]{:S(2)}) copy-start(bf16[64,128]{1,0:T(8,128)(2,1)} %constant.8.clone.refs_5_) | copy-start | bytes 49156
  2.2 27.2 %copy-start.7 = (bf16[64,128]{1,0:T(8,128)(2,1)S(1)}, bf16[64,128]{1,0:T(8,128)(2,1)}, u32[]{:S(2)}) copy-start(bf16[64,128]{1,0:T(8,128)(2,1)} %constant.7.clone.refs_4_) | copy-start | bytes 49156
  2.8 8.0 %collective-permute-start.5 = (bf16[64,512]{1,0:T(8,128)(2,1)S(1)}, bf16[64,512]{1,0:T(8,128)(2,1)S(1)}, u32[]{:S(2)}, u32[]{:S(2)}) collective-permute-start(bf16[64,512]{1,0:T(8,128)(2,1)S(1)} %shard_map.55.refs_0_), channel_id=1, source_target_pairs={{0,6},{1,7},{2,4},{3,5},{4,2},{5,3},{6,0},{7,1},{8,14},{9,15},{10,... | collective-permute-start | bytes 196616 | tf_op jit(solution)/shard_map/ppermute | solution.py:308
  7.9 4.7 %collective-permute-start.3 = (bf16[64,512]{1,0:T(8,128)(2,1)S(1)}, bf16[64,512]{1,0:T(8,128)(2,1)S(1)}, u32[]{:S(2)}, u32[]{:S(2)}) collective-permute-start(bf16[64,512]{1,0:T(8,128)(2,1)S(1)} %shard_map.55.refs_0_), channel_id=1, source_target_pairs={{0,2},{1,3},{2,0},{3,1},{4,6},{5,7},{6,4},{7,5},{8,10},{9,11},{10,... | collective-permute-start | bytes 196616 | tf_op jit(solution)/shard_map/ppermute | solution.py:308
  7.9 5.6 %collective-permute-start.1 = (bf16[64,512]{1,0:T(8,128)(2,1)S(1)}, bf16[64,512]{1,0:T(8,128)(2,1)S(1)}, u32[]{:S(2)}, u32[]{:S(2)}) collective-permute-start(bf16[64,512]{1,0:T(8,128)(2,1)S(1)} %shard_map.55.refs_0_), channel_id=1, source_target_pairs={{0,4},{1,5},{2,6},{3,7},{4,0},{5,1},{6,2},{7,3},{8,12},{9,13},{10,... | collective-permute-start | bytes 196616 | tf_op jit(solution)/shard_map/ppermute | solution.py:308
  8.5 9.5 %collective-permute-start = (bf16[64,512]{1,0:T(8,128)(2,1)S(1)}, bf16[64,512]{1,0:T(8,128)(2,1)S(1)}, u32[]{:S(2)}, u32[]{:S(2)}) collective-permute-start(bf16[64,512]{1,0:T(8,128)(2,1)S(1)} %shard_map.55.refs_0_), channel_id=1, source_target_pairs={{0,1},{1,0},{2,3},{3,2},{4,5},{5,4},{6,7},{7,6},{8,9},{9,8},{10,11... | collective-permute-start | bytes 196616 | tf_op jit(solution)/shard_map/ppermute | solution.py:308
  10.8 7.2 %collective-permute-start.6 = (bf16[64,512]{1,0:T(8,128)(2,1)S(1)}, bf16[64,512]{1,0:T(8,128)(2,1)S(1)}, u32[]{:S(2)}, u32[]{:S(2)}) collective-permute-start(bf16[64,512]{1,0:T(8,128)(2,1)S(1)} %collective-permute-done.5.refs_6_), channel_id=1, source_target_pairs={{0,1},{1,0},{2,3},{3,2},{4,5},{5,4},{6,7},{7,6},{8,9},{9,8},{10,11... | collective-permute-start | bytes 196616 | tf_op jit(solution)/shard_map/ppermute | solution.py:308
  12.6 5.4 %collective-permute-start.4 = (bf16[64,512]{1,0:T(8,128)(2,1)S(1)}, bf16[64,512]{1,0:T(8,128)(2,1)S(1)}, u32[]{:S(2)}, u32[]{:S(2)}) collective-permute-start(bf16[64,512]{1,0:T(8,128)(2,1)S(1)} %collective-permute-done.3.refs_4_), channel_id=1, source_target_pairs={{0,1},{1,0},{2,3},{3,2},{4,5},{5,4},{6,7},{7,6},{8,9},{9,8},{10,11... | collective-permute-start | bytes 196616 | tf_op jit(solution)/shard_map/ppermute | solution.py:308
  13.5 4.4 %collective-permute-start.2 = (bf16[64,512]{1,0:T(8,128)(2,1)S(1)}, bf16[64,512]{1,0:T(8,128)(2,1)S(1)}, u32[]{:S(2)}, u32[]{:S(2)}) collective-permute-start(bf16[64,512]{1,0:T(8,128)(2,1)S(1)} %collective-permute-done.1.refs_2_), channel_id=1, source_target_pairs={{0,1},{1,0},{2,3},{3,2},{4,5},{5,4},{6,7},{7,6},{8,9},{9,8},{10,11... | collective-permute-start | bytes 196616 | tf_op jit(solution)/shard_map/ppermute | solution.py:308
  14.2 10.9 %all-to-all-start = ((bf16[4,64,256]{2,1,0:T(8,128)(2,1)}), bf16[4,64,256]{2,1,0:T(8,128)(2,1)S(1)}, u32[]{:S(2)}, u32[]{:S(2)}) async-start(bf16[4,64,256]{2,1,0:T(8,128)(2,1)} %shard_map.57), calls=%async_computation | async-start | bytes 262144 | tf_op jit(solution)/shard_map/all_to_all | solution.py:342
  18.0 2.2 %copy-start.1 = (bf16[8,2,512,256]{3,2,1,0:T(8,128)(2,1)S(1)}, bf16[8,2,512,256]{3,2,1,0:T(8,128)(2,1)}, u32[]{:S(2)}) copy-start(bf16[8,2,512,256]{3,2,1,0:T(8,128)(2,1)} %orb_ref.7) | copy-start | bytes 12582916
  21.6 5.2 %collective-permute-start.7 = (bf16[128,256]{1,0:T(8,128)(2,1)S(1)}, bf16[128,256]{1,0:T(8,128)(2,1)S(1)}, u32[]{:S(2)}, u32[]{:S(2)}) collective-permute-start(bf16[128,256]{1,0:T(8,128)(2,1)S(1)} %get-tuple-element.19), channel_id=1, source_target_pairs={{0,24},{8,16},{16,8},{24,0},{1,25},{9,17},{17,9},{25,1},{2,26},{10... | collective-permute-start | bytes 196616 | tf_op jit(solution)/shard_map/ppermute | solution.py:308
  24.5 4.3 %collective-permute-start.8 = (bf16[128,256]{1,0:T(8,128)(2,1)S(1)}, bf16[128,256]{1,0:T(8,128)(2,1)S(1)}, u32[]{:S(2)}, u32[]{:S(2)}) collective-permute-start(bf16[128,256]{1,0:T(8,128)(2,1)S(1)} %get-tuple-element.20), channel_id=1, source_target_pairs={{0,16},{8,24},{16,0},{24,8},{1,17},{9,25},{17,1},{25,9},{2,18},{10... | collective-permute-start | bytes 196616 | tf_op jit(solution)/shard_map/ppermute | solution.py:308
  25.1 4.3 %collective-permute-start.9 = (bf16[128,256]{1,0:T(8,128)(2,1)S(1)}, bf16[128,256]{1,0:T(8,128)(2,1)S(1)}, u32[]{:S(2)}, u32[]{:S(2)}) collective-permute-start(bf16[128,256]{1,0:T(8,128)(2,1)S(1)} %get-tuple-element.21), channel_id=1, source_target_pairs={{0,8},{8,0},{16,24},{24,16},{1,9},{9,1},{17,25},{25,17},{2,10},{10... | collective-permute-start | bytes 196616 | tf_op jit(solution)/shard_map/ppermute | solution.py:308
  29.9 5.2 %collective-permute-start.10 = (bf16[128,256]{1,0:T(8,128)(2,1)S(1)}, bf16[128,256]{1,0:T(8,128)(2,1)S(1)}, u32[]{:S(2)}, u32[]{:S(2)}) collective-permute-start(bf16[128,256]{1,0:T(8,128)(2,1)S(1)} %get-tuple-element.23), channel_id=1, source_target_pairs={{0,24},{8,16},{16,8},{24,0},{1,25},{9,17},{17,9},{25,1},{2,26},{10... | collective-permute-start | bytes 196616 | tf_op jit(solution)/shard_map/ppermute | solution.py:308
  31.4 4.4 %collective-permute-start.11 = (bf16[128,256]{1,0:T(8,128)(2,1)S(1)}, bf16[128,256]{1,0:T(8,128)(2,1)S(1)}, u32[]{:S(2)}, u32[]{:S(2)}) collective-permute-start(bf16[128,256]{1,0:T(8,128)(2,1)S(1)} %get-tuple-element.24), channel_id=1, source_target_pairs={{0,16},{8,24},{16,0},{24,8},{1,17},{9,25},{17,1},{25,9},{2,18},{10... | collective-permute-start | bytes 196616 | tf_op jit(solution)/shard_map/ppermute | solution.py:308
  32.0 4.3 %collective-permute-start.12 = (bf16[128,256]{1,0:T(8,128)(2,1)S(1)}, bf16[128,256]{1,0:T(8,128)(2,1)S(1)}, u32[]{:S(2)}, u32[]{:S(2)}) collective-permute-start(bf16[128,256]{1,0:T(8,128)(2,1)S(1)} %get-tuple-element.25), channel_id=1, source_target_pairs={{0,8},{8,0},{16,24},{24,16},{1,9},{9,1},{17,25},{25,17},{2,10},{10... | collective-permute-start | bytes 196616 | tf_op jit(solution)/shard_map/ppermute | solution.py:308
  36.2 2.2 %copy-start.2 = (bf16[8,2,512,256]{3,2,1,0:T(8,128)(2,1)S(1)}, bf16[8,2,512,256]{3,2,1,0:T(8,128)(2,1)}, u32[]{:S(2)}) copy-start(bf16[8,2,512,256]{3,2,1,0:T(8,128)(2,1)} %orb_ref.7) | copy-start | bytes 12582916
  39.1 1.7 %collective-permute-start.13 = (bf16[3,64,512]{2,1,0:T(8,128)(2,1)S(1)}, bf16[3,64,512]{2,1,0:T(8,128)(2,1)S(1)}, u32[]{:S(2)}, u32[]{:S(2)}) collective-permute-start(bf16[3,64,512]{2,1,0:T(8,128)(2,1)S(1)} %get-tuple-element.28.refs_0_), channel_id=1, source_target_pairs={{0,1},{1,0},{2,3},{3,2},{4,5},{5,4},{6,7},{7,6},{8,9},{9,8},{10,11... | collective-permute-start | bytes 589832 | tf_op jit(solution)/shard_map/ppermute | solution.py:308
  39.6 6.1 %copy-start.3 = (bf16[8,2,512,256]{3,2,1,0:T(8,128)(2,1)S(1)}, bf16[8,2,512,256]{3,2,1,0:T(8,128)(2,1)}, u32[]{:S(2)}) copy-start(bf16[8,2,512,256]{3,2,1,0:T(8,128)(2,1)} %orb_ref.7) | copy-start | bytes 12582916
  39.6 6.6 %collective-permute-start.17 = (bf16[1,64,512]{2,1,0:T(8,128)(2,1)S(1)}, bf16[1,64,512]{2,1,0:T(8,128)(2,1)S(1)}, u32[]{:S(2)}, u32[]{:S(2)}) collective-permute-start(bf16[1,64,512]{2,1,0:T(8,128)(2,1)S(1)} %shard_map.60.refs_0_), channel_id=1, source_target_pairs={{0,1},{1,0},{2,3},{3,2},{4,5},{5,4},{6,7},{7,6},{8,9},{9,8},{10,11... | collective-permute-start | bytes 196616 | tf_op jit(solution)/shard_map/ppermute | solution.py:308
  40.8 6.8 %collective-permute-start.14 = (bf16[64,512]{1,0:T(8,128)(2,1)S(1)}, bf16[64,512]{1,0:T(8,128)(2,1)S(1)}, u32[]{:S(2)}, u32[]{:S(2)}) collective-permute-start(bf16[64,512]{1,0:T(8,128)(2,1)S(1)} %get-tuple-element.29), channel_id=1, source_target_pairs={{0,2},{1,3},{2,4},{3,5},{4,6},{5,7},{6,0},{7,1},{8,10},{9,11},{10,... | collective-permute-start | bytes 196616 | tf_op jit(solution)/shard_map/ppermute | solution.py:320
  42.4 7.2 %collective-permute-start.15 = (bf16[64,512]{1,0:T(8,128)(2,1)S(1)}, bf16[64,512]{1,0:T(8,128)(2,1)S(1)}, u32[]{:S(2)}, u32[]{:S(2)}) collective-permute-start(bf16[64,512]{1,0:T(8,128)(2,1)S(1)} %get-tuple-element.30), channel_id=1, source_target_pairs={{0,4},{1,5},{2,6},{3,7},{4,0},{5,1},{6,2},{7,3},{8,12},{9,13},{10,... | collective-permute-start | bytes 196616 | tf_op jit(solution)/shard_map/ppermute | solution.py:320
  43.6 6.0 %collective-permute-start.16 = (bf16[64,512]{1,0:T(8,128)(2,1)S(1)}, bf16[64,512]{1,0:T(8,128)(2,1)S(1)}, u32[]{:S(2)}, u32[]{:S(2)}) collective-permute-start(bf16[64,512]{1,0:T(8,128)(2,1)S(1)} %get-tuple-element.31.refs_0_), channel_id=1, source_target_pairs={{0,6},{1,7},{2,0},{3,1},{4,2},{5,3},{6,4},{7,5},{8,14},{9,15},{10,... | collective-permute-start | bytes 196616 | tf_op jit(solution)/shard_map/ppermute | solution.py:320

commit v21 on v18

--- a/solution.py
+++ b/solution.py
@@ -166,7 +166,7 @@
             halves = [ref[k].reshape(2 * norb, ref.shape[3]) for ref in (orb_ref, rest_ref)]
             tile = dot(form, jnp.concatenate(halves, axis=1))
             for offset in range(shares):
-                form_ref[jnp.bitwise_xor(plane, offset), k] = form[offset * rows : (offset + 1) * rows]
+                form_ref[lax.rem(plane + shares - offset, shares), k] = form[offset * rows : (offset + 1) * rows]
                 for part in range(2):
                     low = offset * rows + part * share
                     start = offset * share * 2 * local_k + 2 * k + part
@@ -174,9 +174,10 @@
     size = share * 2 * local_k
     cells[...] = coulomb_ref[...].astype(F32)
     for s in range(shares):
-        offset = jnp.bitwise_xor(me, s)
+        owned = jnp.bitwise_xor(jnp.bitwise_xor(me, s), plane)
+        offset = lax.rem(plane + shares - owned, shares)
         outs[s][:size] = take(wide, pl.multiple_of(offset * size, size), size).astype(BF16)
-        start = pl.multiple_of(jnp.bitwise_xor(offset, plane) * share, share)
+        start = pl.multiple_of(owned * share, share)
         pieces = [cells[r, pl.ds(start, share), :] for r in range(local_k)]
         outs[s][size:] = jnp.concatenate(pieces, axis=0).astype(BF16)
 
@@ -271,8 +272,8 @@
     weight_rows(offsets, flip, out_rows, right_ref, orb_ref, rest_ref, refs[-1])
 
 
-def pair_kernel(keep_ref, came_ref, *outs):
-    for i, out_ref in enumerate(outs):
+def pair_kernel(many, keep_ref, came_ref, *refs):
+    for i, out_ref in enumerate(refs[-many:]):
         out_ref[...] = (keep_ref[i] + came_ref[i].astype(F32)).astype(out_ref.dtype)
 
 
@@ -377,7 +378,8 @@
     for offset in asked(shares):
         came[offset] = []
         for e in range(per_share // 2):
-            block = swap(edge, "pts", offset * per_share + 2 * e)
+            pairs = [(i, (i + offset * per_share) % blocks ^ (2 * e)) for i in range(blocks)]
+            block = lax.ppermute(edge, "pts", pairs)
             came[offset] += [block, swap(block, "pts", 1)]
     table = column_selector(group, per_share, per_block, 1).reshape(-1, per_share, ROWS)
     places = [[place ^ e for e in range(per_share)] for place in range(per_share)]
@@ -432,13 +434,16 @@
             unread=1,
         )(right, first, rest, before)
 
-    def summed(offsets, keep, came):
+    def summed(offsets, keep, came, *before):
         kinds = [shape((out_rows, lanes), BF16 if offset else F32) for offset in offsets]
-        return call(pair_kernel, kinds, 2)(keep, came)
-
-    sent_late = rows_of(late, 1, BF16, sent)
-    early_sums = summed(early, rows_of(early, 0, F32, sent_late), swap(sent, "pts", 1))
-    late_sums = summed(late, rows_of(late, 0, F32, early_sums[0]), swap(sent_late, "pts", 1))
+        kernel = functools.partial(pair_kernel, len(offsets))
+        return call(kernel, kinds, 2, unread=len(before))(keep, came, *before)
+
+    kept = rows_of(early, 0, F32, sent)
+    sent_late = rows_of(late, 1, BF16, kept)
+    kept_late = rows_of(late, 0, F32, sent_late)
+    early_sums = summed(early, kept, swap(sent, "pts", 1), kept_late)
+    late_sums = summed(late, kept_late, swap(sent_late, "pts", 1))
     sums = [*late_sums, *early_sums]
     sums = shift_along(sums)
     spans = norb // LANES

time: 44.8 us -> 46.9 us (1.047)
  waiting for transfers between devices: 16.1 us -> 18.4 us
    ppermute x0 -> x3, starting transfers between devices: none -> 6.11 us  [body(): block = lax.ppermute(edge, 'pts', pairs)]
    ppermute x15 -> x12, starting transfers between devices: 13.6 us -> 8.31 us  [swap(): return lax.ppermute(value, axis, [(i, i ^ mask) for i in range(size)])]
    ppermute x0 -> x3, waiting for transfers between devices: none -> 4.27 us  [body(): block = lax.ppermute(edge, 'pts', pairs)]
    ppermute x15 -> x12, waiting for transfers between devices: 12.8 us -> 9.45 us  [swap(): return lax.ppermute(value, axis, [(i, i ^ mask) for i in range(size)])]
    ppermute x3, waiting for transfers between devices: 3.32 us -> 4.69 us  [shift_along(): came.append(lax.ppermute(pieces[s], 'pts', pairs))]
    ppermute x3, starting transfers between devices: 4.93 us -> 3.87 us  [shift_along(): came.append(lax.ppermute(pieces[s], 'pts', pairs))]
  transfers between devices with their start and end apart: 18 -> 18, of which waited for: 13 -> 11; matrix products, arithmetic and copies ran while one was open for 0% -> 0% of each run, Pallas kernels for 7% -> 7%
where the time goes in v21:
time: 46.9 us; the launch traced here: 46.8 us
  waiting for transfers between devices  18.4 us (39%)
  starting transfers between devices  18.3 us (39%)
  Pallas kernels  9.89 us (21%)
    ppermute x12, waiting for transfers between devices, swap(): return lax.ppermute(value, axis, [(i, i ^ mask) for i in range(size)])  9.45 us
    ppermute x12, starting transfers between devices, swap(): return lax.ppermute(value, axis, [(i, i ^ mask) for i in range(size)])  8.31 us
    ppermute x3, starting transfers between devices, body(): block = lax.ppermute(edge, 'pts', pairs)  6.11 us
    ppermute x3, waiting for transfers between devices, shift_along(): came.append(lax.ppermute(pieces[s], 'pts', pairs))  4.69 us
    ppermute x3, waiting for transfers between devices, body(): block = lax.ppermute(edge, 'pts', pairs)  4.27 us
    ppermute x3, starting transfers between devices, shift_along(): came.append(lax.ppermute(pieces[s], 'pts', pairs))  3.87 us
    pallas_call x1, Pallas kernels, body(): call(functools.partial(edge_kernel, per_block), [shape((local_k * 2 * per...  2.5 us
    pallas_call x1, Pallas kernels, body(): call(functools.partial(exchange_kernel, chunks, 1.0 / math.sqrt(points *...  1.66 us
  transfers between devices with their start and end apart: 18, of which 11 were waited for; matrix products, arithmetic and copies ran while one was open for 0% of the time, Pallas kernels for 7%

profile of v21, /device:TPU:0, one launch (start us, length us, event | category | flops | bytes accessed | tf_op | source)
XLA Modules:
  0.0 46.8 jit_solution(17647212885479100832)
XLA Ops:
  0.0 2.5 %shard_map.55 = (bf16[64,512]{1,0:T(8,128)(2,1)S(1)}, bf16[8,2,512,128]{3,2,1,0:T(8,128)(2,1)S(1)}) custom-call(bf16[8,2,512,256]{3,2,1,0:T(8,128)(2,1)} %orb_hbm.3), custom_call_target="tpu_custom_call" | custom-call | bytes 4194304 | tf_op jit(solution)/shard_map/pallas_call | solution.py:353
  2.5 5.1 %collective-permute-start.5 = (bf16[64,512]{1,0:T(8,128)(2,1)S(1)}, bf16[64,512]{1,0:T(8,128)(2,1)S(1)}, u32[]{:S(2)}, u32[]{:S(2)}) collective-permute-start(bf16[64,512]{1,0:T(8,128)(2,1)S(1)} %get-tuple-element.23.edge_hbm.refs_0_), channel_id=1, source_target_pairs={{0,6},{1,7},{2,0},{3,1},{4,2},{5,3},{6,4},{7,5},{8,14},{9,15},{10,... | collective-permute-start | bytes 196616 | tf_op jit(solution)/shard_map/ppermute | solution.py:382
  7.6 1.0 %collective-permute-start.1 = (bf16[64,512]{1,0:T(8,128)(2,1)S(1)}, bf16[64,512]{1,0:T(8,128)(2,1)S(1)}, u32[]{:S(2)}, u32[]{:S(2)}) collective-permute-start(bf16[64,512]{1,0:T(8,128)(2,1)S(1)} %get-tuple-element.23.edge_hbm.refs_0_), channel_id=1, source_target_pairs={{0,4},{1,5},{2,6},{3,7},{4,0},{5,1},{6,2},{7,3},{8,12},{9,13},{10,... | collective-permute-start | bytes 196616 | tf_op jit(solution)/shard_map/ppermute | solution.py:382
  8.6 1.6 %shard_map.56 = (bf16[64,512]{1,0:T(8,128)(2,1)S(1)}, bf16[8,2,512,128]{3,2,1,0:T(8,128)(2,1)S(1)}) custom-call(bf16[8,2,512,256]{3,2,1,0:T(8,128)(2,1)} %orb_hbm.3, bf16[64,512]{1,0:T(8,128)(2,1)S(1)} %get-tuple-element.23.edge_hbm.refs_0_), custom_call_target="tpu_custom_call" | custom-call | bytes 4194304 | tf_op jit(solution)/shard_map/pallas_call | solution.py:365
  10.2 0.1 collective-permute-start
  10.3 0.5 %collective-permute-start.6 = (bf16[64,512]{1,0:T(8,128)(2,1)S(1)}, bf16[64,512]{1,0:T(8,128)(2,1)S(1)}, u32[]{:S(2)}, u32[]{:S(2)}) collective-permute-start(bf16[64,512]{1,0:T(8,128)(2,1)S(1)} %collective-permute-done.5.refs_6_), channel_id=1, source_target_pairs={{0,1},{1,0},{2,3},{3,2},{4,5},{5,4},{6,7},{7,6},{8,9},{9,8},{10,11... | collective-permute-start | bytes 196616 | tf_op jit(solution)/shard_map/ppermute | solution.py:325
  10.8 3.0 %collective-permute-done.3.refs_4_ = bf16[64,512]{1,0:T(8,128)(2,1)S(1)} collective-permute-done((bf16[64,512]{1,0:T(8,128)(2,1)S(1)}, bf16[64,512]{1,0:T(8,128)(2,1)S(1)}, u32[]{:S(2)}, u32[]{:S(2)}) %collective-permute-start.3) | collective-permute-done | bytes 65568 | tf_op jit(solution)/shard_map/ppermute | solution.py:382
  13.8 1.3 %collective-permute-done.1.refs_2_ = bf16[64,512]{1,0:T(8,128)(2,1)S(1)} collective-permute-done((bf16[64,512]{1,0:T(8,128)(2,1)S(1)}, bf16[64,512]{1,0:T(8,128)(2,1)S(1)}, u32[]{:S(2)}, u32[]{:S(2)}) %collective-permute-start.1) | collective-permute-done | bytes 65568 | tf_op jit(solution)/shard_map/ppermute | solution.py:382
  15.1 1.2 %collective-permute-done.2.refs_3_ = bf16[64,512]{1,0:T(8,128)(2,1)S(1)} collective-permute-done((bf16[64,512]{1,0:T(8,128)(2,1)S(1)}, bf16[64,512]{1,0:T(8,128)(2,1)S(1)}, u32[]{:S(2)}, u32[]{:S(2)}) %collective-permute-start.2) | collective-permute-done | bytes 65568 | tf_op jit(solution)/shard_map/ppermute | solution.py:325
  16.4 1.4 %shard_map.57 = (bf16[192,256]{1,0:T(8,128)(2,1)S(1)}, bf16[192,256]{1,0:T(8,128)(2,1)S(1)}, bf16[192,256]{1,0:T(8,128)(2,1)S(1)}, bf16[192,256]{1,0:T(8,128)(2,1)S(1)}, bf16[4,8,16,1024]{3,2,1,0:T(8,128)(2,1)S(1)}) custom-call(bf16[64,512]{1,0:T(8,128)(2,1)S(1)} %get-tuple-element.23.edge_hbm.refs_0_, bf16[64,512]{1,0:T(8,128)(2,1)S(1)} %collective-permute-done.refs_1_, ...), custom_call_target="tpu_custom_call" | custom-call | bytes 6291456 | tf_op jit(solution)/shard_map/pallas_call | solution.py:390
  17.8 2.5 %collective-permute-start.7 = (bf16[192,256]{1,0:T(8,128)(2,1)S(1)}, bf16[192,256]{1,0:T(8,128)(2,1)S(1)}, u32[]{:S(2)}, u32[]{:S(2)}) collective-permute-start(bf16[192,256]{1,0:T(8,128)(2,1)S(1)} %get-tuple-element.27), channel_id=1, source_target_pairs={{0,24},{8,16},{16,8},{24,0},{1,25},{9,17},{17,9},{25,1},{2,26},{10... | collective-permute-start | bytes 294920 | tf_op jit(solution)/shard_map/ppermute | solution.py:325
  20.3 0.5 %collective-permute-start.8 = (bf16[192,256]{1,0:T(8,128)(2,1)S(1)}, bf16[192,256]{1,0:T(8,128)(2,1)S(1)}, u32[]{:S(2)}, u32[]{:S(2)}) collective-permute-start(bf16[192,256]{1,0:T(8,128)(2,1)S(1)} %get-tuple-element.28), channel_id=1, source_target_pairs={{0,16},{8,24},{16,0},{24,8},{1,17},{9,25},{17,1},{25,9},{2,18},{10... | collective-permute-start | bytes 294920 | tf_op jit(solution)/shard_map/ppermute | solution.py:325
  20.8 0.5 %collective-permute-start.9 = (bf16[192,256]{1,0:T(8,128)(2,1)S(1)}, bf16[192,256]{1,0:T(8,128)(2,1)S(1)}, u32[]{:S(2)}, u32[]{:S(2)}) collective-permute-start(bf16[192,256]{1,0:T(8,128)(2,1)S(1)} %get-tuple-element.29), channel_id=1, source_target_pairs={{0,8},{8,0},{16,24},{24,16},{1,9},{9,1},{17,25},{25,17},{2,10},{10... | collective-permute-start | bytes 294920 | tf_op jit(solution)/shard_map/ppermute | solution.py:325
  21.3 2.4 %collective-permute-done.7.refs_0_ = bf16[192,256]{1,0:T(8,128)(2,1)S(1)} collective-permute-done((bf16[192,256]{1,0:T(8,128)(2,1)S(1)}, bf16[192,256]{1,0:T(8,128)(2,1)S(1)}, u32[]{:S(2)}, u32[]{:S(2)}) %collective-permute-start.7) | collective-permute-done | bytes 98336 | tf_op jit(solution)/shard_map/ppermute | solution.py:325
  23.7 2.0 %collective-permute-done.8.refs_1_ = bf16[192,256]{1,0:T(8,128)(2,1)S(1)} collective-permute-done((bf16[192,256]{1,0:T(8,128)(2,1)S(1)}, bf16[192,256]{1,0:T(8,128)(2,1)S(1)}, u32[]{:S(2)}, u32[]{:S(2)}) %collective-permute-start.8) | collective-permute-done | bytes 98336 | tf_op jit(solution)/shard_map/ppermute | solution.py:325
  25.7 0.6 %shard_map.58 = (bf16[128,256]{1,0:T(8,128)(2,1)S(1)}, bf16[128,256]{1,0:T(8,128)(2,1)S(1)}, bf16[128,256]{1,0:T(8,128)(2,1)S(1)}, bf16[128,256]{1,0:T(8,128)(2,1)S(1)}) custom-call(bf16[192,256]{1,0:T(8,128)(2,1)S(1)} %collective-permute-done.7.refs_0_, bf16[192,256]{1,0:T(8,128)(2,1)S(1)} %collective-permute-done.8.refs_1_, ...), custom_call_target="tpu_custom_call" | custom-call | bytes 2097152 | tf_op jit(solution)/shard_map/pallas_call | solution.py:403
  26.3 1.8 %collective-permute-start.10 = (bf16[128,256]{1,0:T(8,128)(2,1)S(1)}, bf16[128,256]{1,0:T(8,128)(2,1)S(1)}, u32[]{:S(2)}, u32[]{:S(2)}) collective-permute-start(bf16[128,256]{1,0:T(8,128)(2,1)S(1)} %get-tuple-element.31), channel_id=1, source_target_pairs={{0,24},{8,16},{16,8},{24,0},{1,25},{9,17},{17,9},{25,1},{2,26},{10... | collective-permute-start | bytes 196616 | tf_op jit(solution)/shard_map/ppermute | solution.py:325
  28.1 1.3 %collective-permute-start.11 = (bf16[128,256]{1,0:T(8,128)(2,1)S(1)}, bf16[128,256]{1,0:T(8,128)(2,1)S(1)}, u32[]{:S(2)}, u32[]{:S(2)}) collective-permute-start(bf16[128,256]{1,0:T(8,128)(2,1)S(1)} %get-tuple-element.32), channel_id=1, source_target_pairs={{0,16},{8,24},{16,0},{24,8},{1,17},{9,25},{17,1},{25,9},{2,18},{10... | collective-permute-start | bytes 196616 | tf_op jit(solution)/shard_map/ppermute | solution.py:325
  29.4 0.5 %collective-permute-start.12 = (bf16[128,256]{1,0:T(8,128)(2,1)S(1)}, bf16[128,256]{1,0:T(8,128)(2,1)S(1)}, u32[]{:S(2)}, u32[]{:S(2)}) collective-permute-start(bf16[128,256]{1,0:T(8,128)(2,1)S(1)} %get-tuple-element.33), channel_id=1, source_target_pairs={{0,8},{8,0},{16,24},{24,16},{1,9},{9,1},{17,25},{25,17},{2,10},{10... | collective-permute-start | bytes 196616 | tf_op jit(solution)/shard_map/ppermute | solution.py:325
  29.9 2.1 %collective-permute-done.10.refs_0_ = bf16[128,256]{1,0:T(8,128)(2,1)S(1)} collective-permute-done((bf16[128,256]{1,0:T(8,128)(2,1)S(1)}, bf16[128,256]{1,0:T(8,128)(2,1)S(1)}, u32[]{:S(2)}, u32[]{:S(2)}) %collective-permute-start.10) | collective-permute-done | bytes 65568 | tf_op jit(solution)/shard_map/ppermute | solution.py:325
  32.0 0.5 %collective-permute-done.11.refs_1_ = bf16[128,256]{1,0:T(8,128)(2,1)S(1)} collective-permute-done((bf16[128,256]{1,0:T(8,128)(2,1)S(1)}, bf16[128,256]{1,0:T(8,128)(2,1)S(1)}, u32[]{:S(2)}, u32[]{:S(2)}) %collective-permute-start.11) | collective-permute-done | bytes 65568 | tf_op jit(solution)/shard_map/ppermute | solution.py:325
  32.5 1.1 %collective-permute-done.12.refs_2_ = bf16[128,256]{1,0:T(8,128)(2,1)S(1)} collective-permute-done((bf16[128,256]{1,0:T(8,128)(2,1)S(1)}, bf16[128,256]{1,0:T(8,128)(2,1)S(1)}, u32[]{:S(2)}, u32[]{:S(2)}) %collective-permute-start.12) | collective-permute-done | bytes 65568 | tf_op jit(solution)/shard_map/ppermute | solution.py:325
  33.7 0.6 %shard_map.59 = (bf16[3,64,512]{2,1,0:T(8,128)(2,1)S(1)}, bf16[4,128,1024]{2,1,0:T(8,128)(2,1)S(1)}) custom-call(bf16[128,256]{1,0:T(8,128)(2,1)S(1)} %collective-permute-done.10.refs_0_, bf16[128,256]{1,0:T(8,128)(2,1)S(1)} %collective-permute-done.11.refs_1_, bf16[128,256]{1,0:T(8,128)(2,1)S(1)} %collective-permute-done.12.refs_2_, ...), custom_call_target="tpu_custom_call" | custom-call | tf_op jit(solution)/shard_map/pallas_call | solution.py:419
  34.4 0.6 %shard_map.60.refs_0_.keep_ref = f32[3,64,512]{2,1,0:T(8,128)S(1)} custom-call(bf16[4,128,1024]{2,1,0:T(8,128)(2,1)S(1)} %get-tuple-element.35.right_ref, bf16[8,2,512,128]{3,2,1,0:T(8,128)(2,1)S(1)} %get-tuple-element.25.refs_8_.refs_4_.orb_ref, bf16[8,2,512,128]{3,2,1,0:T(8,128)(2,1)S(1)} %get-tuple-element.26.refs_9_.refs_5_.rest_ref, ...), custom_call_target="tpu_custom_call" | custom-call | tf_op jit(solution)/shard_map/pallas_call | solution.py:430
  34.9 0.5 %shard_map.61.refs_0_ = bf16[1,64,512]{2,1,0:T(8,128)(2,1)S(1)} custom-call(bf16[4,128,1024]{2,1,0:T(8,128)(2,1)S(1)} %get-tuple-element.35.right_ref, bf16[8,2,512,128]{3,2,1,0:T(8,128)(2,1)S(1)} %get-tuple-element.25.refs_8_.refs_4_.orb_ref, bf16[8,2,512,128]{3,2,1,0:T(8,128)(2,1)S(1)} %get-tuple-element.26.refs_9_.refs_5_.rest_ref, ...), custom_call_target="tpu_custom_call" | custom-call | tf_op jit(solution)/shard_map/pallas_call | solution.py:430
  35.4 0.5 %shard_map.62.refs_0_.keep_ref = f32[1,64,512]{2,1,0:T(8,128)S(1)} custom-call(bf16[4,128,1024]{2,1,0:T(8,128)(2,1)S(1)} %get-tuple-element.35.right_ref, bf16[8,2,512,128]{3,2,1,0:T(8,128)(2,1)S(1)} %get-tuple-element.25.refs_8_.refs_4_.orb_ref, bf16[8,2,512,128]{3,2,1,0:T(8,128)(2,1)S(1)} %get-tuple-element.26.refs_9_.refs_5_.rest_ref, ...), custom_call_target="tpu_custom_call" | custom-call | tf_op jit(solution)/shard_map/pallas_call | solution.py:430
  35.9 0.6 %collective-permute-start.17 = (bf16[1,64,512]{2,1,0:T(8,128)(2,1)S(1)}, bf16[1,64,512]{2,1,0:T(8,128)(2,1)S(1)}, u32[]{:S(2)}, u32[]{:S(2)}) collective-permute-start(bf16[1,64,512]{2,1,0:T(8,128)(2,1)S(1)} %shard_map.61.refs_0_), channel_id=1, source_target_pairs={{0,1},{1,0},{2,3},{3,2},{4,5},{5,4},{6,7},{7,6},{8,9},{9,8},{10,11... | collective-permute-start | bytes 196616 | tf_op jit(solution)/shard_map/ppermute | solution.py:325
  36.6 2.2 %collective-permute-start.15 = (bf16[64,512]{1,0:T(8,128)(2,1)S(1)}, bf16[64,512]{1,0:T(8,128)(2,1)S(1)}, u32[]{:S(2)}, u32[]{:S(2)}) collective-permute-start(bf16[64,512]{1,0:T(8,128)(2,1)S(1)} %get-tuple-element.38), channel_id=1, source_target_pairs={{0,4},{1,5},{2,6},{3,7},{4,0},{5,1},{6,2},{7,3},{8,12},{9,13},{10,... | collective-permute-start | bytes 196616 | tf_op jit(solution)/shard_map/ppermute | solution.py:337
  38.8 1.6 %collective-permute-start.16 = (bf16[64,512]{1,0:T(8,128)(2,1)S(1)}, bf16[64,512]{1,0:T(8,128)(2,1)S(1)}, u32[]{:S(2)}, u32[]{:S(2)}) collective-permute-start(bf16[64,512]{1,0:T(8,128)(2,1)S(1)} %get-tuple-element.39), channel_id=1, source_target_pairs={{0,6},{1,7},{2,0},{3,1},{4,2},{5,3},{6,4},{7,5},{8,14},{9,15},{10,... | collective-permute-start | bytes 196616 | tf_op jit(solution)/shard_map/ppermute | solution.py:337
  40.4 2.9 %collective-permute-done.14.refs_0_ = bf16[64,512]{1,0:T(8,128)(2,1)S(1)} collective-permute-done((bf16[64,512]{1,0:T(8,128)(2,1)S(1)}, bf16[64,512]{1,0:T(8,128)(2,1)S(1)}, u32[]{:S(2)}, u32[]{:S(2)}) %collective-permute-start.14) | collective-permute-done | bytes 65568 | tf_op jit(solution)/shard_map/ppermute | solution.py:337
  43.3 1.7 %collective-permute-done.15.refs_1_ = bf16[64,512]{1,0:T(8,128)(2,1)S(1)} collective-permute-done((bf16[64,512]{1,0:T(8,128)(2,1)S(1)}, bf16[64,512]{1,0:T(8,128)(2,1)S(1)}, u32[]{:S(2)}, u32[]{:S(2)}) %collective-permute-start.15) | collective-permute-done | bytes 65568 | tf_op jit(solution)/shard_map/ppermute | solution.py:337
  45.1 1.7 %shard_map.65 = bf16[64,4,16,128]{3,2,1,0:T(8,128)(2,1)} custom-call(bf16[64,512]{1,0:T(8,128)(2,1)S(1)} %collective-permute-done.14.refs_0_, bf16[64,512]{1,0:T(8,128)(2,1)S(1)} %collective-permute-done.15.refs_1_, bf16[64,512]{1,0:T(8,128)(2,1)S(1)} %collective-permute-done.16.refs_2_, f32[64,512]{1,0:T(8,128)S(1)} %shard_map.64.refs_3_, ...), custom_call_target="tpu_custom_call" | custom-call | bytes 4194304 | tf_op jit(solution)/shard_map/pallas_call | solution.py:451
  (23 shorter events, 0.3 us)
Async XLA Ops:
  2.5 13.8 %copy-start = (bf16[8,32,256]{2,1,0:T(8,128)(2,1)S(1)}, bf16[8,32,256]{2,1,0:T(8,128)(2,1)}, u32[]{:S(2)}) copy-start(bf16[8,32,256]{2,1,0:T(8,128)(2,1)} %refs_11_.1) | copy-start | bytes 393220
  2.5 13.8 %copy-start.1 = (bf16[2,256,128]{2,1,0:T(8,128)(2,1)S(1)}, bf16[2,256,128]{2,1,0:T(8,128)(2,1)}, u32[]{:S(2)}) copy-start(bf16[2,256,128]{2,1,0:T(8,128)(2,1)} %constant.6.clone.refs_10_) | copy-start | bytes 393220
  2.5 7.8 %collective-permute-start.5 = (bf16[64,512]{1,0:T(8,128)(2,1)S(1)}, bf16[64,512]{1,0:T(8,128)(2,1)S(1)}, u32[]{:S(2)}, u32[]{:S(2)}) collective-permute-start(bf16[64,512]{1,0:T(8,128)(2,1)S(1)} %get-tuple-element.23.edge_hbm.refs_0_), channel_id=1, source_target_pairs={{0,6},{1,7},{2,0},{3,1},{4,2},{5,3},{6,4},{7,5},{8,14},{9,15},{10,... | collective-permute-start | bytes 196616 | tf_op jit(solution)/shard_map/ppermute | solution.py:382
  7.6 6.2 %collective-permute-start.3 = (bf16[64,512]{1,0:T(8,128)(2,1)S(1)}, bf16[64,512]{1,0:T(8,128)(2,1)S(1)}, u32[]{:S(2)}, u32[]{:S(2)}) collective-permute-start(bf16[64,512]{1,0:T(8,128)(2,1)S(1)} %get-tuple-element.23.edge_hbm.refs_0_), channel_id=1, source_target_pairs={{0,2},{1,3},{2,4},{3,5},{4,6},{5,7},{6,0},{7,1},{8,10},{9,11},{10,... | collective-permute-start | bytes 196616 | tf_op jit(solution)/shard_map/ppermute | solution.py:382
  7.6 7.5 %collective-permute-start.1 = (bf16[64,512]{1,0:T(8,128)(2,1)S(1)}, bf16[64,512]{1,0:T(8,128)(2,1)S(1)}, u32[]{:S(2)}, u32[]{:S(2)}) collective-permute-start(bf16[64,512]{1,0:T(8,128)(2,1)S(1)} %get-tuple-element.23.edge_hbm.refs_0_), channel_id=1, source_target_pairs={{0,4},{1,5},{2,6},{3,7},{4,0},{5,1},{6,2},{7,3},{8,12},{9,13},{10,... | collective-permute-start | bytes 196616 | tf_op jit(solution)/shard_map/ppermute | solution.py:382
  10.2 4.9 %collective-permute-start = (bf16[64,512]{1,0:T(8,128)(2,1)S(1)}, bf16[64,512]{1,0:T(8,128)(2,1)S(1)}, u32[]{:S(2)}, u32[]{:S(2)}) collective-permute-start(bf16[64,512]{1,0:T(8,128)(2,1)S(1)} %get-tuple-element.24), channel_id=1, source_target_pairs={{0,1},{1,0},{2,3},{3,2},{4,5},{5,4},{6,7},{7,6},{8,9},{9,8},{10,11... | collective-permute-start | bytes 196616 | tf_op jit(solution)/shard_map/ppermute | solution.py:325
  10.3 4.8 %collective-permute-start.6 = (bf16[64,512]{1,0:T(8,128)(2,1)S(1)}, bf16[64,512]{1,0:T(8,128)(2,1)S(1)}, u32[]{:S(2)}, u32[]{:S(2)}) collective-permute-start(bf16[64,512]{1,0:T(8,128)(2,1)S(1)} %collective-permute-done.5.refs_6_), channel_id=1, source_target_pairs={{0,1},{1,0},{2,3},{3,2},{4,5},{5,4},{6,7},{7,6},{8,9},{9,8},{10,11... | collective-permute-start | bytes 196616 | tf_op jit(solution)/shard_map/ppermute | solution.py:325
  13.8 1.3 %collective-permute-start.4 = (bf16[64,512]{1,0:T(8,128)(2,1)S(1)}, bf16[64,512]{1,0:T(8,128)(2,1)S(1)}, u32[]{:S(2)}, u32[]{:S(2)}) collective-permute-start(bf16[64,512]{1,0:T(8,128)(2,1)S(1)} %collective-permute-done.3.refs_4_), channel_id=1, source_target_pairs={{0,1},{1,0},{2,3},{3,2},{4,5},{5,4},{6,7},{7,6},{8,9},{9,8},{10,11... | collective-permute-start | bytes 196616 | tf_op jit(solution)/shard_map/ppermute | solution.py:325
  15.1 1.3 %collective-permute-start.2 = (bf16[64,512]{1,0:T(8,128)(2,1)S(1)}, bf16[64,512]{1,0:T(8,128)(2,1)S(1)}, u32[]{:S(2)}, u32[]{:S(2)}) collective-permute-start(bf16[64,512]{1,0:T(8,128)(2,1)S(1)} %collective-permute-done.1.refs_2_), channel_id=1, source_target_pairs={{0,1},{1,0},{2,3},{3,2},{4,5},{5,4},{6,7},{7,6},{8,9},{9,8},{10,11... | collective-permute-start | bytes 196616 | tf_op jit(solution)/shard_map/ppermute | solution.py:325
  16.4 9.4 %copy-start.2 = (bf16[64,128]{1,0:T(8,128)(2,1)S(1)}, bf16[64,128]{1,0:T(8,128)(2,1)}, u32[]{:S(2)}) copy-start(bf16[64,128]{1,0:T(8,128)(2,1)} %constant.8.clone.refs_5_) | copy-start | bytes 49156
  16.4 9.4 %copy-start.3 = (bf16[64,128]{1,0:T(8,128)(2,1)S(1)}, bf16[64,128]{1,0:T(8,128)(2,1)}, u32[]{:S(2)}) copy-start(bf16[64,128]{1,0:T(8,128)(2,1)} %constant.7.clone.refs_4_) | copy-start | bytes 49156
  17.8 5.9 %collective-permute-start.7 = (bf16[192,256]{1,0:T(8,128)(2,1)S(1)}, bf16[192,256]{1,0:T(8,128)(2,1)S(1)}, u32[]{:S(2)}, u32[]{:S(2)}) collective-permute-start(bf16[192,256]{1,0:T(8,128)(2,1)S(1)} %get-tuple-element.27), channel_id=1, source_target_pairs={{0,24},{8,16},{16,8},{24,0},{1,25},{9,17},{17,9},{25,1},{2,26},{10... | collective-permute-start | bytes 294920 | tf_op jit(solution)/shard_map/ppermute | solution.py:325
  20.3 5.4 %collective-permute-start.8 = (bf16[192,256]{1,0:T(8,128)(2,1)S(1)}, bf16[192,256]{1,0:T(8,128)(2,1)S(1)}, u32[]{:S(2)}, u32[]{:S(2)}) collective-permute-start(bf16[192,256]{1,0:T(8,128)(2,1)S(1)} %get-tuple-element.28), channel_id=1, source_target_pairs={{0,16},{8,24},{16,0},{24,8},{1,17},{9,25},{17,1},{25,9},{2,18},{10... | collective-permute-start | bytes 294920 | tf_op jit(solution)/shard_map/ppermute | solution.py:325
  20.8 5.0 %collective-permute-start.9 = (bf16[192,256]{1,0:T(8,128)(2,1)S(1)}, bf16[192,256]{1,0:T(8,128)(2,1)S(1)}, u32[]{:S(2)}, u32[]{:S(2)}) collective-permute-start(bf16[192,256]{1,0:T(8,128)(2,1)S(1)} %get-tuple-element.29), channel_id=1, source_target_pairs={{0,8},{8,0},{16,24},{24,16},{1,9},{9,1},{17,25},{25,17},{2,10},{10... | collective-permute-start | bytes 294920 | tf_op jit(solution)/shard_map/ppermute | solution.py:325
  26.3 5.7 %collective-permute-start.10 = (bf16[128,256]{1,0:T(8,128)(2,1)S(1)}, bf16[128,256]{1,0:T(8,128)(2,1)S(1)}, u32[]{:S(2)}, u32[]{:S(2)}) collective-permute-start(bf16[128,256]{1,0:T(8,128)(2,1)S(1)} %get-tuple-element.31), channel_id=1, source_target_pairs={{0,24},{8,16},{16,8},{24,0},{1,25},{9,17},{17,9},{25,1},{2,26},{10... | collective-permute-start | bytes 196616 | tf_op jit(solution)/shard_map/ppermute | solution.py:325
  28.1 4.4 %collective-permute-start.11 = (bf16[128,256]{1,0:T(8,128)(2,1)S(1)}, bf16[128,256]{1,0:T(8,128)(2,1)S(1)}, u32[]{:S(2)}, u32[]{:S(2)}) collective-permute-start(bf16[128,256]{1,0:T(8,128)(2,1)S(1)} %get-tuple-element.32), channel_id=1, source_target_pairs={{0,16},{8,24},{16,0},{24,8},{1,17},{9,25},{17,1},{25,9},{2,18},{10... | collective-permute-start | bytes 196616 | tf_op jit(solution)/shard_map/ppermute | solution.py:325
  29.4 4.3 %collective-permute-start.12 = (bf16[128,256]{1,0:T(8,128)(2,1)S(1)}, bf16[128,256]{1,0:T(8,128)(2,1)S(1)}, u32[]{:S(2)}, u32[]{:S(2)}) collective-permute-start(bf16[128,256]{1,0:T(8,128)(2,1)S(1)} %get-tuple-element.33), channel_id=1, source_target_pairs={{0,8},{8,0},{16,24},{24,16},{1,9},{9,1},{17,25},{25,17},{2,10},{10... | collective-permute-start | bytes 196616 | tf_op jit(solution)/shard_map/ppermute | solution.py:325
  34.3 2.2 %collective-permute-start.13 = (bf16[3,64,512]{2,1,0:T(8,128)(2,1)S(1)}, bf16[3,64,512]{2,1,0:T(8,128)(2,1)S(1)}, u32[]{:S(2)}, u32[]{:S(2)}) collective-permute-start(bf16[3,64,512]{2,1,0:T(8,128)(2,1)S(1)} %get-tuple-element.36.refs_0_), channel_id=1, source_target_pairs={{0,1},{1,0},{2,3},{3,2},{4,5},{5,4},{6,7},{7,6},{8,9},{9,8},{10,11... | collective-permute-start | bytes 589832 | tf_op jit(solution)/shard_map/ppermute | solution.py:325
  35.9 4.5 %collective-permute-start.17 = (bf16[1,64,512]{2,1,0:T(8,128)(2,1)S(1)}, bf16[1,64,512]{2,1,0:T(8,128)(2,1)S(1)}, u32[]{:S(2)}, u32[]{:S(2)}) collective-permute-start(bf16[1,64,512]{2,1,0:T(8,128)(2,1)S(1)} %shard_map.61.refs_0_), channel_id=1, source_target_pairs={{0,1},{1,0},{2,3},{3,2},{4,5},{5,4},{6,7},{7,6},{8,9},{9,8},{10,11... | collective-permute-start | bytes 196616 | tf_op jit(solution)/shard_map/ppermute | solution.py:325
  36.5 6.8 %collective-permute-start.14 = (bf16[64,512]{1,0:T(8,128)(2,1)S(1)}, bf16[64,512]{1,0:T(8,128)(2,1)S(1)}, u32[]{:S(2)}, u32[]{:S(2)}) collective-permute-start(bf16[64,512]{1,0:T(8,128)(2,1)S(1)} %get-tuple-element.37), channel_id=1, source_target_pairs={{0,2},{1,3},{2,4},{3,5},{4,6},{5,7},{6,0},{7,1},{8,10},{9,11},{10,... | collective-permute-start | bytes 196616 | tf_op jit(solution)/shard_map/ppermute | solution.py:337
  36.6 8.5 %collective-permute-start.15 = (bf16[64,512]{1,0:T(8,128)(2,1)S(1)}, bf16[64,512]{1,0:T(8,128)(2,1)S(1)}, u32[]{:S(2)}, u32[]{:S(2)}) collective-permute-start(bf16[64,512]{1,0:T(8,128)(2,1)S(1)} %get-tuple-element.38), channel_id=1, source_target_pairs={{0,4},{1,5},{2,6},{3,7},{4,0},{5,1},{6,2},{7,3},{8,12},{9,13},{10,... | collective-permute-start | bytes 196616 | tf_op jit(solution)/shard_map/ppermute | solution.py:337
  38.8 6.3 %collective-permute-start.16 = (bf16[64,512]{1,0:T(8,128)(2,1)S(1)}, bf16[64,512]{1,0:T(8,128)(2,1)S(1)}, u32[]{:S(2)}, u32[]{:S(2)}) collective-permute-start(bf16[64,512]{1,0:T(8,128)(2,1)S(1)} %get-tuple-element.39), channel_id=1, source_target_pairs={{0,6},{1,7},{2,0},{3,1},{4,2},{5,3},{6,4},{7,5},{8,14},{9,15},{10,... | collective-permute-start | bytes 196616 | tf_op jit(solution)/shard_map/ppermute | solution.py:337

commit v22 on v18

--- a/solution.py
+++ b/solution.py
@@ -330,10 +330,15 @@
 
 def shift_along(pieces):
     chunks = len(pieces)
+    inner = range(chunks // 4, chunks - chunks // 4)
     came = []
     for s in range(1, chunks):
-        pairs = [(2 * z + core, 2 * ((z - s) % chunks) + core) for z in range(chunks) for core in range(2)]
-        came.append(lax.ppermute(pieces[s], "pts", pairs))
+        sources = [range(chunks)]
+        if 2 * s == chunks:
+            sources = [inner, [z for z in range(chunks) if z not in inner]]
+        for chosen in sources:
+            pairs = [(2 * z + core, 2 * ((z - s) % chunks) + core) for z in chosen for core in range(2)]
+            came.append(lax.ppermute(pieces[s], "pts", pairs))
     return came[::-1] + [pieces[0]]
 
 
@@ -444,9 +449,9 @@
     spans = norb // LANES
     rows = pair * spans * 2
     result = call(
-        functools.partial(exchange_kernel, chunks, 1.0 / math.sqrt(points * blocks)),
+        functools.partial(exchange_kernel, len(sums), 1.0 / math.sqrt(points * blocks)),
         shape((out_rows, local_k // pair, rows, LANES), BF16),
-        chunks + 1,
+        len(sums) + 1,
         [
             pltpu.VMEM((local_k // pair, out_rows * rows, LANES), F32),
             pltpu.VMEM((local_k // pair, out_rows, rows, LANES), BF16),

time: 44.8 us -> 48.8 us (1.089)
  starting transfers between devices: 18.5 us -> 24.2 us
  waiting for transfers between devices: 16.1 us -> 14.2 us
    ppermute x3 -> x4, starting transfers between devices: 4.93 us -> 10.7 us  [shift_along(): came.append(lax.ppermute(pieces[s], 'pts', pairs))]
    ppermute x3 -> x4, waiting for transfers between devices: 3.32 us -> 1.47 us  [shift_along(): came.append(lax.ppermute(pieces[s], 'pts', pairs))]
  transfers between devices with their start and end apart: 18 -> 19, of which waited for: 13 -> 12; matrix products, arithmetic and copies ran while one was open for 0% -> 0% of each run, Pallas kernels for 7% -> 6%
where the time goes in v22:
time: 48.8 us; the launch traced here: 48.6 us
  starting transfers between devices  24.2 us (50%)
  waiting for transfers between devices  14.2 us (29%)
  Pallas kernels  9.89 us (20%)
    ppermute x15, starting transfers between devices, swap(): return lax.ppermute(value, axis, [(i, i ^ mask) for i in range(size)])  13.6 us
    ppermute x15, waiting for transfers between devices, swap(): return lax.ppermute(value, axis, [(i, i ^ mask) for i in range(size)])  12.8 us
    ppermute x4, starting transfers between devices, shift_along(): came.append(lax.ppermute(pieces[s], 'pts', pairs))  10.7 us
    pallas_call x1, Pallas kernels, body(): call(functools.partial(edge_kernel, per_block), [shape((local_k * 2 * per...  2.5 us
    pallas_call x1, Pallas kernels, body(): call(functools.partial(exchange_kernel, len(sums), 1.0 / math.sqrt(points...  1.68 us
    pallas_call x1, Pallas kernels, body(): call(rest_kernel, [shape(edge.shape, BF16), shape((local_k, 2, norb, poin...  1.58 us
    pallas_call x3, Pallas kernels, rows_of(): call(functools.partial(next_weight_kernel, offsets, flip, out_rows), shap...  1.51 us
    ppermute x4, waiting for transfers between devices, shift_along(): came.append(lax.ppermute(pieces[s], 'pts', pairs))  1.47 us
  transfers between devices with their start and end apart: 19, of which 12 were waited for; matrix products, arithmetic and copies ran while one was open for 0% of the time, Pallas kernels for 6%

profile of v22, /device:TPU:0, one launch (start us, length us, event | category | flops | bytes accessed | tf_op | source)
XLA Modules:
  0.0 48.6 jit_solution(8206546076017886569)
XLA Ops:
  0.0 2.5 %shard_map.55 = (bf16[64,512]{1,0:T(8,128)(2,1)S(1)}, bf16[8,2,512,128]{3,2,1,0:T(8,128)(2,1)S(1)}) custom-call(bf16[8,2,512,256]{3,2,1,0:T(8,128)(2,1)} %orb_hbm.3), custom_call_target="tpu_custom_call" | custom-call | bytes 4194304 | tf_op jit(solution)/shard_map/pallas_call | solution.py:357
  2.5 5.1 %collective-permute-start.5 = (bf16[64,512]{1,0:T(8,128)(2,1)S(1)}, bf16[64,512]{1,0:T(8,128)(2,1)S(1)}, u32[]{:S(2)}, u32[]{:S(2)}) collective-permute-start(bf16[64,512]{1,0:T(8,128)(2,1)S(1)} %get-tuple-element.23.edge_hbm.refs_0_), channel_id=1, source_target_pairs={{0,6},{1,7},{2,4},{3,5},{4,2},{5,3},{6,0},{7,1},{8,14},{9,15},{10,... | collective-permute-start | bytes 196616 | tf_op jit(solution)/shard_map/ppermute | solution.py:324
  7.7 0.6 %collective-permute-start.1 = (bf16[64,512]{1,0:T(8,128)(2,1)S(1)}, bf16[64,512]{1,0:T(8,128)(2,1)S(1)}, u32[]{:S(2)}, u32[]{:S(2)}) collective-permute-start(bf16[64,512]{1,0:T(8,128)(2,1)S(1)} %get-tuple-element.23.edge_hbm.refs_0_), channel_id=1, source_target_pairs={{0,4},{1,5},{2,6},{3,7},{4,0},{5,1},{6,2},{7,3},{8,12},{9,13},{10,... | collective-permute-start | bytes 196616 | tf_op jit(solution)/shard_map/ppermute | solution.py:324
  8.3 1.6 %shard_map.56 = (bf16[64,512]{1,0:T(8,128)(2,1)S(1)}, bf16[8,2,512,128]{3,2,1,0:T(8,128)(2,1)S(1)}) custom-call(bf16[8,2,512,256]{3,2,1,0:T(8,128)(2,1)} %orb_hbm.3, bf16[64,512]{1,0:T(8,128)(2,1)S(1)} %get-tuple-element.23.edge_hbm.refs_0_), custom_call_target="tpu_custom_call" | custom-call | bytes 4194304 | tf_op jit(solution)/shard_map/pallas_call | solution.py:369
  10.0 0.6 %collective-permute-done.5.refs_6_ = bf16[64,512]{1,0:T(8,128)(2,1)S(1)} collective-permute-done((bf16[64,512]{1,0:T(8,128)(2,1)S(1)}, bf16[64,512]{1,0:T(8,128)(2,1)S(1)}, u32[]{:S(2)}, u32[]{:S(2)}) %collective-permute-start.5) | collective-permute-done | bytes 65568 | tf_op jit(solution)/shard_map/ppermute | solution.py:324
  10.6 1.8 %collective-permute-done.3.refs_4_ = bf16[64,512]{1,0:T(8,128)(2,1)S(1)} collective-permute-done((bf16[64,512]{1,0:T(8,128)(2,1)S(1)}, bf16[64,512]{1,0:T(8,128)(2,1)S(1)}, u32[]{:S(2)}, u32[]{:S(2)}) %collective-permute-start.3) | collective-permute-done | bytes 65568 | tf_op jit(solution)/shard_map/ppermute | solution.py:324
  12.3 1.0 %collective-permute-done.1.refs_2_ = bf16[64,512]{1,0:T(8,128)(2,1)S(1)} collective-permute-done((bf16[64,512]{1,0:T(8,128)(2,1)S(1)}, bf16[64,512]{1,0:T(8,128)(2,1)S(1)}, u32[]{:S(2)}, u32[]{:S(2)}) %collective-permute-start.1) | collective-permute-done | bytes 65568 | tf_op jit(solution)/shard_map/ppermute | solution.py:324
  13.6 1.0 %collective-permute-done.2.refs_3_ = bf16[64,512]{1,0:T(8,128)(2,1)S(1)} collective-permute-done((bf16[64,512]{1,0:T(8,128)(2,1)S(1)}, bf16[64,512]{1,0:T(8,128)(2,1)S(1)}, u32[]{:S(2)}, u32[]{:S(2)}) %collective-permute-start.2) | collective-permute-done | bytes 65568 | tf_op jit(solution)/shard_map/ppermute | solution.py:324
  14.6 1.4 %shard_map.57 = (bf16[192,256]{1,0:T(8,128)(2,1)S(1)}, bf16[192,256]{1,0:T(8,128)(2,1)S(1)}, bf16[192,256]{1,0:T(8,128)(2,1)S(1)}, bf16[192,256]{1,0:T(8,128)(2,1)S(1)}, bf16[4,8,16,1024]{3,2,1,0:T(8,128)(2,1)S(1)}) custom-call(bf16[64,512]{1,0:T(8,128)(2,1)S(1)} %get-tuple-element.23.edge_hbm.refs_0_, bf16[64,512]{1,0:T(8,128)(2,1)S(1)} %collective-permute-done.refs_1_, ...), custom_call_target="tpu_custom_call" | custom-call | bytes 6291456 | tf_op jit(solution)/shard_map/pallas_call | solution.py:393
  15.9 2.5 %collective-permute-start.7 = (bf16[192,256]{1,0:T(8,128)(2,1)S(1)}, bf16[192,256]{1,0:T(8,128)(2,1)S(1)}, u32[]{:S(2)}, u32[]{:S(2)}) collective-permute-start(bf16[192,256]{1,0:T(8,128)(2,1)S(1)} %get-tuple-element.27), channel_id=1, source_target_pairs={{0,24},{8,16},{16,8},{24,0},{1,25},{9,17},{17,9},{25,1},{2,26},{10... | collective-permute-start | bytes 294920 | tf_op jit(solution)/shard_map/ppermute | solution.py:324
  18.4 0.5 %collective-permute-start.8 = (bf16[192,256]{1,0:T(8,128)(2,1)S(1)}, bf16[192,256]{1,0:T(8,128)(2,1)S(1)}, u32[]{:S(2)}, u32[]{:S(2)}) collective-permute-start(bf16[192,256]{1,0:T(8,128)(2,1)S(1)} %get-tuple-element.28), channel_id=1, source_target_pairs={{0,16},{8,24},{16,0},{24,8},{1,17},{9,25},{17,1},{25,9},{2,18},{10... | collective-permute-start | bytes 294920 | tf_op jit(solution)/shard_map/ppermute | solution.py:324
  18.9 0.5 %collective-permute-start.9 = (bf16[192,256]{1,0:T(8,128)(2,1)S(1)}, bf16[192,256]{1,0:T(8,128)(2,1)S(1)}, u32[]{:S(2)}, u32[]{:S(2)}) collective-permute-start(bf16[192,256]{1,0:T(8,128)(2,1)S(1)} %get-tuple-element.29), channel_id=1, source_target_pairs={{0,8},{8,0},{16,24},{24,16},{1,9},{9,1},{17,25},{25,17},{2,10},{10... | collective-permute-start | bytes 294920 | tf_op jit(solution)/shard_map/ppermute | solution.py:324
  19.5 2.4 %collective-permute-done.7.refs_0_ = bf16[192,256]{1,0:T(8,128)(2,1)S(1)} collective-permute-done((bf16[192,256]{1,0:T(8,128)(2,1)S(1)}, bf16[192,256]{1,0:T(8,128)(2,1)S(1)}, u32[]{:S(2)}, u32[]{:S(2)}) %collective-permute-start.7) | collective-permute-done | bytes 98336 | tf_op jit(solution)/shard_map/ppermute | solution.py:324
  21.8 2.0 %collective-permute-done.8.refs_1_ = bf16[192,256]{1,0:T(8,128)(2,1)S(1)} collective-permute-done((bf16[192,256]{1,0:T(8,128)(2,1)S(1)}, bf16[192,256]{1,0:T(8,128)(2,1)S(1)}, u32[]{:S(2)}, u32[]{:S(2)}) %collective-permute-start.8) | collective-permute-done | bytes 98336 | tf_op jit(solution)/shard_map/ppermute | solution.py:324
  23.9 0.6 %shard_map.58 = (bf16[128,256]{1,0:T(8,128)(2,1)S(1)}, bf16[128,256]{1,0:T(8,128)(2,1)S(1)}, bf16[128,256]{1,0:T(8,128)(2,1)S(1)}, bf16[128,256]{1,0:T(8,128)(2,1)S(1)}) custom-call(bf16[192,256]{1,0:T(8,128)(2,1)S(1)} %collective-permute-done.7.refs_0_, bf16[192,256]{1,0:T(8,128)(2,1)S(1)} %collective-permute-done.8.refs_1_, ...), custom_call_target="tpu_custom_call" | custom-call | bytes 2097152 | tf_op jit(solution)/shard_map/pallas_call | solution.py:406
  24.5 1.8 %collective-permute-start.10 = (bf16[128,256]{1,0:T(8,128)(2,1)S(1)}, bf16[128,256]{1,0:T(8,128)(2,1)S(1)}, u32[]{:S(2)}, u32[]{:S(2)}) collective-permute-start(bf16[128,256]{1,0:T(8,128)(2,1)S(1)} %get-tuple-element.31), channel_id=1, source_target_pairs={{0,24},{8,16},{16,8},{24,0},{1,25},{9,17},{17,9},{25,1},{2,26},{10... | collective-permute-start | bytes 196616 | tf_op jit(solution)/shard_map/ppermute | solution.py:324
  26.3 1.3 %collective-permute-start.11 = (bf16[128,256]{1,0:T(8,128)(2,1)S(1)}, bf16[128,256]{1,0:T(8,128)(2,1)S(1)}, u32[]{:S(2)}, u32[]{:S(2)}) collective-permute-start(bf16[128,256]{1,0:T(8,128)(2,1)S(1)} %get-tuple-element.32), channel_id=1, source_target_pairs={{0,16},{8,24},{16,0},{24,8},{1,17},{9,25},{17,1},{25,9},{2,18},{10... | collective-permute-start | bytes 196616 | tf_op jit(solution)/shard_map/ppermute | solution.py:324
  27.6 0.5 %collective-permute-start.12 = (bf16[128,256]{1,0:T(8,128)(2,1)S(1)}, bf16[128,256]{1,0:T(8,128)(2,1)S(1)}, u32[]{:S(2)}, u32[]{:S(2)}) collective-permute-start(bf16[128,256]{1,0:T(8,128)(2,1)S(1)} %get-tuple-element.33), channel_id=1, source_target_pairs={{0,8},{8,0},{16,24},{24,16},{1,9},{9,1},{17,25},{25,17},{2,10},{10... | collective-permute-start | bytes 196616 | tf_op jit(solution)/shard_map/ppermute | solution.py:324
  28.1 2.1 %collective-permute-done.10.refs_0_ = bf16[128,256]{1,0:T(8,128)(2,1)S(1)} collective-permute-done((bf16[128,256]{1,0:T(8,128)(2,1)S(1)}, bf16[128,256]{1,0:T(8,128)(2,1)S(1)}, u32[]{:S(2)}, u32[]{:S(2)}) %collective-permute-start.10) | collective-permute-done | bytes 65568 | tf_op jit(solution)/shard_map/ppermute | solution.py:324
  30.2 0.5 %collective-permute-done.11.refs_1_ = bf16[128,256]{1,0:T(8,128)(2,1)S(1)} collective-permute-done((bf16[128,256]{1,0:T(8,128)(2,1)S(1)}, bf16[128,256]{1,0:T(8,128)(2,1)S(1)}, u32[]{:S(2)}, u32[]{:S(2)}) %collective-permute-start.11) | collective-permute-done | bytes 65568 | tf_op jit(solution)/shard_map/ppermute | solution.py:324
  30.7 1.1 %collective-permute-done.12.refs_2_ = bf16[128,256]{1,0:T(8,128)(2,1)S(1)} collective-permute-done((bf16[128,256]{1,0:T(8,128)(2,1)S(1)}, bf16[128,256]{1,0:T(8,128)(2,1)S(1)}, u32[]{:S(2)}, u32[]{:S(2)}) %collective-permute-start.12) | collective-permute-done | bytes 65568 | tf_op jit(solution)/shard_map/ppermute | solution.py:324
  31.8 0.6 %shard_map.59 = (bf16[3,64,512]{2,1,0:T(8,128)(2,1)S(1)}, bf16[4,128,1024]{2,1,0:T(8,128)(2,1)S(1)}) custom-call(bf16[128,256]{1,0:T(8,128)(2,1)S(1)} %collective-permute-done.10.refs_0_, bf16[128,256]{1,0:T(8,128)(2,1)S(1)} %collective-permute-done.11.refs_1_, bf16[128,256]{1,0:T(8,128)(2,1)S(1)} %collective-permute-done.12.refs_2_, ...), custom_call_target="tpu_custom_call" | custom-call | tf_op jit(solution)/shard_map/pallas_call | solution.py:422
  32.5 0.5 shard_map.60.refs_0_
  33.0 0.6 %collective-permute-start.18 = (bf16[1,64,512]{2,1,0:T(8,128)(2,1)S(1)}, bf16[1,64,512]{2,1,0:T(8,128)(2,1)S(1)}, u32[]{:S(2)}, u32[]{:S(2)}) collective-permute-start(bf16[1,64,512]{2,1,0:T(8,128)(2,1)S(1)} %shard_map.60.refs_0_), channel_id=1, source_target_pairs={{0,1},{1,0},{2,3},{3,2},{4,5},{5,4},{6,7},{7,6},{8,9},{9,8},{10,11... | collective-permute-start | bytes 196616 | tf_op jit(solution)/shard_map/ppermute | solution.py:324
  33.6 0.6 %shard_map.61.keep_ref = f32[3,64,512]{2,1,0:T(8,128)S(1)} custom-call(bf16[4,128,1024]{2,1,0:T(8,128)(2,1)S(1)} %get-tuple-element.35.right_ref, bf16[8,2,512,128]{3,2,1,0:T(8,128)(2,1)S(1)} %get-tuple-element.25.refs_8_.refs_4_.orb_ref, bf16[8,2,512,128]{3,2,1,0:T(8,128)(2,1)S(1)} %get-tuple-element.26.refs_9_.refs_5_.rest_ref, ...), custom_call_target="tpu_custom_call" | custom-call | tf_op jit(solution)/shard_map/pallas_call | solution.py:433
  34.2 1.6 %collective-permute-start.14 = (bf16[64,512]{1,0:T(8,128)(2,1)S(1)}, bf16[64,512]{1,0:T(8,128)(2,1)S(1)}, u32[]{:S(2)}, u32[]{:S(2)}) collective-permute-start(bf16[64,512]{1,0:T(8,128)(2,1)S(1)} %get-tuple-element.37), channel_id=1, source_target_pairs={{0,2},{1,3},{2,4},{3,5},{4,6},{5,7},{6,0},{7,1},{8,10},{9,11},{10,... | collective-permute-start | bytes 196616 | tf_op jit(solution)/shard_map/ppermute | solution.py:341
  35.8 1.3 %collective-permute-start.16 = (bf16[64,512]{1,0:T(8,128)(2,1)S(1)}, bf16[64,512]{1,0:T(8,128)(2,1)S(1)}, u32[]{:S(2)}, u32[]{:S(2)}) collective-permute-start(bf16[64,512]{1,0:T(8,128)(2,1)S(1)} %get-tuple-element.38), channel_id=1, source_target_pairs={{2,6},{3,7},{4,0},{5,1},{10,14},{11,15},{12,8},{13,9},{18,22},{19,... | collective-permute-start | bytes 196616 | tf_op jit(solution)/shard_map/ppermute | solution.py:341
  37.1 5.4 %collective-permute-start.15 = (bf16[64,512]{1,0:T(8,128)(2,1)S(1)}, bf16[64,512]{1,0:T(8,128)(2,1)S(1)}, u32[]{:S(2)}, u32[]{:S(2)}) collective-permute-start(bf16[64,512]{1,0:T(8,128)(2,1)S(1)} %get-tuple-element.38), channel_id=1, source_target_pairs={{0,4},{1,5},{6,2},{7,3},{8,12},{9,13},{14,10},{15,11},{16,20},{17,... | collective-permute-start | bytes 196616 | tf_op jit(solution)/shard_map/ppermute | solution.py:341
  42.6 2.3 %collective-permute-start.17 = (bf16[64,512]{1,0:T(8,128)(2,1)S(1)}, bf16[64,512]{1,0:T(8,128)(2,1)S(1)}, u32[]{:S(2)}, u32[]{:S(2)}) collective-permute-start(bf16[64,512]{1,0:T(8,128)(2,1)S(1)} %get-tuple-element.39.refs_0_), channel_id=1, source_target_pairs={{0,6},{1,7},{2,0},{3,1},{4,2},{5,3},{6,4},{7,5},{8,14},{9,15},{10,... | collective-permute-start | bytes 196616 | tf_op jit(solution)/shard_map/ppermute | solution.py:341
  44.9 0.5 shard_map.63.keep_ref
  45.4 1.5 %collective-permute-done.17.refs_3_ = bf16[64,512]{1,0:T(8,128)(2,1)S(1)} collective-permute-done((bf16[64,512]{1,0:T(8,128)(2,1)S(1)}, bf16[64,512]{1,0:T(8,128)(2,1)S(1)}, u32[]{:S(2)}, u32[]{:S(2)}) %collective-permute-start.17) | collective-permute-done | bytes 65568 | tf_op jit(solution)/shard_map/ppermute | solution.py:341
  46.9 1.7 %shard_map.65 = bf16[64,4,16,128]{3,2,1,0:T(8,128)(2,1)} custom-call(bf16[64,512]{1,0:T(8,128)(2,1)S(1)} %collective-permute-done.14.refs_0_, bf16[64,512]{1,0:T(8,128)(2,1)S(1)} %collective-permute-done.15.refs_1_, bf16[64,512]{1,0:T(8,128)(2,1)S(1)} %collective-permute-done.16.refs_2_, bf16[64,512]{1,0:T(8,128)(2,1)S(1)} %collective-permute-done.17.refs_3_, ...), custom_call_target="tpu_custom_call" | custom-call | bytes 4194304 | tf_op jit(solution)/shard_map/pallas_call | solution.py:451
  (25 shorter events, 0.6 us)
Async XLA Ops:
  2.5 12.0 %copy-start = (bf16[8,32,256]{2,1,0:T(8,128)(2,1)S(1)}, bf16[8,32,256]{2,1,0:T(8,128)(2,1)}, u32[]{:S(2)}) copy-start(bf16[8,32,256]{2,1,0:T(8,128)(2,1)} %refs_11_.1) | copy-start | bytes 393220
  2.5 12.0 %copy-start.1 = (bf16[2,256,128]{2,1,0:T(8,128)(2,1)S(1)}, bf16[2,256,128]{2,1,0:T(8,128)(2,1)}, u32[]{:S(2)}) copy-start(bf16[2,256,128]{2,1,0:T(8,128)(2,1)} %constant.6.clone.refs_10_) | copy-start | bytes 393220
  2.5 8.0 %collective-permute-start.5 = (bf16[64,512]{1,0:T(8,128)(2,1)S(1)}, bf16[64,512]{1,0:T(8,128)(2,1)S(1)}, u32[]{:S(2)}, u32[]{:S(2)}) collective-permute-start(bf16[64,512]{1,0:T(8,128)(2,1)S(1)} %get-tuple-element.23.edge_hbm.refs_0_), channel_id=1, source_target_pairs={{0,6},{1,7},{2,4},{3,5},{4,2},{5,3},{6,0},{7,1},{8,14},{9,15},{10,... | collective-permute-start | bytes 196616 | tf_op jit(solution)/shard_map/ppermute | solution.py:324
  7.6 4.7 %collective-permute-start.3 = (bf16[64,512]{1,0:T(8,128)(2,1)S(1)}, bf16[64,512]{1,0:T(8,128)(2,1)S(1)}, u32[]{:S(2)}, u32[]{:S(2)}) collective-permute-start(bf16[64,512]{1,0:T(8,128)(2,1)S(1)} %get-tuple-element.23.edge_hbm.refs_0_), channel_id=1, source_target_pairs={{0,2},{1,3},{2,0},{3,1},{4,6},{5,7},{6,4},{7,5},{8,10},{9,11},{10,... | collective-permute-start | bytes 196616 | tf_op jit(solution)/shard_map/ppermute | solution.py:324
  7.7 5.6 %collective-permute-start.1 = (bf16[64,512]{1,0:T(8,128)(2,1)S(1)}, bf16[64,512]{1,0:T(8,128)(2,1)S(1)}, u32[]{:S(2)}, u32[]{:S(2)}) collective-permute-start(bf16[64,512]{1,0:T(8,128)(2,1)S(1)} %get-tuple-element.23.edge_hbm.refs_0_), channel_id=1, source_target_pairs={{0,4},{1,5},{2,6},{3,7},{4,0},{5,1},{6,2},{7,3},{8,12},{9,13},{10,... | collective-permute-start | bytes 196616 | tf_op jit(solution)/shard_map/ppermute | solution.py:324
  9.9 3.4 %collective-permute-start = (bf16[64,512]{1,0:T(8,128)(2,1)S(1)}, bf16[64,512]{1,0:T(8,128)(2,1)S(1)}, u32[]{:S(2)}, u32[]{:S(2)}) collective-permute-start(bf16[64,512]{1,0:T(8,128)(2,1)S(1)} %get-tuple-element.24), channel_id=1, source_target_pairs={{0,1},{1,0},{2,3},{3,2},{4,5},{5,4},{6,7},{7,6},{8,9},{9,8},{10,11... | collective-permute-start | bytes 196616 | tf_op jit(solution)/shard_map/ppermute | solution.py:324
  10.5 2.7 %collective-permute-start.6 = (bf16[64,512]{1,0:T(8,128)(2,1)S(1)}, bf16[64,512]{1,0:T(8,128)(2,1)S(1)}, u32[]{:S(2)}, u32[]{:S(2)}) collective-permute-start(bf16[64,512]{1,0:T(8,128)(2,1)S(1)} %collective-permute-done.5.refs_6_), channel_id=1, source_target_pairs={{0,1},{1,0},{2,3},{3,2},{4,5},{5,4},{6,7},{7,6},{8,9},{9,8},{10,11... | collective-permute-start | bytes 196616 | tf_op jit(solution)/shard_map/ppermute | solution.py:324
  12.3 1.3 %collective-permute-start.4 = (bf16[64,512]{1,0:T(8,128)(2,1)S(1)}, bf16[64,512]{1,0:T(8,128)(2,1)S(1)}, u32[]{:S(2)}, u32[]{:S(2)}) collective-permute-start(bf16[64,512]{1,0:T(8,128)(2,1)S(1)} %collective-permute-done.3.refs_4_), channel_id=1, source_target_pairs={{0,1},{1,0},{2,3},{3,2},{4,5},{5,4},{6,7},{7,6},{8,9},{9,8},{10,11... | collective-permute-start | bytes 196616 | tf_op jit(solution)/shard_map/ppermute | solution.py:324
  13.3 1.3 %collective-permute-start.2 = (bf16[64,512]{1,0:T(8,128)(2,1)S(1)}, bf16[64,512]{1,0:T(8,128)(2,1)S(1)}, u32[]{:S(2)}, u32[]{:S(2)}) collective-permute-start(bf16[64,512]{1,0:T(8,128)(2,1)S(1)} %collective-permute-done.1.refs_2_), channel_id=1, source_target_pairs={{0,1},{1,0},{2,3},{3,2},{4,5},{5,4},{6,7},{7,6},{8,9},{9,8},{10,11... | collective-permute-start | bytes 196616 | tf_op jit(solution)/shard_map/ppermute | solution.py:324
  14.5 9.4 %copy-start.2 = (bf16[64,128]{1,0:T(8,128)(2,1)S(1)}, bf16[64,128]{1,0:T(8,128)(2,1)}, u32[]{:S(2)}) copy-start(bf16[64,128]{1,0:T(8,128)(2,1)} %constant.8.clone.refs_5_) | copy-start | bytes 49156
  14.5 9.4 %copy-start.3 = (bf16[64,128]{1,0:T(8,128)(2,1)S(1)}, bf16[64,128]{1,0:T(8,128)(2,1)}, u32[]{:S(2)}) copy-start(bf16[64,128]{1,0:T(8,128)(2,1)} %constant.7.clone.refs_4_) | copy-start | bytes 49156
  15.9 5.9 %collective-permute-start.7 = (bf16[192,256]{1,0:T(8,128)(2,1)S(1)}, bf16[192,256]{1,0:T(8,128)(2,1)S(1)}, u32[]{:S(2)}, u32[]{:S(2)}) collective-permute-start(bf16[192,256]{1,0:T(8,128)(2,1)S(1)} %get-tuple-element.27), channel_id=1, source_target_pairs={{0,24},{8,16},{16,8},{24,0},{1,25},{9,17},{17,9},{25,1},{2,26},{10... | collective-permute-start | bytes 294920 | tf_op jit(solution)/shard_map/ppermute | solution.py:324
  18.4 5.4 %collective-permute-start.8 = (bf16[192,256]{1,0:T(8,128)(2,1)S(1)}, bf16[192,256]{1,0:T(8,128)(2,1)S(1)}, u32[]{:S(2)}, u32[]{:S(2)}) collective-permute-start(bf16[192,256]{1,0:T(8,128)(2,1)S(1)} %get-tuple-element.28), channel_id=1, source_target_pairs={{0,16},{8,24},{16,0},{24,8},{1,17},{9,25},{17,1},{25,9},{2,18},{10... | collective-permute-start | bytes 294920 | tf_op jit(solution)/shard_map/ppermute | solution.py:324
  18.9 5.0 %collective-permute-start.9 = (bf16[192,256]{1,0:T(8,128)(2,1)S(1)}, bf16[192,256]{1,0:T(8,128)(2,1)S(1)}, u32[]{:S(2)}, u32[]{:S(2)}) collective-permute-start(bf16[192,256]{1,0:T(8,128)(2,1)S(1)} %get-tuple-element.29), channel_id=1, source_target_pairs={{0,8},{8,0},{16,24},{24,16},{1,9},{9,1},{17,25},{25,17},{2,10},{10... | collective-permute-start | bytes 294920 | tf_op jit(solution)/shard_map/ppermute | solution.py:324
  24.5 5.7 %collective-permute-start.10 = (bf16[128,256]{1,0:T(8,128)(2,1)S(1)}, bf16[128,256]{1,0:T(8,128)(2,1)S(1)}, u32[]{:S(2)}, u32[]{:S(2)}) collective-permute-start(bf16[128,256]{1,0:T(8,128)(2,1)S(1)} %get-tuple-element.31), channel_id=1, source_target_pairs={{0,24},{8,16},{16,8},{24,0},{1,25},{9,17},{17,9},{25,1},{2,26},{10... | collective-permute-start | bytes 196616 | tf_op jit(solution)/shard_map/ppermute | solution.py:324
  26.3 4.5 %collective-permute-start.11 = (bf16[128,256]{1,0:T(8,128)(2,1)S(1)}, bf16[128,256]{1,0:T(8,128)(2,1)S(1)}, u32[]{:S(2)}, u32[]{:S(2)}) collective-permute-start(bf16[128,256]{1,0:T(8,128)(2,1)S(1)} %get-tuple-element.32), channel_id=1, source_target_pairs={{0,16},{8,24},{16,0},{24,8},{1,17},{9,25},{17,1},{25,9},{2,18},{10... | collective-permute-start | bytes 196616 | tf_op jit(solution)/shard_map/ppermute | solution.py:324
  27.6 4.3 %collective-permute-start.12 = (bf16[128,256]{1,0:T(8,128)(2,1)S(1)}, bf16[128,256]{1,0:T(8,128)(2,1)S(1)}, u32[]{:S(2)}, u32[]{:S(2)}) collective-permute-start(bf16[128,256]{1,0:T(8,128)(2,1)S(1)} %get-tuple-element.33), channel_id=1, source_target_pairs={{0,8},{8,0},{16,24},{24,16},{1,9},{9,1},{17,25},{25,17},{2,10},{10... | collective-permute-start | bytes 196616 | tf_op jit(solution)/shard_map/ppermute | solution.py:324
  32.5 1.7 %collective-permute-start.13 = (bf16[3,64,512]{2,1,0:T(8,128)(2,1)S(1)}, bf16[3,64,512]{2,1,0:T(8,128)(2,1)S(1)}, u32[]{:S(2)}, u32[]{:S(2)}) collective-permute-start(bf16[3,64,512]{2,1,0:T(8,128)(2,1)S(1)} %get-tuple-element.36.refs_0_), channel_id=1, source_target_pairs={{0,1},{1,0},{2,3},{3,2},{4,5},{5,4},{6,7},{7,6},{8,9},{9,8},{10,11... | collective-permute-start | bytes 589832 | tf_op jit(solution)/shard_map/ppermute | solution.py:324
  33.0 12.3 %collective-permute-start.18 = (bf16[1,64,512]{2,1,0:T(8,128)(2,1)S(1)}, bf16[1,64,512]{2,1,0:T(8,128)(2,1)S(1)}, u32[]{:S(2)}, u32[]{:S(2)}) collective-permute-start(bf16[1,64,512]{2,1,0:T(8,128)(2,1)S(1)} %shard_map.60.refs_0_), channel_id=1, source_target_pairs={{0,1},{1,0},{2,3},{3,2},{4,5},{5,4},{6,7},{7,6},{8,9},{9,8},{10,11... | collective-permute-start | bytes 196616 | tf_op jit(solution)/shard_map/ppermute | solution.py:324
  34.2 11.2 %collective-permute-start.14 = (bf16[64,512]{1,0:T(8,128)(2,1)S(1)}, bf16[64,512]{1,0:T(8,128)(2,1)S(1)}, u32[]{:S(2)}, u32[]{:S(2)}) collective-permute-start(bf16[64,512]{1,0:T(8,128)(2,1)S(1)} %get-tuple-element.37), channel_id=1, source_target_pairs={{0,2},{1,3},{2,4},{3,5},{4,6},{5,7},{6,0},{7,1},{8,10},{9,11},{10,... | collective-permute-start | bytes 196616 | tf_op jit(solution)/shard_map/ppermute | solution.py:341
  35.8 9.6 %collective-permute-start.16 = (bf16[64,512]{1,0:T(8,128)(2,1)S(1)}, bf16[64,512]{1,0:T(8,128)(2,1)S(1)}, u32[]{:S(2)}, u32[]{:S(2)}) collective-permute-start(bf16[64,512]{1,0:T(8,128)(2,1)S(1)} %get-tuple-element.38), channel_id=1, source_target_pairs={{2,6},{3,7},{4,0},{5,1},{10,14},{11,15},{12,8},{13,9},{18,22},{19,... | collective-permute-start | bytes 196616 | tf_op jit(solution)/shard_map/ppermute | solution.py:341
  37.1 8.3 %collective-permute-start.15 = (bf16[64,512]{1,0:T(8,128)(2,1)S(1)}, bf16[64,512]{1,0:T(8,128)(2,1)S(1)}, u32[]{:S(2)}, u32[]{:S(2)}) collective-permute-start(bf16[64,512]{1,0:T(8,128)(2,1)S(1)} %get-tuple-element.38), channel_id=1, source_target_pairs={{0,4},{1,5},{6,2},{7,3},{8,12},{9,13},{14,10},{15,11},{16,20},{17,... | collective-permute-start | bytes 196616 | tf_op jit(solution)/shard_map/ppermute | solution.py:341
  42.6 4.3 %collective-permute-start.17 = (bf16[64,512]{1,0:T(8,128)(2,1)S(1)}, bf16[64,512]{1,0:T(8,128)(2,1)S(1)}, u32[]{:S(2)}, u32[]{:S(2)}) collective-permute-start(bf16[64,512]{1,0:T(8,128)(2,1)S(1)} %get-tuple-element.39.refs_0_), channel_id=1, source_target_pairs={{0,6},{1,7},{2,0},{3,1},{4,2},{5,3},{6,4},{7,5},{8,14},{9,15},{10,... | collective-permute-start | bytes 196616 | tf_op jit(solution)/shard_map/ppermute | solution.py:341

commit v23 on v18

--- a/solution.py
+++ b/solution.py
@@ -181,8 +181,12 @@
         outs[s][size:] = jnp.concatenate(pieces, axis=0).astype(BF16)
 
 
+def own_first(refs):
+    return [refs[-1], *refs[:-1]]
+
+
 def transform_kernel(shares, total, share, *refs):
-    tiles, (fwd_ref, bwd_ref) = refs[:shares][::-1], refs[shares : shares + 2]
+    tiles, (fwd_ref, bwd_ref) = own_first(refs[:shares]), refs[shares : shares + 2]
     outs, (gathered, weight, wide) = refs[shares + 2 : 2 * shares + 2], refs[2 * shares + 2 :]
     local_k = total // shares
     size = 2 * local_k * share
@@ -262,7 +266,7 @@
 
 
 def first_weight_kernel(shares, offsets, out_rows, *refs):
-    pieces, (orb_ref, rest_ref, out_ref, right_ref, gathered) = refs[:shares][::-1], refs[shares:]
+    pieces, (orb_ref, rest_ref, out_ref, right_ref, gathered) = own_first(refs[:shares]), refs[shares:]
     weight_operands(pieces, right_ref, gathered)
     weight_rows(offsets, 1, out_rows, right_ref, orb_ref, rest_ref, out_ref)
 
@@ -325,7 +329,7 @@
 
 
 def trade(pieces, axis, step):
-    return [swap(pieces[s], axis, s * step) for s in reversed(range(1, len(pieces)))] + [pieces[0]]
+    return [swap(pieces[s], axis, s * step) for s in range(1, len(pieces))] + [pieces[0]]
 
 
 def shift_along(pieces):

time: 44.8 us -> 45.1 us (level)
  no operation moved by 1% of the time
where the time goes in v23:
time: 45.1 us; the launch traced here: 44.9 us
  starting transfers between devices  18.5 us (41%)
  waiting for transfers between devices  16.3 us (36%)
  Pallas kernels  9.87 us (22%)
    ppermute x15, starting transfers between devices, swap(): return lax.ppermute(value, axis, [(i, i ^ mask) for i in range(size)])  13.6 us
    ppermute x15, waiting for transfers between devices, swap(): return lax.ppermute(value, axis, [(i, i ^ mask) for i in range(size)])  13 us
    ppermute x3, starting transfers between devices, shift_along(): came.append(lax.ppermute(pieces[s], 'pts', pairs))  4.94 us
    ppermute x3, waiting for transfers between devices, shift_along(): came.append(lax.ppermute(pieces[s], 'pts', pairs))  3.32 us
    pallas_call x1, Pallas kernels, body(): call(functools.partial(edge_kernel, per_block), [shape((local_k * 2 * per...  2.5 us
    pallas_call x1, Pallas kernels, body(): call(functools.partial(exchange_kernel, chunks, 1.0 / math.sqrt(points *...  1.66 us
    pallas_call x1, Pallas kernels, body(): call(rest_kernel, [shape(edge.shape, BF16), shape((local_k, 2, norb, poin...  1.58 us
    pallas_call x3, Pallas kernels, rows_of(): call(functools.partial(next_weight_kernel, offsets, flip, out_rows), shap...  1.51 us
  transfers between devices with their start and end apart: 18, of which 13 were waited for; matrix products, arithmetic and copies ran while one was open for 0% of the time, Pallas kernels for 7%

profile of v23, /device:TPU:0, one launch (start us, length us, event | category | flops | bytes accessed | tf_op | source)
XLA Modules:
  0.0 44.9 jit_solution(3137264391718211474)
XLA Ops:
  0.0 2.5 %shard_map.55 = (bf16[64,512]{1,0:T(8,128)(2,1)S(1)}, bf16[8,2,512,128]{3,2,1,0:T(8,128)(2,1)S(1)}) custom-call(bf16[8,2,512,256]{3,2,1,0:T(8,128)(2,1)} %orb_hbm.3), custom_call_target="tpu_custom_call" | custom-call | bytes 4194304 | tf_op jit(solution)/shard_map/pallas_call | solution.py:356
  2.5 5.1 %collective-permute-start.5 = (bf16[64,512]{1,0:T(8,128)(2,1)S(1)}, bf16[64,512]{1,0:T(8,128)(2,1)S(1)}, u32[]{:S(2)}, u32[]{:S(2)}) collective-permute-start(bf16[64,512]{1,0:T(8,128)(2,1)S(1)} %get-tuple-element.23.edge_hbm.refs_0_), channel_id=1, source_target_pairs={{0,6},{1,7},{2,4},{3,5},{4,2},{5,3},{6,0},{7,1},{8,14},{9,15},{10,... | collective-permute-start | bytes 196616 | tf_op jit(solution)/shard_map/ppermute | solution.py:328
  7.7 0.6 %collective-permute-start.1 = (bf16[64,512]{1,0:T(8,128)(2,1)S(1)}, bf16[64,512]{1,0:T(8,128)(2,1)S(1)}, u32[]{:S(2)}, u32[]{:S(2)}) collective-permute-start(bf16[64,512]{1,0:T(8,128)(2,1)S(1)} %get-tuple-element.23.edge_hbm.refs_0_), channel_id=1, source_target_pairs={{0,4},{1,5},{2,6},{3,7},{4,0},{5,1},{6,2},{7,3},{8,12},{9,13},{10,... | collective-permute-start | bytes 196616 | tf_op jit(solution)/shard_map/ppermute | solution.py:328
  8.3 1.6 %shard_map.56 = (bf16[64,512]{1,0:T(8,128)(2,1)S(1)}, bf16[8,2,512,128]{3,2,1,0:T(8,128)(2,1)S(1)}) custom-call(bf16[8,2,512,256]{3,2,1,0:T(8,128)(2,1)} %orb_hbm.3, bf16[64,512]{1,0:T(8,128)(2,1)S(1)} %get-tuple-element.23.edge_hbm.refs_0_), custom_call_target="tpu_custom_call" | custom-call | bytes 4194304 | tf_op jit(solution)/shard_map/pallas_call | solution.py:368
  10.0 0.6 %collective-permute-done.5.refs_6_ = bf16[64,512]{1,0:T(8,128)(2,1)S(1)} collective-permute-done((bf16[64,512]{1,0:T(8,128)(2,1)S(1)}, bf16[64,512]{1,0:T(8,128)(2,1)S(1)}, u32[]{:S(2)}, u32[]{:S(2)}) %collective-permute-start.5) | collective-permute-done | bytes 65568 | tf_op jit(solution)/shard_map/ppermute | solution.py:328
  10.6 1.8 %collective-permute-done.3.refs_4_ = bf16[64,512]{1,0:T(8,128)(2,1)S(1)} collective-permute-done((bf16[64,512]{1,0:T(8,128)(2,1)S(1)}, bf16[64,512]{1,0:T(8,128)(2,1)S(1)}, u32[]{:S(2)}, u32[]{:S(2)}) %collective-permute-start.3) | collective-permute-done | bytes 65568 | tf_op jit(solution)/shard_map/ppermute | solution.py:328
  12.3 1.0 %collective-permute-done.1.refs_2_ = bf16[64,512]{1,0:T(8,128)(2,1)S(1)} collective-permute-done((bf16[64,512]{1,0:T(8,128)(2,1)S(1)}, bf16[64,512]{1,0:T(8,128)(2,1)S(1)}, u32[]{:S(2)}, u32[]{:S(2)}) %collective-permute-start.1) | collective-permute-done | bytes 65568 | tf_op jit(solution)/shard_map/ppermute | solution.py:328
  13.6 1.0 %collective-permute-done.2.refs_3_ = bf16[64,512]{1,0:T(8,128)(2,1)S(1)} collective-permute-done((bf16[64,512]{1,0:T(8,128)(2,1)S(1)}, bf16[64,512]{1,0:T(8,128)(2,1)S(1)}, u32[]{:S(2)}, u32[]{:S(2)}) %collective-permute-start.2) | collective-permute-done | bytes 65568 | tf_op jit(solution)/shard_map/ppermute | solution.py:328
  14.6 1.4 %shard_map.57 = (bf16[192,256]{1,0:T(8,128)(2,1)S(1)}, bf16[192,256]{1,0:T(8,128)(2,1)S(1)}, bf16[192,256]{1,0:T(8,128)(2,1)S(1)}, bf16[192,256]{1,0:T(8,128)(2,1)S(1)}, bf16[4,8,16,1024]{3,2,1,0:T(8,128)(2,1)S(1)}) custom-call(bf16[64,512]{1,0:T(8,128)(2,1)S(1)} %get-tuple-element.23.edge_hbm.refs_0_, bf16[64,512]{1,0:T(8,128)(2,1)S(1)} %collective-permute-done.refs_1_, ...), custom_call_target="tpu_custom_call" | custom-call | bytes 6291456 | tf_op jit(solution)/shard_map/pallas_call | solution.py:392
  15.9 1.6 %collective-permute-start.7 = (bf16[192,256]{1,0:T(8,128)(2,1)S(1)}, bf16[192,256]{1,0:T(8,128)(2,1)S(1)}, u32[]{:S(2)}, u32[]{:S(2)}) collective-permute-start(bf16[192,256]{1,0:T(8,128)(2,1)S(1)} %get-tuple-element.27), channel_id=1, source_target_pairs={{0,8},{8,0},{16,24},{24,16},{1,9},{9,1},{17,25},{25,17},{2,10},{10... | collective-permute-start | bytes 294920 | tf_op jit(solution)/shard_map/ppermute | solution.py:328
  17.5 1.5 %collective-permute-start.8 = (bf16[192,256]{1,0:T(8,128)(2,1)S(1)}, bf16[192,256]{1,0:T(8,128)(2,1)S(1)}, u32[]{:S(2)}, u32[]{:S(2)}) collective-permute-start(bf16[192,256]{1,0:T(8,128)(2,1)S(1)} %get-tuple-element.28), channel_id=1, source_target_pairs={{0,16},{8,24},{16,0},{24,8},{1,17},{9,25},{17,1},{25,9},{2,18},{10... | collective-permute-start | bytes 294920 | tf_op jit(solution)/shard_map/ppermute | solution.py:328
  19.0 0.5 %collective-permute-start.9 = (bf16[192,256]{1,0:T(8,128)(2,1)S(1)}, bf16[192,256]{1,0:T(8,128)(2,1)S(1)}, u32[]{:S(2)}, u32[]{:S(2)}) collective-permute-start(bf16[192,256]{1,0:T(8,128)(2,1)S(1)} %get-tuple-element.29), channel_id=1, source_target_pairs={{0,24},{8,16},{16,8},{24,0},{1,25},{9,17},{17,9},{25,1},{2,26},{10... | collective-permute-start | bytes 294920 | tf_op jit(solution)/shard_map/ppermute | solution.py:328
  19.5 1.4 %collective-permute-done.7.refs_0_ = bf16[192,256]{1,0:T(8,128)(2,1)S(1)} collective-permute-done((bf16[192,256]{1,0:T(8,128)(2,1)S(1)}, bf16[192,256]{1,0:T(8,128)(2,1)S(1)}, u32[]{:S(2)}, u32[]{:S(2)}) %collective-permute-start.7) | collective-permute-done | bytes 98336 | tf_op jit(solution)/shard_map/ppermute | solution.py:328
  20.8 2.4 %collective-permute-done.8.refs_1_ = bf16[192,256]{1,0:T(8,128)(2,1)S(1)} collective-permute-done((bf16[192,256]{1,0:T(8,128)(2,1)S(1)}, bf16[192,256]{1,0:T(8,128)(2,1)S(1)}, u32[]{:S(2)}, u32[]{:S(2)}) %collective-permute-start.8) | collective-permute-done | bytes 98336 | tf_op jit(solution)/shard_map/ppermute | solution.py:328
  23.3 1.3 %collective-permute-done.9.refs_2_ = bf16[192,256]{1,0:T(8,128)(2,1)S(1)} collective-permute-done((bf16[192,256]{1,0:T(8,128)(2,1)S(1)}, bf16[192,256]{1,0:T(8,128)(2,1)S(1)}, u32[]{:S(2)}, u32[]{:S(2)}) %collective-permute-start.9) | collective-permute-done | bytes 98336 | tf_op jit(solution)/shard_map/ppermute | solution.py:328
  24.5 0.6 %shard_map.58 = (bf16[128,256]{1,0:T(8,128)(2,1)S(1)}, bf16[128,256]{1,0:T(8,128)(2,1)S(1)}, bf16[128,256]{1,0:T(8,128)(2,1)S(1)}, bf16[128,256]{1,0:T(8,128)(2,1)S(1)}) custom-call(bf16[192,256]{1,0:T(8,128)(2,1)S(1)} %collective-permute-done.7.refs_0_, bf16[192,256]{1,0:T(8,128)(2,1)S(1)} %collective-permute-done.8.refs_1_, ...), custom_call_target="tpu_custom_call" | custom-call | bytes 2097152 | tf_op jit(solution)/shard_map/pallas_call | solution.py:405
  25.1 0.9 %collective-permute-start.10 = (bf16[128,256]{1,0:T(8,128)(2,1)S(1)}, bf16[128,256]{1,0:T(8,128)(2,1)S(1)}, u32[]{:S(2)}, u32[]{:S(2)}) collective-permute-start(bf16[128,256]{1,0:T(8,128)(2,1)S(1)} %get-tuple-element.31), channel_id=1, source_target_pairs={{0,8},{8,0},{16,24},{24,16},{1,9},{9,1},{17,25},{25,17},{2,10},{10... | collective-permute-start | bytes 196616 | tf_op jit(solution)/shard_map/ppermute | solution.py:328
  26.1 0.9 %collective-permute-start.11 = (bf16[128,256]{1,0:T(8,128)(2,1)S(1)}, bf16[128,256]{1,0:T(8,128)(2,1)S(1)}, u32[]{:S(2)}, u32[]{:S(2)}) collective-permute-start(bf16[128,256]{1,0:T(8,128)(2,1)S(1)} %get-tuple-element.32), channel_id=1, source_target_pairs={{0,16},{8,24},{16,0},{24,8},{1,17},{9,25},{17,1},{25,9},{2,18},{10... | collective-permute-start | bytes 196616 | tf_op jit(solution)/shard_map/ppermute | solution.py:328
  26.9 1.7 %collective-permute-start.12 = (bf16[128,256]{1,0:T(8,128)(2,1)S(1)}, bf16[128,256]{1,0:T(8,128)(2,1)S(1)}, u32[]{:S(2)}, u32[]{:S(2)}) collective-permute-start(bf16[128,256]{1,0:T(8,128)(2,1)S(1)} %get-tuple-element.33), channel_id=1, source_target_pairs={{0,24},{8,16},{16,8},{24,0},{1,25},{9,17},{17,9},{25,1},{2,26},{10... | collective-permute-start | bytes 196616 | tf_op jit(solution)/shard_map/ppermute | solution.py:328
  28.7 1.3 %collective-permute-done.10.refs_0_ = bf16[128,256]{1,0:T(8,128)(2,1)S(1)} collective-permute-done((bf16[128,256]{1,0:T(8,128)(2,1)S(1)}, bf16[128,256]{1,0:T(8,128)(2,1)S(1)}, u32[]{:S(2)}, u32[]{:S(2)}) %collective-permute-start.10) | collective-permute-done | bytes 65568 | tf_op jit(solution)/shard_map/ppermute | solution.py:328
  30.0 0.5 %collective-permute-done.11.refs_1_ = bf16[128,256]{1,0:T(8,128)(2,1)S(1)} collective-permute-done((bf16[128,256]{1,0:T(8,128)(2,1)S(1)}, bf16[128,256]{1,0:T(8,128)(2,1)S(1)}, u32[]{:S(2)}, u32[]{:S(2)}) %collective-permute-start.11) | collective-permute-done | bytes 65568 | tf_op jit(solution)/shard_map/ppermute | solution.py:328
  30.4 1.6 %collective-permute-done.12.refs_2_ = bf16[128,256]{1,0:T(8,128)(2,1)S(1)} collective-permute-done((bf16[128,256]{1,0:T(8,128)(2,1)S(1)}, bf16[128,256]{1,0:T(8,128)(2,1)S(1)}, u32[]{:S(2)}, u32[]{:S(2)}) %collective-permute-start.12) | collective-permute-done | bytes 65568 | tf_op jit(solution)/shard_map/ppermute | solution.py:328
  32.1 0.6 %shard_map.59 = (bf16[3,64,512]{2,1,0:T(8,128)(2,1)S(1)}, bf16[4,128,1024]{2,1,0:T(8,128)(2,1)S(1)}) custom-call(bf16[128,256]{1,0:T(8,128)(2,1)S(1)} %collective-permute-done.10.refs_0_, bf16[128,256]{1,0:T(8,128)(2,1)S(1)} %collective-permute-done.11.refs_1_, bf16[128,256]{1,0:T(8,128)(2,1)S(1)} %collective-permute-done.12.refs_2_, ...), custom_call_target="tpu_custom_call" | custom-call | tf_op jit(solution)/shard_map/pallas_call | solution.py:421
  32.8 0.5 %shard_map.60.refs_0_ = bf16[1,64,512]{2,1,0:T(8,128)(2,1)S(1)} custom-call(bf16[4,128,1024]{2,1,0:T(8,128)(2,1)S(1)} %get-tuple-element.35.right_ref, bf16[8,2,512,128]{3,2,1,0:T(8,128)(2,1)S(1)} %get-tuple-element.25.refs_8_.refs_4_.orb_ref, bf16[8,2,512,128]{3,2,1,0:T(8,128)(2,1)S(1)} %get-tuple-element.26.refs_9_.refs_5_.rest_ref, ...), custom_call_target="tpu_custom_call" | custom-call | tf_op jit(solution)/shard_map/pallas_call | solution.py:432
  33.3 0.6 %collective-permute-start.17 = (bf16[1,64,512]{2,1,0:T(8,128)(2,1)S(1)}, bf16[1,64,512]{2,1,0:T(8,128)(2,1)S(1)}, u32[]{:S(2)}, u32[]{:S(2)}) collective-permute-start(bf16[1,64,512]{2,1,0:T(8,128)(2,1)S(1)} %shard_map.60.refs_0_), channel_id=1, source_target_pairs={{0,1},{1,0},{2,3},{3,2},{4,5},{5,4},{6,7},{7,6},{8,9},{9,8},{10,11... | collective-permute-start | bytes 196616 | tf_op jit(solution)/shard_map/ppermute | solution.py:328
  33.8 0.6 %shard_map.61.keep_ref = f32[3,64,512]{2,1,0:T(8,128)S(1)} custom-call(bf16[4,128,1024]{2,1,0:T(8,128)(2,1)S(1)} %get-tuple-element.35.right_ref, bf16[8,2,512,128]{3,2,1,0:T(8,128)(2,1)S(1)} %get-tuple-element.25.refs_8_.refs_4_.orb_ref, bf16[8,2,512,128]{3,2,1,0:T(8,128)(2,1)S(1)} %get-tuple-element.26.refs_9_.refs_5_.rest_ref, ...), custom_call_target="tpu_custom_call" | custom-call | tf_op jit(solution)/shard_map/pallas_call | solution.py:432
  34.5 1.6 %collective-permute-start.14 = (bf16[64,512]{1,0:T(8,128)(2,1)S(1)}, bf16[64,512]{1,0:T(8,128)(2,1)S(1)}, u32[]{:S(2)}, u32[]{:S(2)}) collective-permute-start(bf16[64,512]{1,0:T(8,128)(2,1)S(1)} %get-tuple-element.37), channel_id=1, source_target_pairs={{0,2},{1,3},{2,4},{3,5},{4,6},{5,7},{6,0},{7,1},{8,10},{9,11},{10,... | collective-permute-start | bytes 196616 | tf_op jit(solution)/shard_map/ppermute | solution.py:340
  36.1 1.2 %collective-permute-start.15 = (bf16[64,512]{1,0:T(8,128)(2,1)S(1)}, bf16[64,512]{1,0:T(8,128)(2,1)S(1)}, u32[]{:S(2)}, u32[]{:S(2)}) collective-permute-start(bf16[64,512]{1,0:T(8,128)(2,1)S(1)} %get-tuple-element.38), channel_id=1, source_target_pairs={{0,4},{1,5},{2,6},{3,7},{4,0},{5,1},{6,2},{7,3},{8,12},{9,13},{10,... | collective-permute-start | bytes 196616 | tf_op jit(solution)/shard_map/ppermute | solution.py:340
  37.3 2.2 %collective-permute-start.16 = (bf16[64,512]{1,0:T(8,128)(2,1)S(1)}, bf16[64,512]{1,0:T(8,128)(2,1)S(1)}, u32[]{:S(2)}, u32[]{:S(2)}) collective-permute-start(bf16[64,512]{1,0:T(8,128)(2,1)S(1)} %get-tuple-element.39.refs_0_), channel_id=1, source_target_pairs={{0,6},{1,7},{2,0},{3,1},{4,2},{5,3},{6,4},{7,5},{8,14},{9,15},{10,... | collective-permute-start | bytes 196616 | tf_op jit(solution)/shard_map/ppermute | solution.py:340
  39.9 1.4 %collective-permute-done.14.refs_0_ = bf16[64,512]{1,0:T(8,128)(2,1)S(1)} collective-permute-done((bf16[64,512]{1,0:T(8,128)(2,1)S(1)}, bf16[64,512]{1,0:T(8,128)(2,1)S(1)}, u32[]{:S(2)}, u32[]{:S(2)}) %collective-permute-start.14) | collective-permute-done | bytes 65568 | tf_op jit(solution)/shard_map/ppermute | solution.py:340
  41.3 1.9 %collective-permute-done.15.refs_1_ = bf16[64,512]{1,0:T(8,128)(2,1)S(1)} collective-permute-done((bf16[64,512]{1,0:T(8,128)(2,1)S(1)}, bf16[64,512]{1,0:T(8,128)(2,1)S(1)}, u32[]{:S(2)}, u32[]{:S(2)}) %collective-permute-start.15) | collective-permute-done | bytes 65568 | tf_op jit(solution)/shard_map/ppermute | solution.py:340
  43.2 1.7 %shard_map.65 = bf16[64,4,16,128]{3,2,1,0:T(8,128)(2,1)} custom-call(bf16[64,512]{1,0:T(8,128)(2,1)S(1)} %collective-permute-done.14.refs_0_, bf16[64,512]{1,0:T(8,128)(2,1)S(1)} %collective-permute-done.15.refs_1_, bf16[64,512]{1,0:T(8,128)(2,1)S(1)} %collective-permute-done.16.refs_2_, f32[64,512]{1,0:T(8,128)S(1)} %shard_map.64.refs_3_, ...), custom_call_target="tpu_custom_call" | custom-call | bytes 4194304 | tf_op jit(solution)/shard_map/pallas_call | solution.py:450
  (23 shorter events, 1.0 us)
Async XLA Ops:
  2.5 12.0 %copy-start = (bf16[8,32,256]{2,1,0:T(8,128)(2,1)S(1)}, bf16[8,32,256]{2,1,0:T(8,128)(2,1)}, u32[]{:S(2)}) copy-start(bf16[8,32,256]{2,1,0:T(8,128)(2,1)} %refs_11_.1) | copy-start | bytes 393220
  2.5 12.0 %copy-start.1 = (bf16[2,256,128]{2,1,0:T(8,128)(2,1)S(1)}, bf16[2,256,128]{2,1,0:T(8,128)(2,1)}, u32[]{:S(2)}) copy-start(bf16[2,256,128]{2,1,0:T(8,128)(2,1)} %constant.6.clone.refs_10_) | copy-start | bytes 393220
  2.5 8.0 %collective-permute-start.5 = (bf16[64,512]{1,0:T(8,128)(2,1)S(1)}, bf16[64,512]{1,0:T(8,128)(2,1)S(1)}, u32[]{:S(2)}, u32[]{:S(2)}) collective-permute-start(bf16[64,512]{1,0:T(8,128)(2,1)S(1)} %get-tuple-element.23.edge_hbm.refs_0_), channel_id=1, source_target_pairs={{0,6},{1,7},{2,4},{3,5},{4,2},{5,3},{6,0},{7,1},{8,14},{9,15},{10,... | collective-permute-start | bytes 196616 | tf_op jit(solution)/shard_map/ppermute | solution.py:328
  7.6 4.7 %collective-permute-start.3 = (bf16[64,512]{1,0:T(8,128)(2,1)S(1)}, bf16[64,512]{1,0:T(8,128)(2,1)S(1)}, u32[]{:S(2)}, u32[]{:S(2)}) collective-permute-start(bf16[64,512]{1,0:T(8,128)(2,1)S(1)} %get-tuple-element.23.edge_hbm.refs_0_), channel_id=1, source_target_pairs={{0,2},{1,3},{2,0},{3,1},{4,6},{5,7},{6,4},{7,5},{8,10},{9,11},{10,... | collective-permute-start | bytes 196616 | tf_op jit(solution)/shard_map/ppermute | solution.py:328
  7.7 5.6 %collective-permute-start.1 = (bf16[64,512]{1,0:T(8,128)(2,1)S(1)}, bf16[64,512]{1,0:T(8,128)(2,1)S(1)}, u32[]{:S(2)}, u32[]{:S(2)}) collective-permute-start(bf16[64,512]{1,0:T(8,128)(2,1)S(1)} %get-tuple-element.23.edge_hbm.refs_0_), channel_id=1, source_target_pairs={{0,4},{1,5},{2,6},{3,7},{4,0},{5,1},{6,2},{7,3},{8,12},{9,13},{10,... | collective-permute-start | bytes 196616 | tf_op jit(solution)/shard_map/ppermute | solution.py:328
  9.9 3.4 %collective-permute-start = (bf16[64,512]{1,0:T(8,128)(2,1)S(1)}, bf16[64,512]{1,0:T(8,128)(2,1)S(1)}, u32[]{:S(2)}, u32[]{:S(2)}) collective-permute-start(bf16[64,512]{1,0:T(8,128)(2,1)S(1)} %get-tuple-element.24), channel_id=1, source_target_pairs={{0,1},{1,0},{2,3},{3,2},{4,5},{5,4},{6,7},{7,6},{8,9},{9,8},{10,11... | collective-permute-start | bytes 196616 | tf_op jit(solution)/shard_map/ppermute | solution.py:328
  10.5 2.7 %collective-permute-start.6 = (bf16[64,512]{1,0:T(8,128)(2,1)S(1)}, bf16[64,512]{1,0:T(8,128)(2,1)S(1)}, u32[]{:S(2)}, u32[]{:S(2)}) collective-permute-start(bf16[64,512]{1,0:T(8,128)(2,1)S(1)} %collective-permute-done.5.refs_6_), channel_id=1, source_target_pairs={{0,1},{1,0},{2,3},{3,2},{4,5},{5,4},{6,7},{7,6},{8,9},{9,8},{10,11... | collective-permute-start | bytes 196616 | tf_op jit(solution)/shard_map/ppermute | solution.py:328
  12.3 1.3 %collective-permute-start.4 = (bf16[64,512]{1,0:T(8,128)(2,1)S(1)}, bf16[64,512]{1,0:T(8,128)(2,1)S(1)}, u32[]{:S(2)}, u32[]{:S(2)}) collective-permute-start(bf16[64,512]{1,0:T(8,128)(2,1)S(1)} %collective-permute-done.3.refs_4_), channel_id=1, source_target_pairs={{0,1},{1,0},{2,3},{3,2},{4,5},{5,4},{6,7},{7,6},{8,9},{9,8},{10,11... | collective-permute-start | bytes 196616 | tf_op jit(solution)/shard_map/ppermute | solution.py:328
  13.3 1.3 %collective-permute-start.2 = (bf16[64,512]{1,0:T(8,128)(2,1)S(1)}, bf16[64,512]{1,0:T(8,128)(2,1)S(1)}, u32[]{:S(2)}, u32[]{:S(2)}) collective-permute-start(bf16[64,512]{1,0:T(8,128)(2,1)S(1)} %collective-permute-done.1.refs_2_), channel_id=1, source_target_pairs={{0,1},{1,0},{2,3},{3,2},{4,5},{5,4},{6,7},{7,6},{8,9},{9,8},{10,11... | collective-permute-start | bytes 196616 | tf_op jit(solution)/shard_map/ppermute | solution.py:328
  14.5 10.0 %copy-start.2 = (bf16[64,128]{1,0:T(8,128)(2,1)S(1)}, bf16[64,128]{1,0:T(8,128)(2,1)}, u32[]{:S(2)}) copy-start(bf16[64,128]{1,0:T(8,128)(2,1)} %constant.8.clone.refs_5_) | copy-start | bytes 49156
  14.5 10.0 %copy-start.3 = (bf16[64,128]{1,0:T(8,128)(2,1)S(1)}, bf16[64,128]{1,0:T(8,128)(2,1)}, u32[]{:S(2)}) copy-start(bf16[64,128]{1,0:T(8,128)(2,1)} %constant.7.clone.refs_4_) | copy-start | bytes 49156
  15.9 4.9 %collective-permute-start.7 = (bf16[192,256]{1,0:T(8,128)(2,1)S(1)}, bf16[192,256]{1,0:T(8,128)(2,1)S(1)}, u32[]{:S(2)}, u32[]{:S(2)}) collective-permute-start(bf16[192,256]{1,0:T(8,128)(2,1)S(1)} %get-tuple-element.27), channel_id=1, source_target_pairs={{0,8},{8,0},{16,24},{24,16},{1,9},{9,1},{17,25},{25,17},{2,10},{10... | collective-permute-start | bytes 294920 | tf_op jit(solution)/shard_map/ppermute | solution.py:328
  17.5 5.8 %collective-permute-start.8 = (bf16[192,256]{1,0:T(8,128)(2,1)S(1)}, bf16[192,256]{1,0:T(8,128)(2,1)S(1)}, u32[]{:S(2)}, u32[]{:S(2)}) collective-permute-start(bf16[192,256]{1,0:T(8,128)(2,1)S(1)} %get-tuple-element.28), channel_id=1, source_target_pairs={{0,16},{8,24},{16,0},{24,8},{1,17},{9,25},{17,1},{25,9},{2,18},{10... | collective-permute-start | bytes 294920 | tf_op jit(solution)/shard_map/ppermute | solution.py:328
  19.0 5.5 %collective-permute-start.9 = (bf16[192,256]{1,0:T(8,128)(2,1)S(1)}, bf16[192,256]{1,0:T(8,128)(2,1)S(1)}, u32[]{:S(2)}, u32[]{:S(2)}) collective-permute-start(bf16[192,256]{1,0:T(8,128)(2,1)S(1)} %get-tuple-element.29), channel_id=1, source_target_pairs={{0,24},{8,16},{16,8},{24,0},{1,25},{9,17},{17,9},{25,1},{2,26},{10... | collective-permute-start | bytes 294920 | tf_op jit(solution)/shard_map/ppermute | solution.py:328
  25.1 4.8 %collective-permute-start.10 = (bf16[128,256]{1,0:T(8,128)(2,1)S(1)}, bf16[128,256]{1,0:T(8,128)(2,1)S(1)}, u32[]{:S(2)}, u32[]{:S(2)}) collective-permute-start(bf16[128,256]{1,0:T(8,128)(2,1)S(1)} %get-tuple-element.31), channel_id=1, source_target_pairs={{0,8},{8,0},{16,24},{24,16},{1,9},{9,1},{17,25},{25,17},{2,10},{10... | collective-permute-start | bytes 196616 | tf_op jit(solution)/shard_map/ppermute | solution.py:328
  26.1 4.4 %collective-permute-start.11 = (bf16[128,256]{1,0:T(8,128)(2,1)S(1)}, bf16[128,256]{1,0:T(8,128)(2,1)S(1)}, u32[]{:S(2)}, u32[]{:S(2)}) collective-permute-start(bf16[128,256]{1,0:T(8,128)(2,1)S(1)} %get-tuple-element.32), channel_id=1, source_target_pairs={{0,16},{8,24},{16,0},{24,8},{1,17},{9,25},{17,1},{25,9},{2,18},{10... | collective-permute-start | bytes 196616 | tf_op jit(solution)/shard_map/ppermute | solution.py:328
  26.9 5.2 %collective-permute-start.12 = (bf16[128,256]{1,0:T(8,128)(2,1)S(1)}, bf16[128,256]{1,0:T(8,128)(2,1)S(1)}, u32[]{:S(2)}, u32[]{:S(2)}) collective-permute-start(bf16[128,256]{1,0:T(8,128)(2,1)S(1)} %get-tuple-element.33), channel_id=1, source_target_pairs={{0,24},{8,16},{16,8},{24,0},{1,25},{9,17},{17,9},{25,1},{2,26},{10... | collective-permute-start | bytes 196616 | tf_op jit(solution)/shard_map/ppermute | solution.py:328
  32.7 1.7 %collective-permute-start.13 = (bf16[3,64,512]{2,1,0:T(8,128)(2,1)S(1)}, bf16[3,64,512]{2,1,0:T(8,128)(2,1)S(1)}, u32[]{:S(2)}, u32[]{:S(2)}) collective-permute-start(bf16[3,64,512]{2,1,0:T(8,128)(2,1)S(1)} %get-tuple-element.36.refs_0_), channel_id=1, source_target_pairs={{0,1},{1,0},{2,3},{3,2},{4,5},{5,4},{6,7},{7,6},{8,9},{9,8},{10,11... | collective-permute-start | bytes 589832 | tf_op jit(solution)/shard_map/ppermute | solution.py:328
  33.3 6.6 %collective-permute-start.17 = (bf16[1,64,512]{2,1,0:T(8,128)(2,1)S(1)}, bf16[1,64,512]{2,1,0:T(8,128)(2,1)S(1)}, u32[]{:S(2)}, u32[]{:S(2)}) collective-permute-start(bf16[1,64,512]{2,1,0:T(8,128)(2,1)S(1)} %shard_map.60.refs_0_), channel_id=1, source_target_pairs={{0,1},{1,0},{2,3},{3,2},{4,5},{5,4},{6,7},{7,6},{8,9},{9,8},{10,11... | collective-permute-start | bytes 196616 | tf_op jit(solution)/shard_map/ppermute | solution.py:328
  34.5 6.9 %collective-permute-start.14 = (bf16[64,512]{1,0:T(8,128)(2,1)S(1)}, bf16[64,512]{1,0:T(8,128)(2,1)S(1)}, u32[]{:S(2)}, u32[]{:S(2)}) collective-permute-start(bf16[64,512]{1,0:T(8,128)(2,1)S(1)} %get-tuple-element.37), channel_id=1, source_target_pairs={{0,2},{1,3},{2,4},{3,5},{4,6},{5,7},{6,0},{7,1},{8,10},{9,11},{10,... | collective-permute-start | bytes 196616 | tf_op jit(solution)/shard_map/ppermute | solution.py:340
  36.1 7.2 %collective-permute-start.15 = (bf16[64,512]{1,0:T(8,128)(2,1)S(1)}, bf16[64,512]{1,0:T(8,128)(2,1)S(1)}, u32[]{:S(2)}, u32[]{:S(2)}) collective-permute-start(bf16[64,512]{1,0:T(8,128)(2,1)S(1)} %get-tuple-element.38), channel_id=1, source_target_pairs={{0,4},{1,5},{2,6},{3,7},{4,0},{5,1},{6,2},{7,3},{8,12},{9,13},{10,... | collective-permute-start | bytes 196616 | tf_op jit(solution)/shard_map/ppermute | solution.py:340
  37.3 6.0 %collective-permute-start.16 = (bf16[64,512]{1,0:T(8,128)(2,1)S(1)}, bf16[64,512]{1,0:T(8,128)(2,1)S(1)}, u32[]{:S(2)}, u32[]{:S(2)}) collective-permute-start(bf16[64,512]{1,0:T(8,128)(2,1)S(1)} %get-tuple-element.39.refs_0_), channel_id=1, source_target_pairs={{0,6},{1,7},{2,0},{3,1},{4,2},{5,3},{6,4},{7,5},{8,14},{9,15},{10,... | collective-permute-start | bytes 196616 | tf_op jit(solution)/shard_map/ppermute | solution.py:340

commit v24 on v18

--- a/solution.py
+++ b/solution.py
@@ -72,8 +72,8 @@
     return jnp.concatenate([wide[t, pl.ds(start, size), :] for t in range(wide.shape[0])], axis=1)
 
 
-def tiled(rows, lanes):
-    return pltpu.VMEM((lanes // LANES, rows, LANES), F32)
+def tiled(rows, lanes, stride):
+    return pltpu.VMEM((lanes // LANES, rows + stride, LANES), F32)
 
 
 def call(kernel, out_shape, n_in, scratch=(), limit=24, flops=0, size=0, unread=0, result=pltpu.VMEM):
@@ -312,7 +312,8 @@
                     value = result[kk * out_rows : (kk + 1) * out_rows, lane_start : lane_start + LANES]
                     start = (kk * spans + t) * 2 + part
                     wide[g, pl.ds(start, out_rows, stride=2 * spans * group), :] = value
-        out_ref[g] = wide[g].astype(BF16).reshape(out_ref.shape[1:])
+        rows = out_ref.shape[1] * out_ref.shape[2]
+        out_ref[g] = wide[g, :rows].astype(BF16).reshape(out_ref.shape[1:])
         copies.append(pltpu.make_async_copy(out_ref.at[g], out_hbm.at[:, g], sems.at[g]))
         copies[-1].start()
     for copy in copies:
@@ -390,7 +391,7 @@
         [both] * shares + [shape((shares, local_k, 2 * share, 2 * norb), BF16)],
         blocks + 4,
         [
-            tiled(shares * share * 2 * local_k, points),
+            tiled(shares * share * 2 * local_k, points, 2 * local_k),
             pltpu.VMEM(coulomb.shape, F32),
         ],
         size=6 * MIB,
@@ -404,8 +405,8 @@
         shares + 2,
         [
             pltpu.VMEM((shares, share * 2 * local_k, points), BF16 if local_k % 8 == 0 else F32),
-            tiled(share * total, points),
-            tiled(2 * total * share, points),
+            tiled(share * total, points, total),
+            tiled(2 * total * share, points, share),
         ],
         size=2 * MIB,
     )(*tiles, jnp.asarray(forward), jnp.asarray(backward))
@@ -448,7 +449,7 @@
         shape((out_rows, local_k // pair, rows, LANES), BF16),
         chunks + 1,
         [
-            pltpu.VMEM((local_k // pair, out_rows * rows, LANES), F32),
+            pltpu.VMEM((local_k // pair, (out_rows + 1) * rows, LANES), F32),
             pltpu.VMEM((local_k // pair, out_rows, rows, LANES), BF16),
             pltpu.SemaphoreType.DMA((local_k // pair,)),
         ],

time: 44.8 us -> 44.8 us (level)
  no operation moved by 1% of the time
where the time goes in v24:
time: 44.8 us; the launch traced here: 44.7 us
  starting transfers between devices  18.5 us (41%)
  waiting for transfers between devices  16.1 us (36%)
  Pallas kernels  9.9 us (22%)
    ppermute x15, starting transfers between devices, swap(): return lax.ppermute(value, axis, [(i, i ^ mask) for i in range(size)])  13.6 us
    ppermute x15, waiting for transfers between devices, swap(): return lax.ppermute(value, axis, [(i, i ^ mask) for i in range(size)])  12.8 us
    ppermute x3, starting transfers between devices, shift_along(): came.append(lax.ppermute(pieces[s], 'pts', pairs))  4.94 us
    ppermute x3, waiting for transfers between devices, shift_along(): came.append(lax.ppermute(pieces[s], 'pts', pairs))  3.32 us
    pallas_call x1, Pallas kernels, body(): call(functools.partial(edge_kernel, per_block), [shape((local_k * 2 * per...  2.5 us
    pallas_call x1, Pallas kernels, body(): call(functools.partial(exchange_kernel, chunks, 1.0 / math.sqrt(points *...  1.66 us
    pallas_call x1, Pallas kernels, body(): call(rest_kernel, [shape(edge.shape, BF16), shape((local_k, 2, norb, poin...  1.58 us
    pallas_call x3, Pallas kernels, rows_of(): call(functools.partial(next_weight_kernel, offsets, flip, out_rows), shap...  1.51 us
  transfers between devices with their start and end apart: 18, of which 13 were waited for; matrix products, arithmetic and copies ran while one was open for 0% of the time, Pallas kernels for 7%

profile of v24, /device:TPU:0, one launch (start us, length us, event | category | flops | bytes accessed | tf_op | source)
XLA Modules:
  0.0 44.7 jit_solution(5050482022349319810)
XLA Ops:
  0.0 2.5 %shard_map.55 = (bf16[64,512]{1,0:T(8,128)(2,1)S(1)}, bf16[8,2,512,128]{3,2,1,0:T(8,128)(2,1)S(1)}) custom-call(bf16[8,2,512,256]{3,2,1,0:T(8,128)(2,1)} %orb_hbm.3), custom_call_target="tpu_custom_call" | custom-call | bytes 4194304 | tf_op jit(solution)/shard_map/pallas_call | solution.py:353
  2.5 5.1 %collective-permute-start.5 = (bf16[64,512]{1,0:T(8,128)(2,1)S(1)}, bf16[64,512]{1,0:T(8,128)(2,1)S(1)}, u32[]{:S(2)}, u32[]{:S(2)}) collective-permute-start(bf16[64,512]{1,0:T(8,128)(2,1)S(1)} %get-tuple-element.23.edge_hbm.refs_0_), channel_id=1, source_target_pairs={{0,6},{1,7},{2,4},{3,5},{4,2},{5,3},{6,0},{7,1},{8,14},{9,15},{10,... | collective-permute-start | bytes 196616 | tf_op jit(solution)/shard_map/ppermute | solution.py:325
  7.7 0.6 %collective-permute-start.1 = (bf16[64,512]{1,0:T(8,128)(2,1)S(1)}, bf16[64,512]{1,0:T(8,128)(2,1)S(1)}, u32[]{:S(2)}, u32[]{:S(2)}) collective-permute-start(bf16[64,512]{1,0:T(8,128)(2,1)S(1)} %get-tuple-element.23.edge_hbm.refs_0_), channel_id=1, source_target_pairs={{0,4},{1,5},{2,6},{3,7},{4,0},{5,1},{6,2},{7,3},{8,12},{9,13},{10,... | collective-permute-start | bytes 196616 | tf_op jit(solution)/shard_map/ppermute | solution.py:325
  8.3 1.6 %shard_map.56 = (bf16[64,512]{1,0:T(8,128)(2,1)S(1)}, bf16[8,2,512,128]{3,2,1,0:T(8,128)(2,1)S(1)}) custom-call(bf16[8,2,512,256]{3,2,1,0:T(8,128)(2,1)} %orb_hbm.3, bf16[64,512]{1,0:T(8,128)(2,1)S(1)} %get-tuple-element.23.edge_hbm.refs_0_), custom_call_target="tpu_custom_call" | custom-call | bytes 4194304 | tf_op jit(solution)/shard_map/pallas_call | solution.py:365
  10.0 0.6 %collective-permute-done.5.refs_6_ = bf16[64,512]{1,0:T(8,128)(2,1)S(1)} collective-permute-done((bf16[64,512]{1,0:T(8,128)(2,1)S(1)}, bf16[64,512]{1,0:T(8,128)(2,1)S(1)}, u32[]{:S(2)}, u32[]{:S(2)}) %collective-permute-start.5) | collective-permute-done | bytes 65568 | tf_op jit(solution)/shard_map/ppermute | solution.py:325
  10.6 1.8 %collective-permute-done.3.refs_4_ = bf16[64,512]{1,0:T(8,128)(2,1)S(1)} collective-permute-done((bf16[64,512]{1,0:T(8,128)(2,1)S(1)}, bf16[64,512]{1,0:T(8,128)(2,1)S(1)}, u32[]{:S(2)}, u32[]{:S(2)}) %collective-permute-start.3) | collective-permute-done | bytes 65568 | tf_op jit(solution)/shard_map/ppermute | solution.py:325
  12.3 1.0 %collective-permute-done.1.refs_2_ = bf16[64,512]{1,0:T(8,128)(2,1)S(1)} collective-permute-done((bf16[64,512]{1,0:T(8,128)(2,1)S(1)}, bf16[64,512]{1,0:T(8,128)(2,1)S(1)}, u32[]{:S(2)}, u32[]{:S(2)}) %collective-permute-start.1) | collective-permute-done | bytes 65568 | tf_op jit(solution)/shard_map/ppermute | solution.py:325
  13.6 1.0 %collective-permute-done.2.refs_3_ = bf16[64,512]{1,0:T(8,128)(2,1)S(1)} collective-permute-done((bf16[64,512]{1,0:T(8,128)(2,1)S(1)}, bf16[64,512]{1,0:T(8,128)(2,1)S(1)}, u32[]{:S(2)}, u32[]{:S(2)}) %collective-permute-start.2) | collective-permute-done | bytes 65568 | tf_op jit(solution)/shard_map/ppermute | solution.py:325
  14.6 1.4 %shard_map.57 = (bf16[192,256]{1,0:T(8,128)(2,1)S(1)}, bf16[192,256]{1,0:T(8,128)(2,1)S(1)}, bf16[192,256]{1,0:T(8,128)(2,1)S(1)}, bf16[192,256]{1,0:T(8,128)(2,1)S(1)}, bf16[4,8,16,1024]{3,2,1,0:T(8,128)(2,1)S(1)}) custom-call(bf16[64,512]{1,0:T(8,128)(2,1)S(1)} %get-tuple-element.23.edge_hbm.refs_0_, bf16[64,512]{1,0:T(8,128)(2,1)S(1)} %collective-permute-done.refs_1_, ...), custom_call_target="tpu_custom_call" | custom-call | bytes 6291456 | tf_op jit(solution)/shard_map/pallas_call | solution.py:389
  15.9 2.5 %collective-permute-start.7 = (bf16[192,256]{1,0:T(8,128)(2,1)S(1)}, bf16[192,256]{1,0:T(8,128)(2,1)S(1)}, u32[]{:S(2)}, u32[]{:S(2)}) collective-permute-start(bf16[192,256]{1,0:T(8,128)(2,1)S(1)} %get-tuple-element.27), channel_id=1, source_target_pairs={{0,24},{8,16},{16,8},{24,0},{1,25},{9,17},{17,9},{25,1},{2,26},{10... | collective-permute-start | bytes 294920 | tf_op jit(solution)/shard_map/ppermute | solution.py:325
  18.4 0.5 %collective-permute-start.8 = (bf16[192,256]{1,0:T(8,128)(2,1)S(1)}, bf16[192,256]{1,0:T(8,128)(2,1)S(1)}, u32[]{:S(2)}, u32[]{:S(2)}) collective-permute-start(bf16[192,256]{1,0:T(8,128)(2,1)S(1)} %get-tuple-element.28), channel_id=1, source_target_pairs={{0,16},{8,24},{16,0},{24,8},{1,17},{9,25},{17,1},{25,9},{2,18},{10... | collective-permute-start | bytes 294920 | tf_op jit(solution)/shard_map/ppermute | solution.py:325
  18.9 0.5 %collective-permute-start.9 = (bf16[192,256]{1,0:T(8,128)(2,1)S(1)}, bf16[192,256]{1,0:T(8,128)(2,1)S(1)}, u32[]{:S(2)}, u32[]{:S(2)}) collective-permute-start(bf16[192,256]{1,0:T(8,128)(2,1)S(1)} %get-tuple-element.29), channel_id=1, source_target_pairs={{0,8},{8,0},{16,24},{24,16},{1,9},{9,1},{17,25},{25,17},{2,10},{10... | collective-permute-start | bytes 294920 | tf_op jit(solution)/shard_map/ppermute | solution.py:325
  19.5 2.4 %collective-permute-done.7.refs_0_ = bf16[192,256]{1,0:T(8,128)(2,1)S(1)} collective-permute-done((bf16[192,256]{1,0:T(8,128)(2,1)S(1)}, bf16[192,256]{1,0:T(8,128)(2,1)S(1)}, u32[]{:S(2)}, u32[]{:S(2)}) %collective-permute-start.7) | collective-permute-done | bytes 98336 | tf_op jit(solution)/shard_map/ppermute | solution.py:325
  21.8 2.0 %collective-permute-done.8.refs_1_ = bf16[192,256]{1,0:T(8,128)(2,1)S(1)} collective-permute-done((bf16[192,256]{1,0:T(8,128)(2,1)S(1)}, bf16[192,256]{1,0:T(8,128)(2,1)S(1)}, u32[]{:S(2)}, u32[]{:S(2)}) %collective-permute-start.8) | collective-permute-done | bytes 98336 | tf_op jit(solution)/shard_map/ppermute | solution.py:325
  23.9 0.6 %shard_map.58 = (bf16[128,256]{1,0:T(8,128)(2,1)S(1)}, bf16[128,256]{1,0:T(8,128)(2,1)S(1)}, bf16[128,256]{1,0:T(8,128)(2,1)S(1)}, bf16[128,256]{1,0:T(8,128)(2,1)S(1)}) custom-call(bf16[192,256]{1,0:T(8,128)(2,1)S(1)} %collective-permute-done.7.refs_0_, bf16[192,256]{1,0:T(8,128)(2,1)S(1)} %collective-permute-done.8.refs_1_, ...), custom_call_target="tpu_custom_call" | custom-call | bytes 2097152 | tf_op jit(solution)/shard_map/pallas_call | solution.py:402
  24.5 1.8 %collective-permute-start.10 = (bf16[128,256]{1,0:T(8,128)(2,1)S(1)}, bf16[128,256]{1,0:T(8,128)(2,1)S(1)}, u32[]{:S(2)}, u32[]{:S(2)}) collective-permute-start(bf16[128,256]{1,0:T(8,128)(2,1)S(1)} %get-tuple-element.31), channel_id=1, source_target_pairs={{0,24},{8,16},{16,8},{24,0},{1,25},{9,17},{17,9},{25,1},{2,26},{10... | collective-permute-start | bytes 196616 | tf_op jit(solution)/shard_map/ppermute | solution.py:325
  26.3 1.3 %collective-permute-start.11 = (bf16[128,256]{1,0:T(8,128)(2,1)S(1)}, bf16[128,256]{1,0:T(8,128)(2,1)S(1)}, u32[]{:S(2)}, u32[]{:S(2)}) collective-permute-start(bf16[128,256]{1,0:T(8,128)(2,1)S(1)} %get-tuple-element.32), channel_id=1, source_target_pairs={{0,16},{8,24},{16,0},{24,8},{1,17},{9,25},{17,1},{25,9},{2,18},{10... | collective-permute-start | bytes 196616 | tf_op jit(solution)/shard_map/ppermute | solution.py:325
  27.6 0.5 %collective-permute-start.12 = (bf16[128,256]{1,0:T(8,128)(2,1)S(1)}, bf16[128,256]{1,0:T(8,128)(2,1)S(1)}, u32[]{:S(2)}, u32[]{:S(2)}) collective-permute-start(bf16[128,256]{1,0:T(8,128)(2,1)S(1)} %get-tuple-element.33), channel_id=1, source_target_pairs={{0,8},{8,0},{16,24},{24,16},{1,9},{9,1},{17,25},{25,17},{2,10},{10... | collective-permute-start | bytes 196616 | tf_op jit(solution)/shard_map/ppermute | solution.py:325
  28.1 2.1 %collective-permute-done.10.refs_0_ = bf16[128,256]{1,0:T(8,128)(2,1)S(1)} collective-permute-done((bf16[128,256]{1,0:T(8,128)(2,1)S(1)}, bf16[128,256]{1,0:T(8,128)(2,1)S(1)}, u32[]{:S(2)}, u32[]{:S(2)}) %collective-permute-start.10) | collective-permute-done | bytes 65568 | tf_op jit(solution)/shard_map/ppermute | solution.py:325
  30.2 0.5 %collective-permute-done.11.refs_1_ = bf16[128,256]{1,0:T(8,128)(2,1)S(1)} collective-permute-done((bf16[128,256]{1,0:T(8,128)(2,1)S(1)}, bf16[128,256]{1,0:T(8,128)(2,1)S(1)}, u32[]{:S(2)}, u32[]{:S(2)}) %collective-permute-start.11) | collective-permute-done | bytes 65568 | tf_op jit(solution)/shard_map/ppermute | solution.py:325
  30.7 1.1 %collective-permute-done.12.refs_2_ = bf16[128,256]{1,0:T(8,128)(2,1)S(1)} collective-permute-done((bf16[128,256]{1,0:T(8,128)(2,1)S(1)}, bf16[128,256]{1,0:T(8,128)(2,1)S(1)}, u32[]{:S(2)}, u32[]{:S(2)}) %collective-permute-start.12) | collective-permute-done | bytes 65568 | tf_op jit(solution)/shard_map/ppermute | solution.py:325
  31.9 0.6 %shard_map.59 = (bf16[3,64,512]{2,1,0:T(8,128)(2,1)S(1)}, bf16[4,128,1024]{2,1,0:T(8,128)(2,1)S(1)}) custom-call(bf16[128,256]{1,0:T(8,128)(2,1)S(1)} %collective-permute-done.10.refs_0_, bf16[128,256]{1,0:T(8,128)(2,1)S(1)} %collective-permute-done.11.refs_1_, bf16[128,256]{1,0:T(8,128)(2,1)S(1)} %collective-permute-done.12.refs_2_, ...), custom_call_target="tpu_custom_call" | custom-call | tf_op jit(solution)/shard_map/pallas_call | solution.py:418
  32.6 0.5 %shard_map.60.refs_0_ = bf16[1,64,512]{2,1,0:T(8,128)(2,1)S(1)} custom-call(bf16[4,128,1024]{2,1,0:T(8,128)(2,1)S(1)} %get-tuple-element.35.right_ref, bf16[8,2,512,128]{3,2,1,0:T(8,128)(2,1)S(1)} %get-tuple-element.25.refs_8_.refs_4_.orb_ref, bf16[8,2,512,128]{3,2,1,0:T(8,128)(2,1)S(1)} %get-tuple-element.26.refs_9_.refs_5_.rest_ref, ...), custom_call_target="tpu_custom_call" | custom-call | tf_op jit(solution)/shard_map/pallas_call | solution.py:429
  33.1 0.6 %collective-permute-start.17 = (bf16[1,64,512]{2,1,0:T(8,128)(2,1)S(1)}, bf16[1,64,512]{2,1,0:T(8,128)(2,1)S(1)}, u32[]{:S(2)}, u32[]{:S(2)}) collective-permute-start(bf16[1,64,512]{2,1,0:T(8,128)(2,1)S(1)} %shard_map.60.refs_0_), channel_id=1, source_target_pairs={{0,1},{1,0},{2,3},{3,2},{4,5},{5,4},{6,7},{7,6},{8,9},{9,8},{10,11... | collective-permute-start | bytes 196616 | tf_op jit(solution)/shard_map/ppermute | solution.py:325
  33.6 0.6 %shard_map.61.keep_ref = f32[3,64,512]{2,1,0:T(8,128)S(1)} custom-call(bf16[4,128,1024]{2,1,0:T(8,128)(2,1)S(1)} %get-tuple-element.35.right_ref, bf16[8,2,512,128]{3,2,1,0:T(8,128)(2,1)S(1)} %get-tuple-element.25.refs_8_.refs_4_.orb_ref, bf16[8,2,512,128]{3,2,1,0:T(8,128)(2,1)S(1)} %get-tuple-element.26.refs_9_.refs_5_.rest_ref, ...), custom_call_target="tpu_custom_call" | custom-call | tf_op jit(solution)/shard_map/pallas_call | solution.py:429
  34.2 1.6 %collective-permute-start.14 = (bf16[64,512]{1,0:T(8,128)(2,1)S(1)}, bf16[64,512]{1,0:T(8,128)(2,1)S(1)}, u32[]{:S(2)}, u32[]{:S(2)}) collective-permute-start(bf16[64,512]{1,0:T(8,128)(2,1)S(1)} %get-tuple-element.37), channel_id=1, source_target_pairs={{0,2},{1,3},{2,4},{3,5},{4,6},{5,7},{6,0},{7,1},{8,10},{9,11},{10,... | collective-permute-start | bytes 196616 | tf_op jit(solution)/shard_map/ppermute | solution.py:337
  35.9 1.2 %collective-permute-start.15 = (bf16[64,512]{1,0:T(8,128)(2,1)S(1)}, bf16[64,512]{1,0:T(8,128)(2,1)S(1)}, u32[]{:S(2)}, u32[]{:S(2)}) collective-permute-start(bf16[64,512]{1,0:T(8,128)(2,1)S(1)} %get-tuple-element.38), channel_id=1, source_target_pairs={{0,4},{1,5},{2,6},{3,7},{4,0},{5,1},{6,2},{7,3},{8,12},{9,13},{10,... | collective-permute-start | bytes 196616 | tf_op jit(solution)/shard_map/ppermute | solution.py:337
  37.0 2.2 %collective-permute-start.16 = (bf16[64,512]{1,0:T(8,128)(2,1)S(1)}, bf16[64,512]{1,0:T(8,128)(2,1)S(1)}, u32[]{:S(2)}, u32[]{:S(2)}) collective-permute-start(bf16[64,512]{1,0:T(8,128)(2,1)S(1)} %get-tuple-element.39.refs_0_), channel_id=1, source_target_pairs={{0,6},{1,7},{2,0},{3,1},{4,2},{5,3},{6,4},{7,5},{8,14},{9,15},{10,... | collective-permute-start | bytes 196616 | tf_op jit(solution)/shard_map/ppermute | solution.py:337
  39.2 0.5 %shard_map.63.keep_ref = f32[1,64,512]{2,1,0:T(8,128)S(1)} custom-call(bf16[4,128,1024]{2,1,0:T(8,128)(2,1)S(1)} %get-tuple-element.35.right_ref, bf16[8,2,512,128]{3,2,1,0:T(8,128)(2,1)S(1)} %get-tuple-element.25.refs_8_.refs_4_.orb_ref, bf16[8,2,512,128]{3,2,1,0:T(8,128)(2,1)S(1)} %get-tuple-element.26.refs_9_.refs_5_.rest_ref, ...), custom_call_target="tpu_custom_call" | custom-call | tf_op jit(solution)/shard_map/pallas_call | solution.py:429
  39.7 1.4 %collective-permute-done.14.refs_0_ = bf16[64,512]{1,0:T(8,128)(2,1)S(1)} collective-permute-done((bf16[64,512]{1,0:T(8,128)(2,1)S(1)}, bf16[64,512]{1,0:T(8,128)(2,1)S(1)}, u32[]{:S(2)}, u32[]{:S(2)}) %collective-permute-start.14) | collective-permute-done | bytes 65568 | tf_op jit(solution)/shard_map/ppermute | solution.py:337
  41.1 1.9 %collective-permute-done.15.refs_1_ = bf16[64,512]{1,0:T(8,128)(2,1)S(1)} collective-permute-done((bf16[64,512]{1,0:T(8,128)(2,1)S(1)}, bf16[64,512]{1,0:T(8,128)(2,1)S(1)}, u32[]{:S(2)}, u32[]{:S(2)}) %collective-permute-start.15) | collective-permute-done | bytes 65568 | tf_op jit(solution)/shard_map/ppermute | solution.py:337
  43.0 1.7 %shard_map.65 = bf16[64,4,16,128]{3,2,1,0:T(8,128)(2,1)} custom-call(bf16[64,512]{1,0:T(8,128)(2,1)S(1)} %collective-permute-done.14.refs_0_, bf16[64,512]{1,0:T(8,128)(2,1)S(1)} %collective-permute-done.15.refs_1_, bf16[64,512]{1,0:T(8,128)(2,1)S(1)} %collective-permute-done.16.refs_2_, f32[64,512]{1,0:T(8,128)S(1)} %shard_map.64.refs_3_, ...), custom_call_target="tpu_custom_call" | custom-call | bytes 4194304 | tf_op jit(solution)/shard_map/pallas_call | solution.py:447
  (23 shorter events, 0.6 us)
Async XLA Ops:
  2.5 12.0 %copy-start = (bf16[8,32,256]{2,1,0:T(8,128)(2,1)S(1)}, bf16[8,32,256]{2,1,0:T(8,128)(2,1)}, u32[]{:S(2)}) copy-start(bf16[8,32,256]{2,1,0:T(8,128)(2,1)} %refs_11_.1) | copy-start | bytes 393220
  2.5 12.0 %copy-start.1 = (bf16[2,256,128]{2,1,0:T(8,128)(2,1)S(1)}, bf16[2,256,128]{2,1,0:T(8,128)(2,1)}, u32[]{:S(2)}) copy-start(bf16[2,256,128]{2,1,0:T(8,128)(2,1)} %constant.6.clone.refs_10_) | copy-start | bytes 393220
  2.5 8.0 %collective-permute-start.5 = (bf16[64,512]{1,0:T(8,128)(2,1)S(1)}, bf16[64,512]{1,0:T(8,128)(2,1)S(1)}, u32[]{:S(2)}, u32[]{:S(2)}) collective-permute-start(bf16[64,512]{1,0:T(8,128)(2,1)S(1)} %get-tuple-element.23.edge_hbm.refs_0_), channel_id=1, source_target_pairs={{0,6},{1,7},{2,4},{3,5},{4,2},{5,3},{6,0},{7,1},{8,14},{9,15},{10,... | collective-permute-start | bytes 196616 | tf_op jit(solution)/shard_map/ppermute | solution.py:325
  7.6 4.7 %collective-permute-start.3 = (bf16[64,512]{1,0:T(8,128)(2,1)S(1)}, bf16[64,512]{1,0:T(8,128)(2,1)S(1)}, u32[]{:S(2)}, u32[]{:S(2)}) collective-permute-start(bf16[64,512]{1,0:T(8,128)(2,1)S(1)} %get-tuple-element.23.edge_hbm.refs_0_), channel_id=1, source_target_pairs={{0,2},{1,3},{2,0},{3,1},{4,6},{5,7},{6,4},{7,5},{8,10},{9,11},{10,... | collective-permute-start | bytes 196616 | tf_op jit(solution)/shard_map/ppermute | solution.py:325
  7.7 5.6 %collective-permute-start.1 = (bf16[64,512]{1,0:T(8,128)(2,1)S(1)}, bf16[64,512]{1,0:T(8,128)(2,1)S(1)}, u32[]{:S(2)}, u32[]{:S(2)}) collective-permute-start(bf16[64,512]{1,0:T(8,128)(2,1)S(1)} %get-tuple-element.23.edge_hbm.refs_0_), channel_id=1, source_target_pairs={{0,4},{1,5},{2,6},{3,7},{4,0},{5,1},{6,2},{7,3},{8,12},{9,13},{10,... | collective-permute-start | bytes 196616 | tf_op jit(solution)/shard_map/ppermute | solution.py:325
  9.9 3.4 %collective-permute-start = (bf16[64,512]{1,0:T(8,128)(2,1)S(1)}, bf16[64,512]{1,0:T(8,128)(2,1)S(1)}, u32[]{:S(2)}, u32[]{:S(2)}) collective-permute-start(bf16[64,512]{1,0:T(8,128)(2,1)S(1)} %get-tuple-element.24), channel_id=1, source_target_pairs={{0,1},{1,0},{2,3},{3,2},{4,5},{5,4},{6,7},{7,6},{8,9},{9,8},{10,11... | collective-permute-start | bytes 196616 | tf_op jit(solution)/shard_map/ppermute | solution.py:325
  10.5 2.7 %collective-permute-start.6 = (bf16[64,512]{1,0:T(8,128)(2,1)S(1)}, bf16[64,512]{1,0:T(8,128)(2,1)S(1)}, u32[]{:S(2)}, u32[]{:S(2)}) collective-permute-start(bf16[64,512]{1,0:T(8,128)(2,1)S(1)} %collective-permute-done.5.refs_6_), channel_id=1, source_target_pairs={{0,1},{1,0},{2,3},{3,2},{4,5},{5,4},{6,7},{7,6},{8,9},{9,8},{10,11... | collective-permute-start | bytes 196616 | tf_op jit(solution)/shard_map/ppermute | solution.py:325
  12.3 1.3 %collective-permute-start.4 = (bf16[64,512]{1,0:T(8,128)(2,1)S(1)}, bf16[64,512]{1,0:T(8,128)(2,1)S(1)}, u32[]{:S(2)}, u32[]{:S(2)}) collective-permute-start(bf16[64,512]{1,0:T(8,128)(2,1)S(1)} %collective-permute-done.3.refs_4_), channel_id=1, source_target_pairs={{0,1},{1,0},{2,3},{3,2},{4,5},{5,4},{6,7},{7,6},{8,9},{9,8},{10,11... | collective-permute-start | bytes 196616 | tf_op jit(solution)/shard_map/ppermute | solution.py:325
  13.3 1.3 %collective-permute-start.2 = (bf16[64,512]{1,0:T(8,128)(2,1)S(1)}, bf16[64,512]{1,0:T(8,128)(2,1)S(1)}, u32[]{:S(2)}, u32[]{:S(2)}) collective-permute-start(bf16[64,512]{1,0:T(8,128)(2,1)S(1)} %collective-permute-done.1.refs_2_), channel_id=1, source_target_pairs={{0,1},{1,0},{2,3},{3,2},{4,5},{5,4},{6,7},{7,6},{8,9},{9,8},{10,11... | collective-permute-start | bytes 196616 | tf_op jit(solution)/shard_map/ppermute | solution.py:325
  14.5 9.4 %copy-start.2 = (bf16[64,128]{1,0:T(8,128)(2,1)S(1)}, bf16[64,128]{1,0:T(8,128)(2,1)}, u32[]{:S(2)}) copy-start(bf16[64,128]{1,0:T(8,128)(2,1)} %constant.8.clone.refs_5_) | copy-start | bytes 49156
  14.5 9.4 %copy-start.3 = (bf16[64,128]{1,0:T(8,128)(2,1)S(1)}, bf16[64,128]{1,0:T(8,128)(2,1)}, u32[]{:S(2)}) copy-start(bf16[64,128]{1,0:T(8,128)(2,1)} %constant.7.clone.refs_4_) | copy-start | bytes 49156
  15.9 5.9 %collective-permute-start.7 = (bf16[192,256]{1,0:T(8,128)(2,1)S(1)}, bf16[192,256]{1,0:T(8,128)(2,1)S(1)}, u32[]{:S(2)}, u32[]{:S(2)}) collective-permute-start(bf16[192,256]{1,0:T(8,128)(2,1)S(1)} %get-tuple-element.27), channel_id=1, source_target_pairs={{0,24},{8,16},{16,8},{24,0},{1,25},{9,17},{17,9},{25,1},{2,26},{10... | collective-permute-start | bytes 294920 | tf_op jit(solution)/shard_map/ppermute | solution.py:325
  18.4 5.4 %collective-permute-start.8 = (bf16[192,256]{1,0:T(8,128)(2,1)S(1)}, bf16[192,256]{1,0:T(8,128)(2,1)S(1)}, u32[]{:S(2)}, u32[]{:S(2)}) collective-permute-start(bf16[192,256]{1,0:T(8,128)(2,1)S(1)} %get-tuple-element.28), channel_id=1, source_target_pairs={{0,16},{8,24},{16,0},{24,8},{1,17},{9,25},{17,1},{25,9},{2,18},{10... | collective-permute-start | bytes 294920 | tf_op jit(solution)/shard_map/ppermute | solution.py:325
  18.9 5.0 %collective-permute-start.9 = (bf16[192,256]{1,0:T(8,128)(2,1)S(1)}, bf16[192,256]{1,0:T(8,128)(2,1)S(1)}, u32[]{:S(2)}, u32[]{:S(2)}) collective-permute-start(bf16[192,256]{1,0:T(8,128)(2,1)S(1)} %get-tuple-element.29), channel_id=1, source_target_pairs={{0,8},{8,0},{16,24},{24,16},{1,9},{9,1},{17,25},{25,17},{2,10},{10... | collective-permute-start | bytes 294920 | tf_op jit(solution)/shard_map/ppermute | solution.py:325
  24.5 5.7 %collective-permute-start.10 = (bf16[128,256]{1,0:T(8,128)(2,1)S(1)}, bf16[128,256]{1,0:T(8,128)(2,1)S(1)}, u32[]{:S(2)}, u32[]{:S(2)}) collective-permute-start(bf16[128,256]{1,0:T(8,128)(2,1)S(1)} %get-tuple-element.31), channel_id=1, source_target_pairs={{0,24},{8,16},{16,8},{24,0},{1,25},{9,17},{17,9},{25,1},{2,26},{10... | collective-permute-start | bytes 196616 | tf_op jit(solution)/shard_map/ppermute | solution.py:325
  26.3 4.4 %collective-permute-start.11 = (bf16[128,256]{1,0:T(8,128)(2,1)S(1)}, bf16[128,256]{1,0:T(8,128)(2,1)S(1)}, u32[]{:S(2)}, u32[]{:S(2)}) collective-permute-start(bf16[128,256]{1,0:T(8,128)(2,1)S(1)} %get-tuple-element.32), channel_id=1, source_target_pairs={{0,16},{8,24},{16,0},{24,8},{1,17},{9,25},{17,1},{25,9},{2,18},{10... | collective-permute-start | bytes 196616 | tf_op jit(solution)/shard_map/ppermute | solution.py:325
  27.6 4.3 %collective-permute-start.12 = (bf16[128,256]{1,0:T(8,128)(2,1)S(1)}, bf16[128,256]{1,0:T(8,128)(2,1)S(1)}, u32[]{:S(2)}, u32[]{:S(2)}) collective-permute-start(bf16[128,256]{1,0:T(8,128)(2,1)S(1)} %get-tuple-element.33), channel_id=1, source_target_pairs={{0,8},{8,0},{16,24},{24,16},{1,9},{9,1},{17,25},{25,17},{2,10},{10... | collective-permute-start | bytes 196616 | tf_op jit(solution)/shard_map/ppermute | solution.py:325
  32.5 1.7 %collective-permute-start.13 = (bf16[3,64,512]{2,1,0:T(8,128)(2,1)S(1)}, bf16[3,64,512]{2,1,0:T(8,128)(2,1)S(1)}, u32[]{:S(2)}, u32[]{:S(2)}) collective-permute-start(bf16[3,64,512]{2,1,0:T(8,128)(2,1)S(1)} %get-tuple-element.36.refs_0_), channel_id=1, source_target_pairs={{0,1},{1,0},{2,3},{3,2},{4,5},{5,4},{6,7},{7,6},{8,9},{9,8},{10,11... | collective-permute-start | bytes 589832 | tf_op jit(solution)/shard_map/ppermute | solution.py:325
  33.1 6.6 %collective-permute-start.17 = (bf16[1,64,512]{2,1,0:T(8,128)(2,1)S(1)}, bf16[1,64,512]{2,1,0:T(8,128)(2,1)S(1)}, u32[]{:S(2)}, u32[]{:S(2)}) collective-permute-start(bf16[1,64,512]{2,1,0:T(8,128)(2,1)S(1)} %shard_map.60.refs_0_), channel_id=1, source_target_pairs={{0,1},{1,0},{2,3},{3,2},{4,5},{5,4},{6,7},{7,6},{8,9},{9,8},{10,11... | collective-permute-start | bytes 196616 | tf_op jit(solution)/shard_map/ppermute | solution.py:325
  34.2 6.9 %collective-permute-start.14 = (bf16[64,512]{1,0:T(8,128)(2,1)S(1)}, bf16[64,512]{1,0:T(8,128)(2,1)S(1)}, u32[]{:S(2)}, u32[]{:S(2)}) collective-permute-start(bf16[64,512]{1,0:T(8,128)(2,1)S(1)} %get-tuple-element.37), channel_id=1, source_target_pairs={{0,2},{1,3},{2,4},{3,5},{4,6},{5,7},{6,0},{7,1},{8,10},{9,11},{10,... | collective-permute-start | bytes 196616 | tf_op jit(solution)/shard_map/ppermute | solution.py:337
  35.9 7.2 %collective-permute-start.15 = (bf16[64,512]{1,0:T(8,128)(2,1)S(1)}, bf16[64,512]{1,0:T(8,128)(2,1)S(1)}, u32[]{:S(2)}, u32[]{:S(2)}) collective-permute-start(bf16[64,512]{1,0:T(8,128)(2,1)S(1)} %get-tuple-element.38), channel_id=1, source_target_pairs={{0,4},{1,5},{2,6},{3,7},{4,0},{5,1},{6,2},{7,3},{8,12},{9,13},{10,... | collective-permute-start | bytes 196616 | tf_op jit(solution)/shard_map/ppermute | solution.py:337
  37.0 6.0 %collective-permute-start.16 = (bf16[64,512]{1,0:T(8,128)(2,1)S(1)}, bf16[64,512]{1,0:T(8,128)(2,1)S(1)}, u32[]{:S(2)}, u32[]{:S(2)}) collective-permute-start(bf16[64,512]{1,0:T(8,128)(2,1)S(1)} %get-tuple-element.39.refs_0_), channel_id=1, source_target_pairs={{0,6},{1,7},{2,0},{3,1},{4,2},{5,3},{6,4},{7,5},{8,14},{9,15},{10,... | collective-permute-start | bytes 196616 | tf_op jit(solution)/shard_map/ppermute | solution.py:337

commit v25 on v18

--- a/solution.py
+++ b/solution.py
@@ -100,10 +100,18 @@
     return copies
 
 
-def rest_kernel(orb_hbm, edge_hbm, pass_ref, orb_ref, sems, pass_sem):
+def rest_kernel(shares, coulomb_ref, orb_hbm, edge_hbm, pass_ref, orb_ref, cell_ref, wide, sems, pass_sem):
     copies = load_copies(orb_hbm, orb_ref, sems, LANES)
     copies.append(pltpu.make_async_copy(edge_hbm, pass_ref, pass_sem))
     copies[-1].start()
+    share = coulomb_ref.shape[1] // shares
+    me, plane = lax.axis_index("ka"), plane_of(shares)
+    wide[...] = coulomb_ref[...].astype(F32)
+    for s in range(shares):
+        owned = jnp.bitwise_xor(jnp.bitwise_xor(me, s), plane)
+        start = pl.multiple_of(owned * share, share)
+        pieces = [wide[r, pl.ds(start, share), :] for r in range(wide.shape[0])]
+        cell_ref[s] = jnp.concatenate(pieces, axis=0).astype(BF16)
     for copy in copies:
         copy.wait()
 
@@ -134,8 +142,8 @@
 
 
 def tile_kernel(shares, per_share, per_block, *refs):
-    blocks, (orb_ref, rest_ref, sel_ref, coulomb_ref) = refs[: shares * per_share], refs[shares * per_share :][:4]
-    *outs, form_ref, wide, cells = refs[shares * per_share + 4 :]
+    blocks, (orb_ref, rest_ref, sel_ref, cell_ref) = refs[: shares * per_share], refs[shares * per_share :][:4]
+    *outs, form_ref, wide = refs[shares * per_share + 4 :]
     local_k, _, norb, _ = orb_ref.shape
     group = ROWS // (2 * per_block)
     share = per_share * per_block
@@ -172,13 +180,10 @@
                     start = offset * share * 2 * local_k + 2 * k + part
                     spread(wide, start, 2 * local_k, tile[low : low + share])
     size = share * 2 * local_k
-    cells[...] = coulomb_ref[...].astype(F32)
     for s in range(shares):
         offset = jnp.bitwise_xor(me, s)
         outs[s][:size] = take(wide, pl.multiple_of(offset * size, size), size).astype(BF16)
-        start = pl.multiple_of(jnp.bitwise_xor(offset, plane) * share, share)
-        pieces = [cells[r, pl.ds(start, share), :] for r in range(local_k)]
-        outs[s][size:] = jnp.concatenate(pieces, axis=0).astype(BF16)
+        outs[s][size:] = cell_ref[s]
 
 
 def transform_kernel(shares, total, share, *refs):
@@ -361,15 +366,19 @@
         size=4 * MIB,
         unread=1,
     )(orbitals)
-    passed_edge, rest = call(
-        rest_kernel,
-        [shape(edge.shape, BF16), shape((local_k, 2, norb, points - LANES), BF16)],
-        0,
-        [pltpu.SemaphoreType.DMA((local_k,)), pltpu.SemaphoreType.DMA],
+    passed_edge, rest, cells = call(
+        functools.partial(rest_kernel, shares),
+        [
+            shape(edge.shape, BF16),
+            shape((local_k, 2, norb, points - LANES), BF16),
+            shape((shares, local_k * share, points), BF16),
+        ],
+        1,
+        [pltpu.VMEM(coulomb.shape, F32), pltpu.SemaphoreType.DMA((local_k,)), pltpu.SemaphoreType.DMA],
         limit=49,
         size=4 * MIB,
         unread=2,
-    )(orbitals, edge)
+    )(coulomb, orbitals, edge)
     per_share = blocks // shares
     partner = swap(passed_edge, "pts", 1)
     came = [edge, partner] + [swap(edge, "pts", 2 * e + c) for e in range(1, per_share // 2) for c in range(2)]
@@ -391,10 +400,9 @@
         blocks + 4,
         [
             tiled(shares * share * 2 * local_k, points),
-            pltpu.VMEM(coulomb.shape, F32),
         ],
         size=6 * MIB,
-    )(*[block for offset in [0, *asked(shares)] for block in came[offset]], first, rest, selector, coulomb)
+    )(*[block for offset in [0, *asked(shares)] for block in came[offset]], first, rest, selector, cells)
     tiles = trade(tiles, "ka", 1)
 
     forward, backward = phase_tables(total)

time: 44.8 us -> 44.8 us (level)
  no operation moved by 1% of the time
where the time goes in v25:
time: 44.8 us; the launch traced here: 44.7 us
  starting transfers between devices  18.5 us (41%)
  waiting for transfers between devices  16.1 us (36%)
  Pallas kernels  9.91 us (22%)
    ppermute x15, starting transfers between devices, swap(): return lax.ppermute(value, axis, [(i, i ^ mask) for i in range(size)])  13.6 us
    ppermute x15, waiting for transfers between devices, swap(): return lax.ppermute(value, axis, [(i, i ^ mask) for i in range(size)])  12.8 us
    ppermute x3, starting transfers between devices, shift_along(): came.append(lax.ppermute(pieces[s], 'pts', pairs))  4.93 us
    ppermute x3, waiting for transfers between devices, shift_along(): came.append(lax.ppermute(pieces[s], 'pts', pairs))  3.32 us
    pallas_call x1, Pallas kernels, body(): call(functools.partial(edge_kernel, per_block), [shape((local_k * 2 * per...  2.54 us
    pallas_call x1, Pallas kernels, body(): call(functools.partial(exchange_kernel, chunks, 1.0 / math.sqrt(points *...  1.66 us
    pallas_call x1, Pallas kernels, body(): call(functools.partial(rest_kernel, shares), [shape(edge.shape, BF16), sh...  1.58 us
    pallas_call x3, Pallas kernels, rows_of(): call(functools.partial(next_weight_kernel, offsets, flip, out_rows), shap...  1.51 us
  transfers between devices with their start and end apart: 18, of which 13 were waited for; matrix products, arithmetic and copies ran while one was open for 0% of the time, Pallas kernels for 7%

profile of v25, /device:TPU:0, one launch (start us, length us, event | category | flops | bytes accessed | tf_op | source)
XLA Modules:
  0.0 44.7 jit_solution(14141436764487438235)
XLA Ops:
  0.0 2.5 %shard_map.55 = (bf16[64,512]{1,0:T(8,128)(2,1)S(1)}, bf16[8,2,512,128]{3,2,1,0:T(8,128)(2,1)S(1)}) custom-call(bf16[8,2,512,256]{3,2,1,0:T(8,128)(2,1)} %orb_hbm.3), custom_call_target="tpu_custom_call" | custom-call | bytes 4194304 | tf_op jit(solution)/shard_map/pallas_call | solution.py:357
  2.6 5.1 %collective-permute-start.5 = (bf16[64,512]{1,0:T(8,128)(2,1)S(1)}, bf16[64,512]{1,0:T(8,128)(2,1)S(1)}, u32[]{:S(2)}, u32[]{:S(2)}) collective-permute-start(bf16[64,512]{1,0:T(8,128)(2,1)S(1)} %get-tuple-element.24.edge_hbm.refs_0_), channel_id=1, source_target_pairs={{0,6},{1,7},{2,4},{3,5},{4,2},{5,3},{6,0},{7,1},{8,14},{9,15},{10,... | collective-permute-start | bytes 196616 | tf_op jit(solution)/shard_map/ppermute | solution.py:329
  7.7 0.6 %collective-permute-start.1 = (bf16[64,512]{1,0:T(8,128)(2,1)S(1)}, bf16[64,512]{1,0:T(8,128)(2,1)S(1)}, u32[]{:S(2)}, u32[]{:S(2)}) collective-permute-start(bf16[64,512]{1,0:T(8,128)(2,1)S(1)} %get-tuple-element.24.edge_hbm.refs_0_), channel_id=1, source_target_pairs={{0,4},{1,5},{2,6},{3,7},{4,0},{5,1},{6,2},{7,3},{8,12},{9,13},{10,... | collective-permute-start | bytes 196616 | tf_op jit(solution)/shard_map/ppermute | solution.py:329
  8.3 1.6 %shard_map.56 = (bf16[64,512]{1,0:T(8,128)(2,1)S(1)}, bf16[8,2,512,128]{3,2,1,0:T(8,128)(2,1)S(1)}, bf16[4,64,256]{2,1,0:T(8,128)(2,1)S(1)}) custom-call(bf16[8,32,256]{2,1,0:T(8,128)(2,1)S(1)} %copy-done, bf16[8,2,512,256]{3,2,1,0:T(8,128)(2,1)} %orb_hbm.3, bf16[64,512]{1,0:T(8,128)(2,1)S(1)} %get-tuple-element.24.edge_hbm.refs_0_), custom_call_target="tpu_custom_call" | custom-call | bytes 4194304 | tf_op jit(solution)/shard_map/pallas_call | solution.py:369
  10.0 0.6 %collective-permute-done.5.refs_6_ = bf16[64,512]{1,0:T(8,128)(2,1)S(1)} collective-permute-done((bf16[64,512]{1,0:T(8,128)(2,1)S(1)}, bf16[64,512]{1,0:T(8,128)(2,1)S(1)}, u32[]{:S(2)}, u32[]{:S(2)}) %collective-permute-start.5) | collective-permute-done | bytes 65568 | tf_op jit(solution)/shard_map/ppermute | solution.py:329
  10.6 1.8 %collective-permute-done.3.refs_4_ = bf16[64,512]{1,0:T(8,128)(2,1)S(1)} collective-permute-done((bf16[64,512]{1,0:T(8,128)(2,1)S(1)}, bf16[64,512]{1,0:T(8,128)(2,1)S(1)}, u32[]{:S(2)}, u32[]{:S(2)}) %collective-permute-start.3) | collective-permute-done | bytes 65568 | tf_op jit(solution)/shard_map/ppermute | solution.py:329
  12.3 1.0 %collective-permute-done.1.refs_2_ = bf16[64,512]{1,0:T(8,128)(2,1)S(1)} collective-permute-done((bf16[64,512]{1,0:T(8,128)(2,1)S(1)}, bf16[64,512]{1,0:T(8,128)(2,1)S(1)}, u32[]{:S(2)}, u32[]{:S(2)}) %collective-permute-start.1) | collective-permute-done | bytes 65568 | tf_op jit(solution)/shard_map/ppermute | solution.py:329
  13.6 1.0 %collective-permute-done.2.refs_3_ = bf16[64,512]{1,0:T(8,128)(2,1)S(1)} collective-permute-done((bf16[64,512]{1,0:T(8,128)(2,1)S(1)}, bf16[64,512]{1,0:T(8,128)(2,1)S(1)}, u32[]{:S(2)}, u32[]{:S(2)}) %collective-permute-start.2) | collective-permute-done | bytes 65568 | tf_op jit(solution)/shard_map/ppermute | solution.py:329
  14.6 1.4 %shard_map.57 = (bf16[192,256]{1,0:T(8,128)(2,1)S(1)}, bf16[192,256]{1,0:T(8,128)(2,1)S(1)}, bf16[192,256]{1,0:T(8,128)(2,1)S(1)}, bf16[192,256]{1,0:T(8,128)(2,1)S(1)}, bf16[4,8,16,1024]{3,2,1,0:T(8,128)(2,1)S(1)}) custom-call(bf16[64,512]{1,0:T(8,128)(2,1)S(1)} %get-tuple-element.24.edge_hbm.refs_0_, bf16[64,512]{1,0:T(8,128)(2,1)S(1)} %collective-permute-done.refs_1_, ...), custom_call_target="tpu_custom_call" | custom-call | bytes 6291456 | tf_op jit(solution)/shard_map/pallas_call | solution.py:397
  15.9 2.5 %collective-permute-start.7 = (bf16[192,256]{1,0:T(8,128)(2,1)S(1)}, bf16[192,256]{1,0:T(8,128)(2,1)S(1)}, u32[]{:S(2)}, u32[]{:S(2)}) collective-permute-start(bf16[192,256]{1,0:T(8,128)(2,1)S(1)} %get-tuple-element.29), channel_id=1, source_target_pairs={{0,24},{8,16},{16,8},{24,0},{1,25},{9,17},{17,9},{25,1},{2,26},{10... | collective-permute-start | bytes 294920 | tf_op jit(solution)/shard_map/ppermute | solution.py:329
  18.5 0.5 %collective-permute-start.8 = (bf16[192,256]{1,0:T(8,128)(2,1)S(1)}, bf16[192,256]{1,0:T(8,128)(2,1)S(1)}, u32[]{:S(2)}, u32[]{:S(2)}) collective-permute-start(bf16[192,256]{1,0:T(8,128)(2,1)S(1)} %get-tuple-element.30), channel_id=1, source_target_pairs={{0,16},{8,24},{16,0},{24,8},{1,17},{9,25},{17,1},{25,9},{2,18},{10... | collective-permute-start | bytes 294920 | tf_op jit(solution)/shard_map/ppermute | solution.py:329
  19.0 0.5 %collective-permute-start.9 = (bf16[192,256]{1,0:T(8,128)(2,1)S(1)}, bf16[192,256]{1,0:T(8,128)(2,1)S(1)}, u32[]{:S(2)}, u32[]{:S(2)}) collective-permute-start(bf16[192,256]{1,0:T(8,128)(2,1)S(1)} %get-tuple-element.31), channel_id=1, source_target_pairs={{0,8},{8,0},{16,24},{24,16},{1,9},{9,1},{17,25},{25,17},{2,10},{10... | collective-permute-start | bytes 294920 | tf_op jit(solution)/shard_map/ppermute | solution.py:329
  19.5 2.4 %collective-permute-done.7.refs_0_ = bf16[192,256]{1,0:T(8,128)(2,1)S(1)} collective-permute-done((bf16[192,256]{1,0:T(8,128)(2,1)S(1)}, bf16[192,256]{1,0:T(8,128)(2,1)S(1)}, u32[]{:S(2)}, u32[]{:S(2)}) %collective-permute-start.7) | collective-permute-done | bytes 98336 | tf_op jit(solution)/shard_map/ppermute | solution.py:329
  21.9 2.0 %collective-permute-done.8.refs_1_ = bf16[192,256]{1,0:T(8,128)(2,1)S(1)} collective-permute-done((bf16[192,256]{1,0:T(8,128)(2,1)S(1)}, bf16[192,256]{1,0:T(8,128)(2,1)S(1)}, u32[]{:S(2)}, u32[]{:S(2)}) %collective-permute-start.8) | collective-permute-done | bytes 98336 | tf_op jit(solution)/shard_map/ppermute | solution.py:329
  23.9 0.6 %shard_map.58 = (bf16[128,256]{1,0:T(8,128)(2,1)S(1)}, bf16[128,256]{1,0:T(8,128)(2,1)S(1)}, bf16[128,256]{1,0:T(8,128)(2,1)S(1)}, bf16[128,256]{1,0:T(8,128)(2,1)S(1)}) custom-call(bf16[192,256]{1,0:T(8,128)(2,1)S(1)} %collective-permute-done.7.refs_0_, bf16[192,256]{1,0:T(8,128)(2,1)S(1)} %collective-permute-done.8.refs_1_, ...), custom_call_target="tpu_custom_call" | custom-call | bytes 2097152 | tf_op jit(solution)/shard_map/pallas_call | solution.py:409
  24.5 1.8 %collective-permute-start.10 = (bf16[128,256]{1,0:T(8,128)(2,1)S(1)}, bf16[128,256]{1,0:T(8,128)(2,1)S(1)}, u32[]{:S(2)}, u32[]{:S(2)}) collective-permute-start(bf16[128,256]{1,0:T(8,128)(2,1)S(1)} %get-tuple-element.33), channel_id=1, source_target_pairs={{0,24},{8,16},{16,8},{24,0},{1,25},{9,17},{17,9},{25,1},{2,26},{10... | collective-permute-start | bytes 196616 | tf_op jit(solution)/shard_map/ppermute | solution.py:329
  26.3 1.3 %collective-permute-start.11 = (bf16[128,256]{1,0:T(8,128)(2,1)S(1)}, bf16[128,256]{1,0:T(8,128)(2,1)S(1)}, u32[]{:S(2)}, u32[]{:S(2)}) collective-permute-start(bf16[128,256]{1,0:T(8,128)(2,1)S(1)} %get-tuple-element.34), channel_id=1, source_target_pairs={{0,16},{8,24},{16,0},{24,8},{1,17},{9,25},{17,1},{25,9},{2,18},{10... | collective-permute-start | bytes 196616 | tf_op jit(solution)/shard_map/ppermute | solution.py:329
  27.6 0.5 %collective-permute-start.12 = (bf16[128,256]{1,0:T(8,128)(2,1)S(1)}, bf16[128,256]{1,0:T(8,128)(2,1)S(1)}, u32[]{:S(2)}, u32[]{:S(2)}) collective-permute-start(bf16[128,256]{1,0:T(8,128)(2,1)S(1)} %get-tuple-element.35), channel_id=1, source_target_pairs={{0,8},{8,0},{16,24},{24,16},{1,9},{9,1},{17,25},{25,17},{2,10},{10... | collective-permute-start | bytes 196616 | tf_op jit(solution)/shard_map/ppermute | solution.py:329
  28.1 2.1 %collective-permute-done.10.refs_0_ = bf16[128,256]{1,0:T(8,128)(2,1)S(1)} collective-permute-done((bf16[128,256]{1,0:T(8,128)(2,1)S(1)}, bf16[128,256]{1,0:T(8,128)(2,1)S(1)}, u32[]{:S(2)}, u32[]{:S(2)}) %collective-permute-start.10) | collective-permute-done | bytes 65568 | tf_op jit(solution)/shard_map/ppermute | solution.py:329
  30.2 0.5 %collective-permute-done.11.refs_1_ = bf16[128,256]{1,0:T(8,128)(2,1)S(1)} collective-permute-done((bf16[128,256]{1,0:T(8,128)(2,1)S(1)}, bf16[128,256]{1,0:T(8,128)(2,1)S(1)}, u32[]{:S(2)}, u32[]{:S(2)}) %collective-permute-start.11) | collective-permute-done | bytes 65568 | tf_op jit(solution)/shard_map/ppermute | solution.py:329
  30.7 1.1 %collective-permute-done.12.refs_2_ = bf16[128,256]{1,0:T(8,128)(2,1)S(1)} collective-permute-done((bf16[128,256]{1,0:T(8,128)(2,1)S(1)}, bf16[128,256]{1,0:T(8,128)(2,1)S(1)}, u32[]{:S(2)}, u32[]{:S(2)}) %collective-permute-start.12) | collective-permute-done | bytes 65568 | tf_op jit(solution)/shard_map/ppermute | solution.py:329
  31.9 0.6 %shard_map.59 = (bf16[3,64,512]{2,1,0:T(8,128)(2,1)S(1)}, bf16[4,128,1024]{2,1,0:T(8,128)(2,1)S(1)}) custom-call(bf16[128,256]{1,0:T(8,128)(2,1)S(1)} %collective-permute-done.10.refs_0_, bf16[128,256]{1,0:T(8,128)(2,1)S(1)} %collective-permute-done.11.refs_1_, bf16[128,256]{1,0:T(8,128)(2,1)S(1)} %collective-permute-done.12.refs_2_, ...), custom_call_target="tpu_custom_call" | custom-call | tf_op jit(solution)/shard_map/pallas_call | solution.py:425
  32.6 0.5 %shard_map.60.refs_0_ = bf16[1,64,512]{2,1,0:T(8,128)(2,1)S(1)} custom-call(bf16[4,128,1024]{2,1,0:T(8,128)(2,1)S(1)} %get-tuple-element.37.right_ref, bf16[8,2,512,128]{3,2,1,0:T(8,128)(2,1)S(1)} %get-tuple-element.26.refs_8_.refs_4_.orb_ref, bf16[8,2,512,128]{3,2,1,0:T(8,128)(2,1)S(1)} %get-tuple-element.27.refs_9_.refs_5_.rest_ref, ...), custom_call_target="tpu_custom_call" | custom-call | tf_op jit(solution)/shard_map/pallas_call | solution.py:436
  33.0 0.6 %collective-permute-start.17 = (bf16[1,64,512]{2,1,0:T(8,128)(2,1)S(1)}, bf16[1,64,512]{2,1,0:T(8,128)(2,1)S(1)}, u32[]{:S(2)}, u32[]{:S(2)}) collective-permute-start(bf16[1,64,512]{2,1,0:T(8,128)(2,1)S(1)} %shard_map.60.refs_0_), channel_id=1, source_target_pairs={{0,1},{1,0},{2,3},{3,2},{4,5},{5,4},{6,7},{7,6},{8,9},{9,8},{10,11... | collective-permute-start | bytes 196616 | tf_op jit(solution)/shard_map/ppermute | solution.py:329
  33.6 0.6 %shard_map.61.keep_ref = f32[3,64,512]{2,1,0:T(8,128)S(1)} custom-call(bf16[4,128,1024]{2,1,0:T(8,128)(2,1)S(1)} %get-tuple-element.37.right_ref, bf16[8,2,512,128]{3,2,1,0:T(8,128)(2,1)S(1)} %get-tuple-element.26.refs_8_.refs_4_.orb_ref, bf16[8,2,512,128]{3,2,1,0:T(8,128)(2,1)S(1)} %get-tuple-element.27.refs_9_.refs_5_.rest_ref, ...), custom_call_target="tpu_custom_call" | custom-call | tf_op jit(solution)/shard_map/pallas_call | solution.py:436
  34.2 1.6 %collective-permute-start.14 = (bf16[64,512]{1,0:T(8,128)(2,1)S(1)}, bf16[64,512]{1,0:T(8,128)(2,1)S(1)}, u32[]{:S(2)}, u32[]{:S(2)}) collective-permute-start(bf16[64,512]{1,0:T(8,128)(2,1)S(1)} %get-tuple-element.39), channel_id=1, source_target_pairs={{0,2},{1,3},{2,4},{3,5},{4,6},{5,7},{6,0},{7,1},{8,10},{9,11},{10,... | collective-permute-start | bytes 196616 | tf_op jit(solution)/shard_map/ppermute | solution.py:341
  35.8 1.2 %collective-permute-start.15 = (bf16[64,512]{1,0:T(8,128)(2,1)S(1)}, bf16[64,512]{1,0:T(8,128)(2,1)S(1)}, u32[]{:S(2)}, u32[]{:S(2)}) collective-permute-start(bf16[64,512]{1,0:T(8,128)(2,1)S(1)} %get-tuple-element.40), channel_id=1, source_target_pairs={{0,4},{1,5},{2,6},{3,7},{4,0},{5,1},{6,2},{7,3},{8,12},{9,13},{10,... | collective-permute-start | bytes 196616 | tf_op jit(solution)/shard_map/ppermute | solution.py:341
  37.0 2.1 %collective-permute-start.16 = (bf16[64,512]{1,0:T(8,128)(2,1)S(1)}, bf16[64,512]{1,0:T(8,128)(2,1)S(1)}, u32[]{:S(2)}, u32[]{:S(2)}) collective-permute-start(bf16[64,512]{1,0:T(8,128)(2,1)S(1)} %get-tuple-element.41.refs_0_), channel_id=1, source_target_pairs={{0,6},{1,7},{2,0},{3,1},{4,2},{5,3},{6,4},{7,5},{8,14},{9,15},{10,... | collective-permute-start | bytes 196616 | tf_op jit(solution)/shard_map/ppermute | solution.py:341
  39.2 0.5 %shard_map.63.keep_ref = f32[1,64,512]{2,1,0:T(8,128)S(1)} custom-call(bf16[4,128,1024]{2,1,0:T(8,128)(2,1)S(1)} %get-tuple-element.37.right_ref, bf16[8,2,512,128]{3,2,1,0:T(8,128)(2,1)S(1)} %get-tuple-element.26.refs_8_.refs_4_.orb_ref, bf16[8,2,512,128]{3,2,1,0:T(8,128)(2,1)S(1)} %get-tuple-element.27.refs_9_.refs_5_.rest_ref, ...), custom_call_target="tpu_custom_call" | custom-call | tf_op jit(solution)/shard_map/pallas_call | solution.py:436
  39.7 1.4 %collective-permute-done.14.refs_0_ = bf16[64,512]{1,0:T(8,128)(2,1)S(1)} collective-permute-done((bf16[64,512]{1,0:T(8,128)(2,1)S(1)}, bf16[64,512]{1,0:T(8,128)(2,1)S(1)}, u32[]{:S(2)}, u32[]{:S(2)}) %collective-permute-start.14) | collective-permute-done | bytes 65568 | tf_op jit(solution)/shard_map/ppermute | solution.py:341
  41.1 1.9 %collective-permute-done.15.refs_1_ = bf16[64,512]{1,0:T(8,128)(2,1)S(1)} collective-permute-done((bf16[64,512]{1,0:T(8,128)(2,1)S(1)}, bf16[64,512]{1,0:T(8,128)(2,1)S(1)}, u32[]{:S(2)}, u32[]{:S(2)}) %collective-permute-start.15) | collective-permute-done | bytes 65568 | tf_op jit(solution)/shard_map/ppermute | solution.py:341
  43.0 1.7 %shard_map.65 = bf16[64,4,16,128]{3,2,1,0:T(8,128)(2,1)} custom-call(bf16[64,512]{1,0:T(8,128)(2,1)S(1)} %collective-permute-done.14.refs_0_, bf16[64,512]{1,0:T(8,128)(2,1)S(1)} %collective-permute-done.15.refs_1_, bf16[64,512]{1,0:T(8,128)(2,1)S(1)} %collective-permute-done.16.refs_2_, f32[64,512]{1,0:T(8,128)S(1)} %shard_map.64.refs_3_, ...), custom_call_target="tpu_custom_call" | custom-call | bytes 4194304 | tf_op jit(solution)/shard_map/pallas_call | solution.py:454
  (23 shorter events, 0.6 us)
Async XLA Ops:
  0.0 8.3 %copy-start = (bf16[8,32,256]{2,1,0:T(8,128)(2,1)S(1)}, bf16[8,32,256]{2,1,0:T(8,128)(2,1)}, u32[]{:S(2)}) copy-start(bf16[8,32,256]{2,1,0:T(8,128)(2,1)} %coulomb_ref.1) | copy-start | bytes 393220
  2.5 12.0 %copy-start.1 = (bf16[2,256,128]{2,1,0:T(8,128)(2,1)S(1)}, bf16[2,256,128]{2,1,0:T(8,128)(2,1)}, u32[]{:S(2)}) copy-start(bf16[2,256,128]{2,1,0:T(8,128)(2,1)} %constant.6.clone.refs_10_) | copy-start | bytes 393220
  2.6 8.0 %collective-permute-start.5 = (bf16[64,512]{1,0:T(8,128)(2,1)S(1)}, bf16[64,512]{1,0:T(8,128)(2,1)S(1)}, u32[]{:S(2)}, u32[]{:S(2)}) collective-permute-start(bf16[64,512]{1,0:T(8,128)(2,1)S(1)} %get-tuple-element.24.edge_hbm.refs_0_), channel_id=1, source_target_pairs={{0,6},{1,7},{2,4},{3,5},{4,2},{5,3},{6,0},{7,1},{8,14},{9,15},{10,... | collective-permute-start | bytes 196616 | tf_op jit(solution)/shard_map/ppermute | solution.py:329
  7.7 4.7 %collective-permute-start.3 = (bf16[64,512]{1,0:T(8,128)(2,1)S(1)}, bf16[64,512]{1,0:T(8,128)(2,1)S(1)}, u32[]{:S(2)}, u32[]{:S(2)}) collective-permute-start(bf16[64,512]{1,0:T(8,128)(2,1)S(1)} %get-tuple-element.24.edge_hbm.refs_0_), channel_id=1, source_target_pairs={{0,2},{1,3},{2,0},{3,1},{4,6},{5,7},{6,4},{7,5},{8,10},{9,11},{10,... | collective-permute-start | bytes 196616 | tf_op jit(solution)/shard_map/ppermute | solution.py:329
  7.7 5.6 %collective-permute-start.1 = (bf16[64,512]{1,0:T(8,128)(2,1)S(1)}, bf16[64,512]{1,0:T(8,128)(2,1)S(1)}, u32[]{:S(2)}, u32[]{:S(2)}) collective-permute-start(bf16[64,512]{1,0:T(8,128)(2,1)S(1)} %get-tuple-element.24.edge_hbm.refs_0_), channel_id=1, source_target_pairs={{0,4},{1,5},{2,6},{3,7},{4,0},{5,1},{6,2},{7,3},{8,12},{9,13},{10,... | collective-permute-start | bytes 196616 | tf_op jit(solution)/shard_map/ppermute | solution.py:329
  9.9 3.4 %collective-permute-start = (bf16[64,512]{1,0:T(8,128)(2,1)S(1)}, bf16[64,512]{1,0:T(8,128)(2,1)S(1)}, u32[]{:S(2)}, u32[]{:S(2)}) collective-permute-start(bf16[64,512]{1,0:T(8,128)(2,1)S(1)} %get-tuple-element.25), channel_id=1, source_target_pairs={{0,1},{1,0},{2,3},{3,2},{4,5},{5,4},{6,7},{7,6},{8,9},{9,8},{10,11... | collective-permute-start | bytes 196616 | tf_op jit(solution)/shard_map/ppermute | solution.py:329
  10.6 2.7 %collective-permute-start.6 = (bf16[64,512]{1,0:T(8,128)(2,1)S(1)}, bf16[64,512]{1,0:T(8,128)(2,1)S(1)}, u32[]{:S(2)}, u32[]{:S(2)}) collective-permute-start(bf16[64,512]{1,0:T(8,128)(2,1)S(1)} %collective-permute-done.5.refs_6_), channel_id=1, source_target_pairs={{0,1},{1,0},{2,3},{3,2},{4,5},{5,4},{6,7},{7,6},{8,9},{9,8},{10,11... | collective-permute-start | bytes 196616 | tf_op jit(solution)/shard_map/ppermute | solution.py:329
  12.3 1.3 %collective-permute-start.4 = (bf16[64,512]{1,0:T(8,128)(2,1)S(1)}, bf16[64,512]{1,0:T(8,128)(2,1)S(1)}, u32[]{:S(2)}, u32[]{:S(2)}) collective-permute-start(bf16[64,512]{1,0:T(8,128)(2,1)S(1)} %collective-permute-done.3.refs_4_), channel_id=1, source_target_pairs={{0,1},{1,0},{2,3},{3,2},{4,5},{5,4},{6,7},{7,6},{8,9},{9,8},{10,11... | collective-permute-start | bytes 196616 | tf_op jit(solution)/shard_map/ppermute | solution.py:329
  13.3 1.3 %collective-permute-start.2 = (bf16[64,512]{1,0:T(8,128)(2,1)S(1)}, bf16[64,512]{1,0:T(8,128)(2,1)S(1)}, u32[]{:S(2)}, u32[]{:S(2)}) collective-permute-start(bf16[64,512]{1,0:T(8,128)(2,1)S(1)} %collective-permute-done.1.refs_2_), channel_id=1, source_target_pairs={{0,1},{1,0},{2,3},{3,2},{4,5},{5,4},{6,7},{7,6},{8,9},{9,8},{10,11... | collective-permute-start | bytes 196616 | tf_op jit(solution)/shard_map/ppermute | solution.py:329
  14.6 9.4 %copy-start.2 = (bf16[64,128]{1,0:T(8,128)(2,1)S(1)}, bf16[64,128]{1,0:T(8,128)(2,1)}, u32[]{:S(2)}) copy-start(bf16[64,128]{1,0:T(8,128)(2,1)} %constant.8.clone.refs_5_) | copy-start | bytes 49156
  14.6 9.4 %copy-start.3 = (bf16[64,128]{1,0:T(8,128)(2,1)S(1)}, bf16[64,128]{1,0:T(8,128)(2,1)}, u32[]{:S(2)}) copy-start(bf16[64,128]{1,0:T(8,128)(2,1)} %constant.7.clone.refs_4_) | copy-start | bytes 49156
  15.9 5.9 %collective-permute-start.7 = (bf16[192,256]{1,0:T(8,128)(2,1)S(1)}, bf16[192,256]{1,0:T(8,128)(2,1)S(1)}, u32[]{:S(2)}, u32[]{:S(2)}) collective-permute-start(bf16[192,256]{1,0:T(8,128)(2,1)S(1)} %get-tuple-element.29), channel_id=1, source_target_pairs={{0,24},{8,16},{16,8},{24,0},{1,25},{9,17},{17,9},{25,1},{2,26},{10... | collective-permute-start | bytes 294920 | tf_op jit(solution)/shard_map/ppermute | solution.py:329
  18.5 5.4 %collective-permute-start.8 = (bf16[192,256]{1,0:T(8,128)(2,1)S(1)}, bf16[192,256]{1,0:T(8,128)(2,1)S(1)}, u32[]{:S(2)}, u32[]{:S(2)}) collective-permute-start(bf16[192,256]{1,0:T(8,128)(2,1)S(1)} %get-tuple-element.30), channel_id=1, source_target_pairs={{0,16},{8,24},{16,0},{24,8},{1,17},{9,25},{17,1},{25,9},{2,18},{10... | collective-permute-start | bytes 294920 | tf_op jit(solution)/shard_map/ppermute | solution.py:329
  19.0 5.0 %collective-permute-start.9 = (bf16[192,256]{1,0:T(8,128)(2,1)S(1)}, bf16[192,256]{1,0:T(8,128)(2,1)S(1)}, u32[]{:S(2)}, u32[]{:S(2)}) collective-permute-start(bf16[192,256]{1,0:T(8,128)(2,1)S(1)} %get-tuple-element.31), channel_id=1, source_target_pairs={{0,8},{8,0},{16,24},{24,16},{1,9},{9,1},{17,25},{25,17},{2,10},{10... | collective-permute-start | bytes 294920 | tf_op jit(solution)/shard_map/ppermute | solution.py:329
  24.5 5.7 %collective-permute-start.10 = (bf16[128,256]{1,0:T(8,128)(2,1)S(1)}, bf16[128,256]{1,0:T(8,128)(2,1)S(1)}, u32[]{:S(2)}, u32[]{:S(2)}) collective-permute-start(bf16[128,256]{1,0:T(8,128)(2,1)S(1)} %get-tuple-element.33), channel_id=1, source_target_pairs={{0,24},{8,16},{16,8},{24,0},{1,25},{9,17},{17,9},{25,1},{2,26},{10... | collective-permute-start | bytes 196616 | tf_op jit(solution)/shard_map/ppermute | solution.py:329
  26.3 4.4 %collective-permute-start.11 = (bf16[128,256]{1,0:T(8,128)(2,1)S(1)}, bf16[128,256]{1,0:T(8,128)(2,1)S(1)}, u32[]{:S(2)}, u32[]{:S(2)}) collective-permute-start(bf16[128,256]{1,0:T(8,128)(2,1)S(1)} %get-tuple-element.34), channel_id=1, source_target_pairs={{0,16},{8,24},{16,0},{24,8},{1,17},{9,25},{17,1},{25,9},{2,18},{10... | collective-permute-start | bytes 196616 | tf_op jit(solution)/shard_map/ppermute | solution.py:329
  27.6 4.3 %collective-permute-start.12 = (bf16[128,256]{1,0:T(8,128)(2,1)S(1)}, bf16[128,256]{1,0:T(8,128)(2,1)S(1)}, u32[]{:S(2)}, u32[]{:S(2)}) collective-permute-start(bf16[128,256]{1,0:T(8,128)(2,1)S(1)} %get-tuple-element.35), channel_id=1, source_target_pairs={{0,8},{8,0},{16,24},{24,16},{1,9},{9,1},{17,25},{25,17},{2,10},{10... | collective-permute-start | bytes 196616 | tf_op jit(solution)/shard_map/ppermute | solution.py:329
  32.5 1.7 %collective-permute-start.13 = (bf16[3,64,512]{2,1,0:T(8,128)(2,1)S(1)}, bf16[3,64,512]{2,1,0:T(8,128)(2,1)S(1)}, u32[]{:S(2)}, u32[]{:S(2)}) collective-permute-start(bf16[3,64,512]{2,1,0:T(8,128)(2,1)S(1)} %get-tuple-element.38.refs_0_), channel_id=1, source_target_pairs={{0,1},{1,0},{2,3},{3,2},{4,5},{5,4},{6,7},{7,6},{8,9},{9,8},{10,11... | collective-permute-start | bytes 589832 | tf_op jit(solution)/shard_map/ppermute | solution.py:329
  33.0 6.6 %collective-permute-start.17 = (bf16[1,64,512]{2,1,0:T(8,128)(2,1)S(1)}, bf16[1,64,512]{2,1,0:T(8,128)(2,1)S(1)}, u32[]{:S(2)}, u32[]{:S(2)}) collective-permute-start(bf16[1,64,512]{2,1,0:T(8,128)(2,1)S(1)} %shard_map.60.refs_0_), channel_id=1, source_target_pairs={{0,1},{1,0},{2,3},{3,2},{4,5},{5,4},{6,7},{7,6},{8,9},{9,8},{10,11... | collective-permute-start | bytes 196616 | tf_op jit(solution)/shard_map/ppermute | solution.py:329
  34.2 6.9 %collective-permute-start.14 = (bf16[64,512]{1,0:T(8,128)(2,1)S(1)}, bf16[64,512]{1,0:T(8,128)(2,1)S(1)}, u32[]{:S(2)}, u32[]{:S(2)}) collective-permute-start(bf16[64,512]{1,0:T(8,128)(2,1)S(1)} %get-tuple-element.39), channel_id=1, source_target_pairs={{0,2},{1,3},{2,4},{3,5},{4,6},{5,7},{6,0},{7,1},{8,10},{9,11},{10,... | collective-permute-start | bytes 196616 | tf_op jit(solution)/shard_map/ppermute | solution.py:341
  35.8 7.2 %collective-permute-start.15 = (bf16[64,512]{1,0:T(8,128)(2,1)S(1)}, bf16[64,512]{1,0:T(8,128)(2,1)S(1)}, u32[]{:S(2)}, u32[]{:S(2)}) collective-permute-start(bf16[64,512]{1,0:T(8,128)(2,1)S(1)} %get-tuple-element.40), channel_id=1, source_target_pairs={{0,4},{1,5},{2,6},{3,7},{4,0},{5,1},{6,2},{7,3},{8,12},{9,13},{10,... | collective-permute-start | bytes 196616 | tf_op jit(solution)/shard_map/ppermute | solution.py:341
  37.0 6.0 %collective-permute-start.16 = (bf16[64,512]{1,0:T(8,128)(2,1)S(1)}, bf16[64,512]{1,0:T(8,128)(2,1)S(1)}, u32[]{:S(2)}, u32[]{:S(2)}) collective-permute-start(bf16[64,512]{1,0:T(8,128)(2,1)S(1)} %get-tuple-element.41.refs_0_), channel_id=1, source_target_pairs={{0,6},{1,7},{2,0},{3,1},{4,2},{5,3},{6,4},{7,5},{8,14},{9,15},{10,... | collective-permute-start | bytes 196616 | tf_op jit(solution)/shard_map/ppermute | solution.py:341

commit v26 on v18

--- a/solution.py
+++ b/solution.py
@@ -91,9 +91,13 @@
 
 def load_copies(orb_hbm, orb_ref, sems, start):
     lanes = pl.ds(start, orb_ref.shape[3])
+    count = sems.shape[0]
+    step = orb_ref.shape[0] // count
     copies = [
-        pltpu.make_async_copy(orb_hbm.at[k, :, :, lanes], orb_ref.at[k], sems.at[k])
-        for k in range(orb_ref.shape[0])
+        pltpu.make_async_copy(
+            orb_hbm.at[pl.ds(i * step, step), :, :, lanes], orb_ref.at[pl.ds(i * step, step)], sems.at[i]
+        )
+        for i in range(count)
     ]
     for copy in copies:
         copy.start()
@@ -118,8 +122,8 @@
     group = ROWS // (2 * per_block)
     for g in range(local_k // group):
         rows = []
+        copies[g].wait()
         for k in range(g * group, (g + 1) * group):
-            copies[k].wait()
             both = jnp.concatenate([orb_ref[k, 0], orb_ref[k, 1]], axis=1)
             rows.append(dot(chosen, both, ((1,), (1,))))
         edge_ref[g * ROWS : (g + 1) * ROWS] = jnp.concatenate(rows, axis=0).astype(BF16)
@@ -356,7 +360,7 @@
             shape((local_k, 2, norb, LANES), BF16),
         ],
         0,
-        [pltpu.SemaphoreType.DMA((local_k,))],
+        [pltpu.SemaphoreType.DMA((local_k // group,))],
         limit=50,
         size=4 * MIB,
         unread=1,
@@ -365,7 +369,7 @@
         rest_kernel,
         [shape(edge.shape, BF16), shape((local_k, 2, norb, points - LANES), BF16)],
         0,
-        [pltpu.SemaphoreType.DMA((local_k,)), pltpu.SemaphoreType.DMA],
+        [pltpu.SemaphoreType.DMA((local_k // group,)), pltpu.SemaphoreType.DMA],
         limit=49,
         size=4 * MIB,
         unread=2,

time: 44.8 us -> 44.4 us (level)
  no operation moved by 1% of the time
where the time goes in v26:
time: 44.4 us; the launch traced here: 44.2 us
  starting transfers between devices  18.5 us (42%)
  waiting for transfers between devices  16.1 us (36%)
  Pallas kernels  9.44 us (21%)
    ppermute x15, starting transfers between devices, swap(): return lax.ppermute(value, axis, [(i, i ^ mask) for i in range(size)])  13.6 us
    ppermute x15, waiting for transfers between devices, swap(): return lax.ppermute(value, axis, [(i, i ^ mask) for i in range(size)])  12.8 us
    ppermute x3, starting transfers between devices, shift_along(): came.append(lax.ppermute(pieces[s], 'pts', pairs))  4.93 us
    ppermute x3, waiting for transfers between devices, shift_along(): came.append(lax.ppermute(pieces[s], 'pts', pairs))  3.32 us
    pallas_call x1, Pallas kernels, body(): call(functools.partial(edge_kernel, per_block), [shape((local_k * 2 * per...  2.09 us
    pallas_call x1, Pallas kernels, body(): call(functools.partial(exchange_kernel, chunks, 1.0 / math.sqrt(points *...  1.66 us
    pallas_call x1, Pallas kernels, body(): call(rest_kernel, [shape(edge.shape, BF16), shape((local_k, 2, norb, poin...  1.56 us
    pallas_call x3, Pallas kernels, rows_of(): call(functools.partial(next_weight_kernel, offsets, flip, out_rows), shap...  1.51 us
  transfers between devices with their start and end apart: 18, of which 13 were waited for; matrix products, arithmetic and copies ran while one was open for 0% of the time, Pallas kernels for 7%

profile of v26, /device:TPU:0, one launch (start us, length us, event | category | flops | bytes accessed | tf_op | source)
XLA Modules:
  0.0 44.2 jit_solution(13763414063551512286)
XLA Ops:
  0.0 2.1 %shard_map.55 = (bf16[64,512]{1,0:T(8,128)(2,1)S(1)}, bf16[8,2,512,128]{3,2,1,0:T(8,128)(2,1)S(1)}) custom-call(bf16[8,2,512,256]{3,2,1,0:T(8,128)(2,1)} %orb_hbm.3), custom_call_target="tpu_custom_call" | custom-call | bytes 4194304 | tf_op jit(solution)/shard_map/pallas_call | solution.py:356
  2.1 5.1 %collective-permute-start.5 = (bf16[64,512]{1,0:T(8,128)(2,1)S(1)}, bf16[64,512]{1,0:T(8,128)(2,1)S(1)}, u32[]{:S(2)}, u32[]{:S(2)}) collective-permute-start(bf16[64,512]{1,0:T(8,128)(2,1)S(1)} %get-tuple-element.23.edge_hbm.refs_0_), channel_id=1, source_target_pairs={{0,6},{1,7},{2,4},{3,5},{4,2},{5,3},{6,0},{7,1},{8,14},{9,15},{10,... | collective-permute-start | bytes 196616 | tf_op jit(solution)/shard_map/ppermute | solution.py:328
  7.2 0.6 %collective-permute-start.1 = (bf16[64,512]{1,0:T(8,128)(2,1)S(1)}, bf16[64,512]{1,0:T(8,128)(2,1)S(1)}, u32[]{:S(2)}, u32[]{:S(2)}) collective-permute-start(bf16[64,512]{1,0:T(8,128)(2,1)S(1)} %get-tuple-element.23.edge_hbm.refs_0_), channel_id=1, source_target_pairs={{0,4},{1,5},{2,6},{3,7},{4,0},{5,1},{6,2},{7,3},{8,12},{9,13},{10,... | collective-permute-start | bytes 196616 | tf_op jit(solution)/shard_map/ppermute | solution.py:328
  7.9 1.6 %shard_map.56 = (bf16[64,512]{1,0:T(8,128)(2,1)S(1)}, bf16[8,2,512,128]{3,2,1,0:T(8,128)(2,1)S(1)}) custom-call(bf16[8,2,512,256]{3,2,1,0:T(8,128)(2,1)} %orb_hbm.3, bf16[64,512]{1,0:T(8,128)(2,1)S(1)} %get-tuple-element.23.edge_hbm.refs_0_), custom_call_target="tpu_custom_call" | custom-call | bytes 4194304 | tf_op jit(solution)/shard_map/pallas_call | solution.py:368
  9.5 0.6 %collective-permute-done.5.refs_6_ = bf16[64,512]{1,0:T(8,128)(2,1)S(1)} collective-permute-done((bf16[64,512]{1,0:T(8,128)(2,1)S(1)}, bf16[64,512]{1,0:T(8,128)(2,1)S(1)}, u32[]{:S(2)}, u32[]{:S(2)}) %collective-permute-start.5) | collective-permute-done | bytes 65568 | tf_op jit(solution)/shard_map/ppermute | solution.py:328
  10.1 1.8 %collective-permute-done.3.refs_4_ = bf16[64,512]{1,0:T(8,128)(2,1)S(1)} collective-permute-done((bf16[64,512]{1,0:T(8,128)(2,1)S(1)}, bf16[64,512]{1,0:T(8,128)(2,1)S(1)}, u32[]{:S(2)}, u32[]{:S(2)}) %collective-permute-start.3) | collective-permute-done | bytes 65568 | tf_op jit(solution)/shard_map/ppermute | solution.py:328
  11.9 1.0 %collective-permute-done.1.refs_2_ = bf16[64,512]{1,0:T(8,128)(2,1)S(1)} collective-permute-done((bf16[64,512]{1,0:T(8,128)(2,1)S(1)}, bf16[64,512]{1,0:T(8,128)(2,1)S(1)}, u32[]{:S(2)}, u32[]{:S(2)}) %collective-permute-start.1) | collective-permute-done | bytes 65568 | tf_op jit(solution)/shard_map/ppermute | solution.py:328
  13.1 1.0 %collective-permute-done.2.refs_3_ = bf16[64,512]{1,0:T(8,128)(2,1)S(1)} collective-permute-done((bf16[64,512]{1,0:T(8,128)(2,1)S(1)}, bf16[64,512]{1,0:T(8,128)(2,1)S(1)}, u32[]{:S(2)}, u32[]{:S(2)}) %collective-permute-start.2) | collective-permute-done | bytes 65568 | tf_op jit(solution)/shard_map/ppermute | solution.py:328
  14.1 1.4 %shard_map.57 = (bf16[192,256]{1,0:T(8,128)(2,1)S(1)}, bf16[192,256]{1,0:T(8,128)(2,1)S(1)}, bf16[192,256]{1,0:T(8,128)(2,1)S(1)}, bf16[192,256]{1,0:T(8,128)(2,1)S(1)}, bf16[4,8,16,1024]{3,2,1,0:T(8,128)(2,1)S(1)}) custom-call(bf16[64,512]{1,0:T(8,128)(2,1)S(1)} %get-tuple-element.23.edge_hbm.refs_0_, bf16[64,512]{1,0:T(8,128)(2,1)S(1)} %collective-permute-done.refs_1_, ...), custom_call_target="tpu_custom_call" | custom-call | bytes 6291456 | tf_op jit(solution)/shard_map/pallas_call | solution.py:392
  15.5 2.5 %collective-permute-start.7 = (bf16[192,256]{1,0:T(8,128)(2,1)S(1)}, bf16[192,256]{1,0:T(8,128)(2,1)S(1)}, u32[]{:S(2)}, u32[]{:S(2)}) collective-permute-start(bf16[192,256]{1,0:T(8,128)(2,1)S(1)} %get-tuple-element.27), channel_id=1, source_target_pairs={{0,24},{8,16},{16,8},{24,0},{1,25},{9,17},{17,9},{25,1},{2,26},{10... | collective-permute-start | bytes 294920 | tf_op jit(solution)/shard_map/ppermute | solution.py:328
  18.0 0.5 %collective-permute-start.8 = (bf16[192,256]{1,0:T(8,128)(2,1)S(1)}, bf16[192,256]{1,0:T(8,128)(2,1)S(1)}, u32[]{:S(2)}, u32[]{:S(2)}) collective-permute-start(bf16[192,256]{1,0:T(8,128)(2,1)S(1)} %get-tuple-element.28), channel_id=1, source_target_pairs={{0,16},{8,24},{16,0},{24,8},{1,17},{9,25},{17,1},{25,9},{2,18},{10... | collective-permute-start | bytes 294920 | tf_op jit(solution)/shard_map/ppermute | solution.py:328
  18.5 0.5 %collective-permute-start.9 = (bf16[192,256]{1,0:T(8,128)(2,1)S(1)}, bf16[192,256]{1,0:T(8,128)(2,1)S(1)}, u32[]{:S(2)}, u32[]{:S(2)}) collective-permute-start(bf16[192,256]{1,0:T(8,128)(2,1)S(1)} %get-tuple-element.29), channel_id=1, source_target_pairs={{0,8},{8,0},{16,24},{24,16},{1,9},{9,1},{17,25},{25,17},{2,10},{10... | collective-permute-start | bytes 294920 | tf_op jit(solution)/shard_map/ppermute | solution.py:328
  19.1 2.4 %collective-permute-done.7.refs_0_ = bf16[192,256]{1,0:T(8,128)(2,1)S(1)} collective-permute-done((bf16[192,256]{1,0:T(8,128)(2,1)S(1)}, bf16[192,256]{1,0:T(8,128)(2,1)S(1)}, u32[]{:S(2)}, u32[]{:S(2)}) %collective-permute-start.7) | collective-permute-done | bytes 98336 | tf_op jit(solution)/shard_map/ppermute | solution.py:328
  21.4 2.0 %collective-permute-done.8.refs_1_ = bf16[192,256]{1,0:T(8,128)(2,1)S(1)} collective-permute-done((bf16[192,256]{1,0:T(8,128)(2,1)S(1)}, bf16[192,256]{1,0:T(8,128)(2,1)S(1)}, u32[]{:S(2)}, u32[]{:S(2)}) %collective-permute-start.8) | collective-permute-done | bytes 98336 | tf_op jit(solution)/shard_map/ppermute | solution.py:328
  23.5 0.6 %shard_map.58 = (bf16[128,256]{1,0:T(8,128)(2,1)S(1)}, bf16[128,256]{1,0:T(8,128)(2,1)S(1)}, bf16[128,256]{1,0:T(8,128)(2,1)S(1)}, bf16[128,256]{1,0:T(8,128)(2,1)S(1)}) custom-call(bf16[192,256]{1,0:T(8,128)(2,1)S(1)} %collective-permute-done.7.refs_0_, bf16[192,256]{1,0:T(8,128)(2,1)S(1)} %collective-permute-done.8.refs_1_, ...), custom_call_target="tpu_custom_call" | custom-call | bytes 2097152 | tf_op jit(solution)/shard_map/pallas_call | solution.py:405
  24.1 1.8 %collective-permute-start.10 = (bf16[128,256]{1,0:T(8,128)(2,1)S(1)}, bf16[128,256]{1,0:T(8,128)(2,1)S(1)}, u32[]{:S(2)}, u32[]{:S(2)}) collective-permute-start(bf16[128,256]{1,0:T(8,128)(2,1)S(1)} %get-tuple-element.31), channel_id=1, source_target_pairs={{0,24},{8,16},{16,8},{24,0},{1,25},{9,17},{17,9},{25,1},{2,26},{10... | collective-permute-start | bytes 196616 | tf_op jit(solution)/shard_map/ppermute | solution.py:328
  25.9 1.3 %collective-permute-start.11 = (bf16[128,256]{1,0:T(8,128)(2,1)S(1)}, bf16[128,256]{1,0:T(8,128)(2,1)S(1)}, u32[]{:S(2)}, u32[]{:S(2)}) collective-permute-start(bf16[128,256]{1,0:T(8,128)(2,1)S(1)} %get-tuple-element.32), channel_id=1, source_target_pairs={{0,16},{8,24},{16,0},{24,8},{1,17},{9,25},{17,1},{25,9},{2,18},{10... | collective-permute-start | bytes 196616 | tf_op jit(solution)/shard_map/ppermute | solution.py:328
  27.2 0.5 %collective-permute-start.12 = (bf16[128,256]{1,0:T(8,128)(2,1)S(1)}, bf16[128,256]{1,0:T(8,128)(2,1)S(1)}, u32[]{:S(2)}, u32[]{:S(2)}) collective-permute-start(bf16[128,256]{1,0:T(8,128)(2,1)S(1)} %get-tuple-element.33), channel_id=1, source_target_pairs={{0,8},{8,0},{16,24},{24,16},{1,9},{9,1},{17,25},{25,17},{2,10},{10... | collective-permute-start | bytes 196616 | tf_op jit(solution)/shard_map/ppermute | solution.py:328
  27.6 2.1 %collective-permute-done.10.refs_0_ = bf16[128,256]{1,0:T(8,128)(2,1)S(1)} collective-permute-done((bf16[128,256]{1,0:T(8,128)(2,1)S(1)}, bf16[128,256]{1,0:T(8,128)(2,1)S(1)}, u32[]{:S(2)}, u32[]{:S(2)}) %collective-permute-start.10) | collective-permute-done | bytes 65568 | tf_op jit(solution)/shard_map/ppermute | solution.py:328
  29.8 0.5 %collective-permute-done.11.refs_1_ = bf16[128,256]{1,0:T(8,128)(2,1)S(1)} collective-permute-done((bf16[128,256]{1,0:T(8,128)(2,1)S(1)}, bf16[128,256]{1,0:T(8,128)(2,1)S(1)}, u32[]{:S(2)}, u32[]{:S(2)}) %collective-permute-start.11) | collective-permute-done | bytes 65568 | tf_op jit(solution)/shard_map/ppermute | solution.py:328
  30.3 1.1 %collective-permute-done.12.refs_2_ = bf16[128,256]{1,0:T(8,128)(2,1)S(1)} collective-permute-done((bf16[128,256]{1,0:T(8,128)(2,1)S(1)}, bf16[128,256]{1,0:T(8,128)(2,1)S(1)}, u32[]{:S(2)}, u32[]{:S(2)}) %collective-permute-start.12) | collective-permute-done | bytes 65568 | tf_op jit(solution)/shard_map/ppermute | solution.py:328
  31.4 0.6 %shard_map.59 = (bf16[3,64,512]{2,1,0:T(8,128)(2,1)S(1)}, bf16[4,128,1024]{2,1,0:T(8,128)(2,1)S(1)}) custom-call(bf16[128,256]{1,0:T(8,128)(2,1)S(1)} %collective-permute-done.10.refs_0_, bf16[128,256]{1,0:T(8,128)(2,1)S(1)} %collective-permute-done.11.refs_1_, bf16[128,256]{1,0:T(8,128)(2,1)S(1)} %collective-permute-done.12.refs_2_, ...), custom_call_target="tpu_custom_call" | custom-call | tf_op jit(solution)/shard_map/pallas_call | solution.py:421
  32.1 0.5 %shard_map.60.refs_0_ = bf16[1,64,512]{2,1,0:T(8,128)(2,1)S(1)} custom-call(bf16[4,128,1024]{2,1,0:T(8,128)(2,1)S(1)} %get-tuple-element.35.right_ref, bf16[8,2,512,128]{3,2,1,0:T(8,128)(2,1)S(1)} %get-tuple-element.25.refs_8_.refs_4_.orb_ref, bf16[8,2,512,128]{3,2,1,0:T(8,128)(2,1)S(1)} %get-tuple-element.26.refs_9_.refs_5_.rest_ref, ...), custom_call_target="tpu_custom_call" | custom-call | tf_op jit(solution)/shard_map/pallas_call | solution.py:432
  32.6 0.6 %collective-permute-start.17 = (bf16[1,64,512]{2,1,0:T(8,128)(2,1)S(1)}, bf16[1,64,512]{2,1,0:T(8,128)(2,1)S(1)}, u32[]{:S(2)}, u32[]{:S(2)}) collective-permute-start(bf16[1,64,512]{2,1,0:T(8,128)(2,1)S(1)} %shard_map.60.refs_0_), channel_id=1, source_target_pairs={{0,1},{1,0},{2,3},{3,2},{4,5},{5,4},{6,7},{7,6},{8,9},{9,8},{10,11... | collective-permute-start | bytes 196616 | tf_op jit(solution)/shard_map/ppermute | solution.py:328
  33.2 0.6 %shard_map.61.keep_ref = f32[3,64,512]{2,1,0:T(8,128)S(1)} custom-call(bf16[4,128,1024]{2,1,0:T(8,128)(2,1)S(1)} %get-tuple-element.35.right_ref, bf16[8,2,512,128]{3,2,1,0:T(8,128)(2,1)S(1)} %get-tuple-element.25.refs_8_.refs_4_.orb_ref, bf16[8,2,512,128]{3,2,1,0:T(8,128)(2,1)S(1)} %get-tuple-element.26.refs_9_.refs_5_.rest_ref, ...), custom_call_target="tpu_custom_call" | custom-call | tf_op jit(solution)/shard_map/pallas_call | solution.py:432
  33.8 1.6 %collective-permute-start.14 = (bf16[64,512]{1,0:T(8,128)(2,1)S(1)}, bf16[64,512]{1,0:T(8,128)(2,1)S(1)}, u32[]{:S(2)}, u32[]{:S(2)}) collective-permute-start(bf16[64,512]{1,0:T(8,128)(2,1)S(1)} %get-tuple-element.37), channel_id=1, source_target_pairs={{0,2},{1,3},{2,4},{3,5},{4,6},{5,7},{6,0},{7,1},{8,10},{9,11},{10,... | collective-permute-start | bytes 196616 | tf_op jit(solution)/shard_map/ppermute | solution.py:340
  35.4 1.2 %collective-permute-start.15 = (bf16[64,512]{1,0:T(8,128)(2,1)S(1)}, bf16[64,512]{1,0:T(8,128)(2,1)S(1)}, u32[]{:S(2)}, u32[]{:S(2)}) collective-permute-start(bf16[64,512]{1,0:T(8,128)(2,1)S(1)} %get-tuple-element.38), channel_id=1, source_target_pairs={{0,4},{1,5},{2,6},{3,7},{4,0},{5,1},{6,2},{7,3},{8,12},{9,13},{10,... | collective-permute-start | bytes 196616 | tf_op jit(solution)/shard_map/ppermute | solution.py:340
  36.6 2.1 %collective-permute-start.16 = (bf16[64,512]{1,0:T(8,128)(2,1)S(1)}, bf16[64,512]{1,0:T(8,128)(2,1)S(1)}, u32[]{:S(2)}, u32[]{:S(2)}) collective-permute-start(bf16[64,512]{1,0:T(8,128)(2,1)S(1)} %get-tuple-element.39.refs_0_), channel_id=1, source_target_pairs={{0,6},{1,7},{2,0},{3,1},{4,2},{5,3},{6,4},{7,5},{8,14},{9,15},{10,... | collective-permute-start | bytes 196616 | tf_op jit(solution)/shard_map/ppermute | solution.py:340
  38.7 0.5 %shard_map.63.keep_ref = f32[1,64,512]{2,1,0:T(8,128)S(1)} custom-call(bf16[4,128,1024]{2,1,0:T(8,128)(2,1)S(1)} %get-tuple-element.35.right_ref, bf16[8,2,512,128]{3,2,1,0:T(8,128)(2,1)S(1)} %get-tuple-element.25.refs_8_.refs_4_.orb_ref, bf16[8,2,512,128]{3,2,1,0:T(8,128)(2,1)S(1)} %get-tuple-element.26.refs_9_.refs_5_.rest_ref, ...), custom_call_target="tpu_custom_call" | custom-call | tf_op jit(solution)/shard_map/pallas_call | solution.py:432
  39.2 1.4 %collective-permute-done.14.refs_0_ = bf16[64,512]{1,0:T(8,128)(2,1)S(1)} collective-permute-done((bf16[64,512]{1,0:T(8,128)(2,1)S(1)}, bf16[64,512]{1,0:T(8,128)(2,1)S(1)}, u32[]{:S(2)}, u32[]{:S(2)}) %collective-permute-start.14) | collective-permute-done | bytes 65568 | tf_op jit(solution)/shard_map/ppermute | solution.py:340
  40.7 1.9 %collective-permute-done.15.refs_1_ = bf16[64,512]{1,0:T(8,128)(2,1)S(1)} collective-permute-done((bf16[64,512]{1,0:T(8,128)(2,1)S(1)}, bf16[64,512]{1,0:T(8,128)(2,1)S(1)}, u32[]{:S(2)}, u32[]{:S(2)}) %collective-permute-start.15) | collective-permute-done | bytes 65568 | tf_op jit(solution)/shard_map/ppermute | solution.py:340
  42.6 1.7 %shard_map.65 = bf16[64,4,16,128]{3,2,1,0:T(8,128)(2,1)} custom-call(bf16[64,512]{1,0:T(8,128)(2,1)S(1)} %collective-permute-done.14.refs_0_, bf16[64,512]{1,0:T(8,128)(2,1)S(1)} %collective-permute-done.15.refs_1_, bf16[64,512]{1,0:T(8,128)(2,1)S(1)} %collective-permute-done.16.refs_2_, f32[64,512]{1,0:T(8,128)S(1)} %shard_map.64.refs_3_, ...), custom_call_target="tpu_custom_call" | custom-call | bytes 4194304 | tf_op jit(solution)/shard_map/pallas_call | solution.py:450
  (23 shorter events, 0.6 us)
Async XLA Ops:
  2.1 12.0 %copy-start = (bf16[8,32,256]{2,1,0:T(8,128)(2,1)S(1)}, bf16[8,32,256]{2,1,0:T(8,128)(2,1)}, u32[]{:S(2)}) copy-start(bf16[8,32,256]{2,1,0:T(8,128)(2,1)} %refs_11_.1) | copy-start | bytes 393220
  2.1 12.0 %copy-start.1 = (bf16[2,256,128]{2,1,0:T(8,128)(2,1)S(1)}, bf16[2,256,128]{2,1,0:T(8,128)(2,1)}, u32[]{:S(2)}) copy-start(bf16[2,256,128]{2,1,0:T(8,128)(2,1)} %constant.6.clone.refs_10_) | copy-start | bytes 393220
  2.1 8.0 %collective-permute-start.5 = (bf16[64,512]{1,0:T(8,128)(2,1)S(1)}, bf16[64,512]{1,0:T(8,128)(2,1)S(1)}, u32[]{:S(2)}, u32[]{:S(2)}) collective-permute-start(bf16[64,512]{1,0:T(8,128)(2,1)S(1)} %get-tuple-element.23.edge_hbm.refs_0_), channel_id=1, source_target_pairs={{0,6},{1,7},{2,4},{3,5},{4,2},{5,3},{6,0},{7,1},{8,14},{9,15},{10,... | collective-permute-start | bytes 196616 | tf_op jit(solution)/shard_map/ppermute | solution.py:328
  7.2 4.7 %collective-permute-start.3 = (bf16[64,512]{1,0:T(8,128)(2,1)S(1)}, bf16[64,512]{1,0:T(8,128)(2,1)S(1)}, u32[]{:S(2)}, u32[]{:S(2)}) collective-permute-start(bf16[64,512]{1,0:T(8,128)(2,1)S(1)} %get-tuple-element.23.edge_hbm.refs_0_), channel_id=1, source_target_pairs={{0,2},{1,3},{2,0},{3,1},{4,6},{5,7},{6,4},{7,5},{8,10},{9,11},{10,... | collective-permute-start | bytes 196616 | tf_op jit(solution)/shard_map/ppermute | solution.py:328
  7.2 5.6 %collective-permute-start.1 = (bf16[64,512]{1,0:T(8,128)(2,1)S(1)}, bf16[64,512]{1,0:T(8,128)(2,1)S(1)}, u32[]{:S(2)}, u32[]{:S(2)}) collective-permute-start(bf16[64,512]{1,0:T(8,128)(2,1)S(1)} %get-tuple-element.23.edge_hbm.refs_0_), channel_id=1, source_target_pairs={{0,4},{1,5},{2,6},{3,7},{4,0},{5,1},{6,2},{7,3},{8,12},{9,13},{10,... | collective-permute-start | bytes 196616 | tf_op jit(solution)/shard_map/ppermute | solution.py:328
  9.4 3.4 %collective-permute-start = (bf16[64,512]{1,0:T(8,128)(2,1)S(1)}, bf16[64,512]{1,0:T(8,128)(2,1)S(1)}, u32[]{:S(2)}, u32[]{:S(2)}) collective-permute-start(bf16[64,512]{1,0:T(8,128)(2,1)S(1)} %get-tuple-element.24), channel_id=1, source_target_pairs={{0,1},{1,0},{2,3},{3,2},{4,5},{5,4},{6,7},{7,6},{8,9},{9,8},{10,11... | collective-permute-start | bytes 196616 | tf_op jit(solution)/shard_map/ppermute | solution.py:328
  10.1 2.7 %collective-permute-start.6 = (bf16[64,512]{1,0:T(8,128)(2,1)S(1)}, bf16[64,512]{1,0:T(8,128)(2,1)S(1)}, u32[]{:S(2)}, u32[]{:S(2)}) collective-permute-start(bf16[64,512]{1,0:T(8,128)(2,1)S(1)} %collective-permute-done.5.refs_6_), channel_id=1, source_target_pairs={{0,1},{1,0},{2,3},{3,2},{4,5},{5,4},{6,7},{7,6},{8,9},{9,8},{10,11... | collective-permute-start | bytes 196616 | tf_op jit(solution)/shard_map/ppermute | solution.py:328
  11.9 1.3 %collective-permute-start.4 = (bf16[64,512]{1,0:T(8,128)(2,1)S(1)}, bf16[64,512]{1,0:T(8,128)(2,1)S(1)}, u32[]{:S(2)}, u32[]{:S(2)}) collective-permute-start(bf16[64,512]{1,0:T(8,128)(2,1)S(1)} %collective-permute-done.3.refs_4_), channel_id=1, source_target_pairs={{0,1},{1,0},{2,3},{3,2},{4,5},{5,4},{6,7},{7,6},{8,9},{9,8},{10,11... | collective-permute-start | bytes 196616 | tf_op jit(solution)/shard_map/ppermute | solution.py:328
  12.9 1.3 %collective-permute-start.2 = (bf16[64,512]{1,0:T(8,128)(2,1)S(1)}, bf16[64,512]{1,0:T(8,128)(2,1)S(1)}, u32[]{:S(2)}, u32[]{:S(2)}) collective-permute-start(bf16[64,512]{1,0:T(8,128)(2,1)S(1)} %collective-permute-done.1.refs_2_), channel_id=1, source_target_pairs={{0,1},{1,0},{2,3},{3,2},{4,5},{5,4},{6,7},{7,6},{8,9},{9,8},{10,11... | collective-permute-start | bytes 196616 | tf_op jit(solution)/shard_map/ppermute | solution.py:328
  14.1 9.4 %copy-start.2 = (bf16[64,128]{1,0:T(8,128)(2,1)S(1)}, bf16[64,128]{1,0:T(8,128)(2,1)}, u32[]{:S(2)}) copy-start(bf16[64,128]{1,0:T(8,128)(2,1)} %constant.8.clone.refs_5_) | copy-start | bytes 49156
  14.1 9.4 %copy-start.3 = (bf16[64,128]{1,0:T(8,128)(2,1)S(1)}, bf16[64,128]{1,0:T(8,128)(2,1)}, u32[]{:S(2)}) copy-start(bf16[64,128]{1,0:T(8,128)(2,1)} %constant.7.clone.refs_4_) | copy-start | bytes 49156
  15.5 5.9 %collective-permute-start.7 = (bf16[192,256]{1,0:T(8,128)(2,1)S(1)}, bf16[192,256]{1,0:T(8,128)(2,1)S(1)}, u32[]{:S(2)}, u32[]{:S(2)}) collective-permute-start(bf16[192,256]{1,0:T(8,128)(2,1)S(1)} %get-tuple-element.27), channel_id=1, source_target_pairs={{0,24},{8,16},{16,8},{24,0},{1,25},{9,17},{17,9},{25,1},{2,26},{10... | collective-permute-start | bytes 294920 | tf_op jit(solution)/shard_map/ppermute | solution.py:328
  18.0 5.4 %collective-permute-start.8 = (bf16[192,256]{1,0:T(8,128)(2,1)S(1)}, bf16[192,256]{1,0:T(8,128)(2,1)S(1)}, u32[]{:S(2)}, u32[]{:S(2)}) collective-permute-start(bf16[192,256]{1,0:T(8,128)(2,1)S(1)} %get-tuple-element.28), channel_id=1, source_target_pairs={{0,16},{8,24},{16,0},{24,8},{1,17},{9,25},{17,1},{25,9},{2,18},{10... | collective-permute-start | bytes 294920 | tf_op jit(solution)/shard_map/ppermute | solution.py:328
  18.5 5.0 %collective-permute-start.9 = (bf16[192,256]{1,0:T(8,128)(2,1)S(1)}, bf16[192,256]{1,0:T(8,128)(2,1)S(1)}, u32[]{:S(2)}, u32[]{:S(2)}) collective-permute-start(bf16[192,256]{1,0:T(8,128)(2,1)S(1)} %get-tuple-element.29), channel_id=1, source_target_pairs={{0,8},{8,0},{16,24},{24,16},{1,9},{9,1},{17,25},{25,17},{2,10},{10... | collective-permute-start | bytes 294920 | tf_op jit(solution)/shard_map/ppermute | solution.py:328
  24.1 5.7 %collective-permute-start.10 = (bf16[128,256]{1,0:T(8,128)(2,1)S(1)}, bf16[128,256]{1,0:T(8,128)(2,1)S(1)}, u32[]{:S(2)}, u32[]{:S(2)}) collective-permute-start(bf16[128,256]{1,0:T(8,128)(2,1)S(1)} %get-tuple-element.31), channel_id=1, source_target_pairs={{0,24},{8,16},{16,8},{24,0},{1,25},{9,17},{17,9},{25,1},{2,26},{10... | collective-permute-start | bytes 196616 | tf_op jit(solution)/shard_map/ppermute | solution.py:328
  25.9 4.4 %collective-permute-start.11 = (bf16[128,256]{1,0:T(8,128)(2,1)S(1)}, bf16[128,256]{1,0:T(8,128)(2,1)S(1)}, u32[]{:S(2)}, u32[]{:S(2)}) collective-permute-start(bf16[128,256]{1,0:T(8,128)(2,1)S(1)} %get-tuple-element.32), channel_id=1, source_target_pairs={{0,16},{8,24},{16,0},{24,8},{1,17},{9,25},{17,1},{25,9},{2,18},{10... | collective-permute-start | bytes 196616 | tf_op jit(solution)/shard_map/ppermute | solution.py:328
  27.2 4.3 %collective-permute-start.12 = (bf16[128,256]{1,0:T(8,128)(2,1)S(1)}, bf16[128,256]{1,0:T(8,128)(2,1)S(1)}, u32[]{:S(2)}, u32[]{:S(2)}) collective-permute-start(bf16[128,256]{1,0:T(8,128)(2,1)S(1)} %get-tuple-element.33), channel_id=1, source_target_pairs={{0,8},{8,0},{16,24},{24,16},{1,9},{9,1},{17,25},{25,17},{2,10},{10... | collective-permute-start | bytes 196616 | tf_op jit(solution)/shard_map/ppermute | solution.py:328
  32.1 1.7 %collective-permute-start.13 = (bf16[3,64,512]{2,1,0:T(8,128)(2,1)S(1)}, bf16[3,64,512]{2,1,0:T(8,128)(2,1)S(1)}, u32[]{:S(2)}, u32[]{:S(2)}) collective-permute-start(bf16[3,64,512]{2,1,0:T(8,128)(2,1)S(1)} %get-tuple-element.36.refs_0_), channel_id=1, source_target_pairs={{0,1},{1,0},{2,3},{3,2},{4,5},{5,4},{6,7},{7,6},{8,9},{9,8},{10,11... | collective-permute-start | bytes 589832 | tf_op jit(solution)/shard_map/ppermute | solution.py:328
  32.6 6.6 %collective-permute-start.17 = (bf16[1,64,512]{2,1,0:T(8,128)(2,1)S(1)}, bf16[1,64,512]{2,1,0:T(8,128)(2,1)S(1)}, u32[]{:S(2)}, u32[]{:S(2)}) collective-permute-start(bf16[1,64,512]{2,1,0:T(8,128)(2,1)S(1)} %shard_map.60.refs_0_), channel_id=1, source_target_pairs={{0,1},{1,0},{2,3},{3,2},{4,5},{5,4},{6,7},{7,6},{8,9},{9,8},{10,11... | collective-permute-start | bytes 196616 | tf_op jit(solution)/shard_map/ppermute | solution.py:328
  33.8 6.9 %collective-permute-start.14 = (bf16[64,512]{1,0:T(8,128)(2,1)S(1)}, bf16[64,512]{1,0:T(8,128)(2,1)S(1)}, u32[]{:S(2)}, u32[]{:S(2)}) collective-permute-start(bf16[64,512]{1,0:T(8,128)(2,1)S(1)} %get-tuple-element.37), channel_id=1, source_target_pairs={{0,2},{1,3},{2,4},{3,5},{4,6},{5,7},{6,0},{7,1},{8,10},{9,11},{10,... | collective-permute-start | bytes 196616 | tf_op jit(solution)/shard_map/ppermute | solution.py:340
  35.4 7.1 %collective-permute-start.15 = (bf16[64,512]{1,0:T(8,128)(2,1)S(1)}, bf16[64,512]{1,0:T(8,128)(2,1)S(1)}, u32[]{:S(2)}, u32[]{:S(2)}) collective-permute-start(bf16[64,512]{1,0:T(8,128)(2,1)S(1)} %get-tuple-element.38), channel_id=1, source_target_pairs={{0,4},{1,5},{2,6},{3,7},{4,0},{5,1},{6,2},{7,3},{8,12},{9,13},{10,... | collective-permute-start | bytes 196616 | tf_op jit(solution)/shard_map/ppermute | solution.py:340
  36.6 6.0 %collective-permute-start.16 = (bf16[64,512]{1,0:T(8,128)(2,1)S(1)}, bf16[64,512]{1,0:T(8,128)(2,1)S(1)}, u32[]{:S(2)}, u32[]{:S(2)}) collective-permute-start(bf16[64,512]{1,0:T(8,128)(2,1)S(1)} %get-tuple-element.39.refs_0_), channel_id=1, source_target_pairs={{0,6},{1,7},{2,0},{3,1},{4,2},{5,3},{6,4},{7,5},{8,14},{9,15},{10,... | collective-permute-start | bytes 196616 | tf_op jit(solution)/shard_map/ppermute | solution.py:340
